TPU v7x, 32 devices: a whole 2x2x4 slice. The times are simulated.
32 devices in a mesh: groups: 2 (over y), tp: 4 (over z), rep: 2 (over x), sub: 2 (over core).
Axes of the slice: x: 2, y: 2, z: 4, core: 2. Of those that a mesh axis runs over, the one named last changes fastest.
Arguments:
- hidden: bfloat16 [4, 512, 28672], P(None, ('groups', 'rep', 'sub'), 'tp'), parts along dimension 1, may hold values from -6 to 6
- base_weight: bfloat16 [28672, 8192], P('tp', ('rep', 'sub')), may hold values from -0.03125 to 0.03125
- down_a: bfloat16 [4, 28672, 64], P(('rep', 'sub'), 'tp'), may hold values from -0.03125 to 0.03125
- up_b: bfloat16 [4, 64, 8192], P('tp', None, ('rep', 'sub')), may hold values from -0.75 to 0.75
- adapter_ids: int32 [512, 1], P('groups'), parts along dimension 0, may hold values from 0 to 3; in each aligned block of 256 rows (0 to 255, 256 to 511, ...) at most 128 rows name the same one
- owner_map: int32 [4], replicated, may hold values from 0 to 3, each once
Outputs:
- projected: bfloat16 [4, 512, 8192], P(None, ('groups', 'tp'), ('rep', 'sub')), parts along dimension 1
There are 2 independent parts, one for each index of `groups`. A program takes and returns all parts, laid end to end along the dimension named above; an argument that names none is the same for every part. Nothing has to cross between parts.
Inputs may be any that keep to these rules, and one draw needn't show every extreme that they name: `adapter_ids`: no adapter is named by more than 128 requests, a bound that some block reaches. `owner_map`: each slot holds exactly one adapter.
All inputs are finite; a program needn't handle non-finite values.
Results may differ from a plain program's by a relative error of at most 0.0036.
Values may be sent and summed in bfloat16 or wider, within the bound.
No kernel may reach another device: no remote copies, remote signals or barrier semaphores. Data moves between devices by JAX's collectives and lax.ppermute only.
A program may use at most 192 MiB of HBM per device.

v0:
```python
import functools

import jax
import jax.numpy as jnp
from jax import lax
from jax.experimental import pallas as pl
from jax.experimental.pallas import tpu as pltpu
from jax.sharding import PartitionSpec as P

ADAPTER_SCALE = 0.5
BLOCK_N = 256
VMEM_BYTES = 40 * 1024 * 1024


def matmul_body(first, steps, pos_ref, own_ref, sib_ref, w_ref, a_ref,
                send_ref, keep_ref, rank_send_ref, rank_keep_ref, x_ref, sems):
    rows = send_ref.shape[0]
    depth = w_ref.shape[0]
    slots, _, rank = a_ref.shape
    place = pl.program_id(0)

    @pl.when(place == 0)
    def _():
        own_at = pos_ref[0]
        own_copy = pltpu.make_async_copy(own_ref.at[pl.ds(first, steps)], x_ref.at[own_at], sems.at[0])
        sib_copy = pltpu.make_async_copy(sib_ref.at[pl.ds(first, steps)], x_ref.at[1 - own_at], sems.at[1])
        own_copy.start()
        sib_copy.start()
        own_copy.wait()
        sib_copy.wait()
        x = x_ref[...].reshape(2 * rows, depth)
        for slot in range(slots):
            part = jnp.dot(x, a_ref[slot], preferred_element_type=jnp.float32)
            rank_send_ref[:, slot * rank:(slot + 1) * rank] = part[:rows]
            rank_keep_ref[:, slot * rank:(slot + 1) * rank] = part[rows:]

    x = x_ref[...].reshape(2 * rows, depth)
    term = jnp.dot(x, w_ref[...], preferred_element_type=jnp.float32)
    send_ref[...] = term[:rows].astype(send_ref.dtype)
    keep_ref[...] = term[rows:]


def partial_products(pos, own, sib, first, steps, weight, down_a):
    _, per_block, depth = own.shape
    width = weight.shape[1]
    slots, _, rank = down_a.shape
    rows = steps * per_block
    block_n = min(BLOCK_N, width)
    any_spec = pl.BlockSpec(memory_space=pl.ANY)
    flops = 2 * 2 * rows * depth * (width + slots * rank)
    moved = 2 * depth * (2 * rows + width + slots * rank) + 6 * rows * width
    return pl.pallas_call(
        functools.partial(matmul_body, first, steps),
        grid=(width // block_n,),
        in_specs=[
            pl.BlockSpec(memory_space=pltpu.SMEM),
            any_spec,
            any_spec,
            pl.BlockSpec((depth, block_n), lambda i: (0, i)),
            pl.BlockSpec((slots, depth, rank), lambda i: (0, 0, 0)),
        ],
        out_specs=[
            pl.BlockSpec((rows, block_n), lambda i: (0, i)),
            pl.BlockSpec((rows, block_n), lambda i: (0, i)),
            pl.BlockSpec((rows, slots * rank), lambda i: (0, 0)),
            pl.BlockSpec((rows, slots * rank), lambda i: (0, 0)),
        ],
        out_shape=[
            jax.ShapeDtypeStruct((rows, width), jnp.bfloat16),
            jax.ShapeDtypeStruct((rows, width), jnp.float32),
            jax.ShapeDtypeStruct((rows, slots * rank), jnp.float32),
            jax.ShapeDtypeStruct((rows, slots * rank), jnp.float32),
        ],
        scratch_shapes=[
            pltpu.VMEM((2, steps, per_block, depth), jnp.bfloat16),
            pltpu.SemaphoreType.DMA((2,)),
        ],
        compiler_params=pltpu.CompilerParams(
            dimension_semantics=("arbitrary",), vmem_limit_bytes=VMEM_BYTES
        ),
        cost_estimate=pl.CostEstimate(flops=flops, bytes_accessed=moved, transcendentals=0),
        name="partial_products",
    )(pos, own, sib, weight, down_a)


def per_device(hidden, base_weight, down_a, up_b, adapter_ids, owner_map):
    step_count, per_block, _ = hidden.shape
    n_tensor = lax.axis_size("tp")
    n_rep = lax.axis_size("rep")
    n_sub = lax.axis_size("sub")
    n_owners = n_rep * n_sub
    tensor_index = lax.axis_index("tp")
    rep_index = lax.axis_index("rep")
    sub_index = lax.axis_index("sub")
    owner_index = lax.axis_index(("rep", "sub"))
    requests = per_block * n_owners
    rows_mine = requests // n_tensor
    group = n_tensor // n_rep
    group_index = tensor_index // group
    owned_slots, _, rank_size = down_a.shape
    slot_count = owned_slots * n_owners
    width = base_weight.shape[1]

    def swap_cores(value):
        return lax.ppermute(value, "sub", [(i, i ^ 1) for i in range(n_sub)])

    def from_rep(value, shift):
        return lax.ppermute(value, "rep", [((i + shift) % n_rep, i) for i in range(n_rep)])

    def swap_tensor(value, bit):
        return lax.ppermute(value, "tp", [(i, i ^ bit) for i in range(n_tensor)])

    def to_group(value, shift, hop):
        pairs = []
        for rep in range(n_rep):
            target = (rep + shift) % n_rep
            source = (target + hop) % n_rep
            for low in range(group):
                pairs.append(((source * group + low) * n_rep + rep, (target * group + low) * n_rep + rep))
        return lax.ppermute(value, ("tp", "rep"), pairs)

    def reduce_rows(send, keep, steps, shift, kind):
        columns = keep.shape[1]
        total = keep + swap_tensor(send, group // 2).astype(jnp.float32)
        extent, bit = per_block, group // 4
        while bit:
            extent //= 2
            halves = total.reshape(steps, 2, extent, columns)
            mine = (tensor_index // bit) % 2
            kept = lax.dynamic_index_in_dim(halves, mine, 1, keepdims=False)
            sent = lax.dynamic_index_in_dim(halves, 1 - mine, 1, keepdims=False)
            total = kept + swap_tensor(sent.astype(kind), bit).astype(jnp.float32)
            bit //= 2
        total = total.reshape(steps, rows_mine, columns)
        rounded = total.astype(kind)
        for hop in range(1, n_rep):
            total = total + to_group(rounded, shift, hop).astype(jnp.float32)
        return total

    keeps = (tensor_index // (group // 2)) % 2
    pos = (sub_index == keeps).astype(jnp.int32).reshape(1)

    panels = lax.all_gather(up_b, "tp", axis=0, tiled=True).reshape(slot_count * rank_size, width)

    remote = {}
    for step in range(step_count):
        for shift in range(1, n_rep):
            remote[step, shift] = from_rep(hidden[step:step + 1], shift)

    my_ids = lax.dynamic_slice_in_dim(adapter_ids, tensor_index * rows_mine, rows_mine)
    iota = lax.broadcasted_iota(jnp.int32, (rows_mine, slot_count), 1)
    my_slot = jnp.sum((my_ids == iota).astype(jnp.int32) * owner_map[None, :], axis=1)
    slot_hot = my_slot[:, None] == iota

    base_sum = [None] * step_count
    rank_sum = [None] * step_count
    half = step_count // 2
    for first in (0, half):
        sib = swap_cores(hidden[first:first + half])
        own = hidden[first:first + half]
        send, keep, rank_send, rank_keep = partial_products(
            pos, own, sib, 0, half, base_weight, down_a
        )
        ranks = reduce_rows(rank_send, rank_keep, half, 0, jnp.float32)
        sums = reduce_rows(send, keep, half, 0, jnp.bfloat16)
        for step in range(half):
            base_sum[first + step] = sums[step]
            rank_sum[first + step] = ranks[step]

    outputs = []
    for step in range(step_count):
        for shift in range(1, n_rep):
            own = remote[step, shift]
            sib = swap_cores(own)
            send, keep, rank_send, rank_keep = partial_products(
                pos, own, sib, 0, 1, base_weight, down_a
            )
            here = group_index == (rep_index + shift) % n_rep
            ranks = reduce_rows(rank_send, rank_keep, 1, shift, jnp.float32)[0]
            rank_sum[step] = jnp.where(here, ranks, rank_sum[step])
            sums = reduce_rows(send, keep, 1, shift, jnp.bfloat16)[0]
            base_sum[step] = jnp.where(here, sums, base_sum[step])
        finished = rank_sum[step].astype(jnp.bfloat16).reshape(rows_mine, owned_slots, rank_size)
        owned_hot = lax.dynamic_slice_in_dim(slot_hot, owner_index * owned_slots, owned_slots, axis=1)
        masked = jnp.sum(
            jnp.where(owned_hot[:, :, None], finished, 0), axis=1, dtype=jnp.float32
        ).astype(jnp.bfloat16)
        chosen = masked
        for turn in range(1, n_owners):
            chosen = chosen + lax.ppermute(
                masked, ("rep", "sub"), [(i, (i + turn) % n_owners) for i in range(n_owners)]
            )
        spread = jnp.where(slot_hot[:, :, None], chosen[:, None, :], 0).reshape(
            rows_mine, slot_count * rank_size
        )
        lifted = jnp.dot(spread, panels, preferred_element_type=jnp.float32).astype(jnp.bfloat16)
        outputs.append(
            (base_sum[step] + ADAPTER_SCALE * lifted.astype(jnp.float32)).astype(jnp.bfloat16)
        )
    return jnp.stack(outputs, axis=0)


def solution(mesh):
    return jax.shard_map(
        per_device,
        mesh=mesh,
        in_specs=(
            P(None, ("groups", "rep", "sub"), "tp"),
            P("tp", ("rep", "sub")),
            P(("rep", "sub"), "tp", None),
            P("tp", None, ("rep", "sub")),
            P("groups", None),
            P(),
        ),
        out_specs=P(None, ("groups", "tp"), ("rep", "sub")),
        check_vma=False,
    )
```

profile of v0, /device:TPU:0, one launch (start us, length us, event | category | flops | bytes accessed | tf_op | source)
XLA Modules:
  0.0 355.1 jit_solution(4076661694768578473)
XLA Ops:
  6.5 4.3 %fusion.69 = (bf16[2,64,7168]{2,1,0:T(8,128)(2,1)}, bf16[2,64,7168]{2,1,0:T(8,128)(2,1)}) fusion(bf16[4,64,7168]{2,1,0:T(8,128)(2,1)} %param.6), kind=kLoop, calls=%fused_computation.107 | loop fusion | bytes 7340032 | tf_op jit(solution)/shard_map/slice | solution.py:160
  11.3 1.9 fusion.68
  13.2 2.5 collective-permute-start.14
  15.7 2.0 collective-permute-start.37
  17.7 1.9 copy.19.a_ref
  19.8 17.4 %collective-permute-done.14.own_ref = bf16[1,64,7168]{2,1,0:T(8,128)(2,1)} collective-permute-done((bf16[1,64,7168]{2,1,0:T(8,128)(2,1)}, bf16[1,64,7168]{2,1,0:T(8,128)(2,1)}, u32[]{:S(2)}, u32[]{:S(2)}) %collective-permute-start.14) | collective-permute-done | bytes 917536 | tf_op jit(solution)/shard_map/ppermute | solution.py:108
  37.2 19.5 %collective-permute-done.23.own_ref = bf16[1,64,7168]{2,1,0:T(8,128)(2,1)S(1)} collective-permute-done((bf16[1,64,7168]{2,1,0:T(8,128)(2,1)}, bf16[1,64,7168]{2,1,0:T(8,128)(2,1)S(1)}, u32[]{:S(2)}, u32[]{:S(2)}) %collective-permute-start.23) | collective-permute-done | bytes 917536 | tf_op jit(solution)/shard_map/ppermute | solution.py:108
  56.7 19.8 %collective-permute-done.37.own_ref = bf16[1,64,7168]{2,1,0:T(8,128)(2,1)} collective-permute-done((bf16[1,64,7168]{2,1,0:T(8,128)(2,1)}, bf16[1,64,7168]{2,1,0:T(8,128)(2,1)}, u32[]{:S(2)}, u32[]{:S(2)}) %collective-permute-start.37) | collective-permute-done | bytes 917536 | tf_op jit(solution)/shard_map/ppermute | solution.py:108
  76.5 19.5 %collective-permute-done.own_ref = bf16[1,64,7168]{2,1,0:T(8,128)(2,1)} collective-permute-done((bf16[1,64,7168]{2,1,0:T(8,128)(2,1)}, bf16[1,64,7168]{2,1,0:T(8,128)(2,1)}, u32[]{:S(2)}, u32[]{:S(2)}) %collective-permute-start) | collective-permute-done | bytes 917536 | tf_op jit(solution)/shard_map/ppermute | solution.py:108
  96.5 18.5 %partial_products.10 = (bf16[128,2048]{1,0:T(8,128)(2,1)}, f32[128,2048]{1,0:T(8,128)S(1)}, f32[128,64]{1,0:T(8,128)S(1)}, f32[128,64]{1,0:T(8,128)S(1)}) custom-call(s32[1]{0:T(128)} %bitcast.pos_ref, bf16[2,64,7168]{2,1,0:T(8,128)(2,1)} %get-tuple-element.58.own_ref, bf16[2,64,7168]{2,1,0:T(8,128)(2,1)} %collective-permute-done.27.sib_ref, ...), custom_call_target="tpu_custom_call" | custom-call | flops 7751073792 | bytes 35520512 | tf_op jit(solution)/shard_map/partial_products/pallas_call | solution.py:52
  115.0 1.9 collective-permute-start.32
  116.9 14.7 %partial_products.8 = (bf16[64,2048]{1,0:T(8,128)(2,1)S(1)}, f32[64,2048]{1,0:T(8,128)S(1)}, f32[64,64]{1,0:T(8,128)S(1)}, f32[64,64]{1,0:T(8,128)S(1)}) custom-call(s32[1]{0:T(128)} %bitcast.pos_ref, bf16[1,64,7168]{2,1,0:T(8,128)(2,1)} %collective-permute-done.14.own_ref, bf16[1,64,7168]{2,1,0:T(8,128)(2,1)S(1)} %collective-permute-done.15.sib_ref, ...), custom_call_target="tpu_custom_call" | custom-call | flops 3875536896 | bytes 32899072 | tf_op jit(solution)/shard_map/partial_products/pallas_call | solution.py:52
  132.4 13.7 %partial_products.9 = (bf16[64,2048]{1,0:T(8,128)(2,1)S(1)}, f32[64,2048]{1,0:T(8,128)S(1)}, f32[64,64]{1,0:T(8,128)S(1)}, f32[64,64]{1,0:T(8,128)S(1)}) custom-call(s32[1]{0:T(128)} %bitcast.pos_ref, bf16[1,64,7168]{2,1,0:T(8,128)(2,1)S(1)} %copy-done.9, bf16[1,64,7168]{2,1,0:T(8,128)(2,1)S(1)} %collective-permute-done.24.sib_ref, ...), custom_call_target="tpu_custom_call" | custom-call | flops 3875536896 | bytes 32899072 | tf_op jit(solution)/shard_map/partial_products/pallas_call | solution.py:52
  147.6 14.7 %partial_products.11 = (bf16[64,2048]{1,0:T(8,128)(2,1)S(1)}, f32[64,2048]{1,0:T(8,128)S(1)}, f32[64,64]{1,0:T(8,128)S(1)}, f32[64,64]{1,0:T(8,128)S(1)}) custom-call(s32[1]{0:T(128)} %bitcast.pos_ref, bf16[1,64,7168]{2,1,0:T(8,128)(2,1)} %collective-permute-done.37.own_ref, bf16[1,64,7168]{2,1,0:T(8,128)(2,1)S(1)} %collective-permute-done.38.sib_ref, ...), custom_call_target="tpu_custom_call" | custom-call | flops 3875536896 | bytes 32899072 | tf_op jit(solution)/shard_map/partial_products/pallas_call | solution.py:52
  163.7 14.7 %partial_products.6 = (bf16[64,2048]{1,0:T(8,128)(2,1)S(1)}, f32[64,2048]{1,0:T(8,128)S(1)}, f32[64,64]{1,0:T(8,128)S(1)}, f32[64,64]{1,0:T(8,128)S(1)}) custom-call(s32[1]{0:T(128)} %bitcast.pos_ref, bf16[1,64,7168]{2,1,0:T(8,128)(2,1)} %collective-permute-done.own_ref, bf16[1,64,7168]{2,1,0:T(8,128)(2,1)S(1)} %collective-permute-done.1.sib_ref, ...), custom_call_target="tpu_custom_call" | custom-call | flops 3875536896 | bytes 32899072 | tf_op jit(solution)/shard_map/partial_products/pallas_call | solution.py:52
  180.0 15.8 %partial_products.7 = (bf16[128,2048]{1,0:T(8,128)(2,1)S(1)}, f32[128,2048]{1,0:T(8,128)S(1)}, f32[128,64]{1,0:T(8,128)S(1)}, f32[128,64]{1,0:T(8,128)S(1)}) custom-call(s32[1]{0:T(128)} %bitcast.pos_ref, bf16[2,64,7168]{2,1,0:T(8,128)(2,1)S(1)} %copy-done.2, bf16[2,64,7168]{2,1,0:T(8,128)(2,1)S(1)} %collective-permute-done.4.sib_ref, ...), custom_call_target="tpu_custom_call" | custom-call | flops 7751073792 | bytes 35520512 | tf_op jit(solution)/shard_map/partial_products/pallas_call | solution.py:52
  197.3 5.1 %collective-permute-start.19 = (f32[1,64,64]{2,1,0:T(8,128)S(1)}, f32[1,64,64]{2,1,0:T(8,128)}, u32[]{:S(2)}, u32[]{:S(2)}) collective-permute-start(f32[1,64,64]{2,1,0:T(8,128)S(1)} %add_bitcast_fusion.2), channel_id=1, source_target_pairs={{0,8},{4,12},{10,2},{14,6},{1,9},{5,13},{11,3},{15,7},{16,24},{20,... | collective-permute-start | bytes 49160 | tf_op jit(solution)/shard_map/ppermute | solution.py:120
  202.5 1.9 collective-permute-start.31
  204.4 1.9 collective-permute-start.42
  207.6 6.0 %collective-permute-start.8 = (f32[1,64,64]{2,1,0:T(8,128)S(1)}, f32[1,64,64]{2,1,0:T(8,128)}, u32[]{:S(2)}, u32[]{:S(2)}) collective-permute-start(f32[1,64,64]{2,1,0:T(8,128)S(1)} %add_bitcast_fusion.3), channel_id=1, source_target_pairs={{0,8},{4,12},{10,2},{14,6},{1,9},{5,13},{11,3},{15,7},{16,24},{20,... | collective-permute-start | bytes 49160 | tf_op jit(solution)/shard_map/ppermute | solution.py:120
  215.1 5.7 %collective-permute-done.10 = f32[2,64,64]{2,1,0:T(8,128)S(1)} collective-permute-done((f32[2,64,64]{2,1,0:T(8,128)S(1)}, f32[2,64,64]{2,1,0:T(8,128)S(1)}, u32[]{:S(2)}, u32[]{:S(2)}) %collective-permute-start.10) | collective-permute-done | bytes 32800 | tf_op jit(solution)/shard_map/ppermute | solution.py:120
  225.8 1.8 collective-permute-start.21
  229.7 1.7 collective-permute-start.35
  239.6 21.6 %collective-permute-done.2 = bf16[64,2048]{1,0:T(8,128)(2,1)S(1)} collective-permute-done((bf16[64,2048]{1,0:T(8,128)(2,1)S(1)}, bf16[64,2048]{1,0:T(8,128)(2,1)S(1)}, u32[]{:S(2)}, u32[]{:S(2)}) %collective-permute-start.2) | collective-permute-done | bytes 262176 | tf_op jit(solution)/shard_map/ppermute | solution.py:111
  262.1 4.8 %collective-permute-done.16 = bf16[64,2048]{1,0:T(8,128)(2,1)S(1)} collective-permute-done((bf16[64,2048]{1,0:T(8,128)(2,1)S(1)}, bf16[64,2048]{1,0:T(8,128)(2,1)S(1)}, u32[]{:S(2)}, u32[]{:S(2)}) %collective-permute-start.16) | collective-permute-done | bytes 262176 | tf_op jit(solution)/shard_map/ppermute | solution.py:111
  266.9 3.9 %collective-permute-start.3 = (bf16[1,64,2048]{2,1,0:T(8,128)(2,1)}, bf16[1,64,2048]{2,1,0:T(8,128)(2,1)}, u32[]{:S(2)}, u32[]{:S(2)}) collective-permute-start(bf16[1,64,2048]{2,1,0:T(8,128)(2,1)} %fusion.31), channel_id=1, source_target_pairs={{0,8},{4,12},{10,2},{14,6},{1,9},{5,13},{11,3},{15,7},{16,24},{20,... | collective-permute-start | bytes 786440 | tf_op jit(solution)/shard_map/ppermute | solution.py:120
  272.5 15.1 %collective-permute-start.17 = (bf16[1,64,2048]{2,1,0:T(8,128)(2,1)}, bf16[1,64,2048]{2,1,0:T(8,128)(2,1)}, u32[]{:S(2)}, u32[]{:S(2)}) collective-permute-start(bf16[1,64,2048]{2,1,0:T(8,128)(2,1)} %fusion.30), channel_id=1, source_target_pairs={{0,8},{4,12},{10,2},{14,6},{1,9},{5,13},{11,3},{15,7},{16,24},{20,... | collective-permute-start | bytes 786440 | tf_op jit(solution)/shard_map/ppermute | solution.py:120
  288.4 2.0 collective-permute-start.26
  295.5 35.1 %collective-permute-done.6 = bf16[2,64,2048]{2,1,0:T(8,128)(2,1)S(1)} collective-permute-done((bf16[2,64,2048]{2,1,0:T(8,128)(2,1)S(1)}, bf16[2,64,2048]{2,1,0:T(8,128)(2,1)S(1)}, u32[]{:S(2)}, u32[]{:S(2)}) %collective-permute-start.6) | collective-permute-done | bytes 524320 | tf_op jit(solution)/shard_map/ppermute | solution.py:120
  330.6 2.2 collective-permute-start.40
  333.9 5.7 %collective-permute-done.29 = bf16[2,64,2048]{2,1,0:T(8,128)(2,1)S(1)} collective-permute-done((bf16[2,64,2048]{2,1,0:T(8,128)(2,1)S(1)}, bf16[2,64,2048]{2,1,0:T(8,128)(2,1)S(1)}, u32[]{:S(2)}, u32[]{:S(2)}) %collective-permute-start.29) | collective-permute-done | bytes 524320 | tf_op jit(solution)/shard_map/ppermute | solution.py:120
  340.7 2.0 fusion.32
  (168 shorter events, 41.7 us)
Async XLA Ops:
  6.5 334.2 %all-gather.2.cloned.1.call-start = ((), (), s32[]{:S(2)}) async-start(), calls=%async_computation | async-start | bytes 1310720 | tf_op jit(solution)/shard_map/all_gather | solution.py:143
  10.8 85.2 %collective-permute-start.27 = (bf16[2,64,7168]{2,1,0:T(8,128)(2,1)}, bf16[2,64,7168]{2,1,0:T(8,128)(2,1)}, u32[]{:S(2)}, u32[]{:S(2)}) collective-permute-start(bf16[2,64,7168]{2,1,0:T(8,128)(2,1)} %get-tuple-element.58.own_ref), channel_id=1, source_target_pairs={{0,1},{1,0},{2,3},{3,2},{4,5},{5,4},{6,7},{7,6},{8,9},{9,8},{10,11... | collective-permute-start | bytes 5505032 | tf_op jit(solution)/shard_map/ppermute | solution.py:105
  13.2 24.0 %collective-permute-start.14 = (bf16[1,64,7168]{2,1,0:T(8,128)(2,1)}, bf16[1,64,7168]{2,1,0:T(8,128)(2,1)}, u32[]{:S(2)}, u32[]{:S(2)}) collective-permute-start(bf16[1,64,7168]{2,1,0:T(8,128)(2,1)} %get-tuple-element.55), channel_id=1, source_target_pairs={{2,0},{0,2},{3,1},{1,3},{6,4},{4,6},{7,5},{5,7},{10,8},{8,10},{11,... | collective-permute-start | bytes 2752520 | tf_op jit(solution)/shard_map/ppermute | solution.py:108
  15.6 41.1 %collective-permute-start.23 = (bf16[1,64,7168]{2,1,0:T(8,128)(2,1)}, bf16[1,64,7168]{2,1,0:T(8,128)(2,1)S(1)}, u32[]{:S(2)}, u32[]{:S(2)}) collective-permute-start(bf16[1,64,7168]{2,1,0:T(8,128)(2,1)} %get-tuple-element.54), channel_id=1, source_target_pairs={{2,0},{0,2},{3,1},{1,3},{6,4},{4,6},{7,5},{5,7},{10,8},{8,10},{11,... | collective-permute-start | bytes 2752520 | tf_op jit(solution)/shard_map/ppermute | solution.py:108
  15.7 60.8 %collective-permute-start.37 = (bf16[1,64,7168]{2,1,0:T(8,128)(2,1)}, bf16[1,64,7168]{2,1,0:T(8,128)(2,1)}, u32[]{:S(2)}, u32[]{:S(2)}) collective-permute-start(bf16[1,64,7168]{2,1,0:T(8,128)(2,1)} %get-tuple-element.56), channel_id=1, source_target_pairs={{2,0},{0,2},{3,1},{1,3},{6,4},{4,6},{7,5},{5,7},{10,8},{8,10},{11,... | collective-permute-start | bytes 2752520 | tf_op jit(solution)/shard_map/ppermute | solution.py:108
  17.7 78.3 %collective-permute-start = (bf16[1,64,7168]{2,1,0:T(8,128)(2,1)}, bf16[1,64,7168]{2,1,0:T(8,128)(2,1)}, u32[]{:S(2)}, u32[]{:S(2)}) collective-permute-start(bf16[1,64,7168]{2,1,0:T(8,128)(2,1)} %get-tuple-element.53), channel_id=1, source_target_pairs={{2,0},{0,2},{3,1},{1,3},{6,4},{4,6},{7,5},{5,7},{10,8},{8,10},{11,... | collective-permute-start | bytes 2752520 | tf_op jit(solution)/shard_map/ppermute | solution.py:108
  37.2 77.9 %collective-permute-start.15 = (bf16[1,64,7168]{2,1,0:T(8,128)(2,1)}, bf16[1,64,7168]{2,1,0:T(8,128)(2,1)S(1)}, u32[]{:S(2)}, u32[]{:S(2)}) collective-permute-start(bf16[1,64,7168]{2,1,0:T(8,128)(2,1)} %collective-permute-done.14.own_ref), channel_id=1, source_target_pairs={{0,1},{1,0},{2,3},{3,2},{4,5},{5,4},{6,7},{7,6},{8,9},{9,8},{10,11... | collective-permute-start | bytes 2752520 | tf_op jit(solution)/shard_map/ppermute | solution.py:105
  56.7 121.7 %collective-permute-start.4 = (bf16[2,64,7168]{2,1,0:T(8,128)(2,1)}, bf16[2,64,7168]{2,1,0:T(8,128)(2,1)S(1)}, u32[]{:S(2)}, u32[]{:S(2)}) collective-permute-start(bf16[2,64,7168]{2,1,0:T(8,128)(2,1)} %get-tuple-element.57.own_ref), channel_id=1, source_target_pairs={{0,1},{1,0},{2,3},{3,2},{4,5},{5,4},{6,7},{7,6},{8,9},{9,8},{10,11... | collective-permute-start | bytes 5505032 | tf_op jit(solution)/shard_map/ppermute | solution.py:105
  76.5 55.2 %collective-permute-start.24 = (bf16[1,64,7168]{2,1,0:T(8,128)(2,1)S(1)}, bf16[1,64,7168]{2,1,0:T(8,128)(2,1)S(1)}, u32[]{:S(2)}, u32[]{:S(2)}) collective-permute-start(bf16[1,64,7168]{2,1,0:T(8,128)(2,1)S(1)} %collective-permute-done.23.own_ref), channel_id=1, source_target_pairs={{0,1},{1,0},{2,3},{3,2},{4,5},{5,4},{6,7},{7,6},{8,9},{9,8},{10,11... | collective-permute-start | bytes 2752520 | tf_op jit(solution)/shard_map/ppermute | solution.py:105
  96.0 50.1 %collective-permute-start.38 = (bf16[1,64,7168]{2,1,0:T(8,128)(2,1)}, bf16[1,64,7168]{2,1,0:T(8,128)(2,1)S(1)}, u32[]{:S(2)}, u32[]{:S(2)}) collective-permute-start(bf16[1,64,7168]{2,1,0:T(8,128)(2,1)} %collective-permute-done.37.own_ref), channel_id=1, source_target_pairs={{0,1},{1,0},{2,3},{3,2},{4,5},{5,4},{6,7},{7,6},{8,9},{9,8},{10,11... | collective-permute-start | bytes 2752520 | tf_op jit(solution)/shard_map/ppermute | solution.py:105
  96.0 67.1 %collective-permute-start.1 = (bf16[1,64,7168]{2,1,0:T(8,128)(2,1)}, bf16[1,64,7168]{2,1,0:T(8,128)(2,1)S(1)}, u32[]{:S(2)}, u32[]{:S(2)}) collective-permute-start(bf16[1,64,7168]{2,1,0:T(8,128)(2,1)} %collective-permute-done.own_ref), channel_id=1, source_target_pairs={{0,1},{1,0},{2,3},{3,2},{4,5},{5,4},{6,7},{7,6},{8,9},{9,8},{10,11... | collective-permute-start | bytes 2752520 | tf_op jit(solution)/shard_map/ppermute | solution.py:105
  115.0 89.3 %collective-permute-start.32 = (f32[128,64]{1,0:T(8,128)S(1)}, f32[128,64]{1,0:T(8,128)S(1)}, u32[]{:S(2)}, u32[]{:S(2)}) collective-permute-start(f32[128,64]{1,0:T(8,128)S(1)} %get-tuple-element.48), channel_id=1, source_target_pairs={{0,4},{4,0},{8,12},{12,8},{1,5},{5,1},{9,13},{13,9},{2,6},{6,2},{1... | collective-permute-start | bytes 98312 | tf_op jit(solution)/shard_map/ppermute | solution.py:111
  131.7 64.1 %collective-permute-start.18 = (f32[64,64]{1,0:T(8,128)S(1)}, f32[64,64]{1,0:T(8,128)S(1)}, u32[]{:S(2)}, u32[]{:S(2)}) collective-permute-start(f32[64,64]{1,0:T(8,128)S(1)} %get-tuple-element.40), channel_id=1, source_target_pairs={{0,4},{4,0},{8,12},{12,8},{1,5},{5,1},{9,13},{13,9},{2,6},{6,2},{1... | collective-permute-start | bytes 49160 | tf_op jit(solution)/shard_map/ppermute | solution.py:111
  146.1 51.2 %collective-permute-start.30 = (f32[64,64]{1,0:T(8,128)S(1)}, f32[64,64]{1,0:T(8,128)S(1)}, u32[]{:S(2)}, u32[]{:S(2)}) collective-permute-start(f32[64,64]{1,0:T(8,128)S(1)} %get-tuple-element.46), channel_id=1, source_target_pairs={{0,4},{4,0},{8,12},{12,8},{1,5},{5,1},{9,13},{13,9},{2,6},{6,2},{1... | collective-permute-start | bytes 49160 | tf_op jit(solution)/shard_map/ppermute | solution.py:111
  163.1 39.4 %collective-permute-start.41 = (f32[64,64]{1,0:T(8,128)S(1)}, f32[64,64]{1,0:T(8,128)S(1)}, u32[]{:S(2)}, u32[]{:S(2)}) collective-permute-start(f32[64,64]{1,0:T(8,128)S(1)} %get-tuple-element.52), channel_id=1, source_target_pairs={{0,4},{4,0},{8,12},{12,8},{1,5},{5,1},{9,13},{13,9},{2,6},{6,2},{1... | collective-permute-start | bytes 49160 | tf_op jit(solution)/shard_map/ppermute | solution.py:111
  178.4 27.8 %collective-permute-start.7 = (f32[64,64]{1,0:T(8,128)S(1)}, f32[64,64]{1,0:T(8,128)S(1)}, u32[]{:S(2)}, u32[]{:S(2)}) collective-permute-start(f32[64,64]{1,0:T(8,128)S(1)} %get-tuple-element.34), channel_id=1, source_target_pairs={{0,4},{4,0},{8,12},{12,8},{1,5},{5,1},{9,13},{13,9},{2,6},{6,2},{1... | collective-permute-start | bytes 49160 | tf_op jit(solution)/shard_map/ppermute | solution.py:111
  197.3 23.4 %collective-permute-start.19 = (f32[1,64,64]{2,1,0:T(8,128)S(1)}, f32[1,64,64]{2,1,0:T(8,128)}, u32[]{:S(2)}, u32[]{:S(2)}) collective-permute-start(f32[1,64,64]{2,1,0:T(8,128)S(1)} %add_bitcast_fusion.2), channel_id=1, source_target_pairs={{0,8},{4,12},{10,2},{14,6},{1,9},{5,13},{11,3},{15,7},{16,24},{20,... | collective-permute-start | bytes 49160 | tf_op jit(solution)/shard_map/ppermute | solution.py:120
  202.5 18.3 %collective-permute-start.31 = (f32[1,64,64]{2,1,0:T(8,128)S(1)}, f32[1,64,64]{2,1,0:T(8,128)}, u32[]{:S(2)}, u32[]{:S(2)}) collective-permute-start(f32[1,64,64]{2,1,0:T(8,128)S(1)} %add_bitcast_fusion.1), channel_id=1, source_target_pairs={{0,8},{4,12},{10,2},{14,6},{1,9},{5,13},{11,3},{15,7},{16,24},{20,... | collective-permute-start | bytes 49160 | tf_op jit(solution)/shard_map/ppermute | solution.py:120
  204.4 16.4 %collective-permute-start.42 = (f32[1,64,64]{2,1,0:T(8,128)S(1)}, f32[1,64,64]{2,1,0:T(8,128)}, u32[]{:S(2)}, u32[]{:S(2)}) collective-permute-start(f32[1,64,64]{2,1,0:T(8,128)S(1)} %add_bitcast_fusion), channel_id=1, source_target_pairs={{0,8},{4,12},{10,2},{14,6},{1,9},{5,13},{11,3},{15,7},{16,24},{20,... | collective-permute-start | bytes 49160 | tf_op jit(solution)/shard_map/ppermute | solution.py:120
  207.6 13.2 %collective-permute-start.8 = (f32[1,64,64]{2,1,0:T(8,128)S(1)}, f32[1,64,64]{2,1,0:T(8,128)}, u32[]{:S(2)}, u32[]{:S(2)}) collective-permute-start(f32[1,64,64]{2,1,0:T(8,128)S(1)} %add_bitcast_fusion.3), channel_id=1, source_target_pairs={{0,8},{4,12},{10,2},{14,6},{1,9},{5,13},{11,3},{15,7},{16,24},{20,... | collective-permute-start | bytes 49160 | tf_op jit(solution)/shard_map/ppermute | solution.py:120
  223.7 64.7 %collective-permute-start.5 = (bf16[128,2048]{1,0:T(8,128)(2,1)}, bf16[128,2048]{1,0:T(8,128)(2,1)S(1)}, u32[]{:S(2)}, u32[]{:S(2)}) collective-permute-start(bf16[128,2048]{1,0:T(8,128)(2,1)} %copy-done.10), channel_id=1, source_target_pairs={{0,4},{4,0},{8,12},{12,8},{1,5},{5,1},{9,13},{13,9},{2,6},{6,2},{1... | collective-permute-start | bytes 1572872 | tf_op jit(solution)/shard_map/ppermute | solution.py:111
  225.3 36.0 %collective-permute-start.2 = (bf16[64,2048]{1,0:T(8,128)(2,1)S(1)}, bf16[64,2048]{1,0:T(8,128)(2,1)S(1)}, u32[]{:S(2)}, u32[]{:S(2)}) collective-permute-start(bf16[64,2048]{1,0:T(8,128)(2,1)S(1)} %copy-done.18), channel_id=1, source_target_pairs={{0,4},{4,0},{8,12},{12,8},{1,5},{5,1},{9,13},{13,9},{2,6},{6,2},{1... | collective-permute-start | bytes 786440 | tf_op jit(solution)/shard_map/ppermute | solution.py:111
  236.1 30.8 %collective-permute-start.16 = (bf16[64,2048]{1,0:T(8,128)(2,1)S(1)}, bf16[64,2048]{1,0:T(8,128)(2,1)S(1)}, u32[]{:S(2)}, u32[]{:S(2)}) collective-permute-start(bf16[64,2048]{1,0:T(8,128)(2,1)S(1)} %copy-done.14), channel_id=1, source_target_pairs={{0,4},{4,0},{8,12},{12,8},{1,5},{5,1},{9,13},{13,9},{2,6},{6,2},{1... | collective-permute-start | bytes 786440 | tf_op jit(solution)/shard_map/ppermute | solution.py:111
  237.6 34.9 %collective-permute-start.25 = (bf16[64,2048]{1,0:T(8,128)(2,1)S(1)}, bf16[64,2048]{1,0:T(8,128)(2,1)S(1)}, u32[]{:S(2)}, u32[]{:S(2)}) collective-permute-start(bf16[64,2048]{1,0:T(8,128)(2,1)S(1)} %copy-done.16), channel_id=1, source_target_pairs={{0,4},{4,0},{8,12},{12,8},{1,5},{5,1},{9,13},{13,9},{2,6},{6,2},{1... | collective-permute-start | bytes 786440 | tf_op jit(solution)/shard_map/ppermute | solution.py:111
  238.6 53.3 %collective-permute-start.28 = (bf16[128,2048]{1,0:T(8,128)(2,1)}, bf16[128,2048]{1,0:T(8,128)(2,1)S(1)}, u32[]{:S(2)}, u32[]{:S(2)}) collective-permute-start(bf16[128,2048]{1,0:T(8,128)(2,1)} %get-tuple-element.44), channel_id=1, source_target_pairs={{0,4},{4,0},{8,12},{12,8},{1,5},{5,1},{9,13},{13,9},{2,6},{6,2},{1... | collective-permute-start | bytes 1572872 | tf_op jit(solution)/shard_map/ppermute | solution.py:111
  261.3 32.1 %collective-permute-start.39 = (bf16[64,2048]{1,0:T(8,128)(2,1)S(1)}, bf16[64,2048]{1,0:T(8,128)(2,1)S(1)}, u32[]{:S(2)}, u32[]{:S(2)}) collective-permute-start(bf16[64,2048]{1,0:T(8,128)(2,1)S(1)} %copy-done.12), channel_id=1, source_target_pairs={{0,4},{4,0},{8,12},{12,8},{1,5},{5,1},{9,13},{13,9},{2,6},{6,2},{1... | collective-permute-start | bytes 786440 | tf_op jit(solution)/shard_map/ppermute | solution.py:111
  266.9 73.8 %collective-permute-start.3 = (bf16[1,64,2048]{2,1,0:T(8,128)(2,1)}, bf16[1,64,2048]{2,1,0:T(8,128)(2,1)}, u32[]{:S(2)}, u32[]{:S(2)}) collective-permute-start(bf16[1,64,2048]{2,1,0:T(8,128)(2,1)} %fusion.31), channel_id=1, source_target_pairs={{0,8},{4,12},{10,2},{14,6},{1,9},{5,13},{11,3},{15,7},{16,24},{20,... | collective-permute-start | bytes 786440 | tf_op jit(solution)/shard_map/ppermute | solution.py:120
  272.5 70.3 %collective-permute-start.17 = (bf16[1,64,2048]{2,1,0:T(8,128)(2,1)}, bf16[1,64,2048]{2,1,0:T(8,128)(2,1)}, u32[]{:S(2)}, u32[]{:S(2)}) collective-permute-start(bf16[1,64,2048]{2,1,0:T(8,128)(2,1)} %fusion.30), channel_id=1, source_target_pairs={{0,8},{4,12},{10,2},{14,6},{1,9},{5,13},{11,3},{15,7},{16,24},{20,... | collective-permute-start | bytes 786440 | tf_op jit(solution)/shard_map/ppermute | solution.py:120
  288.4 55.9 %collective-permute-start.26 = (bf16[1,64,2048]{2,1,0:T(8,128)(2,1)}, bf16[1,64,2048]{2,1,0:T(8,128)(2,1)}, u32[]{:S(2)}, u32[]{:S(2)}) collective-permute-start(bf16[1,64,2048]{2,1,0:T(8,128)(2,1)} %fusion.29), channel_id=1, source_target_pairs={{0,8},{4,12},{10,2},{14,6},{1,9},{5,13},{11,3},{15,7},{16,24},{20,... | collective-permute-start | bytes 786440 | tf_op jit(solution)/shard_map/ppermute | solution.py:120
  291.9 38.7 %collective-permute-start.6 = (bf16[2,64,2048]{2,1,0:T(8,128)(2,1)S(1)}, bf16[2,64,2048]{2,1,0:T(8,128)(2,1)S(1)}, u32[]{:S(2)}, u32[]{:S(2)}) collective-permute-start(bf16[2,64,2048]{2,1,0:T(8,128)(2,1)S(1)} %convert_element_type.171), channel_id=1, source_target_pairs={{8,0},{12,4},{2,10},{6,14},{9,1},{13,5},{3,11},{7,15},{24,16},{28,... | collective-permute-start | bytes 1572872 | tf_op jit(solution)/shard_map/ppermute | solution.py:120
  293.4 46.2 %collective-permute-start.29 = (bf16[2,64,2048]{2,1,0:T(8,128)(2,1)S(1)}, bf16[2,64,2048]{2,1,0:T(8,128)(2,1)S(1)}, u32[]{:S(2)}, u32[]{:S(2)}) collective-permute-start(bf16[2,64,2048]{2,1,0:T(8,128)(2,1)S(1)} %convert_element_type.192), channel_id=1, source_target_pairs={{8,0},{12,4},{2,10},{6,14},{9,1},{13,5},{3,11},{7,15},{24,16},{28,... | collective-permute-start | bytes 1572872 | tf_op jit(solution)/shard_map/ppermute | solution.py:120
  330.6 15.1 %collective-permute-start.40 = (bf16[1,64,2048]{2,1,0:T(8,128)(2,1)}, bf16[1,64,2048]{2,1,0:T(8,128)(2,1)}, u32[]{:S(2)}, u32[]{:S(2)}) collective-permute-start(bf16[1,64,2048]{2,1,0:T(8,128)(2,1)} %fusion.28), channel_id=1, source_target_pairs={{0,8},{4,12},{10,2},{14,6},{1,9},{5,13},{11,3},{15,7},{16,24},{20,... | collective-permute-start | bytes 786440 | tf_op jit(solution)/shard_map/ppermute | solution.py:120
  (47 other events, 666.5 us)
Sparse Core Ops, SparseCore 0:
  223.9 41.8 all-gather.1
where the time goes:
time: 356 us; the launch traced here: 355 us
  waiting for transfers between devices  152 us (43%)
  Pallas kernels  92.2 us (26%)
  starting transfers between devices  71.9 us (20%)
  between operations  14.1 us (4%)
  local copies, waits for them, and re-layouts  9.91 us (3%)
  other arithmetic  9.17 us (3%)
  matrix products  6.29 us (2%)
    pallas_call x6, Pallas kernels, partial_products(): pl.pallas_call(functools.partial(matmul_body, first, steps), grid=(width...  92.2 us
    ppermute x4, waiting for transfers between devices, from_rep(): lax.ppermute(value, 'rep', [((i + shift) % n_rep, i) for i in range(n_rep)])  76.1 us
    ppermute x12, waiting for transfers between devices, to_group(): return lax.ppermute(value, ('tp', 'rep'), pairs)  46.6 us
    ppermute x12, starting transfers between devices, to_group(): return lax.ppermute(value, ('tp', 'rep'), pairs)  43.2 us
    ppermute x12, waiting for transfers between devices, swap_tensor(): return lax.ppermute(value, 'tp', [(i, i ^ bit) for i in range(n_tensor)])  27.4 us
    ppermute x12, starting transfers between devices, swap_tensor(): return lax.ppermute(value, 'tp', [(i, i ^ bit) for i in range(n_tensor)])  12.4 us
    ppermute x12, starting transfers between devices, per_device(): lax.ppermute(masked, ('rep', 'sub'), [(i, (i + turn) % n_owners) for i in...  10.8 us
  transfers between devices with their start and end apart: 47, of which 12 were waited for; matrix products, arithmetic and copies ran while one was open for 4% of the time, Pallas kernels for 26%

commit v1 on v0

v1 whole, which is shorter than its diff:
```python
import functools

import jax
import jax.numpy as jnp
from jax import lax
from jax.experimental import pallas as pl
from jax.experimental.pallas import tpu as pltpu
from jax.sharding import PartitionSpec as P

ADAPTER_SCALE = 0.5
BLOCK_N = 256
VMEM_BYTES = 6 * 1024 * 1024


def matmul_body(first, steps, pos_ref, own_ref, sib_ref, w_ref, a_ref,
                send_ref, keep_ref, rank_send_ref, rank_keep_ref, x_ref, sems):
    rows, width = send_ref.shape
    depth = w_ref.shape[0]
    slots, _, rank = a_ref.shape
    block_n = min(BLOCK_N, width)
    own_at = pos_ref[0]
    own_copy = pltpu.make_async_copy(own_ref.at[pl.ds(first, steps)], x_ref.at[own_at], sems.at[0])
    sib_copy = pltpu.make_async_copy(sib_ref.at[pl.ds(first, steps)], x_ref.at[1 - own_at], sems.at[1])
    own_copy.start()
    sib_copy.start()
    own_copy.wait()
    sib_copy.wait()
    for slot in range(slots):
        x = x_ref[...].reshape(2 * rows, depth)
        part = jnp.dot(x, a_ref[slot], preferred_element_type=jnp.float32)
        rank_send_ref[:, slot * rank:(slot + 1) * rank] = part[:rows]
        rank_keep_ref[:, slot * rank:(slot + 1) * rank] = part[rows:]

    @pl.loop(0, width // block_n)
    def _(place):
        columns = pl.ds(pl.multiple_of(place * block_n, block_n), block_n)
        x = x_ref[...].reshape(2 * rows, depth)
        term = jnp.dot(x, w_ref[:, columns], preferred_element_type=jnp.float32)
        send_ref[:, columns] = term[:rows].astype(send_ref.dtype)
        keep_ref[:, columns] = term[rows:]


def load_body(weight_ref, out_ref, sem):
    copy = pltpu.make_async_copy(weight_ref, out_ref, sem)
    copy.start()
    copy.wait()


def load_weight(weight):
    return pl.pallas_call(
        load_body,
        in_specs=[pl.BlockSpec(memory_space=pl.ANY)],
        out_specs=pl.BlockSpec(memory_space=pltpu.VMEM),
        out_shape=pltpu.VMEM(weight.shape, weight.dtype),
        scratch_shapes=[pltpu.SemaphoreType.DMA],
        compiler_params=pltpu.CompilerParams(vmem_limit_bytes=1024 * 1024),
        name="load_weight",
    )(weight)


def partial_products(pos, own, sib, first, steps, weight, down_a):
    _, per_block, depth = own.shape
    width = weight.shape[1]
    slots, _, rank = down_a.shape
    rows = steps * per_block
    any_spec = pl.BlockSpec(memory_space=pl.ANY)
    vmem_spec = pl.BlockSpec(memory_space=pltpu.VMEM)
    return pl.pallas_call(
        functools.partial(matmul_body, first, steps),
        in_specs=[pl.BlockSpec(memory_space=pltpu.SMEM), any_spec, any_spec, vmem_spec, vmem_spec],
        out_specs=[vmem_spec] * 4,
        out_shape=[
            jax.ShapeDtypeStruct((rows, width), jnp.bfloat16),
            jax.ShapeDtypeStruct((rows, width), jnp.float32),
            jax.ShapeDtypeStruct((rows, slots * rank), jnp.float32),
            jax.ShapeDtypeStruct((rows, slots * rank), jnp.float32),
        ],
        scratch_shapes=[
            pltpu.VMEM((2, steps, per_block, depth), jnp.bfloat16),
            pltpu.SemaphoreType.DMA((2,)),
        ],
        compiler_params=pltpu.CompilerParams(vmem_limit_bytes=VMEM_BYTES),
        cost_estimate=pl.CostEstimate(flops=0, bytes_accessed=0, transcendentals=0),
        name="partial_products",
    )(pos, own, sib, weight, down_a)


def per_device(hidden, base_weight, down_a, up_b, adapter_ids, owner_map):
    step_count, per_block, _ = hidden.shape
    n_tensor = lax.axis_size("tp")
    n_rep = lax.axis_size("rep")
    n_sub = lax.axis_size("sub")
    n_owners = n_rep * n_sub
    tensor_index = lax.axis_index("tp")
    rep_index = lax.axis_index("rep")
    sub_index = lax.axis_index("sub")
    owner_index = lax.axis_index(("rep", "sub"))
    requests = per_block * n_owners
    rows_mine = requests // n_tensor
    group = n_tensor // n_rep
    group_index = tensor_index // group
    owned_slots, _, rank_size = down_a.shape
    slot_count = owned_slots * n_owners
    width = base_weight.shape[1]

    def swap_cores(value):
        return lax.ppermute(value, "sub", [(i, i ^ 1) for i in range(n_sub)])

    def from_rep(value, shift):
        return lax.ppermute(value, "rep", [((i + shift) % n_rep, i) for i in range(n_rep)])

    def swap_tensor(value, bit):
        return lax.ppermute(value, "tp", [(i, i ^ bit) for i in range(n_tensor)])

    def to_group(value, shift, hop):
        pairs = []
        for rep in range(n_rep):
            target = (rep + shift) % n_rep
            source = (target + hop) % n_rep
            for low in range(group):
                pairs.append(((source * group + low) * n_rep + rep, (target * group + low) * n_rep + rep))
        return lax.ppermute(value, ("tp", "rep"), pairs)

    keeps = (tensor_index // (group // 2)) % 2
    pos = (sub_index == keeps).astype(jnp.int32).reshape(1)

    def after(value, *done):
        return lax.optimization_barrier((value, *done))[0]

    half = step_count // 2
    siblings = swap_cores(hidden)

    remote = {}
    for shift in range(1, n_rep):
        for step in range(step_count):
            piece = hidden[step:step + 1]
            if step >= 2:
                piece = after(piece, remote[step - 2, shift])
            remote[step, shift] = from_rep(piece, shift)

    panels, bit = up_b, 1
    while bit < n_tensor:
        panels = jnp.concatenate([panels, swap_tensor(panels, bit)], axis=0)
        bit *= 2
    panels = panels.reshape(slot_count * rank_size, width)
    panel_slots = (
        (tensor_index ^ lax.broadcasted_iota(jnp.int32, (n_tensor, up_b.shape[0]), 0)) * up_b.shape[0]
        + lax.broadcasted_iota(jnp.int32, (n_tensor, up_b.shape[0]), 1)
    ).reshape(slot_count)

    my_ids = lax.dynamic_slice_in_dim(adapter_ids, tensor_index * rows_mine, rows_mine)
    iota = lax.broadcasted_iota(jnp.int32, (rows_mine, slot_count), 1)
    my_slot = jnp.sum((my_ids == iota).astype(jnp.int32) * owner_map[None, :], axis=1)
    panel_hot = my_slot[:, None] == panel_slots[None, :]
    owned_hot = my_slot[:, None] == (
        owner_index * owned_slots + lax.broadcasted_iota(jnp.int32, (rows_mine, owned_slots), 1)
    )

    weight = pltpu.with_memory_space_constraint(load_weight(base_weight), pltpu.VMEM)
    factor = pltpu.with_memory_space_constraint(down_a, pltpu.VMEM)

    def multiply(own, sib, first, steps):
        return partial_products(pos, own, sib, first, steps, weight, factor)

    def halve(send, keep, steps, kind):
        columns = keep.shape[1]
        total = keep + swap_tensor(send, group // 2).astype(jnp.float32)
        extent, bit = per_block, group // 4
        while bit:
            extent //= 2
            halves = total.reshape(steps, 2, extent, columns)
            mine = (tensor_index // bit) % 2
            kept = lax.dynamic_index_in_dim(halves, mine, 1, keepdims=False)
            sent = lax.dynamic_index_in_dim(halves, 1 - mine, 1, keepdims=False)
            total = kept + swap_tensor(sent.astype(kind), bit).astype(jnp.float32)
            bit //= 2
        total = total.reshape(steps, rows_mine, columns)
        return total, total.astype(kind)

    def collect(total, rounded, shift):
        for hop in range(1, n_rep):
            total = total + to_group(rounded, shift, hop).astype(jnp.float32)
        return total

    def choose(local, others):
        value = local
        for shift, other in others:
            value = jnp.where(group_index == (rep_index + shift) % n_rep, other, value)
        return value

    def exchange(ranks):
        steps = ranks.shape[0]
        finished = ranks.astype(jnp.bfloat16).reshape(steps, rows_mine, owned_slots, rank_size)
        masked = jnp.sum(
            jnp.where(owned_hot[None, :, :, None], finished, 0), axis=2, dtype=jnp.float32
        ).astype(jnp.bfloat16)
        chosen = masked
        for turn in range(1, n_owners):
            chosen = chosen + lax.ppermute(
                masked, ("rep", "sub"), [(i, (i + turn) % n_owners) for i in range(n_owners)]
            )
        spread = jnp.where(panel_hot[None, :, :, None], chosen[:, :, None, :], 0)
        return spread.reshape(steps, rows_mine, slot_count * rank_size)

    def finish(sums, spread):
        lifted = jnp.dot(spread, panels, preferred_element_type=jnp.float32).astype(jnp.bfloat16)
        return (sums + ADAPTER_SCALE * lifted.astype(jnp.float32)).astype(jnp.bfloat16)

    local_parts, local_halved, local_sums = {}, {}, {}
    remote_parts, remote_halved, remote_sums = {}, {}, {}

    def local_rows(index, *done):
        first = index * half
        send, keep, rank_send, rank_keep = multiply(
            hidden, after(siblings, *done), first, half
        )
        local_parts[index] = (rank_send, rank_keep)
        local_halved[index] = halve(send, keep, half, jnp.bfloat16)
        local_sums[index] = collect(*local_halved[index], 0)
        return rank_keep

    def remote_rows(index, *done):
        for shift in range(1, n_rep):
            own = remote[index, shift]
            sib = after(swap_cores(own), *done)
            send, keep, rank_send, rank_keep = multiply(own, sib, 0, 1)
            remote_parts[index, shift] = (rank_send, rank_keep)
            remote_halved[index, shift] = halve(send, keep, 1, jnp.bfloat16)
            remote_sums[index, shift] = collect(*remote_halved[index, shift], shift)
            done = (rank_keep,)
        return done[0]

    def arrived(index):
        return tuple(remote[index, shift] for shift in range(1, n_rep))

    def halved(index):
        return tuple(remote_halved[index, shift][1] for shift in range(1, n_rep))

    token = local_rows(0, *arrived(0))
    token = remote_rows(0, token)
    token = local_rows(1, token, local_halved[0][1], *arrived(1))
    token = remote_rows(1, token, *halved(0))
    token = remote_rows(2, token, local_halved[1][1], *halved(1))
    token = remote_rows(3, token, *halved(2))

    local_ranks = collect(*halve(
        jnp.concatenate([local_parts[0][0], local_parts[1][0]]),
        jnp.concatenate([local_parts[0][1], local_parts[1][1]]),
        step_count, jnp.float32), 0)
    outputs = []
    for begin, end in ((0, step_count - 1), (step_count - 1, step_count)):
        others = []
        for shift in range(1, n_rep):
            parts = [remote_parts[step, shift] for step in range(begin, end)]
            rank = collect(*halve(
                jnp.concatenate([part[0] for part in parts]),
                jnp.concatenate([part[1] for part in parts]),
                end - begin, jnp.float32), shift)
            others.append((shift, rank))
        spread = exchange(choose(local_ranks[begin:end], others))
        for step in range(begin, end):
            sums = choose(
                local_sums[step // half][step % half],
                [(shift, remote_sums[step, shift][0]) for shift in range(1, n_rep)],
            )
            outputs.append(finish(sums, spread[step - begin]))
    return jnp.stack(outputs, axis=0)


def solution(mesh):
    return jax.shard_map(
        per_device,
        mesh=mesh,
        in_specs=(
            P(None, ("groups", "rep", "sub"), "tp"),
            P("tp", ("rep", "sub")),
            P(("rep", "sub"), "tp", None),
            P("tp", None, ("rep", "sub")),
            P("groups", None),
            P(),
        ),
        out_specs=P(None, ("groups", "tp"), ("rep", "sub")),
        check_vma=False,
    )
```

time: 356 us -> 297 us (0.83)
  the two profiles are of different devices: /device:TPU:0 before, /device:TPU:6 now
where the time goes in v1:
time: 297 us; the launch traced here: 296 us
  waiting for transfers between devices  96.5 us (32%)
  Pallas kernels  64.6 us (22%)
  local copies, waits for them, and re-layouts  61.1 us (21%)
  starting transfers between devices  55.5 us (19%)
  other arithmetic  11.3 us (4%)
  matrix products  6.44 us (2%)
    unnamed x65, local copies, waits for them, and re-layouts  56.3 us
    pallas_call x6, Pallas kernels, partial_products(): pl.pallas_call(functools.partial(matmul_body, first, steps), in_specs=[pl...  55.1 us
    ppermute x11, waiting for transfers between devices, swap_tensor(): return lax.ppermute(value, 'tp', [(i, i ^ bit) for i in range(n_tensor)])  46.9 us
    ppermute x9, starting transfers between devices, to_group(): return lax.ppermute(value, ('tp', 'rep'), pairs)  27.9 us
    ppermute x9, waiting for transfers between devices, to_group(): return lax.ppermute(value, ('tp', 'rep'), pairs)  27.2 us
    ppermute x4, waiting for transfers between devices, from_rep(): lax.ppermute(value, 'rep', [((i + shift) % n_rep, i) for i in range(n_rep)])  22.3 us
    ppermute x11, starting transfers between devices, swap_tensor(): return lax.ppermute(value, 'tp', [(i, i ^ bit) for i in range(n_tensor)])  17 us
    pallas_call x1, Pallas kernels, load_weight(): pl.pallas_call(load_body, in_specs=[pl.BlockSpec(memory_space=pl.ANY)], o...  9.44 us
  transfers between devices with their start and end apart: 35, of which 11 were waited for; matrix products, arithmetic and copies ran while one was open for 8% of the time, Pallas kernels for 22%

profile of v1, /device:TPU:6, one launch (start us, length us, event | category | flops | bytes accessed | tf_op | source)
XLA Modules:
  0.0 296.1 jit_solution(9716640440933289105)
XLA Ops:
  0.0 3.6 %fusion.42 = (bf16[1,64,7168]{2,1,0:T(8,128)(2,1)}, bf16[1,64,7168]{2,1,0:T(8,128)(2,1)}, bf16[1,64,7168]{2,1,0:T(8,128)(2,1)S(1)}, bf16[1,64,7168]{2,1,0:T(8,128)(2,1)}) fusion(bf16[4,64,7168]{2,1,0:T(8,128)(2,1)} %own_ref.3), kind=kLoop, calls=%fused_computation.83 | loop fusion | bytes 7340032 | tf_op jit(solution)/shard_map/slice | solution.py:136
  4.1 22.3 %collective-permute-done.own_ref = bf16[1,64,7168]{2,1,0:T(8,128)(2,1)} collective-permute-done((bf16[1,64,7168]{2,1,0:T(8,128)(2,1)S(1)}, bf16[1,64,7168]{2,1,0:T(8,128)(2,1)}, u32[]{:S(2)}, u32[]{:S(2)}) %collective-permute-start) | collective-permute-done | bytes 917536 | tf_op jit(solution)/shard_map/ppermute | solution.py:110
  30.5 9.4 %load_weight.1.w_ref = bf16[7168,2048]{1,0:T(8,128)(2,1)S(1)} custom-call(bf16[7168,2048]{1,0:T(8,128)(2,1)} %weight_ref.1), custom_call_target="tpu_custom_call" | custom-call | tf_op jit(solution)/shard_map/load_weight/pallas_call | solution.py:50
  39.9 9.7 %copy-done.2 = bf16[7168,2048]{1,0:T(8,128)(2,1)} copy-done((bf16[7168,2048]{1,0:T(8,128)(2,1)}, bf16[7168,2048]{1,0:T(8,128)(2,1)S(1)}, u32[]{:S(2)}) %copy-start.2) | copy-done | bytes 29360152
  50.6 9.3 %copy-done.3 = bf16[7168,2048]{1,0:T(8,128)(2,1)S(1)} copy-done((bf16[7168,2048]{1,0:T(8,128)(2,1)S(1)}, bf16[7168,2048]{1,0:T(8,128)(2,1)}, u32[]{:S(2)}) %copy-start.3) | copy-done | bytes 29360152
  60.0 2.0 copy-done.7
  62.0 12.0 %partial_products.6 = (bf16[128,2048]{1,0:T(8,128)(2,1)S(1)}, f32[128,2048]{1,0:T(8,128)S(1)}, f32[128,64]{1,0:T(8,128)S(1)}, f32[128,64]{1,0:T(8,128)S(1)}) custom-call(s32[1]{0:T(128)} %bitcast.pos_ref, bf16[4,64,7168]{2,1,0:T(8,128)(2,1)S(1)} %copy-done.7, bf16[4,64,7168]{2,1,0:T(8,128)(2,1)} %collective-permute-done.2.sib_ref, ...), custom_call_target="tpu_custom_call" | custom-call | tf_op jit(solution)/shard_map/partial_products/pallas_call | solution.py:68
  74.8 8.8 %partial_products.7 = (bf16[64,2048]{1,0:T(8,128)(2,1)}, f32[64,2048]{1,0:T(8,128)S(1)}, f32[64,64]{1,0:T(8,128)S(1)}, f32[64,64]{1,0:T(8,128)S(1)}) custom-call(s32[1]{0:T(128)} %bitcast.pos_ref, bf16[1,64,7168]{2,1,0:T(8,128)(2,1)} %collective-permute-done.own_ref, bf16[1,64,7168]{2,1,0:T(8,128)(2,1)} %collective-permute-done.1.sib_ref, ...), custom_call_target="tpu_custom_call" | custom-call | tf_op jit(solution)/shard_map/partial_products/pallas_call | solution.py:68
  88.2 2.7 collective-permute-start.21
  92.3 13.3 %collective-permute-done.3 = bf16[64,2048]{1,0:T(8,128)(2,1)} collective-permute-done((bf16[64,2048]{1,0:T(8,128)(2,1)}, bf16[64,2048]{1,0:T(8,128)(2,1)}, u32[]{:S(2)}, u32[]{:S(2)}) %collective-permute-start.3) | collective-permute-done | bytes 262176 | tf_op jit(solution)/shard_map/ppermute | solution.py:113
  107.3 8.4 %collective-permute-done.5 = bf16[128,2048]{1,0:T(8,128)(2,1)S(1)} collective-permute-done((bf16[128,2048]{1,0:T(8,128)(2,1)}, bf16[128,2048]{1,0:T(8,128)(2,1)S(1)}, u32[]{:S(2)}, u32[]{:S(2)}) %collective-permute-start.5) | collective-permute-done | bytes 524320 | tf_op jit(solution)/shard_map/ppermute | solution.py:113
  115.9 9.3 %copy-done.4 = bf16[7168,2048]{1,0:T(8,128)(2,1)S(1)} copy-done((bf16[7168,2048]{1,0:T(8,128)(2,1)S(1)}, bf16[7168,2048]{1,0:T(8,128)(2,1)}, u32[]{:S(2)}) %copy-start.4) | copy-done | bytes 29360152
  125.3 12.0 %partial_products.8 = (bf16[128,2048]{1,0:T(8,128)(2,1)S(1)}, f32[128,2048]{1,0:T(8,128)S(1)}, f32[128,64]{1,0:T(8,128)S(1)}, f32[128,64]{1,0:T(8,128)S(1)}) custom-call(s32[1]{0:T(128)} %bitcast.pos_ref, bf16[4,64,7168]{2,1,0:T(8,128)(2,1)S(1)} %copy-done.8, bf16[4,64,7168]{2,1,0:T(8,128)(2,1)} %collective-permute-done.2.sib_ref, ...), custom_call_target="tpu_custom_call" | custom-call | tf_op jit(solution)/shard_map/partial_products/pallas_call | solution.py:68
  137.3 8.0 %partial_products.9 = (bf16[64,2048]{1,0:T(8,128)(2,1)S(1)}, f32[64,2048]{1,0:T(8,128)S(1)}, f32[64,64]{1,0:T(8,128)S(1)}, f32[64,64]{1,0:T(8,128)S(1)}) custom-call(s32[1]{0:T(128)} %bitcast.pos_ref, bf16[1,64,7168]{2,1,0:T(8,128)(2,1)} %collective-permute-done.7.own_ref, bf16[1,64,7168]{2,1,0:T(8,128)(2,1)S(1)} %collective-permute-done.8.sib_ref, ...), custom_call_target="tpu_custom_call" | custom-call | tf_op jit(solution)/shard_map/partial_products/pallas_call | solution.py:68
  150.0 3.9 %collective-permute-done.12 = bf16[64,2048]{1,0:T(8,128)(2,1)S(1)} collective-permute-done((bf16[64,2048]{1,0:T(8,128)(2,1)S(1)}, bf16[64,2048]{1,0:T(8,128)(2,1)S(1)}, u32[]{:S(2)}, u32[]{:S(2)}) %collective-permute-start.12) | collective-permute-done | bytes 262176 | tf_op jit(solution)/shard_map/ppermute | solution.py:113
  154.0 2.5 collective-permute-start.6
  157.2 6.7 %collective-permute-done.11 = bf16[128,2048]{1,0:T(8,128)(2,1)S(1)} collective-permute-done((bf16[128,2048]{1,0:T(8,128)(2,1)S(1)}, bf16[128,2048]{1,0:T(8,128)(2,1)S(1)}, u32[]{:S(2)}, u32[]{:S(2)}) %collective-permute-start.11) | collective-permute-done | bytes 524320 | tf_op jit(solution)/shard_map/ppermute | solution.py:113
  165.8 9.4 %copy-done.5 = bf16[7168,2048]{1,0:T(8,128)(2,1)S(1)} copy-done((bf16[7168,2048]{1,0:T(8,128)(2,1)S(1)}, bf16[7168,2048]{1,0:T(8,128)(2,1)}, u32[]{:S(2)}) %copy-start.5) | copy-done | bytes 29360152
  175.1 7.1 %partial_products.10 = (bf16[64,2048]{1,0:T(8,128)(2,1)S(1)}, f32[64,2048]{1,0:T(8,128)S(1)}, f32[64,64]{1,0:T(8,128)S(1)}, f32[64,64]{1,0:T(8,128)S(1)}) custom-call(s32[1]{0:T(128)} %bitcast.pos_ref, bf16[1,64,7168]{2,1,0:T(8,128)(2,1)S(1)} %collective-permute-done.9.own_ref, bf16[1,64,7168]{2,1,0:T(8,128)(2,1)S(1)} %collective-permute-done.10.sib_ref, ...), custom_call_target="tpu_custom_call" | custom-call | tf_op jit(solution)/shard_map/partial_products/pallas_call | solution.py:68
  183.7 10.4 %collective-permute-start.16 = (f32[4,64,64]{2,1,0:T(8,128)S(1)}, f32[4,64,64]{2,1,0:T(8,128)S(1)}, u32[]{:S(2)}, u32[]{:S(2)}) collective-permute-start(f32[4,64,64]{2,1,0:T(8,128)S(1)} %bitcast.108), channel_id=1, source_target_pairs={{8,0},{12,4},{2,10},{6,14},{9,1},{13,5},{3,11},{7,15},{24,16},{28,... | collective-permute-start | bytes 196616 | tf_op jit(solution)/shard_map/ppermute | solution.py:122
  196.9 4.6 %collective-permute-done.14 = f32[3,64,64]{2,1,0:T(8,128)S(1)} collective-permute-done((f32[3,64,64]{2,1,0:T(8,128)S(1)}, f32[3,64,64]{2,1,0:T(8,128)S(1)}, u32[]{:S(2)}, u32[]{:S(2)}) %collective-permute-start.14) | collective-permute-done | bytes 49184 | tf_op jit(solution)/shard_map/ppermute | solution.py:122
  206.7 6.9 %collective-permute-start.25 = (bf16[2,64,2048]{2,1,0:T(8,128)(2,1)}, bf16[2,64,2048]{2,1,0:T(8,128)(2,1)}, u32[]{:S(2)}, u32[]{:S(2)}) collective-permute-start(bf16[2,64,2048]{2,1,0:T(8,128)(2,1)} %convert_element_type.137), channel_id=1, source_target_pairs={{8,0},{12,4},{2,10},{6,14},{9,1},{13,5},{3,11},{7,15},{24,16},{28,... | collective-permute-start | bytes 1572872 | tf_op jit(solution)/shard_map/ppermute | solution.py:122
  215.7 13.5 %collective-permute-done.23 = bf16[64,2048]{1,0:T(8,128)(2,1)S(1)} collective-permute-done((bf16[64,2048]{1,0:T(8,128)(2,1)S(1)}, bf16[64,2048]{1,0:T(8,128)(2,1)S(1)}, u32[]{:S(2)}, u32[]{:S(2)}) %collective-permute-start.23) | collective-permute-done | bytes 262176 | tf_op jit(solution)/shard_map/ppermute | solution.py:113
  230.1 9.4 %copy-done.6 = bf16[7168,2048]{1,0:T(8,128)(2,1)S(1)} copy-done((bf16[7168,2048]{1,0:T(8,128)(2,1)S(1)}, bf16[7168,2048]{1,0:T(8,128)(2,1)}, u32[]{:S(2)}) %copy-start.6) | copy-done | bytes 29360152
  239.4 7.1 %partial_products.11 = (bf16[64,2048]{1,0:T(8,128)(2,1)S(1)}, f32[64,2048]{1,0:T(8,128)S(1)}, f32[64,64]{1,0:T(8,128)S(1)}, f32[64,64]{1,0:T(8,128)S(1)}) custom-call(s32[1]{0:T(128)} %bitcast.pos_ref, bf16[1,64,7168]{2,1,0:T(8,128)(2,1)S(1)} %collective-permute-done.26.own_ref, bf16[1,64,7168]{2,1,0:T(8,128)(2,1)S(1)} %collective-permute-done.27.sib_ref, ...), custom_call_target="tpu_custom_call" | custom-call | tf_op jit(solution)/shard_map/partial_products/pallas_call | solution.py:68
  248.1 2.5 collective-permute-start.30
  254.5 2.5 fusion.29
  257.1 2.1 collective-permute-start.28
  261.2 2.4 collective-permute-start.33
  265.0 2.2 fusion.30
  271.7 18.7 %collective-permute-done.24 = bf16[1,64,2048]{2,1,0:T(8,128)(2,1)S(1)} collective-permute-done((bf16[1,64,2048]{2,1,0:T(8,128)(2,1)}, bf16[1,64,2048]{2,1,0:T(8,128)(2,1)S(1)}, u32[]{:S(2)}, u32[]{:S(2)}) %collective-permute-start.24) | collective-permute-done | bytes 262176 | tf_op jit(solution)/shard_map/ppermute | solution.py:122
  291.8 2.7 collective-permute-done.29
  (149 shorter events, 49.7 us)
Async XLA Ops:
  0.0 50.6 %collective-permute-start.2 = (bf16[4,64,7168]{2,1,0:T(8,128)(2,1)}, bf16[4,64,7168]{2,1,0:T(8,128)(2,1)}, u32[]{:S(2)}, u32[]{:S(2)}) collective-permute-start(bf16[4,64,7168]{2,1,0:T(8,128)(2,1)} %own_ref.3), channel_id=1, source_target_pairs={{0,1},{1,0},{2,3},{3,2},{4,5},{5,4},{6,7},{7,6},{8,9},{9,8},{10,11... | collective-permute-start | bytes 11010056 | tf_op jit(solution)/shard_map/ppermute | solution.py:107
  3.6 22.8 %collective-permute-start = (bf16[1,64,7168]{2,1,0:T(8,128)(2,1)S(1)}, bf16[1,64,7168]{2,1,0:T(8,128)(2,1)}, u32[]{:S(2)}, u32[]{:S(2)}) collective-permute-start(bf16[1,64,7168]{2,1,0:T(8,128)(2,1)S(1)} %get-tuple-element.71), channel_id=1, source_target_pairs={{2,0},{0,2},{3,1},{1,3},{6,4},{4,6},{7,5},{5,7},{10,8},{8,10},{11,... | collective-permute-start | bytes 2752520 | tf_op jit(solution)/shard_map/ppermute | solution.py:110
  26.5 47.6 %collective-permute-start.1 = (bf16[1,64,7168]{2,1,0:T(8,128)(2,1)}, bf16[1,64,7168]{2,1,0:T(8,128)(2,1)}, u32[]{:S(2)}, u32[]{:S(2)}) collective-permute-start(bf16[1,64,7168]{2,1,0:T(8,128)(2,1)} %collective-permute-done.own_ref), channel_id=1, source_target_pairs={{0,1},{1,0},{2,3},{3,2},{4,5},{5,4},{6,7},{7,6},{8,9},{9,8},{10,11... | collective-permute-start | bytes 2752520 | tf_op jit(solution)/shard_map/ppermute | solution.py:107
  26.5 65.9 %collective-permute-start.7 = (bf16[1,64,7168]{2,1,0:T(8,128)(2,1)}, bf16[1,64,7168]{2,1,0:T(8,128)(2,1)}, u32[]{:S(2)}, u32[]{:S(2)}) collective-permute-start(bf16[1,64,7168]{2,1,0:T(8,128)(2,1)} %get-tuple-element.70), channel_id=1, source_target_pairs={{2,0},{0,2},{3,1},{1,3},{6,4},{4,6},{7,5},{5,7},{10,8},{8,10},{11,... | collective-permute-start | bytes 2752520 | tf_op jit(solution)/shard_map/ppermute | solution.py:110
  27.0 60.1 %collective-permute-start.20 = (bf16[1,64,2048]{2,1,0:T(8,128)(2,1)}, bf16[1,64,2048]{2,1,0:T(8,128)(2,1)}, u32[]{:S(2)}, u32[]{:S(2)}) collective-permute-start(bf16[1,64,2048]{2,1,0:T(8,128)(2,1)} %param.9), channel_id=1, source_target_pairs={{0,4},{4,0},{8,12},{12,8},{1,5},{5,1},{9,13},{13,9},{2,6},{6,2},{1... | collective-permute-start | bytes 786440 | tf_op jit(solution)/shard_map/ppermute | solution.py:113
  84.8 20.7 %collective-permute-start.3 = (bf16[64,2048]{1,0:T(8,128)(2,1)}, bf16[64,2048]{1,0:T(8,128)(2,1)}, u32[]{:S(2)}, u32[]{:S(2)}) collective-permute-start(bf16[64,2048]{1,0:T(8,128)(2,1)} %get-tuple-element.41), channel_id=1, source_target_pairs={{0,4},{4,0},{8,12},{12,8},{1,5},{5,1},{9,13},{13,9},{2,6},{6,2},{1... | collective-permute-start | bytes 786440 | tf_op jit(solution)/shard_map/ppermute | solution.py:113
  85.4 30.2 %collective-permute-start.5 = (bf16[128,2048]{1,0:T(8,128)(2,1)}, bf16[128,2048]{1,0:T(8,128)(2,1)S(1)}, u32[]{:S(2)}, u32[]{:S(2)}) collective-permute-start(bf16[128,2048]{1,0:T(8,128)(2,1)} %copy-done.15), channel_id=1, source_target_pairs={{0,4},{4,0},{8,12},{12,8},{1,5},{5,1},{9,13},{13,9},{2,6},{6,2},{1... | collective-permute-start | bytes 1572872 | tf_op jit(solution)/shard_map/ppermute | solution.py:113
  88.2 107.3 %collective-permute-start.21 = (bf16[2,64,2048]{2,1,0:T(8,128)(2,1)S(1)}, bf16[2,64,2048]{2,1,0:T(8,128)(2,1)S(1)}, u32[]{:S(2)}, u32[]{:S(2)}) collective-permute-start(bf16[2,64,2048]{2,1,0:T(8,128)(2,1)S(1)} %pad_maximum_fusion.1), channel_id=1, source_target_pairs={{0,8},{4,12},{8,0},{12,4},{1,9},{5,13},{9,1},{13,5},{2,10},{6,14},... | collective-permute-start | bytes 1572872 | tf_op jit(solution)/shard_map/ppermute | solution.py:113
  90.8 57.2 %collective-permute-start.9 = (bf16[1,64,7168]{2,1,0:T(8,128)(2,1)}, bf16[1,64,7168]{2,1,0:T(8,128)(2,1)S(1)}, u32[]{:S(2)}, u32[]{:S(2)}) collective-permute-start(bf16[1,64,7168]{2,1,0:T(8,128)(2,1)} %get-tuple-element.49), channel_id=1, source_target_pairs={{2,0},{0,2},{3,1},{1,3},{6,4},{4,6},{7,5},{5,7},{10,8},{8,10},{11,... | collective-permute-start | bytes 2752520 | tf_op jit(solution)/shard_map/ppermute | solution.py:110
  92.3 45.0 %collective-permute-start.8 = (bf16[1,64,7168]{2,1,0:T(8,128)(2,1)}, bf16[1,64,7168]{2,1,0:T(8,128)(2,1)S(1)}, u32[]{:S(2)}, u32[]{:S(2)}) collective-permute-start(bf16[1,64,7168]{2,1,0:T(8,128)(2,1)} %collective-permute-done.7.own_ref), channel_id=1, source_target_pairs={{0,1},{1,0},{2,3},{3,2},{4,5},{5,4},{6,7},{7,6},{8,9},{9,8},{10,11... | collective-permute-start | bytes 2752520 | tf_op jit(solution)/shard_map/ppermute | solution.py:107
  145.3 8.6 %collective-permute-start.12 = (bf16[64,2048]{1,0:T(8,128)(2,1)S(1)}, bf16[64,2048]{1,0:T(8,128)(2,1)S(1)}, u32[]{:S(2)}, u32[]{:S(2)}) collective-permute-start(bf16[64,2048]{1,0:T(8,128)(2,1)S(1)} %get-tuple-element.53), channel_id=1, source_target_pairs={{0,4},{4,0},{8,12},{12,8},{1,5},{5,1},{9,13},{13,9},{2,6},{6,2},{1... | collective-permute-start | bytes 786440 | tf_op jit(solution)/shard_map/ppermute | solution.py:113
  146.4 49.1 %collective-permute-start.26 = (bf16[1,64,7168]{2,1,0:T(8,128)(2,1)S(1)}, bf16[1,64,7168]{2,1,0:T(8,128)(2,1)S(1)}, u32[]{:S(2)}, u32[]{:S(2)}) collective-permute-start(bf16[1,64,7168]{2,1,0:T(8,128)(2,1)S(1)} %copy-done.27), channel_id=1, source_target_pairs={{2,0},{0,2},{3,1},{1,3},{6,4},{4,6},{7,5},{5,7},{10,8},{8,10},{11,... | collective-permute-start | bytes 2752520 | tf_op jit(solution)/shard_map/ppermute | solution.py:110
  148.0 17.8 %collective-permute-start.10 = (bf16[1,64,7168]{2,1,0:T(8,128)(2,1)S(1)}, bf16[1,64,7168]{2,1,0:T(8,128)(2,1)S(1)}, u32[]{:S(2)}, u32[]{:S(2)}) collective-permute-start(bf16[1,64,7168]{2,1,0:T(8,128)(2,1)S(1)} %collective-permute-done.9.own_ref), channel_id=1, source_target_pairs={{0,1},{1,0},{2,3},{3,2},{4,5},{5,4},{6,7},{7,6},{8,9},{9,8},{10,11... | collective-permute-start | bytes 2752520 | tf_op jit(solution)/shard_map/ppermute | solution.py:107
  148.0 15.9 %collective-permute-start.11 = (bf16[128,2048]{1,0:T(8,128)(2,1)S(1)}, bf16[128,2048]{1,0:T(8,128)(2,1)S(1)}, u32[]{:S(2)}, u32[]{:S(2)}) collective-permute-start(bf16[128,2048]{1,0:T(8,128)(2,1)S(1)} %get-tuple-element.51), channel_id=1, source_target_pairs={{0,4},{4,0},{8,12},{12,8},{1,5},{5,1},{9,13},{13,9},{2,6},{6,2},{1... | collective-permute-start | bytes 1572872 | tf_op jit(solution)/shard_map/ppermute | solution.py:113
  154.0 49.3 %collective-permute-start.6 = (bf16[2,64,2048]{2,1,0:T(8,128)(2,1)S(1)}, bf16[2,64,2048]{2,1,0:T(8,128)(2,1)S(1)}, u32[]{:S(2)}, u32[]{:S(2)}) collective-permute-start(bf16[2,64,2048]{2,1,0:T(8,128)(2,1)S(1)} %convert_element_type.134), channel_id=1, source_target_pairs={{8,0},{12,4},{2,10},{6,14},{9,1},{13,5},{3,11},{7,15},{24,16},{28,... | collective-permute-start | bytes 1572872 | tf_op jit(solution)/shard_map/ppermute | solution.py:122
  163.9 19.7 %collective-permute-start.15 = (f32[256,64]{1,0:T(8,128)S(1)}, f32[256,64]{1,0:T(8,128)S(1)}, u32[]{:S(2)}, u32[]{:S(2)}) collective-permute-start(f32[256,64]{1,0:T(8,128)S(1)} %pad_maximum_fusion.2), channel_id=1, source_target_pairs={{0,4},{4,0},{8,12},{12,8},{1,5},{5,1},{9,13},{13,9},{2,6},{6,2},{1... | collective-permute-start | bytes 196616 | tf_op jit(solution)/shard_map/ppermute | solution.py:113
  182.3 11.8 %collective-permute-start.13 = (f32[192,64]{1,0:T(8,128)S(1)}, f32[192,64]{1,0:T(8,128)S(1)}, u32[]{:S(2)}, u32[]{:S(2)}) collective-permute-start(f32[192,64]{1,0:T(8,128)S(1)} %pad_maximum_fusion.3), channel_id=1, source_target_pairs={{0,4},{4,0},{8,12},{12,8},{1,5},{5,1},{9,13},{13,9},{2,6},{6,2},{1... | collective-permute-start | bytes 147464 | tf_op jit(solution)/shard_map/ppermute | solution.py:113
  183.7 13.2 %collective-permute-start.16 = (f32[4,64,64]{2,1,0:T(8,128)S(1)}, f32[4,64,64]{2,1,0:T(8,128)S(1)}, u32[]{:S(2)}, u32[]{:S(2)}) collective-permute-start(f32[4,64,64]{2,1,0:T(8,128)S(1)} %bitcast.108), channel_id=1, source_target_pairs={{8,0},{12,4},{2,10},{6,14},{9,1},{13,5},{3,11},{7,15},{24,16},{28,... | collective-permute-start | bytes 196616 | tf_op jit(solution)/shard_map/ppermute | solution.py:122
  194.1 7.4 %collective-permute-start.14 = (f32[3,64,64]{2,1,0:T(8,128)S(1)}, f32[3,64,64]{2,1,0:T(8,128)S(1)}, u32[]{:S(2)}, u32[]{:S(2)}) collective-permute-start(f32[3,64,64]{2,1,0:T(8,128)S(1)} %bitcast.110), channel_id=1, source_target_pairs={{0,8},{4,12},{10,2},{14,6},{1,9},{5,13},{11,3},{15,7},{16,24},{20,... | collective-permute-start | bytes 147464 | tf_op jit(solution)/shard_map/ppermute | solution.py:122
  195.5 34.6 %collective-permute-start.27 = (bf16[1,64,7168]{2,1,0:T(8,128)(2,1)S(1)}, bf16[1,64,7168]{2,1,0:T(8,128)(2,1)S(1)}, u32[]{:S(2)}, u32[]{:S(2)}) collective-permute-start(bf16[1,64,7168]{2,1,0:T(8,128)(2,1)S(1)} %collective-permute-done.26.own_ref), channel_id=1, source_target_pairs={{0,1},{1,0},{2,3},{3,2},{4,5},{5,4},{6,7},{7,6},{8,9},{9,8},{10,11... | collective-permute-start | bytes 2752520 | tf_op jit(solution)/shard_map/ppermute | solution.py:107
  195.6 58.9 %collective-permute-start.4 = (bf16[1,64,2048]{2,1,0:T(8,128)(2,1)}, bf16[1,64,2048]{2,1,0:T(8,128)(2,1)}, u32[]{:S(2)}, u32[]{:S(2)}) collective-permute-start(bf16[1,64,2048]{2,1,0:T(8,128)(2,1)} %fusion.28), channel_id=1, source_target_pairs={{0,8},{4,12},{10,2},{14,6},{1,9},{5,13},{11,3},{15,7},{16,24},{20,... | collective-permute-start | bytes 786440 | tf_op jit(solution)/shard_map/ppermute | solution.py:122
  203.3 10.3 %collective-permute-start.19 = (bf16[3,64,64]{2,1,0:T(8,128)(2,1)S(1)}, bf16[3,64,64]{2,1,0:T(8,128)(2,1)S(1)}, u32[]{:S(2)}, u32[]{:S(2)}) collective-permute-start(bf16[3,64,64]{2,1,0:T(8,128)(2,1)S(1)} %fusion.36), channel_id=1, source_target_pairs={{0,3},{1,0},{2,1},{3,2},{4,7},{5,4},{6,5},{7,6},{8,11},{9,8},{10,9... | collective-permute-start | bytes 73736 | tf_op jit(solution)/shard_map/ppermute | solution.py:199
  205.4 58.2 %collective-permute-start.22 = (bf16[1,64,2048]{2,1,0:T(8,128)(2,1)}, bf16[1,64,2048]{2,1,0:T(8,128)(2,1)}, u32[]{:S(2)}, u32[]{:S(2)}) collective-permute-start(bf16[1,64,2048]{2,1,0:T(8,128)(2,1)} %fusion.27), channel_id=1, source_target_pairs={{0,8},{4,12},{10,2},{14,6},{1,9},{5,13},{11,3},{15,7},{16,24},{20,... | collective-permute-start | bytes 786440 | tf_op jit(solution)/shard_map/ppermute | solution.py:122
  206.7 63.5 %collective-permute-start.25 = (bf16[2,64,2048]{2,1,0:T(8,128)(2,1)}, bf16[2,64,2048]{2,1,0:T(8,128)(2,1)}, u32[]{:S(2)}, u32[]{:S(2)}) collective-permute-start(bf16[2,64,2048]{2,1,0:T(8,128)(2,1)} %convert_element_type.137), channel_id=1, source_target_pairs={{8,0},{12,4},{2,10},{6,14},{9,1},{13,5},{3,11},{7,15},{24,16},{28,... | collective-permute-start | bytes 1572872 | tf_op jit(solution)/shard_map/ppermute | solution.py:122
  213.6 15.6 %collective-permute-start.23 = (bf16[64,2048]{1,0:T(8,128)(2,1)S(1)}, bf16[64,2048]{1,0:T(8,128)(2,1)S(1)}, u32[]{:S(2)}, u32[]{:S(2)}) collective-permute-start(bf16[64,2048]{1,0:T(8,128)(2,1)S(1)} %get-tuple-element.62), channel_id=1, source_target_pairs={{0,4},{4,0},{8,12},{12,8},{1,5},{5,1},{9,13},{13,9},{2,6},{6,2},{1... | collective-permute-start | bytes 786440 | tf_op jit(solution)/shard_map/ppermute | solution.py:113
  253.1 7.2 %collective-permute-start.31 = (f32[1,64,64]{2,1,0:T(8,128)}, f32[1,64,64]{2,1,0:T(8,128)}, u32[]{:S(2)}, u32[]{:S(2)}) collective-permute-start(f32[1,64,64]{2,1,0:T(8,128)} %add_bitcast_fusion), channel_id=1, source_target_pairs={{0,8},{4,12},{10,2},{14,6},{1,9},{5,13},{11,3},{15,7},{16,24},{20,... | collective-permute-start | bytes 49160 | tf_op jit(solution)/shard_map/ppermute | solution.py:122
  257.1 11.5 %collective-permute-start.28 = (bf16[64,2048]{1,0:T(8,128)(2,1)}, bf16[64,2048]{1,0:T(8,128)(2,1)S(1)}, u32[]{:S(2)}, u32[]{:S(2)}) collective-permute-start(bf16[64,2048]{1,0:T(8,128)(2,1)} %copy-done.16), channel_id=1, source_target_pairs={{0,4},{4,0},{8,12},{12,8},{1,5},{5,1},{9,13},{13,9},{2,6},{6,2},{1... | collective-permute-start | bytes 786440 | tf_op jit(solution)/shard_map/ppermute | solution.py:113
  261.2 6.1 %collective-permute-start.32 = (bf16[1,64,64]{2,1,0:T(8,128)(2,1)S(1)}, bf16[1,64,64]{2,1,0:T(8,128)(2,1)S(1)}, u32[]{:S(2)}, u32[]{:S(2)}) collective-permute-start(bf16[1,64,64]{2,1,0:T(8,128)(2,1)S(1)} %fusion.40), channel_id=1, source_target_pairs={{0,1},{1,2},{2,3},{3,0},{4,5},{5,6},{6,7},{7,4},{8,9},{9,10},{10,1... | collective-permute-start | bytes 24584 | tf_op jit(solution)/shard_map/ppermute | solution.py:199
  261.2 7.4 %collective-permute-start.33 = (bf16[1,64,64]{2,1,0:T(8,128)(2,1)S(1)}, bf16[1,64,64]{2,1,0:T(8,128)(2,1)S(1)}, u32[]{:S(2)}, u32[]{:S(2)}) collective-permute-start(bf16[1,64,64]{2,1,0:T(8,128)(2,1)S(1)} %fusion.40), channel_id=1, source_target_pairs={{0,2},{1,3},{2,0},{3,1},{4,6},{5,7},{6,4},{7,5},{8,10},{9,11},{10,... | collective-permute-start | bytes 24584 | tf_op jit(solution)/shard_map/ppermute | solution.py:199
  263.6 5.0 %collective-permute-start.34 = (bf16[1,64,64]{2,1,0:T(8,128)(2,1)S(1)}, bf16[1,64,64]{2,1,0:T(8,128)(2,1)S(1)}, u32[]{:S(2)}, u32[]{:S(2)}) collective-permute-start(bf16[1,64,64]{2,1,0:T(8,128)(2,1)S(1)} %fusion.40), channel_id=1, source_target_pairs={{0,3},{1,0},{2,1},{3,2},{4,7},{5,4},{6,5},{7,6},{8,11},{9,8},{10,9... | collective-permute-start | bytes 24584 | tf_op jit(solution)/shard_map/ppermute | solution.py:199
  267.3 23.2 %collective-permute-start.24 = (bf16[1,64,2048]{2,1,0:T(8,128)(2,1)}, bf16[1,64,2048]{2,1,0:T(8,128)(2,1)S(1)}, u32[]{:S(2)}, u32[]{:S(2)}) collective-permute-start(bf16[1,64,2048]{2,1,0:T(8,128)(2,1)} %fusion.26), channel_id=1, source_target_pairs={{0,8},{4,12},{10,2},{14,6},{1,9},{5,13},{11,3},{15,7},{16,24},{20,... | collective-permute-start | bytes 786440 | tf_op jit(solution)/shard_map/ppermute | solution.py:122
  268.8 25.7 %collective-permute-start.29 = (bf16[1,64,2048]{2,1,0:T(8,128)(2,1)S(1)}, bf16[1,64,2048]{2,1,0:T(8,128)(2,1)S(1)}, u32[]{:S(2)}, u32[]{:S(2)}) collective-permute-start(bf16[1,64,2048]{2,1,0:T(8,128)(2,1)S(1)} %fusion.25), channel_id=1, source_target_pairs={{0,8},{4,12},{10,2},{14,6},{1,9},{5,13},{11,3},{15,7},{16,24},{20,... | collective-permute-start | bytes 786440 | tf_op jit(solution)/shard_map/ppermute | solution.py:122
  (34 other events, 452.8 us)

commit v2 on v1

v2 whole, which is shorter than its diff:
```python
import functools

import jax
import jax.numpy as jnp
from jax import lax
from jax.experimental import pallas as pl
from jax.experimental.pallas import tpu as pltpu
from jax.sharding import PartitionSpec as P

ADAPTER_SCALE = 0.5
BLOCK_N = 256
WEIGHT_PARTS = 7
VMEM_BYTES = 6 * 1024 * 1024


def load_body(weight_ref, *refs):
    parts, sems = refs[:-1], refs[-1]
    size = parts[0].shape[0]
    copies = [
        pltpu.make_async_copy(weight_ref.at[pl.ds(index * size, size)], part, sems.at[index])
        for index, part in enumerate(parts)
    ]
    for copy in copies:
        copy.start()
    for copy in copies:
        copy.wait()


def load_weight(weight):
    depth, width = weight.shape
    parts = WEIGHT_PARTS if depth % (128 * WEIGHT_PARTS) == 0 else 1
    loaded = pl.pallas_call(
        load_body,
        in_specs=[pl.BlockSpec(memory_space=pl.ANY)],
        out_specs=[pl.BlockSpec(memory_space=pltpu.VMEM)] * parts,
        out_shape=[pltpu.VMEM((depth // parts, width), weight.dtype)] * parts,
        scratch_shapes=[pltpu.SemaphoreType.DMA((parts,))],
        compiler_params=pltpu.CompilerParams(vmem_limit_bytes=1024 * 1024),
        name="load_weight",
    )(weight)
    return [pltpu.with_memory_space_constraint(part, pltpu.VMEM) for part in loaded]


def matmul_body(first, parts, pos_ref, own_ref, sib_ref, a_ref, *refs):
    w_refs = refs[:parts]
    send_ref, keep_ref, rank_send_ref, rank_keep_ref, x_ref, x_sems = refs[parts:]
    rows, width = send_ref.shape
    size = w_refs[0].shape[0]
    depth = parts * size
    _, steps, per_block, _ = x_ref.shape
    slots, _, rank = a_ref.shape
    block_n = min(BLOCK_N, width)

    own_at = pos_ref[0]
    own_copy = pltpu.make_async_copy(own_ref.at[pl.ds(first, steps)], x_ref.at[own_at], x_sems.at[0])
    sib_copy = pltpu.make_async_copy(sib_ref.at[pl.ds(first, steps)], x_ref.at[1 - own_at], x_sems.at[1])
    own_copy.start()
    sib_copy.start()
    own_copy.wait()
    sib_copy.wait()
    for slot in range(slots):
        x = x_ref[...].reshape(2 * rows, depth)
        part = jnp.dot(x, a_ref[slot], preferred_element_type=jnp.float32)
        rank_send_ref[:, slot * rank:(slot + 1) * rank] = part[:rows]
        rank_keep_ref[:, slot * rank:(slot + 1) * rank] = part[rows:]

    @pl.loop(0, width // block_n)
    def _(place):
        columns = pl.ds(pl.multiple_of(place * block_n, block_n), block_n)
        term = None
        for index in range(parts):
            x = x_ref[:, :, :, index * size:(index + 1) * size].reshape(2 * rows, size)
            value = jnp.dot(x, w_refs[index][:, columns], preferred_element_type=jnp.float32)
            term = value if term is None else term + value
        send_ref[:, columns] = term[:rows].astype(send_ref.dtype)
        keep_ref[:, columns] = term[rows:]


def partial_products(pos, own, sib, first, steps, weight, down_a):
    _, per_block, depth = own.shape
    width = weight[0].shape[1]
    slots, _, rank = down_a.shape
    rows = steps * per_block
    any_spec = pl.BlockSpec(memory_space=pl.ANY)
    vmem_spec = pl.BlockSpec(memory_space=pltpu.VMEM)
    return pl.pallas_call(
        functools.partial(matmul_body, first, len(weight)),
        in_specs=[pl.BlockSpec(memory_space=pltpu.SMEM), any_spec, any_spec, vmem_spec] + [vmem_spec] * len(weight),
        out_specs=[vmem_spec] * 4,
        out_shape=[
            jax.ShapeDtypeStruct((rows, width), jnp.bfloat16),
            jax.ShapeDtypeStruct((rows, width), jnp.float32),
            jax.ShapeDtypeStruct((rows, slots * rank), jnp.float32),
            jax.ShapeDtypeStruct((rows, slots * rank), jnp.float32),
        ],
        scratch_shapes=[
            pltpu.VMEM((2, steps, per_block, depth), jnp.bfloat16),
            pltpu.SemaphoreType.DMA((2,)),
        ],
        compiler_params=pltpu.CompilerParams(vmem_limit_bytes=VMEM_BYTES),
        cost_estimate=pl.CostEstimate(flops=0, bytes_accessed=0, transcendentals=0),
        name="partial_products",
    )(pos, own, sib, down_a, *weight)


def per_device(hidden, base_weight, down_a, up_b, adapter_ids, owner_map):
    step_count, per_block, depth = hidden.shape
    n_tensor = lax.axis_size("tp")
    n_rep = lax.axis_size("rep")
    n_sub = lax.axis_size("sub")
    n_owners = n_rep * n_sub
    tensor_index = lax.axis_index("tp")
    rep_index = lax.axis_index("rep")
    sub_index = lax.axis_index("sub")
    owner_index = lax.axis_index(("rep", "sub"))
    requests = per_block * n_owners
    rows_mine = requests // n_tensor
    targets = per_block // rows_mine
    group = n_tensor // n_rep
    group_index = tensor_index // group
    owned_slots, _, rank_size = down_a.shape
    slot_count = owned_slots * n_owners
    width = base_weight.shape[1]

    def after(value, *done):
        return lax.optimization_barrier((value, *done))[0]

    def swap_cores(value):
        return lax.ppermute(value, "sub", [(i, i ^ 1) for i in range(n_sub)])

    def from_rep(value, shift):
        return lax.ppermute(value, "rep", [((i + shift) % n_rep, i) for i in range(n_rep)])

    def swap_tensor(value, bit):
        return lax.ppermute(value, "tp", [(i, i ^ bit) for i in range(n_tensor)])

    def to_group(value, shift, hop):
        pairs = []
        for rep in range(n_rep):
            target = (rep + shift) % n_rep
            source = (target + hop) % n_rep
            for low in range(group):
                pairs.append(((source * group + low) * n_rep + rep, (target * group + low) * n_rep + rep))
        return lax.ppermute(value, ("tp", "rep"), pairs)

    def halve(send, keep, steps, kind):
        rows, columns = keep.shape
        total = keep + swap_tensor(send, group // 2).astype(jnp.float32)
        extent, bit = rows // steps, group // 4
        while bit:
            extent //= 2
            halves = total.reshape(steps, 2, extent, columns)
            mine = (tensor_index // bit) % 2
            kept = lax.dynamic_index_in_dim(halves, mine, 1, keepdims=False)
            sent = lax.dynamic_index_in_dim(halves, 1 - mine, 1, keepdims=False)
            total = kept + swap_tensor(sent.astype(kind), bit).astype(jnp.float32)
            bit //= 2
        total = total.reshape(steps, extent, columns)
        return total, total.astype(kind)

    def collect(total, rounded, shift, *done):
        if done:
            total = after(total, *done)
        for hop in range(1, n_rep):
            total = total + to_group(rounded, shift, hop).astype(jnp.float32)
        return total

    def choose(local, others):
        value = local
        for shift, other in others:
            value = jnp.where(group_index == (rep_index + shift) % n_rep, other, value)
        return value

    keeps = (tensor_index // (group // 2)) % 2
    pos = (sub_index == keeps).astype(jnp.int32).reshape(1)

    pieces = [(step, 0, 2) for step in range(step_count - 1)] + [(step_count - 1, 0, 1), (step_count - 1, 1, 1)]
    share = rows_mine // 2
    remote = {}
    for index, (step, begin, parts) in enumerate(pieces):
        piece = hidden[step].reshape(targets, rows_mine, depth)[:, begin * share:(begin + parts) * share]
        piece = piece.reshape(1, targets * parts * share, depth)
        for shift in range(1, n_rep):
            remote[index, shift] = from_rep(piece, shift)

    siblings = swap_cores(hidden)
    half = step_count // 2

    panels, bit = up_b, 1
    while bit < n_tensor:
        panels = jnp.concatenate([panels, swap_tensor(panels, bit)], axis=0)
        bit *= 2
    panels = panels.reshape(slot_count * rank_size, width)
    panel_slots = (
        (tensor_index ^ lax.broadcasted_iota(jnp.int32, (n_tensor, up_b.shape[0]), 0)) * up_b.shape[0]
        + lax.broadcasted_iota(jnp.int32, (n_tensor, up_b.shape[0]), 1)
    ).reshape(slot_count)

    my_ids = lax.dynamic_slice_in_dim(adapter_ids, tensor_index * rows_mine, rows_mine)
    iota = lax.broadcasted_iota(jnp.int32, (rows_mine, slot_count), 1)
    my_slot = jnp.sum((my_ids == iota).astype(jnp.int32) * owner_map[None, :], axis=1)
    panel_hot = my_slot[:, None] == panel_slots[None, :]
    owned_hot = my_slot[:, None] == (
        owner_index * owned_slots + lax.broadcasted_iota(jnp.int32, (rows_mine, owned_slots), 1)
    )

    weight = load_weight(base_weight)
    factor = pltpu.with_memory_space_constraint(down_a, pltpu.VMEM)
    local_parts, local_halved, local_sums = {}, {}, {}
    remote_parts, remote_halved, remote_sums = {}, {}, {}

    def local_rows(index, *done):
        send, keep, rank_send, rank_keep = partial_products(
            pos, hidden, after(siblings, *done), index * half, half, weight, factor
        )
        local_parts[index] = (rank_send, rank_keep)
        local_halved[index] = halve(send, keep, half, jnp.bfloat16)
        return rank_keep

    def remote_rows(index, *done):
        for shift in range(1, n_rep):
            own = after(remote[index, shift], *done)
            sib = swap_cores(own)
            send, keep, rank_send, rank_keep = partial_products(pos, own, sib, 0, 1, weight, factor)
            remote_parts[index, shift] = (rank_send, rank_keep)
            remote_halved[index, shift] = halve(send, keep, 1, jnp.bfloat16)
            done = (rank_keep,)
        return done[0]

    def arrived(index):
        return tuple(remote[index, shift] for shift in range(1, n_rep))

    def halved(index):
        return tuple(remote_halved[index, shift][1] for shift in range(1, n_rep))

    def local_collect(index, *done):
        local_sums[index] = collect(*local_halved[index], 0, *done)

    def remote_collect(index, *done):
        for shift in range(1, n_rep):
            remote_sums[index, shift] = collect(*remote_halved[index, shift], shift, *done)

    def summed(index):
        return tuple(remote_sums[index, shift] for shift in range(1, n_rep))

    token = local_rows(0)
    token = local_rows(1, token)
    token = remote_rows(0, token, local_halved[0][1])
    token = remote_rows(1, token, local_halved[1][1])
    local_collect(0, token)
    token = remote_rows(2, token, *halved(0))
    local_collect(1, token)
    remote_collect(0, token)
    token = remote_rows(3, token, *halved(1), local_sums[0])
    remote_collect(1, token)
    token = remote_rows(4, token, *halved(2), local_sums[1], *summed(0))
    remote_collect(2, token)
    remote_collect(3, token)
    remote_collect(4, token)

    def joined(parts, at):
        last = [part[at].reshape(targets, -1, owned_slots * rank_size) for part in parts[-2:]]
        last = jnp.concatenate(last, axis=1).reshape(per_block, owned_slots * rank_size)
        return jnp.concatenate([part[at] for part in parts[:-2]] + [last])

    local_ranks = collect(*halve(
        jnp.concatenate([local_parts[0][0], local_parts[1][0]]),
        jnp.concatenate([local_parts[0][1], local_parts[1][1]]),
        step_count, jnp.float32), 0)
    others = []
    for shift in range(1, n_rep):
        parts = [remote_parts[index, shift] for index in range(len(pieces))]
        others.append((shift, collect(
            *halve(joined(parts, 0), joined(parts, 1), step_count, jnp.float32), shift)))
    finished = choose(local_ranks, others).astype(jnp.bfloat16)
    finished = finished.reshape(step_count, rows_mine, owned_slots, rank_size)
    masked = jnp.sum(
        jnp.where(owned_hot[None, :, :, None], finished, 0), axis=2, dtype=jnp.float32
    ).astype(jnp.bfloat16)
    chosen = masked
    for turn in range(1, n_owners):
        chosen = chosen + lax.ppermute(
            masked, ("rep", "sub"), [(i, (i + turn) % n_owners) for i in range(n_owners)]
        )
    spread = jnp.where(panel_hot[None, :, :, None], chosen[:, :, None, :], 0)
    spread = spread.reshape(step_count, rows_mine, slot_count * rank_size)

    outputs = []
    for index, (step, begin, parts) in enumerate(pieces):
        span = slice(begin * share, (begin + parts) * share)
        sums = choose(
            local_sums[step // half][step % half, span],
            [(shift, remote_sums[index, shift][0]) for shift in range(1, n_rep)],
        )
        lifted = jnp.dot(spread[step, span], panels, preferred_element_type=jnp.float32)
        lifted = lifted.astype(jnp.bfloat16).astype(jnp.float32)
        outputs.append((sums + ADAPTER_SCALE * lifted).astype(jnp.bfloat16))
    return jnp.concatenate(outputs).reshape(step_count, rows_mine, width)


def solution(mesh):
    return jax.shard_map(
        per_device,
        mesh=mesh,
        in_specs=(
            P(None, ("groups", "rep", "sub"), "tp"),
            P("tp", ("rep", "sub")),
            P(("rep", "sub"), "tp", None),
            P("tp", None, ("rep", "sub")),
            P("groups", None),
            P(),
        ),
        out_specs=P(None, ("groups", "tp"), ("rep", "sub")),
        check_vma=False,
    )
```

time: 297 us -> 289 us (0.973)
  the two profiles are of different devices: /device:TPU:6 before, /device:TPU:0 now
where the time goes in v2:
time: 289 us; the launch traced here: 288 us
  local copies, waits for them, and re-layouts  80.2 us (28%)
  Pallas kernels  73.4 us (25%)
  waiting for transfers between devices  57.4 us (20%)
  starting transfers between devices  56.4 us (20%)
  other arithmetic  13.2 us (5%)
  matrix products  6.31 us (2%)
    unnamed x115, local copies, waits for them, and re-layouts  68 us
    pallas_call x7, Pallas kernels, partial_products(): pl.pallas_call(functools.partial(matmul_body, first, len(weight)), in_spe...  63.9 us
    ppermute x11, waiting for transfers between devices, swap_tensor(): return lax.ppermute(value, 'tp', [(i, i ^ bit) for i in range(n_tensor)])  46.4 us
    ppermute x9, starting transfers between devices, to_group(): return lax.ppermute(value, ('tp', 'rep'), pairs)  30.3 us
    ppermute x11, starting transfers between devices, swap_tensor(): return lax.ppermute(value, 'tp', [(i, i ^ bit) for i in range(n_tensor)])  12.7 us
    ppermute x9, waiting for transfers between devices, to_group(): return lax.ppermute(value, ('tp', 'rep'), pairs)  10.9 us
    pallas_call x1, Pallas kernels, load_weight(): pl.pallas_call(load_body, in_specs=[pl.BlockSpec(memory_space=pl.ANY)], o...  9.56 us
    ppermute x3, starting transfers between devices, per_device(): lax.ppermute(masked, ('rep', 'sub'), [(i, (i + turn) % n_owners) for i in...  7.71 us
  transfers between devices with their start and end apart: 34, of which 7 were waited for; matrix products, arithmetic and copies ran while one was open for 11% of the time, Pallas kernels for 26%

profile of v2, /device:TPU:0, one launch (start us, length us, event | category | flops | bytes accessed | tf_op | source)
XLA Modules:
  0.0 287.6 jit_solution(2558564622152879694)
XLA Ops:
  0.5 3.3 %fusion.47 = (bf16[1,64,7168]{2,1,0:T(8,128)(2,1)}, bf16[1,64,7168]{2,1,0:T(8,128)(2,1)}, bf16[1,64,7168]{2,1,0:T(8,128)(2,1)}) fusion(bf16[4,64,7168]{2,1,0:T(8,128)(2,1)} %own_ref.3), kind=kLoop, calls=%fused_computation.87 | loop fusion | bytes 5505024 | tf_op jit(solution)/shard_map/slice | solution.py:181
  3.8 2.5 collective-permute-start
  8.3 9.6 %load_weight.1 = (bf16[1024,2048]{1,0:T(8,128)(2,1)S(1)}, bf16[1024,2048]{1,0:T(8,128)(2,1)S(1)}, bf16[1024,2048]{1,0:T(8,128)(2,1)S(1)}, bf16[1024,2048]{1,0:T(...) custom-call(bf16[7168,2048]{1,0:T(8,128)(2,1)} %weight_ref.1), custom_call_target="tpu_custom_call" | custom-call | tf_op jit(solution)/shard_map/load_weight/pallas_call | solution.py:32
  35.2 2.2 copy-done.9
  37.4 2.2 copy-done.15
  39.5 2.2 copy-done.21
  50.3 12.8 %partial_products.7 = (bf16[128,2048]{1,0:T(8,128)(2,1)}, f32[128,2048]{1,0:T(8,128)S(1)}, f32[128,64]{1,0:T(8,128)S(1)}, f32[128,64]{1,0:T(8,128)S(1)}) custom-call(s32[1]{0:T(128)} %bitcast.pos_ref, bf16[4,64,7168]{2,1,0:T(8,128)(2,1)S(1)} %copy-done.36, bf16[4,64,7168]{2,1,0:T(8,128)(2,1)} %collective-permute-done.1.sib_ref, ...), custom_call_target="tpu_custom_call" | custom-call | tf_op jit(solution)/shard_map/partial_products/pallas_call | solution.py:86
  66.3 2.2 copy-done.4
  68.5 2.2 copy-done.10
  70.6 2.2 copy-done.16
  72.8 2.2 copy-done.22
  75.0 2.2 copy-done.26
  77.2 2.2 copy-done.30
  83.6 12.1 %partial_products.8 = (bf16[128,2048]{1,0:T(8,128)(2,1)S(1)}, f32[128,2048]{1,0:T(8,128)S(1)}, f32[128,64]{1,0:T(8,128)S(1)}, f32[128,64]{1,0:T(8,128)S(1)}) custom-call(s32[1]{0:T(128)} %bitcast.pos_ref, bf16[4,64,7168]{2,1,0:T(8,128)(2,1)S(1)} %copy-done.37, bf16[4,64,7168]{2,1,0:T(8,128)(2,1)} %collective-permute-done.1.sib_ref, ...), custom_call_target="tpu_custom_call" | custom-call | tf_op jit(solution)/shard_map/partial_products/pallas_call | solution.py:86
  98.4 10.4 %collective-permute-done.7 = bf16[128,2048]{1,0:T(8,128)(2,1)S(1)} collective-permute-done((bf16[128,2048]{1,0:T(8,128)(2,1)S(1)}, bf16[128,2048]{1,0:T(8,128)(2,1)S(1)}, u32[]{:S(2)}, u32[]{:S(2)}) %collective-permute-start.7) | collective-permute-done | bytes 524320 | tf_op jit(solution)/shard_map/ppermute | solution.py:135
  110.2 7.8 %partial_products.9 = (bf16[64,2048]{1,0:T(8,128)(2,1)S(1)}, f32[64,2048]{1,0:T(8,128)S(1)}, f32[64,64]{1,0:T(8,128)S(1)}, f32[64,64]{1,0:T(8,128)S(1)}) custom-call(s32[1]{0:T(128)} %bitcast.pos_ref, bf16[1,64,7168]{2,1,0:T(8,128)(2,1)} %collective-permute-done.own_ref, bf16[1,64,7168]{2,1,0:T(8,128)(2,1)S(1)} %collective-permute-done.3.sib_ref, ...), custom_call_target="tpu_custom_call" | custom-call | tf_op jit(solution)/shard_map/partial_products/pallas_call | solution.py:86
  126.3 7.0 %collective-permute-done.4 = bf16[64,2048]{1,0:T(8,128)(2,1)S(1)} collective-permute-done((bf16[64,2048]{1,0:T(8,128)(2,1)}, bf16[64,2048]{1,0:T(8,128)(2,1)S(1)}, u32[]{:S(2)}, u32[]{:S(2)}) %collective-permute-start.4) | collective-permute-done | bytes 262176 | tf_op jit(solution)/shard_map/ppermute | solution.py:135
  150.2 8.0 %partial_products.10 = (bf16[64,2048]{1,0:T(8,128)(2,1)S(1)}, f32[64,2048]{1,0:T(8,128)S(1)}, f32[64,64]{1,0:T(8,128)S(1)}, f32[64,64]{1,0:T(8,128)S(1)}) custom-call(s32[1]{0:T(128)} %bitcast.pos_ref, bf16[1,64,7168]{2,1,0:T(8,128)(2,1)} %collective-permute-done.6.own_ref, bf16[1,64,7168]{2,1,0:T(8,128)(2,1)S(1)} %collective-permute-done.8.sib_ref, ...), custom_call_target="tpu_custom_call" | custom-call | tf_op jit(solution)/shard_map/partial_products/pallas_call | solution.py:86
  158.3 7.0 %collective-permute-done.11 = bf16[2,64,2048]{2,1,0:T(8,128)(2,1)S(1)} collective-permute-done((bf16[2,64,2048]{2,1,0:T(8,128)(2,1)}, bf16[2,64,2048]{2,1,0:T(8,128)(2,1)S(1)}, u32[]{:S(2)}, u32[]{:S(2)}) %collective-permute-start.11) | collective-permute-done | bytes 524320 | tf_op jit(solution)/shard_map/ppermute | solution.py:144
  166.4 15.0 %collective-permute-done.13 = bf16[64,2048]{1,0:T(8,128)(2,1)S(1)} collective-permute-done((bf16[64,2048]{1,0:T(8,128)(2,1)S(1)}, bf16[64,2048]{1,0:T(8,128)(2,1)S(1)}, u32[]{:S(2)}, u32[]{:S(2)}) %collective-permute-start.13) | collective-permute-done | bytes 262176 | tf_op jit(solution)/shard_map/ppermute | solution.py:135
  182.2 7.9 %partial_products.11 = (bf16[64,2048]{1,0:T(8,128)(2,1)S(1)}, f32[64,2048]{1,0:T(8,128)S(1)}, f32[64,64]{1,0:T(8,128)S(1)}, f32[64,64]{1,0:T(8,128)S(1)}) custom-call(s32[1]{0:T(128)} %bitcast.pos_ref, bf16[1,64,7168]{2,1,0:T(8,128)(2,1)} %collective-permute-done.5.own_ref, bf16[1,64,7168]{2,1,0:T(8,128)(2,1)S(1)} %collective-permute-done.9.sib_ref, ...), custom_call_target="tpu_custom_call" | custom-call | tf_op jit(solution)/shard_map/partial_products/pallas_call | solution.py:86
  190.1 5.0 %collective-permute-start.10 = (bf16[1,64,2048]{2,1,0:T(8,128)(2,1)S(1)}, bf16[1,64,2048]{2,1,0:T(8,128)(2,1)S(1)}, u32[]{:S(2)}, u32[]{:S(2)}) collective-permute-start(bf16[1,64,2048]{2,1,0:T(8,128)(2,1)S(1)} %get-tuple-element.110), channel_id=1, source_target_pairs={{0,8},{4,12},{10,2},{14,6},{1,9},{5,13},{11,3},{15,7},{16,24},{20,... | collective-permute-start | bytes 786440 | tf_op jit(solution)/shard_map/ppermute | solution.py:144
  198.2 3.9 %collective-permute-done.10 = bf16[1,64,2048]{2,1,0:T(8,128)(2,1)S(1)} collective-permute-done((bf16[1,64,2048]{2,1,0:T(8,128)(2,1)S(1)}, bf16[1,64,2048]{2,1,0:T(8,128)(2,1)S(1)}, u32[]{:S(2)}, u32[]{:S(2)}) %collective-permute-start.10) | collective-permute-done | bytes 262176 | tf_op jit(solution)/shard_map/ppermute | solution.py:144
  203.0 9.0 %collective-permute-done.16 = bf16[64,2048]{1,0:T(8,128)(2,1)S(1)} collective-permute-done((bf16[64,2048]{1,0:T(8,128)(2,1)S(1)}, bf16[64,2048]{1,0:T(8,128)(2,1)S(1)}, u32[]{:S(2)}, u32[]{:S(2)}) %collective-permute-start.16) | collective-permute-done | bytes 262176 | tf_op jit(solution)/shard_map/ppermute | solution.py:135
  212.9 7.9 %partial_products.12 = (bf16[32,2048]{1,0:T(8,128)(2,1)S(1)}, f32[32,2048]{1,0:T(8,128)S(1)}, f32[32,64]{1,0:T(8,128)S(1)}, f32[32,64]{1,0:T(8,128)S(1)}) custom-call(s32[1]{0:T(128)} %bitcast.pos_ref, bf16[1,32,7168]{2,1,0:T(8,128)(2,1)} %collective-permute-done.12.own_ref, bf16[1,32,7168]{2,1,0:T(8,128)(2,1)S(1)} %collective-permute-done.14.sib_ref, ...), custom_call_target="tpu_custom_call" | custom-call | tf_op jit(solution)/shard_map/partial_products/pallas_call | solution.py:86
  223.4 6.2 %collective-permute-start.28 = (bf16[1,64,2048]{2,1,0:T(8,128)(2,1)}, bf16[1,64,2048]{2,1,0:T(8,128)(2,1)}, u32[]{:S(2)}, u32[]{:S(2)}) collective-permute-start(bf16[1,64,2048]{2,1,0:T(8,128)(2,1)} %get-tuple-element.109), channel_id=1, source_target_pairs={{0,8},{4,12},{10,2},{14,6},{1,9},{5,13},{11,3},{15,7},{16,24},{20,... | collective-permute-start | bytes 786440 | tf_op jit(solution)/shard_map/ppermute | solution.py:144
  231.6 4.4 %collective-permute-start.30 = (bf16[32,2048]{1,0:T(8,128)(2,1)S(1)}, bf16[32,2048]{1,0:T(8,128)(2,1)S(1)}, u32[]{:S(2)}, u32[]{:S(2)}) collective-permute-start(bf16[32,2048]{1,0:T(8,128)(2,1)S(1)} %get-tuple-element.96), channel_id=1, source_target_pairs={{0,4},{4,0},{8,12},{12,8},{1,5},{5,1},{9,13},{13,9},{2,6},{6,2},{1... | collective-permute-start | bytes 393224 | tf_op jit(solution)/shard_map/ppermute | solution.py:135
  236.0 7.4 %partial_products.13 = (bf16[32,2048]{1,0:T(8,128)(2,1)S(1)}, f32[32,2048]{1,0:T(8,128)S(1)}, f32[32,64]{1,0:T(8,128)S(1)}, f32[32,64]{1,0:T(8,128)S(1)}) custom-call(s32[1]{0:T(128)} %bitcast.pos_ref, bf16[1,32,7168]{2,1,0:T(8,128)(2,1)S(1)} %collective-permute-done.15.own_ref, bf16[1,32,7168]{2,1,0:T(8,128)(2,1)S(1)} %collective-permute-done.18.sib_ref, ...), custom_call_target="tpu_custom_call" | custom-call | tf_op jit(solution)/shard_map/partial_products/pallas_call | solution.py:86
  243.6 4.9 %collective-permute-done.19 = f32[256,64]{1,0:T(8,128)S(1)} collective-permute-done((f32[256,64]{1,0:T(8,128)S(1)}, f32[256,64]{1,0:T(8,128)S(1)}, u32[]{:S(2)}, u32[]{:S(2)}) %collective-permute-start.19) | collective-permute-done | bytes 65568 | tf_op jit(solution)/shard_map/ppermute | solution.py:135
  248.5 9.2 %collective-permute-start.20 = (f32[4,64,64]{2,1,0:T(8,128)S(1)}, f32[4,64,64]{2,1,0:T(8,128)S(1)}, u32[]{:S(2)}, u32[]{:S(2)}) collective-permute-start(f32[4,64,64]{2,1,0:T(8,128)S(1)} %bitcast.106), channel_id=1, source_target_pairs={{0,8},{4,12},{10,2},{14,6},{1,9},{5,13},{11,3},{15,7},{16,24},{20,... | collective-permute-start | bytes 196616 | tf_op jit(solution)/shard_map/ppermute | solution.py:144
  258.6 2.5 collective-permute-start.32
  261.2 6.3 %collective-permute-start.24 = (bf16[4,64,64]{2,1,0:T(8,128)(2,1)S(1)}, bf16[4,64,64]{2,1,0:T(8,128)(2,1)S(1)}, u32[]{:S(2)}, u32[]{:S(2)}) collective-permute-start(bf16[4,64,64]{2,1,0:T(8,128)(2,1)S(1)} %fusion.45), channel_id=1, source_target_pairs={{0,2},{1,3},{2,0},{3,1},{4,6},{5,7},{6,4},{7,5},{8,10},{9,11},{10,... | collective-permute-start | bytes 98312 | tf_op jit(solution)/shard_map/ppermute | solution.py:282
  (203 shorter events, 97.1 us)
Async XLA Ops:
  0.0 33.0 %collective-permute-start.1 = (bf16[4,64,7168]{2,1,0:T(8,128)(2,1)}, bf16[4,64,7168]{2,1,0:T(8,128)(2,1)}, u32[]{:S(2)}, u32[]{:S(2)}) collective-permute-start(bf16[4,64,7168]{2,1,0:T(8,128)(2,1)} %own_ref.3), channel_id=1, source_target_pairs={{0,1},{1,0},{2,3},{3,2},{4,5},{5,4},{6,7},{7,6},{8,9},{9,8},{10,11... | collective-permute-start | bytes 11010056 | tf_op jit(solution)/shard_map/ppermute | solution.py:129
  3.8 94.3 %collective-permute-start = (bf16[1,64,7168]{2,1,0:T(8,128)(2,1)}, bf16[1,64,7168]{2,1,0:T(8,128)(2,1)}, u32[]{:S(2)}, u32[]{:S(2)}) collective-permute-start(bf16[1,64,7168]{2,1,0:T(8,128)(2,1)} %get-tuple-element.105), channel_id=1, source_target_pairs={{2,0},{0,2},{3,1},{1,3},{6,4},{4,6},{7,5},{5,7},{10,8},{8,10},{11,... | collective-permute-start | bytes 2752520 | tf_op jit(solution)/shard_map/ppermute | solution.py:132
  6.3 113.6 %collective-permute-start.6 = (bf16[1,64,7168]{2,1,0:T(8,128)(2,1)}, bf16[1,64,7168]{2,1,0:T(8,128)(2,1)}, u32[]{:S(2)}, u32[]{:S(2)}) collective-permute-start(bf16[1,64,7168]{2,1,0:T(8,128)(2,1)} %get-tuple-element.103), channel_id=1, source_target_pairs={{2,0},{0,2},{3,1},{1,3},{6,4},{4,6},{7,5},{5,7},{10,8},{8,10},{11,... | collective-permute-start | bytes 2752520 | tf_op jit(solution)/shard_map/ppermute | solution.py:132
  6.3 151.9 %collective-permute-start.5 = (bf16[1,64,7168]{2,1,0:T(8,128)(2,1)}, bf16[1,64,7168]{2,1,0:T(8,128)(2,1)}, u32[]{:S(2)}, u32[]{:S(2)}) collective-permute-start(bf16[1,64,7168]{2,1,0:T(8,128)(2,1)} %get-tuple-element.104), channel_id=1, source_target_pairs={{2,0},{0,2},{3,1},{1,3},{6,4},{4,6},{7,5},{5,7},{10,8},{8,10},{11,... | collective-permute-start | bytes 2752520 | tf_op jit(solution)/shard_map/ppermute | solution.py:132
  63.1 32.7 %collective-permute-start.2 = (bf16[128,2048]{1,0:T(8,128)(2,1)}, bf16[128,2048]{1,0:T(8,128)(2,1)}, u32[]{:S(2)}, u32[]{:S(2)}) collective-permute-start(bf16[128,2048]{1,0:T(8,128)(2,1)} %get-tuple-element.64), channel_id=1, source_target_pairs={{0,4},{4,0},{8,12},{12,8},{1,5},{5,1},{9,13},{13,9},{2,6},{6,2},{1... | collective-permute-start | bytes 1572872 | tf_op jit(solution)/shard_map/ppermute | solution.py:135
  65.7 124.4 %collective-permute-start.12 = (bf16[1,32,7168]{2,1,0:T(8,128)(2,1)}, bf16[1,32,7168]{2,1,0:T(8,128)(2,1)}, u32[]{:S(2)}, u32[]{:S(2)}) collective-permute-start(bf16[1,32,7168]{2,1,0:T(8,128)(2,1)} %get-tuple-element.101), channel_id=1, source_target_pairs={{2,0},{0,2},{3,1},{1,3},{6,4},{4,6},{7,5},{5,7},{10,8},{8,10},{11,... | collective-permute-start | bytes 1376264 | tf_op jit(solution)/shard_map/ppermute | solution.py:132
  95.8 13.0 %collective-permute-start.7 = (bf16[128,2048]{1,0:T(8,128)(2,1)S(1)}, bf16[128,2048]{1,0:T(8,128)(2,1)S(1)}, u32[]{:S(2)}, u32[]{:S(2)}) collective-permute-start(bf16[128,2048]{1,0:T(8,128)(2,1)S(1)} %get-tuple-element.70), channel_id=1, source_target_pairs={{0,4},{4,0},{8,12},{12,8},{1,5},{5,1},{9,13},{13,9},{2,6},{6,2},{1... | collective-permute-start | bytes 1572872 | tf_op jit(solution)/shard_map/ppermute | solution.py:135
  98.1 12.1 %collective-permute-start.3 = (bf16[1,64,7168]{2,1,0:T(8,128)(2,1)}, bf16[1,64,7168]{2,1,0:T(8,128)(2,1)S(1)}, u32[]{:S(2)}, u32[]{:S(2)}) collective-permute-start(bf16[1,64,7168]{2,1,0:T(8,128)(2,1)} %collective-permute-done.own_ref), channel_id=1, source_target_pairs={{0,1},{1,0},{2,3},{3,2},{4,5},{5,4},{6,7},{7,6},{8,9},{9,8},{10,11... | collective-permute-start | bytes 2752520 | tf_op jit(solution)/shard_map/ppermute | solution.py:129
  108.8 15.1 %collective-permute-start.26 = (bf16[1,64,2048]{2,1,0:T(8,128)(2,1)}, bf16[1,64,2048]{2,1,0:T(8,128)(2,1)}, u32[]{:S(2)}, u32[]{:S(2)}) collective-permute-start(bf16[1,64,2048]{2,1,0:T(8,128)(2,1)} %param.9), channel_id=1, source_target_pairs={{0,4},{4,0},{8,12},{12,8},{1,5},{5,1},{9,13},{13,9},{2,6},{6,2},{1... | collective-permute-start | bytes 786440 | tf_op jit(solution)/shard_map/ppermute | solution.py:135
  119.9 13.5 %collective-permute-start.8 = (bf16[1,64,7168]{2,1,0:T(8,128)(2,1)}, bf16[1,64,7168]{2,1,0:T(8,128)(2,1)S(1)}, u32[]{:S(2)}, u32[]{:S(2)}) collective-permute-start(bf16[1,64,7168]{2,1,0:T(8,128)(2,1)} %collective-permute-done.6.own_ref), channel_id=1, source_target_pairs={{0,1},{1,0},{2,3},{3,2},{4,5},{5,4},{6,7},{7,6},{8,9},{9,8},{10,11... | collective-permute-start | bytes 2752520 | tf_op jit(solution)/shard_map/ppermute | solution.py:129
  122.2 11.2 %collective-permute-start.4 = (bf16[64,2048]{1,0:T(8,128)(2,1)}, bf16[64,2048]{1,0:T(8,128)(2,1)S(1)}, u32[]{:S(2)}, u32[]{:S(2)}) collective-permute-start(bf16[64,2048]{1,0:T(8,128)(2,1)} %copy-done.42), channel_id=1, source_target_pairs={{0,4},{4,0},{8,12},{12,8},{1,5},{5,1},{9,13},{13,9},{2,6},{6,2},{1... | collective-permute-start | bytes 786440 | tf_op jit(solution)/shard_map/ppermute | solution.py:135
  125.0 40.3 %collective-permute-start.11 = (bf16[2,64,2048]{2,1,0:T(8,128)(2,1)}, bf16[2,64,2048]{2,1,0:T(8,128)(2,1)S(1)}, u32[]{:S(2)}, u32[]{:S(2)}) collective-permute-start(bf16[2,64,2048]{2,1,0:T(8,128)(2,1)} %convert_element_type.136), channel_id=1, source_target_pairs={{8,0},{12,4},{2,10},{6,14},{9,1},{13,5},{3,11},{7,15},{24,16},{28,... | collective-permute-start | bytes 1572872 | tf_op jit(solution)/shard_map/ppermute | solution.py:144
  133.4 87.5 %collective-permute-start.15 = (bf16[1,32,7168]{2,1,0:T(8,128)(2,1)}, bf16[1,32,7168]{2,1,0:T(8,128)(2,1)S(1)}, u32[]{:S(2)}, u32[]{:S(2)}) collective-permute-start(bf16[1,32,7168]{2,1,0:T(8,128)(2,1)} %get-tuple-element.102), channel_id=1, source_target_pairs={{2,0},{0,2},{3,1},{1,3},{6,4},{4,6},{7,5},{5,7},{10,8},{8,10},{11,... | collective-permute-start | bytes 1376264 | tf_op jit(solution)/shard_map/ppermute | solution.py:132
  133.4 61.7 %collective-permute-start.17 = (bf16[2,64,2048]{2,1,0:T(8,128)(2,1)}, bf16[2,64,2048]{2,1,0:T(8,128)(2,1)S(1)}, u32[]{:S(2)}, u32[]{:S(2)}) collective-permute-start(bf16[2,64,2048]{2,1,0:T(8,128)(2,1)} %convert_element_type.139), channel_id=1, source_target_pairs={{8,0},{12,4},{2,10},{6,14},{9,1},{13,5},{3,11},{7,15},{24,16},{28,... | collective-permute-start | bytes 1572872 | tf_op jit(solution)/shard_map/ppermute | solution.py:144
  158.2 24.0 %collective-permute-start.9 = (bf16[1,64,7168]{2,1,0:T(8,128)(2,1)}, bf16[1,64,7168]{2,1,0:T(8,128)(2,1)S(1)}, u32[]{:S(2)}, u32[]{:S(2)}) collective-permute-start(bf16[1,64,7168]{2,1,0:T(8,128)(2,1)} %collective-permute-done.5.own_ref), channel_id=1, source_target_pairs={{0,1},{1,0},{2,3},{3,2},{4,5},{5,4},{6,7},{7,6},{8,9},{9,8},{10,11... | collective-permute-start | bytes 2752520 | tf_op jit(solution)/shard_map/ppermute | solution.py:129
  165.3 16.1 %collective-permute-start.13 = (bf16[64,2048]{1,0:T(8,128)(2,1)S(1)}, bf16[64,2048]{1,0:T(8,128)(2,1)S(1)}, u32[]{:S(2)}, u32[]{:S(2)}) collective-permute-start(bf16[64,2048]{1,0:T(8,128)(2,1)S(1)} %get-tuple-element.78), channel_id=1, source_target_pairs={{0,4},{4,0},{8,12},{12,8},{1,5},{5,1},{9,13},{13,9},{2,6},{6,2},{1... | collective-permute-start | bytes 786440 | tf_op jit(solution)/shard_map/ppermute | solution.py:135
  181.4 39.5 %collective-permute-start.27 = (bf16[2,64,2048]{2,1,0:T(8,128)(2,1)S(1)}, bf16[2,64,2048]{2,1,0:T(8,128)(2,1)S(1)}, u32[]{:S(2)}, u32[]{:S(2)}) collective-permute-start(bf16[2,64,2048]{2,1,0:T(8,128)(2,1)S(1)} %pad_maximum_fusion.1), channel_id=1, source_target_pairs={{0,8},{4,12},{8,0},{12,4},{1,9},{5,13},{9,1},{13,5},{2,10},{6,14},... | collective-permute-start | bytes 1572872 | tf_op jit(solution)/shard_map/ppermute | solution.py:135
  182.2 39.9 %collective-permute-start.21 = (f32[256,64]{1,0:T(8,128)S(1)}, f32[256,64]{1,0:T(8,128)S(1)}, u32[]{:S(2)}, u32[]{:S(2)}) collective-permute-start(f32[256,64]{1,0:T(8,128)S(1)} %pad_maximum_fusion.3), channel_id=1, source_target_pairs={{0,4},{4,0},{8,12},{12,8},{1,5},{5,1},{9,13},{13,9},{2,6},{6,2},{1... | collective-permute-start | bytes 196616 | tf_op jit(solution)/shard_map/ppermute | solution.py:135
  190.1 12.0 %collective-permute-start.10 = (bf16[1,64,2048]{2,1,0:T(8,128)(2,1)S(1)}, bf16[1,64,2048]{2,1,0:T(8,128)(2,1)S(1)}, u32[]{:S(2)}, u32[]{:S(2)}) collective-permute-start(bf16[1,64,2048]{2,1,0:T(8,128)(2,1)S(1)} %get-tuple-element.110), channel_id=1, source_target_pairs={{0,8},{4,12},{10,2},{14,6},{1,9},{5,13},{11,3},{15,7},{16,24},{20,... | collective-permute-start | bytes 786440 | tf_op jit(solution)/shard_map/ppermute | solution.py:144
  195.2 16.8 %collective-permute-start.16 = (bf16[64,2048]{1,0:T(8,128)(2,1)S(1)}, bf16[64,2048]{1,0:T(8,128)(2,1)S(1)}, u32[]{:S(2)}, u32[]{:S(2)}) collective-permute-start(bf16[64,2048]{1,0:T(8,128)(2,1)S(1)} %get-tuple-element.82), channel_id=1, source_target_pairs={{0,4},{4,0},{8,12},{12,8},{1,5},{5,1},{9,13},{13,9},{2,6},{6,2},{1... | collective-permute-start | bytes 786440 | tf_op jit(solution)/shard_map/ppermute | solution.py:135
  202.1 10.8 %collective-permute-start.14 = (bf16[1,32,7168]{2,1,0:T(8,128)(2,1)}, bf16[1,32,7168]{2,1,0:T(8,128)(2,1)S(1)}, u32[]{:S(2)}, u32[]{:S(2)}) collective-permute-start(bf16[1,32,7168]{2,1,0:T(8,128)(2,1)} %collective-permute-done.12.own_ref), channel_id=1, source_target_pairs={{0,1},{1,0},{2,3},{3,2},{4,5},{5,4},{6,7},{7,6},{8,9},{9,8},{10,11... | collective-permute-start | bytes 1376264 | tf_op jit(solution)/shard_map/ppermute | solution.py:129
  220.9 15.1 %collective-permute-start.18 = (bf16[1,32,7168]{2,1,0:T(8,128)(2,1)S(1)}, bf16[1,32,7168]{2,1,0:T(8,128)(2,1)S(1)}, u32[]{:S(2)}, u32[]{:S(2)}) collective-permute-start(bf16[1,32,7168]{2,1,0:T(8,128)(2,1)S(1)} %collective-permute-done.15.own_ref), channel_id=1, source_target_pairs={{0,1},{1,0},{2,3},{3,2},{4,5},{5,4},{6,7},{7,6},{8,9},{9,8},{10,11... | collective-permute-start | bytes 1376264 | tf_op jit(solution)/shard_map/ppermute | solution.py:129
  222.1 38.9 %collective-permute-start.22 = (f32[4,64,64]{2,1,0:T(8,128)S(1)}, f32[4,64,64]{2,1,0:T(8,128)S(1)}, u32[]{:S(2)}, u32[]{:S(2)}) collective-permute-start(f32[4,64,64]{2,1,0:T(8,128)S(1)} %bitcast.104), channel_id=1, source_target_pairs={{8,0},{12,4},{2,10},{6,14},{9,1},{13,5},{3,11},{7,15},{24,16},{28,... | collective-permute-start | bytes 196616 | tf_op jit(solution)/shard_map/ppermute | solution.py:144
  223.4 57.2 %collective-permute-start.28 = (bf16[1,64,2048]{2,1,0:T(8,128)(2,1)}, bf16[1,64,2048]{2,1,0:T(8,128)(2,1)}, u32[]{:S(2)}, u32[]{:S(2)}) collective-permute-start(bf16[1,64,2048]{2,1,0:T(8,128)(2,1)} %get-tuple-element.109), channel_id=1, source_target_pairs={{0,8},{4,12},{10,2},{14,6},{1,9},{5,13},{11,3},{15,7},{16,24},{20,... | collective-permute-start | bytes 786440 | tf_op jit(solution)/shard_map/ppermute | solution.py:144
  229.6 52.4 %collective-permute-start.29 = (bf16[1,64,2048]{2,1,0:T(8,128)(2,1)}, bf16[1,64,2048]{2,1,0:T(8,128)(2,1)}, u32[]{:S(2)}, u32[]{:S(2)}) collective-permute-start(bf16[1,64,2048]{2,1,0:T(8,128)(2,1)} %get-tuple-element.107), channel_id=1, source_target_pairs={{0,8},{4,12},{10,2},{14,6},{1,9},{5,13},{11,3},{15,7},{16,24},{20,... | collective-permute-start | bytes 786440 | tf_op jit(solution)/shard_map/ppermute | solution.py:144
  231.6 26.2 %collective-permute-start.30 = (bf16[32,2048]{1,0:T(8,128)(2,1)S(1)}, bf16[32,2048]{1,0:T(8,128)(2,1)S(1)}, u32[]{:S(2)}, u32[]{:S(2)}) collective-permute-start(bf16[32,2048]{1,0:T(8,128)(2,1)S(1)} %get-tuple-element.96), channel_id=1, source_target_pairs={{0,4},{4,0},{8,12},{12,8},{1,5},{5,1},{9,13},{13,9},{2,6},{6,2},{1... | collective-permute-start | bytes 393224 | tf_op jit(solution)/shard_map/ppermute | solution.py:135
  248.5 12.5 %collective-permute-start.20 = (f32[4,64,64]{2,1,0:T(8,128)S(1)}, f32[4,64,64]{2,1,0:T(8,128)S(1)}, u32[]{:S(2)}, u32[]{:S(2)}) collective-permute-start(f32[4,64,64]{2,1,0:T(8,128)S(1)} %bitcast.106), channel_id=1, source_target_pairs={{0,8},{4,12},{10,2},{14,6},{1,9},{5,13},{11,3},{15,7},{16,24},{20,... | collective-permute-start | bytes 196616 | tf_op jit(solution)/shard_map/ppermute | solution.py:144
  258.6 8.9 %collective-permute-start.32 = (bf16[32,2048]{1,0:T(8,128)(2,1)S(1)}, bf16[32,2048]{1,0:T(8,128)(2,1)S(1)}, u32[]{:S(2)}, u32[]{:S(2)}) collective-permute-start(bf16[32,2048]{1,0:T(8,128)(2,1)S(1)} %get-tuple-element.99), channel_id=1, source_target_pairs={{0,4},{4,0},{8,12},{12,8},{1,5},{5,1},{9,13},{13,9},{2,6},{6,2},{1... | collective-permute-start | bytes 393224 | tf_op jit(solution)/shard_map/ppermute | solution.py:135
  261.1 8.5 %collective-permute-start.23 = (bf16[4,64,64]{2,1,0:T(8,128)(2,1)S(1)}, bf16[4,64,64]{2,1,0:T(8,128)(2,1)S(1)}, u32[]{:S(2)}, u32[]{:S(2)}) collective-permute-start(bf16[4,64,64]{2,1,0:T(8,128)(2,1)S(1)} %fusion.45), channel_id=1, source_target_pairs={{0,1},{1,2},{2,3},{3,0},{4,5},{5,6},{6,7},{7,4},{8,9},{9,10},{10,1... | collective-permute-start | bytes 98312 | tf_op jit(solution)/shard_map/ppermute | solution.py:282
  261.2 10.5 %collective-permute-start.24 = (bf16[4,64,64]{2,1,0:T(8,128)(2,1)S(1)}, bf16[4,64,64]{2,1,0:T(8,128)(2,1)S(1)}, u32[]{:S(2)}, u32[]{:S(2)}) collective-permute-start(bf16[4,64,64]{2,1,0:T(8,128)(2,1)S(1)} %fusion.45), channel_id=1, source_target_pairs={{0,2},{1,3},{2,0},{3,1},{4,6},{5,7},{6,4},{7,5},{8,10},{9,11},{10,... | collective-permute-start | bytes 98312 | tf_op jit(solution)/shard_map/ppermute | solution.py:282
  269.6 14.5 %collective-permute-start.31 = (bf16[1,32,2048]{2,1,0:T(8,128)(2,1)}, bf16[1,32,2048]{2,1,0:T(8,128)(2,1)}, u32[]{:S(2)}, u32[]{:S(2)}) collective-permute-start(bf16[1,32,2048]{2,1,0:T(8,128)(2,1)} %get-tuple-element.114), channel_id=1, source_target_pairs={{0,8},{4,12},{10,2},{14,6},{1,9},{5,13},{11,3},{15,7},{16,24},{20,... | collective-permute-start | bytes 393224 | tf_op jit(solution)/shard_map/ppermute | solution.py:144
  271.7 13.7 %collective-permute-start.33 = (bf16[1,32,2048]{2,1,0:T(8,128)(2,1)}, bf16[1,32,2048]{2,1,0:T(8,128)(2,1)}, u32[]{:S(2)}, u32[]{:S(2)}) collective-permute-start(bf16[1,32,2048]{2,1,0:T(8,128)(2,1)} %get-tuple-element.112), channel_id=1, source_target_pairs={{0,8},{4,12},{10,2},{14,6},{1,9},{5,13},{11,3},{15,7},{16,24},{20,... | collective-permute-start | bytes 393224 | tf_op jit(solution)/shard_map/ppermute | solution.py:144
  (59 other events, 519.1 us)

commit v3 on v2

v3 whole, which is shorter than its diff:
```python
import functools

import jax
import jax.numpy as jnp
from jax import lax
from jax.experimental import pallas as pl
from jax.experimental.pallas import tpu as pltpu
from jax.sharding import PartitionSpec as P

ADAPTER_SCALE = 0.5
BLOCK_N = 256
BLOCK_VALUES = 1024 * 1024
BUFFERS = 4
VMEM_BYTES = 24 * 1024 * 1024


def block_depth(depth, width):
    for size in (1024, 512, 256):
        if depth % size == 0 and size * width <= BLOCK_VALUES:
            return size
    return depth


def matmul_body(first, left, pos_ref, own_ref, sib_ref, w_ref, a_ref, send_ref, keep_ref, *refs):
    rank_refs = refs[:-5]
    x_ref, w_buf, total_ref, x_sems, w_sems = refs[-5:]
    rows, width = send_ref.shape
    depth = w_ref.shape[0]
    _, steps, per_block, _ = x_ref.shape
    slots, _, rank = a_ref.shape
    buffers, block_k, _ = w_buf.shape
    block_n = min(BLOCK_N, width)
    count = depth // block_k

    def fetch(block, slot):
        return pltpu.make_async_copy(
            w_ref.at[pl.ds(block * block_k, block_k), pl.ds(left, width)], w_buf.at[slot], w_sems.at[slot]
        )

    own_at = pos_ref[0]
    own_copy = pltpu.make_async_copy(own_ref.at[pl.ds(first, steps)], x_ref.at[own_at], x_sems.at[0])
    sib_copy = pltpu.make_async_copy(sib_ref.at[pl.ds(first, steps)], x_ref.at[1 - own_at], x_sems.at[1])
    own_copy.start()
    sib_copy.start()
    for block in range(buffers):
        fetch(block, block).start()
    keep_ref[...] = jnp.zeros_like(keep_ref)
    total_ref[...] = jnp.zeros_like(total_ref)
    own_copy.wait()
    sib_copy.wait()
    if rank_refs:
        for slot in range(slots):
            x = x_ref[...].reshape(2 * rows, depth)
            part = jnp.dot(x, a_ref[slot], preferred_element_type=jnp.float32)
            rank_refs[0][:, slot * rank:(slot + 1) * rank] = part[:rows]
            rank_refs[1][:, slot * rank:(slot + 1) * rank] = part[rows:]

    @pl.loop(0, count)
    def _(block):
        slot = lax.rem(block, buffers)
        fetch(block, slot).wait()
        inner = pl.ds(pl.multiple_of(block * block_k, block_k), block_k)
        x = x_ref[:, :, :, inner].reshape(2 * rows, block_k)
        for place in range(width // block_n):
            columns = slice(place * block_n, (place + 1) * block_n)
            term = jnp.dot(x, w_buf[slot, :, columns], preferred_element_type=jnp.float32)
            total_ref[:, columns] += term[:rows]
            keep_ref[:, columns] += term[rows:]

        @pl.when(block + buffers < count)
        def _():
            fetch(block + buffers, slot).start()

    send_ref[...] = total_ref[...].astype(send_ref.dtype)


def partial_products(pos, own, sib, first, steps, weight, left, width, down_a, with_rank):
    _, per_block, depth = own.shape
    slots, _, rank = down_a.shape
    rows = steps * per_block
    block_k = block_depth(depth, width)
    buffers = min(BUFFERS, depth // block_k)
    any_spec = pl.BlockSpec(memory_space=pl.ANY)
    vmem_spec = pl.BlockSpec(memory_space=pltpu.VMEM)
    ranks = [jax.ShapeDtypeStruct((rows, slots * rank), jnp.float32)] * (2 if with_rank else 0)
    return pl.pallas_call(
        functools.partial(matmul_body, first, left),
        in_specs=[pl.BlockSpec(memory_space=pltpu.SMEM), any_spec, any_spec, any_spec, vmem_spec],
        out_specs=[vmem_spec] * (2 + len(ranks)),
        out_shape=[
            jax.ShapeDtypeStruct((rows, width), jnp.bfloat16),
            jax.ShapeDtypeStruct((rows, width), jnp.float32),
        ] + ranks,
        scratch_shapes=[
            pltpu.VMEM((2, steps, per_block, depth), jnp.bfloat16),
            pltpu.VMEM((buffers, block_k, width), jnp.bfloat16),
            pltpu.VMEM((rows, width), jnp.float32),
            pltpu.SemaphoreType.DMA((2,)),
            pltpu.SemaphoreType.DMA((buffers,)),
        ],
        compiler_params=pltpu.CompilerParams(vmem_limit_bytes=VMEM_BYTES),
        cost_estimate=pl.CostEstimate(flops=0, bytes_accessed=0, transcendentals=0),
        name="partial_products",
    )(pos, own, sib, weight, down_a)


def lift_body(chosen_ref, slot_ref, order_ref, panel_ref, out_ref):
    rank = chosen_ref.shape[1]
    chosen = chosen_ref[...]
    slot = slot_ref[...]
    spread = jnp.concatenate(
        [
            jnp.where(slot == order_ref[place], chosen, jnp.zeros_like(chosen))
            for place in range(panel_ref.shape[0] // rank)
        ],
        axis=1,
    )
    lifted = jnp.dot(spread, panel_ref[...], preferred_element_type=jnp.float32)
    out_ref[...] = lifted.astype(out_ref.dtype)


def lift(chosen, slots, order, panels):
    vmem_spec = pl.BlockSpec(memory_space=pltpu.VMEM)
    return pl.pallas_call(
        lift_body,
        in_specs=[vmem_spec, vmem_spec, pl.BlockSpec(memory_space=pltpu.SMEM), vmem_spec],
        out_specs=vmem_spec,
        out_shape=jax.ShapeDtypeStruct((chosen.shape[0], panels.shape[1]), jnp.bfloat16),
        compiler_params=pltpu.CompilerParams(vmem_limit_bytes=VMEM_BYTES),
        cost_estimate=pl.CostEstimate(flops=0, bytes_accessed=0, transcendentals=0),
        name="lift",
    )(chosen, slots, order, panels)


def per_device(hidden, base_weight, down_a, up_b, adapter_ids, owner_map):
    step_count, per_block, _ = hidden.shape
    n_tensor = lax.axis_size("tp")
    n_rep = lax.axis_size("rep")
    n_sub = lax.axis_size("sub")
    n_owners = n_rep * n_sub
    tensor_index = lax.axis_index("tp")
    rep_index = lax.axis_index("rep")
    sub_index = lax.axis_index("sub")
    owner_index = lax.axis_index(("rep", "sub"))
    requests = per_block * n_owners
    rows_mine = requests // n_tensor
    group = n_tensor // n_rep
    group_index = tensor_index // group
    owned_slots, _, rank_size = down_a.shape
    slot_count = owned_slots * n_owners
    width = base_weight.shape[1]

    def after(value, *done):
        return lax.optimization_barrier((value, *done))[0]

    def swap_cores(value):
        return lax.ppermute(value, "sub", [(i, i ^ 1) for i in range(n_sub)])

    def from_rep(value, shift):
        return lax.ppermute(value, "rep", [((i + shift) % n_rep, i) for i in range(n_rep)])

    def swap_tensor(value, bit):
        return lax.ppermute(value, "tp", [(i, i ^ bit) for i in range(n_tensor)])

    def to_group(value, shift, hop):
        pairs = []
        for rep in range(n_rep):
            target = (rep + shift) % n_rep
            source = (target + hop) % n_rep
            for low in range(group):
                pairs.append(((source * group + low) * n_rep + rep, (target * group + low) * n_rep + rep))
        return lax.ppermute(value, ("tp", "rep"), pairs)

    def halve(send, keep, steps, kind, *done):
        rows, columns = keep.shape
        total = (after(keep, *done) if done else keep) + swap_tensor(send, group // 2).astype(jnp.float32)
        extent, bit = rows // steps, group // 4
        while bit:
            extent //= 2
            halves = total.reshape(steps, 2, extent, columns)
            mine = (tensor_index // bit) % 2
            kept = lax.dynamic_index_in_dim(halves, mine, 1, keepdims=False)
            sent = lax.dynamic_index_in_dim(halves, 1 - mine, 1, keepdims=False)
            total = kept + swap_tensor(sent.astype(kind), bit).astype(jnp.float32)
            bit //= 2
        total = total.reshape(steps, extent, columns)
        return total, total.astype(kind)

    def collect(total, rounded, shift, *done):
        if done:
            total = after(total, *done)
        for hop in range(1, n_rep):
            total = total + to_group(rounded, shift, hop).astype(jnp.float32)
        return total

    def choose(local, others):
        value = local
        for shift, other in others:
            value = jnp.where(group_index == (rep_index + shift) % n_rep, other, value)
        return value

    keeps = (tensor_index // (group // 2)) % 2
    pos = (sub_index == keeps).astype(jnp.int32).reshape(1)

    remote = {}
    for step in range(step_count):
        for shift in range(1, n_rep):
            remote[step, shift] = from_rep(hidden[step:step + 1], shift)

    siblings = swap_cores(hidden)
    half = step_count // 2

    panels, bit = up_b, 1
    while bit < n_tensor:
        panels = jnp.concatenate([panels, swap_tensor(panels, bit)], axis=0)
        bit *= 2
    panels = panels.reshape(slot_count * rank_size, width)
    panel_slots = (
        (tensor_index ^ lax.broadcasted_iota(jnp.int32, (n_tensor, up_b.shape[0]), 0)) * up_b.shape[0]
        + lax.broadcasted_iota(jnp.int32, (n_tensor, up_b.shape[0]), 1)
    ).reshape(slot_count)

    my_ids = lax.dynamic_slice_in_dim(adapter_ids, tensor_index * rows_mine, rows_mine)
    iota = lax.broadcasted_iota(jnp.int32, (rows_mine, slot_count), 1)
    my_slot = jnp.sum((my_ids == iota).astype(jnp.int32) * owner_map[None, :], axis=1)
    owned_hot = my_slot[:, None] == (
        owner_index * owned_slots + lax.broadcasted_iota(jnp.int32, (rows_mine, owned_slots), 1)
    )

    local_halved, local_sums, local_ranks = {}, {}, {}
    remote_halved, remote_sums, remote_ranks = {}, {}, {}
    cuts = {step: [(0, width)] for step in range(step_count)}
    cuts[step_count - 1] = [(0, width // 2), (width // 2, width // 2)]

    def local_rows(index, *done):
        send, keep, *local_ranks[index] = partial_products(
            pos, hidden, after(siblings, *done), index * half, half, base_weight, 0, width, down_a, True
        )
        local_halved[index] = halve(send, keep, half, jnp.bfloat16)
        return local_ranks[index][1]

    def local_collect(index, *done):
        local_sums[index] = collect(*local_halved[index], 0, *done)

    def remote_rows(step, before, done):
        for shift in range(1, n_rep):
            own = after(remote[step, shift], *before)
            sib = after(swap_cores(own), *done)
            products = []
            for cut, (left, size) in enumerate(cuts[step]):
                send, keep, *ranks = partial_products(
                    pos, own, sib, 0, 1, base_weight, left, size, down_a, cut == 0
                )
                products.append((send, keep))
                if cut == 0:
                    remote_ranks[step, shift] = ranks
                    token = ranks[1]
                    before = (token,)
                    if len(cuts[step]) > 1:
                        remote_collect(step - 2, 0, token)
                        sib = after(sib, token, *summed(step - 2))
            held = ()
            if len(products) > 1:
                remote_collect(step - 1, 0, products[1][0])
                held = summed(step - 1)
            for cut, (send, keep) in enumerate(products):
                if cut > 0:
                    send = after(send, *held)
                remote_halved[step, cut, shift] = halve(send, keep, 1, jnp.bfloat16)
                held = (*held, remote_halved[step, cut, shift][1])
        return token, tuple(send for send, _ in products)

    def remote_collect(step, cut, *done):
        for shift in range(1, n_rep):
            remote_sums[step, cut, shift] = collect(*remote_halved[step, cut, shift], shift, *done)

    def halved(step, cut=0):
        return tuple(remote_halved[step, cut, shift][1] for shift in range(1, n_rep))

    def summed(step, cut=0):
        return tuple(remote_sums[step, cut, shift] for shift in range(1, n_rep))

    def rank_sums(ranks, shift):
        return collect(*halve(
            jnp.concatenate([rank[0] for rank in ranks]),
            jnp.concatenate([rank[1] for rank in ranks]),
            step_count, jnp.float32), shift)

    token = local_rows(0)
    token = local_rows(1, token, *(remote[0, shift] for shift in range(1, n_rep)))
    token, _ = remote_rows(0, (token, local_halved[0][1]), ())
    token, _ = remote_rows(1, (token, local_halved[1][1]), (panels,))
    local_rank_sum = rank_sums([local_ranks[index] for index in (0, 1)], 0)
    local_collect(0, token)
    token, _ = remote_rows(2, (token,), (*halved(0), local_sums[0], local_rank_sum))
    local_collect(1, token)
    remote_collect(0, 0, token)
    token, raw = remote_rows(3, (token, *halved(1)), (*halved(2), local_sums[1], *summed(0)))
    remote_collect(3, 0)
    remote_collect(3, 1)
    last = (*halved(3, 0), *raw)

    finished = choose(
        local_rank_sum,
        [
            (shift, rank_sums([[after(rank, *last) for rank in remote_ranks[step, shift]] for step in range(step_count)], shift))
            for shift in range(1, n_rep)
        ],
    ).astype(jnp.bfloat16)
    finished = after(finished, *halved(3, 1), *summed(3, 0))
    finished = finished.reshape(step_count, rows_mine, owned_slots, rank_size)
    masked = jnp.sum(
        jnp.where(owned_hot[None, :, :, None], finished, 0), axis=2, dtype=jnp.float32
    ).astype(jnp.bfloat16)
    chosen = masked
    for turn in range(1, n_owners):
        chosen = chosen + lax.ppermute(
            masked, ("rep", "sub"), [(i, (i + turn) % n_owners) for i in range(n_owners)]
        )
    lifted = lift(
        chosen.reshape(step_count * rows_mine, rank_size),
        jnp.broadcast_to(my_slot, (step_count, rows_mine)).reshape(step_count * rows_mine, 1),
        panel_slots,
        panels,
    ).reshape(step_count, rows_mine, width)

    output = jnp.zeros((step_count, rows_mine, width), jnp.bfloat16)
    for step in range(step_count):
        for cut, (left, size) in enumerate(cuts[step]):
            columns = slice(left, left + size)
            sums = choose(
                local_sums[step // half][step % half, :, columns],
                [(shift, remote_sums[step, cut, shift][0]) for shift in range(1, n_rep)],
            )
            value = sums + ADAPTER_SCALE * lifted[step, :, columns].astype(jnp.float32)
            output = output.at[step, :, columns].set(value.astype(jnp.bfloat16))
    return output


def solution(mesh):
    return jax.shard_map(
        per_device,
        mesh=mesh,
        in_specs=(
            P(None, ("groups", "rep", "sub"), "tp"),
            P("tp", ("rep", "sub")),
            P(("rep", "sub"), "tp", None),
            P("tp", None, ("rep", "sub")),
            P("groups", None),
            P(),
        ),
        out_specs=P(None, ("groups", "tp"), ("rep", "sub")),
        check_vma=False,
    )
```

time: 289 us -> 213 us (0.74)
  local copies, waits for them, and re-layouts: 80.2 us -> 12.8 us
  waiting for transfers between devices: 57.4 us -> 47.5 us
  matrix products: 6.31 us -> 0 us
  Pallas kernels: 73.4 us -> 78.5 us
    unnamed x115 -> x31, local copies, waits for them, and re-layouts: 68 us -> 8.9 us
    ppermute x11, waiting for transfers between devices: 46.4 us -> 27.3 us  [swap_tensor(): return lax.ppermute(value, 'tp', [(i, i ^ bit) for i in range(n_tensor)])]
    ppermute x11, starting transfers between devices: 12.7 us -> 23.5 us  [swap_tensor(): return lax.ppermute(value, 'tp', [(i, i ^ bit) for i in range(n_tensor)])]
    ppermute x9, starting transfers between devices: 30.3 us -> 20.8 us  [to_group(): return lax.ppermute(value, ('tp', 'rep'), pairs)]
    ppermute x9, waiting for transfers between devices: 10.9 us -> 19.9 us  [to_group(): return lax.ppermute(value, ('tp', 'rep'), pairs)]
    dot_general x5 -> x0, matrix products: 6.31 us -> none  [per_device(): jnp.dot(spread[step, span], panels, preferred_element_type=jnp.float32)]
    pallas_call x8, Pallas kernels: 73.4 us -> 78.5 us  [the longest x7 77.4 us: partial_products(): pl.pallas_call(functools.partial(matmul_body, first, left), in_specs=[pl....]
    squeeze x3 -> x0, local copies, waits for them, and re-layouts: 3.84 us -> none  [per_device(): spread[step, span]]
  transfers between devices with their start and end apart: 34 -> 32, of which waited for: 7 -> 9; matrix products, arithmetic and copies ran while one was open for 11% -> 10% of each run, Pallas kernels for 26% -> 37%
where the time goes in v3:
time: 213 us; the launch traced here: 212 us
  Pallas kernels  78.5 us (37%)
  starting transfers between devices  57.4 us (27%)
  waiting for transfers between devices  47.5 us (22%)
  other arithmetic  15.6 us (7%)
  local copies, waits for them, and re-layouts  12.8 us (6%)
    pallas_call x7, Pallas kernels, partial_products(): pl.pallas_call(functools.partial(matmul_body, first, left), in_specs=[pl....  77.4 us
    ppermute x11, waiting for transfers between devices, swap_tensor(): return lax.ppermute(value, 'tp', [(i, i ^ bit) for i in range(n_tensor)])  27.3 us
    ppermute x11, starting transfers between devices, swap_tensor(): return lax.ppermute(value, 'tp', [(i, i ^ bit) for i in range(n_tensor)])  23.5 us
    ppermute x9, starting transfers between devices, to_group(): return lax.ppermute(value, ('tp', 'rep'), pairs)  20.8 us
    ppermute x9, waiting for transfers between devices, to_group(): return lax.ppermute(value, ('tp', 'rep'), pairs)  19.9 us
    unnamed x31, local copies, waits for them, and re-layouts  8.9 us
    ppermute x3, starting transfers between devices, per_device(): lax.ppermute(masked, ('rep', 'sub'), [(i, (i + turn) % n_owners) for i in...  7.06 us
    ppermute x4, starting transfers between devices, from_rep(): lax.ppermute(value, 'rep', [((i + shift) % n_rep, i) for i in range(n_rep)])  5.36 us
  transfers between devices with their start and end apart: 32, of which 9 were waited for; matrix products, arithmetic and copies ran while one was open for 10% of the time, Pallas kernels for 37%

profile of v3, /device:TPU:0, one launch (start us, length us, event | category | flops | bytes accessed | tf_op | source)
XLA Modules:
  0.0 212.5 jit_solution(16742963595263601937)
XLA Ops:
  0.5 3.6 %fusion.34 = (bf16[1,64,7168]{2,1,0:T(8,128)(2,1)}, bf16[1,64,7168]{2,1,0:T(8,128)(2,1)}, bf16[1,64,7168]{2,1,0:T(8,128)(2,1)S(1)}, bf16[1,64,7168]{2,1,0:T(8,128)(2,1)}) fusion(bf16[4,64,7168]{2,1,0:T(8,128)(2,1)} %own_ref.3), kind=kLoop, calls=%fused_computation.67 | loop fusion | bytes 7340032 | tf_op jit(solution)/shard_map/slice | solution.py:208
  4.1 2.5 %collective-permute-start = (bf16[1,64,7168]{2,1,0:T(8,128)(2,1)S(1)}, bf16[1,64,7168]{2,1,0:T(8,128)(2,1)}, u32[]{:S(2)}, u32[]{:S(2)}) collective-permute-start(bf16[1,64,7168]{2,1,0:T(8,128)(2,1)S(1)} %get-tuple-element.167), channel_id=1, source_target_pairs={{2,0},{0,2},{3,1},{1,3},{6,4},{4,6},{7,5},{5,7},{10,8},{8,10},{11,... | collective-permute-start | bytes 2752520 | tf_op jit(solution)/shard_map/ppermute | solution.py:160
  6.6 1.9 copy.22.a_ref
  8.5 2.0 copy-done.2
  10.5 15.6 %partial_products.7 = (bf16[128,2048]{1,0:T(8,128)(2,1)}, f32[128,2048]{1,0:T(8,128)S(1)}, f32[128,64]{1,0:T(8,128)S(1)}, f32[128,64]{1,0:T(8,128)S(1)}) custom-call(s32[1]{0:T(128)} %bitcast.pos_ref, bf16[4,64,7168]{2,1,0:T(8,128)(2,1)S(1)} %copy-done.2, bf16[4,64,7168]{2,1,0:T(8,128)(2,1)} %collective-permute-done.1.sib_ref, bf16[7168,2048]{1,0:T(8,128)(2,1)} %w_ref.13, ...), custom_call_target="tpu_custom_call" | custom-call | tf_op jit(solution)/shard_map/partial_products/pallas_call | solution.py:86
  27.2 1.6 collective-permute-start.2
  31.4 2.0 copy-done.3
  33.4 15.7 %partial_products.8 = (bf16[128,2048]{1,0:T(8,128)(2,1)}, f32[128,2048]{1,0:T(8,128)S(1)}, f32[128,64]{1,0:T(8,128)S(1)}, f32[128,64]{1,0:T(8,128)S(1)}) custom-call(s32[1]{0:T(128)} %bitcast.pos_ref, bf16[4,64,7168]{2,1,0:T(8,128)(2,1)S(1)} %copy-done.3, bf16[4,64,7168]{2,1,0:T(8,128)(2,1)} %collective-permute-done.1.sib_ref, bf16[7168,2048]{1,0:T(8,128)(2,1)} %w_ref.13, ...), custom_call_target="tpu_custom_call" | custom-call | tf_op jit(solution)/shard_map/partial_products/pallas_call | solution.py:86
  49.1 1.7 collective-permute-start.7
  54.9 2.6 %collective-permute-start.10 = (bf16[2,64,2048]{2,1,0:T(8,128)(2,1)S(1)}, bf16[2,64,2048]{2,1,0:T(8,128)(2,1)S(1)}, u32[]{:S(2)}, u32[]{:S(2)}) collective-permute-start(bf16[2,64,2048]{2,1,0:T(8,128)(2,1)S(1)} %pad_maximum_fusion.1), channel_id=1, source_target_pairs={{0,8},{4,12},{8,0},{12,4},{1,9},{5,13},{9,1},{13,5},{2,10},{6,14},... | collective-permute-start | bytes 1572872 | tf_op jit(solution)/shard_map/ppermute | solution.py:163
  57.5 10.5 %collective-permute-done.7 = bf16[128,2048]{1,0:T(8,128)(2,1)} collective-permute-done((bf16[128,2048]{1,0:T(8,128)(2,1)}, bf16[128,2048]{1,0:T(8,128)(2,1)}, u32[]{:S(2)}, u32[]{:S(2)}) %collective-permute-start.7) | collective-permute-done | bytes 524320 | tf_op jit(solution)/shard_map/ppermute | solution.py:163
  69.3 12.2 %partial_products.9 = (bf16[64,2048]{1,0:T(8,128)(2,1)S(1)}, f32[64,2048]{1,0:T(8,128)S(1)}, f32[64,64]{1,0:T(8,128)S(1)}, f32[64,64]{1,0:T(8,128)S(1)}) custom-call(s32[1]{0:T(128)} %bitcast.pos_ref, bf16[1,64,7168]{2,1,0:T(8,128)(2,1)} %collective-permute-done.own_ref, bf16[1,64,7168]{2,1,0:T(8,128)(2,1)} %collective-permute-done.3.sib_ref, ...), custom_call_target="tpu_custom_call" | custom-call | tf_op jit(solution)/shard_map/partial_products/pallas_call | solution.py:86
  81.5 2.1 collective-permute-start.4
  87.3 6.0 %collective-permute-done.14 = f32[4,64,64]{2,1,0:T(8,128)S(1)} collective-permute-done((f32[4,64,64]{2,1,0:T(8,128)S(1)}, f32[4,64,64]{2,1,0:T(8,128)S(1)}, u32[]{:S(2)}, u32[]{:S(2)}) %collective-permute-start.14) | collective-permute-done | bytes 65568 | tf_op jit(solution)/shard_map/ppermute | solution.py:172
  95.6 5.5 %collective-permute-start.15 = (bf16[1,64,2048]{2,1,0:T(8,128)(2,1)S(1)}, bf16[1,64,2048]{2,1,0:T(8,128)(2,1)S(1)}, u32[]{:S(2)}, u32[]{:S(2)}) collective-permute-start(bf16[1,64,2048]{2,1,0:T(8,128)(2,1)S(1)} %get-tuple-element.173), channel_id=1, source_target_pairs={{0,8},{4,12},{10,2},{14,6},{1,9},{5,13},{11,3},{15,7},{16,24},{20,... | collective-permute-start | bytes 786440 | tf_op jit(solution)/shard_map/ppermute | solution.py:172
  101.1 10.5 %partial_products.10 = (bf16[64,2048]{1,0:T(8,128)(2,1)S(1)}, f32[64,2048]{1,0:T(8,128)S(1)}, f32[64,64]{1,0:T(8,128)S(1)}, f32[64,64]{1,0:T(8,128)S(1)}) custom-call(s32[1]{0:T(128)} %bitcast.pos_ref, bf16[1,64,7168]{2,1,0:T(8,128)(2,1)} %collective-permute-done.6.own_ref, bf16[1,64,7168]{2,1,0:T(8,128)(2,1)S(1)} %collective-permute-done.8.sib_ref, ...), custom_call_target="tpu_custom_call" | custom-call | tf_op jit(solution)/shard_map/partial_products/pallas_call | solution.py:86
  111.7 12.0 %collective-permute-done.12 = bf16[2,64,2048]{2,1,0:T(8,128)(2,1)S(1)} collective-permute-done((bf16[2,64,2048]{2,1,0:T(8,128)(2,1)S(1)}, bf16[2,64,2048]{2,1,0:T(8,128)(2,1)S(1)}, u32[]{:S(2)}, u32[]{:S(2)}) %collective-permute-start.12) | collective-permute-done | bytes 524320 | tf_op jit(solution)/shard_map/ppermute | solution.py:172
  123.7 12.7 %collective-permute-start.17 = (bf16[64,2048]{1,0:T(8,128)(2,1)S(1)}, bf16[64,2048]{1,0:T(8,128)(2,1)S(1)}, u32[]{:S(2)}, u32[]{:S(2)}) collective-permute-start(bf16[64,2048]{1,0:T(8,128)(2,1)S(1)} %get-tuple-element.137), channel_id=1, source_target_pairs={{0,4},{4,0},{8,12},{12,8},{1,5},{5,1},{9,13},{13,9},{2,6},{6,2},{1... | collective-permute-start | bytes 786440 | tf_op jit(solution)/shard_map/ppermute | solution.py:163
  137.5 7.9 %collective-permute-done.17 = bf16[64,2048]{1,0:T(8,128)(2,1)S(1)} collective-permute-done((bf16[64,2048]{1,0:T(8,128)(2,1)S(1)}, bf16[64,2048]{1,0:T(8,128)(2,1)S(1)}, u32[]{:S(2)}, u32[]{:S(2)}) %collective-permute-start.17) | collective-permute-done | bytes 262176 | tf_op jit(solution)/shard_map/ppermute | solution.py:163
  145.5 1.3 collective-permute-start.22
  146.8 10.5 %partial_products.11 = (bf16[64,2048]{1,0:T(8,128)(2,1)S(1)}, f32[64,2048]{1,0:T(8,128)S(1)}, f32[64,64]{1,0:T(8,128)S(1)}, f32[64,64]{1,0:T(8,128)S(1)}) custom-call(s32[1]{0:T(128)} %bitcast.pos_ref, bf16[1,64,7168]{2,1,0:T(8,128)(2,1)} %collective-permute-done.5.own_ref, bf16[1,64,7168]{2,1,0:T(8,128)(2,1)S(1)} %collective-permute-done.11.sib_ref, ...), custom_call_target="tpu_custom_call" | custom-call | tf_op jit(solution)/shard_map/partial_products/pallas_call | solution.py:86
  159.5 6.1 %collective-permute-done.19 = bf16[64,2048]{1,0:T(8,128)(2,1)S(1)} collective-permute-done((bf16[64,2048]{1,0:T(8,128)(2,1)S(1)}, bf16[64,2048]{1,0:T(8,128)(2,1)S(1)}, u32[]{:S(2)}, u32[]{:S(2)}) %collective-permute-start.19) | collective-permute-done | bytes 262176 | tf_op jit(solution)/shard_map/ppermute | solution.py:163
  165.7 1.5 collective-permute-start.25
  167.2 6.4 %partial_products.12 = (bf16[64,1024]{1,0:T(8,128)(2,1)S(1)}, f32[64,1024]{1,0:T(8,128)S(1)}, f32[64,64]{1,0:T(8,128)S(1)}, f32[64,64]{1,0:T(8,128)S(1)}) custom-call(s32[1]{0:T(128)} %bitcast.pos_ref, bf16[1,64,7168]{2,1,0:T(8,128)(2,1)S(1)} %collective-permute-done.16.own_ref, bf16[1,64,7168]{2,1,0:T(8,128)(2,1)S(1)} %collective-permute-done.18.sib_ref, ...), custom_call_target="tpu_custom_call" | custom-call | tf_op jit(solution)/shard_map/partial_products/pallas_call | solution.py:86
  173.7 2.1 collective-permute-start.21
  176.5 6.4 %partial_products.13 = (bf16[64,1024]{1,0:T(8,128)(2,1)S(1)}, f32[64,1024]{1,0:T(8,128)S(1)}) custom-call(s32[1]{0:T(128)} %bitcast.pos_ref, bf16[1,64,7168]{2,1,0:T(8,128)(2,1)S(1)} %collective-permute-done.16.own_ref, bf16[1,64,7168]{2,1,0:T(8,128)(2,1)S(1)} %collective-permute-done.18.sib_ref, bf16[7168,2048]{1,0:T(8,128)(2,1)} %w_ref.13, ...), custom_call_target="tpu_custom_call" | custom-call | tf_op jit(solution)/shard_map/partial_products/pallas_call | solution.py:86
  184.0 4.4 %collective-permute-start.27 = (bf16[1,64,1024]{2,1,0:T(8,128)(2,1)S(1)}, bf16[1,64,1024]{2,1,0:T(8,128)(2,1)S(1)}, u32[]{:S(2)}, u32[]{:S(2)}) collective-permute-start(bf16[1,64,1024]{2,1,0:T(8,128)(2,1)S(1)} %fusion.30), channel_id=1, source_target_pairs={{0,8},{4,12},{10,2},{14,6},{1,9},{5,13},{11,3},{15,7},{16,24},{20,... | collective-permute-start | bytes 393224 | tf_op jit(solution)/shard_map/ppermute | solution.py:172
  188.5 2.8 %collective-permute-start.24 = (f32[4,64,64]{2,1,0:T(8,128)S(1)}, f32[4,64,64]{2,1,0:T(8,128)S(1)}, u32[]{:S(2)}, u32[]{:S(2)}) collective-permute-start(f32[4,64,64]{2,1,0:T(8,128)S(1)} %bitcast.80), channel_id=1, source_target_pairs={{0,8},{4,12},{10,2},{14,6},{1,9},{5,13},{11,3},{15,7},{16,24},{20,... | collective-permute-start | bytes 196616 | tf_op jit(solution)/shard_map/ppermute | solution.py:172
  192.3 2.8 %collective-permute-done.26 = bf16[64,1024]{1,0:T(8,128)(2,1)S(1)} collective-permute-done((bf16[64,1024]{1,0:T(8,128)(2,1)S(1)}, bf16[64,1024]{1,0:T(8,128)(2,1)S(1)}, u32[]{:S(2)}, u32[]{:S(2)}) %collective-permute-start.26) | collective-permute-done | bytes 131104 | tf_op jit(solution)/shard_map/ppermute | solution.py:163
  196.9 5.6 %collective-permute-start.29 = (bf16[4,64,64]{2,1,0:T(8,128)(2,1)S(1)}, bf16[4,64,64]{2,1,0:T(8,128)(2,1)S(1)}, u32[]{:S(2)}, u32[]{:S(2)}) collective-permute-start(bf16[4,64,64]{2,1,0:T(8,128)(2,1)S(1)} %broadcast_select_fusion), channel_id=1, source_target_pairs={{0,2},{1,3},{2,0},{3,1},{4,6},{5,7},{6,4},{7,5},{8,10},{9,11},{10,... | collective-permute-start | bytes 98312 | tf_op jit(solution)/shard_map/ppermute | solution.py:317
  202.5 1.4 collective-permute-start.30
  204.0 1.5 collective-permute-start.31
  (109 shorter events, 30.5 us)
Async XLA Ops:
  0.0 8.5 %collective-permute-start.1 = (bf16[4,64,7168]{2,1,0:T(8,128)(2,1)}, bf16[4,64,7168]{2,1,0:T(8,128)(2,1)}, u32[]{:S(2)}, u32[]{:S(2)}) collective-permute-start(bf16[4,64,7168]{2,1,0:T(8,128)(2,1)} %own_ref.3), channel_id=1, source_target_pairs={{0,1},{1,0},{2,3},{3,2},{4,5},{5,4},{6,7},{7,6},{8,9},{9,8},{10,11... | collective-permute-start | bytes 11010056 | tf_op jit(solution)/shard_map/ppermute | solution.py:157
  4.1 27.3 %collective-permute-start = (bf16[1,64,7168]{2,1,0:T(8,128)(2,1)S(1)}, bf16[1,64,7168]{2,1,0:T(8,128)(2,1)}, u32[]{:S(2)}, u32[]{:S(2)}) collective-permute-start(bf16[1,64,7168]{2,1,0:T(8,128)(2,1)S(1)} %get-tuple-element.167), channel_id=1, source_target_pairs={{2,0},{0,2},{3,1},{1,3},{6,4},{4,6},{7,5},{5,7},{10,8},{8,10},{11,... | collective-permute-start | bytes 2752520 | tf_op jit(solution)/shard_map/ppermute | solution.py:160
  27.2 23.6 %collective-permute-start.2 = (bf16[128,2048]{1,0:T(8,128)(2,1)}, bf16[128,2048]{1,0:T(8,128)(2,1)}, u32[]{:S(2)}, u32[]{:S(2)}) collective-permute-start(bf16[128,2048]{1,0:T(8,128)(2,1)} %get-tuple-element.119), channel_id=1, source_target_pairs={{0,4},{4,0},{8,12},{12,8},{1,5},{5,1},{9,13},{13,9},{2,6},{6,2},{1... | collective-permute-start | bytes 1572872 | tf_op jit(solution)/shard_map/ppermute | solution.py:163
  28.8 52.7 %collective-permute-start.6 = (bf16[1,64,7168]{2,1,0:T(8,128)(2,1)}, bf16[1,64,7168]{2,1,0:T(8,128)(2,1)}, u32[]{:S(2)}, u32[]{:S(2)}) collective-permute-start(bf16[1,64,7168]{2,1,0:T(8,128)(2,1)} %get-tuple-element.168), channel_id=1, source_target_pairs={{2,0},{0,2},{3,1},{1,3},{6,4},{4,6},{7,5},{5,7},{10,8},{8,10},{11,... | collective-permute-start | bytes 2752520 | tf_op jit(solution)/shard_map/ppermute | solution.py:160
  29.9 23.9 %collective-permute-start.9 = (bf16[1,64,2048]{2,1,0:T(8,128)(2,1)S(1)}, bf16[1,64,2048]{2,1,0:T(8,128)(2,1)}, u32[]{:S(2)}, u32[]{:S(2)}) collective-permute-start(bf16[1,64,2048]{2,1,0:T(8,128)(2,1)S(1)} %copy-done.11), channel_id=1, source_target_pairs={{0,4},{4,0},{8,12},{12,8},{1,5},{5,1},{9,13},{13,9},{2,6},{6,2},{1... | collective-permute-start | bytes 786440 | tf_op jit(solution)/shard_map/ppermute | solution.py:163
  30.4 81.2 %collective-permute-start.5 = (bf16[1,64,7168]{2,1,0:T(8,128)(2,1)}, bf16[1,64,7168]{2,1,0:T(8,128)(2,1)}, u32[]{:S(2)}, u32[]{:S(2)}) collective-permute-start(bf16[1,64,7168]{2,1,0:T(8,128)(2,1)} %get-tuple-element.166), channel_id=1, source_target_pairs={{2,0},{0,2},{3,1},{1,3},{6,4},{4,6},{7,5},{5,7},{10,8},{8,10},{11,... | collective-permute-start | bytes 2752520 | tf_op jit(solution)/shard_map/ppermute | solution.py:160
  49.1 18.8 %collective-permute-start.7 = (bf16[128,2048]{1,0:T(8,128)(2,1)}, bf16[128,2048]{1,0:T(8,128)(2,1)}, u32[]{:S(2)}, u32[]{:S(2)}) collective-permute-start(bf16[128,2048]{1,0:T(8,128)(2,1)} %get-tuple-element.125), channel_id=1, source_target_pairs={{0,4},{4,0},{8,12},{12,8},{1,5},{5,1},{9,13},{13,9},{2,6},{6,2},{1... | collective-permute-start | bytes 1572872 | tf_op jit(solution)/shard_map/ppermute | solution.py:163
  53.8 15.4 %collective-permute-start.3 = (bf16[1,64,7168]{2,1,0:T(8,128)(2,1)}, bf16[1,64,7168]{2,1,0:T(8,128)(2,1)}, u32[]{:S(2)}, u32[]{:S(2)}) collective-permute-start(bf16[1,64,7168]{2,1,0:T(8,128)(2,1)} %collective-permute-done.own_ref), channel_id=1, source_target_pairs={{0,1},{1,0},{2,3},{3,2},{4,5},{5,4},{6,7},{7,6},{8,9},{9,8},{10,11... | collective-permute-start | bytes 2752520 | tf_op jit(solution)/shard_map/ppermute | solution.py:157
  54.9 30.1 %collective-permute-start.10 = (bf16[2,64,2048]{2,1,0:T(8,128)(2,1)S(1)}, bf16[2,64,2048]{2,1,0:T(8,128)(2,1)S(1)}, u32[]{:S(2)}, u32[]{:S(2)}) collective-permute-start(bf16[2,64,2048]{2,1,0:T(8,128)(2,1)S(1)} %pad_maximum_fusion.1), channel_id=1, source_target_pairs={{0,8},{4,12},{8,0},{12,4},{1,9},{5,13},{9,1},{13,5},{2,10},{6,14},... | collective-permute-start | bytes 1572872 | tf_op jit(solution)/shard_map/ppermute | solution.py:163
  68.0 15.6 %collective-permute-start.13 = (f32[256,64]{1,0:T(8,128)S(1)}, f32[256,64]{1,0:T(8,128)S(1)}, u32[]{:S(2)}, u32[]{:S(2)}) collective-permute-start(f32[256,64]{1,0:T(8,128)S(1)} %pad_maximum_fusion.2), channel_id=1, source_target_pairs={{0,4},{4,0},{8,12},{12,8},{1,5},{5,1},{9,13},{13,9},{2,6},{6,2},{1... | collective-permute-start | bytes 196616 | tf_op jit(solution)/shard_map/ppermute | solution.py:163
  81.5 14.1 %collective-permute-start.8 = (bf16[1,64,7168]{2,1,0:T(8,128)(2,1)}, bf16[1,64,7168]{2,1,0:T(8,128)(2,1)S(1)}, u32[]{:S(2)}, u32[]{:S(2)}) collective-permute-start(bf16[1,64,7168]{2,1,0:T(8,128)(2,1)} %collective-permute-done.6.own_ref), channel_id=1, source_target_pairs={{0,1},{1,0},{2,3},{3,2},{4,5},{5,4},{6,7},{7,6},{8,9},{9,8},{10,11... | collective-permute-start | bytes 2752520 | tf_op jit(solution)/shard_map/ppermute | solution.py:157
  81.5 12.6 %collective-permute-start.4 = (bf16[64,2048]{1,0:T(8,128)(2,1)S(1)}, bf16[64,2048]{1,0:T(8,128)(2,1)S(1)}, u32[]{:S(2)}, u32[]{:S(2)}) collective-permute-start(bf16[64,2048]{1,0:T(8,128)(2,1)S(1)} %get-tuple-element.122), channel_id=1, source_target_pairs={{0,4},{4,0},{8,12},{12,8},{1,5},{5,1},{9,13},{13,9},{2,6},{6,2},{1... | collective-permute-start | bytes 786440 | tf_op jit(solution)/shard_map/ppermute | solution.py:163
  83.6 9.6 %collective-permute-start.14 = (f32[4,64,64]{2,1,0:T(8,128)S(1)}, f32[4,64,64]{2,1,0:T(8,128)S(1)}, u32[]{:S(2)}, u32[]{:S(2)}) collective-permute-start(f32[4,64,64]{2,1,0:T(8,128)S(1)} %bitcast.82), channel_id=1, source_target_pairs={{8,0},{12,4},{2,10},{6,14},{9,1},{13,5},{3,11},{7,15},{24,16},{28,... | collective-permute-start | bytes 196616 | tf_op jit(solution)/shard_map/ppermute | solution.py:172
  85.0 38.8 %collective-permute-start.12 = (bf16[2,64,2048]{2,1,0:T(8,128)(2,1)S(1)}, bf16[2,64,2048]{2,1,0:T(8,128)(2,1)S(1)}, u32[]{:S(2)}, u32[]{:S(2)}) collective-permute-start(bf16[2,64,2048]{2,1,0:T(8,128)(2,1)S(1)} %copy-done.13), channel_id=1, source_target_pairs={{8,0},{12,4},{2,10},{6,14},{9,1},{13,5},{3,11},{7,15},{24,16},{28,... | collective-permute-start | bytes 1572872 | tf_op jit(solution)/shard_map/ppermute | solution.py:172
  93.3 64.1 %collective-permute-start.16 = (bf16[1,64,7168]{2,1,0:T(8,128)(2,1)S(1)}, bf16[1,64,7168]{2,1,0:T(8,128)(2,1)S(1)}, u32[]{:S(2)}, u32[]{:S(2)}) collective-permute-start(bf16[1,64,7168]{2,1,0:T(8,128)(2,1)S(1)} %copy-done.12), channel_id=1, source_target_pairs={{2,0},{0,2},{3,1},{1,3},{6,4},{4,6},{7,5},{5,7},{10,8},{8,10},{11,... | collective-permute-start | bytes 2752520 | tf_op jit(solution)/shard_map/ppermute | solution.py:160
  94.2 63.4 %collective-permute-start.20 = (bf16[2,64,2048]{2,1,0:T(8,128)(2,1)S(1)}, bf16[2,64,2048]{2,1,0:T(8,128)(2,1)S(1)}, u32[]{:S(2)}, u32[]{:S(2)}) collective-permute-start(bf16[2,64,2048]{2,1,0:T(8,128)(2,1)S(1)} %convert_element_type.126), channel_id=1, source_target_pairs={{8,0},{12,4},{2,10},{6,14},{9,1},{13,5},{3,11},{7,15},{24,16},{28,... | collective-permute-start | bytes 1572872 | tf_op jit(solution)/shard_map/ppermute | solution.py:172
  95.6 63.1 %collective-permute-start.15 = (bf16[1,64,2048]{2,1,0:T(8,128)(2,1)S(1)}, bf16[1,64,2048]{2,1,0:T(8,128)(2,1)S(1)}, u32[]{:S(2)}, u32[]{:S(2)}) collective-permute-start(bf16[1,64,2048]{2,1,0:T(8,128)(2,1)S(1)} %get-tuple-element.173), channel_id=1, source_target_pairs={{0,8},{4,12},{10,2},{14,6},{1,9},{5,13},{11,3},{15,7},{16,24},{20,... | collective-permute-start | bytes 786440 | tf_op jit(solution)/shard_map/ppermute | solution.py:172
  111.6 35.2 %collective-permute-start.11 = (bf16[1,64,7168]{2,1,0:T(8,128)(2,1)}, bf16[1,64,7168]{2,1,0:T(8,128)(2,1)S(1)}, u32[]{:S(2)}, u32[]{:S(2)}) collective-permute-start(bf16[1,64,7168]{2,1,0:T(8,128)(2,1)} %collective-permute-done.5.own_ref), channel_id=1, source_target_pairs={{0,1},{1,0},{2,3},{3,2},{4,5},{5,4},{6,7},{7,6},{8,9},{9,8},{10,11... | collective-permute-start | bytes 2752520 | tf_op jit(solution)/shard_map/ppermute | solution.py:157
  123.7 21.7 %collective-permute-start.17 = (bf16[64,2048]{1,0:T(8,128)(2,1)S(1)}, bf16[64,2048]{1,0:T(8,128)(2,1)S(1)}, u32[]{:S(2)}, u32[]{:S(2)}) collective-permute-start(bf16[64,2048]{1,0:T(8,128)(2,1)S(1)} %get-tuple-element.137), channel_id=1, source_target_pairs={{0,4},{4,0},{8,12},{12,8},{1,5},{5,1},{9,13},{13,9},{2,6},{6,2},{1... | collective-permute-start | bytes 786440 | tf_op jit(solution)/shard_map/ppermute | solution.py:163
  145.5 30.2 %collective-permute-start.22 = (bf16[1,64,2048]{2,1,0:T(8,128)(2,1)S(1)}, bf16[1,64,2048]{2,1,0:T(8,128)(2,1)S(1)}, u32[]{:S(2)}, u32[]{:S(2)}) collective-permute-start(bf16[1,64,2048]{2,1,0:T(8,128)(2,1)S(1)} %get-tuple-element.172), channel_id=1, source_target_pairs={{0,8},{4,12},{10,2},{14,6},{1,9},{5,13},{11,3},{15,7},{16,24},{20,... | collective-permute-start | bytes 786440 | tf_op jit(solution)/shard_map/ppermute | solution.py:172
  157.3 8.4 %collective-permute-start.19 = (bf16[64,2048]{1,0:T(8,128)(2,1)S(1)}, bf16[64,2048]{1,0:T(8,128)(2,1)S(1)}, u32[]{:S(2)}, u32[]{:S(2)}) collective-permute-start(bf16[64,2048]{1,0:T(8,128)(2,1)S(1)} %get-tuple-element.140), channel_id=1, source_target_pairs={{0,4},{4,0},{8,12},{12,8},{1,5},{5,1},{9,13},{13,9},{2,6},{6,2},{1... | collective-permute-start | bytes 786440 | tf_op jit(solution)/shard_map/ppermute | solution.py:163
  157.4 9.9 %collective-permute-start.18 = (bf16[1,64,7168]{2,1,0:T(8,128)(2,1)S(1)}, bf16[1,64,7168]{2,1,0:T(8,128)(2,1)S(1)}, u32[]{:S(2)}, u32[]{:S(2)}) collective-permute-start(bf16[1,64,7168]{2,1,0:T(8,128)(2,1)S(1)} %collective-permute-done.16.own_ref), channel_id=1, source_target_pairs={{0,1},{1,0},{2,3},{3,2},{4,5},{5,4},{6,7},{7,6},{8,9},{9,8},{10,11... | collective-permute-start | bytes 2752520 | tf_op jit(solution)/shard_map/ppermute | solution.py:157
  165.7 17.4 %collective-permute-start.25 = (bf16[1,64,2048]{2,1,0:T(8,128)(2,1)S(1)}, bf16[1,64,2048]{2,1,0:T(8,128)(2,1)S(1)}, u32[]{:S(2)}, u32[]{:S(2)}) collective-permute-start(bf16[1,64,2048]{2,1,0:T(8,128)(2,1)S(1)} %get-tuple-element.170), channel_id=1, source_target_pairs={{0,8},{4,12},{10,2},{14,6},{1,9},{5,13},{11,3},{15,7},{16,24},{20,... | collective-permute-start | bytes 786440 | tf_op jit(solution)/shard_map/ppermute | solution.py:172
  173.7 9.3 %collective-permute-start.21 = (bf16[64,1024]{1,0:T(8,128)(2,1)S(1)}, bf16[64,1024]{1,0:T(8,128)(2,1)S(1)}, u32[]{:S(2)}, u32[]{:S(2)}) collective-permute-start(bf16[64,1024]{1,0:T(8,128)(2,1)S(1)} %get-tuple-element.144), channel_id=1, source_target_pairs={{0,4},{4,0},{8,12},{12,8},{1,5},{5,1},{9,13},{13,9},{2,6},{6,2},{1... | collective-permute-start | bytes 393224 | tf_op jit(solution)/shard_map/ppermute | solution.py:163
  183.0 5.5 %collective-permute-start.23 = (f32[256,64]{1,0:T(8,128)S(1)}, f32[256,64]{1,0:T(8,128)S(1)}, u32[]{:S(2)}, u32[]{:S(2)}) collective-permute-start(f32[256,64]{1,0:T(8,128)S(1)} %pad_maximum_fusion.3), channel_id=1, source_target_pairs={{0,4},{4,0},{8,12},{12,8},{1,5},{5,1},{9,13},{13,9},{2,6},{6,2},{1... | collective-permute-start | bytes 196616 | tf_op jit(solution)/shard_map/ppermute | solution.py:163
  184.0 8.3 %collective-permute-start.27 = (bf16[1,64,1024]{2,1,0:T(8,128)(2,1)S(1)}, bf16[1,64,1024]{2,1,0:T(8,128)(2,1)S(1)}, u32[]{:S(2)}, u32[]{:S(2)}) collective-permute-start(bf16[1,64,1024]{2,1,0:T(8,128)(2,1)S(1)} %fusion.30), channel_id=1, source_target_pairs={{0,8},{4,12},{10,2},{14,6},{1,9},{5,13},{11,3},{15,7},{16,24},{20,... | collective-permute-start | bytes 393224 | tf_op jit(solution)/shard_map/ppermute | solution.py:172
  188.4 6.7 %collective-permute-start.26 = (bf16[64,1024]{1,0:T(8,128)(2,1)S(1)}, bf16[64,1024]{1,0:T(8,128)(2,1)S(1)}, u32[]{:S(2)}, u32[]{:S(2)}) collective-permute-start(bf16[64,1024]{1,0:T(8,128)(2,1)S(1)} %get-tuple-element.163), channel_id=1, source_target_pairs={{0,4},{4,0},{8,12},{12,8},{1,5},{5,1},{9,13},{13,9},{2,6},{6,2},{1... | collective-permute-start | bytes 393224 | tf_op jit(solution)/shard_map/ppermute | solution.py:163
  188.5 8.2 %collective-permute-start.24 = (f32[4,64,64]{2,1,0:T(8,128)S(1)}, f32[4,64,64]{2,1,0:T(8,128)S(1)}, u32[]{:S(2)}, u32[]{:S(2)}) collective-permute-start(f32[4,64,64]{2,1,0:T(8,128)S(1)} %bitcast.80), channel_id=1, source_target_pairs={{0,8},{4,12},{10,2},{14,6},{1,9},{5,13},{11,3},{15,7},{16,24},{20,... | collective-permute-start | bytes 196616 | tf_op jit(solution)/shard_map/ppermute | solution.py:172
  196.8 8.7 %collective-permute-start.28 = (bf16[4,64,64]{2,1,0:T(8,128)(2,1)S(1)}, bf16[4,64,64]{2,1,0:T(8,128)(2,1)S(1)}, u32[]{:S(2)}, u32[]{:S(2)}) collective-permute-start(bf16[4,64,64]{2,1,0:T(8,128)(2,1)S(1)} %broadcast_select_fusion), channel_id=1, source_target_pairs={{0,1},{1,2},{2,3},{3,0},{4,5},{5,6},{6,7},{7,4},{8,9},{9,10},{10,1... | collective-permute-start | bytes 98312 | tf_op jit(solution)/shard_map/ppermute | solution.py:317
  196.9 8.6 %collective-permute-start.29 = (bf16[4,64,64]{2,1,0:T(8,128)(2,1)S(1)}, bf16[4,64,64]{2,1,0:T(8,128)(2,1)S(1)}, u32[]{:S(2)}, u32[]{:S(2)}) collective-permute-start(bf16[4,64,64]{2,1,0:T(8,128)(2,1)S(1)} %broadcast_select_fusion), channel_id=1, source_target_pairs={{0,2},{1,3},{2,0},{3,1},{4,6},{5,7},{6,4},{7,5},{8,10},{9,11},{10,... | collective-permute-start | bytes 98312 | tf_op jit(solution)/shard_map/ppermute | solution.py:317
  202.5 3.3 %collective-permute-start.30 = (bf16[4,64,64]{2,1,0:T(8,128)(2,1)S(1)}, bf16[4,64,64]{2,1,0:T(8,128)(2,1)S(1)}, u32[]{:S(2)}, u32[]{:S(2)}) collective-permute-start(bf16[4,64,64]{2,1,0:T(8,128)(2,1)S(1)} %broadcast_select_fusion), channel_id=1, source_target_pairs={{0,3},{1,0},{2,1},{3,2},{4,7},{5,4},{6,5},{7,6},{8,11},{9,8},{10,9... | collective-permute-start | bytes 98312 | tf_op jit(solution)/shard_map/ppermute | solution.py:317
  204.0 6.7 %collective-permute-start.31 = (bf16[1,64,1024]{2,1,0:T(8,128)(2,1)}, bf16[1,64,1024]{2,1,0:T(8,128)(2,1)S(1)}, u32[]{:S(2)}, u32[]{:S(2)}) collective-permute-start(bf16[1,64,1024]{2,1,0:T(8,128)(2,1)} %fusion.29), channel_id=1, source_target_pairs={{0,8},{4,12},{10,2},{14,6},{1,9},{5,13},{11,3},{15,7},{16,24},{20,... | collective-permute-start | bytes 393224 | tf_op jit(solution)/shard_map/ppermute | solution.py:172
  (15 other events, 206.4 us)

commit v4 on v3

v4 whole, which is shorter than its diff:
```python
import functools

import jax
import jax.numpy as jnp
from jax import lax
from jax.experimental import pallas as pl
from jax.experimental.pallas import tpu as pltpu
from jax.sharding import PartitionSpec as P

ADAPTER_SCALE = 0.5
BLOCK_N = 256
BLOCK_VALUES = 1024 * 1024
BUFFERS = 3
WIDE_ROWS = 128
VMEM_BYTES = 24 * 1024 * 1024


def block_depth(depth, width, rows):
    values = BLOCK_VALUES * (2 if rows >= WIDE_ROWS else 1)
    for size in (1024, 512, 256):
        if depth % size == 0 and size * width <= values:
            return size
    return depth


def matmul_body(spans, left, pos_ref, *refs):
    sources = refs[:2 * len(spans)]
    w_ref, a_ref, send_ref, keep_ref = refs[2 * len(spans):2 * len(spans) + 4]
    rank_refs = refs[2 * len(spans) + 4:-5]
    x_ref, w_buf, total_ref, x_sems, w_sems = refs[-5:]
    rows, width = send_ref.shape
    depth = w_ref.shape[0]
    slots, rank, _ = a_ref.shape
    buffers, block_k, _ = w_buf.shape
    block_n = min(BLOCK_N, width)
    count = depth // block_k

    def fetch(block, slot):
        return pltpu.make_async_copy(
            w_ref.at[pl.ds(block * block_k, block_k), pl.ds(left, width)], w_buf.at[slot], w_sems.at[slot]
        )

    own_at = pos_ref[0]
    copies, begin = [], 0
    for index, (first, steps) in enumerate(spans):
        for core, at in enumerate((own_at, 1 - own_at)):
            source = sources[2 * index + core]
            copies.append(pltpu.make_async_copy(
                source.at[pl.ds(first, steps)], x_ref.at[at, pl.ds(begin, steps)], x_sems.at[2 * index + core]
            ))
        begin += steps
    for copy in copies:
        copy.start()
    for block in range(buffers):
        fetch(block, block).start()
    keep_ref[...] = jnp.zeros_like(keep_ref)
    total_ref[...] = jnp.zeros_like(total_ref)
    for copy in copies:
        copy.wait()
    if rank_refs:
        for slot in range(slots):
            x = x_ref[...].reshape(2 * rows, depth)
            part = lax.dot_general(
                x, a_ref[slot], (((1,), (1,)), ((), ())), preferred_element_type=jnp.float32
            )
            rank_refs[0][:, slot * rank:(slot + 1) * rank] = part[:rows]
            rank_refs[1][:, slot * rank:(slot + 1) * rank] = part[rows:]

    @pl.loop(0, count)
    def _(block):
        slot = lax.rem(block, buffers)
        fetch(block, slot).wait()
        inner = pl.ds(pl.multiple_of(block * block_k, block_k), block_k)
        x = x_ref[:, :, :, inner].reshape(2 * rows, block_k)
        for place in range(width // block_n):
            columns = slice(place * block_n, (place + 1) * block_n)
            term = jnp.dot(x, w_buf[slot, :, columns], preferred_element_type=jnp.float32)
            total_ref[:, columns] += term[:rows]
            keep_ref[:, columns] += term[rows:]

        @pl.when(block + buffers < count)
        def _():
            fetch(block + buffers, slot).start()

    send_ref[...] = total_ref[...].astype(send_ref.dtype)


def partial_products(pos, chunks, weight, left, width, factors, with_rank):
    _, per_block, depth = chunks[0][0].shape
    slots, rank, _ = factors.shape
    spans = tuple((first, steps) for _, _, first, steps in chunks)
    steps = sum(length for _, length in spans)
    rows = steps * per_block
    block_k = block_depth(depth, width, rows)
    buffers = min(BUFFERS, depth // block_k)
    any_spec = pl.BlockSpec(memory_space=pl.ANY)
    vmem_spec = pl.BlockSpec(memory_space=pltpu.VMEM)
    ranks = [jax.ShapeDtypeStruct((rows, slots * rank), jnp.float32)] * (2 if with_rank else 0)
    return pl.pallas_call(
        functools.partial(matmul_body, spans, left),
        in_specs=[pl.BlockSpec(memory_space=pltpu.SMEM)] + [any_spec] * (2 * len(chunks) + 1) + [vmem_spec],
        out_specs=[vmem_spec] * (2 + len(ranks)),
        out_shape=[
            jax.ShapeDtypeStruct((rows, width), jnp.bfloat16),
            jax.ShapeDtypeStruct((rows, width), jnp.float32),
        ] + ranks,
        scratch_shapes=[
            pltpu.VMEM((2, steps, per_block, depth), jnp.bfloat16),
            pltpu.VMEM((buffers, block_k, width), jnp.bfloat16),
            pltpu.VMEM((rows, width), jnp.float32),
            pltpu.SemaphoreType.DMA((2 * len(chunks),)),
            pltpu.SemaphoreType.DMA((buffers,)),
        ],
        compiler_params=pltpu.CompilerParams(vmem_limit_bytes=VMEM_BYTES),
        cost_estimate=pl.CostEstimate(flops=0, bytes_accessed=0, transcendentals=0),
        name="partial_products",
    )(pos, *[source for own, sib, _, _ in chunks for source in (own, sib)], weight, factors)


def lift_body(chosen_ref, slot_ref, order_ref, panel_ref, out_ref):
    rank = chosen_ref.shape[1]
    chosen = chosen_ref[...]
    slot = slot_ref[...]
    spread = jnp.concatenate(
        [
            jnp.where(slot == order_ref[place], chosen, jnp.zeros_like(chosen))
            for place in range(panel_ref.shape[0] // rank)
        ],
        axis=1,
    )
    lifted = jnp.dot(spread, panel_ref[...], preferred_element_type=jnp.float32)
    out_ref[...] = lifted.astype(out_ref.dtype)


def lift(chosen, slots, order, panels):
    vmem_spec = pl.BlockSpec(memory_space=pltpu.VMEM)
    return pl.pallas_call(
        lift_body,
        in_specs=[vmem_spec, vmem_spec, pl.BlockSpec(memory_space=pltpu.SMEM), vmem_spec],
        out_specs=vmem_spec,
        out_shape=jax.ShapeDtypeStruct((chosen.shape[0], panels.shape[1]), jnp.bfloat16),
        compiler_params=pltpu.CompilerParams(vmem_limit_bytes=VMEM_BYTES),
        cost_estimate=pl.CostEstimate(flops=0, bytes_accessed=0, transcendentals=0),
        name="lift",
    )(chosen, slots, order, panels)


def per_device(hidden, base_weight, down_a, up_b, adapter_ids, owner_map):
    step_count, per_block, _ = hidden.shape
    n_tensor = lax.axis_size("tp")
    n_rep = lax.axis_size("rep")
    n_sub = lax.axis_size("sub")
    n_owners = n_rep * n_sub
    tensor_index = lax.axis_index("tp")
    rep_index = lax.axis_index("rep")
    sub_index = lax.axis_index("sub")
    owner_index = lax.axis_index(("rep", "sub"))
    requests = per_block * n_owners
    rows_mine = requests // n_tensor
    group = n_tensor // n_rep
    group_index = tensor_index // group
    owned_slots, _, rank_size = down_a.shape
    slot_count = owned_slots * n_owners
    width = base_weight.shape[1]

    def after(value, *done):
        return lax.optimization_barrier((value, *done))[0]

    def swap_cores(value):
        return lax.ppermute(value, "sub", [(i, i ^ 1) for i in range(n_sub)])

    def from_rep(value, shift):
        return lax.ppermute(value, "rep", [((i + shift) % n_rep, i) for i in range(n_rep)])

    def swap_tensor(value, bit):
        return lax.ppermute(value, "tp", [(i, i ^ bit) for i in range(n_tensor)])

    def to_group(value, shift, hop):
        pairs = []
        for rep in range(n_rep):
            target = (rep + shift) % n_rep
            source = (target + hop) % n_rep
            for low in range(group):
                pairs.append(((source * group + low) * n_rep + rep, (target * group + low) * n_rep + rep))
        return lax.ppermute(value, ("tp", "rep"), pairs)

    def choose(local, others):
        value = local
        for shift, other in others:
            value = jnp.where(group_index == (rep_index + shift) % n_rep, other, value)
        return value

    keeps = (tensor_index // (group // 2)) % 2
    pos = (sub_index == keeps).astype(jnp.int32).reshape(1)

    siblings = swap_cores(hidden)
    pieces = [(step, shift) for step in range(step_count) for shift in range(1, n_rep)]
    remote = {}
    for step, shift in pieces:
        source = hidden if step == 0 else after(hidden, siblings)
        remote[step, shift] = from_rep(source[step:step + 1], shift)

    panels, bit = up_b, 1
    while bit < n_tensor:
        panels = jnp.concatenate([panels, swap_tensor(panels, bit)], axis=0)
        bit *= 2
    panels = panels.reshape(slot_count * rank_size, width)
    panel_slots = (
        (tensor_index ^ lax.broadcasted_iota(jnp.int32, (n_tensor, up_b.shape[0]), 0)) * up_b.shape[0]
        + lax.broadcasted_iota(jnp.int32, (n_tensor, up_b.shape[0]), 1)
    ).reshape(slot_count)

    my_ids = lax.dynamic_slice_in_dim(adapter_ids, tensor_index * rows_mine, rows_mine)
    iota = lax.broadcasted_iota(jnp.int32, (rows_mine, slot_count), 1)
    my_slot = jnp.sum((my_ids == iota).astype(jnp.int32) * owner_map[None, :], axis=1)
    owned_hot = my_slot[:, None] == (
        owner_index * owned_slots + lax.broadcasted_iota(jnp.int32, (rows_mine, owned_slots), 1)
    )

    first_leg, second_leg, sums = [], [], {}

    def second_half(total, received, steps, kind):
        total = total + received.astype(jnp.float32)
        rows, columns = total.shape
        extent, bit = rows // steps, group // 4
        while bit:
            extent //= 2
            halves = total.reshape(steps, 2, extent, columns)
            mine = (tensor_index // bit) % 2
            kept = lax.dynamic_index_in_dim(halves, mine, 1, keepdims=False)
            sent = lax.dynamic_index_in_dim(halves, 1 - mine, 1, keepdims=False)
            total = kept + swap_tensor(sent.astype(kind), bit).astype(jnp.float32)
            bit //= 2
        return total.reshape(steps, extent, columns)

    def gap(token, jobs, *extra, short=False):
        nonlocal first_leg, second_leg
        halved = []
        for parts, received, keep, kind in first_leg:
            steps = sum(length for _, length, _ in parts)
            total, begin = second_half(after(keep, token), received, steps, kind), 0
            for key, length, shift in parts:
                part = total[begin:begin + length]
                halved.append((key, part, part.astype(kind), shift))
                begin += length
        waiting, ended = [], {}
        for key, received, total, lag in second_leg:
            if short or lag > 1:
                waiting.append((key, received, total, lag if short else lag - 1))
                continue
            total = after(total, token)
            for value in received:
                total = total + value.astype(jnp.float32)
            ended[key] = total
        sends = [job[1] for job in jobs]
        rounded = [value for _, _, value, _ in halved]
        sends, rounded, extra, totals = lax.optimization_barrier((sends, rounded, extra, list(ended.values())))
        sums.update(zip(ended, totals))
        first_leg = [
            (parts, swap_tensor(send, group // 2), keep, kind) for (parts, _, keep, kind), send in zip(jobs, sends)
        ]
        second_leg = waiting + [
            (key, [to_group(value, shift, hop) for hop in range(1, n_rep)], total, 2 if short else 1)
            for (key, total, _, shift), value in zip(halved, rounded)
        ]
        return extra

    factors = jnp.swapaxes(down_a, 1, 2)

    def multiply(chunks, left=0, columns=width, with_rank=True):
        return partial_products(pos, chunks, base_weight, left, columns, factors, with_rank)

    half = step_count // 2
    send, keep, *ranks = multiply([(hidden, siblings, 0, half)])
    rank_rows = {("local", 0): ranks}
    jobs = [([(("local", 0), half, 0)], send, keep, jnp.bfloat16)]
    token, next_local, rank_jobs = ranks[1], half, []
    for piece, (step, shift) in enumerate(pieces):
        own, siblings, panels = gap(token, jobs + rank_jobs, remote[step, shift], siblings, panels)
        rank_jobs = []
        sib = swap_cores(own)
        if piece == len(pieces) - 1:
            own, sib = gap(token, [], own, sib, short=True)
            cuts = [(0, width // 2), (width // 2, width // 2)]
            send, keep, *rank_rows[step, shift] = multiply([(own, sib, 0, 1)], *cuts[0])
            token = rank_rows[step, shift][1]
            jobs = [([((step, shift, 0), 1, shift)], send, keep, jnp.bfloat16)]
            for along in range(1, n_rep):
                both = [jnp.concatenate([rank_rows[at, along][side] for at in range(step_count)]) for side in (0, 1)]
                jobs.append(([(("ranks", along), step_count, along)], *both, jnp.float32))
            own, sib = gap(token, jobs, own, sib)
            send, keep = multiply([(own, sib, 0, 1)], *cuts[1], with_rank=False)
            token = send
            jobs = [([((step, shift, 1), 1, shift)], send, keep, jnp.bfloat16)]
            break
        chunks, parts = [(own, sib, 0, 1)], [((step, shift, 0), 1, shift)]
        if next_local < step_count:
            chunks.insert(0, (hidden, siblings, next_local, 1))
            parts.insert(0, (("local", next_local), 1, 0))
        send, keep, *ranks = multiply(chunks)
        token = ranks[1]
        rank_rows[step, shift] = [rank[-per_block:] for rank in ranks]
        if next_local < step_count:
            rank_rows["local", next_local] = [rank[:per_block] for rank in ranks]
            next_local += 1
            if next_local == step_count:
                whole = [rank_rows["local", at] for at in (0, *range(half, step_count))]
                both = [jnp.concatenate([rank[side] for rank in whole]) for side in (0, 1)]
                rank_jobs = [([("ranks", step_count, 0)], *both, jnp.float32)]
        jobs = [(parts, send, keep, jnp.bfloat16)]
    gap(token, jobs)
    gap(token, [])

    def local_sum(step):
        return sums["local", 0][step] if step < half else sums["local", step][0]

    finished = choose(
        sums["ranks"], [(shift, sums["ranks", shift]) for shift in range(1, n_rep)]
    ).astype(jnp.bfloat16)
    finished = finished.reshape(step_count, rows_mine, owned_slots, rank_size)
    masked = jnp.sum(
        jnp.where(owned_hot[None, :, :, None], finished, 0), axis=2, dtype=jnp.float32
    ).astype(jnp.bfloat16)
    chosen = masked
    for turn in range(1, n_owners):
        chosen = chosen + lax.ppermute(
            masked, ("rep", "sub"), [(i, (i + turn) % n_owners) for i in range(n_owners)]
        )
    lifted = lift(
        chosen.reshape(step_count * rows_mine, rank_size),
        jnp.broadcast_to(my_slot, (step_count, rows_mine)).reshape(step_count * rows_mine, 1),
        panel_slots,
        panels,
    ).reshape(step_count, rows_mine, width)

    gap(lifted, [])
    output = jnp.zeros((step_count, rows_mine, width), jnp.bfloat16)
    for step in range(step_count):
        for cut, (left, size) in enumerate([(0, width)] if step < step_count - 1 else cuts):
            columns = slice(left, left + size)
            others = []
            for along in range(1, n_rep):
                if (step, along, 1) in sums:
                    others.append((along, sums[step, along, cut][0]))
                else:
                    others.append((along, sums[step, along, 0][0, :, columns]))
            total = choose(local_sum(step)[:, columns], others)
            value = total + ADAPTER_SCALE * lifted[step, :, columns].astype(jnp.float32)
            output = output.at[step, :, columns].set(value.astype(jnp.bfloat16))
    return output


def solution(mesh):
    return jax.shard_map(
        per_device,
        mesh=mesh,
        in_specs=(
            P(None, ("groups", "rep", "sub"), "tp"),
            P("tp", ("rep", "sub")),
            P(("rep", "sub"), "tp", None),
            P("tp", None, ("rep", "sub")),
            P("groups", None),
            P(),
        ),
        out_specs=P(None, ("groups", "tp"), ("rep", "sub")),
        check_vma=False,
    )
```

time: 213 us -> 207 us (0.972)
  Pallas kernels: 78.5 us -> 68.5 us
  waiting for transfers between devices: 47.5 us -> 54.4 us
  starting transfers between devices: 57.4 us -> 51.3 us
  other arithmetic: 15.6 us -> 18.4 us
    ppermute x11 -> x10, waiting for transfers between devices: 27.3 us -> 39.7 us  [swap_tensor(): return lax.ppermute(value, 'tp', [(i, i ^ bit) for i in range(n_tensor)])]
    ppermute x9 -> x10, waiting for transfers between devices: 19.9 us -> 9.64 us  [to_group(): return lax.ppermute(value, ('tp', 'rep'), pairs)]
    pallas_call x7 -> x6, Pallas kernels: 77.4 us -> 67.4 us  [partial_products(): pl.pallas_call(functools.partial(matmul_body, spans, left), in_specs=[pl....]
    ppermute x4, waiting for transfers between devices: 0.01 us -> 5.02 us  [from_rep(): lax.ppermute(value, 'rep', [((i + shift) % n_rep, i) for i in range(n_rep)])]
    ppermute x11 -> x10, starting transfers between devices: 23.5 us -> 20.5 us  [swap_tensor(): return lax.ppermute(value, 'tp', [(i, i ^ bit) for i in range(n_tensor)])]
    ppermute x3, starting transfers between devices: 7.06 us -> 4.77 us  [per_device(): lax.ppermute(masked, ('rep', 'sub'), [(i, (i + turn) % n_owners) for i in...]
    unnamed x31 -> x38, local copies, waits for them, and re-layouts: 8.9 us -> 8.36 us
    add x11 -> x15, other arithmetic: 7.14 us -> 7.47 us  [the longest x10 6.06 us: gap(): total = total + value.astype(jnp.float32)]
  transfers between devices with their start and end apart: 32 -> 32, of which waited for: 9 -> 9; matrix products, arithmetic and copies ran while one was open for 10% -> 9% of each run, Pallas kernels for 37% -> 33%
where the time goes in v4:
time: 207 us; the launch traced here: 206 us
  Pallas kernels  68.5 us (33%)
  waiting for transfers between devices  54.4 us (26%)
  starting transfers between devices  51.3 us (25%)
  other arithmetic  18.4 us (9%)
  local copies, waits for them, and re-layouts  12.6 us (6%)
    pallas_call x6, Pallas kernels, partial_products(): pl.pallas_call(functools.partial(matmul_body, spans, left), in_specs=[pl....  67.4 us
    ppermute x10, waiting for transfers between devices, swap_tensor(): return lax.ppermute(value, 'tp', [(i, i ^ bit) for i in range(n_tensor)])  39.7 us
    ppermute x10, starting transfers between devices, to_group(): return lax.ppermute(value, ('tp', 'rep'), pairs)  21 us
    ppermute x10, starting transfers between devices, swap_tensor(): return lax.ppermute(value, 'tp', [(i, i ^ bit) for i in range(n_tensor)])  20.5 us
    ppermute x10, waiting for transfers between devices, to_group(): return lax.ppermute(value, ('tp', 'rep'), pairs)  9.64 us
    unnamed x38, local copies, waits for them, and re-layouts  8.36 us
    add x10, other arithmetic, gap(): total = total + value.astype(jnp.float32)  6.06 us
    ppermute x4, waiting for transfers between devices, from_rep(): lax.ppermute(value, 'rep', [((i + shift) % n_rep, i) for i in range(n_rep)])  5.02 us
  transfers between devices with their start and end apart: 32, of which 9 were waited for; matrix products, arithmetic and copies ran while one was open for 9% of the time, Pallas kernels for 33%

profile of v4, /device:TPU:0, one launch (start us, length us, event | category | flops | bytes accessed | tf_op | source)
XLA Modules:
  0.0 206.0 jit_solution(5123396158757986721)
XLA Ops:
  0.5 2.6 %collective-permute-start.2 = (bf16[1,64,2048]{2,1,0:T(8,128)(2,1)}, bf16[1,64,2048]{2,1,0:T(8,128)(2,1)S(1)}, u32[]{:S(2)}, u32[]{:S(2)}) collective-permute-start(bf16[1,64,2048]{2,1,0:T(8,128)(2,1)} %param.19), channel_id=1, source_target_pairs={{0,4},{4,0},{8,12},{12,8},{1,5},{5,1},{9,13},{13,9},{2,6},{6,2},{1... | collective-permute-start | bytes 786440 | tf_op jit(solution)/shard_map/ppermute | solution.py:176
  3.1 2.2 %slice.199 = bf16[1,64,7168]{2,1,0:T(8,128)(2,1)} slice(bf16[4,64,7168]{2,1,0:T(8,128)(2,1)} %refs_0_.5), slice={[0:1], [0:64], [0:7168]} | slice | bytes 1835008 | tf_op jit(solution)/shard_map/slice | solution.py:201
  5.3 1.5 collective-permute-start.1
  6.8 3.5 %collective-permute-done.2 = bf16[1,64,2048]{2,1,0:T(8,128)(2,1)S(1)} collective-permute-done((bf16[1,64,2048]{2,1,0:T(8,128)(2,1)}, bf16[1,64,2048]{2,1,0:T(8,128)(2,1)S(1)}, u32[]{:S(2)}, u32[]{:S(2)}) %collective-permute-start.2) | collective-permute-done | bytes 262176 | tf_op jit(solution)/shard_map/ppermute | solution.py:176
  11.2 2.8 %collective-permute-start.3 = (bf16[2,64,2048]{2,1,0:T(8,128)(2,1)S(1)}, bf16[2,64,2048]{2,1,0:T(8,128)(2,1)}, u32[]{:S(2)}, u32[]{:S(2)}) collective-permute-start(bf16[2,64,2048]{2,1,0:T(8,128)(2,1)S(1)} %pad_maximum_fusion.1), channel_id=1, source_target_pairs={{0,8},{4,12},{8,0},{12,4},{1,9},{5,13},{9,1},{13,5},{2,10},{6,14},... | collective-permute-start | bytes 1572872 | tf_op jit(solution)/shard_map/ppermute | solution.py:176
  14.1 23.1 %collective-permute-done.3 = bf16[2,64,2048]{2,1,0:T(8,128)(2,1)} collective-permute-done((bf16[2,64,2048]{2,1,0:T(8,128)(2,1)S(1)}, bf16[2,64,2048]{2,1,0:T(8,128)(2,1)}, u32[]{:S(2)}, u32[]{:S(2)}) %collective-permute-start.3) | collective-permute-done | bytes 524320 | tf_op jit(solution)/shard_map/ppermute | solution.py:176
  38.5 2.0 copy-done.2
  40.5 14.2 %partial_products.6 = (bf16[128,2048]{1,0:T(8,128)(2,1)S(1)}, f32[128,2048]{1,0:T(8,128)S(1)}, f32[128,64]{1,0:T(8,128)S(1)}, f32[128,64]{1,0:T(8,128)S(1)}) custom-call(s32[1]{0:T(128)} %bitcast.pos_ref, bf16[4,64,7168]{2,1,0:T(8,128)(2,1)S(1)} %copy-done.2, bf16[4,64,7168]{2,1,0:T(8,128)(2,1)} %collective-permute-done.refs_1_, bf16[7168,2048]{1,0:T(8,128)(2,1)} %refs_2_.7, ...), custom_call_target="tpu_custom_call" | custom-call | tf_op jit(solution)/shard_map/partial_products/pallas_call | solution.py:99
  56.9 1.5 collective-permute-start.6
  59.5 12.8 %partial_products.7 = (bf16[128,2048]{1,0:T(8,128)(2,1)}, f32[128,2048]{1,0:T(8,128)S(1)}, f32[128,64]{1,0:T(8,128)S(1)}, f32[128,64]{1,0:T(8,128)S(1)}) custom-call(s32[1]{0:T(128)} %bitcast.pos_ref, bf16[4,64,7168]{2,1,0:T(8,128)(2,1)S(1)} %copy-done.2, bf16[4,64,7168]{2,1,0:T(8,128)(2,1)} %collective-permute-done.refs_1_, ...), custom_call_target="tpu_custom_call" | custom-call | tf_op jit(solution)/shard_map/partial_products/pallas_call | solution.py:99
  74.4 5.0 %collective-permute-done.6.refs_2_ = bf16[1,64,7168]{2,1,0:T(8,128)(2,1)} collective-permute-done((bf16[1,64,7168]{2,1,0:T(8,128)(2,1)S(1)}, bf16[1,64,7168]{2,1,0:T(8,128)(2,1)}, u32[]{:S(2)}, u32[]{:S(2)}) %collective-permute-start.6) | collective-permute-done | bytes 917536 | tf_op jit(solution)/shard_map/ppermute | solution.py:173
  79.4 1.5 collective-permute-start.8
  80.9 1.5 collective-permute-start.9
  83.7 2.0 copy-done.3
  85.7 14.5 %partial_products.8 = (bf16[128,2048]{1,0:T(8,128)(2,1)S(1)}, f32[128,2048]{1,0:T(8,128)S(1)}, f32[128,64]{1,0:T(8,128)S(1)}, f32[128,64]{1,0:T(8,128)S(1)}) custom-call(s32[1]{0:T(128)} %bitcast.pos_ref, bf16[4,64,7168]{2,1,0:T(8,128)(2,1)S(1)} %copy-done.3, bf16[4,64,7168]{2,1,0:T(8,128)(2,1)} %collective-permute-done.refs_1_, ...), custom_call_target="tpu_custom_call" | custom-call | tf_op jit(solution)/shard_map/partial_products/pallas_call | solution.py:99
  100.3 2.8 %collective-permute-done.8 = bf16[128,2048]{1,0:T(8,128)(2,1)} collective-permute-done((bf16[128,2048]{1,0:T(8,128)(2,1)}, bf16[128,2048]{1,0:T(8,128)(2,1)}, u32[]{:S(2)}, u32[]{:S(2)}) %collective-permute-start.8) | collective-permute-done | bytes 524320 | tf_op jit(solution)/shard_map/ppermute | solution.py:176
  104.4 6.0 %collective-permute-done.10 = bf16[2,64,2048]{2,1,0:T(8,128)(2,1)S(1)} collective-permute-done((bf16[2,64,2048]{2,1,0:T(8,128)(2,1)}, bf16[2,64,2048]{2,1,0:T(8,128)(2,1)S(1)}, u32[]{:S(2)}, u32[]{:S(2)}) %collective-permute-start.10) | collective-permute-done | bytes 524320 | tf_op jit(solution)/shard_map/ppermute | solution.py:185
  111.6 1.6 collective-permute-start.16
  113.2 5.0 %collective-permute-start.13 = (f32[256,64]{1,0:T(8,128)S(1)}, f32[256,64]{1,0:T(8,128)S(1)}, u32[]{:S(2)}, u32[]{:S(2)}) collective-permute-start(f32[256,64]{1,0:T(8,128)S(1)} %pad_maximum_fusion.2), channel_id=1, source_target_pairs={{0,4},{4,0},{8,12},{12,8},{1,5},{5,1},{9,13},{13,9},{2,6},{6,2},{1... | collective-permute-start | bytes 196616 | tf_op jit(solution)/shard_map/ppermute | solution.py:176
  119.7 11.6 %partial_products.9 = (bf16[64,2048]{1,0:T(8,128)(2,1)S(1)}, f32[64,2048]{1,0:T(8,128)S(1)}, f32[64,64]{1,0:T(8,128)S(1)}, f32[64,64]{1,0:T(8,128)S(1)}) custom-call(s32[1]{0:T(128)} %bitcast.pos_ref, bf16[1,64,7168]{2,1,0:T(8,128)(2,1)S(1)} %collective-permute-done.9.refs_0_, bf16[1,64,7168]{2,1,0:T(8,128)(2,1)S(1)} %collective-permute-done.11.refs_1_, ...), custom_call_target="tpu_custom_call" | custom-call | tf_op jit(solution)/shard_map/partial_products/pallas_call | solution.py:99
  132.2 6.4 %collective-permute-done.12 = bf16[128,2048]{1,0:T(8,128)(2,1)S(1)} collective-permute-done((bf16[128,2048]{1,0:T(8,128)(2,1)S(1)}, bf16[128,2048]{1,0:T(8,128)(2,1)S(1)}, u32[]{:S(2)}, u32[]{:S(2)}) %collective-permute-start.12) | collective-permute-done | bytes 524320 | tf_op jit(solution)/shard_map/ppermute | solution.py:176
  141.0 5.5 %collective-permute-start.20 = (bf16[1,64,2048]{2,1,0:T(8,128)(2,1)S(1)}, bf16[1,64,2048]{2,1,0:T(8,128)(2,1)S(1)}, u32[]{:S(2)}, u32[]{:S(2)}) collective-permute-start(bf16[1,64,2048]{2,1,0:T(8,128)(2,1)S(1)} %get-tuple-element.199), channel_id=1, source_target_pairs={{0,8},{4,12},{10,2},{14,6},{1,9},{5,13},{11,3},{15,7},{16,24},{20,... | collective-permute-start | bytes 786440 | tf_op jit(solution)/shard_map/ppermute | solution.py:185
  149.8 7.5 %partial_products.10 = (bf16[64,1024]{1,0:T(8,128)(2,1)}, f32[64,1024]{1,0:T(8,128)S(1)}, f32[64,64]{1,0:T(8,128)S(1)}, f32[64,64]{1,0:T(8,128)S(1)}) custom-call(s32[1]{0:T(128)} %bitcast.pos_ref, bf16[1,64,7168]{2,1,0:T(8,128)(2,1)S(1)} %collective-permute-done.14.refs_0_, bf16[1,64,7168]{2,1,0:T(8,128)(2,1)S(1)} %collective-permute-done.18.refs_1_, ...), custom_call_target="tpu_custom_call" | custom-call | tf_op jit(solution)/shard_map/partial_products/pallas_call | solution.py:99
  159.4 3.6 %collective-permute-done.19 = bf16[1,64,2048]{2,1,0:T(8,128)(2,1)S(1)} collective-permute-done((bf16[1,64,2048]{2,1,0:T(8,128)(2,1)S(1)}, bf16[1,64,2048]{2,1,0:T(8,128)(2,1)S(1)}, u32[]{:S(2)}, u32[]{:S(2)}) %collective-permute-start.19) | collective-permute-done | bytes 262176 | tf_op jit(solution)/shard_map/ppermute | solution.py:185
  163.9 2.0 collective-permute-start.23
  166.0 1.9 collective-permute-start.24
  169.1 6.8 %partial_products.11 = (bf16[64,1024]{1,0:T(8,128)(2,1)S(1)}, f32[64,1024]{1,0:T(8,128)S(1)}) custom-call(s32[1]{0:T(128)} %bitcast.pos_ref, bf16[1,64,7168]{2,1,0:T(8,128)(2,1)S(1)} %collective-permute-done.14.refs_0_, bf16[1,64,7168]{2,1,0:T(8,128)(2,1)S(1)} %copy-done.6, bf16[7168,2048]{1,0:T(8,128)(2,1)} %refs_2_.7, bf16[1,64,7168]{2,1,0:T(8,128)(2,1)S(1)} %bitcast.108), custom_call_target="tpu_custom_call" | custom-call | tf_op jit(solution)/shard_map/partial_products/pallas_call | solution.py:99
  177.8 3.4 %collective-permute-start.27 = (f32[4,64,64]{2,1,0:T(8,128)S(1)}, f32[4,64,64]{2,1,0:T(8,128)S(1)}, u32[]{:S(2)}, u32[]{:S(2)}) collective-permute-start(f32[4,64,64]{2,1,0:T(8,128)S(1)} %bitcast.117), channel_id=1, source_target_pairs={{0,8},{4,12},{10,2},{14,6},{1,9},{5,13},{11,3},{15,7},{16,24},{20,... | collective-permute-start | bytes 196616 | tf_op jit(solution)/shard_map/ppermute | solution.py:185
  182.5 5.8 %collective-permute-start.25 = (bf16[64,1024]{1,0:T(8,128)(2,1)S(1)}, bf16[64,1024]{1,0:T(8,128)(2,1)S(1)}, u32[]{:S(2)}, u32[]{:S(2)}) collective-permute-start(bf16[64,1024]{1,0:T(8,128)(2,1)S(1)} %get-tuple-element.214), channel_id=1, source_target_pairs={{0,4},{4,0},{8,12},{12,8},{1,5},{5,1},{9,13},{13,9},{2,6},{6,2},{1... | collective-permute-start | bytes 393224 | tf_op jit(solution)/shard_map/ppermute | solution.py:176
  188.4 2.9 %collective-permute-done.25 = bf16[64,1024]{1,0:T(8,128)(2,1)S(1)} collective-permute-done((bf16[64,1024]{1,0:T(8,128)(2,1)S(1)}, bf16[64,1024]{1,0:T(8,128)(2,1)S(1)}, u32[]{:S(2)}, u32[]{:S(2)}) %collective-permute-start.25) | collective-permute-done | bytes 131104 | tf_op jit(solution)/shard_map/ppermute | solution.py:176
  192.4 3.3 %collective-permute-start.29 = (bf16[4,64,64]{2,1,0:T(8,128)(2,1)S(1)}, bf16[4,64,64]{2,1,0:T(8,128)(2,1)}, u32[]{:S(2)}, u32[]{:S(2)}) collective-permute-start(bf16[4,64,64]{2,1,0:T(8,128)(2,1)S(1)} %fusion.29), channel_id=1, source_target_pairs={{0,2},{1,3},{2,0},{3,1},{4,6},{5,7},{6,4},{7,5},{8,10},{9,11},{10,... | collective-permute-start | bytes 98312 | tf_op jit(solution)/shard_map/ppermute | solution.py:326
  197.3 2.3 %collective-permute-start.31 = (bf16[1,64,1024]{2,1,0:T(8,128)(2,1)S(1)}, bf16[1,64,1024]{2,1,0:T(8,128)(2,1)S(1)}, u32[]{:S(2)}, u32[]{:S(2)}) collective-permute-start(bf16[1,64,1024]{2,1,0:T(8,128)(2,1)S(1)} %get-tuple-element.228), channel_id=1, source_target_pairs={{0,8},{4,12},{10,2},{14,6},{1,9},{5,13},{11,3},{15,7},{16,24},{20,... | collective-permute-start | bytes 393224 | tf_op jit(solution)/shard_map/ppermute | solution.py:185
  (124 shorter events, 36.1 us)
Async XLA Ops:
  0.0 38.4 %collective-permute-start = (bf16[4,64,7168]{2,1,0:T(8,128)(2,1)}, bf16[4,64,7168]{2,1,0:T(8,128)(2,1)}, u32[]{:S(2)}, u32[]{:S(2)}) collective-permute-start(bf16[4,64,7168]{2,1,0:T(8,128)(2,1)} %refs_0_.5), channel_id=1, source_target_pairs={{0,1},{1,0},{2,3},{3,2},{4,5},{5,4},{6,7},{7,6},{8,9},{9,8},{10,11... | collective-permute-start | bytes 11010056 | tf_op jit(solution)/shard_map/ppermute | solution.py:170
  0.5 9.8 %collective-permute-start.2 = (bf16[1,64,2048]{2,1,0:T(8,128)(2,1)}, bf16[1,64,2048]{2,1,0:T(8,128)(2,1)S(1)}, u32[]{:S(2)}, u32[]{:S(2)}) collective-permute-start(bf16[1,64,2048]{2,1,0:T(8,128)(2,1)} %param.19), channel_id=1, source_target_pairs={{0,4},{4,0},{8,12},{12,8},{1,5},{5,1},{9,13},{13,9},{2,6},{6,2},{1... | collective-permute-start | bytes 786440 | tf_op jit(solution)/shard_map/ppermute | solution.py:176
  5.3 49.4 %collective-permute-start.1 = (bf16[1,64,7168]{2,1,0:T(8,128)(2,1)}, bf16[1,64,7168]{2,1,0:T(8,128)(2,1)S(1)}, u32[]{:S(2)}, u32[]{:S(2)}) collective-permute-start(bf16[1,64,7168]{2,1,0:T(8,128)(2,1)} %slice.199), channel_id=1, source_target_pairs={{2,0},{0,2},{3,1},{1,3},{6,4},{4,6},{7,5},{5,7},{10,8},{8,10},{11,... | collective-permute-start | bytes 2752520 | tf_op jit(solution)/shard_map/ppermute | solution.py:173
  11.2 26.0 %collective-permute-start.3 = (bf16[2,64,2048]{2,1,0:T(8,128)(2,1)S(1)}, bf16[2,64,2048]{2,1,0:T(8,128)(2,1)}, u32[]{:S(2)}, u32[]{:S(2)}) collective-permute-start(bf16[2,64,2048]{2,1,0:T(8,128)(2,1)S(1)} %pad_maximum_fusion.1), channel_id=1, source_target_pairs={{0,8},{4,12},{8,0},{12,4},{1,9},{5,13},{9,1},{13,5},{2,10},{6,14},... | collective-permute-start | bytes 1572872 | tf_op jit(solution)/shard_map/ppermute | solution.py:176
  54.7 3.6 %collective-permute-start.4 = (bf16[1,64,7168]{2,1,0:T(8,128)(2,1)S(1)}, bf16[1,64,7168]{2,1,0:T(8,128)(2,1)S(1)}, u32[]{:S(2)}, u32[]{:S(2)}) collective-permute-start(bf16[1,64,7168]{2,1,0:T(8,128)(2,1)S(1)} %collective-permute-done.1.refs_2_), channel_id=1, source_target_pairs={{0,1},{1,0},{2,3},{3,2},{4,5},{5,4},{6,7},{7,6},{8,9},{9,8},{10,11... | collective-permute-start | bytes 2752520 | tf_op jit(solution)/shard_map/ppermute | solution.py:170
  54.8 17.6 %collective-permute-start.5 = (bf16[128,2048]{1,0:T(8,128)(2,1)S(1)}, bf16[128,2048]{1,0:T(8,128)(2,1)S(1)}, u32[]{:S(2)}, u32[]{:S(2)}) collective-permute-start(bf16[128,2048]{1,0:T(8,128)(2,1)S(1)} %get-tuple-element.154), channel_id=1, source_target_pairs={{0,4},{4,0},{8,12},{12,8},{1,5},{5,1},{9,13},{13,9},{2,6},{6,2},{1... | collective-permute-start | bytes 1572872 | tf_op jit(solution)/shard_map/ppermute | solution.py:176
  56.9 22.5 %collective-permute-start.6 = (bf16[1,64,7168]{2,1,0:T(8,128)(2,1)S(1)}, bf16[1,64,7168]{2,1,0:T(8,128)(2,1)}, u32[]{:S(2)}, u32[]{:S(2)}) collective-permute-start(bf16[1,64,7168]{2,1,0:T(8,128)(2,1)S(1)} %get-tuple-element.231), channel_id=1, source_target_pairs={{2,0},{0,2},{3,1},{1,3},{6,4},{4,6},{7,5},{5,7},{10,8},{8,10},{11,... | collective-permute-start | bytes 2752520 | tf_op jit(solution)/shard_map/ppermute | solution.py:173
  79.4 4.2 %collective-permute-start.7 = (bf16[1,64,7168]{2,1,0:T(8,128)(2,1)}, bf16[1,64,7168]{2,1,0:T(8,128)(2,1)}, u32[]{:S(2)}, u32[]{:S(2)}) collective-permute-start(bf16[1,64,7168]{2,1,0:T(8,128)(2,1)} %collective-permute-done.6.refs_2_), channel_id=1, source_target_pairs={{0,1},{1,0},{2,3},{3,2},{4,5},{5,4},{6,7},{7,6},{8,9},{9,8},{10,11... | collective-permute-start | bytes 2752520 | tf_op jit(solution)/shard_map/ppermute | solution.py:170
  79.4 23.7 %collective-permute-start.8 = (bf16[128,2048]{1,0:T(8,128)(2,1)}, bf16[128,2048]{1,0:T(8,128)(2,1)}, u32[]{:S(2)}, u32[]{:S(2)}) collective-permute-start(bf16[128,2048]{1,0:T(8,128)(2,1)} %get-tuple-element.166), channel_id=1, source_target_pairs={{0,4},{4,0},{8,12},{12,8},{1,5},{5,1},{9,13},{13,9},{2,6},{6,2},{1... | collective-permute-start | bytes 1572872 | tf_op jit(solution)/shard_map/ppermute | solution.py:176
  80.9 30.6 %collective-permute-start.9 = (bf16[1,64,7168]{2,1,0:T(8,128)(2,1)}, bf16[1,64,7168]{2,1,0:T(8,128)(2,1)S(1)}, u32[]{:S(2)}, u32[]{:S(2)}) collective-permute-start(bf16[1,64,7168]{2,1,0:T(8,128)(2,1)} %get-tuple-element.230), channel_id=1, source_target_pairs={{2,0},{0,2},{3,1},{1,3},{6,4},{4,6},{7,5},{5,7},{10,8},{8,10},{11,... | collective-permute-start | bytes 2752520 | tf_op jit(solution)/shard_map/ppermute | solution.py:173
  82.4 28.0 %collective-permute-start.10 = (bf16[2,64,2048]{2,1,0:T(8,128)(2,1)}, bf16[2,64,2048]{2,1,0:T(8,128)(2,1)S(1)}, u32[]{:S(2)}, u32[]{:S(2)}) collective-permute-start(bf16[2,64,2048]{2,1,0:T(8,128)(2,1)} %convert_element_type.130), channel_id=1, source_target_pairs={{8,0},{12,4},{2,10},{6,14},{9,1},{13,5},{3,11},{7,15},{24,16},{28,... | collective-permute-start | bytes 1572872 | tf_op jit(solution)/shard_map/ppermute | solution.py:185
  111.5 6.9 %collective-permute-start.11 = (bf16[1,64,7168]{2,1,0:T(8,128)(2,1)S(1)}, bf16[1,64,7168]{2,1,0:T(8,128)(2,1)S(1)}, u32[]{:S(2)}, u32[]{:S(2)}) collective-permute-start(bf16[1,64,7168]{2,1,0:T(8,128)(2,1)S(1)} %collective-permute-done.9.refs_0_), channel_id=1, source_target_pairs={{0,1},{1,0},{2,3},{3,2},{4,5},{5,4},{6,7},{7,6},{8,9},{9,8},{10,11... | collective-permute-start | bytes 2752520 | tf_op jit(solution)/shard_map/ppermute | solution.py:170
  111.6 28.1 %collective-permute-start.14 = (bf16[1,64,7168]{2,1,0:T(8,128)(2,1)S(1)}, bf16[1,64,7168]{2,1,0:T(8,128)(2,1)S(1)}, u32[]{:S(2)}, u32[]{:S(2)}) collective-permute-start(bf16[1,64,7168]{2,1,0:T(8,128)(2,1)S(1)} %copy-done.17), channel_id=1, source_target_pairs={{2,0},{0,2},{3,1},{1,3},{6,4},{4,6},{7,5},{5,7},{10,8},{8,10},{11,... | collective-permute-start | bytes 2752520 | tf_op jit(solution)/shard_map/ppermute | solution.py:173
  111.6 19.7 %collective-permute-start.16 = (bf16[1,64,2048]{2,1,0:T(8,128)(2,1)S(1)}, bf16[1,64,2048]{2,1,0:T(8,128)(2,1)S(1)}, u32[]{:S(2)}, u32[]{:S(2)}) collective-permute-start(bf16[1,64,2048]{2,1,0:T(8,128)(2,1)S(1)} %get-tuple-element.183), channel_id=1, source_target_pairs={{0,8},{4,12},{10,2},{14,6},{1,9},{5,13},{11,3},{15,7},{16,24},{20,... | collective-permute-start | bytes 786440 | tf_op jit(solution)/shard_map/ppermute | solution.py:185
  113.2 18.1 %collective-permute-start.13 = (f32[256,64]{1,0:T(8,128)S(1)}, f32[256,64]{1,0:T(8,128)S(1)}, u32[]{:S(2)}, u32[]{:S(2)}) collective-permute-start(f32[256,64]{1,0:T(8,128)S(1)} %pad_maximum_fusion.2), channel_id=1, source_target_pairs={{0,4},{4,0},{8,12},{12,8},{1,5},{5,1},{9,13},{13,9},{2,6},{6,2},{1... | collective-permute-start | bytes 196616 | tf_op jit(solution)/shard_map/ppermute | solution.py:176
  118.2 20.4 %collective-permute-start.12 = (bf16[128,2048]{1,0:T(8,128)(2,1)S(1)}, bf16[128,2048]{1,0:T(8,128)(2,1)S(1)}, u32[]{:S(2)}, u32[]{:S(2)}) collective-permute-start(bf16[128,2048]{1,0:T(8,128)(2,1)S(1)} %get-tuple-element.175), channel_id=1, source_target_pairs={{0,4},{4,0},{8,12},{12,8},{1,5},{5,1},{9,13},{13,9},{2,6},{6,2},{1... | collective-permute-start | bytes 1572872 | tf_op jit(solution)/shard_map/ppermute | solution.py:176
  118.4 20.4 %collective-permute-start.15 = (bf16[1,64,2048]{2,1,0:T(8,128)(2,1)S(1)}, bf16[1,64,2048]{2,1,0:T(8,128)(2,1)S(1)}, u32[]{:S(2)}, u32[]{:S(2)}) collective-permute-start(bf16[1,64,2048]{2,1,0:T(8,128)(2,1)S(1)} %get-tuple-element.181), channel_id=1, source_target_pairs={{8,0},{12,4},{2,10},{6,14},{9,1},{13,5},{3,11},{7,15},{24,16},{28,... | collective-permute-start | bytes 786440 | tf_op jit(solution)/shard_map/ppermute | solution.py:185
  139.7 9.1 %collective-permute-start.17 = (bf16[64,2048]{1,0:T(8,128)(2,1)S(1)}, bf16[64,2048]{1,0:T(8,128)(2,1)S(1)}, u32[]{:S(2)}, u32[]{:S(2)}) collective-permute-start(bf16[64,2048]{1,0:T(8,128)(2,1)S(1)} %get-tuple-element.188), channel_id=1, source_target_pairs={{0,4},{4,0},{8,12},{12,8},{1,5},{5,1},{9,13},{13,9},{2,6},{6,2},{1... | collective-permute-start | bytes 786440 | tf_op jit(solution)/shard_map/ppermute | solution.py:176
  139.7 10.1 %collective-permute-start.18 = (bf16[1,64,7168]{2,1,0:T(8,128)(2,1)S(1)}, bf16[1,64,7168]{2,1,0:T(8,128)(2,1)S(1)}, u32[]{:S(2)}, u32[]{:S(2)}) collective-permute-start(bf16[1,64,7168]{2,1,0:T(8,128)(2,1)S(1)} %collective-permute-done.14.refs_0_), channel_id=1, source_target_pairs={{0,1},{1,0},{2,3},{3,2},{4,5},{5,4},{6,7},{7,6},{8,9},{9,8},{10,11... | collective-permute-start | bytes 2752520 | tf_op jit(solution)/shard_map/ppermute | solution.py:170
  139.7 18.4 %collective-permute-start.21 = (f32[4,64,64]{2,1,0:T(8,128)S(1)}, f32[4,64,64]{2,1,0:T(8,128)S(1)}, u32[]{:S(2)}, u32[]{:S(2)}) collective-permute-start(f32[4,64,64]{2,1,0:T(8,128)S(1)} %bitcast.119), channel_id=1, source_target_pairs={{8,0},{12,4},{2,10},{6,14},{9,1},{13,5},{3,11},{7,15},{24,16},{28,... | collective-permute-start | bytes 196616 | tf_op jit(solution)/shard_map/ppermute | solution.py:185
  141.0 16.3 %collective-permute-start.20 = (bf16[1,64,2048]{2,1,0:T(8,128)(2,1)S(1)}, bf16[1,64,2048]{2,1,0:T(8,128)(2,1)S(1)}, u32[]{:S(2)}, u32[]{:S(2)}) collective-permute-start(bf16[1,64,2048]{2,1,0:T(8,128)(2,1)S(1)} %get-tuple-element.199), channel_id=1, source_target_pairs={{0,8},{4,12},{10,2},{14,6},{1,9},{5,13},{11,3},{15,7},{16,24},{20,... | collective-permute-start | bytes 786440 | tf_op jit(solution)/shard_map/ppermute | solution.py:185
  146.4 16.6 %collective-permute-start.19 = (bf16[1,64,2048]{2,1,0:T(8,128)(2,1)S(1)}, bf16[1,64,2048]{2,1,0:T(8,128)(2,1)S(1)}, u32[]{:S(2)}, u32[]{:S(2)}) collective-permute-start(bf16[1,64,2048]{2,1,0:T(8,128)(2,1)S(1)} %get-tuple-element.197), channel_id=1, source_target_pairs={{8,0},{12,4},{2,10},{6,14},{9,1},{13,5},{3,11},{7,15},{24,16},{28,... | collective-permute-start | bytes 786440 | tf_op jit(solution)/shard_map/ppermute | solution.py:185
  163.8 12.1 %collective-permute-start.22 = (bf16[64,1024]{1,0:T(8,128)(2,1)}, bf16[64,1024]{1,0:T(8,128)(2,1)}, u32[]{:S(2)}, u32[]{:S(2)}) collective-permute-start(bf16[64,1024]{1,0:T(8,128)(2,1)} %get-tuple-element.209), channel_id=1, source_target_pairs={{0,4},{4,0},{8,12},{12,8},{1,5},{5,1},{9,13},{13,9},{2,6},{6,2},{1... | collective-permute-start | bytes 393224 | tf_op jit(solution)/shard_map/ppermute | solution.py:176
  163.9 11.9 %collective-permute-start.23 = (f32[256,64]{1,0:T(8,128)}, f32[256,64]{1,0:T(8,128)S(1)}, u32[]{:S(2)}, u32[]{:S(2)}) collective-permute-start(f32[256,64]{1,0:T(8,128)} %pad_maximum_fusion.4), channel_id=1, source_target_pairs={{0,4},{4,0},{8,12},{12,8},{1,5},{5,1},{9,13},{13,9},{2,6},{6,2},{1... | collective-permute-start | bytes 196616 | tf_op jit(solution)/shard_map/ppermute | solution.py:176
  166.0 10.9 %collective-permute-start.24 = (bf16[1,64,2048]{2,1,0:T(8,128)(2,1)}, bf16[1,64,2048]{2,1,0:T(8,128)(2,1)S(1)}, u32[]{:S(2)}, u32[]{:S(2)}) collective-permute-start(bf16[1,64,2048]{2,1,0:T(8,128)(2,1)} %get-tuple-element.213), channel_id=1, source_target_pairs={{0,8},{4,12},{10,2},{14,6},{1,9},{5,13},{11,3},{15,7},{16,24},{20,... | collective-permute-start | bytes 786440 | tf_op jit(solution)/shard_map/ppermute | solution.py:185
  177.8 10.5 %collective-permute-start.27 = (f32[4,64,64]{2,1,0:T(8,128)S(1)}, f32[4,64,64]{2,1,0:T(8,128)S(1)}, u32[]{:S(2)}, u32[]{:S(2)}) collective-permute-start(f32[4,64,64]{2,1,0:T(8,128)S(1)} %bitcast.117), channel_id=1, source_target_pairs={{0,8},{4,12},{10,2},{14,6},{1,9},{5,13},{11,3},{15,7},{16,24},{20,... | collective-permute-start | bytes 196616 | tf_op jit(solution)/shard_map/ppermute | solution.py:185
  181.2 7.2 %collective-permute-start.26 = (bf16[1,64,1024]{2,1,0:T(8,128)(2,1)S(1)}, bf16[1,64,1024]{2,1,0:T(8,128)(2,1)S(1)}, u32[]{:S(2)}, u32[]{:S(2)}) collective-permute-start(bf16[1,64,1024]{2,1,0:T(8,128)(2,1)S(1)} %get-tuple-element.216), channel_id=1, source_target_pairs={{0,8},{4,12},{10,2},{14,6},{1,9},{5,13},{11,3},{15,7},{16,24},{20,... | collective-permute-start | bytes 393224 | tf_op jit(solution)/shard_map/ppermute | solution.py:185
  182.5 8.8 %collective-permute-start.25 = (bf16[64,1024]{1,0:T(8,128)(2,1)S(1)}, bf16[64,1024]{1,0:T(8,128)(2,1)S(1)}, u32[]{:S(2)}, u32[]{:S(2)}) collective-permute-start(bf16[64,1024]{1,0:T(8,128)(2,1)S(1)} %get-tuple-element.214), channel_id=1, source_target_pairs={{0,4},{4,0},{8,12},{12,8},{1,5},{5,1},{9,13},{13,9},{2,6},{6,2},{1... | collective-permute-start | bytes 393224 | tf_op jit(solution)/shard_map/ppermute | solution.py:176
  192.3 7.3 %collective-permute-start.28 = (bf16[4,64,64]{2,1,0:T(8,128)(2,1)S(1)}, bf16[4,64,64]{2,1,0:T(8,128)(2,1)S(1)}, u32[]{:S(2)}, u32[]{:S(2)}) collective-permute-start(bf16[4,64,64]{2,1,0:T(8,128)(2,1)S(1)} %fusion.29), channel_id=1, source_target_pairs={{0,1},{1,2},{2,3},{3,0},{4,5},{5,6},{6,7},{7,4},{8,9},{9,10},{10,1... | collective-permute-start | bytes 98312 | tf_op jit(solution)/shard_map/ppermute | solution.py:326
  192.4 7.2 %collective-permute-start.29 = (bf16[4,64,64]{2,1,0:T(8,128)(2,1)S(1)}, bf16[4,64,64]{2,1,0:T(8,128)(2,1)}, u32[]{:S(2)}, u32[]{:S(2)}) collective-permute-start(bf16[4,64,64]{2,1,0:T(8,128)(2,1)S(1)} %fusion.29), channel_id=1, source_target_pairs={{0,2},{1,3},{2,0},{3,1},{4,6},{5,7},{6,4},{7,5},{8,10},{9,11},{10,... | collective-permute-start | bytes 98312 | tf_op jit(solution)/shard_map/ppermute | solution.py:326
  195.7 3.9 %collective-permute-start.30 = (bf16[4,64,64]{2,1,0:T(8,128)(2,1)S(1)}, bf16[4,64,64]{2,1,0:T(8,128)(2,1)}, u32[]{:S(2)}, u32[]{:S(2)}) collective-permute-start(bf16[4,64,64]{2,1,0:T(8,128)(2,1)S(1)} %fusion.29), channel_id=1, source_target_pairs={{0,3},{1,0},{2,1},{3,2},{4,7},{5,4},{6,5},{7,6},{8,11},{9,8},{10,9... | collective-permute-start | bytes 98312 | tf_op jit(solution)/shard_map/ppermute | solution.py:326
  197.3 7.0 %collective-permute-start.31 = (bf16[1,64,1024]{2,1,0:T(8,128)(2,1)S(1)}, bf16[1,64,1024]{2,1,0:T(8,128)(2,1)S(1)}, u32[]{:S(2)}, u32[]{:S(2)}) collective-permute-start(bf16[1,64,1024]{2,1,0:T(8,128)(2,1)S(1)} %get-tuple-element.228), channel_id=1, source_target_pairs={{0,8},{4,12},{10,2},{14,6},{1,9},{5,13},{11,3},{15,7},{16,24},{20,... | collective-permute-start | bytes 393224 | tf_op jit(solution)/shard_map/ppermute | solution.py:185
  (19 other events, 272.4 us)

commit v5 on v4

v5 whole, which is shorter than its diff:
```python
import functools

import jax
import jax.numpy as jnp
from jax import lax
from jax.experimental import pallas as pl
from jax.experimental.pallas import tpu as pltpu
from jax.sharding import PartitionSpec as P

ADAPTER_SCALE = 0.5
BLOCK_N = 256
BLOCK_VALUES = 1024 * 1024
BUFFERS = 3
WIDE_ROWS = 128
RANK_NAME = 1000
VMEM_BYTES = 24 * 1024 * 1024


def block_depth(depth, width, rows):
    values = BLOCK_VALUES * (2 if rows >= WIDE_ROWS else 1)
    for size in (1024, 512, 256):
        if depth % size == 0 and size * width <= values:
            return size
    return depth


def matmul_body(spans, pos_ref, *refs):
    sources = refs[:2 * len(spans)]
    w_ref, a_ref, send_ref, keep_ref = refs[2 * len(spans):2 * len(spans) + 4]
    rank_refs = refs[2 * len(spans) + 4:-5]
    x_ref, w_buf, total_ref, x_sems, w_sems = refs[-5:]
    rows = send_ref.shape[0]
    depth, width = w_ref.shape
    slots, rank, _ = a_ref.shape
    buffers, block_k, _ = w_buf.shape
    block_n = min(BLOCK_N, width)
    count = depth // block_k

    def fetch(block, slot):
        return pltpu.make_async_copy(
            w_ref.at[pl.ds(block * block_k, block_k)], w_buf.at[slot], w_sems.at[slot]
        )

    own_at = pos_ref[0]
    copies, begin = [], 0
    for index, (first, steps) in enumerate(spans):
        for core, at in enumerate((own_at, 1 - own_at)):
            source = sources[2 * index + core]
            copies.append(pltpu.make_async_copy(
                source.at[pl.ds(first, steps)], x_ref.at[at, pl.ds(begin, steps)], x_sems.at[2 * index + core]
            ))
        begin += steps
    for copy in copies:
        copy.start()
    for block in range(buffers):
        fetch(block, block).start()
    keep_ref[...] = jnp.zeros_like(keep_ref)
    total_ref[...] = jnp.zeros_like(total_ref)
    for rank_ref in rank_refs:
        rank_ref[...] = jnp.zeros_like(rank_ref)
    for copy in copies:
        copy.wait()
    send_rank, keep_rank = rank_refs or (total_ref, keep_ref)
    for slot in range(slots):
        x = x_ref[...].reshape(2 * rows, depth)
        part = lax.dot_general(
            x, a_ref[slot], (((1,), (1,)), ((), ())), preferred_element_type=jnp.float32
        )
        begin = slot * rank + (0 if rank_refs else width)
        send_rank[:, begin:begin + rank] = part[:rows]
        keep_rank[:, begin:begin + rank] = part[rows:]

    @pl.loop(0, count)
    def _(block):
        slot = lax.rem(block, buffers)
        fetch(block, slot).wait()
        inner = pl.ds(pl.multiple_of(block * block_k, block_k), block_k)
        x = x_ref[:, :, :, inner].reshape(2 * rows, block_k)
        for place in range(width // block_n):
            columns = slice(place * block_n, (place + 1) * block_n)
            term = jnp.dot(x, w_buf[slot, :, columns], preferred_element_type=jnp.float32)
            total_ref[:, columns] += term[:rows]
            keep_ref[:, columns] += term[rows:]

        @pl.when(block + buffers < count)
        def _():
            fetch(block + buffers, slot).start()

    send_ref[...] = total_ref[...].astype(send_ref.dtype)


def rank_columns(factors):
    slots, rank, _ = factors.shape
    return -(-slots * rank // 128) * 128


def partial_products(pos, chunks, weight, factors, apart):
    _, per_block, depth = chunks[0][0].shape
    width = weight.shape[1]
    spans = tuple((first, steps) for _, _, first, steps in chunks)
    steps = sum(length for _, length in spans)
    rows = steps * per_block
    block_k = block_depth(depth, width, rows)
    buffers = min(BUFFERS, depth // block_k)
    any_spec = pl.BlockSpec(memory_space=pl.ANY)
    vmem_spec = pl.BlockSpec(memory_space=pltpu.VMEM)
    extra = rank_columns(factors)
    columns = width + (0 if apart else extra)
    ranks = [jax.ShapeDtypeStruct((rows, extra), jnp.float32)] * (2 if apart else 0)
    return pl.pallas_call(
        functools.partial(matmul_body, spans),
        in_specs=[pl.BlockSpec(memory_space=pltpu.SMEM)] + [any_spec] * (2 * len(chunks) + 1) + [vmem_spec],
        out_specs=[vmem_spec] * (2 + len(ranks)),
        out_shape=[
            jax.ShapeDtypeStruct((rows, columns), jnp.bfloat16),
            jax.ShapeDtypeStruct((rows, columns), jnp.float32),
        ] + ranks,
        scratch_shapes=[
            pltpu.VMEM((2, steps, per_block, depth), jnp.bfloat16),
            pltpu.VMEM((buffers, block_k, width), jnp.bfloat16),
            pltpu.VMEM((rows, columns), jnp.float32),
            pltpu.SemaphoreType.DMA((2 * len(chunks),)),
            pltpu.SemaphoreType.DMA((buffers,)),
        ],
        compiler_params=pltpu.CompilerParams(vmem_limit_bytes=VMEM_BYTES),
        cost_estimate=pl.CostEstimate(flops=0, bytes_accessed=0, transcendentals=0),
        name="partial_products",
    )(pos, *[source for own, sib, _, _ in chunks for source in (own, sib)], weight, factors)


def finish_body(received, chosen_ref, slot_ref, order_ref, panel_ref, *refs):
    out_ref, lifted_ref, done_ref, sem = refs[-4:]
    steps, rows, width = done_ref.shape
    rank = chosen_ref.shape[1]
    chosen = chosen_ref[...]
    slot = slot_ref[...]
    spread = jnp.concatenate(
        [
            jnp.where(slot == order_ref[place], chosen, jnp.zeros_like(chosen))
            for place in range(panel_ref.shape[0] // rank)
        ],
        axis=1,
    )
    block_n = min(BLOCK_N, width)
    for place in range(width // block_n):
        columns = slice(place * block_n, (place + 1) * block_n)
        lifted = jnp.dot(spread, panel_ref[:, columns], preferred_element_type=jnp.float32).astype(jnp.bfloat16)
        for step in range(steps):
            total = refs[step * (received + 1)][:, columns]
            for value_ref in refs[step * (received + 1) + 1:(step + 1) * (received + 1)]:
                total = total + value_ref[:, columns].astype(jnp.float32)
            value = total + ADAPTER_SCALE * lifted[step * rows:(step + 1) * rows].astype(jnp.float32)
            done_ref[step, :, columns] = value.astype(done_ref.dtype)
        lifted_ref[:, columns] = lifted[steps * rows:]
    copy = pltpu.make_async_copy(done_ref, out_ref.at[pl.ds(0, steps)], sem)
    copy.start()
    copy.wait()


def finish_steps(totals, chosen, slots, order, panels):
    steps, width = len(totals), panels.shape[1]
    rows = chosen.shape[0] // (steps + 1)
    vmem_spec = pl.BlockSpec(memory_space=pltpu.VMEM)
    arrays = [value for total in totals for value in total]
    return pl.pallas_call(
        functools.partial(finish_body, len(totals[0]) - 1),
        in_specs=[vmem_spec, vmem_spec, pl.BlockSpec(memory_space=pltpu.SMEM)] + [vmem_spec] * (1 + len(arrays)),
        out_specs=[pl.BlockSpec(memory_space=pl.ANY), vmem_spec],
        out_shape=[
            jax.ShapeDtypeStruct((steps + 1, rows, width), jnp.bfloat16),
            jax.ShapeDtypeStruct((rows, width), jnp.bfloat16),
        ],
        scratch_shapes=[pltpu.VMEM((steps, rows, width), jnp.bfloat16), pltpu.SemaphoreType.DMA],
        compiler_params=pltpu.CompilerParams(vmem_limit_bytes=VMEM_BYTES),
        cost_estimate=pl.CostEstimate(flops=0, bytes_accessed=0, transcendentals=0),
        name="finish_steps",
    )(chosen, slots, order, panels, *arrays)


def last_body(partial_ref, lifted_ref, *refs):
    out_ref, done_ref, sem = refs[-3:]
    total = refs[0][...]
    for value_ref in refs[1:-3]:
        total = total + value_ref[...].astype(jnp.float32)
    value = total + ADAPTER_SCALE * lifted_ref[...].astype(jnp.float32)
    done_ref[0] = value.astype(done_ref.dtype)
    copy = pltpu.make_async_copy(done_ref, out_ref.at[pl.ds(out_ref.shape[0] - 1, 1)], sem)
    copy.start()
    copy.wait()


def finish_last(partial, lifted, arrays):
    vmem_spec = pl.BlockSpec(memory_space=pltpu.VMEM)
    any_spec = pl.BlockSpec(memory_space=pl.ANY)
    return pl.pallas_call(
        last_body,
        in_specs=[any_spec] + [vmem_spec] * (1 + len(arrays)),
        out_specs=any_spec,
        out_shape=jax.ShapeDtypeStruct(partial.shape, partial.dtype),
        input_output_aliases={0: 0},
        scratch_shapes=[pltpu.VMEM((1,) + partial.shape[1:], partial.dtype), pltpu.SemaphoreType.DMA],
        compiler_params=pltpu.CompilerParams(vmem_limit_bytes=VMEM_BYTES),
        cost_estimate=pl.CostEstimate(flops=0, bytes_accessed=0, transcendentals=0),
        name="finish_last",
    )(partial, lifted, *arrays)


def per_device(hidden, base_weight, down_a, up_b, adapter_ids, owner_map):
    step_count, per_block, _ = hidden.shape
    n_tensor = lax.axis_size("tp")
    n_rep = lax.axis_size("rep")
    n_sub = lax.axis_size("sub")
    n_owners = n_rep * n_sub
    tensor_index = lax.axis_index("tp")
    rep_index = lax.axis_index("rep")
    sub_index = lax.axis_index("sub")
    owner_index = lax.axis_index(("rep", "sub"))
    requests = per_block * n_owners
    rows_mine = requests // n_tensor
    group = n_tensor // n_rep
    group_index = tensor_index // group
    owned_slots, _, rank_size = down_a.shape
    slot_count = owned_slots * n_owners
    width = base_weight.shape[1]

    def after(value, *done):
        return lax.optimization_barrier((value, *done))[0]

    def swap_cores(value):
        return lax.ppermute(value, "sub", [(i, i ^ 1) for i in range(n_sub)])

    def from_rep(value, shift):
        return lax.ppermute(value, "rep", [((i + shift) % n_rep, i) for i in range(n_rep)])

    def swap_tensor(value, bit):
        return lax.ppermute(value, "tp", [(i, i ^ bit) for i in range(n_tensor)])

    def to_group(value, hop):
        moved = group * hop
        return lax.ppermute(value, "tp", [(i, (i + moved) % n_tensor) for i in range(n_tensor)])

    def pick(values, index):
        value = values[0]
        for at in range(1, len(values)):
            value = jnp.where(index == at, values[at], value)
        return value

    keeps = (tensor_index // (group // 2)) % 2
    pos = (sub_index == keeps).astype(jnp.int32).reshape(1)

    siblings = swap_cores(hidden)
    pieces = [(step, shift) for step in range(step_count) for shift in range(1, n_rep)]
    remote = {}
    for step, shift in pieces:
        source = hidden if step == 0 else after(hidden, siblings)
        remote[step, shift] = from_rep(source[step:step + 1], shift)

    panels, order, bit = up_b, [0], n_tensor // 2
    while bit:
        panels = jnp.concatenate([panels, swap_tensor(panels, bit)], axis=0)
        order = order + [at ^ bit for at in order]
        bit //= 2
    panels = panels.reshape(slot_count * rank_size, width)
    panel_slots = jnp.stack([
        (tensor_index ^ at) * up_b.shape[0] + each for at in order for each in range(up_b.shape[0])
    ]).astype(jnp.int32)

    my_ids = lax.dynamic_slice_in_dim(adapter_ids, tensor_index * rows_mine, rows_mine)
    iota = lax.broadcasted_iota(jnp.int32, (rows_mine, slot_count), 1)
    my_slot = jnp.sum((my_ids == iota).astype(jnp.int32) * owner_map[None, :], axis=1)
    owned_hot = my_slot[:, None] == (
        owner_index * owned_slots + lax.broadcasted_iota(jnp.int32, (rows_mine, owned_slots), 1)
    )

    first_leg, halved, begun, second_leg, ended = [], {}, set(), [], {}

    def second_half(total, received, steps, kind):
        total = total + received.astype(jnp.float32)
        rows, columns = total.shape
        extent, bit = rows // steps, group // 4
        while bit:
            extent //= 2
            halves = total.reshape(steps, 2, extent, columns)
            mine = (tensor_index // bit) % 2
            kept = lax.dynamic_index_in_dim(halves, mine, 1, keepdims=False)
            sent = lax.dynamic_index_in_dim(halves, 1 - mine, 1, keepdims=False)
            total = kept + swap_tensor(sent.astype(kind), bit).astype(jnp.float32)
            bit //= 2
        return total.reshape(steps, extent, columns)

    def gap(token, jobs, *extra):
        nonlocal first_leg, second_leg
        for parts, received, keep, kind in first_leg:
            steps = sum(length for _, length in parts)
            total, begin = second_half(after(keep, token), received, steps, kind), 0
            for key, length in parts:
                for at in range(begin, begin + length):
                    halved[key[0] + at - begin, key[1]] = total[at]
                    if key == (step_count - 1, 0):
                        halved[RANK_NAME, 0] = total[at][:, width:]
                begin += length
        closed = {}
        for name, kept, received in second_leg:
            closed[name] = (kept, *received)
        started, sends = [], []
        for name in sorted({name for name, _ in halved}):
            if name in begun or any((name, at) not in halved for at in range(n_rep)):
                continue
            begun.add(name)
            values = [halved[name, at] for at in range(n_rep)]
            columns = min(value.shape[1] for value in values)
            values = [value[:, :columns] for value in values]
            kind = jnp.float32 if name >= RANK_NAME else jnp.bfloat16
            kept = pick(values, (group_index - rep_index) % n_rep)
            sent = [pick(values, (group_index + hop - rep_index) % n_rep).astype(kind) for hop in range(1, n_rep)]
            started.append((name, kept))
            sends.append(sent)
        first_sends = [job[1] for job in jobs]
        first_sends, sends, extra, closed = lax.optimization_barrier((first_sends, sends, extra, closed))
        ended.update(closed)
        first_leg = [
            (parts, swap_tensor(send, group // 2), keep, kind) for (parts, _, keep, kind), send in zip(jobs, first_sends)
        ]
        second_leg = [
            (name, kept, [to_group(value, hop + 1) for hop, value in enumerate(sent)])
            for (name, kept), sent in zip(started, sends)
        ]
        return extra

    factors = jnp.swapaxes(down_a, 1, 2)

    def multiply(chunks, apart=False):
        return partial_products(pos, chunks, base_weight, factors, apart)

    half = step_count // 2
    send, keep = multiply([(hidden, siblings, 0, half)])
    jobs = [([((0, 0), half)], send, keep, jnp.bfloat16)]
    next_local = half
    for piece, (step, shift) in enumerate(pieces):
        own, siblings = gap(send, jobs, remote[step, shift], siblings)
        if piece == 1:
            siblings, panels = lax.optimization_barrier((siblings, panels))
        sib = swap_cores(own)
        chunks, parts = [(own, sib, 0, 1)], [((step, shift), 1)]
        if next_local < step_count:
            chunks.insert(0, (hidden, siblings, next_local, 1))
            parts.insert(0, ((next_local, 0), 1))
            next_local += 1
        send, keep, *ranks = multiply(chunks, step == step_count - 1)
        jobs = [(parts, send, keep, jnp.bfloat16)]
        if ranks:
            jobs.insert(0, ([((RANK_NAME, shift), 1)], *ranks, jnp.float32))
    gap(send, jobs)
    gap(send, [])
    ended.update((name, (kept, *received)) for name, kept, received in second_leg)

    def rank_sum(name):
        kept, *received = [value[:, -rank_columns(factors):] for value in ended[name]]
        for value in received:
            kept = kept + value.astype(jnp.float32)
        return kept[:, :owned_slots * rank_size]

    finished = jnp.stack([rank_sum(step) for step in range(step_count - 1)] + [rank_sum(RANK_NAME)])
    finished = finished.astype(jnp.bfloat16).reshape(step_count, rows_mine, owned_slots, rank_size)
    masked = jnp.sum(
        jnp.where(owned_hot[None, :, :, None], finished, 0), axis=2, dtype=jnp.float32
    ).astype(jnp.bfloat16)
    chosen = masked
    for turn in range(1, n_owners):
        chosen = chosen + lax.ppermute(
            masked, ("rep", "sub"), [(i, (i + turn) % n_owners) for i in range(n_owners)]
        )
    partial, lifted = finish_steps(
        [ended[step] for step in range(step_count - 1)],
        chosen.reshape(step_count * rows_mine, rank_size),
        jnp.broadcast_to(my_slot, (step_count, rows_mine)).reshape(step_count * rows_mine, 1),
        panel_slots,
        panels,
    )
    return finish_last(partial, lifted, ended[step_count - 1])


def solution(mesh):
    return jax.shard_map(
        per_device,
        mesh=mesh,
        in_specs=(
            P(None, ("groups", "rep", "sub"), "tp"),
            P("tp", ("rep", "sub")),
            P(("rep", "sub"), "tp", None),
            P("tp", None, ("rep", "sub")),
            P("groups", None),
            P(),
        ),
        out_specs=P(None, ("groups", "tp"), ("rep", "sub")),
        check_vma=False,
    )
```

time: 207 us -> 151 us (0.73)
  waiting for transfers between devices: 54.4 us -> 28.2 us
  starting transfers between devices: 51.3 us -> 30.8 us
  other arithmetic: 18.4 us -> 9.74 us
  Pallas kernels: 68.5 us -> 71 us
  local copies, waits for them, and re-layouts: 12.6 us -> 10.1 us
    ppermute x10 -> x8, waiting for transfers between devices: 39.7 us -> 15.4 us  [swap_tensor(): return lax.ppermute(value, 'tp', [(i, i ^ bit) for i in range(n_tensor)])]
    ppermute x10 -> x5, starting transfers between devices: 21 us -> 10.2 us  [to_group(): lax.ppermute(value, 'tp', [(i, (i + moved) % n_tensor) for i in range(n_t...]
    ppermute x10 -> x8, starting transfers between devices: 20.5 us -> 10.4 us  [swap_tensor(): return lax.ppermute(value, 'tp', [(i, i ^ bit) for i in range(n_tensor)])]
    add x10 -> x0, other arithmetic: 6.06 us -> none  [gap(): total = total + value.astype(jnp.float32)]
    ppermute x10 -> x5, waiting for transfers between devices: 9.64 us -> 5.79 us  [to_group(): lax.ppermute(value, 'tp', [(i, (i + moved) % n_tensor) for i in range(n_t...]
    ppermute x3, waiting for transfers between devices: 0.01 us -> 3.61 us  [per_device(): lax.ppermute(masked, ('rep', 'sub'), [(i, (i + turn) % n_owners) for i in...]
    ppermute x4, starting transfers between devices: 4.48 us -> 7.65 us  [from_rep(): lax.ppermute(value, 'rep', [((i + shift) % n_rep, i) for i in range(n_rep)])]
    ppermute x3, starting transfers between devices: 4.77 us -> 2.05 us  [per_device(): lax.ppermute(masked, ('rep', 'sub'), [(i, (i + turn) % n_owners) for i in...]
  transfers between devices with their start and end apart: 32 -> 25, of which waited for: 9 -> 13; matrix products, arithmetic and copies ran while one was open for 9% -> 9% of each run, Pallas kernels for 33% -> 47%
where the time goes in v5:
time: 151 us; the launch traced here: 150 us
  Pallas kernels  71 us (47%)
  starting transfers between devices  30.8 us (20%)
  waiting for transfers between devices  28.2 us (19%)
  local copies, waits for them, and re-layouts  10.1 us (7%)
  other arithmetic  9.74 us (6%)
    pallas_call x5, Pallas kernels, partial_products(): pl.pallas_call(functools.partial(matmul_body, spans), in_specs=[pl.BlockS...  68 us
    ppermute x8, waiting for transfers between devices, swap_tensor(): return lax.ppermute(value, 'tp', [(i, i ^ bit) for i in range(n_tensor)])  15.4 us
    ppermute x8, starting transfers between devices, swap_tensor(): return lax.ppermute(value, 'tp', [(i, i ^ bit) for i in range(n_tensor)])  10.4 us
    ppermute x5, starting transfers between devices, to_group(): lax.ppermute(value, 'tp', [(i, (i + moved) % n_tensor) for i in range(n_t...  10.2 us
    ppermute x4, starting transfers between devices, from_rep(): lax.ppermute(value, 'rep', [((i + shift) % n_rep, i) for i in range(n_rep)])  7.65 us
    unnamed x38, local copies, waits for them, and re-layouts  6.04 us
    ppermute x5, waiting for transfers between devices, to_group(): lax.ppermute(value, 'tp', [(i, (i + moved) % n_tensor) for i in range(n_t...  5.79 us
    slice x2, local copies, waits for them, and re-layouts, per_device(): remote[step, shift] = from_rep(source[step:step + 1], shift)  3.77 us
  transfers between devices with their start and end apart: 25, of which 13 were waited for; matrix products, arithmetic and copies ran while one was open for 9% of the time, Pallas kernels for 47%

profile of v5, /device:TPU:0, one launch (start us, length us, event | category | flops | bytes accessed | tf_op | source)
XLA Modules:
  0.0 150.2 jit_solution(15950703964580239582)
XLA Ops:
  0.5 2.2 %slice.77 = bf16[1,64,7168]{2,1,0:T(8,128)(2,1)} slice(bf16[4,64,7168]{2,1,0:T(8,128)(2,1)} %refs_0_.5), slice={[0:1], [0:64], [0:7168]} | slice | bytes 1835008 | tf_op jit(solution)/shard_map/slice | solution.py:256
  2.7 2.6 %collective-permute-start.1 = (bf16[1,64,7168]{2,1,0:T(8,128)(2,1)}, bf16[1,64,7168]{2,1,0:T(8,128)(2,1)S(1)}, u32[]{:S(2)}, u32[]{:S(2)}) collective-permute-start(bf16[1,64,7168]{2,1,0:T(8,128)(2,1)} %slice.77), channel_id=1, source_target_pairs={{2,0},{0,2},{3,1},{1,3},{6,4},{4,6},{7,5},{5,7},{10,8},{8,10},{11,... | collective-permute-start | bytes 2752520 | tf_op jit(solution)/shard_map/ppermute | solution.py:233
  5.3 2.6 %collective-permute-start.4 = (bf16[1,64,2048]{2,1,0:T(8,128)(2,1)S(1)}, bf16[1,64,2048]{2,1,0:T(8,128)(2,1)}, u32[]{:S(2)}, u32[]{:S(2)}) collective-permute-start(bf16[1,64,2048]{2,1,0:T(8,128)(2,1)S(1)} %copy-done.16), channel_id=1, source_target_pairs={{0,8},{4,12},{8,0},{12,4},{1,9},{5,13},{9,1},{13,5},{2,10},{6,14},... | collective-permute-start | bytes 786440 | tf_op jit(solution)/shard_map/ppermute | solution.py:236
  7.9 2.0 %copy-done.1 = bf16[4,64,7168]{2,1,0:T(8,128)(2,1)S(1)} copy-done((bf16[4,64,7168]{2,1,0:T(8,128)(2,1)S(1)}, bf16[4,64,7168]{2,1,0:T(8,128)(2,1)}, u32[]{:S(2)}) %copy-start.1) | copy-done | bytes 3670040
  9.9 15.1 %partial_products.5 = (bf16[128,2176]{1,0:T(8,128)(2,1)}, f32[128,2176]{1,0:T(8,128)S(1)}) custom-call(s32[1]{0:T(128)} %bitcast.1.pos_ref, bf16[4,64,7168]{2,1,0:T(8,128)(2,1)S(1)} %copy-done.1, bf16[4,64,7168]{2,1,0:T(8,128)(2,1)} %collective-permute-done.refs_1_, bf16[7168,2048]{1,0:T(8,128)(2,1)} %refs_2_.5, bf16[1,64,7168]{2,1,0:T(8,128)(2,1)S(1)} %bitcast.18), custom_call_target="tpu_custom_call" | custom-call | tf_op jit(solution)/shard_map/partial_products/pallas_call | solution.py:110
  25.0 1.4 collective-permute-done.1.refs_2_
  26.4 1.6 %fusion.8 = (bf16[1,64,7168]{2,1,0:T(8,128)(2,1)}, bf16[1,64,7168]{2,1,0:T(8,128)(2,1)}, bf16[1,64,7168]{2,1,0:T(8,128)(2,1)}) fusion(bf16[4,64,7168]{2,1,0:T(8,128)(2,1)S(1)} %copy-done.1), kind=kLoop, calls=%fused_computation.36 | loop fusion | bytes 5505024 | tf_op jit(solution)/shard_map/slice | solution.py:256
  28.0 1.8 %collective-permute-start.3 = (bf16[1,64,7168]{2,1,0:T(8,128)(2,1)}, bf16[1,64,7168]{2,1,0:T(8,128)(2,1)}, u32[]{:S(2)}, u32[]{:S(2)}) collective-permute-start(bf16[1,64,7168]{2,1,0:T(8,128)(2,1)} %get-tuple-element.101), channel_id=1, source_target_pairs={{2,0},{0,2},{3,1},{1,3},{6,4},{4,6},{7,5},{5,7},{10,8},{8,10},{11,... | collective-permute-start | bytes 2752520 | tf_op jit(solution)/shard_map/ppermute | solution.py:233
  29.8 1.8 %pad_maximum_fusion.1 = bf16[2,64,2048]{2,1,0:T(8,128)(2,1)} fusion(bf16[1,64,2048]{2,1,0:T(8,128)(2,1)} %collective-permute-done.4, bf16[1,64,2048]{2,1,0:T(8,128)(2,1)S(1)} %copy-done.16), kind=kLoop, calls=%fused_computation.8 | loop fusion | flops 262144 | bytes 1048576 | tf_op jit(solution)/shard_map/concatenate | solution.py:260
  31.6 1.6 %collective-permute-start.5 = (bf16[2,64,2048]{2,1,0:T(8,128)(2,1)}, bf16[2,64,2048]{2,1,0:T(8,128)(2,1)}, u32[]{:S(2)}, u32[]{:S(2)}) collective-permute-start(bf16[2,64,2048]{2,1,0:T(8,128)(2,1)} %pad_maximum_fusion.1), channel_id=1, source_target_pairs={{0,4},{4,0},{8,12},{12,8},{1,5},{5,1},{9,13},{13,9},{2,6},{6,2},{1... | collective-permute-start | bytes 1572872 | tf_op jit(solution)/shard_map/ppermute | solution.py:236
  33.6 2.0 %copy-done.2 = bf16[4,64,7168]{2,1,0:T(8,128)(2,1)S(1)} copy-done((bf16[4,64,7168]{2,1,0:T(8,128)(2,1)S(1)}, bf16[4,64,7168]{2,1,0:T(8,128)(2,1)}, u32[]{:S(2)}) %copy-start.2) | copy-done | bytes 3670040
  35.6 14.3 %partial_products.6 = (bf16[128,2176]{1,0:T(8,128)(2,1)S(1)}, f32[128,2176]{1,0:T(8,128)S(1)}) custom-call(s32[1]{0:T(128)} %bitcast.1.pos_ref, bf16[4,64,7168]{2,1,0:T(8,128)(2,1)S(1)} %copy-done.2, bf16[4,64,7168]{2,1,0:T(8,128)(2,1)} %collective-permute-done.refs_1_, bf16[1,64,7168]{2,1,0:T(8,128)(2,1)S(1)} %collective-permute-done.1.refs_2_, ...), custom_call_target="tpu_custom_call" | custom-call | tf_op jit(solution)/shard_map/partial_products/pallas_call | solution.py:110
  51.1 1.2 pad_maximum_fusion
  52.4 1.8 %collective-permute-start.9 = (bf16[1,64,7168]{2,1,0:T(8,128)(2,1)S(1)}, bf16[1,64,7168]{2,1,0:T(8,128)(2,1)}, u32[]{:S(2)}, u32[]{:S(2)}) collective-permute-start(bf16[1,64,7168]{2,1,0:T(8,128)(2,1)S(1)} %copy-done.17), channel_id=1, source_target_pairs={{2,0},{0,2},{3,1},{1,3},{6,4},{4,6},{7,5},{5,7},{10,8},{8,10},{11,... | collective-permute-start | bytes 2752520 | tf_op jit(solution)/shard_map/ppermute | solution.py:233
  54.2 1.6 %collective-permute-start.7 = (bf16[128,2176]{1,0:T(8,128)(2,1)S(1)}, bf16[128,2176]{1,0:T(8,128)(2,1)S(1)}, u32[]{:S(2)}, u32[]{:S(2)}) collective-permute-start(bf16[128,2176]{1,0:T(8,128)(2,1)S(1)} %get-tuple-element.62), channel_id=1, source_target_pairs={{0,4},{4,0},{8,12},{12,8},{1,5},{5,1},{9,13},{13,9},{2,6},{6,2},{1... | collective-permute-start | bytes 1671176 | tf_op jit(solution)/shard_map/ppermute | solution.py:236
  55.7 2.8 %collective-permute-done.8 = bf16[128,2176]{1,0:T(8,128)(2,1)} collective-permute-done((bf16[128,2176]{1,0:T(8,128)(2,1)}, bf16[128,2176]{1,0:T(8,128)(2,1)}, u32[]{:S(2)}, u32[]{:S(2)}) %collective-permute-start.8) | collective-permute-done | bytes 557088 | tf_op jit(solution)/shard_map/ppermute | solution.py:236
  59.8 13.0 %partial_products.7 = (bf16[128,2176]{1,0:T(8,128)(2,1)}, f32[128,2176]{1,0:T(8,128)S(1)}) custom-call(s32[1]{0:T(128)} %bitcast.1.pos_ref, bf16[4,64,7168]{2,1,0:T(8,128)(2,1)S(1)} %copy-done.2, bf16[4,64,7168]{2,1,0:T(8,128)(2,1)} %collective-permute-done.refs_1_, bf16[1,64,7168]{2,1,0:T(8,128)(2,1)} %collective-permute-done.3.refs_2_, ...), custom_call_target="tpu_custom_call" | custom-call | tf_op jit(solution)/shard_map/partial_products/pallas_call | solution.py:110
  75.3 1.8 %collective-permute-start.11 = (bf16[128,2176]{1,0:T(8,128)(2,1)}, bf16[128,2176]{1,0:T(8,128)(2,1)}, u32[]{:S(2)}, u32[]{:S(2)}) collective-permute-start(bf16[128,2176]{1,0:T(8,128)(2,1)} %get-tuple-element.70), channel_id=1, source_target_pairs={{0,4},{4,0},{8,12},{12,8},{1,5},{5,1},{9,13},{13,9},{2,6},{6,2},{1... | collective-permute-start | bytes 1671176 | tf_op jit(solution)/shard_map/ppermute | solution.py:236
  77.1 1.5 collective-permute-start.12
  78.6 2.6 %collective-permute-start.13 = (bf16[64,2176]{1,0:T(8,128)(2,1)}, bf16[64,2176]{1,0:T(8,128)(2,1)S(1)}, u32[]{:S(2)}, u32[]{:S(2)}) collective-permute-start(bf16[64,2176]{1,0:T(8,128)(2,1)} %select_convert_fusion.2), channel_id=1, source_target_pairs={{0,8},{4,12},{8,0},{12,4},{1,9},{5,13},{9,1},{13,5},{2,10},{6,14},... | collective-permute-start | bytes 835592 | tf_op jit(solution)/shard_map/ppermute | solution.py:240
  81.2 12.9 %partial_products.8 = (bf16[64,2176]{1,0:T(8,128)(2,1)S(1)}, f32[64,2176]{1,0:T(8,128)S(1)}) custom-call(s32[1]{0:T(128)} %bitcast.1.pos_ref, bf16[1,64,7168]{2,1,0:T(8,128)(2,1)} %collective-permute-done.9.refs_0_, bf16[1,64,7168]{2,1,0:T(8,128)(2,1)} %collective-permute-done.10.refs_1_, bf16[7168,2048]{1,0:T(8,128)(2,1)} %refs_2_.5, ...), custom_call_target="tpu_custom_call" | custom-call | tf_op jit(solution)/shard_map/partial_products/pallas_call | solution.py:110
  94.1 2.6 %collective-permute-done.11 = bf16[128,2176]{1,0:T(8,128)(2,1)} collective-permute-done((bf16[128,2176]{1,0:T(8,128)(2,1)}, bf16[128,2176]{1,0:T(8,128)(2,1)}, u32[]{:S(2)}, u32[]{:S(2)}) %collective-permute-start.11) | collective-permute-done | bytes 557088 | tf_op jit(solution)/shard_map/ppermute | solution.py:236
  100.7 4.0 %collective-permute-start.16 = (bf16[64,2176]{1,0:T(8,128)(2,1)}, bf16[64,2176]{1,0:T(8,128)(2,1)S(1)}, u32[]{:S(2)}, u32[]{:S(2)}) collective-permute-start(bf16[64,2176]{1,0:T(8,128)(2,1)} %select_convert_fusion.1), channel_id=1, source_target_pairs={{0,8},{4,12},{8,0},{12,4},{1,9},{5,13},{9,1},{13,5},{2,10},{6,14},... | collective-permute-start | bytes 835592 | tf_op jit(solution)/shard_map/ppermute | solution.py:240
  104.7 12.8 %partial_products.9 = (bf16[64,2048]{1,0:T(8,128)(2,1)S(1)}, f32[64,2048]{1,0:T(8,128)S(1)}, f32[64,128]{1,0:T(8,128)S(1)}, f32[64,128]{1,0:T(8,128)S(1)}) custom-call(s32[1]{0:T(128)} %bitcast.1.pos_ref, bf16[1,64,7168]{2,1,0:T(8,128)(2,1)} %collective-permute-done.12.refs_0_, bf16[1,64,7168]{2,1,0:T(8,128)(2,1)} %collective-permute-done.14.refs_1_, ...), custom_call_target="tpu_custom_call" | custom-call | tf_op jit(solution)/shard_map/partial_products/pallas_call | solution.py:110
  119.1 1.6 %collective-permute-start.17 = (bf16[64,2048]{1,0:T(8,128)(2,1)S(1)}, bf16[64,2048]{1,0:T(8,128)(2,1)S(1)}, u32[]{:S(2)}, u32[]{:S(2)}) collective-permute-start(bf16[64,2048]{1,0:T(8,128)(2,1)S(1)} %get-tuple-element.85), channel_id=1, source_target_pairs={{0,4},{4,0},{8,12},{12,8},{1,5},{5,1},{9,13},{13,9},{2,6},{6,2},{1... | collective-permute-start | bytes 786440 | tf_op jit(solution)/shard_map/ppermute | solution.py:236
  123.0 9.5 %collective-permute-done.17 = bf16[64,2048]{1,0:T(8,128)(2,1)S(1)} collective-permute-done((bf16[64,2048]{1,0:T(8,128)(2,1)S(1)}, bf16[64,2048]{1,0:T(8,128)(2,1)S(1)}, u32[]{:S(2)}, u32[]{:S(2)}) %collective-permute-start.17) | collective-permute-done | bytes 262176 | tf_op jit(solution)/shard_map/ppermute | solution.py:236
  132.6 3.3 %collective-permute-done.19.refs_5_ = bf16[64,2176]{1,0:T(8,128)(2,1)S(1)} collective-permute-done((bf16[64,2176]{1,0:T(8,128)(2,1)S(1)}, bf16[64,2176]{1,0:T(8,128)(2,1)S(1)}, u32[]{:S(2)}, u32[]{:S(2)}) %collective-permute-start.19) | collective-permute-done | bytes 278560 | tf_op jit(solution)/shard_map/ppermute | solution.py:240
  135.9 2.9 %collective-permute-start.24 = (bf16[64,2048]{1,0:T(8,128)(2,1)S(1)}, bf16[64,2048]{1,0:T(8,128)(2,1)S(1)}, u32[]{:S(2)}, u32[]{:S(2)}) collective-permute-start(bf16[64,2048]{1,0:T(8,128)(2,1)S(1)} %select_convert_fusion.3), channel_id=1, source_target_pairs={{0,8},{4,12},{8,0},{12,4},{1,9},{5,13},{9,1},{13,5},{2,10},{6,14},... | collective-permute-start | bytes 786440 | tf_op jit(solution)/shard_map/ppermute | solution.py:240
  138.8 2.5 %collective-permute-done.20 = f32[64,128]{1,0:T(8,128)S(1)} collective-permute-done((f32[64,128]{1,0:T(8,128)S(1)}, f32[64,128]{1,0:T(8,128)S(1)}, u32[]{:S(2)}, u32[]{:S(2)}) %collective-permute-start.20) | collective-permute-done | bytes 32800 | tf_op jit(solution)/shard_map/ppermute | solution.py:240
  141.4 1.5 %collective-permute-start.22 = (bf16[4,64,64]{2,1,0:T(8,128)(2,1)S(1)}, bf16[4,64,64]{2,1,0:T(8,128)(2,1)S(1)}, u32[]{:S(2)}, u32[]{:S(2)}) collective-permute-start(bf16[4,64,64]{2,1,0:T(8,128)(2,1)S(1)} %maximum_select_fusion), channel_id=1, source_target_pairs={{0,2},{1,3},{2,0},{3,1},{4,6},{5,7},{6,4},{7,5},{8,10},{9,11},{10,... | collective-permute-start | bytes 98312 | tf_op jit(solution)/shard_map/ppermute | solution.py:370
  143.5 2.2 %collective-permute-done.22 = bf16[4,64,64]{2,1,0:T(8,128)(2,1)S(1)} collective-permute-done((bf16[4,64,64]{2,1,0:T(8,128)(2,1)S(1)}, bf16[4,64,64]{2,1,0:T(8,128)(2,1)S(1)}, u32[]{:S(2)}, u32[]{:S(2)}) %collective-permute-start.22) | collective-permute-done | bytes 32800 | tf_op jit(solution)/shard_map/ppermute | solution.py:370
  147.3 2.1 %finish_steps.1 = (bf16[4,64,2048]{2,1,0:T(8,128)(2,1)}, bf16[64,2048]{1,0:T(8,128)(2,1)S(1)}) custom-call(bf16[256,64]{1,0:T(8,128)(2,1)S(1)} %bitcast.24, s32[256,1]{1,0:T(8,128)S(1)} %reshape.68.slot_ref, s32[4]{0:T(128)S(1)} %pad_add_fusion.order_ref, bf16[256,2048]{1,0:T(8,128)(2,1)S(1)} %bitcast.23, f32[64,2176]{1,0:T(8,128)S(1)} %get-tuple-element.72.refs_0_, ...), custom_call_target="tpu_custom_call" | custom-call | tf_op jit(solution)/shard_map/finish_steps/pallas_call | solution.py:165
  (96 shorter events, 16.6 us)
Async XLA Ops:
  0.0 99.9 %copy-start = (s32[256,1]{0,1:T(1,128)S(1)}, s32[256,1]{0,1:T(1,128)}, u32[]{:S(2)}) copy-start(s32[256,1]{0,1:T(1,128)} %param.10) | copy-start | bytes 3076
  0.0 7.9 %copy-start.3 = (bf16[1,7168,64]{1,2,0:T(8,128)(2,1)S(1)}, bf16[1,7168,64]{1,2,0:T(8,128)(2,1)}, u32[]{:S(2)}) copy-start(bf16[1,7168,64]{1,2,0:T(8,128)(2,1)} %param.8) | copy-start | bytes 2752516
  0.0 7.9 %collective-permute-start = (bf16[4,64,7168]{2,1,0:T(8,128)(2,1)}, bf16[4,64,7168]{2,1,0:T(8,128)(2,1)}, u32[]{:S(2)}, u32[]{:S(2)}) collective-permute-start(bf16[4,64,7168]{2,1,0:T(8,128)(2,1)} %refs_0_.5), channel_id=1, source_target_pairs={{0,1},{1,0},{2,3},{3,2},{4,5},{5,4},{6,7},{7,6},{8,9},{9,8},{10,11... | collective-permute-start | bytes 11010056 | tf_op jit(solution)/shard_map/ppermute | solution.py:230
  2.7 23.7 %collective-permute-start.1 = (bf16[1,64,7168]{2,1,0:T(8,128)(2,1)}, bf16[1,64,7168]{2,1,0:T(8,128)(2,1)S(1)}, u32[]{:S(2)}, u32[]{:S(2)}) collective-permute-start(bf16[1,64,7168]{2,1,0:T(8,128)(2,1)} %slice.77), channel_id=1, source_target_pairs={{2,0},{0,2},{3,1},{1,3},{6,4},{4,6},{7,5},{5,7},{10,8},{8,10},{11,... | collective-permute-start | bytes 2752520 | tf_op jit(solution)/shard_map/ppermute | solution.py:233
  5.3 24.5 %collective-permute-start.4 = (bf16[1,64,2048]{2,1,0:T(8,128)(2,1)S(1)}, bf16[1,64,2048]{2,1,0:T(8,128)(2,1)}, u32[]{:S(2)}, u32[]{:S(2)}) collective-permute-start(bf16[1,64,2048]{2,1,0:T(8,128)(2,1)S(1)} %copy-done.16), channel_id=1, source_target_pairs={{0,8},{4,12},{8,0},{12,4},{1,9},{5,13},{9,1},{13,5},{2,10},{6,14},... | collective-permute-start | bytes 786440 | tf_op jit(solution)/shard_map/ppermute | solution.py:236
  26.4 7.2 %collective-permute-start.2 = (bf16[1,64,7168]{2,1,0:T(8,128)(2,1)S(1)}, bf16[1,64,7168]{2,1,0:T(8,128)(2,1)}, u32[]{:S(2)}, u32[]{:S(2)}) collective-permute-start(bf16[1,64,7168]{2,1,0:T(8,128)(2,1)S(1)} %collective-permute-done.1.refs_2_), channel_id=1, source_target_pairs={{0,1},{1,0},{2,3},{3,2},{4,5},{5,4},{6,7},{7,6},{8,9},{9,8},{10,11... | collective-permute-start | bytes 2752520 | tf_op jit(solution)/shard_map/ppermute | solution.py:230
  28.0 23.1 %collective-permute-start.3 = (bf16[1,64,7168]{2,1,0:T(8,128)(2,1)}, bf16[1,64,7168]{2,1,0:T(8,128)(2,1)}, u32[]{:S(2)}, u32[]{:S(2)}) collective-permute-start(bf16[1,64,7168]{2,1,0:T(8,128)(2,1)} %get-tuple-element.101), channel_id=1, source_target_pairs={{2,0},{0,2},{3,1},{1,3},{6,4},{4,6},{7,5},{5,7},{10,8},{8,10},{11,... | collective-permute-start | bytes 2752520 | tf_op jit(solution)/shard_map/ppermute | solution.py:233
  31.6 19.6 %collective-permute-start.5 = (bf16[2,64,2048]{2,1,0:T(8,128)(2,1)}, bf16[2,64,2048]{2,1,0:T(8,128)(2,1)}, u32[]{:S(2)}, u32[]{:S(2)}) collective-permute-start(bf16[2,64,2048]{2,1,0:T(8,128)(2,1)} %pad_maximum_fusion.1), channel_id=1, source_target_pairs={{0,4},{4,0},{8,12},{12,8},{1,5},{5,1},{9,13},{13,9},{2,6},{6,2},{1... | collective-permute-start | bytes 1572872 | tf_op jit(solution)/shard_map/ppermute | solution.py:236
  33.1 25.4 %collective-permute-start.8 = (bf16[128,2176]{1,0:T(8,128)(2,1)}, bf16[128,2176]{1,0:T(8,128)(2,1)}, u32[]{:S(2)}, u32[]{:S(2)}) collective-permute-start(bf16[128,2176]{1,0:T(8,128)(2,1)} %get-tuple-element.65), channel_id=1, source_target_pairs={{0,4},{4,0},{8,12},{12,8},{1,5},{5,1},{9,13},{13,9},{2,6},{6,2},{1... | collective-permute-start | bytes 1671176 | tf_op jit(solution)/shard_map/ppermute | solution.py:236
  51.1 8.7 %collective-permute-start.6 = (bf16[1,64,7168]{2,1,0:T(8,128)(2,1)}, bf16[1,64,7168]{2,1,0:T(8,128)(2,1)S(1)}, u32[]{:S(2)}, u32[]{:S(2)}) collective-permute-start(bf16[1,64,7168]{2,1,0:T(8,128)(2,1)} %collective-permute-done.3.refs_2_), channel_id=1, source_target_pairs={{0,1},{1,0},{2,3},{3,2},{4,5},{5,4},{6,7},{7,6},{8,9},{9,8},{10,11... | collective-permute-start | bytes 2752520 | tf_op jit(solution)/shard_map/ppermute | solution.py:230
  52.4 22.9 %collective-permute-start.9 = (bf16[1,64,7168]{2,1,0:T(8,128)(2,1)S(1)}, bf16[1,64,7168]{2,1,0:T(8,128)(2,1)}, u32[]{:S(2)}, u32[]{:S(2)}) collective-permute-start(bf16[1,64,7168]{2,1,0:T(8,128)(2,1)S(1)} %copy-done.17), channel_id=1, source_target_pairs={{2,0},{0,2},{3,1},{1,3},{6,4},{4,6},{7,5},{5,7},{10,8},{8,10},{11,... | collective-permute-start | bytes 2752520 | tf_op jit(solution)/shard_map/ppermute | solution.py:233
  54.2 18.6 %collective-permute-start.7 = (bf16[128,2176]{1,0:T(8,128)(2,1)S(1)}, bf16[128,2176]{1,0:T(8,128)(2,1)S(1)}, u32[]{:S(2)}, u32[]{:S(2)}) collective-permute-start(bf16[128,2176]{1,0:T(8,128)(2,1)S(1)} %get-tuple-element.62), channel_id=1, source_target_pairs={{0,4},{4,0},{8,12},{12,8},{1,5},{5,1},{9,13},{13,9},{2,6},{6,2},{1... | collective-permute-start | bytes 1671176 | tf_op jit(solution)/shard_map/ppermute | solution.py:236
  59.8 13.1 %copy-start.12 = (f32[128,2176]{1,0:T(8,128)}, f32[128,2176]{1,0:T(8,128)S(1)}, u32[]{:S(2)}) copy-start(f32[128,2176]{1,0:T(8,128)S(1)} %convert_add_fusion.1) | copy-start | bytes 3342340
  75.3 5.9 %collective-permute-start.10 = (bf16[1,64,7168]{2,1,0:T(8,128)(2,1)}, bf16[1,64,7168]{2,1,0:T(8,128)(2,1)}, u32[]{:S(2)}, u32[]{:S(2)}) collective-permute-start(bf16[1,64,7168]{2,1,0:T(8,128)(2,1)} %collective-permute-done.9.refs_0_), channel_id=1, source_target_pairs={{0,1},{1,0},{2,3},{3,2},{4,5},{5,4},{6,7},{7,6},{8,9},{9,8},{10,11... | collective-permute-start | bytes 2752520 | tf_op jit(solution)/shard_map/ppermute | solution.py:230
  75.3 21.4 %collective-permute-start.11 = (bf16[128,2176]{1,0:T(8,128)(2,1)}, bf16[128,2176]{1,0:T(8,128)(2,1)}, u32[]{:S(2)}, u32[]{:S(2)}) collective-permute-start(bf16[128,2176]{1,0:T(8,128)(2,1)} %get-tuple-element.70), channel_id=1, source_target_pairs={{0,4},{4,0},{8,12},{12,8},{1,5},{5,1},{9,13},{13,9},{2,6},{6,2},{1... | collective-permute-start | bytes 1671176 | tf_op jit(solution)/shard_map/ppermute | solution.py:236
  77.1 22.8 %collective-permute-start.12 = (bf16[1,64,7168]{2,1,0:T(8,128)(2,1)}, bf16[1,64,7168]{2,1,0:T(8,128)(2,1)}, u32[]{:S(2)}, u32[]{:S(2)}) collective-permute-start(bf16[1,64,7168]{2,1,0:T(8,128)(2,1)} %get-tuple-element.99), channel_id=1, source_target_pairs={{2,0},{0,2},{3,1},{1,3},{6,4},{4,6},{7,5},{5,7},{10,8},{8,10},{11,... | collective-permute-start | bytes 2752520 | tf_op jit(solution)/shard_map/ppermute | solution.py:233
  78.6 21.3 %collective-permute-start.13 = (bf16[64,2176]{1,0:T(8,128)(2,1)}, bf16[64,2176]{1,0:T(8,128)(2,1)S(1)}, u32[]{:S(2)}, u32[]{:S(2)}) collective-permute-start(bf16[64,2176]{1,0:T(8,128)(2,1)} %select_convert_fusion.2), channel_id=1, source_target_pairs={{0,8},{4,12},{8,0},{12,4},{1,9},{5,13},{9,1},{13,5},{2,10},{6,14},... | collective-permute-start | bytes 835592 | tf_op jit(solution)/shard_map/ppermute | solution.py:240
  99.9 17.6 %copy-start.6 = (bf16[64,2176]{1,0:T(8,128)(2,1)}, bf16[64,2176]{1,0:T(8,128)(2,1)S(1)}, u32[]{:S(2)}) copy-start(bf16[64,2176]{1,0:T(8,128)(2,1)S(1)} %collective-permute-done.13.refs_1_) | copy-start | bytes 835588
  99.9 4.7 %collective-permute-start.14 = (bf16[1,64,7168]{2,1,0:T(8,128)(2,1)}, bf16[1,64,7168]{2,1,0:T(8,128)(2,1)}, u32[]{:S(2)}, u32[]{:S(2)}) collective-permute-start(bf16[1,64,7168]{2,1,0:T(8,128)(2,1)} %collective-permute-done.12.refs_0_), channel_id=1, source_target_pairs={{0,1},{1,0},{2,3},{3,2},{4,5},{5,4},{6,7},{7,6},{8,9},{9,8},{10,11... | collective-permute-start | bytes 2752520 | tf_op jit(solution)/shard_map/ppermute | solution.py:230
  100.1 17.4 %collective-permute-start.15 = (bf16[64,2176]{1,0:T(8,128)(2,1)}, bf16[64,2176]{1,0:T(8,128)(2,1)}, u32[]{:S(2)}, u32[]{:S(2)}) collective-permute-start(bf16[64,2176]{1,0:T(8,128)(2,1)} %copy-done.8), channel_id=1, source_target_pairs={{0,4},{4,0},{8,12},{12,8},{1,5},{5,1},{9,13},{13,9},{2,6},{6,2},{1... | collective-permute-start | bytes 835592 | tf_op jit(solution)/shard_map/ppermute | solution.py:236
  100.6 16.9 %copy-start.5 = (f32[64,2176]{1,0:T(8,128)S(1)}, f32[64,2176]{1,0:T(8,128)}, u32[]{:S(2)}) copy-start(f32[64,2176]{1,0:T(8,128)} %copy-done.4) | copy-start | bytes 1671172
  100.7 16.9 %copy-start.11 = (f32[128,2176]{1,0:T(8,128)S(1)}, f32[128,2176]{1,0:T(8,128)}, u32[]{:S(2)}) copy-start(f32[128,2176]{1,0:T(8,128)} %copy-done.9) | copy-start | bytes 3342340
  100.7 18.0 %collective-permute-start.16 = (bf16[64,2176]{1,0:T(8,128)(2,1)}, bf16[64,2176]{1,0:T(8,128)(2,1)S(1)}, u32[]{:S(2)}, u32[]{:S(2)}) collective-permute-start(bf16[64,2176]{1,0:T(8,128)(2,1)} %select_convert_fusion.1), channel_id=1, source_target_pairs={{0,8},{4,12},{8,0},{12,4},{1,9},{5,13},{9,1},{13,5},{2,10},{6,14},... | collective-permute-start | bytes 835592 | tf_op jit(solution)/shard_map/ppermute | solution.py:240
  118.7 4.3 %collective-permute-start.18 = (f32[64,128]{1,0:T(8,128)S(1)}, f32[64,128]{1,0:T(8,128)S(1)}, u32[]{:S(2)}, u32[]{:S(2)}) collective-permute-start(f32[64,128]{1,0:T(8,128)S(1)} %get-tuple-element.88), channel_id=1, source_target_pairs={{0,4},{4,0},{8,12},{12,8},{1,5},{5,1},{9,13},{13,9},{2,6},{6,2},{1... | collective-permute-start | bytes 98312 | tf_op jit(solution)/shard_map/ppermute | solution.py:236
  119.1 13.4 %collective-permute-start.17 = (bf16[64,2048]{1,0:T(8,128)(2,1)S(1)}, bf16[64,2048]{1,0:T(8,128)(2,1)S(1)}, u32[]{:S(2)}, u32[]{:S(2)}) collective-permute-start(bf16[64,2048]{1,0:T(8,128)(2,1)S(1)} %get-tuple-element.85), channel_id=1, source_target_pairs={{0,4},{4,0},{8,12},{12,8},{1,5},{5,1},{9,13},{13,9},{2,6},{6,2},{1... | collective-permute-start | bytes 786440 | tf_op jit(solution)/shard_map/ppermute | solution.py:236
  120.8 15.1 %collective-permute-start.19 = (bf16[64,2176]{1,0:T(8,128)(2,1)S(1)}, bf16[64,2176]{1,0:T(8,128)(2,1)S(1)}, u32[]{:S(2)}, u32[]{:S(2)}) collective-permute-start(bf16[64,2176]{1,0:T(8,128)(2,1)S(1)} %select_convert_fusion), channel_id=1, source_target_pairs={{0,8},{4,12},{8,0},{12,4},{1,9},{5,13},{9,1},{13,5},{2,10},{6,14},... | collective-permute-start | bytes 835592 | tf_op jit(solution)/shard_map/ppermute | solution.py:240
  135.9 5.4 %collective-permute-start.20 = (f32[64,128]{1,0:T(8,128)S(1)}, f32[64,128]{1,0:T(8,128)S(1)}, u32[]{:S(2)}, u32[]{:S(2)}) collective-permute-start(f32[64,128]{1,0:T(8,128)S(1)} %get-tuple-element.92), channel_id=1, source_target_pairs={{0,8},{4,12},{8,0},{12,4},{1,9},{5,13},{9,1},{13,5},{2,10},{6,14},... | collective-permute-start | bytes 98312 | tf_op jit(solution)/shard_map/ppermute | solution.py:240
  135.9 13.5 %collective-permute-start.24 = (bf16[64,2048]{1,0:T(8,128)(2,1)S(1)}, bf16[64,2048]{1,0:T(8,128)(2,1)S(1)}, u32[]{:S(2)}, u32[]{:S(2)}) collective-permute-start(bf16[64,2048]{1,0:T(8,128)(2,1)S(1)} %select_convert_fusion.3), channel_id=1, source_target_pairs={{0,8},{4,12},{8,0},{12,4},{1,9},{5,13},{9,1},{13,5},{2,10},{6,14},... | collective-permute-start | bytes 786440 | tf_op jit(solution)/shard_map/ppermute | solution.py:240
  141.4 5.8 %copy-start.7 = (bf16[64,2176]{1,0:T(8,128)(2,1)S(1)}, bf16[64,2176]{1,0:T(8,128)(2,1)}, u32[]{:S(2)}) copy-start(bf16[64,2176]{1,0:T(8,128)(2,1)} %copy-done.6) | copy-start | bytes 835588
  141.4 4.3 %collective-permute-start.22 = (bf16[4,64,64]{2,1,0:T(8,128)(2,1)S(1)}, bf16[4,64,64]{2,1,0:T(8,128)(2,1)S(1)}, u32[]{:S(2)}, u32[]{:S(2)}) collective-permute-start(bf16[4,64,64]{2,1,0:T(8,128)(2,1)S(1)} %maximum_select_fusion), channel_id=1, source_target_pairs={{0,2},{1,3},{2,0},{3,1},{4,6},{5,7},{6,4},{7,5},{8,10},{9,11},{10,... | collective-permute-start | bytes 98312 | tf_op jit(solution)/shard_map/ppermute | solution.py:370
  143.0 3.2 %collective-permute-start.23 = (bf16[4,64,64]{2,1,0:T(8,128)(2,1)S(1)}, bf16[4,64,64]{2,1,0:T(8,128)(2,1)S(1)}, u32[]{:S(2)}, u32[]{:S(2)}) collective-permute-start(bf16[4,64,64]{2,1,0:T(8,128)(2,1)S(1)} %maximum_select_fusion), channel_id=1, source_target_pairs={{0,3},{1,0},{2,1},{3,2},{4,7},{5,4},{6,5},{7,6},{8,11},{9,8},{10,9... | collective-permute-start | bytes 98312 | tf_op jit(solution)/shard_map/ppermute | solution.py:370
  143.0 4.2 %collective-permute-start.21 = (bf16[4,64,64]{2,1,0:T(8,128)(2,1)S(1)}, bf16[4,64,64]{2,1,0:T(8,128)(2,1)S(1)}, u32[]{:S(2)}, u32[]{:S(2)}) collective-permute-start(bf16[4,64,64]{2,1,0:T(8,128)(2,1)S(1)} %maximum_select_fusion), channel_id=1, source_target_pairs={{0,1},{1,2},{2,3},{3,0},{4,5},{5,6},{6,7},{7,4},{8,9},{9,10},{10,1... | collective-permute-start | bytes 98312 | tf_op jit(solution)/shard_map/ppermute | solution.py:370
  (13 other events, 39.4 us)

commit v6 on v5

v6 whole, which is shorter than its diff:
```python
import functools

import jax
import jax.numpy as jnp
from jax import lax
from jax.experimental import pallas as pl
from jax.experimental.pallas import tpu as pltpu
from jax.sharding import PartitionSpec as P

ADAPTER_SCALE = 0.5
BLOCK_N = 256
BLOCK_VALUES = 1024 * 1024
BUFFERS = 3
WIDE_ROWS = 128
RANK_NAME = 1000
VMEM_BYTES = 24 * 1024 * 1024


def block_depth(depth, width, rows):
    values = BLOCK_VALUES * (2 if rows >= WIDE_ROWS else 1)
    for size in (1024, 512, 256):
        if depth % size == 0 and size * width <= values:
            return size
    return depth


def rank_columns(factors):
    slots, rank, _ = factors.shape
    return -(-slots * rank // 128) * 128


def matmul_body(spans, begin, mixed, kind, pos_ref, *refs):
    sources = refs[:len(spans)]
    mine_ref = refs[len(spans)] if mixed else None
    refs = refs[len(spans) + mixed:]
    w_ref, a_ref = refs[:2]
    outs = refs[2:-5]
    x_ref, w_buf, total_ref, x_sems, w_sems = refs[-5:]
    blocks, per_block, depth = x_ref.shape
    rows = blocks * per_block
    width = w_ref.shape[1]
    slots, rank, _ = a_ref.shape
    buffers, block_k, _ = w_buf.shape
    block_n = min(BLOCK_N, width)
    count = depth // block_k
    own_at = pos_ref[0]

    def fetch(block, slot):
        return pltpu.make_async_copy(
            w_ref.at[pl.ds(block * block_k, block_k)], w_buf.at[slot], w_sems.at[slot]
        )

    copies = []
    for index, (first, steps, place, core) in enumerate(spans):
        at = place if core is None else place + (own_at if core == 0 else 1 - own_at)
        copies.append(pltpu.make_async_copy(
            sources[index].at[pl.ds(first, steps)], x_ref.at[pl.ds(at, steps)], x_sems.at[index]
        ))
    for copy in copies:
        copy.start()
    for block in range(buffers):
        fetch(block, block).start()
    pieces = []
    if kind == "own":
        for index, out_ref in enumerate(outs[1:]):
            pieces.append(pltpu.make_async_copy(
                sources[0].at[pl.ds(index + 1, 1)], out_ref, x_sems.at[len(spans) + index]
            ))
            pieces[-1].start()
    total_ref[...] = jnp.zeros_like(total_ref)
    for copy in copies:
        copy.wait()
    for slot in range(slots):
        total_ref[:, width + slot * rank:width + (slot + 1) * rank] = lax.dot_general(
            x_ref[...].reshape(rows, depth), a_ref[slot], (((1,), (1,)), ((), ())),
            preferred_element_type=jnp.float32,
        )

    @pl.loop(0, count)
    def _(block):
        slot = lax.rem(block, buffers)
        fetch(block, slot).wait()
        inner = pl.ds(pl.multiple_of(block * block_k, block_k), block_k)
        x = x_ref[:, :, inner].reshape(rows, block_k)
        for place in range(width // block_n):
            columns = slice(place * block_n, (place + 1) * block_n)
            total_ref[:, columns] += jnp.dot(x, w_buf[slot, :, columns], preferred_element_type=jnp.float32)

        @pl.when(block + buffers < count)
        def _():
            fetch(block + buffers, slot).start()

    if kind == "own":
        outs[0][...] = total_ref[...]
        for copy in pieces:
            copy.wait()
        return
    send_ref, keep_ref = outs[:2]
    columns = slice(0, send_ref.shape[1])
    split = rows - 2 * per_block
    if mixed:
        own_sent = own_at == 0
        mine, other = mine_ref[begin * per_block:begin * per_block + split], total_ref[:split]
        send_ref[:split] = jnp.where(own_sent, mine, other).astype(send_ref.dtype)
        keep_ref[:split] = jnp.where(own_sent, other, mine)
    send_ref[split:] = total_ref[split:split + per_block, columns].astype(send_ref.dtype)
    keep_ref[split:] = total_ref[split + per_block:, columns]
    if kind == "apart":
        outs[2][...] = total_ref[split:split + per_block, width:]
        outs[3][...] = total_ref[split + per_block:, width:]


def call_matmul(name, body, pos, sources, mine, weight, factors, blocks, out_shape, out_specs, copies):
    _, per_block, depth = sources[0].shape
    width = weight.shape[1]
    block_k = block_depth(depth, width, blocks * per_block // 2)
    buffers = min(BUFFERS if blocks * per_block >= 2 * WIDE_ROWS else 2 * BUFFERS, depth // block_k)
    any_spec = pl.BlockSpec(memory_space=pl.ANY)
    vmem_spec = pl.BlockSpec(memory_space=pltpu.VMEM)
    return pl.pallas_call(
        body,
        in_specs=[pl.BlockSpec(memory_space=pltpu.SMEM)] + [any_spec] * len(sources)
        + [vmem_spec] * len(mine) + [any_spec, vmem_spec],
        out_specs=out_specs,
        out_shape=out_shape,
        scratch_shapes=[
            pltpu.VMEM((blocks, per_block, depth), jnp.bfloat16),
            pltpu.VMEM((buffers, block_k, width), jnp.bfloat16),
            pltpu.VMEM((blocks * per_block, width + rank_columns(factors)), jnp.float32),
            pltpu.SemaphoreType.DMA((copies,)),
            pltpu.SemaphoreType.DMA((buffers,)),
        ],
        compiler_params=pltpu.CompilerParams(vmem_limit_bytes=VMEM_BYTES),
        cost_estimate=pl.CostEstimate(flops=0, bytes_accessed=0, transcendentals=0),
        name=name,
    )(pos, *sources, *mine, weight, factors)


def own_products(pos, hidden, weight, factors):
    steps, per_block, depth = hidden.shape
    columns = weight.shape[1] + rank_columns(factors)
    spans = ((0, steps, 0, None),)
    any_spec = pl.BlockSpec(memory_space=pl.ANY)
    return call_matmul(
        "own_products", functools.partial(matmul_body, spans, 0, 0, "own"), pos, [hidden], [], weight, factors, steps,
        [jax.ShapeDtypeStruct((steps * per_block, columns), jnp.float32)]
        + [jax.ShapeDtypeStruct((1, per_block, depth), hidden.dtype)] * (steps - 1),
        [pl.BlockSpec(memory_space=pltpu.VMEM)] + [any_spec] * (steps - 1),
        steps,
    )


def pair_products(pos, own, sib, weight, factors, apart, siblings=None, mine=None, first=0, steps=0):
    _, per_block, _ = own.shape
    width, extra = weight.shape[1], rank_columns(factors)
    spans = ((first, steps, 0, None),) if steps else ()
    spans += ((0, 1, steps, 0), (0, 1, steps, 1))
    rows = (steps + 1) * per_block
    columns = width + (0 if apart else extra)
    out_shape = [
        jax.ShapeDtypeStruct((rows, columns), jnp.bfloat16),
        jax.ShapeDtypeStruct((rows, columns), jnp.float32),
    ] + [jax.ShapeDtypeStruct((rows, extra), jnp.float32)] * (2 if apart else 0)
    body = functools.partial(matmul_body, spans, first, 1 if steps else 0, "apart" if apart else "joined")
    return call_matmul(
        "pair_products", body, pos, ([siblings] if steps else []) + [own, sib], [mine] if steps else [], weight,
        factors, steps + 2, out_shape, [pl.BlockSpec(memory_space=pltpu.VMEM)] * len(out_shape), len(spans),
    )


def finish_body(received, panels, chosen_ref, slot_ref, order_ref, *refs):
    panel_refs, refs = refs[:panels], refs[panels:]
    per_panel = panel_refs[0].shape[0]
    out_ref, lifted_ref, done_ref, sem = refs[-4:]
    steps, rows, width = done_ref.shape
    rank = chosen_ref.shape[1]
    chosen = chosen_ref[...]
    slot = slot_ref[...]
    spread = jnp.concatenate(
        [
            jnp.where(slot == order_ref[place], chosen, jnp.zeros_like(chosen))
            for place in range(panels * per_panel // rank)
        ],
        axis=1,
    )
    block_n = min(BLOCK_N, width)
    for place in range(width // block_n):
        columns = slice(place * block_n, (place + 1) * block_n)
        panel = jnp.concatenate([panel_ref[:, columns] for panel_ref in panel_refs], axis=0)
        lifted = jnp.dot(spread, panel, preferred_element_type=jnp.float32).astype(jnp.bfloat16)
        for step in range(steps):
            total = refs[step * (received + 1)][:, columns]
            for value_ref in refs[step * (received + 1) + 1:(step + 1) * (received + 1)]:
                total = total + value_ref[:, columns].astype(jnp.float32)
            value = total + ADAPTER_SCALE * lifted[step * rows:(step + 1) * rows].astype(jnp.float32)
            done_ref[step, :, columns] = value.astype(done_ref.dtype)
        lifted_ref[:, columns] = lifted[steps * rows:]
    copy = pltpu.make_async_copy(done_ref, out_ref.at[pl.ds(0, steps)], sem)
    copy.start()
    copy.wait()


def finish_steps(totals, chosen, slots, order, panels):
    steps, width = len(totals), panels[0].shape[1]
    rows = chosen.shape[0] // (steps + 1)
    vmem_spec = pl.BlockSpec(memory_space=pltpu.VMEM)
    arrays = [value for total in totals for value in total]
    return pl.pallas_call(
        functools.partial(finish_body, len(totals[0]) - 1, len(panels)),
        in_specs=[vmem_spec, vmem_spec, pl.BlockSpec(memory_space=pltpu.SMEM)] + [vmem_spec] * (len(panels) + len(arrays)),
        out_specs=[pl.BlockSpec(memory_space=pl.ANY), vmem_spec],
        out_shape=[
            jax.ShapeDtypeStruct((steps + 1, rows, width), jnp.bfloat16),
            jax.ShapeDtypeStruct((rows, width), jnp.bfloat16),
        ],
        scratch_shapes=[pltpu.VMEM((steps, rows, width), jnp.bfloat16), pltpu.SemaphoreType.DMA],
        compiler_params=pltpu.CompilerParams(vmem_limit_bytes=VMEM_BYTES),
        cost_estimate=pl.CostEstimate(flops=0, bytes_accessed=0, transcendentals=0),
        name="finish_steps",
    )(chosen, slots, order, *panels, *arrays)


def last_body(partial_ref, lifted_ref, *refs):
    out_ref, done_ref, sem = refs[-3:]
    total = refs[0][...]
    for value_ref in refs[1:-3]:
        total = total + value_ref[...].astype(jnp.float32)
    value = total + ADAPTER_SCALE * lifted_ref[...].astype(jnp.float32)
    done_ref[0] = value.astype(done_ref.dtype)
    copy = pltpu.make_async_copy(done_ref, out_ref.at[pl.ds(out_ref.shape[0] - 1, 1)], sem)
    copy.start()
    copy.wait()


def finish_last(partial, lifted, arrays):
    vmem_spec = pl.BlockSpec(memory_space=pltpu.VMEM)
    any_spec = pl.BlockSpec(memory_space=pl.ANY)
    return pl.pallas_call(
        last_body,
        in_specs=[any_spec] + [vmem_spec] * (1 + len(arrays)),
        out_specs=any_spec,
        out_shape=jax.ShapeDtypeStruct(partial.shape, partial.dtype),
        input_output_aliases={0: 0},
        scratch_shapes=[pltpu.VMEM((1,) + partial.shape[1:], partial.dtype), pltpu.SemaphoreType.DMA],
        compiler_params=pltpu.CompilerParams(vmem_limit_bytes=VMEM_BYTES),
        cost_estimate=pl.CostEstimate(flops=0, bytes_accessed=0, transcendentals=0),
        name="finish_last",
    )(partial, lifted, *arrays)


def per_device(hidden, base_weight, down_a, up_b, adapter_ids, owner_map):
    step_count, per_block, _ = hidden.shape
    n_tensor = lax.axis_size("tp")
    n_rep = lax.axis_size("rep")
    n_sub = lax.axis_size("sub")
    n_owners = n_rep * n_sub
    tensor_index = lax.axis_index("tp")
    rep_index = lax.axis_index("rep")
    sub_index = lax.axis_index("sub")
    owner_index = lax.axis_index(("rep", "sub"))
    requests = per_block * n_owners
    rows_mine = requests // n_tensor
    group = n_tensor // n_rep
    group_index = tensor_index // group
    owned_slots, _, rank_size = down_a.shape
    slot_count = owned_slots * n_owners
    width = base_weight.shape[1]

    def after(value, *done):
        return lax.optimization_barrier((value, *done))[0]

    def swap_cores(value):
        return lax.ppermute(value, "sub", [(i, i ^ 1) for i in range(n_sub)])

    def from_rep(value, shift):
        return lax.ppermute(value, "rep", [((i + shift) % n_rep, i) for i in range(n_rep)])

    def swap_tensor(value, bit):
        return lax.ppermute(value, "tp", [(i, i ^ bit) for i in range(n_tensor)])

    def to_group(value, hop):
        moved = group * hop
        return lax.ppermute(value, "tp", [(i, (i + moved) % n_tensor) for i in range(n_tensor)])

    def pick(values, index):
        value = values[0]
        for at in range(1, len(values)):
            value = jnp.where(index == at, values[at], value)
        return value

    keeps = (tensor_index // (group // 2)) % 2
    pos = (sub_index == keeps).astype(jnp.int32).reshape(1)

    siblings = swap_cores(hidden)
    pieces = [(step, shift) for step in range(step_count) for shift in range(1, n_rep)]
    remote = {(0, shift): from_rep(hidden[:1], shift) for shift in range(1, n_rep)}

    def spread_panels(panels, order, bits):
        for bit in bits:
            panels = panels + [swap_tensor(panel, bit) for panel in panels]
            order = order + [at ^ bit for at in order]
        return panels, order

    bits = [n_tensor >> at for at in range(1, n_tensor.bit_length())]
    panels, order = spread_panels([up_b], [0], bits[:1])
    my_ids = lax.dynamic_slice_in_dim(adapter_ids, tensor_index * rows_mine, rows_mine)
    iota = lax.broadcasted_iota(jnp.int32, (rows_mine, slot_count), 1)
    my_slot = jnp.sum((my_ids == iota).astype(jnp.int32) * owner_map[None, :], axis=1)
    owned_hot = my_slot[:, None] == (
        owner_index * owned_slots + lax.broadcasted_iota(jnp.int32, (rows_mine, owned_slots), 1)
    )

    first_leg, halved, begun, second_leg, ended = [], {}, set(), [], {}

    def second_half(total, received, steps, kind):
        total = total + received.astype(jnp.float32)
        rows, columns = total.shape
        extent, bit = rows // steps, group // 4
        while bit:
            extent //= 2
            halves = total.reshape(steps, 2, extent, columns)
            mine = (tensor_index // bit) % 2
            kept = lax.dynamic_index_in_dim(halves, mine, 1, keepdims=False)
            sent = lax.dynamic_index_in_dim(halves, 1 - mine, 1, keepdims=False)
            total = kept + swap_tensor(sent.astype(kind), bit).astype(jnp.float32)
            bit //= 2
        return total.reshape(steps, extent, columns)

    def gap(token, jobs, *extra, short=False):
        nonlocal first_leg, second_leg
        for parts, received, keep, kind in first_leg:
            steps = sum(length for _, length in parts)
            total, begin = second_half(after(keep, token), received, steps, kind), 0
            for key, length in parts:
                for at in range(begin, begin + length):
                    halved[key[0] + at - begin, key[1]] = total[at]
                    if (key[0] + at - begin, key[1]) == (step_count - 1, 0):
                        halved[RANK_NAME, 0] = total[at][:, width:]
                begin += length
        closed, waiting = {}, second_leg if short else []
        for name, kept, received in [] if short else second_leg:
            closed[name] = (after(kept, token), *received)
        started, sends = [], []
        for name in sorted({name for name, _ in halved}):
            if name in begun or name == RANK_NAME or any((name, at) not in halved for at in range(n_rep)):
                continue
            begun.add(name)
            values = [halved[name, at] for at in range(n_rep)]
            columns = min(value.shape[1] for value in values)
            values = [value[:, :columns] for value in values]
            kept = pick(values, (group_index - rep_index) % n_rep)
            sent = [pick(values, (group_index + hop - rep_index) % n_rep).astype(jnp.bfloat16) for hop in range(1, n_rep)]
            started.append((name, kept))
            sends.append(sent)
        first_sends = [job[1] for job in jobs]
        first_sends, sends, extra, closed, _ = lax.optimization_barrier((first_sends, sends, extra, closed, token))
        ended.update(closed)
        first_leg = [
            (parts, swap_tensor(send, group // 2), keep, kind) for (parts, _, keep, kind), send in zip(jobs, first_sends)
        ]
        second_leg = waiting + [
            (name, kept, [to_group(value, hop + 1) for hop, value in enumerate(sent)])
            for (name, kept), sent in zip(started, sends)
        ]
        return extra

    factors = jnp.swapaxes(down_a, 1, 2)

    half = step_count // 2
    source = pltpu.with_memory_space_constraint(hidden, pltpu.HBM)
    mine, *slices = own_products(pos, source, base_weight, factors)
    for step in range(1, step_count):
        for shift in range(1, n_rep):
            remote[step, shift] = from_rep(slices[step - 1], shift)
    send, jobs, joined, last_ranks = mine, [], 0, {}
    for piece, (step, shift) in enumerate(pieces):
        own, siblings, panels = gap(send, jobs, remote[step, shift], siblings, panels)
        if piece == 0:
            panels, order = spread_panels(panels, order, bits[1:])
        sib = swap_cores(own)
        if piece == len(pieces) - 1:
            own, sib = gap(send, [], own, sib, short=True)
        last, parts, extra = step == step_count - 1, [((step, shift), 1)], {}
        if joined < step_count:
            parts.insert(0, ((joined, 0), half))
            extra = dict(
                siblings=siblings, mine=mine, first=joined, steps=half
            )
            joined += half
        send, keep, *ranks = pair_products(pos, own, sib, base_weight, factors, last, **extra)
        jobs = [(parts, send, keep, jnp.bfloat16)]
        if last:
            last_ranks[shift] = ranks
    last_ranks, = gap(send, jobs, last_ranks)
    for shift, ranks in last_ranks.items():
        halved[RANK_NAME, shift] = second_half(ranks[1], swap_tensor(ranks[0], group // 2), 1, jnp.float32)[0]
    values = [halved[RANK_NAME, at] for at in range(n_rep)]
    ended[RANK_NAME] = (pick(values, (group_index - rep_index) % n_rep), *[
        to_group(pick(values, (group_index + hop - rep_index) % n_rep), hop) for hop in range(1, n_rep)
    ])
    def rank_sum(name):
        kept, *received = [value[:, -rank_columns(factors):] for value in ended[name]]
        for value in received:
            kept = kept + value.astype(jnp.float32)
        return kept[:, :owned_slots * rank_size]

    finished = jnp.stack([rank_sum(step) for step in range(step_count - 1)] + [rank_sum(RANK_NAME)])
    finished = finished.astype(jnp.bfloat16).reshape(step_count, rows_mine, owned_slots, rank_size)
    finished, = gap(send, [], finished)
    ended.update((name, (kept, *received)) for name, kept, received in second_leg)
    masked = jnp.sum(
        jnp.where(owned_hot[None, :, :, None], finished, 0), axis=2, dtype=jnp.float32
    ).astype(jnp.bfloat16)
    chosen = masked
    for turn in range(1, n_owners):
        chosen = chosen + lax.ppermute(
            masked, ("rep", "sub"), [(i, (i + turn) % n_owners) for i in range(n_owners)]
        )
    panel_slots = jnp.stack([
        (tensor_index ^ at) * up_b.shape[0] + each for at in order for each in range(up_b.shape[0])
    ]).astype(jnp.int32)

    panels = [panel.reshape(-1, width) for panel in panels]
    partial, lifted = finish_steps(
        [ended[step] for step in range(step_count - 1)],
        chosen.reshape(step_count * rows_mine, rank_size),
        jnp.broadcast_to(my_slot, (step_count, rows_mine)).reshape(step_count * rows_mine, 1),
        panel_slots,
        panels,
    )
    return finish_last(partial, lifted, ended[step_count - 1])


def solution(mesh):
    return jax.shard_map(
        per_device,
        mesh=mesh,
        in_specs=(
            P(None, ("groups", "rep", "sub"), "tp"),
            P("tp", ("rep", "sub")),
            P(("rep", "sub"), "tp", None),
            P("tp", None, ("rep", "sub")),
            P("groups", None),
            P(),
        ),
        out_specs=P(None, ("groups", "tp"), ("rep", "sub")),
        check_vma=False,
    )
```

time: 151 us -> 207 us (1.37)
  Pallas kernels: 71 us -> 111 us
  waiting for transfers between devices: 28.2 us -> 56.5 us
  starting transfers between devices: 30.8 us -> 19.6 us
  local copies, waits for them, and re-layouts: 10.1 us -> 5.49 us
  other arithmetic: 9.74 us -> 13.5 us
    pallas_call x6, Pallas kernels: 70.1 us -> 110 us  [the longest x5 107 us: call_matmul(): pl.pallas_call(body, in_specs=[pl.BlockSpec(memory_space=pltpu.SMEM)] + [...]
    ppermute x8, waiting for transfers between devices: 15.4 us -> 31.5 us  [swap_tensor(): return lax.ppermute(value, 'tp', [(i, i ^ bit) for i in range(n_tensor)])]
    ppermute x5, waiting for transfers between devices: 5.79 us -> 16.4 us  [to_group(): lax.ppermute(value, 'tp', [(i, (i + moved) % n_tensor) for i in range(n_t...]
    ppermute x5, starting transfers between devices: 10.2 us -> 2.95 us  [to_group(): lax.ppermute(value, 'tp', [(i, (i + moved) % n_tensor) for i in range(n_t...]
    ppermute x4, waiting for transfers between devices: 3.35 us -> 7.02 us  [from_rep(): lax.ppermute(value, 'rep', [((i + shift) % n_rep, i) for i in range(n_rep)])]
    select_n x4, other arithmetic: 1.23 us -> 4.81 us  [pick(): value = jnp.where(index == at, values[at], value)]
    concatenate x2 -> x0, other arithmetic: 2.99 us -> none  [per_device(): panels = jnp.concatenate([panels, swap_tensor(panels, bit)], axis=0)]
    convert_element_type x4 -> x5, other arithmetic: 2.7 us -> 5.68 us  [the longest x4 5.6 us: gap(): pick(values, (group_index + hop - rep_index) % n_rep).astype(jnp.bfloat16)]
  transfers between devices with their start and end apart: 25 -> 25, of which waited for: 13 -> 11; matrix products, arithmetic and copies ran while one was open for 9% -> 7% of each run, Pallas kernels for 47% -> 53%
where the time goes in v6:
time: 207 us; the launch traced here: 206 us
  Pallas kernels  111 us (54%)
  waiting for transfers between devices  56.5 us (27%)
  starting transfers between devices  19.6 us (9%)
  other arithmetic  13.5 us (7%)
  local copies, waits for them, and re-layouts  5.49 us (3%)
    pallas_call x5, Pallas kernels, call_matmul(): pl.pallas_call(body, in_specs=[pl.BlockSpec(memory_space=pltpu.SMEM)] + [...  107 us
    ppermute x8, waiting for transfers between devices, swap_tensor(): return lax.ppermute(value, 'tp', [(i, i ^ bit) for i in range(n_tensor)])  31.5 us
    ppermute x5, waiting for transfers between devices, to_group(): lax.ppermute(value, 'tp', [(i, (i + moved) % n_tensor) for i in range(n_t...  16.4 us
    ppermute x8, starting transfers between devices, swap_tensor(): return lax.ppermute(value, 'tp', [(i, i ^ bit) for i in range(n_tensor)])  8.69 us
    ppermute x4, waiting for transfers between devices, from_rep(): lax.ppermute(value, 'rep', [((i + shift) % n_rep, i) for i in range(n_rep)])  7.02 us
    convert_element_type x4, other arithmetic, gap(): pick(values, (group_index + hop - rep_index) % n_rep).astype(jnp.bfloat16)  5.6 us
    ppermute x4, starting transfers between devices, from_rep(): lax.ppermute(value, 'rep', [((i + shift) % n_rep, i) for i in range(n_rep)])  5.21 us
    select_n x4, other arithmetic, pick(): value = jnp.where(index == at, values[at], value)  4.81 us
  transfers between devices with their start and end apart: 25, of which 11 were waited for; matrix products, arithmetic and copies ran while one was open for 7% of the time, Pallas kernels for 53%

profile of v6, /device:TPU:0, one launch (start us, length us, event | category | flops | bytes accessed | tf_op | source)
XLA Modules:
  0.0 206.2 jit_solution(14118847432259764000)
XLA Ops:
  0.5 2.2 %slice.68 = bf16[1,64,7168]{2,1,0:T(8,128)(2,1)} slice(bf16[4,64,7168]{2,1,0:T(8,128)(2,1)} %refs_0_.1), slice={[0:1], [0:64], [0:7168]} | slice | bytes 1835008 | tf_op jit(solution)/shard_map/slice | solution.py:296
  2.7 2.6 %collective-permute-start = (bf16[1,64,7168]{2,1,0:T(8,128)(2,1)}, bf16[1,64,7168]{2,1,0:T(8,128)(2,1)}, u32[]{:S(2)}, u32[]{:S(2)}) collective-permute-start(bf16[1,64,7168]{2,1,0:T(8,128)(2,1)} %slice.68), channel_id=1, source_target_pairs={{2,0},{0,2},{3,1},{1,3},{6,4},{4,6},{7,5},{5,7},{10,8},{8,10},{11,... | collective-permute-start | bytes 2752520 | tf_op jit(solution)/shard_map/ppermute | solution.py:276
  5.3 2.6 %collective-permute-start.2 = (bf16[1,64,2048]{2,1,0:T(8,128)(2,1)S(1)}, bf16[1,64,2048]{2,1,0:T(8,128)(2,1)}, u32[]{:S(2)}, u32[]{:S(2)}) collective-permute-start(bf16[1,64,2048]{2,1,0:T(8,128)(2,1)S(1)} %copy-done.9), channel_id=1, source_target_pairs={{0,8},{4,12},{8,0},{12,4},{1,9},{5,13},{9,1},{13,5},{2,10},{6,14},... | collective-permute-start | bytes 786440 | tf_op jit(solution)/shard_map/ppermute | solution.py:279
  7.9 56.8 %own_products.1 = (f32[256,2176]{1,0:T(8,128)S(1)}, bf16[1,64,7168]{2,1,0:T(8,128)(2,1)S(1)}, bf16[1,64,7168]{2,1,0:T(8,128)(2,1)}, bf16[1,64,7168]{2,1,0:T(8,128)(2,1)}) custom-call(s32[1]{0:T(128)} %bitcast.1.pos_ref, bf16[4,64,7168]{2,1,0:T(8,128)(2,1)} %refs_0_.1, bf16[7168,2048]{1,0:T(8,128)(2,1)} %refs_2_.3, bf16[1,64,7168]{2,1,0:T(8,128)(2,1)S(1)} %bitcast.25), custom_call_target="tpu_custom_call" | custom-call | tf_op jit(solution)/shard_map/own_products/pallas_call | solution.py:120
  65.3 1.6 collective-permute-start.5
  67.4 13.1 %pair_products.4 = (bf16[192,2176]{1,0:T(8,128)(2,1)}, f32[192,2176]{1,0:T(8,128)S(1)}) custom-call(s32[1]{0:T(128)} %bitcast.1.pos_ref, bf16[4,64,7168]{2,1,0:T(8,128)(2,1)} %collective-permute-done.1.refs_0_, bf16[1,64,7168]{2,1,0:T(8,128)(2,1)} %collective-permute-done.refs_1_, bf16[1,64,7168]{2,1,0:T(8,128)(2,1)S(1)} %collective-permute-done.3.refs_2_, ...), custom_call_target="tpu_custom_call" | custom-call | tf_op jit(solution)/shard_map/pair_products/pallas_call | solution.py:120
  80.5 1.2 copy-done.5
  81.7 5.9 %collective-permute-done.4.refs_1_ = bf16[1,64,7168]{2,1,0:T(8,128)(2,1)} collective-permute-done((bf16[1,64,7168]{2,1,0:T(8,128)(2,1)S(1)}, bf16[1,64,7168]{2,1,0:T(8,128)(2,1)}, u32[]{:S(2)}, u32[]{:S(2)}) %collective-permute-start.4) | collective-permute-done | bytes 917536 | tf_op jit(solution)/shard_map/ppermute | solution.py:276
  89.0 1.6 collective-permute-start.8
  91.1 1.5 collective-permute-start.12
  92.6 15.6 %pair_products.5 = (bf16[192,2176]{1,0:T(8,128)(2,1)}, f32[192,2176]{1,0:T(8,128)S(1)}) custom-call(s32[1]{0:T(128)} %bitcast.1.pos_ref, bf16[4,64,7168]{2,1,0:T(8,128)(2,1)} %collective-permute-done.1.refs_0_, bf16[1,64,7168]{2,1,0:T(8,128)(2,1)} %collective-permute-done.4.refs_1_, bf16[1,64,7168]{2,1,0:T(8,128)(2,1)} %collective-permute-done.7.refs_2_, ...), custom_call_target="tpu_custom_call" | custom-call | tf_op jit(solution)/shard_map/pair_products/pallas_call | solution.py:120
  108.3 2.1 collective-permute-done.8
  110.4 1.3 convert_add_fusion.1
  115.1 1.3 slice_select_fusion.2.refs_4_
  116.8 11.5 %pair_products.6 = (bf16[64,2176]{1,0:T(8,128)(2,1)}, f32[64,2176]{1,0:T(8,128)S(1)}) custom-call(s32[1]{0:T(128)} %bitcast.1.pos_ref, bf16[1,64,7168]{2,1,0:T(8,128)(2,1)} %collective-permute-done.9.refs_0_, bf16[1,64,7168]{2,1,0:T(8,128)(2,1)S(1)} %collective-permute-done.10.refs_1_, bf16[7168,2048]{1,0:T(8,128)(2,1)} %refs_2_.3, ...), custom_call_target="tpu_custom_call" | custom-call | tf_op jit(solution)/shard_map/pair_products/pallas_call | solution.py:120
  128.3 13.1 %collective-permute-done.11 = bf16[192,2176]{1,0:T(8,128)(2,1)} collective-permute-done((bf16[192,2176]{1,0:T(8,128)(2,1)}, bf16[192,2176]{1,0:T(8,128)(2,1)}, u32[]{:S(2)}, u32[]{:S(2)}) %collective-permute-start.11) | collective-permute-done | bytes 835616 | tf_op jit(solution)/shard_map/ppermute | solution.py:279
  141.4 1.3 convert_add_fusion
  142.8 2.3 %select_convert_fusion.1 = bf16[64,2176]{1,0:T(8,128)(2,1)} fusion(f32[192,2176]{1,0:T(8,128)} %copy-done.14, f32[192,2176]{1,0:T(8,128)S(1)} %convert_add_fusion, pred[]{:T(512)S(6)} %eq.52), kind=kLoop, calls=%fused_computation.4 | loop fusion | flops 139264 | bytes 835585 | tf_op jit(solution)/shard_map/convert_element_type | solution.py:352
  146.2 9.8 %collective-permute-done.14 = bf16[64,2176]{1,0:T(8,128)(2,1)S(1)} collective-permute-done((bf16[64,2176]{1,0:T(8,128)(2,1)}, bf16[64,2176]{1,0:T(8,128)(2,1)S(1)}, u32[]{:S(2)}, u32[]{:S(2)}) %collective-permute-start.14) | collective-permute-done | bytes 278560 | tf_op jit(solution)/shard_map/ppermute | solution.py:279
  156.0 1.3 select_convert_fusion
  157.7 1.6 slice_select_fusion
  159.3 10.5 %pair_products.7 = (bf16[64,2048]{1,0:T(8,128)(2,1)S(1)}, f32[64,2048]{1,0:T(8,128)S(1)}, f32[64,128]{1,0:T(8,128)S(1)}, f32[64,128]{1,0:T(8,128)S(1)}) custom-call(s32[1]{0:T(128)} %bitcast.1.pos_ref, bf16[1,64,7168]{2,1,0:T(8,128)(2,1)} %collective-permute-done.12.refs_0_, bf16[1,64,7168]{2,1,0:T(8,128)(2,1)S(1)} %collective-permute-done.15.refs_1_, ...), custom_call_target="tpu_custom_call" | custom-call | tf_op jit(solution)/shard_map/pair_products/pallas_call | solution.py:120
  169.9 3.6 %collective-permute-done.17.refs_9_ = bf16[64,2176]{1,0:T(8,128)(2,1)S(1)} collective-permute-done((bf16[64,2176]{1,0:T(8,128)(2,1)S(1)}, bf16[64,2176]{1,0:T(8,128)(2,1)S(1)}, u32[]{:S(2)}, u32[]{:S(2)}) %collective-permute-start.17) | collective-permute-done | bytes 278560 | tf_op jit(solution)/shard_map/ppermute | solution.py:283
  173.5 2.0 collective-permute-start.19
  175.6 6.5 %collective-permute-done.19 = f32[64,128]{1,0:T(8,128)S(1)} collective-permute-done((f32[64,128]{1,0:T(8,128)S(1)}, f32[64,128]{1,0:T(8,128)S(1)}, u32[]{:S(2)}, u32[]{:S(2)}) %collective-permute-start.19) | collective-permute-done | bytes 32800 | tf_op jit(solution)/shard_map/ppermute | solution.py:279
  183.6 4.1 %collective-permute-done.20 = f32[64,128]{1,0:T(8,128)S(1)} collective-permute-done((f32[64,128]{1,0:T(8,128)S(1)}, f32[64,128]{1,0:T(8,128)S(1)}, u32[]{:S(2)}, u32[]{:S(2)}) %collective-permute-start.20) | collective-permute-done | bytes 32800 | tf_op jit(solution)/shard_map/ppermute | solution.py:283
  187.8 1.2 select_convert_fusion.3
  189.8 1.4 collective-permute-start.23
  191.8 1.1 slice_select_fusion.3.refs_0_
  193.0 1.2 collective-permute-done.22
  194.3 2.5 %finish_steps.1 = (bf16[4,64,2048]{2,1,0:T(8,128)(2,1)}, bf16[64,2048]{1,0:T(8,128)(2,1)S(1)}) custom-call(bf16[256,64]{1,0:T(8,128)(2,1)S(1)} %bitcast.30, s32[256,1]{1,0:T(8,128)S(1)} %reshape.121.slot_ref, s32[4]{0:T(128)S(1)} %pad_add_fusion.order_ref, bf16[64,2048]{1,0:T(8,128)(2,1)S(1)} %bitcast.31, bf16[64,2048]{1,0:T(8,128)(2,1)} %bitcast.14.refs_1_, ...), custom_call_target="tpu_custom_call" | custom-call | tf_op jit(solution)/shard_map/finish_steps/pallas_call | solution.py:208
  196.8 8.6 %collective-permute-done.24.refs_1_ = bf16[64,2048]{1,0:T(8,128)(2,1)S(1)} collective-permute-done((bf16[64,2048]{1,0:T(8,128)(2,1)S(1)}, bf16[64,2048]{1,0:T(8,128)(2,1)S(1)}, u32[]{:S(2)}, u32[]{:S(2)}) %collective-permute-start.24) | collective-permute-done | bytes 262176 | tf_op jit(solution)/shard_map/ppermute | solution.py:283
  (91 shorter events, 12.9 us)
Async XLA Ops:
  0.0 114.6 %copy-start = (s32[256,1]{0,1:T(1,128)S(1)}, s32[256,1]{0,1:T(1,128)}, u32[]{:S(2)}) copy-start(s32[256,1]{0,1:T(1,128)} %param.10) | copy-start | bytes 3076
  0.0 7.9 %copy-start.2 = (bf16[1,7168,64]{1,2,0:T(8,128)(2,1)S(1)}, bf16[1,7168,64]{1,2,0:T(8,128)(2,1)}, u32[]{:S(2)}) copy-start(bf16[1,7168,64]{1,2,0:T(8,128)(2,1)} %param.8) | copy-start | bytes 2752516
  0.0 64.7 %collective-permute-start.1 = (bf16[4,64,7168]{2,1,0:T(8,128)(2,1)}, bf16[4,64,7168]{2,1,0:T(8,128)(2,1)}, u32[]{:S(2)}, u32[]{:S(2)}) collective-permute-start(bf16[4,64,7168]{2,1,0:T(8,128)(2,1)} %refs_0_.1), channel_id=1, source_target_pairs={{0,1},{1,0},{2,3},{3,2},{4,5},{5,4},{6,7},{7,6},{8,9},{9,8},{10,11... | collective-permute-start | bytes 11010056 | tf_op jit(solution)/shard_map/ppermute | solution.py:273
  2.7 62.0 %collective-permute-start = (bf16[1,64,7168]{2,1,0:T(8,128)(2,1)}, bf16[1,64,7168]{2,1,0:T(8,128)(2,1)}, u32[]{:S(2)}, u32[]{:S(2)}) collective-permute-start(bf16[1,64,7168]{2,1,0:T(8,128)(2,1)} %slice.68), channel_id=1, source_target_pairs={{2,0},{0,2},{3,1},{1,3},{6,4},{4,6},{7,5},{5,7},{10,8},{8,10},{11,... | collective-permute-start | bytes 2752520 | tf_op jit(solution)/shard_map/ppermute | solution.py:276
  5.3 59.4 %collective-permute-start.2 = (bf16[1,64,2048]{2,1,0:T(8,128)(2,1)S(1)}, bf16[1,64,2048]{2,1,0:T(8,128)(2,1)}, u32[]{:S(2)}, u32[]{:S(2)}) collective-permute-start(bf16[1,64,2048]{2,1,0:T(8,128)(2,1)S(1)} %copy-done.9), channel_id=1, source_target_pairs={{0,8},{4,12},{8,0},{12,4},{1,9},{5,13},{9,1},{13,5},{2,10},{6,14},... | collective-permute-start | bytes 786440 | tf_op jit(solution)/shard_map/ppermute | solution.py:279
  64.7 2.7 %collective-permute-start.3 = (bf16[1,64,7168]{2,1,0:T(8,128)(2,1)}, bf16[1,64,7168]{2,1,0:T(8,128)(2,1)S(1)}, u32[]{:S(2)}, u32[]{:S(2)}) collective-permute-start(bf16[1,64,7168]{2,1,0:T(8,128)(2,1)} %collective-permute-done.refs_1_), channel_id=1, source_target_pairs={{0,1},{1,0},{2,3},{3,2},{4,5},{5,4},{6,7},{7,6},{8,9},{9,8},{10,11... | collective-permute-start | bytes 2752520 | tf_op jit(solution)/shard_map/ppermute | solution.py:273
  64.7 22.9 %collective-permute-start.4 = (bf16[1,64,7168]{2,1,0:T(8,128)(2,1)S(1)}, bf16[1,64,7168]{2,1,0:T(8,128)(2,1)}, u32[]{:S(2)}, u32[]{:S(2)}) collective-permute-start(bf16[1,64,7168]{2,1,0:T(8,128)(2,1)S(1)} %get-tuple-element.71), channel_id=1, source_target_pairs={{2,0},{0,2},{3,1},{1,3},{6,4},{4,6},{7,5},{5,7},{10,8},{8,10},{11,... | collective-permute-start | bytes 2752520 | tf_op jit(solution)/shard_map/ppermute | solution.py:276
  65.3 22.3 %collective-permute-start.5 = (bf16[1,64,2048]{2,1,0:T(8,128)(2,1)S(1)}, bf16[1,64,2048]{2,1,0:T(8,128)(2,1)S(1)}, u32[]{:S(2)}, u32[]{:S(2)}) collective-permute-start(bf16[1,64,2048]{2,1,0:T(8,128)(2,1)S(1)} %copy-done.9), channel_id=1, source_target_pairs={{0,4},{4,0},{8,12},{12,8},{1,5},{5,1},{9,13},{13,9},{2,6},{6,2},{1... | collective-permute-start | bytes 786440 | tf_op jit(solution)/shard_map/ppermute | solution.py:279
  66.9 21.4 %collective-permute-start.6 = (bf16[1,64,2048]{2,1,0:T(8,128)(2,1)}, bf16[1,64,2048]{2,1,0:T(8,128)(2,1)S(1)}, u32[]{:S(2)}, u32[]{:S(2)}) collective-permute-start(bf16[1,64,2048]{2,1,0:T(8,128)(2,1)} %collective-permute-done.2), channel_id=1, source_target_pairs={{0,4},{4,0},{8,12},{12,8},{1,5},{5,1},{9,13},{13,9},{2,6},{6,2},{1... | collective-permute-start | bytes 786440 | tf_op jit(solution)/shard_map/ppermute | solution.py:279
  89.0 3.6 %collective-permute-start.7 = (bf16[1,64,7168]{2,1,0:T(8,128)(2,1)}, bf16[1,64,7168]{2,1,0:T(8,128)(2,1)}, u32[]{:S(2)}, u32[]{:S(2)}) collective-permute-start(bf16[1,64,7168]{2,1,0:T(8,128)(2,1)} %collective-permute-done.4.refs_1_), channel_id=1, source_target_pairs={{0,1},{1,0},{2,3},{3,2},{4,5},{5,4},{6,7},{7,6},{8,9},{9,8},{10,11... | collective-permute-start | bytes 2752520 | tf_op jit(solution)/shard_map/ppermute | solution.py:273
  89.0 21.3 %collective-permute-start.8 = (bf16[192,2176]{1,0:T(8,128)(2,1)}, bf16[192,2176]{1,0:T(8,128)(2,1)}, u32[]{:S(2)}, u32[]{:S(2)}) collective-permute-start(bf16[192,2176]{1,0:T(8,128)(2,1)} %get-tuple-element.79), channel_id=1, source_target_pairs={{0,4},{4,0},{8,12},{12,8},{1,5},{5,1},{9,13},{13,9},{2,6},{6,2},{1... | collective-permute-start | bytes 2506760 | tf_op jit(solution)/shard_map/ppermute | solution.py:279
  90.6 23.5 %collective-permute-start.9 = (bf16[1,64,7168]{2,1,0:T(8,128)(2,1)}, bf16[1,64,7168]{2,1,0:T(8,128)(2,1)}, u32[]{:S(2)}, u32[]{:S(2)}) collective-permute-start(bf16[1,64,7168]{2,1,0:T(8,128)(2,1)} %get-tuple-element.80), channel_id=1, source_target_pairs={{2,0},{0,2},{3,1},{1,3},{6,4},{4,6},{7,5},{5,7},{10,8},{8,10},{11,... | collective-permute-start | bytes 2752520 | tf_op jit(solution)/shard_map/ppermute | solution.py:276
  91.1 53.9 %collective-permute-start.12 = (bf16[1,64,7168]{2,1,0:T(8,128)(2,1)}, bf16[1,64,7168]{2,1,0:T(8,128)(2,1)}, u32[]{:S(2)}, u32[]{:S(2)}) collective-permute-start(bf16[1,64,7168]{2,1,0:T(8,128)(2,1)} %get-tuple-element.92), channel_id=1, source_target_pairs={{2,0},{0,2},{3,1},{1,3},{6,4},{4,6},{7,5},{5,7},{10,8},{8,10},{11,... | collective-permute-start | bytes 2752520 | tf_op jit(solution)/shard_map/ppermute | solution.py:276
  92.6 17.7 %copy-start.6 = (f32[192,2176]{1,0:T(8,128)S(1)}, f32[192,2176]{1,0:T(8,128)}, u32[]{:S(2)}) copy-start(f32[192,2176]{1,0:T(8,128)} %copy-done.5) | copy-start | bytes 5013508
  114.1 2.7 %collective-permute-start.10 = (bf16[1,64,7168]{2,1,0:T(8,128)(2,1)}, bf16[1,64,7168]{2,1,0:T(8,128)(2,1)S(1)}, u32[]{:S(2)}, u32[]{:S(2)}) collective-permute-start(bf16[1,64,7168]{2,1,0:T(8,128)(2,1)} %collective-permute-done.9.refs_0_), channel_id=1, source_target_pairs={{0,1},{1,0},{2,3},{3,2},{4,5},{5,4},{6,7},{7,6},{8,9},{9,8},{10,11... | collective-permute-start | bytes 2752520 | tf_op jit(solution)/shard_map/ppermute | solution.py:273
  114.1 27.3 %collective-permute-start.11 = (bf16[192,2176]{1,0:T(8,128)(2,1)}, bf16[192,2176]{1,0:T(8,128)(2,1)}, u32[]{:S(2)}, u32[]{:S(2)}) collective-permute-start(bf16[192,2176]{1,0:T(8,128)(2,1)} %get-tuple-element.91), channel_id=1, source_target_pairs={{0,4},{4,0},{8,12},{12,8},{1,5},{5,1},{9,13},{13,9},{2,6},{6,2},{1... | collective-permute-start | bytes 2506760 | tf_op jit(solution)/shard_map/ppermute | solution.py:279
  114.8 30.3 %collective-permute-start.13 = (bf16[64,2176]{1,0:T(8,128)(2,1)}, bf16[64,2176]{1,0:T(8,128)(2,1)S(1)}, u32[]{:S(2)}, u32[]{:S(2)}) collective-permute-start(bf16[64,2176]{1,0:T(8,128)(2,1)} %select_convert_fusion.2), channel_id=1, source_target_pairs={{0,8},{4,12},{8,0},{12,4},{1,9},{5,13},{9,1},{13,5},{2,10},{6,14},... | collective-permute-start | bytes 835592 | tf_op jit(solution)/shard_map/ppermute | solution.py:283
  116.4 29.9 %copy-start.3 = (f32[64,2176]{1,0:T(8,128)}, f32[64,2176]{1,0:T(8,128)S(1)}, u32[]{:S(2)}) copy-start(f32[64,2176]{1,0:T(8,128)S(1)} %slice_select_fusion.2.refs_4_) | copy-start | bytes 1671172
  116.4 25.0 %copy-start.8 = (f32[192,2176]{1,0:T(8,128)S(1)}, f32[192,2176]{1,0:T(8,128)}, u32[]{:S(2)}) copy-start(f32[192,2176]{1,0:T(8,128)} %copy-done.7) | copy-start | bytes 5013508
  145.0 11.0 %collective-permute-start.14 = (bf16[64,2176]{1,0:T(8,128)(2,1)}, bf16[64,2176]{1,0:T(8,128)(2,1)S(1)}, u32[]{:S(2)}, u32[]{:S(2)}) collective-permute-start(bf16[64,2176]{1,0:T(8,128)(2,1)} %get-tuple-element.99), channel_id=1, source_target_pairs={{0,4},{4,0},{8,12},{12,8},{1,5},{5,1},{9,13},{13,9},{2,6},{6,2},{1... | collective-permute-start | bytes 835592 | tf_op jit(solution)/shard_map/ppermute | solution.py:279
  145.3 12.0 %collective-permute-start.15 = (bf16[1,64,7168]{2,1,0:T(8,128)(2,1)}, bf16[1,64,7168]{2,1,0:T(8,128)(2,1)S(1)}, u32[]{:S(2)}, u32[]{:S(2)}) collective-permute-start(bf16[1,64,7168]{2,1,0:T(8,128)(2,1)} %collective-permute-done.12.refs_0_), channel_id=1, source_target_pairs={{0,1},{1,0},{2,3},{3,2},{4,5},{5,4},{6,7},{7,6},{8,9},{9,8},{10,11... | collective-permute-start | bytes 2752520 | tf_op jit(solution)/shard_map/ppermute | solution.py:273
  145.4 24.5 %collective-permute-start.16 = (bf16[64,2176]{1,0:T(8,128)(2,1)}, bf16[64,2176]{1,0:T(8,128)(2,1)S(1)}, u32[]{:S(2)}, u32[]{:S(2)}) collective-permute-start(bf16[64,2176]{1,0:T(8,128)(2,1)} %select_convert_fusion.1), channel_id=1, source_target_pairs={{0,8},{4,12},{8,0},{12,4},{1,9},{5,13},{9,1},{13,5},{2,10},{6,14},... | collective-permute-start | bytes 835592 | tf_op jit(solution)/shard_map/ppermute | solution.py:283
  157.3 16.2 %collective-permute-start.17 = (bf16[64,2176]{1,0:T(8,128)(2,1)S(1)}, bf16[64,2176]{1,0:T(8,128)(2,1)S(1)}, u32[]{:S(2)}, u32[]{:S(2)}) collective-permute-start(bf16[64,2176]{1,0:T(8,128)(2,1)S(1)} %select_convert_fusion), channel_id=1, source_target_pairs={{0,8},{4,12},{8,0},{12,4},{1,9},{5,13},{9,1},{13,5},{2,10},{6,14},... | collective-permute-start | bytes 835592 | tf_op jit(solution)/shard_map/ppermute | solution.py:283
  159.3 16.2 %slice-start = ((f32[64,2176]{1,0:T(8,128)}), f32[64,128]{1,0:T(8,128)S(1)}, s32[]{:S(2)}) async-start(f32[64,2176]{1,0:T(8,128)} %copy-done.3), calls=%async_computation | async-start | bytes 65536 | tf_op jit(solution)/shard_map/slice | solution.py:402
  173.5 14.3 %collective-permute-start.18 = (bf16[64,2048]{1,0:T(8,128)(2,1)S(1)}, bf16[64,2048]{1,0:T(8,128)(2,1)S(1)}, u32[]{:S(2)}, u32[]{:S(2)}) collective-permute-start(bf16[64,2048]{1,0:T(8,128)(2,1)S(1)} %get-tuple-element.112), channel_id=1, source_target_pairs={{0,4},{4,0},{8,12},{12,8},{1,5},{5,1},{9,13},{13,9},{2,6},{6,2},{1... | collective-permute-start | bytes 786440 | tf_op jit(solution)/shard_map/ppermute | solution.py:279
  173.5 8.5 %collective-permute-start.19 = (f32[64,128]{1,0:T(8,128)S(1)}, f32[64,128]{1,0:T(8,128)S(1)}, u32[]{:S(2)}, u32[]{:S(2)}) collective-permute-start(f32[64,128]{1,0:T(8,128)S(1)} %get-tuple-element.120), channel_id=1, source_target_pairs={{0,4},{4,0},{8,12},{12,8},{1,5},{5,1},{9,13},{13,9},{2,6},{6,2},{1... | collective-permute-start | bytes 98312 | tf_op jit(solution)/shard_map/ppermute | solution.py:279
  182.8 4.9 %collective-permute-start.20 = (f32[64,128]{1,0:T(8,128)S(1)}, f32[64,128]{1,0:T(8,128)S(1)}, u32[]{:S(2)}, u32[]{:S(2)}) collective-permute-start(f32[64,128]{1,0:T(8,128)S(1)} %get-tuple-element.129), channel_id=1, source_target_pairs={{0,8},{4,12},{8,0},{12,4},{1,9},{5,13},{9,1},{13,5},{2,10},{6,14},... | collective-permute-start | bytes 98312 | tf_op jit(solution)/shard_map/ppermute | solution.py:283
  189.1 3.9 %collective-permute-start.21 = (bf16[4,64,64]{2,1,0:T(8,128)(2,1)S(1)}, bf16[4,64,64]{2,1,0:T(8,128)(2,1)S(1)}, u32[]{:S(2)}, u32[]{:S(2)}) collective-permute-start(bf16[4,64,64]{2,1,0:T(8,128)(2,1)S(1)} %select_bitcast_fusion), channel_id=1, source_target_pairs={{0,1},{1,2},{2,3},{3,0},{4,5},{5,6},{6,7},{7,4},{8,9},{9,10},{10,1... | collective-permute-start | bytes 98312 | tf_op jit(solution)/shard_map/ppermute | solution.py:416
  189.2 5.0 %collective-permute-start.22 = (bf16[4,64,64]{2,1,0:T(8,128)(2,1)S(1)}, bf16[4,64,64]{2,1,0:T(8,128)(2,1)S(1)}, u32[]{:S(2)}, u32[]{:S(2)}) collective-permute-start(bf16[4,64,64]{2,1,0:T(8,128)(2,1)S(1)} %select_bitcast_fusion), channel_id=1, source_target_pairs={{0,2},{1,3},{2,0},{3,1},{4,6},{5,7},{6,4},{7,5},{8,10},{9,11},{10,... | collective-permute-start | bytes 98312 | tf_op jit(solution)/shard_map/ppermute | solution.py:416
  189.8 4.4 %collective-permute-start.23 = (bf16[4,64,64]{2,1,0:T(8,128)(2,1)S(1)}, bf16[4,64,64]{2,1,0:T(8,128)(2,1)S(1)}, u32[]{:S(2)}, u32[]{:S(2)}) collective-permute-start(bf16[4,64,64]{2,1,0:T(8,128)(2,1)S(1)} %select_bitcast_fusion), channel_id=1, source_target_pairs={{0,3},{1,0},{2,1},{3,2},{4,7},{5,4},{6,5},{7,6},{8,11},{9,8},{10,9... | collective-permute-start | bytes 98312 | tf_op jit(solution)/shard_map/ppermute | solution.py:416
  191.2 14.2 %collective-permute-start.24 = (bf16[64,2048]{1,0:T(8,128)(2,1)S(1)}, bf16[64,2048]{1,0:T(8,128)(2,1)S(1)}, u32[]{:S(2)}, u32[]{:S(2)}) collective-permute-start(bf16[64,2048]{1,0:T(8,128)(2,1)S(1)} %select_convert_fusion.3), channel_id=1, source_target_pairs={{0,8},{4,12},{8,0},{12,4},{1,9},{5,13},{9,1},{13,5},{2,10},{6,14},... | collective-permute-start | bytes 786440 | tf_op jit(solution)/shard_map/ppermute | solution.py:283
  194.3 11.9 %copy-start.1 = (s32[256,1]{0,1:T(1,128)S(1)}, s32[256,1]{0,1:T(1,128)}, u32[]{:S(2)}) copy-start(s32[256,1]{0,1:T(1,128)} %param.10) | copy-start | bytes 3076
  (12 other events, 42.0 us)

commit v7 on v5

--- a/solution.py
+++ b/solution.py
@@ -24,10 +24,15 @@
     return depth
 
 
-def matmul_body(spans, pos_ref, *refs):
+def rank_columns(factors):
+    slots, rank, _ = factors.shape
+    return -(-slots * rank // 128) * 128
+
+
+def matmul_body(spans, emitted, apart, pos_ref, *refs):
     sources = refs[:2 * len(spans)]
     w_ref, a_ref, send_ref, keep_ref = refs[2 * len(spans):2 * len(spans) + 4]
-    rank_refs = refs[2 * len(spans) + 4:-5]
+    outs = refs[2 * len(spans) + 4:-5]
     x_ref, w_buf, total_ref, x_sems, w_sems = refs[-5:]
     rows = send_ref.shape[0]
     depth, width = w_ref.shape
@@ -56,17 +61,24 @@
         fetch(block, block).start()
     keep_ref[...] = jnp.zeros_like(keep_ref)
     total_ref[...] = jnp.zeros_like(total_ref)
-    for rank_ref in rank_refs:
-        rank_ref[...] = jnp.zeros_like(rank_ref)
+    send_rank, keep_rank = outs[:2] if apart else (total_ref, keep_ref)
+    if apart:
+        send_rank[...] = jnp.zeros_like(send_rank)
+        keep_rank[...] = jnp.zeros_like(keep_rank)
     for copy in copies:
         copy.wait()
-    send_rank, keep_rank = rank_refs or (total_ref, keep_ref)
+    emit = None
+    if emitted is not None:
+        emit = pltpu.make_async_copy(
+            x_ref.at[own_at, pl.ds(emitted, 1)], outs[-1], x_sems.at[2 * len(spans)]
+        )
+        emit.start()
     for slot in range(slots):
         x = x_ref[...].reshape(2 * rows, depth)
         part = lax.dot_general(
             x, a_ref[slot], (((1,), (1,)), ((), ())), preferred_element_type=jnp.float32
         )
-        begin = slot * rank + (0 if rank_refs else width)
+        begin = slot * rank + (0 if apart else width)
         send_rank[:, begin:begin + rank] = part[:rows]
         keep_rank[:, begin:begin + rank] = part[rows:]
 
@@ -87,39 +99,40 @@
             fetch(block + buffers, slot).start()
 
     send_ref[...] = total_ref[...].astype(send_ref.dtype)
-
-
-def rank_columns(factors):
-    slots, rank, _ = factors.shape
-    return -(-slots * rank // 128) * 128
-
-
-def partial_products(pos, chunks, weight, factors, apart):
+    if emit is not None:
+        emit.wait()
+
+
+def partial_products(pos, chunks, weight, factors, apart=False, emitted=None):
     _, per_block, depth = chunks[0][0].shape
     width = weight.shape[1]
     spans = tuple((first, steps) for _, _, first, steps in chunks)
     steps = sum(length for _, length in spans)
     rows = steps * per_block
     block_k = block_depth(depth, width, rows)
-    buffers = min(BUFFERS, depth // block_k)
+    buffers = min(BUFFERS if rows >= WIDE_ROWS else 2 * BUFFERS, depth // block_k)
     any_spec = pl.BlockSpec(memory_space=pl.ANY)
     vmem_spec = pl.BlockSpec(memory_space=pltpu.VMEM)
     extra = rank_columns(factors)
     columns = width + (0 if apart else extra)
-    ranks = [jax.ShapeDtypeStruct((rows, extra), jnp.float32)] * (2 if apart else 0)
+    out_shape = [
+        jax.ShapeDtypeStruct((rows, columns), jnp.bfloat16),
+        jax.ShapeDtypeStruct((rows, columns), jnp.float32),
+    ] + [jax.ShapeDtypeStruct((rows, extra), jnp.float32)] * (2 if apart else 0)
+    out_specs = [vmem_spec] * len(out_shape)
+    if emitted is not None:
+        out_shape.append(jax.ShapeDtypeStruct((1, per_block, depth), jnp.bfloat16))
+        out_specs.append(any_spec)
     return pl.pallas_call(
-        functools.partial(matmul_body, spans),
+        functools.partial(matmul_body, spans, emitted, apart),
         in_specs=[pl.BlockSpec(memory_space=pltpu.SMEM)] + [any_spec] * (2 * len(chunks) + 1) + [vmem_spec],
-        out_specs=[vmem_spec] * (2 + len(ranks)),
-        out_shape=[
-            jax.ShapeDtypeStruct((rows, columns), jnp.bfloat16),
-            jax.ShapeDtypeStruct((rows, columns), jnp.float32),
-        ] + ranks,
+        out_specs=out_specs,
+        out_shape=out_shape,
         scratch_shapes=[
             pltpu.VMEM((2, steps, per_block, depth), jnp.bfloat16),
             pltpu.VMEM((buffers, block_k, width), jnp.bfloat16),
             pltpu.VMEM((rows, columns), jnp.float32),
-            pltpu.SemaphoreType.DMA((2 * len(chunks),)),
+            pltpu.SemaphoreType.DMA((2 * len(chunks) + 1,)),
             pltpu.SemaphoreType.DMA((buffers,)),
         ],
         compiler_params=pltpu.CompilerParams(vmem_limit_bytes=VMEM_BYTES),
@@ -128,7 +141,9 @@
     )(pos, *[source for own, sib, _, _ in chunks for source in (own, sib)], weight, factors)
 
 
-def finish_body(received, chosen_ref, slot_ref, order_ref, panel_ref, *refs):
+def finish_body(received, panels, chosen_ref, slot_ref, order_ref, *refs):
+    panel_refs, refs = refs[:panels], refs[panels:]
+    per_panel = panel_refs[0].shape[0]
     out_ref, lifted_ref, done_ref, sem = refs[-4:]
     steps, rows, width = done_ref.shape
     rank = chosen_ref.shape[1]
@@ -137,14 +152,15 @@
     spread = jnp.concatenate(
         [
             jnp.where(slot == order_ref[place], chosen, jnp.zeros_like(chosen))
-            for place in range(panel_ref.shape[0] // rank)
+            for place in range(panels * per_panel // rank)
         ],
         axis=1,
     )
     block_n = min(BLOCK_N, width)
     for place in range(width // block_n):
         columns = slice(place * block_n, (place + 1) * block_n)
-        lifted = jnp.dot(spread, panel_ref[:, columns], preferred_element_type=jnp.float32).astype(jnp.bfloat16)
+        panel = jnp.concatenate([panel_ref[:, columns] for panel_ref in panel_refs], axis=0)
+        lifted = jnp.dot(spread, panel, preferred_element_type=jnp.float32).astype(jnp.bfloat16)
         for step in range(steps):
             total = refs[step * (received + 1)][:, columns]
             for value_ref in refs[step * (received + 1) + 1:(step + 1) * (received + 1)]:
@@ -158,13 +174,13 @@
 
 
 def finish_steps(totals, chosen, slots, order, panels):
-    steps, width = len(totals), panels.shape[1]
+    steps, width = len(totals), panels[0].shape[1]
     rows = chosen.shape[0] // (steps + 1)
     vmem_spec = pl.BlockSpec(memory_space=pltpu.VMEM)
     arrays = [value for total in totals for value in total]
     return pl.pallas_call(
-        functools.partial(finish_body, len(totals[0]) - 1),
-        in_specs=[vmem_spec, vmem_spec, pl.BlockSpec(memory_space=pltpu.SMEM)] + [vmem_spec] * (1 + len(arrays)),
+        functools.partial(finish_body, len(totals[0]) - 1, len(panels)),
+        in_specs=[vmem_spec, vmem_spec, pl.BlockSpec(memory_space=pltpu.SMEM)] + [vmem_spec] * (len(panels) + len(arrays)),
         out_specs=[pl.BlockSpec(memory_space=pl.ANY), vmem_spec],
         out_shape=[
             jax.ShapeDtypeStruct((steps + 1, rows, width), jnp.bfloat16),
@@ -174,7 +190,7 @@
         compiler_params=pltpu.CompilerParams(vmem_limit_bytes=VMEM_BYTES),
         cost_estimate=pl.CostEstimate(flops=0, bytes_accessed=0, transcendentals=0),
         name="finish_steps",
-    )(chosen, slots, order, panels, *arrays)
+    )(chosen, slots, order, *panels, *arrays)
 
 
 def last_body(partial_ref, lifted_ref, *refs):
@@ -250,21 +266,16 @@
 
     siblings = swap_cores(hidden)
     pieces = [(step, shift) for step in range(step_count) for shift in range(1, n_rep)]
-    remote = {}
-    for step, shift in pieces:
-        source = hidden if step == 0 else after(hidden, siblings)
-        remote[step, shift] = from_rep(source[step:step + 1], shift)
-
-    panels, order, bit = up_b, [0], n_tensor // 2
-    while bit:
-        panels = jnp.concatenate([panels, swap_tensor(panels, bit)], axis=0)
-        order = order + [at ^ bit for at in order]
-        bit //= 2
-    panels = panels.reshape(slot_count * rank_size, width)
-    panel_slots = jnp.stack([
-        (tensor_index ^ at) * up_b.shape[0] + each for at in order for each in range(up_b.shape[0])
-    ]).astype(jnp.int32)
-
+    remote = {(0, shift): from_rep(hidden[:1], shift) for shift in range(1, n_rep)}
+
+    def spread_panels(panels, order, bits):
+        for bit in bits:
+            panels = panels + [swap_tensor(panel, bit) for panel in panels]
+            order = order + [at ^ bit for at in order]
+        return panels, order
+
+    bits = [n_tensor >> at for at in range(1, n_tensor.bit_length())]
+    panels, order = spread_panels([up_b], [0], bits[:1])
     my_ids = lax.dynamic_slice_in_dim(adapter_ids, tensor_index * rows_mine, rows_mine)
     iota = lax.broadcasted_iota(jnp.int32, (rows_mine, slot_count), 1)
     my_slot = jnp.sum((my_ids == iota).astype(jnp.int32) * owner_map[None, :], axis=1)
@@ -288,7 +299,7 @@
             bit //= 2
         return total.reshape(steps, extent, columns)
 
-    def gap(token, jobs, *extra):
+    def gap(token, jobs, *extra, short=False):
         nonlocal first_leg, second_leg
         for parts, received, keep, kind in first_leg:
             steps = sum(length for _, length in parts)
@@ -296,32 +307,31 @@
             for key, length in parts:
                 for at in range(begin, begin + length):
                     halved[key[0] + at - begin, key[1]] = total[at]
-                    if key == (step_count - 1, 0):
+                    if (key[0] + at - begin, key[1]) == (step_count - 1, 0):
                         halved[RANK_NAME, 0] = total[at][:, width:]
                 begin += length
-        closed = {}
-        for name, kept, received in second_leg:
-            closed[name] = (kept, *received)
+        closed, waiting = {}, second_leg if short else []
+        for name, kept, received in [] if short else second_leg:
+            closed[name] = (after(kept, token), *received)
         started, sends = [], []
         for name in sorted({name for name, _ in halved}):
-            if name in begun or any((name, at) not in halved for at in range(n_rep)):
+            if name in begun or name == RANK_NAME or any((name, at) not in halved for at in range(n_rep)):
                 continue
             begun.add(name)
             values = [halved[name, at] for at in range(n_rep)]
             columns = min(value.shape[1] for value in values)
             values = [value[:, :columns] for value in values]
-            kind = jnp.float32 if name >= RANK_NAME else jnp.bfloat16
             kept = pick(values, (group_index - rep_index) % n_rep)
-            sent = [pick(values, (group_index + hop - rep_index) % n_rep).astype(kind) for hop in range(1, n_rep)]
+            sent = [pick(values, (group_index + hop - rep_index) % n_rep).astype(jnp.bfloat16) for hop in range(1, n_rep)]
             started.append((name, kept))
             sends.append(sent)
         first_sends = [job[1] for job in jobs]
-        first_sends, sends, extra, closed = lax.optimization_barrier((first_sends, sends, extra, closed))
+        first_sends, sends, extra, closed, _ = lax.optimization_barrier((first_sends, sends, extra, closed, token))
         ended.update(closed)
         first_leg = [
             (parts, swap_tensor(send, group // 2), keep, kind) for (parts, _, keep, kind), send in zip(jobs, first_sends)
         ]
-        second_leg = [
+        second_leg = waiting + [
             (name, kept, [to_group(value, hop + 1) for hop, value in enumerate(sent)])
             for (name, kept), sent in zip(started, sends)
         ]
@@ -329,31 +339,41 @@
 
     factors = jnp.swapaxes(down_a, 1, 2)
 
-    def multiply(chunks, apart=False):
-        return partial_products(pos, chunks, base_weight, factors, apart)
-
     half = step_count // 2
-    send, keep = multiply([(hidden, siblings, 0, half)])
-    jobs = [([((0, 0), half)], send, keep, jnp.bfloat16)]
-    next_local = half
+    source = pltpu.with_memory_space_constraint(hidden, pltpu.HBM)
+    jobs, next_local, last_ranks = [([((0, 0), half)], *partial_products(
+        pos, [(source, siblings, 0, half)], base_weight, factors, emitted=half - 1
+    ))], half, {}
     for piece, (step, shift) in enumerate(pieces):
-        own, siblings = gap(send, jobs, remote[step, shift], siblings)
-        if piece == 1:
-            siblings, panels = lax.optimization_barrier((siblings, panels))
+        (parts, send, keep, *emitted), *others = jobs
+        jobs = [(parts, send, keep, jnp.bfloat16)]
+        if emitted:
+            for along in range(1, n_rep):
+                remote[next_local - 1, along] = from_rep(emitted[0], along)
+        own, siblings, panels = gap(send, jobs, remote[step, shift], siblings, panels)
+        if piece == 0:
+            panels, order = spread_panels(panels, order, bits[1:])
         sib = swap_cores(own)
-        chunks, parts = [(own, sib, 0, 1)], [((step, shift), 1)]
+        if piece == len(pieces) - 1:
+            own, sib = gap(send, [], own, sib, short=True)
+        last, chunks, parts, place = step == step_count - 1, [(own, sib, 0, 1)], [((step, shift), 1)], None
         if next_local < step_count:
-            chunks.insert(0, (hidden, siblings, next_local, 1))
+            chunks.insert(0, (source, siblings, next_local, 1))
             parts.insert(0, ((next_local, 0), 1))
-            next_local += 1
-        send, keep, *ranks = multiply(chunks, step == step_count - 1)
-        jobs = [(parts, send, keep, jnp.bfloat16)]
-        if ranks:
-            jobs.insert(0, ([((RANK_NAME, shift), 1)], *ranks, jnp.float32))
-    gap(send, jobs)
-    gap(send, [])
-    ended.update((name, (kept, *received)) for name, kept, received in second_leg)
-
+            next_local, place = next_local + 1, 0
+        send, keep, *outs = partial_products(pos, chunks, base_weight, factors, last, place)
+        if last:
+            last_ranks[shift] = outs
+            outs = []
+        jobs = [(parts, send, keep, *outs)]
+    jobs = [(parts, send, keep, jnp.bfloat16)]
+    last_ranks, = gap(send, jobs, last_ranks)
+    for shift, ranks in last_ranks.items():
+        halved[RANK_NAME, shift] = second_half(ranks[1], swap_tensor(ranks[0], group // 2), 1, jnp.float32)[0]
+    values = [halved[RANK_NAME, at] for at in range(n_rep)]
+    ended[RANK_NAME] = (pick(values, (group_index - rep_index) % n_rep), *[
+        to_group(pick(values, (group_index + hop - rep_index) % n_rep), hop) for hop in range(1, n_rep)
+    ])
     def rank_sum(name):
         kept, *received = [value[:, -rank_columns(factors):] for value in ended[name]]
         for value in received:
@@ -362,6 +382,8 @@
 
     finished = jnp.stack([rank_sum(step) for step in range(step_count - 1)] + [rank_sum(RANK_NAME)])
     finished = finished.astype(jnp.bfloat16).reshape(step_count, rows_mine, owned_slots, rank_size)
+    finished, = gap(send, [], finished)
+    ended.update((name, (kept, *received)) for name, kept, received in second_leg)
     masked = jnp.sum(
         jnp.where(owned_hot[None, :, :, None], finished, 0), axis=2, dtype=jnp.float32
     ).astype(jnp.bfloat16)
@@ -370,6 +392,11 @@
         chosen = chosen + lax.ppermute(
             masked, ("rep", "sub"), [(i, (i + turn) % n_owners) for i in range(n_owners)]
         )
+    panel_slots = jnp.stack([
+        (tensor_index ^ at) * up_b.shape[0] + each for at in order for each in range(up_b.shape[0])
+    ]).astype(jnp.int32)
+
+    panels = [panel.reshape(-1, width) for panel in panels]
     partial, lifted = finish_steps(
         [ended[step] for step in range(step_count - 1)],
         chosen.reshape(step_count * rows_mine, rank_size),

time: 151 us -> 163 us (1.079)
  waiting for transfers between devices: 28.2 us -> 48 us
  starting transfers between devices: 30.8 us -> 26.3 us
  other arithmetic: 9.74 us -> 7.13 us
    ppermute x5, waiting for transfers between devices: 5.79 us -> 18.7 us  [to_group(): lax.ppermute(value, 'tp', [(i, (i + moved) % n_tensor) for i in range(n_t...]
    ppermute x8 -> x9, waiting for transfers between devices: 15.4 us -> 20.5 us  [swap_tensor(): return lax.ppermute(value, 'tp', [(i, i ^ bit) for i in range(n_tensor)])]
    ppermute x4, waiting for transfers between devices: 3.35 us -> 6.94 us  [from_rep(): lax.ppermute(value, 'rep', [((i + shift) % n_rep, i) for i in range(n_rep)])]
    concatenate x2 -> x0, other arithmetic: 2.99 us -> none  [per_device(): panels = jnp.concatenate([panels, swap_tensor(panels, bit)], axis=0)]
    ppermute x5, starting transfers between devices: 10.2 us -> 7.4 us  [to_group(): lax.ppermute(value, 'tp', [(i, (i + moved) % n_tensor) for i in range(n_t...]
    ppermute x4, starting transfers between devices: 7.65 us -> 5.25 us  [from_rep(): lax.ppermute(value, 'rep', [((i + shift) % n_rep, i) for i in range(n_rep)])]
    ppermute x3, waiting for transfers between devices: 3.61 us -> 1.82 us  [per_device(): lax.ppermute(masked, ('rep', 'sub'), [(i, (i + turn) % n_owners) for i in...]
    ppermute x8 -> x9, starting transfers between devices: 10.4 us -> 12 us  [swap_tensor(): return lax.ppermute(value, 'tp', [(i, i ^ bit) for i in range(n_tensor)])]
  transfers between devices with their start and end apart: 25 -> 26, of which waited for: 13 -> 12; matrix products, arithmetic and copies ran while one was open for 9% -> 6% of each run, Pallas kernels for 47% -> 43%
where the time goes in v7:
time: 163 us
  Pallas kernels  70.4 us (43%)
  waiting for transfers between devices  48 us (29%)
  starting transfers between devices  26.3 us (16%)
  local copies, waits for them, and re-layouts  10.3 us (6%)
  other arithmetic  7.13 us (4%)
    pallas_call x5, Pallas kernels, partial_products(): pl.pallas_call(functools.partial(matmul_body, spans, emitted, apart), in_...  67.1 us
    ppermute x9, waiting for transfers between devices, swap_tensor(): return lax.ppermute(value, 'tp', [(i, i ^ bit) for i in range(n_tensor)])  20.5 us
    ppermute x5, waiting for transfers between devices, to_group(): lax.ppermute(value, 'tp', [(i, (i + moved) % n_tensor) for i in range(n_t...  18.7 us
    ppermute x9, starting transfers between devices, swap_tensor(): return lax.ppermute(value, 'tp', [(i, i ^ bit) for i in range(n_tensor)])  12 us
    ppermute x5, starting transfers between devices, to_group(): lax.ppermute(value, 'tp', [(i, (i + moved) % n_tensor) for i in range(n_t...  7.4 us
    unnamed x48, local copies, waits for them, and re-layouts  7.22 us
    ppermute x4, waiting for transfers between devices, from_rep(): lax.ppermute(value, 'rep', [((i + shift) % n_rep, i) for i in range(n_rep)])  6.94 us
    ppermute x4, starting transfers between devices, from_rep(): lax.ppermute(value, 'rep', [((i + shift) % n_rep, i) for i in range(n_rep)])  5.25 us
  transfers between devices with their start and end apart: 26, of which 12 were waited for; matrix products, arithmetic and copies ran while one was open for 6% of the time, Pallas kernels for 43%

profile of v7, /device:TPU:0, one launch (start us, length us, event | category | flops | bytes accessed | tf_op | source)
XLA Modules:
  0.0 162.6 jit_solution(17749660318186327872)
XLA Ops:
  0.5 2.2 %slice.68 = bf16[1,64,7168]{2,1,0:T(8,128)(2,1)} slice(bf16[4,64,7168]{2,1,0:T(8,128)(2,1)} %refs_0_.5), slice={[0:1], [0:64], [0:7168]} | slice | bytes 1835008 | tf_op jit(solution)/shard_map/slice | solution.py:269
  2.7 2.6 %collective-permute-start.1 = (bf16[1,64,7168]{2,1,0:T(8,128)(2,1)}, bf16[1,64,7168]{2,1,0:T(8,128)(2,1)S(1)}, u32[]{:S(2)}, u32[]{:S(2)}) collective-permute-start(bf16[1,64,7168]{2,1,0:T(8,128)(2,1)} %slice.68), channel_id=1, source_target_pairs={{2,0},{0,2},{3,1},{1,3},{6,4},{4,6},{7,5},{5,7},{10,8},{8,10},{11,... | collective-permute-start | bytes 2752520 | tf_op jit(solution)/shard_map/ppermute | solution.py:249
  5.3 2.6 %collective-permute-start.2 = (bf16[1,64,2048]{2,1,0:T(8,128)(2,1)S(1)}, bf16[1,64,2048]{2,1,0:T(8,128)(2,1)}, u32[]{:S(2)}, u32[]{:S(2)}) collective-permute-start(bf16[1,64,2048]{2,1,0:T(8,128)(2,1)S(1)} %copy-done.7), channel_id=1, source_target_pairs={{0,8},{4,12},{8,0},{12,4},{1,9},{5,13},{9,1},{13,5},{2,10},{6,14},... | collective-permute-start | bytes 786440 | tf_op jit(solution)/shard_map/ppermute | solution.py:252
  7.9 15.7 %partial_products.5 = (bf16[128,2176]{1,0:T(8,128)(2,1)}, f32[128,2176]{1,0:T(8,128)S(1)}, bf16[1,64,7168]{2,1,0:T(8,128)(2,1)S(1)}) custom-call(s32[1]{0:T(128)} %bitcast.1.pos_ref, bf16[4,64,7168]{2,1,0:T(8,128)(2,1)} %refs_0_.5, bf16[4,64,7168]{2,1,0:T(8,128)(2,1)} %collective-permute-done.refs_1_, bf16[7168,2048]{1,0:T(8,128)(2,1)} %refs_2_.5, ...), custom_call_target="tpu_custom_call" | custom-call | tf_op jit(solution)/shard_map/partial_products/pallas_call | solution.py:126
  23.6 2.8 %collective-permute-done.1.refs_2_ = bf16[1,64,7168]{2,1,0:T(8,128)(2,1)S(1)} collective-permute-done((bf16[1,64,7168]{2,1,0:T(8,128)(2,1)}, bf16[1,64,7168]{2,1,0:T(8,128)(2,1)S(1)}, u32[]{:S(2)}, u32[]{:S(2)}) %collective-permute-start.1) | collective-permute-done | bytes 917536 | tf_op jit(solution)/shard_map/ppermute | solution.py:249
  27.3 1.8 %collective-permute-start.4 = (bf16[1,64,7168]{2,1,0:T(8,128)(2,1)S(1)}, bf16[1,64,7168]{2,1,0:T(8,128)(2,1)}, u32[]{:S(2)}, u32[]{:S(2)}) collective-permute-start(bf16[1,64,7168]{2,1,0:T(8,128)(2,1)S(1)} %get-tuple-element.74), channel_id=1, source_target_pairs={{2,0},{0,2},{3,1},{1,3},{6,4},{4,6},{7,5},{5,7},{10,8},{8,10},{11,... | collective-permute-start | bytes 2752520 | tf_op jit(solution)/shard_map/ppermute | solution.py:249
  29.1 1.6 collective-permute-start.9
  31.1 1.6 collective-permute-start.6
  33.9 11.9 %partial_products.6 = (bf16[128,2176]{1,0:T(8,128)(2,1)S(1)}, f32[128,2176]{1,0:T(8,128)S(1)}, bf16[1,64,7168]{2,1,0:T(8,128)(2,1)S(1)}) custom-call(s32[1]{0:T(128)} %bitcast.1.pos_ref, bf16[4,64,7168]{2,1,0:T(8,128)(2,1)} %refs_0_.5, bf16[4,64,7168]{2,1,0:T(8,128)(2,1)} %collective-permute-done.refs_1_, bf16[1,64,7168]{2,1,0:T(8,128)(2,1)S(1)} %copy-done.3, ...), custom_call_target="tpu_custom_call" | custom-call | tf_op jit(solution)/shard_map/partial_products/pallas_call | solution.py:126
  47.6 2.8 %collective-permute-done.5 = bf16[1,64,2048]{2,1,0:T(8,128)(2,1)S(1)} collective-permute-done((bf16[1,64,2048]{2,1,0:T(8,128)(2,1)S(1)}, bf16[1,64,2048]{2,1,0:T(8,128)(2,1)S(1)}, u32[]{:S(2)}, u32[]{:S(2)}) %collective-permute-start.5) | collective-permute-done | bytes 262176 | tf_op jit(solution)/shard_map/ppermute | solution.py:252
  51.1 4.2 %collective-permute-done.6 = bf16[1,64,2048]{2,1,0:T(8,128)(2,1)S(1)} collective-permute-done((bf16[1,64,2048]{2,1,0:T(8,128)(2,1)}, bf16[1,64,2048]{2,1,0:T(8,128)(2,1)S(1)}, u32[]{:S(2)}, u32[]{:S(2)}) %collective-permute-start.6) | collective-permute-done | bytes 262176 | tf_op jit(solution)/shard_map/ppermute | solution.py:252
  56.4 1.7 %collective-permute-start.8 = (bf16[128,2176]{1,0:T(8,128)(2,1)}, bf16[128,2176]{1,0:T(8,128)(2,1)S(1)}, u32[]{:S(2)}, u32[]{:S(2)}) collective-permute-start(bf16[128,2176]{1,0:T(8,128)(2,1)} %copy-done.15), channel_id=1, source_target_pairs={{0,4},{4,0},{8,12},{12,8},{1,5},{5,1},{9,13},{13,9},{2,6},{6,2},{1... | collective-permute-start | bytes 1671176 | tf_op jit(solution)/shard_map/ppermute | solution.py:252
  58.1 1.2 convert_add_fusion.1
  59.3 16.0 %partial_products.7 = (bf16[128,2176]{1,0:T(8,128)(2,1)}, f32[128,2176]{1,0:T(8,128)S(1)}, bf16[1,64,7168]{2,1,0:T(8,128)(2,1)S(1)}) custom-call(s32[1]{0:T(128)} %bitcast.1.pos_ref, bf16[4,64,7168]{2,1,0:T(8,128)(2,1)} %refs_0_.5, bf16[4,64,7168]{2,1,0:T(8,128)(2,1)} %collective-permute-done.refs_1_, bf16[1,64,7168]{2,1,0:T(8,128)(2,1)} %collective-permute-done.4.refs_2_, ...), custom_call_target="tpu_custom_call" | custom-call | tf_op jit(solution)/shard_map/partial_products/pallas_call | solution.py:126
  77.4 1.7 %collective-permute-done.10.refs_0_ = bf16[1,64,7168]{2,1,0:T(8,128)(2,1)} collective-permute-done((bf16[1,64,7168]{2,1,0:T(8,128)(2,1)}, bf16[1,64,7168]{2,1,0:T(8,128)(2,1)}, u32[]{:S(2)}, u32[]{:S(2)}) %collective-permute-start.10) | collective-permute-done | bytes 917536 | tf_op jit(solution)/shard_map/ppermute | solution.py:249
  79.1 1.6 collective-permute-start.12
  80.8 2.6 %collective-permute-start.14 = (bf16[64,2176]{1,0:T(8,128)(2,1)}, bf16[64,2176]{1,0:T(8,128)(2,1)S(1)}, u32[]{:S(2)}, u32[]{:S(2)}) collective-permute-start(bf16[64,2176]{1,0:T(8,128)(2,1)} %select_convert_fusion.2), channel_id=1, source_target_pairs={{0,8},{4,12},{8,0},{12,4},{1,9},{5,13},{9,1},{13,5},{2,10},{6,14},... | collective-permute-start | bytes 835592 | tf_op jit(solution)/shard_map/ppermute | solution.py:256
  84.0 12.8 %partial_products.8 = (bf16[64,2176]{1,0:T(8,128)(2,1)}, f32[64,2176]{1,0:T(8,128)S(1)}) custom-call(s32[1]{0:T(128)} %bitcast.1.pos_ref, bf16[1,64,7168]{2,1,0:T(8,128)(2,1)} %collective-permute-done.10.refs_0_, bf16[1,64,7168]{2,1,0:T(8,128)(2,1)} %collective-permute-done.11.refs_1_, bf16[7168,2048]{1,0:T(8,128)(2,1)} %refs_2_.5, ...), custom_call_target="tpu_custom_call" | custom-call | tf_op jit(solution)/shard_map/partial_products/pallas_call | solution.py:126
  96.8 3.6 %collective-permute-done.12 = bf16[128,2176]{1,0:T(8,128)(2,1)} collective-permute-done((bf16[128,2176]{1,0:T(8,128)(2,1)}, bf16[128,2176]{1,0:T(8,128)(2,1)}, u32[]{:S(2)}, u32[]{:S(2)}) %collective-permute-start.12) | collective-permute-done | bytes 557088 | tf_op jit(solution)/shard_map/ppermute | solution.py:252
  103.4 2.4 %collective-permute-done.13.refs_0_ = bf16[1,64,7168]{2,1,0:T(8,128)(2,1)S(1)} collective-permute-done((bf16[1,64,7168]{2,1,0:T(8,128)(2,1)}, bf16[1,64,7168]{2,1,0:T(8,128)(2,1)S(1)}, u32[]{:S(2)}, u32[]{:S(2)}) %collective-permute-start.13) | collective-permute-done | bytes 917536 | tf_op jit(solution)/shard_map/ppermute | solution.py:249
  107.2 2.0 %collective-permute-start.17 = (bf16[64,2176]{1,0:T(8,128)(2,1)}, bf16[64,2176]{1,0:T(8,128)(2,1)S(1)}, u32[]{:S(2)}, u32[]{:S(2)}) collective-permute-start(bf16[64,2176]{1,0:T(8,128)(2,1)} %select_convert_fusion.1), channel_id=1, source_target_pairs={{0,8},{4,12},{8,0},{12,4},{1,9},{5,13},{9,1},{13,5},{2,10},{6,14},... | collective-permute-start | bytes 835592 | tf_op jit(solution)/shard_map/ppermute | solution.py:256
  109.3 7.6 %collective-permute-done.15 = bf16[64,2176]{1,0:T(8,128)(2,1)} collective-permute-done((bf16[64,2176]{1,0:T(8,128)(2,1)}, bf16[64,2176]{1,0:T(8,128)(2,1)}, u32[]{:S(2)}, u32[]{:S(2)}) %collective-permute-start.15) | collective-permute-done | bytes 278560 | tf_op jit(solution)/shard_map/ppermute | solution.py:252
  116.9 1.2 select_convert_fusion
  119.9 10.7 %partial_products.9 = (bf16[64,2048]{1,0:T(8,128)(2,1)S(1)}, f32[64,2048]{1,0:T(8,128)S(1)}, f32[64,128]{1,0:T(8,128)S(1)}, f32[64,128]{1,0:T(8,128)S(1)}) custom-call(s32[1]{0:T(128)} %bitcast.1.pos_ref, bf16[1,64,7168]{2,1,0:T(8,128)(2,1)S(1)} %collective-permute-done.13.refs_0_, bf16[1,64,7168]{2,1,0:T(8,128)(2,1)S(1)} %collective-permute-done.16.refs_1_, ...), custom_call_target="tpu_custom_call" | custom-call | tf_op jit(solution)/shard_map/partial_products/pallas_call | solution.py:126
  130.6 4.8 %collective-permute-done.18.refs_9_ = bf16[64,2176]{1,0:T(8,128)(2,1)S(1)} collective-permute-done((bf16[64,2176]{1,0:T(8,128)(2,1)S(1)}, bf16[64,2176]{1,0:T(8,128)(2,1)S(1)}, u32[]{:S(2)}, u32[]{:S(2)}) %collective-permute-start.18) | collective-permute-done | bytes 278560 | tf_op jit(solution)/shard_map/ppermute | solution.py:256
  135.5 2.0 %collective-permute-start.19 = (bf16[64,2048]{1,0:T(8,128)(2,1)S(1)}, bf16[64,2048]{1,0:T(8,128)(2,1)S(1)}, u32[]{:S(2)}, u32[]{:S(2)}) collective-permute-start(bf16[64,2048]{1,0:T(8,128)(2,1)S(1)} %get-tuple-element.118), channel_id=1, source_target_pairs={{0,4},{4,0},{8,12},{12,8},{1,5},{5,1},{9,13},{13,9},{2,6},{6,2},{1... | collective-permute-start | bytes 786440 | tf_op jit(solution)/shard_map/ppermute | solution.py:252
  137.5 2.2 %collective-permute-done.20 = f32[64,128]{1,0:T(8,128)S(1)} collective-permute-done((f32[64,128]{1,0:T(8,128)S(1)}, f32[64,128]{1,0:T(8,128)S(1)}, u32[]{:S(2)}, u32[]{:S(2)}) %collective-permute-start.20) | collective-permute-done | bytes 32800 | tf_op jit(solution)/shard_map/ppermute | solution.py:252
  139.9 4.9 %collective-permute-done.21 = f32[64,128]{1,0:T(8,128)S(1)} collective-permute-done((f32[64,128]{1,0:T(8,128)S(1)}, f32[64,128]{1,0:T(8,128)S(1)}, u32[]{:S(2)}, u32[]{:S(2)}) %collective-permute-start.21) | collective-permute-done | bytes 32800 | tf_op jit(solution)/shard_map/ppermute | solution.py:256
  146.2 2.0 %collective-permute-start.25 = (bf16[64,2048]{1,0:T(8,128)(2,1)S(1)}, bf16[64,2048]{1,0:T(8,128)(2,1)S(1)}, u32[]{:S(2)}, u32[]{:S(2)}) collective-permute-start(bf16[64,2048]{1,0:T(8,128)(2,1)S(1)} %select_convert_fusion.3), channel_id=1, source_target_pairs={{0,8},{4,12},{8,0},{12,4},{1,9},{5,13},{9,1},{13,5},{2,10},{6,14},... | collective-permute-start | bytes 786440 | tf_op jit(solution)/shard_map/ppermute | solution.py:256
  148.2 1.8 %collective-permute-done.23 = bf16[4,64,64]{2,1,0:T(8,128)(2,1)S(1)} collective-permute-done((bf16[4,64,64]{2,1,0:T(8,128)(2,1)S(1)}, bf16[4,64,64]{2,1,0:T(8,128)(2,1)S(1)}, u32[]{:S(2)}, u32[]{:S(2)}) %collective-permute-start.23) | collective-permute-done | bytes 32800 | tf_op jit(solution)/shard_map/ppermute | solution.py:392
  150.2 2.5 %finish_steps.1 = (bf16[4,64,2048]{2,1,0:T(8,128)(2,1)}, bf16[64,2048]{1,0:T(8,128)(2,1)S(1)}) custom-call(bf16[256,64]{1,0:T(8,128)(2,1)S(1)} %bitcast.30, s32[256,1]{1,0:T(8,128)S(1)} %copy-done.4, s32[4]{0:T(128)S(1)} %pad_add_fusion.order_ref, bf16[64,2048]{1,0:T(8,128)(2,1)S(1)} %bitcast.31, bf16[64,2048]{1,0:T(8,128)(2,1)} %bitcast.14.refs_1_, ...), custom_call_target="tpu_custom_call" | custom-call | tf_op jit(solution)/shard_map/finish_steps/pallas_call | solution.py:181
  152.7 9.0 %collective-permute-done.25.refs_1_ = bf16[64,2048]{1,0:T(8,128)(2,1)S(1)} collective-permute-done((bf16[64,2048]{1,0:T(8,128)(2,1)S(1)}, bf16[64,2048]{1,0:T(8,128)(2,1)S(1)}, u32[]{:S(2)}, u32[]{:S(2)}) %collective-permute-start.25) | collective-permute-done | bytes 262176 | tf_op jit(solution)/shard_map/ppermute | solution.py:256
  (106 shorter events, 18.0 us)
Async XLA Ops:
  0.0 80.7 %copy-start = (s32[256,1]{0,1:T(1,128)S(1)}, s32[256,1]{0,1:T(1,128)}, u32[]{:S(2)}) copy-start(s32[256,1]{0,1:T(1,128)} %param.10) | copy-start | bytes 3076
  0.0 7.9 %copy-start.1 = (bf16[1,7168,64]{1,2,0:T(8,128)(2,1)S(1)}, bf16[1,7168,64]{1,2,0:T(8,128)(2,1)}, u32[]{:S(2)}) copy-start(bf16[1,7168,64]{1,2,0:T(8,128)(2,1)} %param.8) | copy-start | bytes 2752516
  0.0 7.9 %collective-permute-start = (bf16[4,64,7168]{2,1,0:T(8,128)(2,1)}, bf16[4,64,7168]{2,1,0:T(8,128)(2,1)}, u32[]{:S(2)}, u32[]{:S(2)}) collective-permute-start(bf16[4,64,7168]{2,1,0:T(8,128)(2,1)} %refs_0_.5), channel_id=1, source_target_pairs={{0,1},{1,0},{2,3},{3,2},{4,5},{5,4},{6,7},{7,6},{8,9},{9,8},{10,11... | collective-permute-start | bytes 11010056 | tf_op jit(solution)/shard_map/ppermute | solution.py:246
  2.7 23.7 %collective-permute-start.1 = (bf16[1,64,7168]{2,1,0:T(8,128)(2,1)}, bf16[1,64,7168]{2,1,0:T(8,128)(2,1)S(1)}, u32[]{:S(2)}, u32[]{:S(2)}) collective-permute-start(bf16[1,64,7168]{2,1,0:T(8,128)(2,1)} %slice.68), channel_id=1, source_target_pairs={{2,0},{0,2},{3,1},{1,3},{6,4},{4,6},{7,5},{5,7},{10,8},{8,10},{11,... | collective-permute-start | bytes 2752520 | tf_op jit(solution)/shard_map/ppermute | solution.py:249
  5.3 18.3 %collective-permute-start.2 = (bf16[1,64,2048]{2,1,0:T(8,128)(2,1)S(1)}, bf16[1,64,2048]{2,1,0:T(8,128)(2,1)}, u32[]{:S(2)}, u32[]{:S(2)}) collective-permute-start(bf16[1,64,2048]{2,1,0:T(8,128)(2,1)S(1)} %copy-done.7), channel_id=1, source_target_pairs={{0,8},{4,12},{8,0},{12,4},{1,9},{5,13},{9,1},{13,5},{2,10},{6,14},... | collective-permute-start | bytes 786440 | tf_op jit(solution)/shard_map/ppermute | solution.py:252
  26.4 6.3 %collective-permute-start.3 = (bf16[1,64,7168]{2,1,0:T(8,128)(2,1)S(1)}, bf16[1,64,7168]{2,1,0:T(8,128)(2,1)S(1)}, u32[]{:S(2)}, u32[]{:S(2)}) collective-permute-start(bf16[1,64,7168]{2,1,0:T(8,128)(2,1)S(1)} %collective-permute-done.1.refs_2_), channel_id=1, source_target_pairs={{0,1},{1,0},{2,3},{3,2},{4,5},{5,4},{6,7},{7,6},{8,9},{9,8},{10,11... | collective-permute-start | bytes 2752520 | tf_op jit(solution)/shard_map/ppermute | solution.py:246
  27.3 28.7 %collective-permute-start.4 = (bf16[1,64,7168]{2,1,0:T(8,128)(2,1)S(1)}, bf16[1,64,7168]{2,1,0:T(8,128)(2,1)}, u32[]{:S(2)}, u32[]{:S(2)}) collective-permute-start(bf16[1,64,7168]{2,1,0:T(8,128)(2,1)S(1)} %get-tuple-element.74), channel_id=1, source_target_pairs={{2,0},{0,2},{3,1},{1,3},{6,4},{4,6},{7,5},{5,7},{10,8},{8,10},{11,... | collective-permute-start | bytes 2752520 | tf_op jit(solution)/shard_map/ppermute | solution.py:249
  29.1 29.0 %collective-permute-start.9 = (bf16[128,2176]{1,0:T(8,128)(2,1)}, bf16[128,2176]{1,0:T(8,128)(2,1)}, u32[]{:S(2)}, u32[]{:S(2)}) collective-permute-start(bf16[128,2176]{1,0:T(8,128)(2,1)} %get-tuple-element.85), channel_id=1, source_target_pairs={{0,4},{4,0},{8,12},{12,8},{1,5},{5,1},{9,13},{13,9},{2,6},{6,2},{1... | collective-permute-start | bytes 1671176 | tf_op jit(solution)/shard_map/ppermute | solution.py:252
  30.7 19.7 %collective-permute-start.5 = (bf16[1,64,2048]{2,1,0:T(8,128)(2,1)S(1)}, bf16[1,64,2048]{2,1,0:T(8,128)(2,1)S(1)}, u32[]{:S(2)}, u32[]{:S(2)}) collective-permute-start(bf16[1,64,2048]{2,1,0:T(8,128)(2,1)S(1)} %copy-done.7), channel_id=1, source_target_pairs={{0,4},{4,0},{8,12},{12,8},{1,5},{5,1},{9,13},{13,9},{2,6},{6,2},{1... | collective-permute-start | bytes 786440 | tf_op jit(solution)/shard_map/ppermute | solution.py:252
  31.1 24.2 %collective-permute-start.6 = (bf16[1,64,2048]{2,1,0:T(8,128)(2,1)}, bf16[1,64,2048]{2,1,0:T(8,128)(2,1)S(1)}, u32[]{:S(2)}, u32[]{:S(2)}) collective-permute-start(bf16[1,64,2048]{2,1,0:T(8,128)(2,1)} %collective-permute-done.2), channel_id=1, source_target_pairs={{0,4},{4,0},{8,12},{12,8},{1,5},{5,1},{9,13},{13,9},{2,6},{6,2},{1... | collective-permute-start | bytes 786440 | tf_op jit(solution)/shard_map/ppermute | solution.py:252
  56.0 3.3 %collective-permute-start.7 = (bf16[1,64,7168]{2,1,0:T(8,128)(2,1)}, bf16[1,64,7168]{2,1,0:T(8,128)(2,1)}, u32[]{:S(2)}, u32[]{:S(2)}) collective-permute-start(bf16[1,64,7168]{2,1,0:T(8,128)(2,1)} %collective-permute-done.4.refs_2_), channel_id=1, source_target_pairs={{0,1},{1,0},{2,3},{3,2},{4,5},{5,4},{6,7},{7,6},{8,9},{9,8},{10,11... | collective-permute-start | bytes 2752520 | tf_op jit(solution)/shard_map/ppermute | solution.py:246
  56.0 23.1 %collective-permute-start.10 = (bf16[1,64,7168]{2,1,0:T(8,128)(2,1)}, bf16[1,64,7168]{2,1,0:T(8,128)(2,1)}, u32[]{:S(2)}, u32[]{:S(2)}) collective-permute-start(bf16[1,64,7168]{2,1,0:T(8,128)(2,1)} %copy-done.13), channel_id=1, source_target_pairs={{2,0},{0,2},{3,1},{1,3},{6,4},{4,6},{7,5},{5,7},{10,8},{8,10},{11,... | collective-permute-start | bytes 2752520 | tf_op jit(solution)/shard_map/ppermute | solution.py:249
  56.4 19.0 %collective-permute-start.8 = (bf16[128,2176]{1,0:T(8,128)(2,1)}, bf16[128,2176]{1,0:T(8,128)(2,1)S(1)}, u32[]{:S(2)}, u32[]{:S(2)}) collective-permute-start(bf16[128,2176]{1,0:T(8,128)(2,1)} %copy-done.15), channel_id=1, source_target_pairs={{0,4},{4,0},{8,12},{12,8},{1,5},{5,1},{9,13},{13,9},{2,6},{6,2},{1... | collective-permute-start | bytes 1671176 | tf_op jit(solution)/shard_map/ppermute | solution.py:252
  59.3 16.2 %copy-start.19 = (f32[128,2176]{1,0:T(8,128)}, f32[128,2176]{1,0:T(8,128)S(1)}, u32[]{:S(2)}) copy-start(f32[128,2176]{1,0:T(8,128)S(1)} %convert_add_fusion.1) | copy-start | bytes 3342340
  79.1 4.9 %collective-permute-start.11 = (bf16[1,64,7168]{2,1,0:T(8,128)(2,1)}, bf16[1,64,7168]{2,1,0:T(8,128)(2,1)}, u32[]{:S(2)}, u32[]{:S(2)}) collective-permute-start(bf16[1,64,7168]{2,1,0:T(8,128)(2,1)} %collective-permute-done.10.refs_0_), channel_id=1, source_target_pairs={{0,1},{1,0},{2,3},{3,2},{4,5},{5,4},{6,7},{7,6},{8,9},{9,8},{10,11... | collective-permute-start | bytes 2752520 | tf_op jit(solution)/shard_map/ppermute | solution.py:246
  79.1 21.3 %collective-permute-start.12 = (bf16[128,2176]{1,0:T(8,128)(2,1)}, bf16[128,2176]{1,0:T(8,128)(2,1)}, u32[]{:S(2)}, u32[]{:S(2)}) collective-permute-start(bf16[128,2176]{1,0:T(8,128)(2,1)} %get-tuple-element.97), channel_id=1, source_target_pairs={{0,4},{4,0},{8,12},{12,8},{1,5},{5,1},{9,13},{13,9},{2,6},{6,2},{1... | collective-permute-start | bytes 1671176 | tf_op jit(solution)/shard_map/ppermute | solution.py:252
  80.8 22.6 %collective-permute-start.14 = (bf16[64,2176]{1,0:T(8,128)(2,1)}, bf16[64,2176]{1,0:T(8,128)(2,1)S(1)}, u32[]{:S(2)}, u32[]{:S(2)}) collective-permute-start(bf16[64,2176]{1,0:T(8,128)(2,1)} %select_convert_fusion.2), channel_id=1, source_target_pairs={{0,8},{4,12},{8,0},{12,4},{1,9},{5,13},{9,1},{13,5},{2,10},{6,14},... | collective-permute-start | bytes 835592 | tf_op jit(solution)/shard_map/ppermute | solution.py:256
  83.4 22.4 %collective-permute-start.13 = (bf16[1,64,7168]{2,1,0:T(8,128)(2,1)}, bf16[1,64,7168]{2,1,0:T(8,128)(2,1)S(1)}, u32[]{:S(2)}, u32[]{:S(2)}) collective-permute-start(bf16[1,64,7168]{2,1,0:T(8,128)(2,1)} %copy-done.14), channel_id=1, source_target_pairs={{2,0},{0,2},{3,1},{1,3},{6,4},{4,6},{7,5},{5,7},{10,8},{8,10},{11,... | collective-permute-start | bytes 2752520 | tf_op jit(solution)/shard_map/ppermute | solution.py:249
  105.9 11.0 %collective-permute-start.15 = (bf16[64,2176]{1,0:T(8,128)(2,1)}, bf16[64,2176]{1,0:T(8,128)(2,1)}, u32[]{:S(2)}, u32[]{:S(2)}) collective-permute-start(bf16[64,2176]{1,0:T(8,128)(2,1)} %get-tuple-element.105), channel_id=1, source_target_pairs={{0,4},{4,0},{8,12},{12,8},{1,5},{5,1},{9,13},{13,9},{2,6},{6,2},{1... | collective-permute-start | bytes 835592 | tf_op jit(solution)/shard_map/ppermute | solution.py:252
  107.2 11.7 %copy-start.18 = (f32[128,2176]{1,0:T(8,128)S(1)}, f32[128,2176]{1,0:T(8,128)}, u32[]{:S(2)}) copy-start(f32[128,2176]{1,0:T(8,128)} %copy-done.16) | copy-start | bytes 3342340
  107.2 10.9 %collective-permute-start.16 = (bf16[1,64,7168]{2,1,0:T(8,128)(2,1)S(1)}, bf16[1,64,7168]{2,1,0:T(8,128)(2,1)S(1)}, u32[]{:S(2)}, u32[]{:S(2)}) collective-permute-start(bf16[1,64,7168]{2,1,0:T(8,128)(2,1)S(1)} %collective-permute-done.13.refs_0_), channel_id=1, source_target_pairs={{0,1},{1,0},{2,3},{3,2},{4,5},{5,4},{6,7},{7,6},{8,9},{9,8},{10,11... | collective-permute-start | bytes 2752520 | tf_op jit(solution)/shard_map/ppermute | solution.py:246
  107.2 23.4 %collective-permute-start.17 = (bf16[64,2176]{1,0:T(8,128)(2,1)}, bf16[64,2176]{1,0:T(8,128)(2,1)S(1)}, u32[]{:S(2)}, u32[]{:S(2)}) collective-permute-start(bf16[64,2176]{1,0:T(8,128)(2,1)} %select_convert_fusion.1), channel_id=1, source_target_pairs={{0,8},{4,12},{8,0},{12,4},{1,9},{5,13},{9,1},{13,5},{2,10},{6,14},... | collective-permute-start | bytes 835592 | tf_op jit(solution)/shard_map/ppermute | solution.py:256
  118.1 17.3 %collective-permute-start.18 = (bf16[64,2176]{1,0:T(8,128)(2,1)S(1)}, bf16[64,2176]{1,0:T(8,128)(2,1)S(1)}, u32[]{:S(2)}, u32[]{:S(2)}) collective-permute-start(bf16[64,2176]{1,0:T(8,128)(2,1)S(1)} %select_convert_fusion), channel_id=1, source_target_pairs={{0,8},{4,12},{8,0},{12,4},{1,9},{5,13},{9,1},{13,5},{2,10},{6,14},... | collective-permute-start | bytes 835592 | tf_op jit(solution)/shard_map/ppermute | solution.py:256
  119.9 17.6 %slice-start = ((bf16[64,2176]{1,0:T(8,128)(2,1)}), bf16[64,128]{1,0:T(8,128)(2,1)S(1)}, s32[]{:S(2)}) async-start(bf16[64,2176]{1,0:T(8,128)(2,1)} %copy-done.5), calls=%async_computation | async-start | bytes 32768 | tf_op jit(solution)/shard_map/slice | solution.py:378
  119.9 19.9 %copy-start.22 = (f32[128,2176]{1,0:T(8,128)S(1)}, f32[128,2176]{1,0:T(8,128)}, u32[]{:S(2)}) copy-start(f32[128,2176]{1,0:T(8,128)} %copy-done.21) | copy-start | bytes 3342340
  135.4 4.4 %collective-permute-start.20 = (f32[64,128]{1,0:T(8,128)S(1)}, f32[64,128]{1,0:T(8,128)S(1)}, u32[]{:S(2)}, u32[]{:S(2)}) collective-permute-start(f32[64,128]{1,0:T(8,128)S(1)} %get-tuple-element.126), channel_id=1, source_target_pairs={{0,4},{4,0},{8,12},{12,8},{1,5},{5,1},{9,13},{13,9},{2,6},{6,2},{1... | collective-permute-start | bytes 98312 | tf_op jit(solution)/shard_map/ppermute | solution.py:252
  135.5 9.3 %collective-permute-start.19 = (bf16[64,2048]{1,0:T(8,128)(2,1)S(1)}, bf16[64,2048]{1,0:T(8,128)(2,1)S(1)}, u32[]{:S(2)}, u32[]{:S(2)}) collective-permute-start(bf16[64,2048]{1,0:T(8,128)(2,1)S(1)} %get-tuple-element.118), channel_id=1, source_target_pairs={{0,4},{4,0},{8,12},{12,8},{1,5},{5,1},{9,13},{13,9},{2,6},{6,2},{1... | collective-permute-start | bytes 786440 | tf_op jit(solution)/shard_map/ppermute | solution.py:252
  139.8 5.0 %collective-permute-start.21 = (f32[64,128]{1,0:T(8,128)S(1)}, f32[64,128]{1,0:T(8,128)S(1)}, u32[]{:S(2)}, u32[]{:S(2)}) collective-permute-start(f32[64,128]{1,0:T(8,128)S(1)} %get-tuple-element.135), channel_id=1, source_target_pairs={{0,8},{4,12},{8,0},{12,4},{1,9},{5,13},{9,1},{13,5},{2,10},{6,14},... | collective-permute-start | bytes 98312 | tf_op jit(solution)/shard_map/ppermute | solution.py:256
  145.1 5.0 %collective-permute-start.23 = (bf16[4,64,64]{2,1,0:T(8,128)(2,1)S(1)}, bf16[4,64,64]{2,1,0:T(8,128)(2,1)S(1)}, u32[]{:S(2)}, u32[]{:S(2)}) collective-permute-start(bf16[4,64,64]{2,1,0:T(8,128)(2,1)S(1)} %select_bitcast_fusion), channel_id=1, source_target_pairs={{0,2},{1,3},{2,0},{3,1},{4,6},{5,7},{6,4},{7,5},{8,10},{9,11},{10,... | collective-permute-start | bytes 98312 | tf_op jit(solution)/shard_map/ppermute | solution.py:392
  145.7 4.4 %collective-permute-start.24 = (bf16[4,64,64]{2,1,0:T(8,128)(2,1)S(1)}, bf16[4,64,64]{2,1,0:T(8,128)(2,1)S(1)}, u32[]{:S(2)}, u32[]{:S(2)}) collective-permute-start(bf16[4,64,64]{2,1,0:T(8,128)(2,1)S(1)} %select_bitcast_fusion), channel_id=1, source_target_pairs={{0,3},{1,0},{2,1},{3,2},{4,7},{5,4},{6,5},{7,6},{8,11},{9,8},{10,9... | collective-permute-start | bytes 98312 | tf_op jit(solution)/shard_map/ppermute | solution.py:392
  145.7 4.4 %collective-permute-start.22 = (bf16[4,64,64]{2,1,0:T(8,128)(2,1)S(1)}, bf16[4,64,64]{2,1,0:T(8,128)(2,1)S(1)}, u32[]{:S(2)}, u32[]{:S(2)}) collective-permute-start(bf16[4,64,64]{2,1,0:T(8,128)(2,1)S(1)} %select_bitcast_fusion), channel_id=1, source_target_pairs={{0,1},{1,2},{2,3},{3,0},{4,5},{5,6},{6,7},{7,4},{8,9},{9,10},{10,1... | collective-permute-start | bytes 98312 | tf_op jit(solution)/shard_map/ppermute | solution.py:392
  146.2 15.6 %collective-permute-start.25 = (bf16[64,2048]{1,0:T(8,128)(2,1)S(1)}, bf16[64,2048]{1,0:T(8,128)(2,1)S(1)}, u32[]{:S(2)}, u32[]{:S(2)}) collective-permute-start(bf16[64,2048]{1,0:T(8,128)(2,1)S(1)} %select_convert_fusion.3), channel_id=1, source_target_pairs={{0,8},{4,12},{8,0},{12,4},{1,9},{5,13},{9,1},{13,5},{2,10},{6,14},... | collective-permute-start | bytes 786440 | tf_op jit(solution)/shard_map/ppermute | solution.py:256
  (19 other events, 57.0 us)

commit v8 on v7

--- a/solution.py
+++ b/solution.py
@@ -9,19 +9,18 @@
 
 ADAPTER_SCALE = 0.5
 BLOCK_N = 256
-BLOCK_VALUES = 1024 * 1024
-BUFFERS = 3
-WIDE_ROWS = 128
+BLOCK = 1024
+BUFFERS = 4
 RANK_NAME = 1000
-VMEM_BYTES = 24 * 1024 * 1024
-
-
-def block_depth(depth, width, rows):
-    values = BLOCK_VALUES * (2 if rows >= WIDE_ROWS else 1)
-    for size in (1024, 512, 256):
-        if depth % size == 0 and size * width <= values:
-            return size
-    return depth
+VMEM_BYTES = 17 * 1024 * 1024
+
+
+def block_shape(depth, width):
+    columns = BLOCK if width % BLOCK == 0 else width
+    for size in (BLOCK, BLOCK // 2, BLOCK // 4):
+        if depth % size == 0:
+            return size, columns
+    return depth, columns
 
 
 def rank_columns(factors):
@@ -37,13 +36,15 @@
     rows = send_ref.shape[0]
     depth, width = w_ref.shape
     slots, rank, _ = a_ref.shape
-    buffers, block_k, _ = w_buf.shape
-    block_n = min(BLOCK_N, width)
-    count = depth // block_k
+    buffers, block_k, block_w = w_buf.shape
+    block_n = min(BLOCK_N, block_w)
+    depths, count = depth // block_k, (depth // block_k) * (width // block_w)
 
     def fetch(block, slot):
+        begin = pl.multiple_of(lax.rem(block, depths) * block_k, block_k)
+        left = pl.multiple_of(lax.div(block, depths) * block_w, block_w)
         return pltpu.make_async_copy(
-            w_ref.at[pl.ds(block * block_k, block_k)], w_buf.at[slot], w_sems.at[slot]
+            w_ref.at[pl.ds(begin, block_k), pl.ds(left, block_w)], w_buf.at[slot], w_sems.at[slot]
         )
 
     own_at = pos_ref[0]
@@ -58,7 +59,7 @@
     for copy in copies:
         copy.start()
     for block in range(buffers):
-        fetch(block, block).start()
+        fetch(jnp.int32(block), block).start()
     keep_ref[...] = jnp.zeros_like(keep_ref)
     total_ref[...] = jnp.zeros_like(total_ref)
     send_rank, keep_rank = outs[:2] if apart else (total_ref, keep_ref)
@@ -86,11 +87,14 @@
     def _(block):
         slot = lax.rem(block, buffers)
         fetch(block, slot).wait()
-        inner = pl.ds(pl.multiple_of(block * block_k, block_k), block_k)
+        inner = pl.ds(pl.multiple_of(lax.rem(block, depths) * block_k, block_k), block_k)
+        left = pl.multiple_of(lax.div(block, depths) * block_w, block_w)
         x = x_ref[:, :, :, inner].reshape(2 * rows, block_k)
-        for place in range(width // block_n):
-            columns = slice(place * block_n, (place + 1) * block_n)
-            term = jnp.dot(x, w_buf[slot, :, columns], preferred_element_type=jnp.float32)
+        for place in range(block_w // block_n):
+            columns = pl.ds(left + place * block_n, block_n)
+            term = jnp.dot(
+                x, w_buf[slot, :, place * block_n:(place + 1) * block_n], preferred_element_type=jnp.float32
+            )
             total_ref[:, columns] += term[:rows]
             keep_ref[:, columns] += term[rows:]
 
@@ -109,8 +113,8 @@
     spans = tuple((first, steps) for _, _, first, steps in chunks)
     steps = sum(length for _, length in spans)
     rows = steps * per_block
-    block_k = block_depth(depth, width, rows)
-    buffers = min(BUFFERS if rows >= WIDE_ROWS else 2 * BUFFERS, depth // block_k)
+    block_k, block_w = block_shape(depth, width)
+    buffers = min(BUFFERS, (depth // block_k) * (width // block_w))
     any_spec = pl.BlockSpec(memory_space=pl.ANY)
     vmem_spec = pl.BlockSpec(memory_space=pltpu.VMEM)
     extra = rank_columns(factors)
@@ -130,7 +134,7 @@
         out_shape=out_shape,
         scratch_shapes=[
             pltpu.VMEM((2, steps, per_block, depth), jnp.bfloat16),
-            pltpu.VMEM((buffers, block_k, width), jnp.bfloat16),
+            pltpu.VMEM((buffers, block_k, block_w), jnp.bfloat16),
             pltpu.VMEM((rows, columns), jnp.float32),
             pltpu.SemaphoreType.DMA((2 * len(chunks) + 1,)),
             pltpu.SemaphoreType.DMA((buffers,)),
@@ -139,6 +143,24 @@
         cost_estimate=pl.CostEstimate(flops=0, bytes_accessed=0, transcendentals=0),
         name="partial_products",
     )(pos, *[source for own, sib, _, _ in chunks for source in (own, sib)], weight, factors)
+
+
+def cut_body(source_ref, out_ref, sem):
+    copy = pltpu.make_async_copy(source_ref.at[pl.ds(0, 1)], out_ref, sem)
+    copy.start()
+    copy.wait()
+
+
+def cut_first(hidden):
+    return pl.pallas_call(
+        cut_body,
+        in_specs=[pl.BlockSpec(memory_space=pl.ANY)],
+        out_specs=pl.BlockSpec(memory_space=pltpu.VMEM),
+        out_shape=jax.ShapeDtypeStruct((1,) + hidden.shape[1:], hidden.dtype),
+        scratch_shapes=[pltpu.SemaphoreType.DMA],
+        cost_estimate=pl.CostEstimate(flops=0, bytes_accessed=0, transcendentals=0),
+        name="cut_first",
+    )(hidden)
 
 
 def finish_body(received, panels, chosen_ref, slot_ref, order_ref, *refs):
@@ -266,7 +288,9 @@
 
     siblings = swap_cores(hidden)
     pieces = [(step, shift) for step in range(step_count) for shift in range(1, n_rep)]
-    remote = {(0, shift): from_rep(hidden[:1], shift) for shift in range(1, n_rep)}
+    source = pltpu.with_memory_space_constraint(hidden, pltpu.HBM)
+    first_rows = cut_first(source)
+    remote = {(0, shift): from_rep(first_rows, shift) for shift in range(1, n_rep)}
 
     def spread_panels(panels, order, bits):
         for bit in bits:
@@ -275,7 +299,8 @@
         return panels, order
 
     bits = [n_tensor >> at for at in range(1, n_tensor.bit_length())]
-    panels, order = spread_panels([up_b], [0], bits[:1])
+    order = [0] + [at for at in range(1, n_tensor) if at % (n_tensor // 4) == 0]
+    panels = [up_b] + [swap_tensor(up_b, at) for at in order[1:]]
     my_ids = lax.dynamic_slice_in_dim(adapter_ids, tensor_index * rows_mine, rows_mine)
     iota = lax.broadcasted_iota(jnp.int32, (rows_mine, slot_count), 1)
     my_slot = jnp.sum((my_ids == iota).astype(jnp.int32) * owner_map[None, :], axis=1)
@@ -299,7 +324,7 @@
             bit //= 2
         return total.reshape(steps, extent, columns)
 
-    def gap(token, jobs, *extra, short=False):
+    def gap(token, jobs, *extra):
         nonlocal first_leg, second_leg
         for parts, received, keep, kind in first_leg:
             steps = sum(length for _, length in parts)
@@ -310,8 +335,8 @@
                     if (key[0] + at - begin, key[1]) == (step_count - 1, 0):
                         halved[RANK_NAME, 0] = total[at][:, width:]
                 begin += length
-        closed, waiting = {}, second_leg if short else []
-        for name, kept, received in [] if short else second_leg:
+        closed = {}
+        for name, kept, received in second_leg:
             closed[name] = (after(kept, token), *received)
         started, sends = [], []
         for name in sorted({name for name, _ in halved}):
@@ -331,16 +356,15 @@
         first_leg = [
             (parts, swap_tensor(send, group // 2), keep, kind) for (parts, _, keep, kind), send in zip(jobs, first_sends)
         ]
-        second_leg = waiting + [
+        second_leg = [
             (name, kept, [to_group(value, hop + 1) for hop, value in enumerate(sent)])
             for (name, kept), sent in zip(started, sends)
         ]
-        return extra
+        return extra if extra else [sent for sent in sends]
 
     factors = jnp.swapaxes(down_a, 1, 2)
 
     half = step_count // 2
-    source = pltpu.with_memory_space_constraint(hidden, pltpu.HBM)
     jobs, next_local, last_ranks = [([((0, 0), half)], *partial_products(
         pos, [(source, siblings, 0, half)], base_weight, factors, emitted=half - 1
     ))], half, {}
@@ -352,10 +376,8 @@
                 remote[next_local - 1, along] = from_rep(emitted[0], along)
         own, siblings, panels = gap(send, jobs, remote[step, shift], siblings, panels)
         if piece == 0:
-            panels, order = spread_panels(panels, order, bits[1:])
+            panels, order = spread_panels(panels, order, bits[2:])
         sib = swap_cores(own)
-        if piece == len(pieces) - 1:
-            own, sib = gap(send, [], own, sib, short=True)
         last, chunks, parts, place = step == step_count - 1, [(own, sib, 0, 1)], [((step, shift), 1)], None
         if next_local < step_count:
             chunks.insert(0, (source, siblings, next_local, 1))
@@ -374,6 +396,8 @@
     ended[RANK_NAME] = (pick(values, (group_index - rep_index) % n_rep), *[
         to_group(pick(values, (group_index + hop - rep_index) % n_rep), hop) for hop in range(1, n_rep)
     ])
+    rounded = gap(send, [])
+
     def rank_sum(name):
         kept, *received = [value[:, -rank_columns(factors):] for value in ended[name]]
         for value in received:
@@ -382,7 +406,7 @@
 
     finished = jnp.stack([rank_sum(step) for step in range(step_count - 1)] + [rank_sum(RANK_NAME)])
     finished = finished.astype(jnp.bfloat16).reshape(step_count, rows_mine, owned_slots, rank_size)
-    finished, = gap(send, [], finished)
+    finished = lax.optimization_barrier((finished, rounded))[0]
     ended.update((name, (kept, *received)) for name, kept, received in second_leg)
     masked = jnp.sum(
         jnp.where(owned_hot[None, :, :, None], finished, 0), axis=2, dtype=jnp.float32

time: 163 us -> 191 us (1.17)
  local copies, waits for them, and re-layouts: 10.3 us -> 46.3 us
  waiting for transfers between devices: 48 us -> 24.2 us
  Pallas kernels: 70.4 us -> 86.8 us
    unnamed x48 -> x54, local copies, waits for them, and re-layouts: 7.22 us -> 45.4 us
    ppermute x9, waiting for transfers between devices: 20.5 us -> 0.02 us  [swap_tensor(): return lax.ppermute(value, 'tp', [(i, i ^ bit) for i in range(n_tensor)])]
    pallas_call x5, Pallas kernels: 67.1 us -> 81.2 us  [partial_products(): pl.pallas_call(functools.partial(matmul_body, spans, emitted, apart), in_...]
    ppermute x4, waiting for transfers between devices: 6.94 us -> 0.18 us  [from_rep(): lax.ppermute(value, 'rep', [((i + shift) % n_rep, i) for i in range(n_rep)])]
    slice x1 -> x0, local copies, waits for them, and re-layouts: 2.16 us -> none  [per_device(): hidden[:1]]
    pallas_call x0 -> x1, Pallas kernels: none -> 2.11 us  [cut_first(): pl.pallas_call(cut_body, in_specs=[pl.BlockSpec(memory_space=pl.ANY)], ou...]
    ppermute x3, waiting for transfers between devices: 1.82 us -> 3.81 us  [per_device(): lax.ppermute(masked, ('rep', 'sub'), [(i, (i + turn) % n_owners) for i in...]
  transfers between devices with their start and end apart: 26 -> 26, of which waited for: 12 -> 5; matrix products, arithmetic and copies ran while one was open for 6% -> 4% of each run, Pallas kernels for 43% -> 45%
where the time goes in v8:
time: 191 us; the launch traced here: 190 us
  Pallas kernels  86.8 us (45%)
  local copies, waits for them, and re-layouts  46.3 us (24%)
  starting transfers between devices  25.4 us (13%)
  waiting for transfers between devices  24.2 us (13%)
  other arithmetic  7.11 us (4%)
    pallas_call x5, Pallas kernels, partial_products(): pl.pallas_call(functools.partial(matmul_body, spans, emitted, apart), in_...  81.2 us
    unnamed x54, local copies, waits for them, and re-layouts  45.4 us
    ppermute x5, waiting for transfers between devices, to_group(): lax.ppermute(value, 'tp', [(i, (i + moved) % n_tensor) for i in range(n_t...  20.2 us
    ppermute x9, starting transfers between devices, swap_tensor(): return lax.ppermute(value, 'tp', [(i, i ^ bit) for i in range(n_tensor)])  11.4 us
    ppermute x5, starting transfers between devices, to_group(): lax.ppermute(value, 'tp', [(i, (i + moved) % n_tensor) for i in range(n_t...  7.66 us
    ppermute x4, starting transfers between devices, from_rep(): lax.ppermute(value, 'rep', [((i + shift) % n_rep, i) for i in range(n_rep)])  4.24 us
  transfers between devices with their start and end apart: 26, of which 5 were waited for; matrix products, arithmetic and copies ran while one was open for 4% of the time, Pallas kernels for 45%

profile of v8, /device:TPU:0, one launch (start us, length us, event | category | flops | bytes accessed | tf_op | source)
XLA Modules:
  0.0 190.2 jit_solution(2378074798892497972)
XLA Ops:
  0.5 2.1 %cut_first.1 = bf16[1,64,7168]{2,1,0:T(8,128)(2,1)} custom-call(bf16[4,64,7168]{2,1,0:T(8,128)(2,1)} %refs_0_.5), custom_call_target="tpu_custom_call" | custom-call | tf_op jit(solution)/shard_map/cut_first/pallas_call | solution.py:155
  2.6 2.7 %collective-permute-start.1 = (bf16[1,64,7168]{2,1,0:T(8,128)(2,1)}, bf16[1,64,7168]{2,1,0:T(8,128)(2,1)S(1)}, u32[]{:S(2)}, u32[]{:S(2)}) collective-permute-start(bf16[1,64,7168]{2,1,0:T(8,128)(2,1)} %cut_first.1), channel_id=1, source_target_pairs={{2,0},{0,2},{3,1},{1,3},{6,4},{4,6},{7,5},{5,7},{10,8},{8,10},{11,... | collective-permute-start | bytes 2752520 | tf_op jit(solution)/shard_map/ppermute | solution.py:271
  5.3 2.6 %collective-permute-start.3 = (bf16[1,64,2048]{2,1,0:T(8,128)(2,1)S(1)}, bf16[1,64,2048]{2,1,0:T(8,128)(2,1)S(1)}, u32[]{:S(2)}, u32[]{:S(2)}) collective-permute-start(bf16[1,64,2048]{2,1,0:T(8,128)(2,1)S(1)} %copy-done.11), channel_id=1, source_target_pairs={{0,8},{4,12},{8,0},{12,4},{1,9},{5,13},{9,1},{13,5},{2,10},{6,14},... | collective-permute-start | bytes 786440 | tf_op jit(solution)/shard_map/ppermute | solution.py:274
  7.9 1.6 collective-permute-start.2
  9.7 9.4 %copy-done.1 = bf16[7168,2048]{1,0:T(8,128)(2,1)S(1)} copy-done((bf16[7168,2048]{1,0:T(8,128)(2,1)S(1)}, bf16[7168,2048]{1,0:T(8,128)(2,1)}, u32[]{:S(2)}) %copy-start.1) | copy-done | bytes 29360152
  19.0 18.6 %partial_products.5 = (bf16[128,2176]{1,0:T(8,128)(2,1)}, f32[128,2176]{1,0:T(8,128)S(1)}, bf16[1,64,7168]{2,1,0:T(8,128)(2,1)S(1)}) custom-call(s32[1]{0:T(128)} %bitcast.1.pos_ref, bf16[4,64,7168]{2,1,0:T(8,128)(2,1)} %refs_0_.5, bf16[4,64,7168]{2,1,0:T(8,128)(2,1)} %collective-permute-done.refs_1_, bf16[7168,2048]{1,0:T(8,128)(2,1)S(1)} %copy-done.1, ...), custom_call_target="tpu_custom_call" | custom-call | tf_op jit(solution)/shard_map/partial_products/pallas_call | solution.py:130
  39.7 1.5 collective-permute-start.9
  41.2 1.2 copy-done.7
  42.4 18.0 %partial_products.6 = (bf16[128,2176]{1,0:T(8,128)(2,1)S(1)}, f32[128,2176]{1,0:T(8,128)S(1)}, bf16[1,64,7168]{2,1,0:T(8,128)(2,1)S(1)}) custom-call(s32[1]{0:T(128)} %bitcast.1.pos_ref, bf16[4,64,7168]{2,1,0:T(8,128)(2,1)} %refs_0_.5, bf16[4,64,7168]{2,1,0:T(8,128)(2,1)} %collective-permute-done.refs_1_, bf16[1,64,7168]{2,1,0:T(8,128)(2,1)S(1)} %copy-done.7, ...), custom_call_target="tpu_custom_call" | custom-call | tf_op jit(solution)/shard_map/partial_products/pallas_call | solution.py:130
  63.0 1.4 collective-permute-start.8
  64.4 1.2 convert_add_fusion.1
  65.6 9.7 %copy-done.2 = bf16[7168,2048]{1,0:T(8,128)(2,1)S(1)} copy-done((bf16[7168,2048]{1,0:T(8,128)(2,1)S(1)}, bf16[7168,2048]{1,0:T(8,128)(2,1)}, u32[]{:S(2)}) %copy-start.2) | copy-done | bytes 29360152
  75.3 18.6 %partial_products.7 = (bf16[128,2176]{1,0:T(8,128)(2,1)}, f32[128,2176]{1,0:T(8,128)S(1)}, bf16[1,64,7168]{2,1,0:T(8,128)(2,1)S(1)}) custom-call(s32[1]{0:T(128)} %bitcast.1.pos_ref, bf16[4,64,7168]{2,1,0:T(8,128)(2,1)} %refs_0_.5, bf16[4,64,7168]{2,1,0:T(8,128)(2,1)} %collective-permute-done.refs_1_, bf16[1,64,7168]{2,1,0:T(8,128)(2,1)} %collective-permute-done.6.refs_2_, ...), custom_call_target="tpu_custom_call" | custom-call | tf_op jit(solution)/shard_map/partial_products/pallas_call | solution.py:130
  94.9 0.9 select_convert_fusion.2
  96.7 3.5 %collective-permute-start.14 = (bf16[64,2176]{1,0:T(8,128)(2,1)}, bf16[64,2176]{1,0:T(8,128)(2,1)S(1)}, u32[]{:S(2)}, u32[]{:S(2)}) collective-permute-start(bf16[64,2176]{1,0:T(8,128)(2,1)} %select_convert_fusion.2), channel_id=1, source_target_pairs={{0,8},{4,12},{8,0},{12,4},{1,9},{5,13},{9,1},{13,5},{2,10},{6,14},... | collective-permute-start | bytes 835592 | tf_op jit(solution)/shard_map/ppermute | solution.py:278
  100.7 9.3 %copy-done.3 = bf16[7168,2048]{1,0:T(8,128)(2,1)S(1)} copy-done((bf16[7168,2048]{1,0:T(8,128)(2,1)S(1)}, bf16[7168,2048]{1,0:T(8,128)(2,1)}, u32[]{:S(2)}) %copy-start.3) | copy-done | bytes 29360152
  110.0 12.9 %partial_products.8 = (bf16[64,2176]{1,0:T(8,128)(2,1)S(1)}, f32[64,2176]{1,0:T(8,128)S(1)}) custom-call(s32[1]{0:T(128)} %bitcast.1.pos_ref, bf16[1,64,7168]{2,1,0:T(8,128)(2,1)} %collective-permute-done.10.refs_0_, bf16[1,64,7168]{2,1,0:T(8,128)(2,1)} %collective-permute-done.11.refs_1_, bf16[7168,2048]{1,0:T(8,128)(2,1)S(1)} %copy-done.3, ...), custom_call_target="tpu_custom_call" | custom-call | tf_op jit(solution)/shard_map/partial_products/pallas_call | solution.py:130
  123.0 1.3 convert_add_fusion
  127.5 1.4 collective-permute-start.16
  129.8 1.1 collective-permute-start.17
  130.9 9.3 %copy-done.4 = bf16[7168,2048]{1,0:T(8,128)(2,1)S(1)} copy-done((bf16[7168,2048]{1,0:T(8,128)(2,1)S(1)}, bf16[7168,2048]{1,0:T(8,128)(2,1)}, u32[]{:S(2)}) %copy-start.4) | copy-done | bytes 29360152
  140.2 13.1 %partial_products.9 = (bf16[64,2048]{1,0:T(8,128)(2,1)S(1)}, f32[64,2048]{1,0:T(8,128)S(1)}, f32[64,128]{1,0:T(8,128)S(1)}, f32[64,128]{1,0:T(8,128)S(1)}) custom-call(s32[1]{0:T(128)} %bitcast.1.pos_ref, bf16[1,64,7168]{2,1,0:T(8,128)(2,1)S(1)} %collective-permute-done.13.refs_0_, bf16[1,64,7168]{2,1,0:T(8,128)(2,1)} %collective-permute-done.15.refs_1_, ...), custom_call_target="tpu_custom_call" | custom-call | tf_op jit(solution)/shard_map/partial_products/pallas_call | solution.py:130
  153.4 1.1 select_convert_fusion
  155.0 1.5 collective-permute-start.18
  156.6 1.9 %collective-permute-start.19 = (bf16[64,2176]{1,0:T(8,128)(2,1)S(1)}, bf16[64,2176]{1,0:T(8,128)(2,1)S(1)}, u32[]{:S(2)}, u32[]{:S(2)}) collective-permute-start(bf16[64,2176]{1,0:T(8,128)(2,1)S(1)} %select_convert_fusion), channel_id=1, source_target_pairs={{0,8},{4,12},{8,0},{12,4},{1,9},{5,13},{9,1},{13,5},{2,10},{6,14},... | collective-permute-start | bytes 835592 | tf_op jit(solution)/shard_map/ppermute | solution.py:278
  158.5 1.1 slice_select_fusion.refs_8_
  159.7 1.2 collective-permute-start.21
  160.8 11.9 %collective-permute-done.21 = f32[64,128]{1,0:T(8,128)S(1)} collective-permute-done((f32[64,128]{1,0:T(8,128)S(1)}, f32[64,128]{1,0:T(8,128)S(1)}, u32[]{:S(2)}, u32[]{:S(2)}) %collective-permute-start.21) | collective-permute-done | bytes 32800 | tf_op jit(solution)/shard_map/ppermute | solution.py:278
  173.0 1.0 collective-permute-start.23
  174.5 3.2 %collective-permute-done.23 = bf16[4,64,64]{2,1,0:T(8,128)(2,1)S(1)} collective-permute-done((bf16[4,64,64]{2,1,0:T(8,128)(2,1)S(1)}, bf16[4,64,64]{2,1,0:T(8,128)(2,1)S(1)}, u32[]{:S(2)}, u32[]{:S(2)}) %collective-permute-start.23) | collective-permute-done | bytes 32800 | tf_op jit(solution)/shard_map/ppermute | solution.py:416
  178.5 2.6 %finish_steps.1 = (bf16[4,64,2048]{2,1,0:T(8,128)(2,1)}, bf16[64,2048]{1,0:T(8,128)(2,1)S(1)}) custom-call(bf16[256,64]{1,0:T(8,128)(2,1)S(1)} %bitcast.30, s32[256,1]{1,0:T(8,128)S(1)} %copy-done.8, s32[4]{0:T(128)S(1)} %pad_add_fusion.order_ref, bf16[64,2048]{1,0:T(8,128)(2,1)S(1)} %bitcast.31, bf16[64,2048]{1,0:T(8,128)(2,1)} %bitcast.14.refs_1_, ...), custom_call_target="tpu_custom_call" | custom-call | tf_op jit(solution)/shard_map/finish_steps/pallas_call | solution.py:203
  181.1 8.3 %collective-permute-done.25.refs_1_ = bf16[64,2048]{1,0:T(8,128)(2,1)S(1)} collective-permute-done((bf16[64,2048]{1,0:T(8,128)(2,1)S(1)}, bf16[64,2048]{1,0:T(8,128)(2,1)S(1)}, u32[]{:S(2)}, u32[]{:S(2)}) %collective-permute-start.25) | collective-permute-done | bytes 262176 | tf_op jit(solution)/shard_map/ppermute | solution.py:278
  (112 shorter events, 14.7 us)
Async XLA Ops:
  0.0 127.3 %copy-start = (s32[256,1]{0,1:T(1,128)S(1)}, s32[256,1]{0,1:T(1,128)}, u32[]{:S(2)}) copy-start(s32[256,1]{0,1:T(1,128)} %param.10) | copy-start | bytes 3076
  0.0 9.7 %copy-start.5 = (bf16[1,7168,64]{1,2,0:T(8,128)(2,1)S(1)}, bf16[1,7168,64]{1,2,0:T(8,128)(2,1)}, u32[]{:S(2)}) copy-start(bf16[1,7168,64]{1,2,0:T(8,128)(2,1)} %param.8) | copy-start | bytes 2752516
  0.0 9.7 %collective-permute-start = (bf16[4,64,7168]{2,1,0:T(8,128)(2,1)}, bf16[4,64,7168]{2,1,0:T(8,128)(2,1)}, u32[]{:S(2)}, u32[]{:S(2)}) collective-permute-start(bf16[4,64,7168]{2,1,0:T(8,128)(2,1)} %refs_0_.5), channel_id=1, source_target_pairs={{0,1},{1,0},{2,3},{3,2},{4,5},{5,4},{6,7},{7,6},{8,9},{9,8},{10,11... | collective-permute-start | bytes 11010056 | tf_op jit(solution)/shard_map/ppermute | solution.py:268
  2.6 35.8 %collective-permute-start.1 = (bf16[1,64,7168]{2,1,0:T(8,128)(2,1)}, bf16[1,64,7168]{2,1,0:T(8,128)(2,1)S(1)}, u32[]{:S(2)}, u32[]{:S(2)}) collective-permute-start(bf16[1,64,7168]{2,1,0:T(8,128)(2,1)} %cut_first.1), channel_id=1, source_target_pairs={{2,0},{0,2},{3,1},{1,3},{6,4},{4,6},{7,5},{5,7},{10,8},{8,10},{11,... | collective-permute-start | bytes 2752520 | tf_op jit(solution)/shard_map/ppermute | solution.py:271
  5.3 32.4 %collective-permute-start.3 = (bf16[1,64,2048]{2,1,0:T(8,128)(2,1)S(1)}, bf16[1,64,2048]{2,1,0:T(8,128)(2,1)S(1)}, u32[]{:S(2)}, u32[]{:S(2)}) collective-permute-start(bf16[1,64,2048]{2,1,0:T(8,128)(2,1)S(1)} %copy-done.11), channel_id=1, source_target_pairs={{0,8},{4,12},{8,0},{12,4},{1,9},{5,13},{9,1},{13,5},{2,10},{6,14},... | collective-permute-start | bytes 786440 | tf_op jit(solution)/shard_map/ppermute | solution.py:274
  7.9 30.5 %collective-permute-start.2 = (bf16[1,64,2048]{2,1,0:T(8,128)(2,1)S(1)}, bf16[1,64,2048]{2,1,0:T(8,128)(2,1)}, u32[]{:S(2)}, u32[]{:S(2)}) collective-permute-start(bf16[1,64,2048]{2,1,0:T(8,128)(2,1)S(1)} %copy-done.11), channel_id=1, source_target_pairs={{0,4},{4,0},{8,12},{12,8},{1,5},{5,1},{9,13},{13,9},{2,6},{6,2},{1... | collective-permute-start | bytes 786440 | tf_op jit(solution)/shard_map/ppermute | solution.py:274
  9.5 28.9 %collective-permute-start.4 = (bf16[1,64,2048]{2,1,0:T(8,128)(2,1)S(1)}, bf16[1,64,2048]{2,1,0:T(8,128)(2,1)}, u32[]{:S(2)}, u32[]{:S(2)}) collective-permute-start(bf16[1,64,2048]{2,1,0:T(8,128)(2,1)S(1)} %copy-done.11), channel_id=1, source_target_pairs={{0,12},{4,8},{8,4},{12,0},{1,13},{5,9},{9,5},{13,1},{2,14},{6,10},... | collective-permute-start | bytes 786440 | tf_op jit(solution)/shard_map/ppermute | solution.py:274
  9.7 9.4 %copy-start.1 = (bf16[7168,2048]{1,0:T(8,128)(2,1)S(1)}, bf16[7168,2048]{1,0:T(8,128)(2,1)}, u32[]{:S(2)}) copy-start(bf16[7168,2048]{1,0:T(8,128)(2,1)} %refs_2_.5) | copy-start | bytes 88080384
  38.4 2.8 %collective-permute-start.5 = (bf16[1,64,7168]{2,1,0:T(8,128)(2,1)S(1)}, bf16[1,64,7168]{2,1,0:T(8,128)(2,1)S(1)}, u32[]{:S(2)}, u32[]{:S(2)}) collective-permute-start(bf16[1,64,7168]{2,1,0:T(8,128)(2,1)S(1)} %collective-permute-done.1.refs_2_), channel_id=1, source_target_pairs={{0,1},{1,0},{2,3},{3,2},{4,5},{5,4},{6,7},{7,6},{8,9},{9,8},{10,11... | collective-permute-start | bytes 2752520 | tf_op jit(solution)/shard_map/ppermute | solution.py:268
  39.4 22.9 %collective-permute-start.6 = (bf16[1,64,7168]{2,1,0:T(8,128)(2,1)S(1)}, bf16[1,64,7168]{2,1,0:T(8,128)(2,1)}, u32[]{:S(2)}, u32[]{:S(2)}) collective-permute-start(bf16[1,64,7168]{2,1,0:T(8,128)(2,1)S(1)} %get-tuple-element.74), channel_id=1, source_target_pairs={{2,0},{0,2},{3,1},{1,3},{6,4},{4,6},{7,5},{5,7},{10,8},{8,10},{11,... | collective-permute-start | bytes 2752520 | tf_op jit(solution)/shard_map/ppermute | solution.py:271
  39.7 24.6 %collective-permute-start.9 = (bf16[128,2176]{1,0:T(8,128)(2,1)}, bf16[128,2176]{1,0:T(8,128)(2,1)}, u32[]{:S(2)}, u32[]{:S(2)}) collective-permute-start(bf16[128,2176]{1,0:T(8,128)(2,1)} %get-tuple-element.87), channel_id=1, source_target_pairs={{0,4},{4,0},{8,12},{12,8},{1,5},{5,1},{9,13},{13,9},{2,6},{6,2},{1... | collective-permute-start | bytes 1671176 | tf_op jit(solution)/shard_map/ppermute | solution.py:274
  62.3 3.3 %collective-permute-start.7 = (bf16[1,64,7168]{2,1,0:T(8,128)(2,1)}, bf16[1,64,7168]{2,1,0:T(8,128)(2,1)}, u32[]{:S(2)}, u32[]{:S(2)}) collective-permute-start(bf16[1,64,7168]{2,1,0:T(8,128)(2,1)} %collective-permute-done.6.refs_2_), channel_id=1, source_target_pairs={{0,1},{1,0},{2,3},{3,2},{4,5},{5,4},{6,7},{7,6},{8,9},{9,8},{10,11... | collective-permute-start | bytes 2752520 | tf_op jit(solution)/shard_map/ppermute | solution.py:268
  62.3 33.7 %collective-permute-start.10 = (bf16[1,64,7168]{2,1,0:T(8,128)(2,1)}, bf16[1,64,7168]{2,1,0:T(8,128)(2,1)}, u32[]{:S(2)}, u32[]{:S(2)}) collective-permute-start(bf16[1,64,7168]{2,1,0:T(8,128)(2,1)} %copy-done.15), channel_id=1, source_target_pairs={{2,0},{0,2},{3,1},{1,3},{6,4},{4,6},{7,5},{5,7},{10,8},{8,10},{11,... | collective-permute-start | bytes 2752520 | tf_op jit(solution)/shard_map/ppermute | solution.py:271
  63.0 30.9 %collective-permute-start.8 = (bf16[128,2176]{1,0:T(8,128)(2,1)}, bf16[128,2176]{1,0:T(8,128)(2,1)S(1)}, u32[]{:S(2)}, u32[]{:S(2)}) collective-permute-start(bf16[128,2176]{1,0:T(8,128)(2,1)} %copy-done.17), channel_id=1, source_target_pairs={{0,4},{4,0},{8,12},{12,8},{1,5},{5,1},{9,13},{13,9},{2,6},{6,2},{1... | collective-permute-start | bytes 1671176 | tf_op jit(solution)/shard_map/ppermute | solution.py:274
  65.5 28.5 %copy-start.22 = (f32[128,2176]{1,0:T(8,128)}, f32[128,2176]{1,0:T(8,128)S(1)}, u32[]{:S(2)}) copy-start(f32[128,2176]{1,0:T(8,128)S(1)} %convert_add_fusion.1) | copy-start | bytes 3342340
  65.6 9.8 %copy-start.2 = (bf16[7168,2048]{1,0:T(8,128)(2,1)S(1)}, bf16[7168,2048]{1,0:T(8,128)(2,1)}, u32[]{:S(2)}) copy-start(bf16[7168,2048]{1,0:T(8,128)(2,1)} %refs_2_.5) | copy-start | bytes 88080384
  96.0 4.7 %collective-permute-start.11 = (bf16[1,64,7168]{2,1,0:T(8,128)(2,1)}, bf16[1,64,7168]{2,1,0:T(8,128)(2,1)}, u32[]{:S(2)}, u32[]{:S(2)}) collective-permute-start(bf16[1,64,7168]{2,1,0:T(8,128)(2,1)} %collective-permute-done.10.refs_0_), channel_id=1, source_target_pairs={{0,1},{1,0},{2,3},{3,2},{4,5},{5,4},{6,7},{7,6},{8,9},{9,8},{10,11... | collective-permute-start | bytes 2752520 | tf_op jit(solution)/shard_map/ppermute | solution.py:268
  96.0 27.0 %collective-permute-start.12 = (bf16[128,2176]{1,0:T(8,128)(2,1)}, bf16[128,2176]{1,0:T(8,128)(2,1)}, u32[]{:S(2)}, u32[]{:S(2)}) collective-permute-start(bf16[128,2176]{1,0:T(8,128)(2,1)} %get-tuple-element.97), channel_id=1, source_target_pairs={{0,4},{4,0},{8,12},{12,8},{1,5},{5,1},{9,13},{13,9},{2,6},{6,2},{1... | collective-permute-start | bytes 1671176 | tf_op jit(solution)/shard_map/ppermute | solution.py:274
  96.7 29.9 %collective-permute-start.14 = (bf16[64,2176]{1,0:T(8,128)(2,1)}, bf16[64,2176]{1,0:T(8,128)(2,1)S(1)}, u32[]{:S(2)}, u32[]{:S(2)}) collective-permute-start(bf16[64,2176]{1,0:T(8,128)(2,1)} %select_convert_fusion.2), channel_id=1, source_target_pairs={{0,8},{4,12},{8,0},{12,4},{1,9},{5,13},{9,1},{13,5},{2,10},{6,14},... | collective-permute-start | bytes 835592 | tf_op jit(solution)/shard_map/ppermute | solution.py:278
  100.1 26.4 %collective-permute-start.13 = (bf16[1,64,7168]{2,1,0:T(8,128)(2,1)}, bf16[1,64,7168]{2,1,0:T(8,128)(2,1)S(1)}, u32[]{:S(2)}, u32[]{:S(2)}) collective-permute-start(bf16[1,64,7168]{2,1,0:T(8,128)(2,1)} %copy-done.16), channel_id=1, source_target_pairs={{2,0},{0,2},{3,1},{1,3},{6,4},{4,6},{7,5},{5,7},{10,8},{8,10},{11,... | collective-permute-start | bytes 2752520 | tf_op jit(solution)/shard_map/ppermute | solution.py:271
  127.3 3.5 %collective-permute-start.15 = (bf16[1,64,7168]{2,1,0:T(8,128)(2,1)S(1)}, bf16[1,64,7168]{2,1,0:T(8,128)(2,1)}, u32[]{:S(2)}, u32[]{:S(2)}) collective-permute-start(bf16[1,64,7168]{2,1,0:T(8,128)(2,1)S(1)} %collective-permute-done.13.refs_0_), channel_id=1, source_target_pairs={{0,1},{1,0},{2,3},{3,2},{4,5},{5,4},{6,7},{7,6},{8,9},{9,8},{10,11... | collective-permute-start | bytes 2752520 | tf_op jit(solution)/shard_map/ppermute | solution.py:268
  127.5 25.9 %collective-permute-start.16 = (bf16[64,2176]{1,0:T(8,128)(2,1)}, bf16[64,2176]{1,0:T(8,128)(2,1)}, u32[]{:S(2)}, u32[]{:S(2)}) collective-permute-start(bf16[64,2176]{1,0:T(8,128)(2,1)} %copy-done.18), channel_id=1, source_target_pairs={{0,4},{4,0},{8,12},{12,8},{1,5},{5,1},{9,13},{13,9},{2,6},{6,2},{1... | collective-permute-start | bytes 835592 | tf_op jit(solution)/shard_map/ppermute | solution.py:274
  129.8 24.7 %collective-permute-start.17 = (bf16[64,2176]{1,0:T(8,128)(2,1)}, bf16[64,2176]{1,0:T(8,128)(2,1)S(1)}, u32[]{:S(2)}, u32[]{:S(2)}) collective-permute-start(bf16[64,2176]{1,0:T(8,128)(2,1)} %select_convert_fusion.1), channel_id=1, source_target_pairs={{0,8},{4,12},{8,0},{12,4},{1,9},{5,13},{9,1},{13,5},{2,10},{6,14},... | collective-permute-start | bytes 835592 | tf_op jit(solution)/shard_map/ppermute | solution.py:278
  140.2 13.2 %copy-start.21 = (f32[128,2176]{1,0:T(8,128)S(1)}, f32[128,2176]{1,0:T(8,128)}, u32[]{:S(2)}) copy-start(f32[128,2176]{1,0:T(8,128)} %copy-done.19) | copy-start | bytes 3342340
  154.5 5.1 %collective-permute-start.20 = (f32[64,128]{1,0:T(8,128)S(1)}, f32[64,128]{1,0:T(8,128)S(1)}, u32[]{:S(2)}, u32[]{:S(2)}) collective-permute-start(f32[64,128]{1,0:T(8,128)S(1)} %get-tuple-element.126), channel_id=1, source_target_pairs={{0,4},{4,0},{8,12},{12,8},{1,5},{5,1},{9,13},{13,9},{2,6},{6,2},{1... | collective-permute-start | bytes 98312 | tf_op jit(solution)/shard_map/ppermute | solution.py:274
  155.0 17.7 %collective-permute-start.18 = (bf16[64,2048]{1,0:T(8,128)(2,1)S(1)}, bf16[64,2048]{1,0:T(8,128)(2,1)S(1)}, u32[]{:S(2)}, u32[]{:S(2)}) collective-permute-start(bf16[64,2048]{1,0:T(8,128)(2,1)S(1)} %get-tuple-element.120), channel_id=1, source_target_pairs={{0,4},{4,0},{8,12},{12,8},{1,5},{5,1},{9,13},{13,9},{2,6},{6,2},{1... | collective-permute-start | bytes 786440 | tf_op jit(solution)/shard_map/ppermute | solution.py:274
  156.6 16.2 %collective-permute-start.19 = (bf16[64,2176]{1,0:T(8,128)(2,1)S(1)}, bf16[64,2176]{1,0:T(8,128)(2,1)S(1)}, u32[]{:S(2)}, u32[]{:S(2)}) collective-permute-start(bf16[64,2176]{1,0:T(8,128)(2,1)S(1)} %select_convert_fusion), channel_id=1, source_target_pairs={{0,8},{4,12},{8,0},{12,4},{1,9},{5,13},{9,1},{13,5},{2,10},{6,14},... | collective-permute-start | bytes 835592 | tf_op jit(solution)/shard_map/ppermute | solution.py:278
  159.7 13.1 %collective-permute-start.21 = (f32[64,128]{1,0:T(8,128)S(1)}, f32[64,128]{1,0:T(8,128)S(1)}, u32[]{:S(2)}, u32[]{:S(2)}) collective-permute-start(f32[64,128]{1,0:T(8,128)S(1)} %get-tuple-element.135), channel_id=1, source_target_pairs={{0,8},{4,12},{8,0},{12,4},{1,9},{5,13},{9,1},{13,5},{2,10},{6,14},... | collective-permute-start | bytes 98312 | tf_op jit(solution)/shard_map/ppermute | solution.py:278
  173.0 4.7 %collective-permute-start.23 = (bf16[4,64,64]{2,1,0:T(8,128)(2,1)S(1)}, bf16[4,64,64]{2,1,0:T(8,128)(2,1)S(1)}, u32[]{:S(2)}, u32[]{:S(2)}) collective-permute-start(bf16[4,64,64]{2,1,0:T(8,128)(2,1)S(1)} %select_bitcast_fusion), channel_id=1, source_target_pairs={{0,2},{1,3},{2,0},{3,1},{4,6},{5,7},{6,4},{7,5},{8,10},{9,11},{10,... | collective-permute-start | bytes 98312 | tf_op jit(solution)/shard_map/ppermute | solution.py:416
  174.0 3.8 %collective-permute-start.24 = (bf16[4,64,64]{2,1,0:T(8,128)(2,1)S(1)}, bf16[4,64,64]{2,1,0:T(8,128)(2,1)S(1)}, u32[]{:S(2)}, u32[]{:S(2)}) collective-permute-start(bf16[4,64,64]{2,1,0:T(8,128)(2,1)S(1)} %select_bitcast_fusion), channel_id=1, source_target_pairs={{0,3},{1,0},{2,1},{3,2},{4,7},{5,4},{6,5},{7,6},{8,11},{9,8},{10,9... | collective-permute-start | bytes 98312 | tf_op jit(solution)/shard_map/ppermute | solution.py:416
  174.0 4.4 %collective-permute-start.22 = (bf16[4,64,64]{2,1,0:T(8,128)(2,1)S(1)}, bf16[4,64,64]{2,1,0:T(8,128)(2,1)S(1)}, u32[]{:S(2)}, u32[]{:S(2)}) collective-permute-start(bf16[4,64,64]{2,1,0:T(8,128)(2,1)S(1)} %select_bitcast_fusion), channel_id=1, source_target_pairs={{0,1},{1,2},{2,3},{3,0},{4,5},{5,6},{6,7},{7,4},{8,9},{9,10},{10,1... | collective-permute-start | bytes 98312 | tf_op jit(solution)/shard_map/ppermute | solution.py:416
  174.5 14.9 %collective-permute-start.25 = (bf16[64,2048]{1,0:T(8,128)(2,1)S(1)}, bf16[64,2048]{1,0:T(8,128)(2,1)S(1)}, u32[]{:S(2)}, u32[]{:S(2)}) collective-permute-start(bf16[64,2048]{1,0:T(8,128)(2,1)S(1)} %select_convert_fusion.3), channel_id=1, source_target_pairs={{0,8},{4,12},{8,0},{12,4},{1,9},{5,13},{9,1},{13,5},{2,10},{6,14},... | collective-permute-start | bytes 786440 | tf_op jit(solution)/shard_map/ppermute | solution.py:278
  (22 other events, 73.0 us)

commit v9 on v8

--- a/solution.py
+++ b/solution.py
@@ -145,24 +145,6 @@
     )(pos, *[source for own, sib, _, _ in chunks for source in (own, sib)], weight, factors)
 
 
-def cut_body(source_ref, out_ref, sem):
-    copy = pltpu.make_async_copy(source_ref.at[pl.ds(0, 1)], out_ref, sem)
-    copy.start()
-    copy.wait()
-
-
-def cut_first(hidden):
-    return pl.pallas_call(
-        cut_body,
-        in_specs=[pl.BlockSpec(memory_space=pl.ANY)],
-        out_specs=pl.BlockSpec(memory_space=pltpu.VMEM),
-        out_shape=jax.ShapeDtypeStruct((1,) + hidden.shape[1:], hidden.dtype),
-        scratch_shapes=[pltpu.SemaphoreType.DMA],
-        cost_estimate=pl.CostEstimate(flops=0, bytes_accessed=0, transcendentals=0),
-        name="cut_first",
-    )(hidden)
-
-
 def finish_body(received, panels, chosen_ref, slot_ref, order_ref, *refs):
     panel_refs, refs = refs[:panels], refs[panels:]
     per_panel = panel_refs[0].shape[0]
@@ -289,8 +271,8 @@
     siblings = swap_cores(hidden)
     pieces = [(step, shift) for step in range(step_count) for shift in range(1, n_rep)]
     source = pltpu.with_memory_space_constraint(hidden, pltpu.HBM)
-    first_rows = cut_first(source)
-    remote = {(0, shift): from_rep(first_rows, shift) for shift in range(1, n_rep)}
+    weight = pltpu.with_memory_space_constraint(base_weight, pltpu.HBM)
+    remote = {(0, shift): from_rep(hidden[:1], shift) for shift in range(1, n_rep)}
 
     def spread_panels(panels, order, bits):
         for bit in bits:
@@ -366,7 +348,7 @@
 
     half = step_count // 2
     jobs, next_local, last_ranks = [([((0, 0), half)], *partial_products(
-        pos, [(source, siblings, 0, half)], base_weight, factors, emitted=half - 1
+        pos, [(source, siblings, 0, half)], weight, factors, emitted=half - 1
     ))], half, {}
     for piece, (step, shift) in enumerate(pieces):
         (parts, send, keep, *emitted), *others = jobs
@@ -383,7 +365,7 @@
             chunks.insert(0, (source, siblings, next_local, 1))
             parts.insert(0, ((next_local, 0), 1))
             next_local, place = next_local + 1, 0
-        send, keep, *outs = partial_products(pos, chunks, base_weight, factors, last, place)
+        send, keep, *outs = partial_products(pos, chunks, weight, factors, last, place)
         if last:
             last_ranks[shift] = outs
             outs = []

time: 191 us -> 157 us (0.82)
  local copies, waits for them, and re-layouts: 46.3 us -> 9.47 us
  Pallas kernels: 86.8 us -> 72.9 us
  waiting for transfers between devices: 24.2 us -> 32.6 us
  starting transfers between devices: 25.4 us -> 33.8 us
    unnamed x54 -> x46, local copies, waits for them, and re-layouts: 45.4 us -> 6.42 us
    pallas_call x5, Pallas kernels: 81.2 us -> 69.5 us  [partial_products(): pl.pallas_call(functools.partial(matmul_body, spans, emitted, apart), in_...]
    ppermute x9, starting transfers between devices: 11.4 us -> 19.5 us  [swap_tensor(): return lax.ppermute(value, 'tp', [(i, i ^ bit) for i in range(n_tensor)])]
    ppermute x9, waiting for transfers between devices: 0.02 us -> 5.61 us  [swap_tensor(): return lax.ppermute(value, 'tp', [(i, i ^ bit) for i in range(n_tensor)])]
    ppermute x4, waiting for transfers between devices: 0.18 us -> 3.21 us  [from_rep(): lax.ppermute(value, 'rep', [((i + shift) % n_rep, i) for i in range(n_rep)])]
    slice x0 -> x1, local copies, waits for them, and re-layouts: none -> 2.16 us  [per_device(): hidden[:1]]
    pallas_call x1 -> x0, Pallas kernels: 2.11 us -> none  [cut_first(): pl.pallas_call(cut_body, in_specs=[pl.BlockSpec(memory_space=pl.ANY)], ou...]
  transfers between devices with their start and end apart: 26 -> 26, of which waited for: 5 -> 8; matrix products, arithmetic and copies ran while one was open for 4% -> 6% of each run, Pallas kernels for 45% -> 46%
where the time goes in v9:
time: 157 us; the launch traced here: 156 us
  Pallas kernels  72.9 us (46%)
  starting transfers between devices  33.8 us (22%)
  waiting for transfers between devices  32.6 us (21%)
  local copies, waits for them, and re-layouts  9.47 us (6%)
  other arithmetic  6.98 us (4%)
    pallas_call x5, Pallas kernels, partial_products(): pl.pallas_call(functools.partial(matmul_body, spans, emitted, apart), in_...  69.5 us
    ppermute x5, waiting for transfers between devices, to_group(): lax.ppermute(value, 'tp', [(i, (i + moved) % n_tensor) for i in range(n_t...  19.9 us
    ppermute x9, starting transfers between devices, swap_tensor(): return lax.ppermute(value, 'tp', [(i, i ^ bit) for i in range(n_tensor)])  19.5 us
    ppermute x5, starting transfers between devices, to_group(): lax.ppermute(value, 'tp', [(i, (i + moved) % n_tensor) for i in range(n_t...  6.76 us
    unnamed x46, local copies, waits for them, and re-layouts  6.42 us
    ppermute x4, starting transfers between devices, from_rep(): lax.ppermute(value, 'rep', [((i + shift) % n_rep, i) for i in range(n_rep)])  5.87 us
    ppermute x9, waiting for transfers between devices, swap_tensor(): return lax.ppermute(value, 'tp', [(i, i ^ bit) for i in range(n_tensor)])  5.61 us
    ppermute x3, waiting for transfers between devices, per_device(): lax.ppermute(masked, ('rep', 'sub'), [(i, (i + turn) % n_owners) for i in...  3.82 us
  transfers between devices with their start and end apart: 26, of which 8 were waited for; matrix products, arithmetic and copies ran while one was open for 6% of the time, Pallas kernels for 46%

profile of v9, /device:TPU:0, one launch (start us, length us, event | category | flops | bytes accessed | tf_op | source)
XLA Modules:
  0.0 156.2 jit_solution(9439970574705743406)
XLA Ops:
  0.5 2.2 %slice.68 = bf16[1,64,7168]{2,1,0:T(8,128)(2,1)} slice(bf16[4,64,7168]{2,1,0:T(8,128)(2,1)} %refs_0_.5), slice={[0:1], [0:64], [0:7168]} | slice | bytes 1835008 | tf_op jit(solution)/shard_map/slice | solution.py:275
  2.7 2.6 %collective-permute-start.1 = (bf16[1,64,7168]{2,1,0:T(8,128)(2,1)}, bf16[1,64,7168]{2,1,0:T(8,128)(2,1)S(1)}, u32[]{:S(2)}, u32[]{:S(2)}) collective-permute-start(bf16[1,64,7168]{2,1,0:T(8,128)(2,1)} %slice.68), channel_id=1, source_target_pairs={{2,0},{0,2},{3,1},{1,3},{6,4},{4,6},{7,5},{5,7},{10,8},{8,10},{11,... | collective-permute-start | bytes 2752520 | tf_op jit(solution)/shard_map/ppermute | solution.py:253
  5.3 2.6 %collective-permute-start.3 = (bf16[1,64,2048]{2,1,0:T(8,128)(2,1)S(1)}, bf16[1,64,2048]{2,1,0:T(8,128)(2,1)S(1)}, u32[]{:S(2)}, u32[]{:S(2)}) collective-permute-start(bf16[1,64,2048]{2,1,0:T(8,128)(2,1)S(1)} %copy-done.7), channel_id=1, source_target_pairs={{0,8},{4,12},{8,0},{12,4},{1,9},{5,13},{9,1},{13,5},{2,10},{6,14},... | collective-permute-start | bytes 786440 | tf_op jit(solution)/shard_map/ppermute | solution.py:256
  7.9 1.6 %collective-permute-start.2 = (bf16[1,64,2048]{2,1,0:T(8,128)(2,1)S(1)}, bf16[1,64,2048]{2,1,0:T(8,128)(2,1)}, u32[]{:S(2)}, u32[]{:S(2)}) collective-permute-start(bf16[1,64,2048]{2,1,0:T(8,128)(2,1)S(1)} %copy-done.7), channel_id=1, source_target_pairs={{0,4},{4,0},{8,12},{12,8},{1,5},{5,1},{9,13},{13,9},{2,6},{6,2},{1... | collective-permute-start | bytes 786440 | tf_op jit(solution)/shard_map/ppermute | solution.py:256
  9.7 16.6 %partial_products.5 = (bf16[128,2176]{1,0:T(8,128)(2,1)}, f32[128,2176]{1,0:T(8,128)S(1)}, bf16[1,64,7168]{2,1,0:T(8,128)(2,1)S(1)}) custom-call(s32[1]{0:T(128)} %bitcast.1.pos_ref, bf16[4,64,7168]{2,1,0:T(8,128)(2,1)} %refs_0_.5, bf16[4,64,7168]{2,1,0:T(8,128)(2,1)} %collective-permute-done.refs_1_, bf16[7168,2048]{1,0:T(8,128)(2,1)} %refs_2_.5, ...), custom_call_target="tpu_custom_call" | custom-call | tf_op jit(solution)/shard_map/partial_products/pallas_call | solution.py:130
  28.0 1.1 collective-permute-start.6
  29.1 4.5 %collective-permute-start.9 = (bf16[128,2176]{1,0:T(8,128)(2,1)}, bf16[128,2176]{1,0:T(8,128)(2,1)}, u32[]{:S(2)}, u32[]{:S(2)}) collective-permute-start(bf16[128,2176]{1,0:T(8,128)(2,1)} %get-tuple-element.87), channel_id=1, source_target_pairs={{0,4},{4,0},{8,12},{12,8},{1,5},{5,1},{9,13},{13,9},{2,6},{6,2},{1... | collective-permute-start | bytes 1671176 | tf_op jit(solution)/shard_map/ppermute | solution.py:256
  33.6 1.2 copy-done.3
  34.7 13.3 %partial_products.6 = (bf16[128,2176]{1,0:T(8,128)(2,1)S(1)}, f32[128,2176]{1,0:T(8,128)S(1)}, bf16[1,64,7168]{2,1,0:T(8,128)(2,1)S(1)}) custom-call(s32[1]{0:T(128)} %bitcast.1.pos_ref, bf16[4,64,7168]{2,1,0:T(8,128)(2,1)} %refs_0_.5, bf16[4,64,7168]{2,1,0:T(8,128)(2,1)} %collective-permute-done.refs_1_, bf16[1,64,7168]{2,1,0:T(8,128)(2,1)S(1)} %copy-done.3, ...), custom_call_target="tpu_custom_call" | custom-call | tf_op jit(solution)/shard_map/partial_products/pallas_call | solution.py:130
  49.8 1.1 collective-permute-done.6.refs_2_
  50.9 1.1 collective-permute-start.10
  52.0 4.4 %collective-permute-start.8 = (bf16[128,2176]{1,0:T(8,128)(2,1)}, bf16[128,2176]{1,0:T(8,128)(2,1)S(1)}, u32[]{:S(2)}, u32[]{:S(2)}) collective-permute-start(bf16[128,2176]{1,0:T(8,128)(2,1)} %copy-done.13), channel_id=1, source_target_pairs={{0,4},{4,0},{8,12},{12,8},{1,5},{5,1},{9,13},{13,9},{2,6},{6,2},{1... | collective-permute-start | bytes 1671176 | tf_op jit(solution)/shard_map/ppermute | solution.py:256
  56.4 1.2 convert_add_fusion.1
  57.6 16.9 %partial_products.7 = (bf16[128,2176]{1,0:T(8,128)(2,1)}, f32[128,2176]{1,0:T(8,128)S(1)}, bf16[1,64,7168]{2,1,0:T(8,128)(2,1)S(1)}) custom-call(s32[1]{0:T(128)} %bitcast.1.pos_ref, bf16[4,64,7168]{2,1,0:T(8,128)(2,1)} %refs_0_.5, bf16[4,64,7168]{2,1,0:T(8,128)(2,1)} %collective-permute-done.refs_1_, bf16[1,64,7168]{2,1,0:T(8,128)(2,1)} %collective-permute-done.6.refs_2_, ...), custom_call_target="tpu_custom_call" | custom-call | tf_op jit(solution)/shard_map/partial_products/pallas_call | solution.py:130
  76.5 2.5 %collective-permute-start.12 = (bf16[128,2176]{1,0:T(8,128)(2,1)}, bf16[128,2176]{1,0:T(8,128)(2,1)}, u32[]{:S(2)}, u32[]{:S(2)}) collective-permute-start(bf16[128,2176]{1,0:T(8,128)(2,1)} %get-tuple-element.97), channel_id=1, source_target_pairs={{0,4},{4,0},{8,12},{12,8},{1,5},{5,1},{9,13},{13,9},{2,6},{6,2},{1... | collective-permute-start | bytes 1671176 | tf_op jit(solution)/shard_map/ppermute | solution.py:256
  79.0 2.0 %collective-permute-start.14 = (bf16[64,2176]{1,0:T(8,128)(2,1)}, bf16[64,2176]{1,0:T(8,128)(2,1)S(1)}, u32[]{:S(2)}, u32[]{:S(2)}) collective-permute-start(bf16[64,2176]{1,0:T(8,128)(2,1)} %select_convert_fusion.2), channel_id=1, source_target_pairs={{0,8},{4,12},{8,0},{12,4},{1,9},{5,13},{9,1},{13,5},{2,10},{6,14},... | collective-permute-start | bytes 835592 | tf_op jit(solution)/shard_map/ppermute | solution.py:260
  81.0 1.1 collective-permute-start.13
  82.1 12.1 %partial_products.8 = (bf16[64,2176]{1,0:T(8,128)(2,1)S(1)}, f32[64,2176]{1,0:T(8,128)S(1)}) custom-call(s32[1]{0:T(128)} %bitcast.1.pos_ref, bf16[1,64,7168]{2,1,0:T(8,128)(2,1)} %collective-permute-done.10.refs_0_, bf16[1,64,7168]{2,1,0:T(8,128)(2,1)} %collective-permute-done.11.refs_1_, bf16[7168,2048]{1,0:T(8,128)(2,1)} %refs_2_.5, ...), custom_call_target="tpu_custom_call" | custom-call | tf_op jit(solution)/shard_map/partial_products/pallas_call | solution.py:130
  94.2 4.3 %collective-permute-done.12 = bf16[128,2176]{1,0:T(8,128)(2,1)} collective-permute-done((bf16[128,2176]{1,0:T(8,128)(2,1)}, bf16[128,2176]{1,0:T(8,128)(2,1)}, u32[]{:S(2)}, u32[]{:S(2)}) %collective-permute-start.12) | collective-permute-done | bytes 557088 | tf_op jit(solution)/shard_map/ppermute | solution.py:256
  98.6 1.2 convert_add_fusion
  101.6 2.1 %collective-permute-done.13.refs_0_ = bf16[1,64,7168]{2,1,0:T(8,128)(2,1)S(1)} collective-permute-done((bf16[1,64,7168]{2,1,0:T(8,128)(2,1)}, bf16[1,64,7168]{2,1,0:T(8,128)(2,1)S(1)}, u32[]{:S(2)}, u32[]{:S(2)}) %collective-permute-start.13) | collective-permute-done | bytes 917536 | tf_op jit(solution)/shard_map/ppermute | solution.py:253
  103.8 1.7 %collective-permute-start.16 = (bf16[64,2176]{1,0:T(8,128)(2,1)}, bf16[64,2176]{1,0:T(8,128)(2,1)}, u32[]{:S(2)}, u32[]{:S(2)}) collective-permute-start(bf16[64,2176]{1,0:T(8,128)(2,1)} %copy-done.14), channel_id=1, source_target_pairs={{0,4},{4,0},{8,12},{12,8},{1,5},{5,1},{9,13},{13,9},{2,6},{6,2},{1... | collective-permute-start | bytes 835592 | tf_op jit(solution)/shard_map/ppermute | solution.py:256
  107.4 10.7 %partial_products.9 = (bf16[64,2048]{1,0:T(8,128)(2,1)S(1)}, f32[64,2048]{1,0:T(8,128)S(1)}, f32[64,128]{1,0:T(8,128)S(1)}, f32[64,128]{1,0:T(8,128)S(1)}) custom-call(s32[1]{0:T(128)} %bitcast.1.pos_ref, bf16[1,64,7168]{2,1,0:T(8,128)(2,1)S(1)} %collective-permute-done.13.refs_0_, bf16[1,64,7168]{2,1,0:T(8,128)(2,1)} %collective-permute-done.15.refs_1_, ...), custom_call_target="tpu_custom_call" | custom-call | tf_op jit(solution)/shard_map/partial_products/pallas_call | solution.py:130
  119.2 3.2 %collective-permute-done.17.refs_7_ = bf16[64,2176]{1,0:T(8,128)(2,1)S(1)} collective-permute-done((bf16[64,2176]{1,0:T(8,128)(2,1)}, bf16[64,2176]{1,0:T(8,128)(2,1)S(1)}, u32[]{:S(2)}, u32[]{:S(2)}) %collective-permute-start.17) | collective-permute-done | bytes 278560 | tf_op jit(solution)/shard_map/ppermute | solution.py:260
  122.5 2.0 %collective-permute-start.18 = (bf16[64,2048]{1,0:T(8,128)(2,1)S(1)}, bf16[64,2048]{1,0:T(8,128)(2,1)S(1)}, u32[]{:S(2)}, u32[]{:S(2)}) collective-permute-start(bf16[64,2048]{1,0:T(8,128)(2,1)S(1)} %get-tuple-element.120), channel_id=1, source_target_pairs={{0,4},{4,0},{8,12},{12,8},{1,5},{5,1},{9,13},{13,9},{2,6},{6,2},{1... | collective-permute-start | bytes 786440 | tf_op jit(solution)/shard_map/ppermute | solution.py:256
  124.5 1.1 slice_select_fusion.refs_8_
  125.6 1.2 collective-permute-done.20
  126.8 3.8 %collective-permute-start.21 = (f32[64,128]{1,0:T(8,128)S(1)}, f32[64,128]{1,0:T(8,128)S(1)}, u32[]{:S(2)}, u32[]{:S(2)}) collective-permute-start(f32[64,128]{1,0:T(8,128)S(1)} %get-tuple-element.135), channel_id=1, source_target_pairs={{0,8},{4,12},{8,0},{12,4},{1,9},{5,13},{9,1},{13,5},{2,10},{6,14},... | collective-permute-start | bytes 98312 | tf_op jit(solution)/shard_map/ppermute | solution.py:260
  130.7 9.5 %collective-permute-done.21 = f32[64,128]{1,0:T(8,128)S(1)} collective-permute-done((f32[64,128]{1,0:T(8,128)S(1)}, f32[64,128]{1,0:T(8,128)S(1)}, u32[]{:S(2)}, u32[]{:S(2)}) %collective-permute-start.21) | collective-permute-done | bytes 32800 | tf_op jit(solution)/shard_map/ppermute | solution.py:260
  141.7 3.8 %collective-permute-done.23 = bf16[4,64,64]{2,1,0:T(8,128)(2,1)S(1)} collective-permute-done((bf16[4,64,64]{2,1,0:T(8,128)(2,1)S(1)}, bf16[4,64,64]{2,1,0:T(8,128)(2,1)S(1)}, u32[]{:S(2)}, u32[]{:S(2)}) %collective-permute-start.23) | collective-permute-done | bytes 32800 | tf_op jit(solution)/shard_map/ppermute | solution.py:398
  145.6 2.6 %finish_steps.1 = (bf16[4,64,2048]{2,1,0:T(8,128)(2,1)}, bf16[64,2048]{1,0:T(8,128)(2,1)S(1)}) custom-call(bf16[256,64]{1,0:T(8,128)(2,1)S(1)} %bitcast.30, s32[256,1]{1,0:T(8,128)S(1)} %copy-done.4, s32[4]{0:T(128)S(1)} %pad_add_fusion.order_ref, bf16[64,2048]{1,0:T(8,128)(2,1)S(1)} %bitcast.31, bf16[64,2048]{1,0:T(8,128)(2,1)} %bitcast.14.refs_1_, ...), custom_call_target="tpu_custom_call" | custom-call | tf_op jit(solution)/shard_map/finish_steps/pallas_call | solution.py:185
  148.2 7.2 %collective-permute-done.25.refs_1_ = bf16[64,2048]{1,0:T(8,128)(2,1)S(1)} collective-permute-done((bf16[64,2048]{1,0:T(8,128)(2,1)S(1)}, bf16[64,2048]{1,0:T(8,128)(2,1)S(1)}, u32[]{:S(2)}, u32[]{:S(2)}) %collective-permute-start.25) | collective-permute-done | bytes 262176 | tf_op jit(solution)/shard_map/ppermute | solution.py:260
  (104 shorter events, 13.4 us)
Async XLA Ops:
  0.0 103.7 %copy-start = (s32[256,1]{0,1:T(1,128)S(1)}, s32[256,1]{0,1:T(1,128)}, u32[]{:S(2)}) copy-start(s32[256,1]{0,1:T(1,128)} %param.10) | copy-start | bytes 3076
  0.0 9.7 %copy-start.1 = (bf16[1,7168,64]{1,2,0:T(8,128)(2,1)S(1)}, bf16[1,7168,64]{1,2,0:T(8,128)(2,1)}, u32[]{:S(2)}) copy-start(bf16[1,7168,64]{1,2,0:T(8,128)(2,1)} %param.8) | copy-start | bytes 2752516
  0.0 9.7 %collective-permute-start = (bf16[4,64,7168]{2,1,0:T(8,128)(2,1)}, bf16[4,64,7168]{2,1,0:T(8,128)(2,1)}, u32[]{:S(2)}, u32[]{:S(2)}) collective-permute-start(bf16[4,64,7168]{2,1,0:T(8,128)(2,1)} %refs_0_.5), channel_id=1, source_target_pairs={{0,1},{1,0},{2,3},{3,2},{4,5},{5,4},{6,7},{7,6},{8,9},{9,8},{10,11... | collective-permute-start | bytes 11010056 | tf_op jit(solution)/shard_map/ppermute | solution.py:250
  2.7 24.4 %collective-permute-start.1 = (bf16[1,64,7168]{2,1,0:T(8,128)(2,1)}, bf16[1,64,7168]{2,1,0:T(8,128)(2,1)S(1)}, u32[]{:S(2)}, u32[]{:S(2)}) collective-permute-start(bf16[1,64,7168]{2,1,0:T(8,128)(2,1)} %slice.68), channel_id=1, source_target_pairs={{2,0},{0,2},{3,1},{1,3},{6,4},{4,6},{7,5},{5,7},{10,8},{8,10},{11,... | collective-permute-start | bytes 2752520 | tf_op jit(solution)/shard_map/ppermute | solution.py:253
  5.3 21.0 %collective-permute-start.3 = (bf16[1,64,2048]{2,1,0:T(8,128)(2,1)S(1)}, bf16[1,64,2048]{2,1,0:T(8,128)(2,1)S(1)}, u32[]{:S(2)}, u32[]{:S(2)}) collective-permute-start(bf16[1,64,2048]{2,1,0:T(8,128)(2,1)S(1)} %copy-done.7), channel_id=1, source_target_pairs={{0,8},{4,12},{8,0},{12,4},{1,9},{5,13},{9,1},{13,5},{2,10},{6,14},... | collective-permute-start | bytes 786440 | tf_op jit(solution)/shard_map/ppermute | solution.py:256
  7.9 19.1 %collective-permute-start.2 = (bf16[1,64,2048]{2,1,0:T(8,128)(2,1)S(1)}, bf16[1,64,2048]{2,1,0:T(8,128)(2,1)}, u32[]{:S(2)}, u32[]{:S(2)}) collective-permute-start(bf16[1,64,2048]{2,1,0:T(8,128)(2,1)S(1)} %copy-done.7), channel_id=1, source_target_pairs={{0,4},{4,0},{8,12},{12,8},{1,5},{5,1},{9,13},{13,9},{2,6},{6,2},{1... | collective-permute-start | bytes 786440 | tf_op jit(solution)/shard_map/ppermute | solution.py:256
  9.4 17.6 %collective-permute-start.4 = (bf16[1,64,2048]{2,1,0:T(8,128)(2,1)S(1)}, bf16[1,64,2048]{2,1,0:T(8,128)(2,1)}, u32[]{:S(2)}, u32[]{:S(2)}) collective-permute-start(bf16[1,64,2048]{2,1,0:T(8,128)(2,1)S(1)} %copy-done.7), channel_id=1, source_target_pairs={{0,12},{4,8},{8,4},{12,0},{1,13},{5,9},{9,5},{13,1},{2,14},{6,10},... | collective-permute-start | bytes 786440 | tf_op jit(solution)/shard_map/ppermute | solution.py:256
  27.0 6.5 %collective-permute-start.5 = (bf16[1,64,7168]{2,1,0:T(8,128)(2,1)S(1)}, bf16[1,64,7168]{2,1,0:T(8,128)(2,1)S(1)}, u32[]{:S(2)}, u32[]{:S(2)}) collective-permute-start(bf16[1,64,7168]{2,1,0:T(8,128)(2,1)S(1)} %collective-permute-done.1.refs_2_), channel_id=1, source_target_pairs={{0,1},{1,0},{2,3},{3,2},{4,5},{5,4},{6,7},{7,6},{8,9},{9,8},{10,11... | collective-permute-start | bytes 2752520 | tf_op jit(solution)/shard_map/ppermute | solution.py:250
  28.0 22.9 %collective-permute-start.6 = (bf16[1,64,7168]{2,1,0:T(8,128)(2,1)S(1)}, bf16[1,64,7168]{2,1,0:T(8,128)(2,1)}, u32[]{:S(2)}, u32[]{:S(2)}) collective-permute-start(bf16[1,64,7168]{2,1,0:T(8,128)(2,1)S(1)} %get-tuple-element.74), channel_id=1, source_target_pairs={{2,0},{0,2},{3,1},{1,3},{6,4},{4,6},{7,5},{5,7},{10,8},{8,10},{11,... | collective-permute-start | bytes 2752520 | tf_op jit(solution)/shard_map/ppermute | solution.py:253
  29.1 27.3 %collective-permute-start.9 = (bf16[128,2176]{1,0:T(8,128)(2,1)}, bf16[128,2176]{1,0:T(8,128)(2,1)}, u32[]{:S(2)}, u32[]{:S(2)}) collective-permute-start(bf16[128,2176]{1,0:T(8,128)(2,1)} %get-tuple-element.87), channel_id=1, source_target_pairs={{0,4},{4,0},{8,12},{12,8},{1,5},{5,1},{9,13},{13,9},{2,6},{6,2},{1... | collective-permute-start | bytes 1671176 | tf_op jit(solution)/shard_map/ppermute | solution.py:256
  50.9 6.8 %collective-permute-start.7 = (bf16[1,64,7168]{2,1,0:T(8,128)(2,1)}, bf16[1,64,7168]{2,1,0:T(8,128)(2,1)}, u32[]{:S(2)}, u32[]{:S(2)}) collective-permute-start(bf16[1,64,7168]{2,1,0:T(8,128)(2,1)} %collective-permute-done.6.refs_2_), channel_id=1, source_target_pairs={{0,1},{1,0},{2,3},{3,2},{4,5},{5,4},{6,7},{7,6},{8,9},{9,8},{10,11... | collective-permute-start | bytes 2752520 | tf_op jit(solution)/shard_map/ppermute | solution.py:250
  50.9 25.7 %collective-permute-start.10 = (bf16[1,64,7168]{2,1,0:T(8,128)(2,1)}, bf16[1,64,7168]{2,1,0:T(8,128)(2,1)}, u32[]{:S(2)}, u32[]{:S(2)}) collective-permute-start(bf16[1,64,7168]{2,1,0:T(8,128)(2,1)} %copy-done.11), channel_id=1, source_target_pairs={{2,0},{0,2},{3,1},{1,3},{6,4},{4,6},{7,5},{5,7},{10,8},{8,10},{11,... | collective-permute-start | bytes 2752520 | tf_op jit(solution)/shard_map/ppermute | solution.py:253
  52.0 22.5 %collective-permute-start.8 = (bf16[128,2176]{1,0:T(8,128)(2,1)}, bf16[128,2176]{1,0:T(8,128)(2,1)S(1)}, u32[]{:S(2)}, u32[]{:S(2)}) collective-permute-start(bf16[128,2176]{1,0:T(8,128)(2,1)} %copy-done.13), channel_id=1, source_target_pairs={{0,4},{4,0},{8,12},{12,8},{1,5},{5,1},{9,13},{13,9},{2,6},{6,2},{1... | collective-permute-start | bytes 1671176 | tf_op jit(solution)/shard_map/ppermute | solution.py:256
  57.6 17.0 %copy-start.18 = (f32[128,2176]{1,0:T(8,128)}, f32[128,2176]{1,0:T(8,128)S(1)}, u32[]{:S(2)}) copy-start(f32[128,2176]{1,0:T(8,128)S(1)} %convert_add_fusion.1) | copy-start | bytes 3342340
  76.5 5.5 %collective-permute-start.11 = (bf16[1,64,7168]{2,1,0:T(8,128)(2,1)}, bf16[1,64,7168]{2,1,0:T(8,128)(2,1)}, u32[]{:S(2)}, u32[]{:S(2)}) collective-permute-start(bf16[1,64,7168]{2,1,0:T(8,128)(2,1)} %collective-permute-done.10.refs_0_), channel_id=1, source_target_pairs={{0,1},{1,0},{2,3},{3,2},{4,5},{5,4},{6,7},{7,6},{8,9},{9,8},{10,11... | collective-permute-start | bytes 2752520 | tf_op jit(solution)/shard_map/ppermute | solution.py:250
  76.5 22.0 %collective-permute-start.12 = (bf16[128,2176]{1,0:T(8,128)(2,1)}, bf16[128,2176]{1,0:T(8,128)(2,1)}, u32[]{:S(2)}, u32[]{:S(2)}) collective-permute-start(bf16[128,2176]{1,0:T(8,128)(2,1)} %get-tuple-element.97), channel_id=1, source_target_pairs={{0,4},{4,0},{8,12},{12,8},{1,5},{5,1},{9,13},{13,9},{2,6},{6,2},{1... | collective-permute-start | bytes 1671176 | tf_op jit(solution)/shard_map/ppermute | solution.py:256
  79.0 22.6 %collective-permute-start.14 = (bf16[64,2176]{1,0:T(8,128)(2,1)}, bf16[64,2176]{1,0:T(8,128)(2,1)S(1)}, u32[]{:S(2)}, u32[]{:S(2)}) collective-permute-start(bf16[64,2176]{1,0:T(8,128)(2,1)} %select_convert_fusion.2), channel_id=1, source_target_pairs={{0,8},{4,12},{8,0},{12,4},{1,9},{5,13},{9,1},{13,5},{2,10},{6,14},... | collective-permute-start | bytes 835592 | tf_op jit(solution)/shard_map/ppermute | solution.py:260
  81.0 22.7 %collective-permute-start.13 = (bf16[1,64,7168]{2,1,0:T(8,128)(2,1)}, bf16[1,64,7168]{2,1,0:T(8,128)(2,1)S(1)}, u32[]{:S(2)}, u32[]{:S(2)}) collective-permute-start(bf16[1,64,7168]{2,1,0:T(8,128)(2,1)} %copy-done.12), channel_id=1, source_target_pairs={{2,0},{0,2},{3,1},{1,3},{6,4},{4,6},{7,5},{5,7},{10,8},{8,10},{11,... | collective-permute-start | bytes 2752520 | tf_op jit(solution)/shard_map/ppermute | solution.py:253
  103.7 3.7 %collective-permute-start.15 = (bf16[1,64,7168]{2,1,0:T(8,128)(2,1)S(1)}, bf16[1,64,7168]{2,1,0:T(8,128)(2,1)}, u32[]{:S(2)}, u32[]{:S(2)}) collective-permute-start(bf16[1,64,7168]{2,1,0:T(8,128)(2,1)S(1)} %collective-permute-done.13.refs_0_), channel_id=1, source_target_pairs={{0,1},{1,0},{2,3},{3,2},{4,5},{5,4},{6,7},{7,6},{8,9},{9,8},{10,11... | collective-permute-start | bytes 2752520 | tf_op jit(solution)/shard_map/ppermute | solution.py:250
  103.8 14.3 %collective-permute-start.16 = (bf16[64,2176]{1,0:T(8,128)(2,1)}, bf16[64,2176]{1,0:T(8,128)(2,1)}, u32[]{:S(2)}, u32[]{:S(2)}) collective-permute-start(bf16[64,2176]{1,0:T(8,128)(2,1)} %copy-done.14), channel_id=1, source_target_pairs={{0,4},{4,0},{8,12},{12,8},{1,5},{5,1},{9,13},{13,9},{2,6},{6,2},{1... | collective-permute-start | bytes 835592 | tf_op jit(solution)/shard_map/ppermute | solution.py:256
  106.5 11.7 %copy-start.17 = (f32[128,2176]{1,0:T(8,128)S(1)}, f32[128,2176]{1,0:T(8,128)}, u32[]{:S(2)}) copy-start(f32[128,2176]{1,0:T(8,128)} %copy-done.15) | copy-start | bytes 3342340
  106.5 16.0 %collective-permute-start.17 = (bf16[64,2176]{1,0:T(8,128)(2,1)}, bf16[64,2176]{1,0:T(8,128)(2,1)S(1)}, u32[]{:S(2)}, u32[]{:S(2)}) collective-permute-start(bf16[64,2176]{1,0:T(8,128)(2,1)} %select_convert_fusion.1), channel_id=1, source_target_pairs={{0,8},{4,12},{8,0},{12,4},{1,9},{5,13},{9,1},{13,5},{2,10},{6,14},... | collective-permute-start | bytes 835592 | tf_op jit(solution)/shard_map/ppermute | solution.py:260
  119.2 7.6 %copy-start.21 = (f32[128,2176]{1,0:T(8,128)S(1)}, f32[128,2176]{1,0:T(8,128)}, u32[]{:S(2)}) copy-start(f32[128,2176]{1,0:T(8,128)} %copy-done.20) | copy-start | bytes 3342340
  122.5 8.2 %slice-start = ((bf16[64,2176]{1,0:T(8,128)(2,1)}), bf16[64,128]{1,0:T(8,128)(2,1)S(1)}, s32[]{:S(2)}) async-start(bf16[64,2176]{1,0:T(8,128)(2,1)} %copy-done.5), calls=%async_computation | async-start | bytes 32768 | tf_op jit(solution)/shard_map/slice | solution.py:384
  122.5 4.3 %collective-permute-start.20 = (f32[64,128]{1,0:T(8,128)S(1)}, f32[64,128]{1,0:T(8,128)S(1)}, u32[]{:S(2)}, u32[]{:S(2)}) collective-permute-start(f32[64,128]{1,0:T(8,128)S(1)} %get-tuple-element.126), channel_id=1, source_target_pairs={{0,4},{4,0},{8,12},{12,8},{1,5},{5,1},{9,13},{13,9},{2,6},{6,2},{1... | collective-permute-start | bytes 98312 | tf_op jit(solution)/shard_map/ppermute | solution.py:256
  122.5 17.8 %collective-permute-start.18 = (bf16[64,2048]{1,0:T(8,128)(2,1)S(1)}, bf16[64,2048]{1,0:T(8,128)(2,1)S(1)}, u32[]{:S(2)}, u32[]{:S(2)}) collective-permute-start(bf16[64,2048]{1,0:T(8,128)(2,1)S(1)} %get-tuple-element.120), channel_id=1, source_target_pairs={{0,4},{4,0},{8,12},{12,8},{1,5},{5,1},{9,13},{13,9},{2,6},{6,2},{1... | collective-permute-start | bytes 786440 | tf_op jit(solution)/shard_map/ppermute | solution.py:256
  124.5 15.8 %collective-permute-start.19 = (bf16[64,2176]{1,0:T(8,128)(2,1)S(1)}, bf16[64,2176]{1,0:T(8,128)(2,1)S(1)}, u32[]{:S(2)}, u32[]{:S(2)}) collective-permute-start(bf16[64,2176]{1,0:T(8,128)(2,1)S(1)} %select_convert_fusion), channel_id=1, source_target_pairs={{0,8},{4,12},{8,0},{12,4},{1,9},{5,13},{9,1},{13,5},{2,10},{6,14},... | collective-permute-start | bytes 835592 | tf_op jit(solution)/shard_map/ppermute | solution.py:260
  126.8 13.4 %collective-permute-start.21 = (f32[64,128]{1,0:T(8,128)S(1)}, f32[64,128]{1,0:T(8,128)S(1)}, u32[]{:S(2)}, u32[]{:S(2)}) collective-permute-start(f32[64,128]{1,0:T(8,128)S(1)} %get-tuple-element.135), channel_id=1, source_target_pairs={{0,8},{4,12},{8,0},{12,4},{1,9},{5,13},{9,1},{13,5},{2,10},{6,14},... | collective-permute-start | bytes 98312 | tf_op jit(solution)/shard_map/ppermute | solution.py:260
  140.5 5.0 %collective-permute-start.23 = (bf16[4,64,64]{2,1,0:T(8,128)(2,1)S(1)}, bf16[4,64,64]{2,1,0:T(8,128)(2,1)S(1)}, u32[]{:S(2)}, u32[]{:S(2)}) collective-permute-start(bf16[4,64,64]{2,1,0:T(8,128)(2,1)S(1)} %select_bitcast_fusion), channel_id=1, source_target_pairs={{0,2},{1,3},{2,0},{3,1},{4,6},{5,7},{6,4},{7,5},{8,10},{9,11},{10,... | collective-permute-start | bytes 98312 | tf_op jit(solution)/shard_map/ppermute | solution.py:398
  141.1 4.4 %collective-permute-start.24 = (bf16[4,64,64]{2,1,0:T(8,128)(2,1)S(1)}, bf16[4,64,64]{2,1,0:T(8,128)(2,1)S(1)}, u32[]{:S(2)}, u32[]{:S(2)}) collective-permute-start(bf16[4,64,64]{2,1,0:T(8,128)(2,1)S(1)} %select_bitcast_fusion), channel_id=1, source_target_pairs={{0,3},{1,0},{2,1},{3,2},{4,7},{5,4},{6,5},{7,6},{8,11},{9,8},{10,9... | collective-permute-start | bytes 98312 | tf_op jit(solution)/shard_map/ppermute | solution.py:398
  141.1 4.4 %collective-permute-start.22 = (bf16[4,64,64]{2,1,0:T(8,128)(2,1)S(1)}, bf16[4,64,64]{2,1,0:T(8,128)(2,1)S(1)}, u32[]{:S(2)}, u32[]{:S(2)}) collective-permute-start(bf16[4,64,64]{2,1,0:T(8,128)(2,1)S(1)} %select_bitcast_fusion), channel_id=1, source_target_pairs={{0,1},{1,2},{2,3},{3,0},{4,5},{5,6},{6,7},{7,4},{8,9},{9,10},{10,1... | collective-permute-start | bytes 98312 | tf_op jit(solution)/shard_map/ppermute | solution.py:398
  141.6 13.8 %collective-permute-start.25 = (bf16[64,2048]{1,0:T(8,128)(2,1)S(1)}, bf16[64,2048]{1,0:T(8,128)(2,1)S(1)}, u32[]{:S(2)}, u32[]{:S(2)}) collective-permute-start(bf16[64,2048]{1,0:T(8,128)(2,1)S(1)} %select_convert_fusion.3), channel_id=1, source_target_pairs={{0,8},{4,12},{8,0},{12,4},{1,9},{5,13},{9,1},{13,5},{2,10},{6,14},... | collective-permute-start | bytes 786440 | tf_op jit(solution)/shard_map/ppermute | solution.py:260
  (18 other events, 56.2 us)

commit v10 on v9

--- a/solution.py
+++ b/solution.py
@@ -12,7 +12,7 @@
 BLOCK = 1024
 BUFFERS = 4
 RANK_NAME = 1000
-VMEM_BYTES = 17 * 1024 * 1024
+VMEM_BYTES = 22 * 1024 * 1024
 
 
 def block_shape(depth, width):
@@ -68,11 +68,11 @@
         keep_rank[...] = jnp.zeros_like(keep_rank)
     for copy in copies:
         copy.wait()
-    emit = None
-    if emitted is not None:
-        emit = pltpu.make_async_copy(
-            x_ref.at[own_at, pl.ds(emitted, 1)], outs[-1], x_sems.at[2 * len(spans)]
-        )
+    emits = [
+        pltpu.make_async_copy(x_ref.at[own_at, pl.ds(block, 1)], out_ref, x_sems.at[2 * len(spans) + index])
+        for index, (block, out_ref) in enumerate(zip(emitted, outs[2 if apart else 0:]))
+    ]
+    for emit in emits:
         emit.start()
     for slot in range(slots):
         x = x_ref[...].reshape(2 * rows, depth)
@@ -103,11 +103,11 @@
             fetch(block + buffers, slot).start()
 
     send_ref[...] = total_ref[...].astype(send_ref.dtype)
-    if emit is not None:
+    for emit in emits:
         emit.wait()
 
 
-def partial_products(pos, chunks, weight, factors, apart=False, emitted=None):
+def partial_products(pos, chunks, weight, factors, apart=False, emitted=()):
     _, per_block, depth = chunks[0][0].shape
     width = weight.shape[1]
     spans = tuple((first, steps) for _, _, first, steps in chunks)
@@ -124,9 +124,8 @@
         jax.ShapeDtypeStruct((rows, columns), jnp.float32),
     ] + [jax.ShapeDtypeStruct((rows, extra), jnp.float32)] * (2 if apart else 0)
     out_specs = [vmem_spec] * len(out_shape)
-    if emitted is not None:
-        out_shape.append(jax.ShapeDtypeStruct((1, per_block, depth), jnp.bfloat16))
-        out_specs.append(any_spec)
+    out_shape += [jax.ShapeDtypeStruct((1, per_block, depth), jnp.bfloat16)] * len(emitted)
+    out_specs += [any_spec] * len(emitted)
     return pl.pallas_call(
         functools.partial(matmul_body, spans, emitted, apart),
         in_specs=[pl.BlockSpec(memory_space=pltpu.SMEM)] + [any_spec] * (2 * len(chunks) + 1) + [vmem_spec],
@@ -136,7 +135,7 @@
             pltpu.VMEM((2, steps, per_block, depth), jnp.bfloat16),
             pltpu.VMEM((buffers, block_k, block_w), jnp.bfloat16),
             pltpu.VMEM((rows, columns), jnp.float32),
-            pltpu.SemaphoreType.DMA((2 * len(chunks) + 1,)),
+            pltpu.SemaphoreType.DMA((2 * len(chunks) + len(emitted),)),
             pltpu.SemaphoreType.DMA((buffers,)),
         ],
         compiler_params=pltpu.CompilerParams(vmem_limit_bytes=VMEM_BYTES),
@@ -306,7 +305,7 @@
             bit //= 2
         return total.reshape(steps, extent, columns)
 
-    def gap(token, jobs, *extra):
+    def gap(token, jobs, short=False):
         nonlocal first_leg, second_leg
         for parts, received, keep, kind in first_leg:
             steps = sum(length for _, length in parts)
@@ -317,9 +316,12 @@
                     if (key[0] + at - begin, key[1]) == (step_count - 1, 0):
                         halved[RANK_NAME, 0] = total[at][:, width:]
                 begin += length
-        closed = {}
-        for name, kept, received in second_leg:
-            closed[name] = (after(kept, token), *received)
+        closed, waiting = {}, []
+        for name, kept, received, lag in second_leg:
+            if short or lag > 1:
+                waiting.append((name, kept, received, lag if short else lag - 1))
+            else:
+                closed[name] = (after(kept, token), *received)
         started, sends = [], []
         for name in sorted({name for name, _ in halved}):
             if name in begun or name == RANK_NAME or any((name, at) not in halved for at in range(n_rep)):
@@ -329,49 +331,52 @@
             columns = min(value.shape[1] for value in values)
             values = [value[:, :columns] for value in values]
             kept = pick(values, (group_index - rep_index) % n_rep)
-            sent = [pick(values, (group_index + hop - rep_index) % n_rep).astype(jnp.bfloat16) for hop in range(1, n_rep)]
+            sends.append([
+                pick(values, (group_index + hop - rep_index) % n_rep).astype(jnp.bfloat16) for hop in range(1, n_rep)
+            ])
             started.append((name, kept))
-            sends.append(sent)
-        first_sends = [job[1] for job in jobs]
-        first_sends, sends, extra, closed, _ = lax.optimization_barrier((first_sends, sends, extra, closed, token))
+        sends, token = lax.optimization_barrier((sends, token))
+        first_sends, closed = lax.optimization_barrier(([job[1] for job in jobs], closed))
         ended.update(closed)
         first_leg = [
             (parts, swap_tensor(send, group // 2), keep, kind) for (parts, _, keep, kind), send in zip(jobs, first_sends)
         ]
-        second_leg = [
-            (name, kept, [to_group(value, hop + 1) for hop, value in enumerate(sent)])
+        second_leg = waiting + [
+            (name, kept, [to_group(value, hop + 1) for hop, value in enumerate(sent)], 2 if short else 1)
             for (name, kept), sent in zip(started, sends)
         ]
-        return extra if extra else [sent for sent in sends]
+        return sends
 
     factors = jnp.swapaxes(down_a, 1, 2)
 
-    half = step_count // 2
-    jobs, next_local, last_ranks = [([((0, 0), half)], *partial_products(
-        pos, [(source, siblings, 0, half)], weight, factors, emitted=half - 1
-    ))], half, {}
+    lead = step_count - 1
+    parts, last_ranks = [((0, 0), lead)], {}
+    send, keep, *emitted = partial_products(
+        pos, [(source, siblings, 0, lead)], weight, factors, emitted=tuple(range(1, lead))
+    )
+    for step, rows in enumerate(emitted, 1):
+        remote.update({(step, shift): from_rep(rows, shift) for shift in range(1, n_rep)})
     for piece, (step, shift) in enumerate(pieces):
-        (parts, send, keep, *emitted), *others = jobs
-        jobs = [(parts, send, keep, jnp.bfloat16)]
-        if emitted:
-            for along in range(1, n_rep):
-                remote[next_local - 1, along] = from_rep(emitted[0], along)
-        own, siblings, panels = gap(send, jobs, remote[step, shift], siblings, panels)
+        sends = gap(send, [(parts, send, keep, jnp.bfloat16)])
+        own, panels, _ = lax.optimization_barrier((remote[step, shift], panels, send))
         if piece == 0:
             panels, order = spread_panels(panels, order, bits[2:])
         sib = swap_cores(own)
-        last, chunks, parts, place = step == step_count - 1, [(own, sib, 0, 1)], [((step, shift), 1)], None
-        if next_local < step_count:
-            chunks.insert(0, (source, siblings, next_local, 1))
-            parts.insert(0, ((next_local, 0), 1))
-            next_local, place = next_local + 1, 0
-        send, keep, *outs = partial_products(pos, chunks, weight, factors, last, place)
+        held = [sends, siblings] if piece == 0 else [sends]
+        if piece == len(pieces) - 1:
+            held += gap(lax.optimization_barrier((send, sends))[0], [], short=True)
+        own, sib, held = lax.optimization_barrier((own, sib, held))
+        last, chunks, parts, places = step == step_count - 1, [(own, sib, 0, 1)], [((step, shift), 1)], ()
+        if piece == 0:
+            chunks.insert(0, (source, held[1], lead, 1))
+            parts.insert(0, ((lead, 0), 1))
+            places = (0,)
+        send, keep, *outs = partial_products(pos, chunks, weight, factors, last, places)
         if last:
             last_ranks[shift] = outs
-            outs = []
-        jobs = [(parts, send, keep, *outs)]
-    jobs = [(parts, send, keep, jnp.bfloat16)]
-    last_ranks, = gap(send, jobs, last_ranks)
+        elif outs:
+            remote.update({(lead, along): from_rep(outs[0], along) for along in range(1, n_rep)})
+    gap(send, [(parts, send, keep, jnp.bfloat16)])
     for shift, ranks in last_ranks.items():
         halved[RANK_NAME, shift] = second_half(ranks[1], swap_tensor(ranks[0], group // 2), 1, jnp.float32)[0]
     values = [halved[RANK_NAME, at] for at in range(n_rep)]
@@ -389,7 +394,7 @@
     finished = jnp.stack([rank_sum(step) for step in range(step_count - 1)] + [rank_sum(RANK_NAME)])
     finished = finished.astype(jnp.bfloat16).reshape(step_count, rows_mine, owned_slots, rank_size)
     finished = lax.optimization_barrier((finished, rounded))[0]
-    ended.update((name, (kept, *received)) for name, kept, received in second_leg)
+    ended.update((name, (kept, *received)) for name, kept, received, _ in second_leg)
     masked = jnp.sum(
         jnp.where(owned_hot[None, :, :, None], finished, 0), axis=2, dtype=jnp.float32
     ).astype(jnp.bfloat16)

time: 157 us -> 146 us (0.930)
  starting transfers between devices: 33.8 us -> 28 us
  other arithmetic: 6.98 us -> 2.35 us
  waiting for transfers between devices: 32.6 us -> 37.2 us
  local copies, waits for them, and re-layouts: 9.47 us -> 5.41 us
    ppermute x9, starting transfers between devices: 19.5 us -> 9.59 us  [swap_tensor(): return lax.ppermute(value, 'tp', [(i, i ^ bit) for i in range(n_tensor)])]
    ppermute x5, waiting for transfers between devices: 19.9 us -> 12.7 us  [to_group(): lax.ppermute(value, 'tp', [(i, (i + moved) % n_tensor) for i in range(n_t...]
    ppermute x9, waiting for transfers between devices: 5.61 us -> 12.8 us  [swap_tensor(): return lax.ppermute(value, 'tp', [(i, i ^ bit) for i in range(n_tensor)])]
    ppermute x4, waiting for transfers between devices: 3.21 us -> 9.73 us  [from_rep(): lax.ppermute(value, 'rep', [((i + shift) % n_rep, i) for i in range(n_rep)])]
    ppermute x5, starting transfers between devices: 6.76 us -> 12 us  [to_group(): lax.ppermute(value, 'tp', [(i, (i + moved) % n_tensor) for i in range(n_t...]
    unnamed x46 -> x28, local copies, waits for them, and re-layouts: 6.42 us -> 2.36 us
    convert_element_type x4, other arithmetic: 2.81 us -> 0.26 us  [gap(): pick(values, (group_index + hop - rep_index) % n_rep).astype(jnp.bfloat16)]
    ppermute x3, waiting for transfers between devices: 3.82 us -> 1.92 us  [per_device(): lax.ppermute(masked, ('rep', 'sub'), [(i, (i + turn) % n_owners) for i in...]
  transfers between devices with their start and end apart: 26 -> 26, of which waited for: 8 -> 11; matrix products, arithmetic and copies ran while one was open for 6% -> 4% of each run, Pallas kernels for 46% -> 49%
where the time goes in v10:
time: 146 us
  Pallas kernels  72.8 us (50%)
  waiting for transfers between devices  37.2 us (25%)
  starting transfers between devices  28 us (19%)
  local copies, waits for them, and re-layouts  5.41 us (4%)
  other arithmetic  2.35 us (2%)
    pallas_call x5, Pallas kernels, partial_products(): pl.pallas_call(functools.partial(matmul_body, spans, emitted, apart), in_...  69.5 us
    ppermute x9, waiting for transfers between devices, swap_tensor(): return lax.ppermute(value, 'tp', [(i, i ^ bit) for i in range(n_tensor)])  12.8 us
    ppermute x5, waiting for transfers between devices, to_group(): lax.ppermute(value, 'tp', [(i, (i + moved) % n_tensor) for i in range(n_t...  12.7 us
    ppermute x5, starting transfers between devices, to_group(): lax.ppermute(value, 'tp', [(i, (i + moved) % n_tensor) for i in range(n_t...  12 us
    ppermute x4, waiting for transfers between devices, from_rep(): lax.ppermute(value, 'rep', [((i + shift) % n_rep, i) for i in range(n_rep)])  9.73 us
    ppermute x9, starting transfers between devices, swap_tensor(): return lax.ppermute(value, 'tp', [(i, i ^ bit) for i in range(n_tensor)])  9.59 us
    ppermute x4, starting transfers between devices, from_rep(): lax.ppermute(value, 'rep', [((i + shift) % n_rep, i) for i in range(n_rep)])  5.02 us
  transfers between devices with their start and end apart: 26, of which 11 were waited for; matrix products, arithmetic and copies ran while one was open for 4% of the time, Pallas kernels for 49%

profile of v10, /device:TPU:0, one launch (start us, length us, event | category | flops | bytes accessed | tf_op | source)
XLA Modules:
  0.0 146.1 jit_solution(11852929499680596887)
XLA Ops:
  0.5 2.2 %slice.64 = bf16[1,64,7168]{2,1,0:T(8,128)(2,1)} slice(bf16[4,64,7168]{2,1,0:T(8,128)(2,1)} %refs_0_.3), slice={[0:1], [0:64], [0:7168]} | slice | bytes 1835008 | tf_op jit(solution)/shard_map/slice | solution.py:274
  2.7 2.6 %collective-permute-start.3 = (bf16[1,64,7168]{2,1,0:T(8,128)(2,1)}, bf16[1,64,7168]{2,1,0:T(8,128)(2,1)}, u32[]{:S(2)}, u32[]{:S(2)}) collective-permute-start(bf16[1,64,7168]{2,1,0:T(8,128)(2,1)} %slice.64), channel_id=1, source_target_pairs={{2,0},{0,2},{3,1},{1,3},{6,4},{4,6},{7,5},{5,7},{10,8},{8,10},{11,... | collective-permute-start | bytes 2752520 | tf_op jit(solution)/shard_map/ppermute | solution.py:252
  5.3 1.6 %collective-permute-start.4 = (bf16[1,64,2048]{2,1,0:T(8,128)(2,1)S(1)}, bf16[1,64,2048]{2,1,0:T(8,128)(2,1)S(1)}, u32[]{:S(2)}, u32[]{:S(2)}) collective-permute-start(bf16[1,64,2048]{2,1,0:T(8,128)(2,1)S(1)} %copy-done.6), channel_id=1, source_target_pairs={{0,4},{4,0},{8,12},{12,8},{1,5},{5,1},{9,13},{13,9},{2,6},{6,2},{1... | collective-permute-start | bytes 786440 | tf_op jit(solution)/shard_map/ppermute | solution.py:255
  6.9 2.6 %collective-permute-start.5 = (bf16[1,64,2048]{2,1,0:T(8,128)(2,1)S(1)}, bf16[1,64,2048]{2,1,0:T(8,128)(2,1)S(1)}, u32[]{:S(2)}, u32[]{:S(2)}) collective-permute-start(bf16[1,64,2048]{2,1,0:T(8,128)(2,1)S(1)} %copy-done.6), channel_id=1, source_target_pairs={{0,8},{4,12},{8,0},{12,4},{1,9},{5,13},{9,1},{13,5},{2,10},{6,14},... | collective-permute-start | bytes 786440 | tf_op jit(solution)/shard_map/ppermute | solution.py:255
  9.7 21.8 %partial_products.5 = (bf16[192,2176]{1,0:T(8,128)(2,1)}, f32[192,2176]{1,0:T(8,128)S(1)}, bf16[1,64,7168]{2,1,0:T(8,128)(2,1)}, bf16[1,64,7168]{2,1,0:T(8,128)(2,1)S(1)}) custom-call(s32[1]{0:T(128)} %bitcast.1.pos_ref, bf16[4,64,7168]{2,1,0:T(8,128)(2,1)} %refs_0_.3, bf16[4,64,7168]{2,1,0:T(8,128)(2,1)} %collective-permute-done.refs_1_, ...), custom_call_target="tpu_custom_call" | custom-call | tf_op jit(solution)/shard_map/partial_products/pallas_call | solution.py:129
  31.5 0.9 copy-done.12
  34.2 1.5 %collective-permute-start.11 = (bf16[192,2176]{1,0:T(8,128)(2,1)}, bf16[192,2176]{1,0:T(8,128)(2,1)}, u32[]{:S(2)}, u32[]{:S(2)}) collective-permute-start(bf16[192,2176]{1,0:T(8,128)(2,1)} %get-tuple-element.75), channel_id=1, source_target_pairs={{0,4},{4,0},{8,12},{12,8},{1,5},{5,1},{9,13},{13,9},{2,6},{6,2},{1... | collective-permute-start | bytes 2506760 | tf_op jit(solution)/shard_map/ppermute | solution.py:255
  35.9 0.8 reshape.119.slot_ref
  36.7 1.0 collective-permute-start.1
  37.6 15.6 %partial_products.6 = (bf16[128,2176]{1,0:T(8,128)(2,1)S(1)}, f32[128,2176]{1,0:T(8,128)S(1)}, bf16[1,64,7168]{2,1,0:T(8,128)(2,1)S(1)}) custom-call(s32[1]{0:T(128)} %bitcast.1.pos_ref, bf16[4,64,7168]{2,1,0:T(8,128)(2,1)} %refs_0_.3, bf16[4,64,7168]{2,1,0:T(8,128)(2,1)} %collective-permute-done.refs_1_, ...), custom_call_target="tpu_custom_call" | custom-call | tf_op jit(solution)/shard_map/partial_products/pallas_call | solution.py:129
  53.3 4.0 %collective-permute-done.2.refs_0_ = bf16[1,64,7168]{2,1,0:T(8,128)(2,1)S(1)} collective-permute-done((bf16[1,64,7168]{2,1,0:T(8,128)(2,1)}, bf16[1,64,7168]{2,1,0:T(8,128)(2,1)S(1)}, u32[]{:S(2)}, u32[]{:S(2)}) %collective-permute-start.2) | collective-permute-done | bytes 917536 | tf_op jit(solution)/shard_map/ppermute | solution.py:252
  57.4 0.7 collective-permute-start.10
  58.1 1.1 collective-permute-start.13
  59.2 1.3 convert_add_fusion
  60.5 10.7 %partial_products.7 = (bf16[64,2176]{1,0:T(8,128)(2,1)S(1)}, f32[64,2176]{1,0:T(8,128)S(1)}) custom-call(s32[1]{0:T(128)} %bitcast.1.pos_ref, bf16[1,64,7168]{2,1,0:T(8,128)(2,1)S(1)} %collective-permute-done.2.refs_0_, bf16[1,64,7168]{2,1,0:T(8,128)(2,1)S(1)} %collective-permute-done.8.refs_1_, bf16[7168,2048]{1,0:T(8,128)(2,1)} %refs_2_.7, ...), custom_call_target="tpu_custom_call" | custom-call | tf_op jit(solution)/shard_map/partial_products/pallas_call | solution.py:129
  71.2 5.7 %collective-permute-done.1.refs_0_ = bf16[1,64,7168]{2,1,0:T(8,128)(2,1)S(1)} collective-permute-done((bf16[1,64,7168]{2,1,0:T(8,128)(2,1)}, bf16[1,64,7168]{2,1,0:T(8,128)(2,1)S(1)}, u32[]{:S(2)}, u32[]{:S(2)}) %collective-permute-start.1) | collective-permute-done | bytes 917536 | tf_op jit(solution)/shard_map/ppermute | solution.py:252
  76.9 0.7 collective-permute-start.15
  77.8 3.5 %collective-permute-start.12 = (bf16[64,2176]{1,0:T(8,128)(2,1)S(1)}, bf16[64,2176]{1,0:T(8,128)(2,1)S(1)}, u32[]{:S(2)}, u32[]{:S(2)}) collective-permute-start(bf16[64,2176]{1,0:T(8,128)(2,1)S(1)} %select_convert_fusion.2), channel_id=1, source_target_pairs={{0,8},{4,12},{8,0},{12,4},{1,9},{5,13},{9,1},{13,5},{2,10},{6,14},... | collective-permute-start | bytes 835592 | tf_op jit(solution)/shard_map/ppermute | solution.py:259
  81.3 10.7 %partial_products.8 = (bf16[64,2176]{1,0:T(8,128)(2,1)S(1)}, f32[64,2176]{1,0:T(8,128)S(1)}) custom-call(s32[1]{0:T(128)} %bitcast.1.pos_ref, bf16[1,64,7168]{2,1,0:T(8,128)(2,1)S(1)} %collective-permute-done.1.refs_0_, bf16[1,64,7168]{2,1,0:T(8,128)(2,1)S(1)} %collective-permute-done.9.refs_1_, bf16[7168,2048]{1,0:T(8,128)(2,1)} %refs_2_.7, ...), custom_call_target="tpu_custom_call" | custom-call | tf_op jit(solution)/shard_map/partial_products/pallas_call | solution.py:129
  92.2 2.2 %collective-permute-done.12.refs_5_ = bf16[64,2176]{1,0:T(8,128)(2,1)S(1)} collective-permute-done((bf16[64,2176]{1,0:T(8,128)(2,1)S(1)}, bf16[64,2176]{1,0:T(8,128)(2,1)S(1)}, u32[]{:S(2)}, u32[]{:S(2)}) %collective-permute-start.12) | collective-permute-done | bytes 278560 | tf_op jit(solution)/shard_map/ppermute | solution.py:259
  94.6 2.9 %collective-permute-start.17 = (bf16[64,2176]{1,0:T(8,128)(2,1)S(1)}, bf16[64,2176]{1,0:T(8,128)(2,1)S(1)}, u32[]{:S(2)}, u32[]{:S(2)}) collective-permute-start(bf16[64,2176]{1,0:T(8,128)(2,1)S(1)} %select_convert_fusion.1), channel_id=1, source_target_pairs={{0,8},{4,12},{8,0},{12,4},{1,9},{5,13},{9,1},{13,5},{2,10},{6,14},... | collective-permute-start | bytes 835592 | tf_op jit(solution)/shard_map/ppermute | solution.py:259
  97.5 10.8 %collective-permute-done.16 = bf16[64,2176]{1,0:T(8,128)(2,1)S(1)} collective-permute-done((bf16[64,2176]{1,0:T(8,128)(2,1)S(1)}, bf16[64,2176]{1,0:T(8,128)(2,1)S(1)}, u32[]{:S(2)}, u32[]{:S(2)}) %collective-permute-start.16) | collective-permute-done | bytes 278560 | tf_op jit(solution)/shard_map/ppermute | solution.py:255
  108.6 10.7 %partial_products.9 = (bf16[64,2048]{1,0:T(8,128)(2,1)S(1)}, f32[64,2048]{1,0:T(8,128)S(1)}, f32[64,128]{1,0:T(8,128)S(1)}, f32[64,128]{1,0:T(8,128)S(1)}) custom-call(s32[1]{0:T(128)} %bitcast.1.pos_ref, bf16[1,64,7168]{2,1,0:T(8,128)(2,1)S(1)} %collective-permute-done.13.refs_0_, bf16[1,64,7168]{2,1,0:T(8,128)(2,1)S(1)} %collective-permute-done.14.refs_1_, ...), custom_call_target="tpu_custom_call" | custom-call | tf_op jit(solution)/shard_map/partial_products/pallas_call | solution.py:129
  119.3 2.1 %collective-permute-start.19 = (f32[64,128]{1,0:T(8,128)S(1)}, f32[64,128]{1,0:T(8,128)S(1)}, u32[]{:S(2)}, u32[]{:S(2)}) collective-permute-start(f32[64,128]{1,0:T(8,128)S(1)} %get-tuple-element.129), channel_id=1, source_target_pairs={{0,4},{4,0},{8,12},{12,8},{1,5},{5,1},{9,13},{13,9},{2,6},{6,2},{1... | collective-permute-start | bytes 98312 | tf_op jit(solution)/shard_map/ppermute | solution.py:255
  121.9 1.6 %collective-permute-done.19 = f32[64,128]{1,0:T(8,128)S(1)} collective-permute-done((f32[64,128]{1,0:T(8,128)S(1)}, f32[64,128]{1,0:T(8,128)S(1)}, u32[]{:S(2)}, u32[]{:S(2)}) %collective-permute-start.19) | collective-permute-done | bytes 32800 | tf_op jit(solution)/shard_map/ppermute | solution.py:255
  123.5 3.1 %collective-permute-start.20 = (f32[64,128]{1,0:T(8,128)S(1)}, f32[64,128]{1,0:T(8,128)S(1)}, u32[]{:S(2)}, u32[]{:S(2)}) collective-permute-start(f32[64,128]{1,0:T(8,128)S(1)} %get-tuple-element.141), channel_id=1, source_target_pairs={{0,8},{4,12},{8,0},{12,4},{1,9},{5,13},{9,1},{13,5},{2,10},{6,14},... | collective-permute-start | bytes 98312 | tf_op jit(solution)/shard_map/ppermute | solution.py:259
  126.6 2.0 %collective-permute-done.20 = f32[64,128]{1,0:T(8,128)S(1)} collective-permute-done((f32[64,128]{1,0:T(8,128)S(1)}, f32[64,128]{1,0:T(8,128)S(1)}, u32[]{:S(2)}, u32[]{:S(2)}) %collective-permute-start.20) | collective-permute-done | bytes 32800 | tf_op jit(solution)/shard_map/ppermute | solution.py:259
  130.0 2.5 %collective-permute-start.25 = (bf16[64,2048]{1,0:T(8,128)(2,1)S(1)}, bf16[64,2048]{1,0:T(8,128)(2,1)S(1)}, u32[]{:S(2)}, u32[]{:S(2)}) collective-permute-start(bf16[64,2048]{1,0:T(8,128)(2,1)S(1)} %select_convert_fusion.3), channel_id=1, source_target_pairs={{0,8},{4,12},{8,0},{12,4},{1,9},{5,13},{9,1},{13,5},{2,10},{6,14},... | collective-permute-start | bytes 786440 | tf_op jit(solution)/shard_map/ppermute | solution.py:259
  132.6 1.7 %collective-permute-done.23 = bf16[4,64,64]{2,1,0:T(8,128)(2,1)S(1)} collective-permute-done((bf16[4,64,64]{2,1,0:T(8,128)(2,1)S(1)}, bf16[4,64,64]{2,1,0:T(8,128)(2,1)S(1)}, u32[]{:S(2)}, u32[]{:S(2)}) %collective-permute-start.23) | collective-permute-done | bytes 32800 | tf_op jit(solution)/shard_map/ppermute | solution.py:403
  134.6 2.5 %finish_steps.1 = (bf16[4,64,2048]{2,1,0:T(8,128)(2,1)}, bf16[64,2048]{1,0:T(8,128)(2,1)S(1)}) custom-call(bf16[256,64]{1,0:T(8,128)(2,1)S(1)} %bitcast.30, s32[256,1]{1,0:T(8,128)S(1)} %copy-done.3, s32[4]{0:T(128)S(1)} %pad_add_fusion.order_ref, bf16[64,2048]{1,0:T(8,128)(2,1)S(1)} %bitcast.31, bf16[64,2048]{1,0:T(8,128)(2,1)S(1)} %bitcast.32, ...), custom_call_target="tpu_custom_call" | custom-call | tf_op jit(solution)/shard_map/finish_steps/pallas_call | solution.py:184
  137.1 8.1 %collective-permute-done.25.refs_1_ = bf16[64,2048]{1,0:T(8,128)(2,1)S(1)} collective-permute-done((bf16[64,2048]{1,0:T(8,128)(2,1)S(1)}, bf16[64,2048]{1,0:T(8,128)(2,1)S(1)}, u32[]{:S(2)}, u32[]{:S(2)}) %collective-permute-start.25) | collective-permute-done | bytes 262176 | tf_op jit(solution)/shard_map/ppermute | solution.py:259
  145.2 0.8 finish_last.1
  (85 shorter events, 5.8 us)
Async XLA Ops:
  0.0 35.7 %copy-start = (s32[256,1]{0,1:T(1,128)S(1)}, s32[256,1]{0,1:T(1,128)}, u32[]{:S(2)}) copy-start(s32[256,1]{0,1:T(1,128)} %param.10) | copy-start | bytes 3076
  0.0 9.7 %copy-start.2 = (bf16[1,7168,64]{1,2,0:T(8,128)(2,1)S(1)}, bf16[1,7168,64]{1,2,0:T(8,128)(2,1)}, u32[]{:S(2)}) copy-start(bf16[1,7168,64]{1,2,0:T(8,128)(2,1)} %param.8) | copy-start | bytes 2752516
  0.0 9.7 %collective-permute-start = (bf16[4,64,7168]{2,1,0:T(8,128)(2,1)}, bf16[4,64,7168]{2,1,0:T(8,128)(2,1)}, u32[]{:S(2)}, u32[]{:S(2)}) collective-permute-start(bf16[4,64,7168]{2,1,0:T(8,128)(2,1)} %refs_0_.3), channel_id=1, source_target_pairs={{0,1},{1,0},{2,3},{3,2},{4,5},{5,4},{6,7},{7,6},{8,9},{9,8},{10,11... | collective-permute-start | bytes 11010056 | tf_op jit(solution)/shard_map/ppermute | solution.py:249
  2.7 31.1 %collective-permute-start.3 = (bf16[1,64,7168]{2,1,0:T(8,128)(2,1)}, bf16[1,64,7168]{2,1,0:T(8,128)(2,1)}, u32[]{:S(2)}, u32[]{:S(2)}) collective-permute-start(bf16[1,64,7168]{2,1,0:T(8,128)(2,1)} %slice.64), channel_id=1, source_target_pairs={{2,0},{0,2},{3,1},{1,3},{6,4},{4,6},{7,5},{5,7},{10,8},{8,10},{11,... | collective-permute-start | bytes 2752520 | tf_op jit(solution)/shard_map/ppermute | solution.py:252
  5.3 27.2 %collective-permute-start.4 = (bf16[1,64,2048]{2,1,0:T(8,128)(2,1)S(1)}, bf16[1,64,2048]{2,1,0:T(8,128)(2,1)S(1)}, u32[]{:S(2)}, u32[]{:S(2)}) collective-permute-start(bf16[1,64,2048]{2,1,0:T(8,128)(2,1)S(1)} %copy-done.6), channel_id=1, source_target_pairs={{0,4},{4,0},{8,12},{12,8},{1,5},{5,1},{9,13},{13,9},{2,6},{6,2},{1... | collective-permute-start | bytes 786440 | tf_op jit(solution)/shard_map/ppermute | solution.py:255
  6.9 26.3 %collective-permute-start.5 = (bf16[1,64,2048]{2,1,0:T(8,128)(2,1)S(1)}, bf16[1,64,2048]{2,1,0:T(8,128)(2,1)S(1)}, u32[]{:S(2)}, u32[]{:S(2)}) collective-permute-start(bf16[1,64,2048]{2,1,0:T(8,128)(2,1)S(1)} %copy-done.6), channel_id=1, source_target_pairs={{0,8},{4,12},{8,0},{12,4},{1,9},{5,13},{9,1},{13,5},{2,10},{6,14},... | collective-permute-start | bytes 786440 | tf_op jit(solution)/shard_map/ppermute | solution.py:255
  9.4 24.4 %collective-permute-start.6 = (bf16[1,64,2048]{2,1,0:T(8,128)(2,1)S(1)}, bf16[1,64,2048]{2,1,0:T(8,128)(2,1)}, u32[]{:S(2)}, u32[]{:S(2)}) collective-permute-start(bf16[1,64,2048]{2,1,0:T(8,128)(2,1)S(1)} %copy-done.6), channel_id=1, source_target_pairs={{0,12},{4,8},{8,4},{12,0},{1,13},{5,9},{9,5},{13,1},{2,14},{6,10},... | collective-permute-start | bytes 786440 | tf_op jit(solution)/shard_map/ppermute | solution.py:255
  9.7 26.1 %copy-start.13 = (s32[4]{0:T(128)S(1)}, s32[4]{0:T(128)}, u32[]{:S(2)}) copy-start(s32[4]{0:T(128)} %param.11) | copy-start | bytes 52
  33.8 3.8 %collective-permute-start.7 = (bf16[1,64,7168]{2,1,0:T(8,128)(2,1)}, bf16[1,64,7168]{2,1,0:T(8,128)(2,1)}, u32[]{:S(2)}, u32[]{:S(2)}) collective-permute-start(bf16[1,64,7168]{2,1,0:T(8,128)(2,1)} %collective-permute-done.3.refs_2_), channel_id=1, source_target_pairs={{0,1},{1,0},{2,3},{3,2},{4,5},{5,4},{6,7},{7,6},{8,9},{9,8},{10,11... | collective-permute-start | bytes 2752520 | tf_op jit(solution)/shard_map/ppermute | solution.py:249
  33.8 23.4 %collective-permute-start.2 = (bf16[1,64,7168]{2,1,0:T(8,128)(2,1)}, bf16[1,64,7168]{2,1,0:T(8,128)(2,1)S(1)}, u32[]{:S(2)}, u32[]{:S(2)}) collective-permute-start(bf16[1,64,7168]{2,1,0:T(8,128)(2,1)} %get-tuple-element.74), channel_id=1, source_target_pairs={{2,0},{0,2},{3,1},{1,3},{6,4},{4,6},{7,5},{5,7},{10,8},{8,10},{11,... | collective-permute-start | bytes 2752520 | tf_op jit(solution)/shard_map/ppermute | solution.py:252
  34.2 24.9 %collective-permute-start.11 = (bf16[192,2176]{1,0:T(8,128)(2,1)}, bf16[192,2176]{1,0:T(8,128)(2,1)}, u32[]{:S(2)}, u32[]{:S(2)}) collective-permute-start(bf16[192,2176]{1,0:T(8,128)(2,1)} %get-tuple-element.75), channel_id=1, source_target_pairs={{0,4},{4,0},{8,12},{12,8},{1,5},{5,1},{9,13},{13,9},{2,6},{6,2},{1... | collective-permute-start | bytes 2506760 | tf_op jit(solution)/shard_map/ppermute | solution.py:255
  36.7 40.3 %collective-permute-start.1 = (bf16[1,64,7168]{2,1,0:T(8,128)(2,1)}, bf16[1,64,7168]{2,1,0:T(8,128)(2,1)S(1)}, u32[]{:S(2)}, u32[]{:S(2)}) collective-permute-start(bf16[1,64,7168]{2,1,0:T(8,128)(2,1)} %copy-done.12), channel_id=1, source_target_pairs={{2,0},{0,2},{3,1},{1,3},{6,4},{4,6},{7,5},{5,7},{10,8},{8,10},{11,... | collective-permute-start | bytes 2752520 | tf_op jit(solution)/shard_map/ppermute | solution.py:252
  57.3 3.2 %collective-permute-start.8 = (bf16[1,64,7168]{2,1,0:T(8,128)(2,1)S(1)}, bf16[1,64,7168]{2,1,0:T(8,128)(2,1)S(1)}, u32[]{:S(2)}, u32[]{:S(2)}) collective-permute-start(bf16[1,64,7168]{2,1,0:T(8,128)(2,1)S(1)} %collective-permute-done.2.refs_0_), channel_id=1, source_target_pairs={{0,1},{1,0},{2,3},{3,2},{4,5},{5,4},{6,7},{7,6},{8,9},{9,8},{10,11... | collective-permute-start | bytes 2752520 | tf_op jit(solution)/shard_map/ppermute | solution.py:249
  57.4 20.3 %collective-permute-start.10 = (bf16[128,2176]{1,0:T(8,128)(2,1)S(1)}, bf16[128,2176]{1,0:T(8,128)(2,1)S(1)}, u32[]{:S(2)}, u32[]{:S(2)}) collective-permute-start(bf16[128,2176]{1,0:T(8,128)(2,1)S(1)} %get-tuple-element.84), channel_id=1, source_target_pairs={{0,4},{4,0},{8,12},{12,8},{1,5},{5,1},{9,13},{13,9},{2,6},{6,2},{1... | collective-permute-start | bytes 1671176 | tf_op jit(solution)/shard_map/ppermute | solution.py:255
  58.1 39.4 %collective-permute-start.13 = (bf16[1,64,7168]{2,1,0:T(8,128)(2,1)S(1)}, bf16[1,64,7168]{2,1,0:T(8,128)(2,1)S(1)}, u32[]{:S(2)}, u32[]{:S(2)}) collective-permute-start(bf16[1,64,7168]{2,1,0:T(8,128)(2,1)S(1)} %get-tuple-element.105), channel_id=1, source_target_pairs={{2,0},{0,2},{3,1},{1,3},{6,4},{4,6},{7,5},{5,7},{10,8},{8,10},{11,... | collective-permute-start | bytes 2752520 | tf_op jit(solution)/shard_map/ppermute | solution.py:252
  76.9 4.4 %collective-permute-start.9 = (bf16[1,64,7168]{2,1,0:T(8,128)(2,1)S(1)}, bf16[1,64,7168]{2,1,0:T(8,128)(2,1)S(1)}, u32[]{:S(2)}, u32[]{:S(2)}) collective-permute-start(bf16[1,64,7168]{2,1,0:T(8,128)(2,1)S(1)} %collective-permute-done.1.refs_0_), channel_id=1, source_target_pairs={{0,1},{1,0},{2,3},{3,2},{4,5},{5,4},{6,7},{7,6},{8,9},{9,8},{10,11... | collective-permute-start | bytes 2752520 | tf_op jit(solution)/shard_map/ppermute | solution.py:249
  76.9 15.1 %collective-permute-start.15 = (bf16[64,2176]{1,0:T(8,128)(2,1)S(1)}, bf16[64,2176]{1,0:T(8,128)(2,1)S(1)}, u32[]{:S(2)}, u32[]{:S(2)}) collective-permute-start(bf16[64,2176]{1,0:T(8,128)(2,1)S(1)} %get-tuple-element.92), channel_id=1, source_target_pairs={{0,4},{4,0},{8,12},{12,8},{1,5},{5,1},{9,13},{13,9},{2,6},{6,2},{1... | collective-permute-start | bytes 835592 | tf_op jit(solution)/shard_map/ppermute | solution.py:255
  77.8 16.6 %collective-permute-start.12 = (bf16[64,2176]{1,0:T(8,128)(2,1)S(1)}, bf16[64,2176]{1,0:T(8,128)(2,1)S(1)}, u32[]{:S(2)}, u32[]{:S(2)}) collective-permute-start(bf16[64,2176]{1,0:T(8,128)(2,1)S(1)} %select_convert_fusion.2), channel_id=1, source_target_pairs={{0,8},{4,12},{8,0},{12,4},{1,9},{5,13},{9,1},{13,5},{2,10},{6,14},... | collective-permute-start | bytes 835592 | tf_op jit(solution)/shard_map/ppermute | solution.py:259
  94.4 14.1 %copy-start.4 = (bf16[64,2176]{1,0:T(8,128)(2,1)}, bf16[64,2176]{1,0:T(8,128)(2,1)S(1)}, u32[]{:S(2)}) copy-start(bf16[64,2176]{1,0:T(8,128)(2,1)S(1)} %collective-permute-done.12.refs_5_) | copy-start | bytes 835588
  94.4 13.9 %collective-permute-start.16 = (bf16[64,2176]{1,0:T(8,128)(2,1)S(1)}, bf16[64,2176]{1,0:T(8,128)(2,1)S(1)}, u32[]{:S(2)}, u32[]{:S(2)}) collective-permute-start(bf16[64,2176]{1,0:T(8,128)(2,1)S(1)} %get-tuple-element.117), channel_id=1, source_target_pairs={{0,4},{4,0},{8,12},{12,8},{1,5},{5,1},{9,13},{13,9},{2,6},{6,2},{1... | collective-permute-start | bytes 835592 | tf_op jit(solution)/shard_map/ppermute | solution.py:255
  94.6 26.8 %collective-permute-start.17 = (bf16[64,2176]{1,0:T(8,128)(2,1)S(1)}, bf16[64,2176]{1,0:T(8,128)(2,1)S(1)}, u32[]{:S(2)}, u32[]{:S(2)}) collective-permute-start(bf16[64,2176]{1,0:T(8,128)(2,1)S(1)} %select_convert_fusion.1), channel_id=1, source_target_pairs={{0,8},{4,12},{8,0},{12,4},{1,9},{5,13},{9,1},{13,5},{2,10},{6,14},... | collective-permute-start | bytes 835592 | tf_op jit(solution)/shard_map/ppermute | solution.py:259
  97.5 11.1 %collective-permute-start.14 = (bf16[1,64,7168]{2,1,0:T(8,128)(2,1)S(1)}, bf16[1,64,7168]{2,1,0:T(8,128)(2,1)S(1)}, u32[]{:S(2)}, u32[]{:S(2)}) collective-permute-start(bf16[1,64,7168]{2,1,0:T(8,128)(2,1)S(1)} %collective-permute-done.13.refs_0_), channel_id=1, source_target_pairs={{0,1},{1,0},{2,3},{3,2},{4,5},{5,4},{6,7},{7,6},{8,9},{9,8},{10,11... | collective-permute-start | bytes 2752520 | tf_op jit(solution)/shard_map/ppermute | solution.py:249
  108.4 13.5 %collective-permute-start.18 = (bf16[64,2176]{1,0:T(8,128)(2,1)S(1)}, bf16[64,2176]{1,0:T(8,128)(2,1)S(1)}, u32[]{:S(2)}, u32[]{:S(2)}) collective-permute-start(bf16[64,2176]{1,0:T(8,128)(2,1)S(1)} %select_convert_fusion), channel_id=1, source_target_pairs={{0,8},{4,12},{8,0},{12,4},{1,9},{5,13},{9,1},{13,5},{2,10},{6,14},... | collective-permute-start | bytes 835592 | tf_op jit(solution)/shard_map/ppermute | solution.py:259
  108.5 12.9 %slice-start = ((bf16[64,2176]{1,0:T(8,128)(2,1)}), bf16[64,128]{1,0:T(8,128)(2,1)S(1)}, s32[]{:S(2)}) async-start(bf16[64,2176]{1,0:T(8,128)(2,1)} %copy-done.4), calls=%async_computation | async-start | bytes 32768 | tf_op jit(solution)/shard_map/slice | solution.py:389
  119.3 4.3 %collective-permute-start.19 = (f32[64,128]{1,0:T(8,128)S(1)}, f32[64,128]{1,0:T(8,128)S(1)}, u32[]{:S(2)}, u32[]{:S(2)}) collective-permute-start(f32[64,128]{1,0:T(8,128)S(1)} %get-tuple-element.129), channel_id=1, source_target_pairs={{0,4},{4,0},{8,12},{12,8},{1,5},{5,1},{9,13},{13,9},{2,6},{6,2},{1... | collective-permute-start | bytes 98312 | tf_op jit(solution)/shard_map/ppermute | solution.py:255
  121.3 7.7 %collective-permute-start.21 = (bf16[64,2048]{1,0:T(8,128)(2,1)S(1)}, bf16[64,2048]{1,0:T(8,128)(2,1)S(1)}, u32[]{:S(2)}, u32[]{:S(2)}) collective-permute-start(bf16[64,2048]{1,0:T(8,128)(2,1)S(1)} %get-tuple-element.132), channel_id=1, source_target_pairs={{0,4},{4,0},{8,12},{12,8},{1,5},{5,1},{9,13},{13,9},{2,6},{6,2},{1... | collective-permute-start | bytes 786440 | tf_op jit(solution)/shard_map/ppermute | solution.py:255
  123.5 5.1 %collective-permute-start.20 = (f32[64,128]{1,0:T(8,128)S(1)}, f32[64,128]{1,0:T(8,128)S(1)}, u32[]{:S(2)}, u32[]{:S(2)}) collective-permute-start(f32[64,128]{1,0:T(8,128)S(1)} %get-tuple-element.141), channel_id=1, source_target_pairs={{0,8},{4,12},{8,0},{12,4},{1,9},{5,13},{9,1},{13,5},{2,10},{6,14},... | collective-permute-start | bytes 98312 | tf_op jit(solution)/shard_map/ppermute | solution.py:259
  129.2 3.3 %collective-permute-start.24 = (bf16[4,64,64]{2,1,0:T(8,128)(2,1)S(1)}, bf16[4,64,64]{2,1,0:T(8,128)(2,1)S(1)}, u32[]{:S(2)}, u32[]{:S(2)}) collective-permute-start(bf16[4,64,64]{2,1,0:T(8,128)(2,1)S(1)} %select_bitcast_fusion), channel_id=1, source_target_pairs={{0,3},{1,0},{2,1},{3,2},{4,7},{5,4},{6,5},{7,6},{8,11},{9,8},{10,9... | collective-permute-start | bytes 98312 | tf_op jit(solution)/shard_map/ppermute | solution.py:403
  129.3 5.0 %collective-permute-start.23 = (bf16[4,64,64]{2,1,0:T(8,128)(2,1)S(1)}, bf16[4,64,64]{2,1,0:T(8,128)(2,1)S(1)}, u32[]{:S(2)}, u32[]{:S(2)}) collective-permute-start(bf16[4,64,64]{2,1,0:T(8,128)(2,1)S(1)} %select_bitcast_fusion), channel_id=1, source_target_pairs={{0,2},{1,3},{2,0},{3,1},{4,6},{5,7},{6,4},{7,5},{8,10},{9,11},{10,... | collective-permute-start | bytes 98312 | tf_op jit(solution)/shard_map/ppermute | solution.py:403
  129.8 4.7 %collective-permute-start.22 = (bf16[4,64,64]{2,1,0:T(8,128)(2,1)S(1)}, bf16[4,64,64]{2,1,0:T(8,128)(2,1)S(1)}, u32[]{:S(2)}, u32[]{:S(2)}) collective-permute-start(bf16[4,64,64]{2,1,0:T(8,128)(2,1)S(1)} %select_bitcast_fusion), channel_id=1, source_target_pairs={{0,1},{1,2},{2,3},{3,0},{4,5},{5,6},{6,7},{7,4},{8,9},{9,10},{10,1... | collective-permute-start | bytes 98312 | tf_op jit(solution)/shard_map/ppermute | solution.py:403
  130.0 15.3 %collective-permute-start.25 = (bf16[64,2048]{1,0:T(8,128)(2,1)S(1)}, bf16[64,2048]{1,0:T(8,128)(2,1)S(1)}, u32[]{:S(2)}, u32[]{:S(2)}) collective-permute-start(bf16[64,2048]{1,0:T(8,128)(2,1)S(1)} %select_convert_fusion.3), channel_id=1, source_target_pairs={{0,8},{4,12},{8,0},{12,4},{1,9},{5,13},{9,1},{13,5},{2,10},{6,14},... | collective-permute-start | bytes 786440 | tf_op jit(solution)/shard_map/ppermute | solution.py:259
  134.6 11.4 %copy-start.1 = (s32[256,1]{0,1:T(1,128)S(1)}, s32[256,1]{0,1:T(1,128)}, u32[]{:S(2)}) copy-start(s32[256,1]{0,1:T(1,128)} %param.10) | copy-start | bytes 3076
  (9 other events, 37.1 us)

commit v11 on v10

--- a/solution.py
+++ b/solution.py
@@ -12,7 +12,7 @@
 BLOCK = 1024
 BUFFERS = 4
 RANK_NAME = 1000
-VMEM_BYTES = 22 * 1024 * 1024
+VMEM_BYTES = 17 * 1024 * 1024
 
 
 def block_shape(depth, width):
@@ -305,7 +305,7 @@
             bit //= 2
         return total.reshape(steps, extent, columns)
 
-    def gap(token, jobs, short=False):
+    def gap(token, jobs, held_back=False):
         nonlocal first_leg, second_leg
         for parts, received, keep, kind in first_leg:
             steps = sum(length for _, length in parts)
@@ -316,12 +316,7 @@
                     if (key[0] + at - begin, key[1]) == (step_count - 1, 0):
                         halved[RANK_NAME, 0] = total[at][:, width:]
                 begin += length
-        closed, waiting = {}, []
-        for name, kept, received, lag in second_leg:
-            if short or lag > 1:
-                waiting.append((name, kept, received, lag if short else lag - 1))
-            else:
-                closed[name] = (after(kept, token), *received)
+        closed = {name: (after(kept, token), *received) for name, kept, received in second_leg}
         started, sends = [], []
         for name in sorted({name for name, _ in halved}):
             if name in begun or name == RANK_NAME or any((name, at) not in halved for at in range(n_rep)):
@@ -336,54 +331,57 @@
             ])
             started.append((name, kept))
         sends, token = lax.optimization_barrier((sends, token))
-        first_sends, closed = lax.optimization_barrier(([job[1] for job in jobs], closed))
+        first_sends = [job[1] for job in jobs]
+        if held_back:
+            first_sends, closed = lax.optimization_barrier((first_sends, closed))
         ended.update(closed)
         first_leg = [
             (parts, swap_tensor(send, group // 2), keep, kind) for (parts, _, keep, kind), send in zip(jobs, first_sends)
         ]
-        second_leg = waiting + [
-            (name, kept, [to_group(value, hop + 1) for hop, value in enumerate(sent)], 2 if short else 1)
+        second_leg = [
+            (name, kept, [to_group(value, hop + 1) for hop, value in enumerate(sent)])
             for (name, kept), sent in zip(started, sends)
         ]
-        return sends
+        return sends, closed
 
     factors = jnp.swapaxes(down_a, 1, 2)
 
-    lead = step_count - 1
-    parts, last_ranks = [((0, 0), lead)], {}
+    lead = step_count // 2
+    parts, last_ranks, next_local = [((0, 0), lead)], {}, lead
     send, keep, *emitted = partial_products(
         pos, [(source, siblings, 0, lead)], weight, factors, emitted=tuple(range(1, lead))
     )
     for step, rows in enumerate(emitted, 1):
         remote.update({(step, shift): from_rep(rows, shift) for shift in range(1, n_rep)})
     for piece, (step, shift) in enumerate(pieces):
-        sends = gap(send, [(parts, send, keep, jnp.bfloat16)])
-        own, panels, _ = lax.optimization_barrier((remote[step, shift], panels, send))
+        sends, closed = gap(send, [(parts, send, keep, jnp.bfloat16)])
+        own, panels, closed, _ = lax.optimization_barrier((remote[step, shift], panels, closed, send))
+        ended.update(closed)
         if piece == 0:
             panels, order = spread_panels(panels, order, bits[2:])
         sib = swap_cores(own)
-        held = [sends, siblings] if piece == 0 else [sends]
-        if piece == len(pieces) - 1:
-            held += gap(lax.optimization_barrier((send, sends))[0], [], short=True)
-        own, sib, held = lax.optimization_barrier((own, sib, held))
+        own, sib, siblings, _ = lax.optimization_barrier((own, sib, siblings, sends))
         last, chunks, parts, places = step == step_count - 1, [(own, sib, 0, 1)], [((step, shift), 1)], ()
-        if piece == 0:
-            chunks.insert(0, (source, held[1], lead, 1))
-            parts.insert(0, ((lead, 0), 1))
+        if next_local < step_count:
+            chunks.insert(0, (source, siblings, next_local, 1))
+            parts.insert(0, ((next_local, 0), 1))
             places = (0,)
         send, keep, *outs = partial_products(pos, chunks, weight, factors, last, places)
         if last:
             last_ranks[shift] = outs
         elif outs:
-            remote.update({(lead, along): from_rep(outs[0], along) for along in range(1, n_rep)})
-    gap(send, [(parts, send, keep, jnp.bfloat16)])
+            remote.update({(next_local, along): from_rep(outs[0], along) for along in range(1, n_rep)})
+            next_local += 1
+    gap(send, [(parts, send, keep, jnp.bfloat16)], held_back=True)
     for shift, ranks in last_ranks.items():
         halved[RANK_NAME, shift] = second_half(ranks[1], swap_tensor(ranks[0], group // 2), 1, jnp.float32)[0]
     values = [halved[RANK_NAME, at] for at in range(n_rep)]
     ended[RANK_NAME] = (pick(values, (group_index - rep_index) % n_rep), *[
         to_group(pick(values, (group_index + hop - rep_index) % n_rep), hop) for hop in range(1, n_rep)
     ])
-    rounded = gap(send, [])
+    rounded, _ = gap(send, [])
+    kept, *received = ended[RANK_NAME]
+    ended[RANK_NAME] = (after(kept, rounded), *received)
 
     def rank_sum(name):
         kept, *received = [value[:, -rank_columns(factors):] for value in ended[name]]
@@ -394,7 +392,7 @@
     finished = jnp.stack([rank_sum(step) for step in range(step_count - 1)] + [rank_sum(RANK_NAME)])
     finished = finished.astype(jnp.bfloat16).reshape(step_count, rows_mine, owned_slots, rank_size)
     finished = lax.optimization_barrier((finished, rounded))[0]
-    ended.update((name, (kept, *received)) for name, kept, received, _ in second_leg)
+    ended.update((name, (kept, *received)) for name, kept, received in second_leg)
     masked = jnp.sum(
         jnp.where(owned_hot[None, :, :, None], finished, 0), axis=2, dtype=jnp.float32
     ).astype(jnp.bfloat16)

time: 146 us -> 154 us (1.055)
  starting transfers between devices: 28 us -> 33.3 us
  other arithmetic: 2.35 us -> 5.01 us
  local copies, waits for them, and re-layouts: 5.41 us -> 7.63 us
  Pallas kernels: 72.8 us -> 70.8 us
    ppermute x9, starting transfers between devices: 9.59 us -> 19.3 us  [swap_tensor(): return lax.ppermute(value, 'tp', [(i, i ^ bit) for i in range(n_tensor)])]
    ppermute x5, starting transfers between devices: 12 us -> 6.67 us  [to_group(): lax.ppermute(value, 'tp', [(i, (i + moved) % n_tensor) for i in range(n_t...]
    ppermute x5, waiting for transfers between devices: 12.7 us -> 17.8 us  [to_group(): lax.ppermute(value, 'tp', [(i, (i + moved) % n_tensor) for i in range(n_t...]
    ppermute x9, waiting for transfers between devices: 12.8 us -> 8.69 us  [swap_tensor(): return lax.ppermute(value, 'tp', [(i, i ^ bit) for i in range(n_tensor)])]
    ppermute x4, waiting for transfers between devices: 9.73 us -> 5.71 us  [from_rep(): lax.ppermute(value, 'rep', [((i + shift) % n_rep, i) for i in range(n_rep)])]
    pallas_call x5, Pallas kernels: 69.5 us -> 67.4 us  [partial_products(): pl.pallas_call(functools.partial(matmul_body, spans, emitted, apart), in_...]
    ppermute x3, waiting for transfers between devices: 1.92 us -> 3.82 us  [per_device(): lax.ppermute(masked, ('rep', 'sub'), [(i, (i + turn) % n_owners) for i in...]
    convert_element_type x4, other arithmetic: 0.26 us -> 1.95 us  [gap(): pick(values, (group_index + hop - rep_index) % n_rep).astype(jnp.bfloat16)]
  transfers between devices with their start and end apart: 26 -> 26, of which waited for: 11 -> 9; matrix products, arithmetic and copies ran while one was open for 4% -> 6% of each run, Pallas kernels for 49% -> 46%
where the time goes in v11:
time: 154 us
  Pallas kernels  70.8 us (46%)
  waiting for transfers between devices  36.6 us (24%)
  starting transfers between devices  33.3 us (22%)
  local copies, waits for them, and re-layouts  7.63 us (5%)
  other arithmetic  5.01 us (3%)
    pallas_call x5, Pallas kernels, partial_products(): pl.pallas_call(functools.partial(matmul_body, spans, emitted, apart), in_...  67.4 us
    ppermute x9, starting transfers between devices, swap_tensor(): return lax.ppermute(value, 'tp', [(i, i ^ bit) for i in range(n_tensor)])  19.3 us
    ppermute x5, waiting for transfers between devices, to_group(): lax.ppermute(value, 'tp', [(i, (i + moved) % n_tensor) for i in range(n_t...  17.8 us
    ppermute x9, waiting for transfers between devices, swap_tensor(): return lax.ppermute(value, 'tp', [(i, i ^ bit) for i in range(n_tensor)])  8.69 us
    ppermute x5, starting transfers between devices, to_group(): lax.ppermute(value, 'tp', [(i, (i + moved) % n_tensor) for i in range(n_t...  6.67 us
    ppermute x4, starting transfers between devices, from_rep(): lax.ppermute(value, 'rep', [((i + shift) % n_rep, i) for i in range(n_rep)])  5.74 us
    ppermute x4, waiting for transfers between devices, from_rep(): lax.ppermute(value, 'rep', [((i + shift) % n_rep, i) for i in range(n_rep)])  5.71 us
    unnamed x36, local copies, waits for them, and re-layouts  3.86 us
  transfers between devices with their start and end apart: 26, of which 9 were waited for; matrix products, arithmetic and copies ran while one was open for 6% of the time, Pallas kernels for 46%

profile of v11, /device:TPU:0, one launch (start us, length us, event | category | flops | bytes accessed | tf_op | source)
XLA Modules:
  0.0 153.8 jit_solution(7406943031573243772)
XLA Ops:
  0.5 2.2 %slice.68 = bf16[1,64,7168]{2,1,0:T(8,128)(2,1)} slice(bf16[4,64,7168]{2,1,0:T(8,128)(2,1)} %refs_0_.5), slice={[0:1], [0:64], [0:7168]} | slice | bytes 1835008 | tf_op jit(solution)/shard_map/slice | solution.py:274
  2.7 2.6 %collective-permute-start.2 = (bf16[1,64,7168]{2,1,0:T(8,128)(2,1)}, bf16[1,64,7168]{2,1,0:T(8,128)(2,1)S(1)}, u32[]{:S(2)}, u32[]{:S(2)}) collective-permute-start(bf16[1,64,7168]{2,1,0:T(8,128)(2,1)} %slice.68), channel_id=1, source_target_pairs={{2,0},{0,2},{3,1},{1,3},{6,4},{4,6},{7,5},{5,7},{10,8},{8,10},{11,... | collective-permute-start | bytes 2752520 | tf_op jit(solution)/shard_map/ppermute | solution.py:252
  5.3 2.6 %collective-permute-start.4 = (bf16[1,64,2048]{2,1,0:T(8,128)(2,1)S(1)}, bf16[1,64,2048]{2,1,0:T(8,128)(2,1)S(1)}, u32[]{:S(2)}, u32[]{:S(2)}) collective-permute-start(bf16[1,64,2048]{2,1,0:T(8,128)(2,1)S(1)} %copy-done.8), channel_id=1, source_target_pairs={{0,8},{4,12},{8,0},{12,4},{1,9},{5,13},{9,1},{13,5},{2,10},{6,14},... | collective-permute-start | bytes 786440 | tf_op jit(solution)/shard_map/ppermute | solution.py:255
  7.9 1.6 %collective-permute-start.3 = (bf16[1,64,2048]{2,1,0:T(8,128)(2,1)S(1)}, bf16[1,64,2048]{2,1,0:T(8,128)(2,1)}, u32[]{:S(2)}, u32[]{:S(2)}) collective-permute-start(bf16[1,64,2048]{2,1,0:T(8,128)(2,1)S(1)} %copy-done.8), channel_id=1, source_target_pairs={{0,4},{4,0},{8,12},{12,8},{1,5},{5,1},{9,13},{13,9},{2,6},{6,2},{1... | collective-permute-start | bytes 786440 | tf_op jit(solution)/shard_map/ppermute | solution.py:255
  9.7 16.4 %partial_products.5 = (bf16[128,2176]{1,0:T(8,128)(2,1)}, f32[128,2176]{1,0:T(8,128)S(1)}, bf16[1,64,7168]{2,1,0:T(8,128)(2,1)}) custom-call(s32[1]{0:T(128)} %bitcast.1.pos_ref, bf16[4,64,7168]{2,1,0:T(8,128)(2,1)} %refs_0_.5, bf16[4,64,7168]{2,1,0:T(8,128)(2,1)} %collective-permute-done.refs_1_, bf16[7168,2048]{1,0:T(8,128)(2,1)} %refs_2_.5, ...), custom_call_target="tpu_custom_call" | custom-call | tf_op jit(solution)/shard_map/partial_products/pallas_call | solution.py:129
  27.1 1.0 copy-done.3
  28.0 1.1 collective-permute-start.1
  29.1 4.5 %collective-permute-start.11 = (bf16[128,2176]{1,0:T(8,128)(2,1)}, bf16[128,2176]{1,0:T(8,128)(2,1)}, u32[]{:S(2)}, u32[]{:S(2)}) collective-permute-start(bf16[128,2176]{1,0:T(8,128)(2,1)} %get-tuple-element.72), channel_id=1, source_target_pairs={{0,4},{4,0},{8,12},{12,8},{1,5},{5,1},{9,13},{13,9},{2,6},{6,2},{1... | collective-permute-start | bytes 1671176 | tf_op jit(solution)/shard_map/ppermute | solution.py:255
  33.6 1.2 copy-done.4
  34.8 13.4 %partial_products.6 = (bf16[128,2176]{1,0:T(8,128)(2,1)S(1)}, f32[128,2176]{1,0:T(8,128)S(1)}, bf16[1,64,7168]{2,1,0:T(8,128)(2,1)}) custom-call(s32[1]{0:T(128)} %bitcast.1.pos_ref, bf16[4,64,7168]{2,1,0:T(8,128)(2,1)} %refs_0_.5, bf16[4,64,7168]{2,1,0:T(8,128)(2,1)} %collective-permute-done.refs_1_, bf16[1,64,7168]{2,1,0:T(8,128)(2,1)S(1)} %copy-done.4, ...), custom_call_target="tpu_custom_call" | custom-call | tf_op jit(solution)/shard_map/partial_products/pallas_call | solution.py:129
  48.2 0.9 copy-done.12
  49.1 1.5 collective-permute-start.9
  51.3 5.4 %collective-permute-start.10 = (bf16[128,2176]{1,0:T(8,128)(2,1)}, bf16[128,2176]{1,0:T(8,128)(2,1)S(1)}, u32[]{:S(2)}, u32[]{:S(2)}) collective-permute-start(bf16[128,2176]{1,0:T(8,128)(2,1)} %copy-done.12), channel_id=1, source_target_pairs={{0,4},{4,0},{8,12},{12,8},{1,5},{5,1},{9,13},{13,9},{2,6},{6,2},{1... | collective-permute-start | bytes 1671176 | tf_op jit(solution)/shard_map/ppermute | solution.py:255
  56.7 1.2 convert_add_fusion.1
  57.9 15.7 %partial_products.7 = (bf16[128,2176]{1,0:T(8,128)(2,1)S(1)}, f32[128,2176]{1,0:T(8,128)S(1)}, bf16[1,64,7168]{2,1,0:T(8,128)(2,1)S(1)}) custom-call(s32[1]{0:T(128)} %bitcast.1.pos_ref, bf16[4,64,7168]{2,1,0:T(8,128)(2,1)} %refs_0_.5, bf16[4,64,7168]{2,1,0:T(8,128)(2,1)} %collective-permute-done.refs_1_, ...), custom_call_target="tpu_custom_call" | custom-call | tf_op jit(solution)/shard_map/partial_products/pallas_call | solution.py:129
  73.6 1.5 collective-permute-start.15
  75.3 2.8 %collective-permute-start.13 = (bf16[64,2176]{1,0:T(8,128)(2,1)S(1)}, bf16[64,2176]{1,0:T(8,128)(2,1)S(1)}, u32[]{:S(2)}, u32[]{:S(2)}) collective-permute-start(bf16[64,2176]{1,0:T(8,128)(2,1)S(1)} %select_convert_fusion.2), channel_id=1, source_target_pairs={{0,8},{4,12},{8,0},{12,4},{1,9},{5,13},{9,1},{13,5},{2,10},{6,14},... | collective-permute-start | bytes 835592 | tf_op jit(solution)/shard_map/ppermute | solution.py:259
  78.6 11.2 %partial_products.8 = (bf16[64,2176]{1,0:T(8,128)(2,1)}, f32[64,2176]{1,0:T(8,128)S(1)}) custom-call(s32[1]{0:T(128)} %bitcast.1.pos_ref, bf16[1,64,7168]{2,1,0:T(8,128)(2,1)} %collective-permute-done.9.refs_0_, bf16[1,64,7168]{2,1,0:T(8,128)(2,1)S(1)} %collective-permute-done.12.refs_1_, bf16[7168,2048]{1,0:T(8,128)(2,1)} %refs_2_.5, ...), custom_call_target="tpu_custom_call" | custom-call | tf_op jit(solution)/shard_map/partial_products/pallas_call | solution.py:129
  89.8 1.4 collective-permute-start.17
  91.2 3.9 %collective-permute-done.15 = bf16[128,2176]{1,0:T(8,128)(2,1)S(1)} collective-permute-done((bf16[128,2176]{1,0:T(8,128)(2,1)S(1)}, bf16[128,2176]{1,0:T(8,128)(2,1)S(1)}, u32[]{:S(2)}, u32[]{:S(2)}) %collective-permute-start.15) | collective-permute-done | bytes 557088 | tf_op jit(solution)/shard_map/ppermute | solution.py:255
  95.3 5.2 %collective-permute-done.8.refs_0_ = bf16[1,64,7168]{2,1,0:T(8,128)(2,1)S(1)} collective-permute-done((bf16[1,64,7168]{2,1,0:T(8,128)(2,1)S(1)}, bf16[1,64,7168]{2,1,0:T(8,128)(2,1)S(1)}, u32[]{:S(2)}, u32[]{:S(2)}) %collective-permute-start.8) | collective-permute-done | bytes 917536 | tf_op jit(solution)/shard_map/ppermute | solution.py:252
  103.1 10.7 %partial_products.9 = (bf16[64,2048]{1,0:T(8,128)(2,1)S(1)}, f32[64,2048]{1,0:T(8,128)S(1)}, f32[64,128]{1,0:T(8,128)S(1)}, f32[64,128]{1,0:T(8,128)S(1)}) custom-call(s32[1]{0:T(128)} %bitcast.1.pos_ref, bf16[1,64,7168]{2,1,0:T(8,128)(2,1)S(1)} %collective-permute-done.8.refs_0_, bf16[1,64,7168]{2,1,0:T(8,128)(2,1)} %collective-permute-done.14.refs_1_, ...), custom_call_target="tpu_custom_call" | custom-call | tf_op jit(solution)/shard_map/partial_products/pallas_call | solution.py:129
  113.8 3.7 %collective-permute-done.16.refs_7_ = bf16[64,2176]{1,0:T(8,128)(2,1)} collective-permute-done((bf16[64,2176]{1,0:T(8,128)(2,1)}, bf16[64,2176]{1,0:T(8,128)(2,1)}, u32[]{:S(2)}, u32[]{:S(2)}) %collective-permute-start.16) | collective-permute-done | bytes 278560 | tf_op jit(solution)/shard_map/ppermute | solution.py:259
  118.3 2.0 %collective-permute-start.20 = (bf16[64,2048]{1,0:T(8,128)(2,1)S(1)}, bf16[64,2048]{1,0:T(8,128)(2,1)S(1)}, u32[]{:S(2)}, u32[]{:S(2)}) collective-permute-start(bf16[64,2048]{1,0:T(8,128)(2,1)S(1)} %get-tuple-element.127), channel_id=1, source_target_pairs={{0,4},{4,0},{8,12},{12,8},{1,5},{5,1},{9,13},{13,9},{2,6},{6,2},{1... | collective-permute-start | bytes 786440 | tf_op jit(solution)/shard_map/ppermute | solution.py:255
  120.3 1.0 select_convert_fusion
  121.5 1.1 slice_select_fusion.refs_8_
  122.7 2.8 %collective-permute-start.21 = (f32[64,128]{1,0:T(8,128)S(1)}, f32[64,128]{1,0:T(8,128)S(1)}, u32[]{:S(2)}, u32[]{:S(2)}) collective-permute-start(f32[64,128]{1,0:T(8,128)S(1)} %get-tuple-element.138), channel_id=1, source_target_pairs={{0,8},{4,12},{8,0},{12,4},{1,9},{5,13},{9,1},{13,5},{2,10},{6,14},... | collective-permute-start | bytes 98312 | tf_op jit(solution)/shard_map/ppermute | solution.py:259
  125.6 4.6 %collective-permute-done.20 = bf16[64,2048]{1,0:T(8,128)(2,1)S(1)} collective-permute-done((bf16[64,2048]{1,0:T(8,128)(2,1)S(1)}, bf16[64,2048]{1,0:T(8,128)(2,1)S(1)}, u32[]{:S(2)}, u32[]{:S(2)}) %collective-permute-start.20) | collective-permute-done | bytes 262176 | tf_op jit(solution)/shard_map/ppermute | solution.py:255
  130.9 14.1 %collective-permute-done.21 = f32[64,128]{1,0:T(8,128)S(1)} collective-permute-done((f32[64,128]{1,0:T(8,128)S(1)}, f32[64,128]{1,0:T(8,128)S(1)}, u32[]{:S(2)}, u32[]{:S(2)}) %collective-permute-start.21) | collective-permute-done | bytes 32800 | tf_op jit(solution)/shard_map/ppermute | solution.py:259
  146.3 3.8 %collective-permute-done.23 = bf16[4,64,64]{2,1,0:T(8,128)(2,1)S(1)} collective-permute-done((bf16[4,64,64]{2,1,0:T(8,128)(2,1)S(1)}, bf16[4,64,64]{2,1,0:T(8,128)(2,1)S(1)}, u32[]{:S(2)}, u32[]{:S(2)}) %collective-permute-start.23) | collective-permute-done | bytes 32800 | tf_op jit(solution)/shard_map/ppermute | solution.py:401
  150.3 2.7 %finish_steps.1 = (bf16[4,64,2048]{2,1,0:T(8,128)(2,1)}, bf16[64,2048]{1,0:T(8,128)(2,1)S(1)}) custom-call(bf16[256,64]{1,0:T(8,128)(2,1)S(1)} %bitcast.30, s32[256,1]{1,0:T(8,128)S(1)} %copy-done.5, s32[4]{0:T(128)S(1)} %pad_add_fusion.order_ref, bf16[64,2048]{1,0:T(8,128)(2,1)S(1)} %bitcast.31, bf16[64,2048]{1,0:T(8,128)(2,1)} %bitcast.14.refs_1_, ...), custom_call_target="tpu_custom_call" | custom-call | tf_op jit(solution)/shard_map/finish_steps/pallas_call | solution.py:184
  153.0 0.8 finish_last.1
  (94 shorter events, 8.9 us)
Async XLA Ops:
  0.0 51.1 %copy-start = (s32[256,1]{0,1:T(1,128)S(1)}, s32[256,1]{0,1:T(1,128)}, u32[]{:S(2)}) copy-start(s32[256,1]{0,1:T(1,128)} %param.10) | copy-start | bytes 3076
  0.0 9.7 %copy-start.2 = (bf16[1,7168,64]{1,2,0:T(8,128)(2,1)S(1)}, bf16[1,7168,64]{1,2,0:T(8,128)(2,1)}, u32[]{:S(2)}) copy-start(bf16[1,7168,64]{1,2,0:T(8,128)(2,1)} %param.8) | copy-start | bytes 2752516
  0.0 9.7 %collective-permute-start = (bf16[4,64,7168]{2,1,0:T(8,128)(2,1)}, bf16[4,64,7168]{2,1,0:T(8,128)(2,1)}, u32[]{:S(2)}, u32[]{:S(2)}) collective-permute-start(bf16[4,64,7168]{2,1,0:T(8,128)(2,1)} %refs_0_.5), channel_id=1, source_target_pairs={{0,1},{1,0},{2,3},{3,2},{4,5},{5,4},{6,7},{7,6},{8,9},{9,8},{10,11... | collective-permute-start | bytes 11010056 | tf_op jit(solution)/shard_map/ppermute | solution.py:249
  2.7 24.4 %collective-permute-start.2 = (bf16[1,64,7168]{2,1,0:T(8,128)(2,1)}, bf16[1,64,7168]{2,1,0:T(8,128)(2,1)S(1)}, u32[]{:S(2)}, u32[]{:S(2)}) collective-permute-start(bf16[1,64,7168]{2,1,0:T(8,128)(2,1)} %slice.68), channel_id=1, source_target_pairs={{2,0},{0,2},{3,1},{1,3},{6,4},{4,6},{7,5},{5,7},{10,8},{8,10},{11,... | collective-permute-start | bytes 2752520 | tf_op jit(solution)/shard_map/ppermute | solution.py:252
  5.3 20.8 %collective-permute-start.4 = (bf16[1,64,2048]{2,1,0:T(8,128)(2,1)S(1)}, bf16[1,64,2048]{2,1,0:T(8,128)(2,1)S(1)}, u32[]{:S(2)}, u32[]{:S(2)}) collective-permute-start(bf16[1,64,2048]{2,1,0:T(8,128)(2,1)S(1)} %copy-done.8), channel_id=1, source_target_pairs={{0,8},{4,12},{8,0},{12,4},{1,9},{5,13},{9,1},{13,5},{2,10},{6,14},... | collective-permute-start | bytes 786440 | tf_op jit(solution)/shard_map/ppermute | solution.py:255
  7.9 19.0 %collective-permute-start.3 = (bf16[1,64,2048]{2,1,0:T(8,128)(2,1)S(1)}, bf16[1,64,2048]{2,1,0:T(8,128)(2,1)}, u32[]{:S(2)}, u32[]{:S(2)}) collective-permute-start(bf16[1,64,2048]{2,1,0:T(8,128)(2,1)S(1)} %copy-done.8), channel_id=1, source_target_pairs={{0,4},{4,0},{8,12},{12,8},{1,5},{5,1},{9,13},{13,9},{2,6},{6,2},{1... | collective-permute-start | bytes 786440 | tf_op jit(solution)/shard_map/ppermute | solution.py:255
  9.4 17.6 %collective-permute-start.5 = (bf16[1,64,2048]{2,1,0:T(8,128)(2,1)S(1)}, bf16[1,64,2048]{2,1,0:T(8,128)(2,1)}, u32[]{:S(2)}, u32[]{:S(2)}) collective-permute-start(bf16[1,64,2048]{2,1,0:T(8,128)(2,1)S(1)} %copy-done.8), channel_id=1, source_target_pairs={{0,12},{4,8},{8,4},{12,0},{1,13},{5,9},{9,5},{13,1},{2,14},{6,10},... | collective-permute-start | bytes 786440 | tf_op jit(solution)/shard_map/ppermute | solution.py:255
  27.0 6.6 %collective-permute-start.6 = (bf16[1,64,7168]{2,1,0:T(8,128)(2,1)S(1)}, bf16[1,64,7168]{2,1,0:T(8,128)(2,1)}, u32[]{:S(2)}, u32[]{:S(2)}) collective-permute-start(bf16[1,64,7168]{2,1,0:T(8,128)(2,1)S(1)} %collective-permute-done.2.refs_2_), channel_id=1, source_target_pairs={{0,1},{1,0},{2,3},{3,2},{4,5},{5,4},{6,7},{7,6},{8,9},{9,8},{10,11... | collective-permute-start | bytes 2752520 | tf_op jit(solution)/shard_map/ppermute | solution.py:249
  28.0 23.1 %collective-permute-start.1 = (bf16[1,64,7168]{2,1,0:T(8,128)(2,1)}, bf16[1,64,7168]{2,1,0:T(8,128)(2,1)}, u32[]{:S(2)}, u32[]{:S(2)}) collective-permute-start(bf16[1,64,7168]{2,1,0:T(8,128)(2,1)} %get-tuple-element.71), channel_id=1, source_target_pairs={{2,0},{0,2},{3,1},{1,3},{6,4},{4,6},{7,5},{5,7},{10,8},{8,10},{11,... | collective-permute-start | bytes 2752520 | tf_op jit(solution)/shard_map/ppermute | solution.py:252
  29.1 27.6 %collective-permute-start.11 = (bf16[128,2176]{1,0:T(8,128)(2,1)}, bf16[128,2176]{1,0:T(8,128)(2,1)}, u32[]{:S(2)}, u32[]{:S(2)}) collective-permute-start(bf16[128,2176]{1,0:T(8,128)(2,1)} %get-tuple-element.72), channel_id=1, source_target_pairs={{0,4},{4,0},{8,12},{12,8},{1,5},{5,1},{9,13},{13,9},{2,6},{6,2},{1... | collective-permute-start | bytes 1671176 | tf_op jit(solution)/shard_map/ppermute | solution.py:255
  34.8 16.4 %copy-start.17 = (s32[4]{0:T(128)S(1)}, s32[4]{0:T(128)}, u32[]{:S(2)}) copy-start(s32[4]{0:T(128)} %param.11) | copy-start | bytes 52
  49.1 26.0 %collective-permute-start.9 = (bf16[1,64,7168]{2,1,0:T(8,128)(2,1)}, bf16[1,64,7168]{2,1,0:T(8,128)(2,1)}, u32[]{:S(2)}, u32[]{:S(2)}) collective-permute-start(bf16[1,64,7168]{2,1,0:T(8,128)(2,1)} %get-tuple-element.87), channel_id=1, source_target_pairs={{2,0},{0,2},{3,1},{1,3},{6,4},{4,6},{7,5},{5,7},{10,8},{8,10},{11,... | collective-permute-start | bytes 2752520 | tf_op jit(solution)/shard_map/ppermute | solution.py:252
  51.1 6.8 %collective-permute-start.7 = (bf16[1,64,7168]{2,1,0:T(8,128)(2,1)}, bf16[1,64,7168]{2,1,0:T(8,128)(2,1)}, u32[]{:S(2)}, u32[]{:S(2)}) collective-permute-start(bf16[1,64,7168]{2,1,0:T(8,128)(2,1)} %collective-permute-done.1.refs_2_), channel_id=1, source_target_pairs={{0,1},{1,0},{2,3},{3,2},{4,5},{5,4},{6,7},{7,6},{8,9},{9,8},{10,11... | collective-permute-start | bytes 2752520 | tf_op jit(solution)/shard_map/ppermute | solution.py:249
  51.3 23.8 %collective-permute-start.10 = (bf16[128,2176]{1,0:T(8,128)(2,1)}, bf16[128,2176]{1,0:T(8,128)(2,1)S(1)}, u32[]{:S(2)}, u32[]{:S(2)}) collective-permute-start(bf16[128,2176]{1,0:T(8,128)(2,1)} %copy-done.12), channel_id=1, source_target_pairs={{0,4},{4,0},{8,12},{12,8},{1,5},{5,1},{9,13},{13,9},{2,6},{6,2},{1... | collective-permute-start | bytes 1671176 | tf_op jit(solution)/shard_map/ppermute | solution.py:255
  73.6 21.5 %collective-permute-start.15 = (bf16[128,2176]{1,0:T(8,128)(2,1)S(1)}, bf16[128,2176]{1,0:T(8,128)(2,1)S(1)}, u32[]{:S(2)}, u32[]{:S(2)}) collective-permute-start(bf16[128,2176]{1,0:T(8,128)(2,1)S(1)} %get-tuple-element.92), channel_id=1, source_target_pairs={{0,4},{4,0},{8,12},{12,8},{1,5},{5,1},{9,13},{13,9},{2,6},{6,2},{1... | collective-permute-start | bytes 1671176 | tf_op jit(solution)/shard_map/ppermute | solution.py:255
  75.1 3.5 %collective-permute-start.12 = (bf16[1,64,7168]{2,1,0:T(8,128)(2,1)}, bf16[1,64,7168]{2,1,0:T(8,128)(2,1)S(1)}, u32[]{:S(2)}, u32[]{:S(2)}) collective-permute-start(bf16[1,64,7168]{2,1,0:T(8,128)(2,1)} %collective-permute-done.9.refs_0_), channel_id=1, source_target_pairs={{0,1},{1,0},{2,3},{3,2},{4,5},{5,4},{6,7},{7,6},{8,9},{9,8},{10,11... | collective-permute-start | bytes 2752520 | tf_op jit(solution)/shard_map/ppermute | solution.py:249
  75.2 20.0 %copy-start.13 = (f32[128,2176]{1,0:T(8,128)}, f32[128,2176]{1,0:T(8,128)S(1)}, u32[]{:S(2)}) copy-start(f32[128,2176]{1,0:T(8,128)S(1)} %convert_add_fusion.2) | copy-start | bytes 3342340
  75.3 20.0 %collective-permute-start.13 = (bf16[64,2176]{1,0:T(8,128)(2,1)S(1)}, bf16[64,2176]{1,0:T(8,128)(2,1)S(1)}, u32[]{:S(2)}, u32[]{:S(2)}) collective-permute-start(bf16[64,2176]{1,0:T(8,128)(2,1)S(1)} %select_convert_fusion.2), channel_id=1, source_target_pairs={{0,8},{4,12},{8,0},{12,4},{1,9},{5,13},{9,1},{13,5},{2,10},{6,14},... | collective-permute-start | bytes 835592 | tf_op jit(solution)/shard_map/ppermute | solution.py:259
  78.1 22.5 %collective-permute-start.8 = (bf16[1,64,7168]{2,1,0:T(8,128)(2,1)S(1)}, bf16[1,64,7168]{2,1,0:T(8,128)(2,1)S(1)}, u32[]{:S(2)}, u32[]{:S(2)}) collective-permute-start(bf16[1,64,7168]{2,1,0:T(8,128)(2,1)S(1)} %get-tuple-element.86), channel_id=1, source_target_pairs={{2,0},{0,2},{3,1},{1,3},{6,4},{4,6},{7,5},{5,7},{10,8},{8,10},{11,... | collective-permute-start | bytes 2752520 | tf_op jit(solution)/shard_map/ppermute | solution.py:252
  89.8 30.6 %collective-permute-start.17 = (bf16[64,2176]{1,0:T(8,128)(2,1)}, bf16[64,2176]{1,0:T(8,128)(2,1)}, u32[]{:S(2)}, u32[]{:S(2)}) collective-permute-start(bf16[64,2176]{1,0:T(8,128)(2,1)} %get-tuple-element.105), channel_id=1, source_target_pairs={{0,4},{4,0},{8,12},{12,8},{1,5},{5,1},{9,13},{13,9},{2,6},{6,2},{1... | collective-permute-start | bytes 835592 | tf_op jit(solution)/shard_map/ppermute | solution.py:255
  95.2 5.3 %copy-start.15 = (f32[128,2176]{1,0:T(8,128)}, f32[128,2176]{1,0:T(8,128)S(1)}, u32[]{:S(2)}) copy-start(f32[128,2176]{1,0:T(8,128)S(1)} %convert_add_fusion) | copy-start | bytes 3342340
  100.5 2.6 %collective-permute-start.14 = (bf16[1,64,7168]{2,1,0:T(8,128)(2,1)S(1)}, bf16[1,64,7168]{2,1,0:T(8,128)(2,1)}, u32[]{:S(2)}, u32[]{:S(2)}) collective-permute-start(bf16[1,64,7168]{2,1,0:T(8,128)(2,1)S(1)} %collective-permute-done.8.refs_0_), channel_id=1, source_target_pairs={{0,1},{1,0},{2,3},{3,2},{4,5},{5,4},{6,7},{7,6},{8,9},{9,8},{10,11... | collective-permute-start | bytes 2752520 | tf_op jit(solution)/shard_map/ppermute | solution.py:249
  101.3 16.2 %collective-permute-start.16 = (bf16[64,2176]{1,0:T(8,128)(2,1)}, bf16[64,2176]{1,0:T(8,128)(2,1)}, u32[]{:S(2)}, u32[]{:S(2)}) collective-permute-start(bf16[64,2176]{1,0:T(8,128)(2,1)} %select_convert_fusion.1), channel_id=1, source_target_pairs={{0,8},{4,12},{8,0},{12,4},{1,9},{5,13},{9,1},{13,5},{2,10},{6,14},... | collective-permute-start | bytes 835592 | tf_op jit(solution)/shard_map/ppermute | solution.py:259
  102.6 17.8 %copy-start.14 = (f32[128,2176]{1,0:T(8,128)S(1)}, f32[128,2176]{1,0:T(8,128)}, u32[]{:S(2)}) copy-start(f32[128,2176]{1,0:T(8,128)} %copy-done.13) | copy-start | bytes 3342340
  118.3 4.4 %collective-permute-start.19 = (f32[64,128]{1,0:T(8,128)S(1)}, f32[64,128]{1,0:T(8,128)S(1)}, u32[]{:S(2)}, u32[]{:S(2)}) collective-permute-start(f32[64,128]{1,0:T(8,128)S(1)} %get-tuple-element.124), channel_id=1, source_target_pairs={{0,4},{4,0},{8,12},{12,8},{1,5},{5,1},{9,13},{13,9},{2,6},{6,2},{1... | collective-permute-start | bytes 98312 | tf_op jit(solution)/shard_map/ppermute | solution.py:255
  118.3 11.9 %collective-permute-start.20 = (bf16[64,2048]{1,0:T(8,128)(2,1)S(1)}, bf16[64,2048]{1,0:T(8,128)(2,1)S(1)}, u32[]{:S(2)}, u32[]{:S(2)}) collective-permute-start(bf16[64,2048]{1,0:T(8,128)(2,1)S(1)} %get-tuple-element.127), channel_id=1, source_target_pairs={{0,4},{4,0},{8,12},{12,8},{1,5},{5,1},{9,13},{13,9},{2,6},{6,2},{1... | collective-permute-start | bytes 786440 | tf_op jit(solution)/shard_map/ppermute | solution.py:255
  121.4 23.5 %collective-permute-start.18 = (bf16[64,2176]{1,0:T(8,128)(2,1)S(1)}, bf16[64,2176]{1,0:T(8,128)(2,1)S(1)}, u32[]{:S(2)}, u32[]{:S(2)}) collective-permute-start(bf16[64,2176]{1,0:T(8,128)(2,1)S(1)} %select_convert_fusion), channel_id=1, source_target_pairs={{0,8},{4,12},{8,0},{12,4},{1,9},{5,13},{9,1},{13,5},{2,10},{6,14},... | collective-permute-start | bytes 835592 | tf_op jit(solution)/shard_map/ppermute | solution.py:259
  122.7 22.2 %collective-permute-start.21 = (f32[64,128]{1,0:T(8,128)S(1)}, f32[64,128]{1,0:T(8,128)S(1)}, u32[]{:S(2)}, u32[]{:S(2)}) collective-permute-start(f32[64,128]{1,0:T(8,128)S(1)} %get-tuple-element.138), channel_id=1, source_target_pairs={{0,8},{4,12},{8,0},{12,4},{1,9},{5,13},{9,1},{13,5},{2,10},{6,14},... | collective-permute-start | bytes 98312 | tf_op jit(solution)/shard_map/ppermute | solution.py:259
  130.2 22.7 %collective-permute-start.25 = (bf16[64,2048]{1,0:T(8,128)(2,1)S(1)}, bf16[64,2048]{1,0:T(8,128)(2,1)S(1)}, u32[]{:S(2)}, u32[]{:S(2)}) collective-permute-start(bf16[64,2048]{1,0:T(8,128)(2,1)S(1)} %select_convert_fusion.3), channel_id=1, source_target_pairs={{0,8},{4,12},{8,0},{12,4},{1,9},{5,13},{9,1},{13,5},{2,10},{6,14},... | collective-permute-start | bytes 786440 | tf_op jit(solution)/shard_map/ppermute | solution.py:259
  145.1 5.0 %collective-permute-start.23 = (bf16[4,64,64]{2,1,0:T(8,128)(2,1)S(1)}, bf16[4,64,64]{2,1,0:T(8,128)(2,1)S(1)}, u32[]{:S(2)}, u32[]{:S(2)}) collective-permute-start(bf16[4,64,64]{2,1,0:T(8,128)(2,1)S(1)} %select_bitcast_fusion), channel_id=1, source_target_pairs={{0,2},{1,3},{2,0},{3,1},{4,6},{5,7},{6,4},{7,5},{8,10},{9,11},{10,... | collective-permute-start | bytes 98312 | tf_op jit(solution)/shard_map/ppermute | solution.py:401
  145.7 4.4 %collective-permute-start.24 = (bf16[4,64,64]{2,1,0:T(8,128)(2,1)S(1)}, bf16[4,64,64]{2,1,0:T(8,128)(2,1)S(1)}, u32[]{:S(2)}, u32[]{:S(2)}) collective-permute-start(bf16[4,64,64]{2,1,0:T(8,128)(2,1)S(1)} %select_bitcast_fusion), channel_id=1, source_target_pairs={{0,3},{1,0},{2,1},{3,2},{4,7},{5,4},{6,5},{7,6},{8,11},{9,8},{10,9... | collective-permute-start | bytes 98312 | tf_op jit(solution)/shard_map/ppermute | solution.py:401
  145.7 4.4 %collective-permute-start.22 = (bf16[4,64,64]{2,1,0:T(8,128)(2,1)S(1)}, bf16[4,64,64]{2,1,0:T(8,128)(2,1)S(1)}, u32[]{:S(2)}, u32[]{:S(2)}) collective-permute-start(bf16[4,64,64]{2,1,0:T(8,128)(2,1)S(1)} %select_bitcast_fusion), channel_id=1, source_target_pairs={{0,1},{1,2},{2,3},{3,0},{4,5},{5,6},{6,7},{7,4},{8,9},{9,10},{10,1... | collective-permute-start | bytes 98312 | tf_op jit(solution)/shard_map/ppermute | solution.py:401
  (13 other events, 38.2 us)

commit v12 on v11

--- a/solution.py
+++ b/solution.py
@@ -12,7 +12,7 @@
 BLOCK = 1024
 BUFFERS = 4
 RANK_NAME = 1000
-VMEM_BYTES = 17 * 1024 * 1024
+VMEM_BYTES = 20 * 1024 * 1024
 
 
 def block_shape(depth, width):
@@ -28,11 +28,12 @@
     return -(-slots * rank // 128) * 128
 
 
-def matmul_body(spans, emitted, apart, pos_ref, *refs):
+def matmul_body(spans, staged, apart, pos_ref, token_ref, *refs):
     sources = refs[:2 * len(spans)]
     w_ref, a_ref, send_ref, keep_ref = refs[2 * len(spans):2 * len(spans) + 4]
-    outs = refs[2 * len(spans) + 4:-5]
-    x_ref, w_buf, total_ref, x_sems, w_sems = refs[-5:]
+    outs, refs = refs[2 * len(spans) + 4:], ()
+    outs, refs = (outs[:-7], outs[-7:]) if staged else (outs[:-5], outs[-5:])
+    x_ref, w_buf, total_ref, x_sems, w_sems = refs[:5]
     rows = send_ref.shape[0]
     depth, width = w_ref.shape
     slots, rank, _ = a_ref.shape
@@ -58,6 +59,14 @@
         begin += steps
     for copy in copies:
         copy.start()
+    if staged:
+        stage_ref, stage_sems = refs[5:]
+        stage_in = pltpu.make_async_copy(sources[0].at[pl.ds(1, staged)], stage_ref, stage_sems.at[staged])
+        stage_in.start()
+        stage_out = [
+            pltpu.make_async_copy(stage_ref.at[pl.ds(index, 1)], out_ref, stage_sems.at[index])
+            for index, out_ref in enumerate(outs)
+        ]
     for block in range(buffers):
         fetch(jnp.int32(block), block).start()
     keep_ref[...] = jnp.zeros_like(keep_ref)
@@ -68,12 +77,10 @@
         keep_rank[...] = jnp.zeros_like(keep_rank)
     for copy in copies:
         copy.wait()
-    emits = [
-        pltpu.make_async_copy(x_ref.at[own_at, pl.ds(block, 1)], out_ref, x_sems.at[2 * len(spans) + index])
-        for index, (block, out_ref) in enumerate(zip(emitted, outs[2 if apart else 0:]))
-    ]
-    for emit in emits:
-        emit.start()
+    if staged:
+        stage_in.wait()
+        for copy in stage_out:
+            copy.start()
     for slot in range(slots):
         x = x_ref[...].reshape(2 * rows, depth)
         part = lax.dot_general(
@@ -103,11 +110,12 @@
             fetch(block + buffers, slot).start()
 
     send_ref[...] = total_ref[...].astype(send_ref.dtype)
-    for emit in emits:
-        emit.wait()
-
-
-def partial_products(pos, chunks, weight, factors, apart=False, emitted=()):
+    if staged:
+        for copy in stage_out:
+            copy.wait()
+
+
+def partial_products(pos, token, chunks, weight, factors, apart=False, staged=0):
     _, per_block, depth = chunks[0][0].shape
     width = weight.shape[1]
     spans = tuple((first, steps) for _, _, first, steps in chunks)
@@ -124,27 +132,30 @@
         jax.ShapeDtypeStruct((rows, columns), jnp.float32),
     ] + [jax.ShapeDtypeStruct((rows, extra), jnp.float32)] * (2 if apart else 0)
     out_specs = [vmem_spec] * len(out_shape)
-    out_shape += [jax.ShapeDtypeStruct((1, per_block, depth), jnp.bfloat16)] * len(emitted)
-    out_specs += [any_spec] * len(emitted)
+    out_shape += [jax.ShapeDtypeStruct((1, per_block, depth), jnp.bfloat16)] * staged
+    out_specs += [any_spec] * staged
     return pl.pallas_call(
-        functools.partial(matmul_body, spans, emitted, apart),
-        in_specs=[pl.BlockSpec(memory_space=pltpu.SMEM)] + [any_spec] * (2 * len(chunks) + 1) + [vmem_spec],
+        functools.partial(matmul_body, spans, staged, apart),
+        in_specs=[pl.BlockSpec(memory_space=pltpu.SMEM)] + [any_spec] * (2 * len(chunks) + 2) + [vmem_spec],
         out_specs=out_specs,
         out_shape=out_shape,
         scratch_shapes=[
             pltpu.VMEM((2, steps, per_block, depth), jnp.bfloat16),
             pltpu.VMEM((buffers, block_k, block_w), jnp.bfloat16),
             pltpu.VMEM((rows, columns), jnp.float32),
-            pltpu.SemaphoreType.DMA((2 * len(chunks) + len(emitted),)),
+            pltpu.SemaphoreType.DMA((2 * len(chunks),)),
             pltpu.SemaphoreType.DMA((buffers,)),
-        ],
+        ] + ([
+            pltpu.VMEM((staged, per_block, depth), jnp.bfloat16),
+            pltpu.SemaphoreType.DMA((staged + 1,)),
+        ] if staged else []),
         compiler_params=pltpu.CompilerParams(vmem_limit_bytes=VMEM_BYTES),
         cost_estimate=pl.CostEstimate(flops=0, bytes_accessed=0, transcendentals=0),
         name="partial_products",
-    )(pos, *[source for own, sib, _, _ in chunks for source in (own, sib)], weight, factors)
-
-
-def finish_body(received, panels, chosen_ref, slot_ref, order_ref, *refs):
+    )(pos, token, *[source for own, sib, _, _ in chunks for source in (own, sib)], weight, factors)
+
+
+def finish_body(received, panels, token_ref, chosen_ref, slot_ref, order_ref, *refs):
     panel_refs, refs = refs[:panels], refs[panels:]
     per_panel = panel_refs[0].shape[0]
     out_ref, lifted_ref, done_ref, sem = refs[-4:]
@@ -176,14 +187,15 @@
     copy.wait()
 
 
-def finish_steps(totals, chosen, slots, order, panels):
+def finish_steps(totals, chosen, slots, order, panels, token):
     steps, width = len(totals), panels[0].shape[1]
     rows = chosen.shape[0] // (steps + 1)
     vmem_spec = pl.BlockSpec(memory_space=pltpu.VMEM)
     arrays = [value for total in totals for value in total]
     return pl.pallas_call(
         functools.partial(finish_body, len(totals[0]) - 1, len(panels)),
-        in_specs=[vmem_spec, vmem_spec, pl.BlockSpec(memory_space=pltpu.SMEM)] + [vmem_spec] * (len(panels) + len(arrays)),
+        in_specs=[pl.BlockSpec(memory_space=pl.ANY), vmem_spec, vmem_spec, pl.BlockSpec(memory_space=pltpu.SMEM)]
+        + [vmem_spec] * (len(panels) + len(arrays)),
         out_specs=[pl.BlockSpec(memory_space=pl.ANY), vmem_spec],
         out_shape=[
             jax.ShapeDtypeStruct((steps + 1, rows, width), jnp.bfloat16),
@@ -193,7 +205,7 @@
         compiler_params=pltpu.CompilerParams(vmem_limit_bytes=VMEM_BYTES),
         cost_estimate=pl.CostEstimate(flops=0, bytes_accessed=0, transcendentals=0),
         name="finish_steps",
-    )(chosen, slots, order, *panels, *arrays)
+    )(token, chosen, slots, order, *panels, *arrays)
 
 
 def last_body(partial_ref, lifted_ref, *refs):
@@ -280,8 +292,9 @@
         return panels, order
 
     bits = [n_tensor >> at for at in range(1, n_tensor.bit_length())]
-    order = [0] + [at for at in range(1, n_tensor) if at % (n_tensor // 4) == 0]
+    order = [0, bits[0], bits[1]]
     panels = [up_b] + [swap_tensor(up_b, at) for at in order[1:]]
+
     my_ids = lax.dynamic_slice_in_dim(adapter_ids, tensor_index * rows_mine, rows_mine)
     iota = lax.broadcasted_iota(jnp.int32, (rows_mine, slot_count), 1)
     my_slot = jnp.sum((my_ids == iota).astype(jnp.int32) * owner_map[None, :], axis=1)
@@ -305,7 +318,7 @@
             bit //= 2
         return total.reshape(steps, extent, columns)
 
-    def gap(token, jobs, held_back=False):
+    def gap(token, jobs, short=False):
         nonlocal first_leg, second_leg
         for parts, received, keep, kind in first_leg:
             steps = sum(length for _, length in parts)
@@ -316,7 +329,6 @@
                     if (key[0] + at - begin, key[1]) == (step_count - 1, 0):
                         halved[RANK_NAME, 0] = total[at][:, width:]
                 begin += length
-        closed = {name: (after(kept, token), *received) for name, kept, received in second_leg}
         started, sends = [], []
         for name in sorted({name for name, _ in halved}):
             if name in begun or name == RANK_NAME or any((name, at) not in halved for at in range(n_rep)):
@@ -331,57 +343,61 @@
             ])
             started.append((name, kept))
         sends, token = lax.optimization_barrier((sends, token))
+        closed, waiting = {}, []
+        for name, kept, received, lag in second_leg:
+            if short or lag > 1:
+                waiting.append((name, kept, received, lag if short else lag - 1))
+            else:
+                closed[name], token = lax.optimization_barrier(((kept, *received), token))
         first_sends = [job[1] for job in jobs]
-        if held_back:
-            first_sends, closed = lax.optimization_barrier((first_sends, closed))
         ended.update(closed)
         first_leg = [
             (parts, swap_tensor(send, group // 2), keep, kind) for (parts, _, keep, kind), send in zip(jobs, first_sends)
         ]
-        second_leg = [
-            (name, kept, [to_group(value, hop + 1) for hop, value in enumerate(sent)])
+        second_leg = waiting + [
+            (name, kept, [to_group(value, hop + 1) for hop, value in enumerate(sent)], 2 if short else 1)
             for (name, kept), sent in zip(started, sends)
         ]
-        return sends, closed
+        return sends, token
 
     factors = jnp.swapaxes(down_a, 1, 2)
 
     lead = step_count // 2
     parts, last_ranks, next_local = [((0, 0), lead)], {}, lead
-    send, keep, *emitted = partial_products(
-        pos, [(source, siblings, 0, lead)], weight, factors, emitted=tuple(range(1, lead))
+    send, keep, *slices = partial_products(
+        pos, up_b, [(source, siblings, 0, lead)], weight, factors, staged=step_count - 1
     )
-    for step, rows in enumerate(emitted, 1):
+    for step, rows in enumerate(slices, 1):
         remote.update({(step, shift): from_rep(rows, shift) for shift in range(1, n_rep)})
+    send, panels = lax.optimization_barrier((send, panels))
     for piece, (step, shift) in enumerate(pieces):
-        sends, closed = gap(send, [(parts, send, keep, jnp.bfloat16)])
-        own, panels, closed, _ = lax.optimization_barrier((remote[step, shift], panels, closed, send))
-        ended.update(closed)
+        sends, token = gap(send, [(parts, send, keep, jnp.bfloat16)])
+        own, panels, token = lax.optimization_barrier((remote[step, shift], panels, token))
         if piece == 0:
+            panels, order = panels + [swap_tensor(panels[1], bits[1])], order + [bits[0] ^ bits[1]]
             panels, order = spread_panels(panels, order, bits[2:])
         sib = swap_cores(own)
-        own, sib, siblings, _ = lax.optimization_barrier((own, sib, siblings, sends))
-        last, chunks, parts, places = step == step_count - 1, [(own, sib, 0, 1)], [((step, shift), 1)], ()
+        if piece == len(pieces) - 1:
+            more, token = gap(token, [], short=True)
+            sends = sends + more
+        own, sib, siblings, sends, token = lax.optimization_barrier((own, sib, siblings, sends, token))
+        last, chunks, parts = step == step_count - 1, [(own, sib, 0, 1)], [((step, shift), 1)]
         if next_local < step_count:
             chunks.insert(0, (source, siblings, next_local, 1))
             parts.insert(0, ((next_local, 0), 1))
-            places = (0,)
-        send, keep, *outs = partial_products(pos, chunks, weight, factors, last, places)
+            next_local += 1
+        send, keep, *ranks = partial_products(pos, token, chunks, weight, factors, last)
         if last:
-            last_ranks[shift] = outs
-        elif outs:
-            remote.update({(next_local, along): from_rep(outs[0], along) for along in range(1, n_rep)})
-            next_local += 1
-    gap(send, [(parts, send, keep, jnp.bfloat16)], held_back=True)
+            last_ranks[shift] = ranks
+    _, token = gap(send, [(parts, send, keep, jnp.bfloat16)])
     for shift, ranks in last_ranks.items():
         halved[RANK_NAME, shift] = second_half(ranks[1], swap_tensor(ranks[0], group // 2), 1, jnp.float32)[0]
     values = [halved[RANK_NAME, at] for at in range(n_rep)]
     ended[RANK_NAME] = (pick(values, (group_index - rep_index) % n_rep), *[
         to_group(pick(values, (group_index + hop - rep_index) % n_rep), hop) for hop in range(1, n_rep)
     ])
-    rounded, _ = gap(send, [])
-    kept, *received = ended[RANK_NAME]
-    ended[RANK_NAME] = (after(kept, rounded), *received)
+    _, token = gap(token, [])
+    ended[RANK_NAME], token = lax.optimization_barrier((ended[RANK_NAME], token))
 
     def rank_sum(name):
         kept, *received = [value[:, -rank_columns(factors):] for value in ended[name]]
@@ -391,8 +407,8 @@
 
     finished = jnp.stack([rank_sum(step) for step in range(step_count - 1)] + [rank_sum(RANK_NAME)])
     finished = finished.astype(jnp.bfloat16).reshape(step_count, rows_mine, owned_slots, rank_size)
-    finished = lax.optimization_barrier((finished, rounded))[0]
-    ended.update((name, (kept, *received)) for name, kept, received in second_leg)
+    finished, token = lax.optimization_barrier((finished, token))
+    ended.update((name, (kept, *received)) for name, kept, received, _ in second_leg)
     masked = jnp.sum(
         jnp.where(owned_hot[None, :, :, None], finished, 0), axis=2, dtype=jnp.float32
     ).astype(jnp.bfloat16)
@@ -412,6 +428,7 @@
         jnp.broadcast_to(my_slot, (step_count, rows_mine)).reshape(step_count * rows_mine, 1),
         panel_slots,
         panels,
+        token,
     )
     return finish_last(partial, lifted, ended[step_count - 1])
 

time: 154 us -> 157 us (1.019)
  waiting for transfers between devices: 36.6 us -> 44 us
  starting transfers between devices: 33.3 us -> 26.5 us
  local copies, waits for them, and re-layouts: 7.63 us -> 10.5 us
    ppermute x9, waiting for transfers between devices: 8.69 us -> 21.1 us  [swap_tensor(): return lax.ppermute(value, 'tp', [(i, i ^ bit) for i in range(n_tensor)])]
    ppermute x9, starting transfers between devices: 19.3 us -> 10.2 us  [swap_tensor(): return lax.ppermute(value, 'tp', [(i, i ^ bit) for i in range(n_tensor)])]
    unnamed x36 -> x44, local copies, waits for them, and re-layouts: 3.86 us -> 8.14 us
    ppermute x3, waiting for transfers between devices: 3.82 us -> 1.24 us  [per_device(): lax.ppermute(masked, ('rep', 'sub'), [(i, (i + turn) % n_owners) for i in...]
    ppermute x4, waiting for transfers between devices: 5.71 us -> 3.59 us  [from_rep(): lax.ppermute(value, 'rep', [((i + shift) % n_rep, i) for i in range(n_rep)])]
    ppermute x3, starting transfers between devices: 1.1 us -> 2.94 us  [per_device(): lax.ppermute(masked, ('rep', 'sub'), [(i, (i + turn) % n_owners) for i in...]
  transfers between devices with their start and end apart: 26 -> 26, of which waited for: 9 -> 13; matrix products, arithmetic and copies ran while one was open for 6% -> 4% of each run, Pallas kernels for 46% -> 45%
where the time goes in v12:
time: 157 us
  Pallas kernels  71.2 us (45%)
  waiting for transfers between devices  44 us (28%)
  starting transfers between devices  26.5 us (17%)
  local copies, waits for them, and re-layouts  10.5 us (7%)
  other arithmetic  4.47 us (3%)
    pallas_call x5, Pallas kernels, partial_products(): pl.pallas_call(functools.partial(matmul_body, spans, staged, apart), in_s...  67.9 us
    ppermute x9, waiting for transfers between devices, swap_tensor(): return lax.ppermute(value, 'tp', [(i, i ^ bit) for i in range(n_tensor)])  21.1 us
    ppermute x5, waiting for transfers between devices, to_group(): lax.ppermute(value, 'tp', [(i, (i + moved) % n_tensor) for i in range(n_t...  18.1 us
    ppermute x9, starting transfers between devices, swap_tensor(): return lax.ppermute(value, 'tp', [(i, i ^ bit) for i in range(n_tensor)])  10.2 us
    unnamed x44, local copies, waits for them, and re-layouts  8.14 us
    ppermute x5, starting transfers between devices, to_group(): lax.ppermute(value, 'tp', [(i, (i + moved) % n_tensor) for i in range(n_t...  7.73 us
    ppermute x4, starting transfers between devices, from_rep(): lax.ppermute(value, 'rep', [((i + shift) % n_rep, i) for i in range(n_rep)])  5.12 us
    ppermute x4, waiting for transfers between devices, from_rep(): lax.ppermute(value, 'rep', [((i + shift) % n_rep, i) for i in range(n_rep)])  3.59 us
  transfers between devices with their start and end apart: 26, of which 13 were waited for; matrix products, arithmetic and copies ran while one was open for 4% of the time, Pallas kernels for 45%

profile of v12, /device:TPU:0, one launch (start us, length us, event | category | flops | bytes accessed | tf_op | source)
XLA Modules:
  0.0 157.1 jit_solution(15445385957342489304)
XLA Ops:
  0.5 2.2 %slice.68 = bf16[1,64,7168]{2,1,0:T(8,128)(2,1)} slice(bf16[4,64,7168]{2,1,0:T(8,128)(2,1)} %refs_0_.5), slice={[0:1], [0:64], [0:7168]} | slice | bytes 1835008 | tf_op jit(solution)/shard_map/slice | solution.py:286
  2.7 2.6 %collective-permute-start = (bf16[1,64,7168]{2,1,0:T(8,128)(2,1)}, bf16[1,64,7168]{2,1,0:T(8,128)(2,1)S(1)}, u32[]{:S(2)}, u32[]{:S(2)}) collective-permute-start(bf16[1,64,7168]{2,1,0:T(8,128)(2,1)} %slice.68), channel_id=1, source_target_pairs={{2,0},{0,2},{3,1},{1,3},{6,4},{4,6},{7,5},{5,7},{10,8},{8,10},{11,... | collective-permute-start | bytes 2752520 | tf_op jit(solution)/shard_map/ppermute | solution.py:264
  5.3 2.6 %collective-permute-start.2 = (bf16[1,64,2048]{2,1,0:T(8,128)(2,1)S(1)}, bf16[1,64,2048]{2,1,0:T(8,128)(2,1)}, u32[]{:S(2)}, u32[]{:S(2)}) collective-permute-start(bf16[1,64,2048]{2,1,0:T(8,128)(2,1)S(1)} %copy-done.2), channel_id=1, source_target_pairs={{0,8},{4,12},{8,0},{12,4},{1,9},{5,13},{9,1},{13,5},{2,10},{6,14},... | collective-permute-start | bytes 786440 | tf_op jit(solution)/shard_map/ppermute | solution.py:267
  7.9 1.6 %collective-permute-start.3 = (bf16[1,64,2048]{2,1,0:T(8,128)(2,1)S(1)}, bf16[1,64,2048]{2,1,0:T(8,128)(2,1)S(1)}, u32[]{:S(2)}, u32[]{:S(2)}) collective-permute-start(bf16[1,64,2048]{2,1,0:T(8,128)(2,1)S(1)} %copy-done.2), channel_id=1, source_target_pairs={{0,4},{4,0},{8,12},{12,8},{1,5},{5,1},{9,13},{13,9},{2,6},{6,2},{1... | collective-permute-start | bytes 786440 | tf_op jit(solution)/shard_map/ppermute | solution.py:267
  9.4 17.9 %partial_products.5 = (bf16[128,2176]{1,0:T(8,128)(2,1)}, f32[128,2176]{1,0:T(8,128)S(1)}, bf16[1,64,7168]{2,1,0:T(8,128)(2,1)S(1)}, bf16[1,64,7168]{2,1,0:T(8,128)(2,1)S(1)}, bf16[1,64,7168]{2,1,0:T(8,128)(2,1)S(1)}) custom-call(s32[1]{0:T(128)} %bitcast.pos_ref, bf16[1,64,2048]{2,1,0:T(8,128)(2,1)S(1)} %copy-done.2, bf16[4,64,7168]{2,1,0:T(8,128)(2,1)} %refs_0_.5, ...), custom_call_target="tpu_custom_call" | custom-call | tf_op jit(solution)/shard_map/partial_products/pallas_call | solution.py:137
  31.4 1.5 collective-permute-start.9
  33.4 1.2 copy-done.4
  34.6 13.1 %partial_products.6 = (bf16[128,2176]{1,0:T(8,128)(2,1)S(1)}, f32[128,2176]{1,0:T(8,128)S(1)}) custom-call(s32[1]{0:T(128)} %bitcast.pos_ref, bf16[128,2176]{1,0:T(8,128)(2,1)} %get-tuple-element.97.token_ref, bf16[4,64,7168]{2,1,0:T(8,128)(2,1)} %refs_0_.5, bf16[4,64,7168]{2,1,0:T(8,128)(2,1)} %collective-permute-done.1.refs_1_, ...), custom_call_target="tpu_custom_call" | custom-call | tf_op jit(solution)/shard_map/partial_products/pallas_call | solution.py:137
  48.5 3.5 %collective-permute-done.6 = bf16[1,64,2048]{2,1,0:T(8,128)(2,1)S(1)} collective-permute-done((bf16[1,64,2048]{2,1,0:T(8,128)(2,1)}, bf16[1,64,2048]{2,1,0:T(8,128)(2,1)S(1)}, u32[]{:S(2)}, u32[]{:S(2)}) %collective-permute-start.6) | collective-permute-done | bytes 262176 | tf_op jit(solution)/shard_map/ppermute | solution.py:267
  52.7 1.0 collective-permute-done.5.refs_2_
  54.3 1.4 collective-permute-start.8
  55.6 1.2 convert_add_fusion.1
  56.9 15.8 %partial_products.7 = (bf16[128,2176]{1,0:T(8,128)(2,1)S(1)}, f32[128,2176]{1,0:T(8,128)S(1)}) custom-call(s32[1]{0:T(128)} %bitcast.pos_ref, bf16[128,2176]{1,0:T(8,128)(2,1)S(1)} %copy-done.8, bf16[4,64,7168]{2,1,0:T(8,128)(2,1)} %refs_0_.5, bf16[4,64,7168]{2,1,0:T(8,128)(2,1)} %collective-permute-done.1.refs_1_, ...), custom_call_target="tpu_custom_call" | custom-call | tf_op jit(solution)/shard_map/partial_products/pallas_call | solution.py:137
  74.7 2.1 %collective-permute-done.11.refs_0_ = bf16[1,64,7168]{2,1,0:T(8,128)(2,1)} collective-permute-done((bf16[1,64,7168]{2,1,0:T(8,128)(2,1)}, bf16[1,64,7168]{2,1,0:T(8,128)(2,1)}, u32[]{:S(2)}, u32[]{:S(2)}) %collective-permute-start.11) | collective-permute-done | bytes 917536 | tf_op jit(solution)/shard_map/ppermute | solution.py:264
  77.7 1.5 collective-permute-start.15
  79.1 2.6 %collective-permute-start.10 = (bf16[64,2176]{1,0:T(8,128)(2,1)}, bf16[64,2176]{1,0:T(8,128)(2,1)S(1)}, u32[]{:S(2)}, u32[]{:S(2)}) collective-permute-start(bf16[64,2176]{1,0:T(8,128)(2,1)} %select_convert_fusion.2), channel_id=1, source_target_pairs={{0,8},{4,12},{8,0},{12,4},{1,9},{5,13},{9,1},{13,5},{2,10},{6,14},... | collective-permute-start | bytes 835592 | tf_op jit(solution)/shard_map/ppermute | solution.py:271
  81.7 1.1 copy-done.6
  82.8 10.5 %partial_products.8 = (bf16[64,2176]{1,0:T(8,128)(2,1)S(1)}, f32[64,2176]{1,0:T(8,128)S(1)}) custom-call(s32[1]{0:T(128)} %bitcast.pos_ref, bf16[128,2176]{1,0:T(8,128)(2,1)S(1)} %copy-done.6, bf16[1,64,7168]{2,1,0:T(8,128)(2,1)} %collective-permute-done.11.refs_0_, bf16[1,64,7168]{2,1,0:T(8,128)(2,1)S(1)} %collective-permute-done.12.refs_1_, ...), custom_call_target="tpu_custom_call" | custom-call | tf_op jit(solution)/shard_map/partial_products/pallas_call | solution.py:137
  93.8 4.7 %collective-permute-done.13 = bf16[128,2176]{1,0:T(8,128)(2,1)} collective-permute-done((bf16[128,2176]{1,0:T(8,128)(2,1)}, bf16[128,2176]{1,0:T(8,128)(2,1)}, u32[]{:S(2)}, u32[]{:S(2)}) %collective-permute-start.13) | collective-permute-done | bytes 557088 | tf_op jit(solution)/shard_map/ppermute | solution.py:267
  98.5 1.2 convert_add_fusion
  100.4 2.5 %collective-permute-start.14 = (bf16[64,2176]{1,0:T(8,128)(2,1)S(1)}, bf16[64,2176]{1,0:T(8,128)(2,1)S(1)}, u32[]{:S(2)}, u32[]{:S(2)}) collective-permute-start(bf16[64,2176]{1,0:T(8,128)(2,1)S(1)} %select_convert_fusion.1), channel_id=1, source_target_pairs={{0,8},{4,12},{8,0},{12,4},{1,9},{5,13},{9,1},{13,5},{2,10},{6,14},... | collective-permute-start | bytes 835592 | tf_op jit(solution)/shard_map/ppermute | solution.py:271
  102.9 1.1 collective-permute-done.17
  104.1 1.5 collective-permute-start.18
  105.7 10.7 %partial_products.9 = (bf16[64,2048]{1,0:T(8,128)(2,1)S(1)}, f32[64,2048]{1,0:T(8,128)S(1)}, f32[64,128]{1,0:T(8,128)S(1)}, f32[64,128]{1,0:T(8,128)S(1)}) custom-call(s32[1]{0:T(128)} %bitcast.pos_ref, bf16[64,2176]{1,0:T(8,128)(2,1)S(1)} %get-tuple-element.148.token_ref, bf16[1,64,7168]{2,1,0:T(8,128)(2,1)S(1)} %collective-permute-done.15.refs_0_, ...), custom_call_target="tpu_custom_call" | custom-call | tf_op jit(solution)/shard_map/partial_products/pallas_call | solution.py:137
  116.4 1.6 %collective-permute-start.19 = (bf16[64,2048]{1,0:T(8,128)(2,1)S(1)}, bf16[64,2048]{1,0:T(8,128)(2,1)S(1)}, u32[]{:S(2)}, u32[]{:S(2)}) collective-permute-start(bf16[64,2048]{1,0:T(8,128)(2,1)S(1)} %get-tuple-element.166.token_ref), channel_id=1, source_target_pairs={{0,4},{4,0},{8,12},{12,8},{1,5},{5,1},{9,13},{13,9},{2,6},{6,2},{1... | collective-permute-start | bytes 786440 | tf_op jit(solution)/shard_map/ppermute | solution.py:267
  118.0 4.7 %collective-permute-done.14.refs_7_ = bf16[64,2176]{1,0:T(8,128)(2,1)S(1)} collective-permute-done((bf16[64,2176]{1,0:T(8,128)(2,1)S(1)}, bf16[64,2176]{1,0:T(8,128)(2,1)S(1)}, u32[]{:S(2)}, u32[]{:S(2)}) %collective-permute-start.14) | collective-permute-done | bytes 278560 | tf_op jit(solution)/shard_map/ppermute | solution.py:271
  122.8 11.8 %collective-permute-done.20 = f32[64,128]{1,0:T(8,128)S(1)} collective-permute-done((f32[64,128]{1,0:T(8,128)S(1)}, f32[64,128]{1,0:T(8,128)S(1)}, u32[]{:S(2)}, u32[]{:S(2)}) %collective-permute-start.20) | collective-permute-done | bytes 32800 | tf_op jit(solution)/shard_map/ppermute | solution.py:267
  135.3 4.2 %collective-permute-done.21 = f32[64,128]{1,0:T(8,128)S(1)} collective-permute-done((f32[64,128]{1,0:T(8,128)S(1)}, f32[64,128]{1,0:T(8,128)S(1)}, u32[]{:S(2)}, u32[]{:S(2)}) %collective-permute-start.21) | collective-permute-done | bytes 32800 | tf_op jit(solution)/shard_map/ppermute | solution.py:271
  139.7 1.5 collective-permute-start.23
  141.2 1.4 collective-permute-start.24
  144.6 2.5 %finish_steps.1 = (bf16[4,64,2048]{2,1,0:T(8,128)(2,1)}, bf16[64,2048]{1,0:T(8,128)(2,1)S(1)}) custom-call(bf16[64,2048]{1,0:T(8,128)(2,1)S(1)} %get-tuple-element.166.token_ref, bf16[256,64]{1,0:T(8,128)(2,1)S(1)} %bitcast.31, s32[256,1]{1,0:T(8,128)S(1)} %reshape.122.slot_ref, s32[4]{0:T(128)S(1)} %pad_add_fusion.order_ref, bf16[64,2048]{1,0:T(8,128)(2,1)S(1)} %bitcast.30, ...), custom_call_target="tpu_custom_call" | custom-call | tf_op jit(solution)/shard_map/finish_steps/pallas_call | solution.py:195
  147.1 9.1 %collective-permute-done.25.refs_1_ = bf16[64,2048]{1,0:T(8,128)(2,1)S(1)} collective-permute-done((bf16[64,2048]{1,0:T(8,128)(2,1)S(1)}, bf16[64,2048]{1,0:T(8,128)(2,1)S(1)}, u32[]{:S(2)}, u32[]{:S(2)}) %collective-permute-start.25) | collective-permute-done | bytes 262176 | tf_op jit(solution)/shard_map/ppermute | solution.py:271
  (102 shorter events, 15.0 us)
Async XLA Ops:
  0.0 77.3 %copy-start = (s32[256,1]{0,1:T(1,128)S(1)}, s32[256,1]{0,1:T(1,128)}, u32[]{:S(2)}) copy-start(s32[256,1]{0,1:T(1,128)} %param.10) | copy-start | bytes 3076
  0.0 9.4 %copy-start.1 = (bf16[1,7168,64]{1,2,0:T(8,128)(2,1)S(1)}, bf16[1,7168,64]{1,2,0:T(8,128)(2,1)}, u32[]{:S(2)}) copy-start(bf16[1,7168,64]{1,2,0:T(8,128)(2,1)} %param.8) | copy-start | bytes 2752516
  0.0 9.4 %collective-permute-start.1 = (bf16[4,64,7168]{2,1,0:T(8,128)(2,1)}, bf16[4,64,7168]{2,1,0:T(8,128)(2,1)}, u32[]{:S(2)}, u32[]{:S(2)}) collective-permute-start(bf16[4,64,7168]{2,1,0:T(8,128)(2,1)} %refs_0_.5), channel_id=1, source_target_pairs={{0,1},{1,0},{2,3},{3,2},{4,5},{5,4},{6,7},{7,6},{8,9},{9,8},{10,11... | collective-permute-start | bytes 11010056 | tf_op jit(solution)/shard_map/ppermute | solution.py:261
  2.7 27.2 %collective-permute-start = (bf16[1,64,7168]{2,1,0:T(8,128)(2,1)}, bf16[1,64,7168]{2,1,0:T(8,128)(2,1)S(1)}, u32[]{:S(2)}, u32[]{:S(2)}) collective-permute-start(bf16[1,64,7168]{2,1,0:T(8,128)(2,1)} %slice.68), channel_id=1, source_target_pairs={{2,0},{0,2},{3,1},{1,3},{6,4},{4,6},{7,5},{5,7},{10,8},{8,10},{11,... | collective-permute-start | bytes 2752520 | tf_op jit(solution)/shard_map/ppermute | solution.py:264
  5.3 23.9 %collective-permute-start.2 = (bf16[1,64,2048]{2,1,0:T(8,128)(2,1)S(1)}, bf16[1,64,2048]{2,1,0:T(8,128)(2,1)}, u32[]{:S(2)}, u32[]{:S(2)}) collective-permute-start(bf16[1,64,2048]{2,1,0:T(8,128)(2,1)S(1)} %copy-done.2), channel_id=1, source_target_pairs={{0,8},{4,12},{8,0},{12,4},{1,9},{5,13},{9,1},{13,5},{2,10},{6,14},... | collective-permute-start | bytes 786440 | tf_op jit(solution)/shard_map/ppermute | solution.py:267
  7.9 21.3 %collective-permute-start.3 = (bf16[1,64,2048]{2,1,0:T(8,128)(2,1)S(1)}, bf16[1,64,2048]{2,1,0:T(8,128)(2,1)S(1)}, u32[]{:S(2)}, u32[]{:S(2)}) collective-permute-start(bf16[1,64,2048]{2,1,0:T(8,128)(2,1)S(1)} %copy-done.2), channel_id=1, source_target_pairs={{0,4},{4,0},{8,12},{12,8},{1,5},{5,1},{9,13},{13,9},{2,6},{6,2},{1... | collective-permute-start | bytes 786440 | tf_op jit(solution)/shard_map/ppermute | solution.py:267
  29.9 3.5 %collective-permute-start.4 = (bf16[1,64,7168]{2,1,0:T(8,128)(2,1)S(1)}, bf16[1,64,7168]{2,1,0:T(8,128)(2,1)S(1)}, u32[]{:S(2)}, u32[]{:S(2)}) collective-permute-start(bf16[1,64,7168]{2,1,0:T(8,128)(2,1)S(1)} %collective-permute-done.refs_2_), channel_id=1, source_target_pairs={{0,1},{1,0},{2,3},{3,2},{4,5},{5,4},{6,7},{7,6},{8,9},{9,8},{10,11... | collective-permute-start | bytes 2752520 | tf_op jit(solution)/shard_map/ppermute | solution.py:261
  30.8 22.9 %collective-permute-start.5 = (bf16[1,64,7168]{2,1,0:T(8,128)(2,1)S(1)}, bf16[1,64,7168]{2,1,0:T(8,128)(2,1)}, u32[]{:S(2)}, u32[]{:S(2)}) collective-permute-start(bf16[1,64,7168]{2,1,0:T(8,128)(2,1)S(1)} %get-tuple-element.102), channel_id=1, source_target_pairs={{2,0},{0,2},{3,1},{1,3},{6,4},{4,6},{7,5},{5,7},{10,8},{8,10},{11,... | collective-permute-start | bytes 2752520 | tf_op jit(solution)/shard_map/ppermute | solution.py:264
  31.4 24.2 %collective-permute-start.9 = (bf16[128,2176]{1,0:T(8,128)(2,1)}, bf16[128,2176]{1,0:T(8,128)(2,1)}, u32[]{:S(2)}, u32[]{:S(2)}) collective-permute-start(bf16[128,2176]{1,0:T(8,128)(2,1)} %get-tuple-element.97.token_ref), channel_id=1, source_target_pairs={{0,4},{4,0},{8,12},{12,8},{1,5},{5,1},{9,13},{13,9},{2,6},{6,2},{1... | collective-permute-start | bytes 1671176 | tf_op jit(solution)/shard_map/ppermute | solution.py:267
  32.9 19.1 %collective-permute-start.6 = (bf16[1,64,2048]{2,1,0:T(8,128)(2,1)}, bf16[1,64,2048]{2,1,0:T(8,128)(2,1)S(1)}, u32[]{:S(2)}, u32[]{:S(2)}) collective-permute-start(bf16[1,64,2048]{2,1,0:T(8,128)(2,1)} %collective-permute-done.2), channel_id=1, source_target_pairs={{0,4},{4,0},{8,12},{12,8},{1,5},{5,1},{9,13},{13,9},{2,6},{6,2},{1... | collective-permute-start | bytes 786440 | tf_op jit(solution)/shard_map/ppermute | solution.py:267
  53.7 3.2 %collective-permute-start.7 = (bf16[1,64,7168]{2,1,0:T(8,128)(2,1)}, bf16[1,64,7168]{2,1,0:T(8,128)(2,1)}, u32[]{:S(2)}, u32[]{:S(2)}) collective-permute-start(bf16[1,64,7168]{2,1,0:T(8,128)(2,1)} %collective-permute-done.5.refs_2_), channel_id=1, source_target_pairs={{0,1},{1,0},{2,3},{3,2},{4,5},{5,4},{6,7},{7,6},{8,9},{9,8},{10,11... | collective-permute-start | bytes 2752520 | tf_op jit(solution)/shard_map/ppermute | solution.py:261
  53.7 23.1 %collective-permute-start.11 = (bf16[1,64,7168]{2,1,0:T(8,128)(2,1)}, bf16[1,64,7168]{2,1,0:T(8,128)(2,1)}, u32[]{:S(2)}, u32[]{:S(2)}) collective-permute-start(bf16[1,64,7168]{2,1,0:T(8,128)(2,1)} %copy-done.16), channel_id=1, source_target_pairs={{2,0},{0,2},{3,1},{1,3},{6,4},{4,6},{7,5},{5,7},{10,8},{8,10},{11,... | collective-permute-start | bytes 2752520 | tf_op jit(solution)/shard_map/ppermute | solution.py:264
  54.3 18.5 %collective-permute-start.8 = (bf16[128,2176]{1,0:T(8,128)(2,1)}, bf16[128,2176]{1,0:T(8,128)(2,1)S(1)}, u32[]{:S(2)}, u32[]{:S(2)}) collective-permute-start(bf16[128,2176]{1,0:T(8,128)(2,1)} %copy-done.7), channel_id=1, source_target_pairs={{0,4},{4,0},{8,12},{12,8},{1,5},{5,1},{9,13},{13,9},{2,6},{6,2},{1... | collective-permute-start | bytes 1671176 | tf_op jit(solution)/shard_map/ppermute | solution.py:267
  56.9 16.0 %copy-start.19 = (f32[128,2176]{1,0:T(8,128)}, f32[128,2176]{1,0:T(8,128)S(1)}, u32[]{:S(2)}) copy-start(f32[128,2176]{1,0:T(8,128)S(1)} %convert_add_fusion.1) | copy-start | bytes 3342340
  76.8 4.9 %collective-permute-start.12 = (bf16[1,64,7168]{2,1,0:T(8,128)(2,1)}, bf16[1,64,7168]{2,1,0:T(8,128)(2,1)S(1)}, u32[]{:S(2)}, u32[]{:S(2)}) collective-permute-start(bf16[1,64,7168]{2,1,0:T(8,128)(2,1)} %collective-permute-done.11.refs_0_), channel_id=1, source_target_pairs={{0,1},{1,0},{2,3},{3,2},{4,5},{5,4},{6,7},{7,6},{8,9},{9,8},{10,11... | collective-permute-start | bytes 2752520 | tf_op jit(solution)/shard_map/ppermute | solution.py:261
  76.8 21.7 %collective-permute-start.13 = (bf16[128,2176]{1,0:T(8,128)(2,1)}, bf16[128,2176]{1,0:T(8,128)(2,1)}, u32[]{:S(2)}, u32[]{:S(2)}) collective-permute-start(bf16[128,2176]{1,0:T(8,128)(2,1)} %copy-done.5), channel_id=1, source_target_pairs={{0,4},{4,0},{8,12},{12,8},{1,5},{5,1},{9,13},{13,9},{2,6},{6,2},{1... | collective-permute-start | bytes 1671176 | tf_op jit(solution)/shard_map/ppermute | solution.py:267
  77.7 22.7 %collective-permute-start.15 = (bf16[1,64,7168]{2,1,0:T(8,128)(2,1)}, bf16[1,64,7168]{2,1,0:T(8,128)(2,1)S(1)}, u32[]{:S(2)}, u32[]{:S(2)}) collective-permute-start(bf16[1,64,7168]{2,1,0:T(8,128)(2,1)} %copy-done.15), channel_id=1, source_target_pairs={{2,0},{0,2},{3,1},{1,3},{6,4},{4,6},{7,5},{5,7},{10,8},{8,10},{11,... | collective-permute-start | bytes 2752520 | tf_op jit(solution)/shard_map/ppermute | solution.py:264
  79.1 20.8 %collective-permute-start.10 = (bf16[64,2176]{1,0:T(8,128)(2,1)}, bf16[64,2176]{1,0:T(8,128)(2,1)S(1)}, u32[]{:S(2)}, u32[]{:S(2)}) collective-permute-start(bf16[64,2176]{1,0:T(8,128)(2,1)} %select_convert_fusion.2), channel_id=1, source_target_pairs={{0,8},{4,12},{8,0},{12,4},{1,9},{5,13},{9,1},{13,5},{2,10},{6,14},... | collective-permute-start | bytes 835592 | tf_op jit(solution)/shard_map/ppermute | solution.py:271
  93.3 10.7 %collective-permute-start.17 = (bf16[64,2176]{1,0:T(8,128)(2,1)S(1)}, bf16[64,2176]{1,0:T(8,128)(2,1)S(1)}, u32[]{:S(2)}, u32[]{:S(2)}) collective-permute-start(bf16[64,2176]{1,0:T(8,128)(2,1)S(1)} %get-tuple-element.148.token_ref), channel_id=1, source_target_pairs={{0,4},{4,0},{8,12},{12,8},{1,5},{5,1},{9,13},{13,9},{2,6},{6,2},{1... | collective-permute-start | bytes 835592 | tf_op jit(solution)/shard_map/ppermute | solution.py:267
  93.8 5.9 %copy-start.18 = (f32[128,2176]{1,0:T(8,128)S(1)}, f32[128,2176]{1,0:T(8,128)}, u32[]{:S(2)}) copy-start(f32[128,2176]{1,0:T(8,128)} %copy-done.17) | copy-start | bytes 3342340
  93.8 5.9 %copy-start.20 = (f32[128,2176]{1,0:T(8,128)S(1)}, f32[128,2176]{1,0:T(8,128)}, u32[]{:S(2)}) copy-start(f32[128,2176]{1,0:T(8,128)} %copy-done.19) | copy-start | bytes 3342340
  100.4 5.3 %collective-permute-start.16 = (bf16[1,64,7168]{2,1,0:T(8,128)(2,1)S(1)}, bf16[1,64,7168]{2,1,0:T(8,128)(2,1)S(1)}, u32[]{:S(2)}, u32[]{:S(2)}) collective-permute-start(bf16[1,64,7168]{2,1,0:T(8,128)(2,1)S(1)} %collective-permute-done.15.refs_0_), channel_id=1, source_target_pairs={{0,1},{1,0},{2,3},{3,2},{4,5},{5,4},{6,7},{7,6},{8,9},{9,8},{10,11... | collective-permute-start | bytes 2752520 | tf_op jit(solution)/shard_map/ppermute | solution.py:261
  100.4 22.4 %collective-permute-start.14 = (bf16[64,2176]{1,0:T(8,128)(2,1)S(1)}, bf16[64,2176]{1,0:T(8,128)(2,1)S(1)}, u32[]{:S(2)}, u32[]{:S(2)}) collective-permute-start(bf16[64,2176]{1,0:T(8,128)(2,1)S(1)} %select_convert_fusion.1), channel_id=1, source_target_pairs={{0,8},{4,12},{8,0},{12,4},{1,9},{5,13},{9,1},{13,5},{2,10},{6,14},... | collective-permute-start | bytes 835592 | tf_op jit(solution)/shard_map/ppermute | solution.py:271
  104.1 31.2 %collective-permute-start.18 = (bf16[64,2176]{1,0:T(8,128)(2,1)S(1)}, bf16[64,2176]{1,0:T(8,128)(2,1)S(1)}, u32[]{:S(2)}, u32[]{:S(2)}) collective-permute-start(bf16[64,2176]{1,0:T(8,128)(2,1)S(1)} %select_convert_fusion), channel_id=1, source_target_pairs={{0,8},{4,12},{8,0},{12,4},{1,9},{5,13},{9,1},{13,5},{2,10},{6,14},... | collective-permute-start | bytes 835592 | tf_op jit(solution)/shard_map/ppermute | solution.py:271
  105.7 17.1 %slice-start = ((bf16[64,2176]{1,0:T(8,128)(2,1)}), bf16[64,128]{1,0:T(8,128)(2,1)S(1)}, s32[]{:S(2)}) async-start(bf16[64,2176]{1,0:T(8,128)(2,1)} %copy-done.9), calls=%async_computation | async-start | bytes 32768 | tf_op jit(solution)/shard_map/slice | solution.py:403
  116.4 18.8 %collective-permute-start.19 = (bf16[64,2048]{1,0:T(8,128)(2,1)S(1)}, bf16[64,2048]{1,0:T(8,128)(2,1)S(1)}, u32[]{:S(2)}, u32[]{:S(2)}) collective-permute-start(bf16[64,2048]{1,0:T(8,128)(2,1)S(1)} %get-tuple-element.166.token_ref), channel_id=1, source_target_pairs={{0,4},{4,0},{8,12},{12,8},{1,5},{5,1},{9,13},{13,9},{2,6},{6,2},{1... | collective-permute-start | bytes 786440 | tf_op jit(solution)/shard_map/ppermute | solution.py:267
  122.8 11.8 %collective-permute-start.20 = (f32[64,128]{1,0:T(8,128)S(1)}, f32[64,128]{1,0:T(8,128)S(1)}, u32[]{:S(2)}, u32[]{:S(2)}) collective-permute-start(f32[64,128]{1,0:T(8,128)S(1)} %get-tuple-element.161), channel_id=1, source_target_pairs={{0,4},{4,0},{8,12},{12,8},{1,5},{5,1},{9,13},{13,9},{2,6},{6,2},{1... | collective-permute-start | bytes 98312 | tf_op jit(solution)/shard_map/ppermute | solution.py:267
  134.6 4.9 %collective-permute-start.21 = (f32[64,128]{1,0:T(8,128)S(1)}, f32[64,128]{1,0:T(8,128)S(1)}, u32[]{:S(2)}, u32[]{:S(2)}) collective-permute-start(f32[64,128]{1,0:T(8,128)S(1)} %get-tuple-element.175), channel_id=1, source_target_pairs={{0,8},{4,12},{8,0},{12,4},{1,9},{5,13},{9,1},{13,5},{2,10},{6,14},... | collective-permute-start | bytes 98312 | tf_op jit(solution)/shard_map/ppermute | solution.py:271
  139.6 3.8 %collective-permute-start.22 = (bf16[4,64,64]{2,1,0:T(8,128)(2,1)S(1)}, bf16[4,64,64]{2,1,0:T(8,128)(2,1)S(1)}, u32[]{:S(2)}, u32[]{:S(2)}) collective-permute-start(bf16[4,64,64]{2,1,0:T(8,128)(2,1)S(1)} %select_bitcast_fusion), channel_id=1, source_target_pairs={{0,1},{1,2},{2,3},{3,0},{4,5},{5,6},{6,7},{7,4},{8,9},{9,10},{10,1... | collective-permute-start | bytes 98312 | tf_op jit(solution)/shard_map/ppermute | solution.py:417
  139.7 4.7 %collective-permute-start.23 = (bf16[4,64,64]{2,1,0:T(8,128)(2,1)S(1)}, bf16[4,64,64]{2,1,0:T(8,128)(2,1)S(1)}, u32[]{:S(2)}, u32[]{:S(2)}) collective-permute-start(bf16[4,64,64]{2,1,0:T(8,128)(2,1)S(1)} %select_bitcast_fusion), channel_id=1, source_target_pairs={{0,2},{1,3},{2,0},{3,1},{4,6},{5,7},{6,4},{7,5},{8,10},{9,11},{10,... | collective-permute-start | bytes 98312 | tf_op jit(solution)/shard_map/ppermute | solution.py:417
  141.2 3.3 %collective-permute-start.24 = (bf16[4,64,64]{2,1,0:T(8,128)(2,1)S(1)}, bf16[4,64,64]{2,1,0:T(8,128)(2,1)S(1)}, u32[]{:S(2)}, u32[]{:S(2)}) collective-permute-start(bf16[4,64,64]{2,1,0:T(8,128)(2,1)S(1)} %select_bitcast_fusion), channel_id=1, source_target_pairs={{0,3},{1,0},{2,1},{3,2},{4,7},{5,4},{6,5},{7,6},{8,11},{9,8},{10,9... | collective-permute-start | bytes 98312 | tf_op jit(solution)/shard_map/ppermute | solution.py:417
  142.6 13.7 %collective-permute-start.25 = (bf16[64,2048]{1,0:T(8,128)(2,1)S(1)}, bf16[64,2048]{1,0:T(8,128)(2,1)S(1)}, u32[]{:S(2)}, u32[]{:S(2)}) collective-permute-start(bf16[64,2048]{1,0:T(8,128)(2,1)S(1)} %select_convert_fusion.3), channel_id=1, source_target_pairs={{0,8},{4,12},{8,0},{12,4},{1,9},{5,13},{9,1},{13,5},{2,10},{6,14},... | collective-permute-start | bytes 786440 | tf_op jit(solution)/shard_map/ppermute | solution.py:271
  (17 other events, 41.0 us)

commit v13 on v10

--- a/solution.py
+++ b/solution.py
@@ -28,11 +28,12 @@
     return -(-slots * rank // 128) * 128
 
 
-def matmul_body(spans, emitted, apart, pos_ref, *refs):
+def matmul_body(spans, staged, apart, pos_ref, *refs):
     sources = refs[:2 * len(spans)]
     w_ref, a_ref, send_ref, keep_ref = refs[2 * len(spans):2 * len(spans) + 4]
-    outs = refs[2 * len(spans) + 4:-5]
-    x_ref, w_buf, total_ref, x_sems, w_sems = refs[-5:]
+    outs, refs = refs[2 * len(spans) + 4:], ()
+    outs, refs = (outs[:-7], outs[-7:]) if staged else (outs[:-5], outs[-5:])
+    x_ref, w_buf, total_ref, x_sems, w_sems = refs[:5]
     rows = send_ref.shape[0]
     depth, width = w_ref.shape
     slots, rank, _ = a_ref.shape
@@ -58,6 +59,14 @@
         begin += steps
     for copy in copies:
         copy.start()
+    if staged:
+        stage_ref, stage_sems = refs[5:]
+        stage_in = pltpu.make_async_copy(sources[0].at[pl.ds(1, staged)], stage_ref, stage_sems.at[staged])
+        stage_in.start()
+        stage_out = [
+            pltpu.make_async_copy(stage_ref.at[pl.ds(index, 1)], out_ref, stage_sems.at[index])
+            for index, out_ref in enumerate(outs)
+        ]
     for block in range(buffers):
         fetch(jnp.int32(block), block).start()
     keep_ref[...] = jnp.zeros_like(keep_ref)
@@ -68,12 +77,10 @@
         keep_rank[...] = jnp.zeros_like(keep_rank)
     for copy in copies:
         copy.wait()
-    emits = [
-        pltpu.make_async_copy(x_ref.at[own_at, pl.ds(block, 1)], out_ref, x_sems.at[2 * len(spans) + index])
-        for index, (block, out_ref) in enumerate(zip(emitted, outs[2 if apart else 0:]))
-    ]
-    for emit in emits:
-        emit.start()
+    if staged:
+        stage_in.wait()
+        for copy in stage_out:
+            copy.start()
     for slot in range(slots):
         x = x_ref[...].reshape(2 * rows, depth)
         part = lax.dot_general(
@@ -103,11 +110,12 @@
             fetch(block + buffers, slot).start()
 
     send_ref[...] = total_ref[...].astype(send_ref.dtype)
-    for emit in emits:
-        emit.wait()
-
-
-def partial_products(pos, chunks, weight, factors, apart=False, emitted=()):
+    if staged:
+        for copy in stage_out:
+            copy.wait()
+
+
+def partial_products(pos, chunks, weight, factors, apart=False, staged=0):
     _, per_block, depth = chunks[0][0].shape
     width = weight.shape[1]
     spans = tuple((first, steps) for _, _, first, steps in chunks)
@@ -124,10 +132,10 @@
         jax.ShapeDtypeStruct((rows, columns), jnp.float32),
     ] + [jax.ShapeDtypeStruct((rows, extra), jnp.float32)] * (2 if apart else 0)
     out_specs = [vmem_spec] * len(out_shape)
-    out_shape += [jax.ShapeDtypeStruct((1, per_block, depth), jnp.bfloat16)] * len(emitted)
-    out_specs += [any_spec] * len(emitted)
+    out_shape += [jax.ShapeDtypeStruct((1, per_block, depth), jnp.bfloat16)] * staged
+    out_specs += [any_spec] * staged
     return pl.pallas_call(
-        functools.partial(matmul_body, spans, emitted, apart),
+        functools.partial(matmul_body, spans, staged, apart),
         in_specs=[pl.BlockSpec(memory_space=pltpu.SMEM)] + [any_spec] * (2 * len(chunks) + 1) + [vmem_spec],
         out_specs=out_specs,
         out_shape=out_shape,
@@ -135,9 +143,12 @@
             pltpu.VMEM((2, steps, per_block, depth), jnp.bfloat16),
             pltpu.VMEM((buffers, block_k, block_w), jnp.bfloat16),
             pltpu.VMEM((rows, columns), jnp.float32),
-            pltpu.SemaphoreType.DMA((2 * len(chunks) + len(emitted),)),
+            pltpu.SemaphoreType.DMA((2 * len(chunks),)),
             pltpu.SemaphoreType.DMA((buffers,)),
-        ],
+        ] + ([
+            pltpu.VMEM((staged, per_block, depth), jnp.bfloat16),
+            pltpu.SemaphoreType.DMA((staged + 1,)),
+        ] if staged else []),
         compiler_params=pltpu.CompilerParams(vmem_limit_bytes=VMEM_BYTES),
         cost_estimate=pl.CostEstimate(flops=0, bytes_accessed=0, transcendentals=0),
         name="partial_products",
@@ -351,10 +362,10 @@
 
     lead = step_count - 1
     parts, last_ranks = [((0, 0), lead)], {}
-    send, keep, *emitted = partial_products(
-        pos, [(source, siblings, 0, lead)], weight, factors, emitted=tuple(range(1, lead))
+    send, keep, *slices = partial_products(
+        pos, [(source, siblings, 0, lead)], weight, factors, staged=step_count - 1
     )
-    for step, rows in enumerate(emitted, 1):
+    for step, rows in enumerate(slices, 1):
         remote.update({(step, shift): from_rep(rows, shift) for shift in range(1, n_rep)})
     for piece, (step, shift) in enumerate(pieces):
         sends = gap(send, [(parts, send, keep, jnp.bfloat16)])
@@ -363,19 +374,14 @@
             panels, order = spread_panels(panels, order, bits[2:])
         sib = swap_cores(own)
         held = [sends, siblings] if piece == 0 else [sends]
-        if piece == len(pieces) - 1:
-            held += gap(lax.optimization_barrier((send, sends))[0], [], short=True)
         own, sib, held = lax.optimization_barrier((own, sib, held))
-        last, chunks, parts, places = step == step_count - 1, [(own, sib, 0, 1)], [((step, shift), 1)], ()
+        last, chunks, parts = step == step_count - 1, [(own, sib, 0, 1)], [((step, shift), 1)]
         if piece == 0:
             chunks.insert(0, (source, held[1], lead, 1))
             parts.insert(0, ((lead, 0), 1))
-            places = (0,)
-        send, keep, *outs = partial_products(pos, chunks, weight, factors, last, places)
+        send, keep, *ranks = partial_products(pos, chunks, weight, factors, last)
         if last:
-            last_ranks[shift] = outs
-        elif outs:
-            remote.update({(lead, along): from_rep(outs[0], along) for along in range(1, n_rep)})
+            last_ranks[shift] = ranks
     gap(send, [(parts, send, keep, jnp.bfloat16)])
     for shift, ranks in last_ranks.items():
         halved[RANK_NAME, shift] = second_half(ranks[1], swap_tensor(ranks[0], group // 2), 1, jnp.float32)[0]

time: 146 us -> 145 us (level)
  starting transfers between devices: 28 us -> 25.2 us
    ppermute x9, waiting for transfers between devices: 12.8 us -> 2.77 us  [swap_tensor(): return lax.ppermute(value, 'tp', [(i, i ^ bit) for i in range(n_tensor)])]
    ppermute x4, waiting for transfers between devices: 9.73 us -> 14.1 us  [from_rep(): lax.ppermute(value, 'rep', [((i + shift) % n_rep, i) for i in range(n_rep)])]
    ppermute x5, waiting for transfers between devices: 12.7 us -> 15.7 us  [to_group(): lax.ppermute(value, 'tp', [(i, (i + moved) % n_tensor) for i in range(n_t...]
    ppermute x3, waiting for transfers between devices: 1.92 us -> 4.31 us  [per_device(): lax.ppermute(masked, ('rep', 'sub'), [(i, (i + turn) % n_owners) for i in...]
    ppermute x5, starting transfers between devices: 12 us -> 10.5 us  [to_group(): lax.ppermute(value, 'tp', [(i, (i + moved) % n_tensor) for i in range(n_t...]
    unnamed x28 -> x32, local copies, waits for them, and re-layouts: 2.36 us -> 3.33 us
  transfers between devices with their start and end apart: 26 -> 26, of which waited for: 11 -> 10; matrix products, arithmetic and copies ran while one was open for 4% -> 4% of each run, Pallas kernels for 49% -> 50%
where the time goes in v13:
time: 145 us
  Pallas kernels  73.6 us (51%)
  waiting for transfers between devices  36.9 us (25%)
  starting transfers between devices  25.2 us (17%)
  local copies, waits for them, and re-layouts  6.38 us (4%)
  other arithmetic  2.39 us (2%)
    pallas_call x5, Pallas kernels, partial_products(): pl.pallas_call(functools.partial(matmul_body, spans, staged, apart), in_s...  70.3 us
    ppermute x5, waiting for transfers between devices, to_group(): lax.ppermute(value, 'tp', [(i, (i + moved) % n_tensor) for i in range(n_t...  15.7 us
    ppermute x4, waiting for transfers between devices, from_rep(): lax.ppermute(value, 'rep', [((i + shift) % n_rep, i) for i in range(n_rep)])  14.1 us
    ppermute x5, starting transfers between devices, to_group(): lax.ppermute(value, 'tp', [(i, (i + moved) % n_tensor) for i in range(n_t...  10.5 us
    ppermute x9, starting transfers between devices, swap_tensor(): return lax.ppermute(value, 'tp', [(i, i ^ bit) for i in range(n_tensor)])  8.89 us
    ppermute x4, starting transfers between devices, from_rep(): lax.ppermute(value, 'rep', [((i + shift) % n_rep, i) for i in range(n_rep)])  4.41 us
    ppermute x3, waiting for transfers between devices, per_device(): lax.ppermute(masked, ('rep', 'sub'), [(i, (i + turn) % n_owners) for i in...  4.31 us
    unnamed x32, local copies, waits for them, and re-layouts  3.33 us
  transfers between devices with their start and end apart: 26, of which 10 were waited for; matrix products, arithmetic and copies ran while one was open for 4% of the time, Pallas kernels for 50%

profile of v13, /device:TPU:0, one launch (start us, length us, event | category | flops | bytes accessed | tf_op | source)
XLA Modules:
  0.0 144.8 jit_solution(11757574190613764442)
XLA Ops:
  0.5 2.2 %slice.64 = bf16[1,64,7168]{2,1,0:T(8,128)(2,1)} slice(bf16[4,64,7168]{2,1,0:T(8,128)(2,1)} %refs_0_.3), slice={[0:1], [0:64], [0:7168]} | slice | bytes 1835008 | tf_op jit(solution)/shard_map/slice | solution.py:285
  2.7 2.6 %collective-permute-start.3 = (bf16[1,64,7168]{2,1,0:T(8,128)(2,1)}, bf16[1,64,7168]{2,1,0:T(8,128)(2,1)}, u32[]{:S(2)}, u32[]{:S(2)}) collective-permute-start(bf16[1,64,7168]{2,1,0:T(8,128)(2,1)} %slice.64), channel_id=1, source_target_pairs={{2,0},{0,2},{3,1},{1,3},{6,4},{4,6},{7,5},{5,7},{10,8},{8,10},{11,... | collective-permute-start | bytes 2752520 | tf_op jit(solution)/shard_map/ppermute | solution.py:263
  5.3 1.6 %collective-permute-start.4 = (bf16[1,64,2048]{2,1,0:T(8,128)(2,1)S(1)}, bf16[1,64,2048]{2,1,0:T(8,128)(2,1)S(1)}, u32[]{:S(2)}, u32[]{:S(2)}) collective-permute-start(bf16[1,64,2048]{2,1,0:T(8,128)(2,1)S(1)} %copy-done.6), channel_id=1, source_target_pairs={{0,4},{4,0},{8,12},{12,8},{1,5},{5,1},{9,13},{13,9},{2,6},{6,2},{1... | collective-permute-start | bytes 786440 | tf_op jit(solution)/shard_map/ppermute | solution.py:266
  6.9 2.6 %collective-permute-start.5 = (bf16[1,64,2048]{2,1,0:T(8,128)(2,1)S(1)}, bf16[1,64,2048]{2,1,0:T(8,128)(2,1)S(1)}, u32[]{:S(2)}, u32[]{:S(2)}) collective-permute-start(bf16[1,64,2048]{2,1,0:T(8,128)(2,1)S(1)} %copy-done.6), channel_id=1, source_target_pairs={{0,8},{4,12},{8,0},{12,4},{1,9},{5,13},{9,1},{13,5},{2,10},{6,14},... | collective-permute-start | bytes 786440 | tf_op jit(solution)/shard_map/ppermute | solution.py:266
  9.7 22.8 %partial_products.5 = (bf16[192,2176]{1,0:T(8,128)(2,1)}, f32[192,2176]{1,0:T(8,128)S(1)}, bf16[1,64,7168]{2,1,0:T(8,128)(2,1)}, bf16[1,64,7168]{2,1,0:T(8,128)(2,1)S(1)}, bf16[1,64,7168]{2,1,0:T(8,128)(2,1)S(1)}) custom-call(s32[1]{0:T(128)} %bitcast.1.pos_ref, bf16[4,64,7168]{2,1,0:T(8,128)(2,1)} %refs_0_.3, ...), custom_call_target="tpu_custom_call" | custom-call | tf_op jit(solution)/shard_map/partial_products/pallas_call | solution.py:137
  32.5 0.9 copy-done.12
  33.5 0.9 copy-done.14
  36.3 1.4 collective-permute-start.11
  37.8 0.8 reshape.119.slot_ref
  38.6 1.0 collective-permute-start.1
  39.6 15.4 %partial_products.6 = (bf16[128,2176]{1,0:T(8,128)(2,1)S(1)}, f32[128,2176]{1,0:T(8,128)S(1)}) custom-call(s32[1]{0:T(128)} %bitcast.1.pos_ref, bf16[4,64,7168]{2,1,0:T(8,128)(2,1)} %refs_0_.3, bf16[4,64,7168]{2,1,0:T(8,128)(2,1)} %collective-permute-done.refs_1_, bf16[1,64,7168]{2,1,0:T(8,128)(2,1)} %collective-permute-done.3.refs_2_, ...), custom_call_target="tpu_custom_call" | custom-call | tf_op jit(solution)/shard_map/partial_products/pallas_call | solution.py:137
  55.0 4.3 %collective-permute-done.2.refs_0_ = bf16[1,64,7168]{2,1,0:T(8,128)(2,1)S(1)} collective-permute-done((bf16[1,64,7168]{2,1,0:T(8,128)(2,1)}, bf16[1,64,7168]{2,1,0:T(8,128)(2,1)S(1)}, u32[]{:S(2)}, u32[]{:S(2)}) %collective-permute-start.2) | collective-permute-done | bytes 917536 | tf_op jit(solution)/shard_map/ppermute | solution.py:263
  59.7 1.4 collective-permute-start.10
  61.1 1.3 convert_add_fusion
  62.5 10.7 %partial_products.7 = (bf16[64,2176]{1,0:T(8,128)(2,1)S(1)}, f32[64,2176]{1,0:T(8,128)S(1)}) custom-call(s32[1]{0:T(128)} %bitcast.1.pos_ref, bf16[1,64,7168]{2,1,0:T(8,128)(2,1)S(1)} %collective-permute-done.2.refs_0_, bf16[1,64,7168]{2,1,0:T(8,128)(2,1)S(1)} %collective-permute-done.8.refs_1_, bf16[7168,2048]{1,0:T(8,128)(2,1)} %refs_2_.7, ...), custom_call_target="tpu_custom_call" | custom-call | tf_op jit(solution)/shard_map/partial_products/pallas_call | solution.py:137
  73.2 5.8 %collective-permute-done.1.refs_0_ = bf16[1,64,7168]{2,1,0:T(8,128)(2,1)S(1)} collective-permute-done((bf16[1,64,7168]{2,1,0:T(8,128)(2,1)}, bf16[1,64,7168]{2,1,0:T(8,128)(2,1)S(1)}, u32[]{:S(2)}, u32[]{:S(2)}) %collective-permute-start.1) | collective-permute-done | bytes 917536 | tf_op jit(solution)/shard_map/ppermute | solution.py:263
  78.9 0.7 collective-permute-start.15
  79.8 3.5 %collective-permute-start.12 = (bf16[64,2176]{1,0:T(8,128)(2,1)S(1)}, bf16[64,2176]{1,0:T(8,128)(2,1)S(1)}, u32[]{:S(2)}, u32[]{:S(2)}) collective-permute-start(bf16[64,2176]{1,0:T(8,128)(2,1)S(1)} %select_convert_fusion.2), channel_id=1, source_target_pairs={{0,8},{4,12},{8,0},{12,4},{1,9},{5,13},{9,1},{13,5},{2,10},{6,14},... | collective-permute-start | bytes 835592 | tf_op jit(solution)/shard_map/ppermute | solution.py:270
  83.3 10.7 %partial_products.8 = (bf16[64,2176]{1,0:T(8,128)(2,1)S(1)}, f32[64,2176]{1,0:T(8,128)S(1)}) custom-call(s32[1]{0:T(128)} %bitcast.1.pos_ref, bf16[1,64,7168]{2,1,0:T(8,128)(2,1)S(1)} %collective-permute-done.1.refs_0_, bf16[1,64,7168]{2,1,0:T(8,128)(2,1)S(1)} %collective-permute-done.9.refs_1_, bf16[7168,2048]{1,0:T(8,128)(2,1)} %refs_2_.7, ...), custom_call_target="tpu_custom_call" | custom-call | tf_op jit(solution)/shard_map/partial_products/pallas_call | solution.py:137
  94.0 4.1 %collective-permute-done.13.refs_0_ = bf16[1,64,7168]{2,1,0:T(8,128)(2,1)S(1)} collective-permute-done((bf16[1,64,7168]{2,1,0:T(8,128)(2,1)S(1)}, bf16[1,64,7168]{2,1,0:T(8,128)(2,1)S(1)}, u32[]{:S(2)}, u32[]{:S(2)}) %collective-permute-start.13) | collective-permute-done | bytes 917536 | tf_op jit(solution)/shard_map/ppermute | solution.py:263
  98.3 0.8 collective-permute-start.17
  99.2 3.5 %collective-permute-start.16 = (bf16[64,2176]{1,0:T(8,128)(2,1)S(1)}, bf16[64,2176]{1,0:T(8,128)(2,1)S(1)}, u32[]{:S(2)}, u32[]{:S(2)}) collective-permute-start(bf16[64,2176]{1,0:T(8,128)(2,1)S(1)} %select_convert_fusion.1), channel_id=1, source_target_pairs={{0,8},{4,12},{8,0},{12,4},{1,9},{5,13},{9,1},{13,5},{2,10},{6,14},... | collective-permute-start | bytes 835592 | tf_op jit(solution)/shard_map/ppermute | solution.py:270
  102.7 10.7 %partial_products.9 = (bf16[64,2048]{1,0:T(8,128)(2,1)S(1)}, f32[64,2048]{1,0:T(8,128)S(1)}, f32[64,128]{1,0:T(8,128)S(1)}, f32[64,128]{1,0:T(8,128)S(1)}) custom-call(s32[1]{0:T(128)} %bitcast.1.pos_ref, bf16[1,64,7168]{2,1,0:T(8,128)(2,1)S(1)} %collective-permute-done.13.refs_0_, bf16[1,64,7168]{2,1,0:T(8,128)(2,1)S(1)} %collective-permute-done.14.refs_1_, ...), custom_call_target="tpu_custom_call" | custom-call | tf_op jit(solution)/shard_map/partial_products/pallas_call | solution.py:137
  113.6 2.1 %collective-permute-start.18 = (bf16[64,2176]{1,0:T(8,128)(2,1)S(1)}, bf16[64,2176]{1,0:T(8,128)(2,1)S(1)}, u32[]{:S(2)}, u32[]{:S(2)}) collective-permute-start(bf16[64,2176]{1,0:T(8,128)(2,1)S(1)} %select_convert_fusion), channel_id=1, source_target_pairs={{0,8},{4,12},{8,0},{12,4},{1,9},{5,13},{9,1},{13,5},{2,10},{6,14},... | collective-permute-start | bytes 835592 | tf_op jit(solution)/shard_map/ppermute | solution.py:270
  116.0 2.7 %collective-permute-done.19 = f32[64,128]{1,0:T(8,128)S(1)} collective-permute-done((f32[64,128]{1,0:T(8,128)S(1)}, f32[64,128]{1,0:T(8,128)S(1)}, u32[]{:S(2)}, u32[]{:S(2)}) %collective-permute-start.19) | collective-permute-done | bytes 32800 | tf_op jit(solution)/shard_map/ppermute | solution.py:266
  118.9 11.2 %collective-permute-done.20 = f32[64,128]{1,0:T(8,128)S(1)} collective-permute-done((f32[64,128]{1,0:T(8,128)S(1)}, f32[64,128]{1,0:T(8,128)S(1)}, u32[]{:S(2)}, u32[]{:S(2)}) %collective-permute-start.20) | collective-permute-done | bytes 32800 | tf_op jit(solution)/shard_map/ppermute | solution.py:270
  130.3 1.3 collective-permute-start.25
  132.7 1.4 collective-permute-done.24
  134.1 2.6 %collective-permute-done.23 = bf16[4,64,64]{2,1,0:T(8,128)(2,1)S(1)} collective-permute-done((bf16[4,64,64]{2,1,0:T(8,128)(2,1)S(1)}, bf16[4,64,64]{2,1,0:T(8,128)(2,1)S(1)}, u32[]{:S(2)}, u32[]{:S(2)}) %collective-permute-start.23) | collective-permute-done | bytes 32800 | tf_op jit(solution)/shard_map/ppermute | solution.py:409
  137.1 2.5 %finish_steps.1 = (bf16[4,64,2048]{2,1,0:T(8,128)(2,1)}, bf16[64,2048]{1,0:T(8,128)(2,1)S(1)}) custom-call(bf16[256,64]{1,0:T(8,128)(2,1)S(1)} %bitcast.30, s32[256,1]{1,0:T(8,128)S(1)} %copy-done.3, s32[4]{0:T(128)S(1)} %pad_add_fusion.order_ref, bf16[64,2048]{1,0:T(8,128)(2,1)S(1)} %bitcast.31, bf16[64,2048]{1,0:T(8,128)(2,1)S(1)} %bitcast.32, ...), custom_call_target="tpu_custom_call" | custom-call | tf_op jit(solution)/shard_map/finish_steps/pallas_call | solution.py:195
  139.6 4.4 %collective-permute-done.25.refs_1_ = bf16[64,2048]{1,0:T(8,128)(2,1)S(1)} collective-permute-done((bf16[64,2048]{1,0:T(8,128)(2,1)S(1)}, bf16[64,2048]{1,0:T(8,128)(2,1)S(1)}, u32[]{:S(2)}, u32[]{:S(2)}) %collective-permute-start.25) | collective-permute-done | bytes 262176 | tf_op jit(solution)/shard_map/ppermute | solution.py:270
  144.0 0.8 finish_last.1
  (89 shorter events, 5.9 us)
Async XLA Ops:
  0.0 37.6 %copy-start = (s32[256,1]{0,1:T(1,128)S(1)}, s32[256,1]{0,1:T(1,128)}, u32[]{:S(2)}) copy-start(s32[256,1]{0,1:T(1,128)} %param.10) | copy-start | bytes 3076
  0.0 9.7 %copy-start.2 = (bf16[1,7168,64]{1,2,0:T(8,128)(2,1)S(1)}, bf16[1,7168,64]{1,2,0:T(8,128)(2,1)}, u32[]{:S(2)}) copy-start(bf16[1,7168,64]{1,2,0:T(8,128)(2,1)} %param.8) | copy-start | bytes 2752516
  0.0 9.7 %collective-permute-start = (bf16[4,64,7168]{2,1,0:T(8,128)(2,1)}, bf16[4,64,7168]{2,1,0:T(8,128)(2,1)}, u32[]{:S(2)}, u32[]{:S(2)}) collective-permute-start(bf16[4,64,7168]{2,1,0:T(8,128)(2,1)} %refs_0_.3), channel_id=1, source_target_pairs={{0,1},{1,0},{2,3},{3,2},{4,5},{5,4},{6,7},{7,6},{8,9},{9,8},{10,11... | collective-permute-start | bytes 11010056 | tf_op jit(solution)/shard_map/ppermute | solution.py:260
  2.7 33.1 %collective-permute-start.3 = (bf16[1,64,7168]{2,1,0:T(8,128)(2,1)}, bf16[1,64,7168]{2,1,0:T(8,128)(2,1)}, u32[]{:S(2)}, u32[]{:S(2)}) collective-permute-start(bf16[1,64,7168]{2,1,0:T(8,128)(2,1)} %slice.64), channel_id=1, source_target_pairs={{2,0},{0,2},{3,1},{1,3},{6,4},{4,6},{7,5},{5,7},{10,8},{8,10},{11,... | collective-permute-start | bytes 2752520 | tf_op jit(solution)/shard_map/ppermute | solution.py:263
  5.3 29.1 %collective-permute-start.4 = (bf16[1,64,2048]{2,1,0:T(8,128)(2,1)S(1)}, bf16[1,64,2048]{2,1,0:T(8,128)(2,1)S(1)}, u32[]{:S(2)}, u32[]{:S(2)}) collective-permute-start(bf16[1,64,2048]{2,1,0:T(8,128)(2,1)S(1)} %copy-done.6), channel_id=1, source_target_pairs={{0,4},{4,0},{8,12},{12,8},{1,5},{5,1},{9,13},{13,9},{2,6},{6,2},{1... | collective-permute-start | bytes 786440 | tf_op jit(solution)/shard_map/ppermute | solution.py:266
  6.9 28.3 %collective-permute-start.5 = (bf16[1,64,2048]{2,1,0:T(8,128)(2,1)S(1)}, bf16[1,64,2048]{2,1,0:T(8,128)(2,1)S(1)}, u32[]{:S(2)}, u32[]{:S(2)}) collective-permute-start(bf16[1,64,2048]{2,1,0:T(8,128)(2,1)S(1)} %copy-done.6), channel_id=1, source_target_pairs={{0,8},{4,12},{8,0},{12,4},{1,9},{5,13},{9,1},{13,5},{2,10},{6,14},... | collective-permute-start | bytes 786440 | tf_op jit(solution)/shard_map/ppermute | solution.py:266
  9.4 26.4 %collective-permute-start.6 = (bf16[1,64,2048]{2,1,0:T(8,128)(2,1)S(1)}, bf16[1,64,2048]{2,1,0:T(8,128)(2,1)}, u32[]{:S(2)}, u32[]{:S(2)}) collective-permute-start(bf16[1,64,2048]{2,1,0:T(8,128)(2,1)S(1)} %copy-done.6), channel_id=1, source_target_pairs={{0,12},{4,8},{8,4},{12,0},{1,13},{5,9},{9,5},{13,1},{2,14},{6,10},... | collective-permute-start | bytes 786440 | tf_op jit(solution)/shard_map/ppermute | solution.py:266
  9.7 28.0 %copy-start.15 = (s32[4]{0:T(128)S(1)}, s32[4]{0:T(128)}, u32[]{:S(2)}) copy-start(s32[4]{0:T(128)} %param.11) | copy-start | bytes 52
  35.8 3.8 %collective-permute-start.7 = (bf16[1,64,7168]{2,1,0:T(8,128)(2,1)}, bf16[1,64,7168]{2,1,0:T(8,128)(2,1)}, u32[]{:S(2)}, u32[]{:S(2)}) collective-permute-start(bf16[1,64,7168]{2,1,0:T(8,128)(2,1)} %collective-permute-done.3.refs_2_), channel_id=1, source_target_pairs={{0,1},{1,0},{2,3},{3,2},{4,5},{5,4},{6,7},{7,6},{8,9},{9,8},{10,11... | collective-permute-start | bytes 2752520 | tf_op jit(solution)/shard_map/ppermute | solution.py:260
  35.8 23.4 %collective-permute-start.2 = (bf16[1,64,7168]{2,1,0:T(8,128)(2,1)}, bf16[1,64,7168]{2,1,0:T(8,128)(2,1)S(1)}, u32[]{:S(2)}, u32[]{:S(2)}) collective-permute-start(bf16[1,64,7168]{2,1,0:T(8,128)(2,1)} %get-tuple-element.73), channel_id=1, source_target_pairs={{2,0},{0,2},{3,1},{1,3},{6,4},{4,6},{7,5},{5,7},{10,8},{8,10},{11,... | collective-permute-start | bytes 2752520 | tf_op jit(solution)/shard_map/ppermute | solution.py:263
  36.3 24.8 %collective-permute-start.11 = (bf16[192,2176]{1,0:T(8,128)(2,1)}, bf16[192,2176]{1,0:T(8,128)(2,1)}, u32[]{:S(2)}, u32[]{:S(2)}) collective-permute-start(bf16[192,2176]{1,0:T(8,128)(2,1)} %get-tuple-element.74), channel_id=1, source_target_pairs={{0,4},{4,0},{8,12},{12,8},{1,5},{5,1},{9,13},{13,9},{2,6},{6,2},{1... | collective-permute-start | bytes 2506760 | tf_op jit(solution)/shard_map/ppermute | solution.py:266
  38.6 20.7 %copy-start.13 = (bf16[1,64,7168]{2,1,0:T(8,128)(2,1)S(1)}, bf16[1,64,7168]{2,1,0:T(8,128)(2,1)}, u32[]{:S(2)}) copy-start(bf16[1,64,7168]{2,1,0:T(8,128)(2,1)} %copy-done.12) | copy-start | bytes 2752516
  38.6 40.3 %collective-permute-start.1 = (bf16[1,64,7168]{2,1,0:T(8,128)(2,1)}, bf16[1,64,7168]{2,1,0:T(8,128)(2,1)S(1)}, u32[]{:S(2)}, u32[]{:S(2)}) collective-permute-start(bf16[1,64,7168]{2,1,0:T(8,128)(2,1)} %copy-done.14), channel_id=1, source_target_pairs={{2,0},{0,2},{3,1},{1,3},{6,4},{4,6},{7,5},{5,7},{10,8},{8,10},{11,... | collective-permute-start | bytes 2752520 | tf_op jit(solution)/shard_map/ppermute | solution.py:263
  59.3 3.2 %collective-permute-start.8 = (bf16[1,64,7168]{2,1,0:T(8,128)(2,1)S(1)}, bf16[1,64,7168]{2,1,0:T(8,128)(2,1)S(1)}, u32[]{:S(2)}, u32[]{:S(2)}) collective-permute-start(bf16[1,64,7168]{2,1,0:T(8,128)(2,1)S(1)} %collective-permute-done.2.refs_0_), channel_id=1, source_target_pairs={{0,1},{1,0},{2,3},{3,2},{4,5},{5,4},{6,7},{7,6},{8,9},{9,8},{10,11... | collective-permute-start | bytes 2752520 | tf_op jit(solution)/shard_map/ppermute | solution.py:260
  59.4 38.8 %collective-permute-start.13 = (bf16[1,64,7168]{2,1,0:T(8,128)(2,1)S(1)}, bf16[1,64,7168]{2,1,0:T(8,128)(2,1)S(1)}, u32[]{:S(2)}, u32[]{:S(2)}) collective-permute-start(bf16[1,64,7168]{2,1,0:T(8,128)(2,1)S(1)} %copy-done.13), channel_id=1, source_target_pairs={{2,0},{0,2},{3,1},{1,3},{6,4},{4,6},{7,5},{5,7},{10,8},{8,10},{11,... | collective-permute-start | bytes 2752520 | tf_op jit(solution)/shard_map/ppermute | solution.py:263
  59.7 19.9 %collective-permute-start.10 = (bf16[128,2176]{1,0:T(8,128)(2,1)S(1)}, bf16[128,2176]{1,0:T(8,128)(2,1)S(1)}, u32[]{:S(2)}, u32[]{:S(2)}) collective-permute-start(bf16[128,2176]{1,0:T(8,128)(2,1)S(1)} %get-tuple-element.83), channel_id=1, source_target_pairs={{0,4},{4,0},{8,12},{12,8},{1,5},{5,1},{9,13},{13,9},{2,6},{6,2},{1... | collective-permute-start | bytes 1671176 | tf_op jit(solution)/shard_map/ppermute | solution.py:266
  78.9 4.4 %collective-permute-start.9 = (bf16[1,64,7168]{2,1,0:T(8,128)(2,1)S(1)}, bf16[1,64,7168]{2,1,0:T(8,128)(2,1)S(1)}, u32[]{:S(2)}, u32[]{:S(2)}) collective-permute-start(bf16[1,64,7168]{2,1,0:T(8,128)(2,1)S(1)} %collective-permute-done.1.refs_0_), channel_id=1, source_target_pairs={{0,1},{1,0},{2,3},{3,2},{4,5},{5,4},{6,7},{7,6},{8,9},{9,8},{10,11... | collective-permute-start | bytes 2752520 | tf_op jit(solution)/shard_map/ppermute | solution.py:260
  78.9 19.2 %collective-permute-start.15 = (bf16[64,2176]{1,0:T(8,128)(2,1)S(1)}, bf16[64,2176]{1,0:T(8,128)(2,1)S(1)}, u32[]{:S(2)}, u32[]{:S(2)}) collective-permute-start(bf16[64,2176]{1,0:T(8,128)(2,1)S(1)} %get-tuple-element.91), channel_id=1, source_target_pairs={{0,4},{4,0},{8,12},{12,8},{1,5},{5,1},{9,13},{13,9},{2,6},{6,2},{1... | collective-permute-start | bytes 835592 | tf_op jit(solution)/shard_map/ppermute | solution.py:266
  79.8 18.5 %collective-permute-start.12 = (bf16[64,2176]{1,0:T(8,128)(2,1)S(1)}, bf16[64,2176]{1,0:T(8,128)(2,1)S(1)}, u32[]{:S(2)}, u32[]{:S(2)}) collective-permute-start(bf16[64,2176]{1,0:T(8,128)(2,1)S(1)} %select_convert_fusion.2), channel_id=1, source_target_pairs={{0,8},{4,12},{8,0},{12,4},{1,9},{5,13},{9,1},{13,5},{2,10},{6,14},... | collective-permute-start | bytes 835592 | tf_op jit(solution)/shard_map/ppermute | solution.py:270
  98.1 4.6 %collective-permute-start.14 = (bf16[1,64,7168]{2,1,0:T(8,128)(2,1)S(1)}, bf16[1,64,7168]{2,1,0:T(8,128)(2,1)S(1)}, u32[]{:S(2)}, u32[]{:S(2)}) collective-permute-start(bf16[1,64,7168]{2,1,0:T(8,128)(2,1)S(1)} %collective-permute-done.13.refs_0_), channel_id=1, source_target_pairs={{0,1},{1,0},{2,3},{3,2},{4,5},{5,4},{6,7},{7,6},{8,9},{9,8},{10,11... | collective-permute-start | bytes 2752520 | tf_op jit(solution)/shard_map/ppermute | solution.py:260
  98.3 15.1 %copy-start.4 = (bf16[64,2176]{1,0:T(8,128)(2,1)}, bf16[64,2176]{1,0:T(8,128)(2,1)S(1)}, u32[]{:S(2)}) copy-start(bf16[64,2176]{1,0:T(8,128)(2,1)S(1)} %collective-permute-done.12.refs_5_) | copy-start | bytes 835588
  98.3 15.2 %collective-permute-start.17 = (bf16[64,2176]{1,0:T(8,128)(2,1)S(1)}, bf16[64,2176]{1,0:T(8,128)(2,1)S(1)}, u32[]{:S(2)}, u32[]{:S(2)}) collective-permute-start(bf16[64,2176]{1,0:T(8,128)(2,1)S(1)} %get-tuple-element.121), channel_id=1, source_target_pairs={{0,4},{4,0},{8,12},{12,8},{1,5},{5,1},{9,13},{13,9},{2,6},{6,2},{1... | collective-permute-start | bytes 835592 | tf_op jit(solution)/shard_map/ppermute | solution.py:266
  99.2 16.6 %collective-permute-start.16 = (bf16[64,2176]{1,0:T(8,128)(2,1)S(1)}, bf16[64,2176]{1,0:T(8,128)(2,1)S(1)}, u32[]{:S(2)}, u32[]{:S(2)}) collective-permute-start(bf16[64,2176]{1,0:T(8,128)(2,1)S(1)} %select_convert_fusion.1), channel_id=1, source_target_pairs={{0,8},{4,12},{8,0},{12,4},{1,9},{5,13},{9,1},{13,5},{2,10},{6,14},... | collective-permute-start | bytes 835592 | tf_op jit(solution)/shard_map/ppermute | solution.py:270
  113.4 5.4 %collective-permute-start.19 = (f32[64,128]{1,0:T(8,128)S(1)}, f32[64,128]{1,0:T(8,128)S(1)}, u32[]{:S(2)}, u32[]{:S(2)}) collective-permute-start(f32[64,128]{1,0:T(8,128)S(1)} %get-tuple-element.127), channel_id=1, source_target_pairs={{0,4},{4,0},{8,12},{12,8},{1,5},{5,1},{9,13},{13,9},{2,6},{6,2},{1... | collective-permute-start | bytes 98312 | tf_op jit(solution)/shard_map/ppermute | solution.py:266
  113.6 18.0 %collective-permute-start.18 = (bf16[64,2176]{1,0:T(8,128)(2,1)S(1)}, bf16[64,2176]{1,0:T(8,128)(2,1)S(1)}, u32[]{:S(2)}, u32[]{:S(2)}) collective-permute-start(bf16[64,2176]{1,0:T(8,128)(2,1)S(1)} %select_convert_fusion), channel_id=1, source_target_pairs={{0,8},{4,12},{8,0},{12,4},{1,9},{5,13},{9,1},{13,5},{2,10},{6,14},... | collective-permute-start | bytes 835592 | tf_op jit(solution)/shard_map/ppermute | solution.py:270
  115.8 14.4 %collective-permute-start.21 = (bf16[64,2048]{1,0:T(8,128)(2,1)S(1)}, bf16[64,2048]{1,0:T(8,128)(2,1)S(1)}, u32[]{:S(2)}, u32[]{:S(2)}) collective-permute-start(bf16[64,2048]{1,0:T(8,128)(2,1)S(1)} %get-tuple-element.130), channel_id=1, source_target_pairs={{0,4},{4,0},{8,12},{12,8},{1,5},{5,1},{9,13},{13,9},{2,6},{6,2},{1... | collective-permute-start | bytes 786440 | tf_op jit(solution)/shard_map/ppermute | solution.py:266
  118.8 11.3 %collective-permute-start.20 = (f32[64,128]{1,0:T(8,128)S(1)}, f32[64,128]{1,0:T(8,128)S(1)}, u32[]{:S(2)}, u32[]{:S(2)}) collective-permute-start(f32[64,128]{1,0:T(8,128)S(1)} %get-tuple-element.139), channel_id=1, source_target_pairs={{0,8},{4,12},{8,0},{12,4},{1,9},{5,13},{9,1},{13,5},{2,10},{6,14},... | collective-permute-start | bytes 98312 | tf_op jit(solution)/shard_map/ppermute | solution.py:270
  130.3 13.8 %collective-permute-start.25 = (bf16[64,2048]{1,0:T(8,128)(2,1)S(1)}, bf16[64,2048]{1,0:T(8,128)(2,1)S(1)}, u32[]{:S(2)}, u32[]{:S(2)}) collective-permute-start(bf16[64,2048]{1,0:T(8,128)(2,1)S(1)} %select_convert_fusion.3), channel_id=1, source_target_pairs={{0,8},{4,12},{8,0},{12,4},{1,9},{5,13},{9,1},{13,5},{2,10},{6,14},... | collective-permute-start | bytes 786440 | tf_op jit(solution)/shard_map/ppermute | solution.py:270
  131.7 2.4 %collective-permute-start.24 = (bf16[4,64,64]{2,1,0:T(8,128)(2,1)S(1)}, bf16[4,64,64]{2,1,0:T(8,128)(2,1)S(1)}, u32[]{:S(2)}, u32[]{:S(2)}) collective-permute-start(bf16[4,64,64]{2,1,0:T(8,128)(2,1)S(1)} %select_bitcast_fusion), channel_id=1, source_target_pairs={{0,3},{1,0},{2,1},{3,2},{4,7},{5,4},{6,5},{7,6},{8,11},{9,8},{10,9... | collective-permute-start | bytes 98312 | tf_op jit(solution)/shard_map/ppermute | solution.py:409
  131.8 5.0 %collective-permute-start.23 = (bf16[4,64,64]{2,1,0:T(8,128)(2,1)S(1)}, bf16[4,64,64]{2,1,0:T(8,128)(2,1)S(1)}, u32[]{:S(2)}, u32[]{:S(2)}) collective-permute-start(bf16[4,64,64]{2,1,0:T(8,128)(2,1)S(1)} %select_bitcast_fusion), channel_id=1, source_target_pairs={{0,2},{1,3},{2,0},{3,1},{4,6},{5,7},{6,4},{7,5},{8,10},{9,11},{10,... | collective-permute-start | bytes 98312 | tf_op jit(solution)/shard_map/ppermute | solution.py:409
  132.4 4.6 %collective-permute-start.22 = (bf16[4,64,64]{2,1,0:T(8,128)(2,1)S(1)}, bf16[4,64,64]{2,1,0:T(8,128)(2,1)S(1)}, u32[]{:S(2)}, u32[]{:S(2)}) collective-permute-start(bf16[4,64,64]{2,1,0:T(8,128)(2,1)S(1)} %select_bitcast_fusion), channel_id=1, source_target_pairs={{0,1},{1,2},{2,3},{3,0},{4,5},{5,6},{6,7},{7,4},{8,9},{9,10},{10,1... | collective-permute-start | bytes 98312 | tf_op jit(solution)/shard_map/ppermute | solution.py:409
  137.1 7.7 %copy-start.1 = (s32[256,1]{0,1:T(1,128)S(1)}, s32[256,1]{0,1:T(1,128)}, u32[]{:S(2)}) copy-start(s32[256,1]{0,1:T(1,128)} %param.10) | copy-start | bytes 3076
  (11 other events, 48.7 us)

commit v14 on v13

--- a/solution.py
+++ b/solution.py
@@ -12,7 +12,7 @@
 BLOCK = 1024
 BUFFERS = 4
 RANK_NAME = 1000
-VMEM_BYTES = 22 * 1024 * 1024
+VMEM_BYTES = 20 * 1024 * 1024
 
 
 def block_shape(depth, width):
@@ -132,7 +132,7 @@
         jax.ShapeDtypeStruct((rows, columns), jnp.float32),
     ] + [jax.ShapeDtypeStruct((rows, extra), jnp.float32)] * (2 if apart else 0)
     out_specs = [vmem_spec] * len(out_shape)
-    out_shape += [jax.ShapeDtypeStruct((1, per_block, depth), jnp.bfloat16)] * staged
+    out_shape += [pltpu.HBM((1, per_block, depth), jnp.bfloat16)] * staged
     out_specs += [any_spec] * staged
     return pl.pallas_call(
         functools.partial(matmul_body, spans, staged, apart),
@@ -291,8 +291,9 @@
         return panels, order
 
     bits = [n_tensor >> at for at in range(1, n_tensor.bit_length())]
-    order = [0] + [at for at in range(1, n_tensor) if at % (n_tensor // 4) == 0]
+    order = [0, bits[0], bits[1]]
     panels = [up_b] + [swap_tensor(up_b, at) for at in order[1:]]
+
     my_ids = lax.dynamic_slice_in_dim(adapter_ids, tensor_index * rows_mine, rows_mine)
     iota = lax.broadcasted_iota(jnp.int32, (rows_mine, slot_count), 1)
     my_slot = jnp.sum((my_ids == iota).astype(jnp.int32) * owner_map[None, :], axis=1)
@@ -316,7 +317,7 @@
             bit //= 2
         return total.reshape(steps, extent, columns)
 
-    def gap(token, jobs, short=False):
+    def gap(token, jobs):
         nonlocal first_leg, second_leg
         for parts, received, keep, kind in first_leg:
             steps = sum(length for _, length in parts)
@@ -327,12 +328,7 @@
                     if (key[0] + at - begin, key[1]) == (step_count - 1, 0):
                         halved[RANK_NAME, 0] = total[at][:, width:]
                 begin += length
-        closed, waiting = {}, []
-        for name, kept, received, lag in second_leg:
-            if short or lag > 1:
-                waiting.append((name, kept, received, lag if short else lag - 1))
-            else:
-                closed[name] = (after(kept, token), *received)
+        closed = {name: (after(kept, token), *received) for name, kept, received in second_leg}
         started, sends = [], []
         for name in sorted({name for name, _ in halved}):
             if name in begun or name == RANK_NAME or any((name, at) not in halved for at in range(n_rep)):
@@ -352,16 +348,16 @@
         first_leg = [
             (parts, swap_tensor(send, group // 2), keep, kind) for (parts, _, keep, kind), send in zip(jobs, first_sends)
         ]
-        second_leg = waiting + [
-            (name, kept, [to_group(value, hop + 1) for hop, value in enumerate(sent)], 2 if short else 1)
+        second_leg = [
+            (name, kept, [to_group(value, hop + 1) for hop, value in enumerate(sent)])
             for (name, kept), sent in zip(started, sends)
         ]
         return sends
 
     factors = jnp.swapaxes(down_a, 1, 2)
 
-    lead = step_count - 1
-    parts, last_ranks = [((0, 0), lead)], {}
+    lead = step_count // 2
+    parts, last_ranks, next_local = [((0, 0), lead)], {}, lead
     send, keep, *slices = partial_products(
         pos, [(source, siblings, 0, lead)], weight, factors, staged=step_count - 1
     )
@@ -371,14 +367,15 @@
         sends = gap(send, [(parts, send, keep, jnp.bfloat16)])
         own, panels, _ = lax.optimization_barrier((remote[step, shift], panels, send))
         if piece == 0:
+            panels, order = panels + [swap_tensor(panels[1], bits[1])], order + [bits[0] ^ bits[1]]
             panels, order = spread_panels(panels, order, bits[2:])
         sib = swap_cores(own)
-        held = [sends, siblings] if piece == 0 else [sends]
-        own, sib, held = lax.optimization_barrier((own, sib, held))
+        own, sib, siblings, _ = lax.optimization_barrier((own, sib, siblings, sends))
         last, chunks, parts = step == step_count - 1, [(own, sib, 0, 1)], [((step, shift), 1)]
-        if piece == 0:
-            chunks.insert(0, (source, held[1], lead, 1))
-            parts.insert(0, ((lead, 0), 1))
+        if next_local < step_count:
+            chunks.insert(0, (source, siblings, next_local, 1))
+            parts.insert(0, ((next_local, 0), 1))
+            next_local += 1
         send, keep, *ranks = partial_products(pos, chunks, weight, factors, last)
         if last:
             last_ranks[shift] = ranks
@@ -400,7 +397,7 @@
     finished = jnp.stack([rank_sum(step) for step in range(step_count - 1)] + [rank_sum(RANK_NAME)])
     finished = finished.astype(jnp.bfloat16).reshape(step_count, rows_mine, owned_slots, rank_size)
     finished = lax.optimization_barrier((finished, rounded))[0]
-    ended.update((name, (kept, *received)) for name, kept, received, _ in second_leg)
+    ended.update((name, (kept, *received)) for name, kept, received in second_leg)
     masked = jnp.sum(
         jnp.where(owned_hot[None, :, :, None], finished, 0), axis=2, dtype=jnp.float32
     ).astype(jnp.bfloat16)

time: 145 us -> 143 us (0.986)
  waiting for transfers between devices: 36.9 us -> 28.5 us
  starting transfers between devices: 25.2 us -> 29.2 us
  other arithmetic: 2.39 us -> 4.92 us
  Pallas kernels: 73.6 us -> 71.3 us
  local copies, waits for them, and re-layouts: 6.38 us -> 8.39 us
    ppermute x4, waiting for transfers between devices: 14.1 us -> 1.36 us  [from_rep(): lax.ppermute(value, 'rep', [((i + shift) % n_rep, i) for i in range(n_rep)])]
    ppermute x9, starting transfers between devices: 8.89 us -> 13.3 us  [swap_tensor(): return lax.ppermute(value, 'tp', [(i, i ^ bit) for i in range(n_tensor)])]
    ppermute x9, waiting for transfers between devices: 2.77 us -> 7.12 us  [swap_tensor(): return lax.ppermute(value, 'tp', [(i, i ^ bit) for i in range(n_tensor)])]
    ppermute x5, starting transfers between devices: 10.5 us -> 6.9 us  [to_group(): lax.ppermute(value, 'tp', [(i, (i + moved) % n_tensor) for i in range(n_t...]
    pallas_call x5, Pallas kernels: 70.3 us -> 67.8 us  [partial_products(): pl.pallas_call(functools.partial(matmul_body, spans, staged, apart), in_s...]
    convert_element_type x4, other arithmetic: 0.29 us -> 1.94 us  [gap(): pick(values, (group_index + hop - rep_index) % n_rep).astype(jnp.bfloat16)]
    ppermute x4, starting transfers between devices: 4.41 us -> 6.03 us  [from_rep(): lax.ppermute(value, 'rep', [((i + shift) % n_rep, i) for i in range(n_rep)])]
    ppermute x3, starting transfers between devices: 0.88 us -> 2.41 us  [per_device(): lax.ppermute(masked, ('rep', 'sub'), [(i, (i + turn) % n_owners) for i in...]
  transfers between devices with their start and end apart: 26 -> 26, of which waited for: 10 -> 9; matrix products, arithmetic and copies ran while one was open for 4% -> 6% of each run, Pallas kernels for 50% -> 49%
where the time goes in v14:
time: 143 us
  Pallas kernels  71.3 us (50%)
  starting transfers between devices  29.2 us (20%)
  waiting for transfers between devices  28.5 us (20%)
  local copies, waits for them, and re-layouts  8.39 us (6%)
  other arithmetic  4.92 us (3%)
    pallas_call x5, Pallas kernels, partial_products(): pl.pallas_call(functools.partial(matmul_body, spans, staged, apart), in_s...  67.8 us
    ppermute x5, waiting for transfers between devices, to_group(): lax.ppermute(value, 'tp', [(i, (i + moved) % n_tensor) for i in range(n_t...  16.8 us
    ppermute x9, starting transfers between devices, swap_tensor(): return lax.ppermute(value, 'tp', [(i, i ^ bit) for i in range(n_tensor)])  13.3 us
    ppermute x9, waiting for transfers between devices, swap_tensor(): return lax.ppermute(value, 'tp', [(i, i ^ bit) for i in range(n_tensor)])  7.12 us
    ppermute x5, starting transfers between devices, to_group(): lax.ppermute(value, 'tp', [(i, (i + moved) % n_tensor) for i in range(n_t...  6.9 us
    ppermute x4, starting transfers between devices, from_rep(): lax.ppermute(value, 'rep', [((i + shift) % n_rep, i) for i in range(n_rep)])  6.03 us
    unnamed x36, local copies, waits for them, and re-layouts  4.59 us
    ppermute x3, waiting for transfers between devices, per_device(): lax.ppermute(masked, ('rep', 'sub'), [(i, (i + turn) % n_owners) for i in...  3.26 us
  transfers between devices with their start and end apart: 26, of which 9 were waited for; matrix products, arithmetic and copies ran while one was open for 6% of the time, Pallas kernels for 49%

profile of v14, /device:TPU:0, one launch (start us, length us, event | category | flops | bytes accessed | tf_op | source)
XLA Modules:
  0.0 142.7 jit_solution(2681362702157305490)
XLA Ops:
  0.5 2.2 %slice.68 = bf16[1,64,7168]{2,1,0:T(8,128)(2,1)} slice(bf16[4,64,7168]{2,1,0:T(8,128)(2,1)} %refs_0_.5), slice={[0:1], [0:64], [0:7168]} | slice | bytes 1835008 | tf_op jit(solution)/shard_map/slice | solution.py:285
  2.7 2.6 %collective-permute-start.3 = (bf16[1,64,7168]{2,1,0:T(8,128)(2,1)}, bf16[1,64,7168]{2,1,0:T(8,128)(2,1)S(1)}, u32[]{:S(2)}, u32[]{:S(2)}) collective-permute-start(bf16[1,64,7168]{2,1,0:T(8,128)(2,1)} %slice.68), channel_id=1, source_target_pairs={{2,0},{0,2},{3,1},{1,3},{6,4},{4,6},{7,5},{5,7},{10,8},{8,10},{11,... | collective-permute-start | bytes 2752520 | tf_op jit(solution)/shard_map/ppermute | solution.py:263
  5.3 2.6 %collective-permute-start.4 = (bf16[1,64,2048]{2,1,0:T(8,128)(2,1)S(1)}, bf16[1,64,2048]{2,1,0:T(8,128)(2,1)S(1)}, u32[]{:S(2)}, u32[]{:S(2)}) collective-permute-start(bf16[1,64,2048]{2,1,0:T(8,128)(2,1)S(1)} %copy-done.8), channel_id=1, source_target_pairs={{0,8},{4,12},{8,0},{12,4},{1,9},{5,13},{9,1},{13,5},{2,10},{6,14},... | collective-permute-start | bytes 786440 | tf_op jit(solution)/shard_map/ppermute | solution.py:266
  7.9 1.6 %collective-permute-start.5 = (bf16[1,64,2048]{2,1,0:T(8,128)(2,1)S(1)}, bf16[1,64,2048]{2,1,0:T(8,128)(2,1)}, u32[]{:S(2)}, u32[]{:S(2)}) collective-permute-start(bf16[1,64,2048]{2,1,0:T(8,128)(2,1)S(1)} %copy-done.8), channel_id=1, source_target_pairs={{0,4},{4,0},{8,12},{12,8},{1,5},{5,1},{9,13},{13,9},{2,6},{6,2},{1... | collective-permute-start | bytes 786440 | tf_op jit(solution)/shard_map/ppermute | solution.py:266
  9.5 17.2 %partial_products.5 = (bf16[128,2176]{1,0:T(8,128)(2,1)}, f32[128,2176]{1,0:T(8,128)S(1)}, bf16[1,64,7168]{2,1,0:T(8,128)(2,1)}, bf16[1,64,7168]{2,1,0:T(8,128)(2,1)}, bf16[1,64,7168]{2,1,0:T(8,128)(2,1)}) custom-call(s32[1]{0:T(128)} %bitcast.1.pos_ref, bf16[4,64,7168]{2,1,0:T(8,128)(2,1)} %refs_0_.5, bf16[4,64,7168]{2,1,0:T(8,128)(2,1)} %collective-permute-done.refs_1_, ...), custom_call_target="tpu_custom_call" | custom-call | tf_op jit(solution)/shard_map/partial_products/pallas_call | solution.py:137
  27.7 1.4 collective-permute-start.2
  29.2 1.6 %collective-permute-start.11 = (bf16[128,2176]{1,0:T(8,128)(2,1)}, bf16[128,2176]{1,0:T(8,128)(2,1)}, u32[]{:S(2)}, u32[]{:S(2)}) collective-permute-start(bf16[128,2176]{1,0:T(8,128)(2,1)} %get-tuple-element.74), channel_id=1, source_target_pairs={{0,4},{4,0},{8,12},{12,8},{1,5},{5,1},{9,13},{13,9},{2,6},{6,2},{1... | collective-permute-start | bytes 1671176 | tf_op jit(solution)/shard_map/ppermute | solution.py:266
  32.5 1.2 copy-done.4
  33.7 13.4 %partial_products.6 = (bf16[128,2176]{1,0:T(8,128)(2,1)S(1)}, f32[128,2176]{1,0:T(8,128)S(1)}) custom-call(s32[1]{0:T(128)} %bitcast.1.pos_ref, bf16[4,64,7168]{2,1,0:T(8,128)(2,1)} %refs_0_.5, bf16[4,64,7168]{2,1,0:T(8,128)(2,1)} %collective-permute-done.refs_1_, bf16[1,64,7168]{2,1,0:T(8,128)(2,1)S(1)} %copy-done.4, ...), custom_call_target="tpu_custom_call" | custom-call | tf_op jit(solution)/shard_map/partial_products/pallas_call | solution.py:137
  47.9 1.9 %collective-permute-done.6 = bf16[1,64,2048]{2,1,0:T(8,128)(2,1)} collective-permute-done((bf16[1,64,2048]{2,1,0:T(8,128)(2,1)S(1)}, bf16[1,64,2048]{2,1,0:T(8,128)(2,1)}, u32[]{:S(2)}, u32[]{:S(2)}) %collective-permute-start.6) | collective-permute-done | bytes 262176 | tf_op jit(solution)/shard_map/ppermute | solution.py:266
  49.8 1.4 collective-permute-done.2.refs_2_
  51.4 1.4 collective-permute-start.13
  52.8 1.6 %collective-permute-start.10 = (bf16[128,2176]{1,0:T(8,128)(2,1)}, bf16[128,2176]{1,0:T(8,128)(2,1)S(1)}, u32[]{:S(2)}, u32[]{:S(2)}) collective-permute-start(bf16[128,2176]{1,0:T(8,128)(2,1)} %copy-done.12), channel_id=1, source_target_pairs={{0,4},{4,0},{8,12},{12,8},{1,5},{5,1},{9,13},{13,9},{2,6},{6,2},{1... | collective-permute-start | bytes 1671176 | tf_op jit(solution)/shard_map/ppermute | solution.py:266
  54.4 1.2 convert_add_fusion.1
  55.6 15.5 %partial_products.7 = (bf16[128,2176]{1,0:T(8,128)(2,1)S(1)}, f32[128,2176]{1,0:T(8,128)S(1)}) custom-call(s32[1]{0:T(128)} %bitcast.1.pos_ref, bf16[4,64,7168]{2,1,0:T(8,128)(2,1)} %refs_0_.5, bf16[4,64,7168]{2,1,0:T(8,128)(2,1)} %collective-permute-done.refs_1_, bf16[1,64,7168]{2,1,0:T(8,128)(2,1)} %collective-permute-done.2.refs_2_, ...), custom_call_target="tpu_custom_call" | custom-call | tf_op jit(solution)/shard_map/partial_products/pallas_call | solution.py:137
  71.0 1.3 collective-permute-start.15
  72.5 2.7 %collective-permute-start.12 = (bf16[64,2176]{1,0:T(8,128)(2,1)S(1)}, bf16[64,2176]{1,0:T(8,128)(2,1)S(1)}, u32[]{:S(2)}, u32[]{:S(2)}) collective-permute-start(bf16[64,2176]{1,0:T(8,128)(2,1)S(1)} %select_convert_fusion.2), channel_id=1, source_target_pairs={{0,8},{4,12},{8,0},{12,4},{1,9},{5,13},{9,1},{13,5},{2,10},{6,14},... | collective-permute-start | bytes 835592 | tf_op jit(solution)/shard_map/ppermute | solution.py:270
  75.2 11.2 %partial_products.8 = (bf16[64,2176]{1,0:T(8,128)(2,1)}, f32[64,2176]{1,0:T(8,128)S(1)}) custom-call(s32[1]{0:T(128)} %bitcast.1.pos_ref, bf16[1,64,7168]{2,1,0:T(8,128)(2,1)} %collective-permute-done.1.refs_0_, bf16[1,64,7168]{2,1,0:T(8,128)(2,1)S(1)} %collective-permute-done.9.refs_1_, bf16[7168,2048]{1,0:T(8,128)(2,1)} %refs_2_.5, ...), custom_call_target="tpu_custom_call" | custom-call | tf_op jit(solution)/shard_map/partial_products/pallas_call | solution.py:137
  86.4 5.2 %collective-permute-done.15 = bf16[128,2176]{1,0:T(8,128)(2,1)S(1)} collective-permute-done((bf16[128,2176]{1,0:T(8,128)(2,1)S(1)}, bf16[128,2176]{1,0:T(8,128)(2,1)S(1)}, u32[]{:S(2)}, u32[]{:S(2)}) %collective-permute-start.15) | collective-permute-done | bytes 557088 | tf_op jit(solution)/shard_map/ppermute | solution.py:266
  93.5 1.1 collective-permute-start.16
  94.6 2.1 %collective-permute-start.17 = (bf16[64,2176]{1,0:T(8,128)(2,1)}, bf16[64,2176]{1,0:T(8,128)(2,1)}, u32[]{:S(2)}, u32[]{:S(2)}) collective-permute-start(bf16[64,2176]{1,0:T(8,128)(2,1)} %get-tuple-element.121), channel_id=1, source_target_pairs={{0,4},{4,0},{8,12},{12,8},{1,5},{5,1},{9,13},{13,9},{2,6},{6,2},{1... | collective-permute-start | bytes 835592 | tf_op jit(solution)/shard_map/ppermute | solution.py:266
  97.6 10.6 %partial_products.9 = (bf16[64,2048]{1,0:T(8,128)(2,1)S(1)}, f32[64,2048]{1,0:T(8,128)S(1)}, f32[64,128]{1,0:T(8,128)S(1)}, f32[64,128]{1,0:T(8,128)S(1)}) custom-call(s32[1]{0:T(128)} %bitcast.1.pos_ref, bf16[1,64,7168]{2,1,0:T(8,128)(2,1)} %collective-permute-done.13.refs_0_, bf16[1,64,7168]{2,1,0:T(8,128)(2,1)S(1)} %collective-permute-done.14.refs_1_, ...), custom_call_target="tpu_custom_call" | custom-call | tf_op jit(solution)/shard_map/partial_products/pallas_call | solution.py:137
  108.2 1.4 %collective-permute-done.16.refs_7_ = bf16[64,2176]{1,0:T(8,128)(2,1)} collective-permute-done((bf16[64,2176]{1,0:T(8,128)(2,1)}, bf16[64,2176]{1,0:T(8,128)(2,1)}, u32[]{:S(2)}, u32[]{:S(2)}) %collective-permute-start.16) | collective-permute-done | bytes 278560 | tf_op jit(solution)/shard_map/ppermute | solution.py:270
  109.7 2.0 %collective-permute-start.21 = (bf16[64,2048]{1,0:T(8,128)(2,1)S(1)}, bf16[64,2048]{1,0:T(8,128)(2,1)S(1)}, u32[]{:S(2)}, u32[]{:S(2)}) collective-permute-start(bf16[64,2048]{1,0:T(8,128)(2,1)S(1)} %get-tuple-element.130), channel_id=1, source_target_pairs={{0,4},{4,0},{8,12},{12,8},{1,5},{5,1},{9,13},{13,9},{2,6},{6,2},{1... | collective-permute-start | bytes 786440 | tf_op jit(solution)/shard_map/ppermute | solution.py:266
  111.7 1.0 select_convert_fusion
  113.6 1.0 slice_select_fusion.refs_8_
  115.4 2.2 %collective-permute-start.20 = (f32[64,128]{1,0:T(8,128)S(1)}, f32[64,128]{1,0:T(8,128)S(1)}, u32[]{:S(2)}, u32[]{:S(2)}) collective-permute-start(f32[64,128]{1,0:T(8,128)S(1)} %get-tuple-element.139), channel_id=1, source_target_pairs={{0,8},{4,12},{8,0},{12,4},{1,9},{5,13},{9,1},{13,5},{2,10},{6,14},... | collective-permute-start | bytes 98312 | tf_op jit(solution)/shard_map/ppermute | solution.py:270
  117.6 11.2 %collective-permute-done.20 = f32[64,128]{1,0:T(8,128)S(1)} collective-permute-done((f32[64,128]{1,0:T(8,128)S(1)}, f32[64,128]{1,0:T(8,128)S(1)}, u32[]{:S(2)}, u32[]{:S(2)}) %collective-permute-start.20) | collective-permute-done | bytes 32800 | tf_op jit(solution)/shard_map/ppermute | solution.py:270
  129.2 1.9 %collective-permute-start.23 = (bf16[4,64,64]{2,1,0:T(8,128)(2,1)S(1)}, bf16[4,64,64]{2,1,0:T(8,128)(2,1)S(1)}, u32[]{:S(2)}, u32[]{:S(2)}) collective-permute-start(bf16[4,64,64]{2,1,0:T(8,128)(2,1)S(1)} %select_bitcast_fusion), channel_id=1, source_target_pairs={{0,2},{1,3},{2,0},{3,1},{4,6},{5,7},{6,4},{7,5},{8,10},{9,11},{10,... | collective-permute-start | bytes 98312 | tf_op jit(solution)/shard_map/ppermute | solution.py:406
  131.7 1.9 %collective-permute-done.23 = bf16[4,64,64]{2,1,0:T(8,128)(2,1)S(1)} collective-permute-done((bf16[4,64,64]{2,1,0:T(8,128)(2,1)S(1)}, bf16[4,64,64]{2,1,0:T(8,128)(2,1)S(1)}, u32[]{:S(2)}, u32[]{:S(2)}) %collective-permute-start.23) | collective-permute-done | bytes 32800 | tf_op jit(solution)/shard_map/ppermute | solution.py:406
  135.0 2.7 %finish_steps.1 = (bf16[4,64,2048]{2,1,0:T(8,128)(2,1)}, bf16[64,2048]{1,0:T(8,128)(2,1)S(1)}) custom-call(bf16[256,64]{1,0:T(8,128)(2,1)S(1)} %bitcast.30, s32[256,1]{1,0:T(8,128)S(1)} %copy-done.5, s32[4]{0:T(128)S(1)} %pad_add_fusion.order_ref, bf16[64,2048]{1,0:T(8,128)(2,1)S(1)} %bitcast.31, bf16[64,2048]{1,0:T(8,128)(2,1)S(1)} %bitcast.32, ...), custom_call_target="tpu_custom_call" | custom-call | tf_op jit(solution)/shard_map/finish_steps/pallas_call | solution.py:195
  137.7 4.2 %collective-permute-done.25.refs_1_ = bf16[64,2048]{1,0:T(8,128)(2,1)S(1)} collective-permute-done((bf16[64,2048]{1,0:T(8,128)(2,1)S(1)}, bf16[64,2048]{1,0:T(8,128)(2,1)S(1)}, u32[]{:S(2)}, u32[]{:S(2)}) %collective-permute-start.25) | collective-permute-done | bytes 262176 | tf_op jit(solution)/shard_map/ppermute | solution.py:270
  (94 shorter events, 12.0 us)
Async XLA Ops:
  0.0 51.2 %copy-start = (s32[256,1]{0,1:T(1,128)S(1)}, s32[256,1]{0,1:T(1,128)}, u32[]{:S(2)}) copy-start(s32[256,1]{0,1:T(1,128)} %param.10) | copy-start | bytes 3076
  0.0 9.5 %copy-start.2 = (bf16[1,7168,64]{1,2,0:T(8,128)(2,1)S(1)}, bf16[1,7168,64]{1,2,0:T(8,128)(2,1)}, u32[]{:S(2)}) copy-start(bf16[1,7168,64]{1,2,0:T(8,128)(2,1)} %param.8) | copy-start | bytes 2752516
  0.0 9.5 %collective-permute-start = (bf16[4,64,7168]{2,1,0:T(8,128)(2,1)}, bf16[4,64,7168]{2,1,0:T(8,128)(2,1)}, u32[]{:S(2)}, u32[]{:S(2)}) collective-permute-start(bf16[4,64,7168]{2,1,0:T(8,128)(2,1)} %refs_0_.5), channel_id=1, source_target_pairs={{0,1},{1,0},{2,3},{3,2},{4,5},{5,4},{6,7},{7,6},{8,9},{9,8},{10,11... | collective-permute-start | bytes 11010056 | tf_op jit(solution)/shard_map/ppermute | solution.py:260
  2.7 24.0 %collective-permute-start.3 = (bf16[1,64,7168]{2,1,0:T(8,128)(2,1)}, bf16[1,64,7168]{2,1,0:T(8,128)(2,1)S(1)}, u32[]{:S(2)}, u32[]{:S(2)}) collective-permute-start(bf16[1,64,7168]{2,1,0:T(8,128)(2,1)} %slice.68), channel_id=1, source_target_pairs={{2,0},{0,2},{3,1},{1,3},{6,4},{4,6},{7,5},{5,7},{10,8},{8,10},{11,... | collective-permute-start | bytes 2752520 | tf_op jit(solution)/shard_map/ppermute | solution.py:263
  5.3 21.4 %collective-permute-start.4 = (bf16[1,64,2048]{2,1,0:T(8,128)(2,1)S(1)}, bf16[1,64,2048]{2,1,0:T(8,128)(2,1)S(1)}, u32[]{:S(2)}, u32[]{:S(2)}) collective-permute-start(bf16[1,64,2048]{2,1,0:T(8,128)(2,1)S(1)} %copy-done.8), channel_id=1, source_target_pairs={{0,8},{4,12},{8,0},{12,4},{1,9},{5,13},{9,1},{13,5},{2,10},{6,14},... | collective-permute-start | bytes 786440 | tf_op jit(solution)/shard_map/ppermute | solution.py:266
  7.9 18.8 %collective-permute-start.5 = (bf16[1,64,2048]{2,1,0:T(8,128)(2,1)S(1)}, bf16[1,64,2048]{2,1,0:T(8,128)(2,1)}, u32[]{:S(2)}, u32[]{:S(2)}) collective-permute-start(bf16[1,64,2048]{2,1,0:T(8,128)(2,1)S(1)} %copy-done.8), channel_id=1, source_target_pairs={{0,4},{4,0},{8,12},{12,8},{1,5},{5,1},{9,13},{13,9},{2,6},{6,2},{1... | collective-permute-start | bytes 786440 | tf_op jit(solution)/shard_map/ppermute | solution.py:266
  26.7 5.8 %collective-permute-start.7 = (bf16[1,64,7168]{2,1,0:T(8,128)(2,1)S(1)}, bf16[1,64,7168]{2,1,0:T(8,128)(2,1)}, u32[]{:S(2)}, u32[]{:S(2)}) collective-permute-start(bf16[1,64,7168]{2,1,0:T(8,128)(2,1)S(1)} %collective-permute-done.3.refs_2_), channel_id=1, source_target_pairs={{0,1},{1,0},{2,3},{3,2},{4,5},{5,4},{6,7},{7,6},{8,9},{9,8},{10,11... | collective-permute-start | bytes 2752520 | tf_op jit(solution)/shard_map/ppermute | solution.py:260
  27.7 23.5 %collective-permute-start.2 = (bf16[1,64,7168]{2,1,0:T(8,128)(2,1)}, bf16[1,64,7168]{2,1,0:T(8,128)(2,1)}, u32[]{:S(2)}, u32[]{:S(2)}) collective-permute-start(bf16[1,64,7168]{2,1,0:T(8,128)(2,1)} %get-tuple-element.73), channel_id=1, source_target_pairs={{2,0},{0,2},{3,1},{1,3},{6,4},{4,6},{7,5},{5,7},{10,8},{8,10},{11,... | collective-permute-start | bytes 2752520 | tf_op jit(solution)/shard_map/ppermute | solution.py:263
  29.2 25.2 %collective-permute-start.11 = (bf16[128,2176]{1,0:T(8,128)(2,1)}, bf16[128,2176]{1,0:T(8,128)(2,1)}, u32[]{:S(2)}, u32[]{:S(2)}) collective-permute-start(bf16[128,2176]{1,0:T(8,128)(2,1)} %get-tuple-element.74), channel_id=1, source_target_pairs={{0,4},{4,0},{8,12},{12,8},{1,5},{5,1},{9,13},{13,9},{2,6},{6,2},{1... | collective-permute-start | bytes 1671176 | tf_op jit(solution)/shard_map/ppermute | solution.py:266
  30.7 19.1 %collective-permute-start.6 = (bf16[1,64,2048]{2,1,0:T(8,128)(2,1)S(1)}, bf16[1,64,2048]{2,1,0:T(8,128)(2,1)}, u32[]{:S(2)}, u32[]{:S(2)}) collective-permute-start(bf16[1,64,2048]{2,1,0:T(8,128)(2,1)S(1)} %collective-permute-done.4), channel_id=1, source_target_pairs={{0,4},{4,0},{8,12},{12,8},{1,5},{5,1},{9,13},{13,9},{2,6},{6,2},{1... | collective-permute-start | bytes 786440 | tf_op jit(solution)/shard_map/ppermute | solution.py:266
  31.9 19.4 %copy-start.17 = (s32[4]{0:T(128)S(1)}, s32[4]{0:T(128)}, u32[]{:S(2)}) copy-start(s32[4]{0:T(128)} %param.11) | copy-start | bytes 52
  31.9 39.1 %collective-permute-start.1 = (bf16[1,64,7168]{2,1,0:T(8,128)(2,1)}, bf16[1,64,7168]{2,1,0:T(8,128)(2,1)}, u32[]{:S(2)}, u32[]{:S(2)}) collective-permute-start(bf16[1,64,7168]{2,1,0:T(8,128)(2,1)} %get-tuple-element.72), channel_id=1, source_target_pairs={{2,0},{0,2},{3,1},{1,3},{6,4},{4,6},{7,5},{5,7},{10,8},{8,10},{11,... | collective-permute-start | bytes 2752520 | tf_op jit(solution)/shard_map/ppermute | solution.py:263
  51.2 4.3 %collective-permute-start.8 = (bf16[1,64,7168]{2,1,0:T(8,128)(2,1)}, bf16[1,64,7168]{2,1,0:T(8,128)(2,1)}, u32[]{:S(2)}, u32[]{:S(2)}) collective-permute-start(bf16[1,64,7168]{2,1,0:T(8,128)(2,1)} %collective-permute-done.2.refs_2_), channel_id=1, source_target_pairs={{0,1},{1,0},{2,3},{3,2},{4,5},{5,4},{6,7},{7,6},{8,9},{9,8},{10,11... | collective-permute-start | bytes 2752520 | tf_op jit(solution)/shard_map/ppermute | solution.py:260
  51.4 41.3 %collective-permute-start.13 = (bf16[1,64,7168]{2,1,0:T(8,128)(2,1)}, bf16[1,64,7168]{2,1,0:T(8,128)(2,1)}, u32[]{:S(2)}, u32[]{:S(2)}) collective-permute-start(bf16[1,64,7168]{2,1,0:T(8,128)(2,1)} %get-tuple-element.104), channel_id=1, source_target_pairs={{2,0},{0,2},{3,1},{1,3},{6,4},{4,6},{7,5},{5,7},{10,8},{8,10},{11,... | collective-permute-start | bytes 2752520 | tf_op jit(solution)/shard_map/ppermute | solution.py:263
  52.8 19.6 %collective-permute-start.10 = (bf16[128,2176]{1,0:T(8,128)(2,1)}, bf16[128,2176]{1,0:T(8,128)(2,1)S(1)}, u32[]{:S(2)}, u32[]{:S(2)}) collective-permute-start(bf16[128,2176]{1,0:T(8,128)(2,1)} %copy-done.12), channel_id=1, source_target_pairs={{0,4},{4,0},{8,12},{12,8},{1,5},{5,1},{9,13},{13,9},{2,6},{6,2},{1... | collective-permute-start | bytes 1671176 | tf_op jit(solution)/shard_map/ppermute | solution.py:266
  71.0 20.5 %collective-permute-start.15 = (bf16[128,2176]{1,0:T(8,128)(2,1)S(1)}, bf16[128,2176]{1,0:T(8,128)(2,1)S(1)}, u32[]{:S(2)}, u32[]{:S(2)}) collective-permute-start(bf16[128,2176]{1,0:T(8,128)(2,1)S(1)} %get-tuple-element.91), channel_id=1, source_target_pairs={{0,4},{4,0},{8,12},{12,8},{1,5},{5,1},{9,13},{13,9},{2,6},{6,2},{1... | collective-permute-start | bytes 1671176 | tf_op jit(solution)/shard_map/ppermute | solution.py:266
  72.4 2.8 %collective-permute-start.9 = (bf16[1,64,7168]{2,1,0:T(8,128)(2,1)}, bf16[1,64,7168]{2,1,0:T(8,128)(2,1)S(1)}, u32[]{:S(2)}, u32[]{:S(2)}) collective-permute-start(bf16[1,64,7168]{2,1,0:T(8,128)(2,1)} %collective-permute-done.1.refs_0_), channel_id=1, source_target_pairs={{0,1},{1,0},{2,3},{3,2},{4,5},{5,4},{6,7},{7,6},{8,9},{9,8},{10,11... | collective-permute-start | bytes 2752520 | tf_op jit(solution)/shard_map/ppermute | solution.py:260
  72.5 19.2 %copy-start.13 = (f32[128,2176]{1,0:T(8,128)}, f32[128,2176]{1,0:T(8,128)S(1)}, u32[]{:S(2)}) copy-start(f32[128,2176]{1,0:T(8,128)S(1)} %convert_add_fusion.2) | copy-start | bytes 3342340
  72.5 19.2 %collective-permute-start.12 = (bf16[64,2176]{1,0:T(8,128)(2,1)S(1)}, bf16[64,2176]{1,0:T(8,128)(2,1)S(1)}, u32[]{:S(2)}, u32[]{:S(2)}) collective-permute-start(bf16[64,2176]{1,0:T(8,128)(2,1)S(1)} %select_convert_fusion.2), channel_id=1, source_target_pairs={{0,8},{4,12},{8,0},{12,4},{1,9},{5,13},{9,1},{13,5},{2,10},{6,14},... | collective-permute-start | bytes 835592 | tf_op jit(solution)/shard_map/ppermute | solution.py:270
  92.6 5.0 %collective-permute-start.14 = (bf16[1,64,7168]{2,1,0:T(8,128)(2,1)}, bf16[1,64,7168]{2,1,0:T(8,128)(2,1)S(1)}, u32[]{:S(2)}, u32[]{:S(2)}) collective-permute-start(bf16[1,64,7168]{2,1,0:T(8,128)(2,1)} %collective-permute-done.13.refs_0_), channel_id=1, source_target_pairs={{0,1},{1,0},{2,3},{3,2},{4,5},{5,4},{6,7},{7,6},{8,9},{9,8},{10,11... | collective-permute-start | bytes 2752520 | tf_op jit(solution)/shard_map/ppermute | solution.py:260
  93.5 16.2 %collective-permute-start.16 = (bf16[64,2176]{1,0:T(8,128)(2,1)}, bf16[64,2176]{1,0:T(8,128)(2,1)}, u32[]{:S(2)}, u32[]{:S(2)}) collective-permute-start(bf16[64,2176]{1,0:T(8,128)(2,1)} %select_convert_fusion.1), channel_id=1, source_target_pairs={{0,8},{4,12},{8,0},{12,4},{1,9},{5,13},{9,1},{13,5},{2,10},{6,14},... | collective-permute-start | bytes 835592 | tf_op jit(solution)/shard_map/ppermute | solution.py:270
  94.6 17.1 %collective-permute-start.17 = (bf16[64,2176]{1,0:T(8,128)(2,1)}, bf16[64,2176]{1,0:T(8,128)(2,1)}, u32[]{:S(2)}, u32[]{:S(2)}) collective-permute-start(bf16[64,2176]{1,0:T(8,128)(2,1)} %get-tuple-element.121), channel_id=1, source_target_pairs={{0,4},{4,0},{8,12},{12,8},{1,5},{5,1},{9,13},{13,9},{2,6},{6,2},{1... | collective-permute-start | bytes 835592 | tf_op jit(solution)/shard_map/ppermute | solution.py:266
  97.6 14.1 %copy-start.14 = (f32[128,2176]{1,0:T(8,128)S(1)}, f32[128,2176]{1,0:T(8,128)}, u32[]{:S(2)}) copy-start(f32[128,2176]{1,0:T(8,128)} %copy-done.13) | copy-start | bytes 3342340
  109.7 5.7 %collective-permute-start.19 = (f32[64,128]{1,0:T(8,128)S(1)}, f32[64,128]{1,0:T(8,128)S(1)}, u32[]{:S(2)}, u32[]{:S(2)}) collective-permute-start(f32[64,128]{1,0:T(8,128)S(1)} %get-tuple-element.127), channel_id=1, source_target_pairs={{0,4},{4,0},{8,12},{12,8},{1,5},{5,1},{9,13},{13,9},{2,6},{6,2},{1... | collective-permute-start | bytes 98312 | tf_op jit(solution)/shard_map/ppermute | solution.py:266
  109.7 19.1 %collective-permute-start.21 = (bf16[64,2048]{1,0:T(8,128)(2,1)S(1)}, bf16[64,2048]{1,0:T(8,128)(2,1)S(1)}, u32[]{:S(2)}, u32[]{:S(2)}) collective-permute-start(bf16[64,2048]{1,0:T(8,128)(2,1)S(1)} %get-tuple-element.130), channel_id=1, source_target_pairs={{0,4},{4,0},{8,12},{12,8},{1,5},{5,1},{9,13},{13,9},{2,6},{6,2},{1... | collective-permute-start | bytes 786440 | tf_op jit(solution)/shard_map/ppermute | solution.py:266
  112.8 16.2 %collective-permute-start.18 = (bf16[64,2176]{1,0:T(8,128)(2,1)S(1)}, bf16[64,2176]{1,0:T(8,128)(2,1)S(1)}, u32[]{:S(2)}, u32[]{:S(2)}) collective-permute-start(bf16[64,2176]{1,0:T(8,128)(2,1)S(1)} %select_convert_fusion), channel_id=1, source_target_pairs={{0,8},{4,12},{8,0},{12,4},{1,9},{5,13},{9,1},{13,5},{2,10},{6,14},... | collective-permute-start | bytes 835592 | tf_op jit(solution)/shard_map/ppermute | solution.py:270
  115.4 13.4 %collective-permute-start.20 = (f32[64,128]{1,0:T(8,128)S(1)}, f32[64,128]{1,0:T(8,128)S(1)}, u32[]{:S(2)}, u32[]{:S(2)}) collective-permute-start(f32[64,128]{1,0:T(8,128)S(1)} %get-tuple-element.139), channel_id=1, source_target_pairs={{0,8},{4,12},{8,0},{12,4},{1,9},{5,13},{9,1},{13,5},{2,10},{6,14},... | collective-permute-start | bytes 98312 | tf_op jit(solution)/shard_map/ppermute | solution.py:270
  128.9 13.0 %collective-permute-start.25 = (bf16[64,2048]{1,0:T(8,128)(2,1)S(1)}, bf16[64,2048]{1,0:T(8,128)(2,1)S(1)}, u32[]{:S(2)}, u32[]{:S(2)}) collective-permute-start(bf16[64,2048]{1,0:T(8,128)(2,1)S(1)} %select_convert_fusion.3), channel_id=1, source_target_pairs={{0,8},{4,12},{8,0},{12,4},{1,9},{5,13},{9,1},{13,5},{2,10},{6,14},... | collective-permute-start | bytes 786440 | tf_op jit(solution)/shard_map/ppermute | solution.py:270
  129.1 5.9 %copy-start.7 = (bf16[64,2176]{1,0:T(8,128)(2,1)S(1)}, bf16[64,2176]{1,0:T(8,128)(2,1)}, u32[]{:S(2)}) copy-start(bf16[64,2176]{1,0:T(8,128)(2,1)} %copy-done.6) | copy-start | bytes 835588
  129.2 4.3 %collective-permute-start.23 = (bf16[4,64,64]{2,1,0:T(8,128)(2,1)S(1)}, bf16[4,64,64]{2,1,0:T(8,128)(2,1)S(1)}, u32[]{:S(2)}, u32[]{:S(2)}) collective-permute-start(bf16[4,64,64]{2,1,0:T(8,128)(2,1)S(1)} %select_bitcast_fusion), channel_id=1, source_target_pairs={{0,2},{1,3},{2,0},{3,1},{4,6},{5,7},{6,4},{7,5},{8,10},{9,11},{10,... | collective-permute-start | bytes 98312 | tf_op jit(solution)/shard_map/ppermute | solution.py:406
  131.1 3.0 %collective-permute-start.24 = (bf16[4,64,64]{2,1,0:T(8,128)(2,1)S(1)}, bf16[4,64,64]{2,1,0:T(8,128)(2,1)S(1)}, u32[]{:S(2)}, u32[]{:S(2)}) collective-permute-start(bf16[4,64,64]{2,1,0:T(8,128)(2,1)S(1)} %select_bitcast_fusion), channel_id=1, source_target_pairs={{0,3},{1,0},{2,1},{3,2},{4,7},{5,4},{6,5},{7,6},{8,11},{9,8},{10,9... | collective-permute-start | bytes 98312 | tf_op jit(solution)/shard_map/ppermute | solution.py:406
  131.1 3.8 %collective-permute-start.22 = (bf16[4,64,64]{2,1,0:T(8,128)(2,1)S(1)}, bf16[4,64,64]{2,1,0:T(8,128)(2,1)S(1)}, u32[]{:S(2)}, u32[]{:S(2)}) collective-permute-start(bf16[4,64,64]{2,1,0:T(8,128)(2,1)S(1)} %select_bitcast_fusion), channel_id=1, source_target_pairs={{0,1},{1,2},{2,3},{3,0},{4,5},{5,6},{6,7},{7,4},{8,9},{9,10},{10,1... | collective-permute-start | bytes 98312 | tf_op jit(solution)/shard_map/ppermute | solution.py:406
  (13 other events, 36.8 us)

commit v15 on v14

--- a/solution.py
+++ b/solution.py
@@ -30,11 +30,15 @@
 
 def matmul_body(spans, staged, apart, pos_ref, *refs):
     sources = refs[:2 * len(spans)]
-    w_ref, a_ref, send_ref, keep_ref = refs[2 * len(spans):2 * len(spans) + 4]
-    outs, refs = refs[2 * len(spans) + 4:], ()
+    w_ref, a_ref = refs[2 * len(spans):2 * len(spans) + 2]
+    outs = refs[2 * len(spans) + 2:]
+    send_refs, keep_refs, outs = outs[:len(spans)], outs[len(spans):2 * len(spans)], outs[2 * len(spans):]
     outs, refs = (outs[:-7], outs[-7:]) if staged else (outs[:-5], outs[-5:])
     x_ref, w_buf, total_ref, x_sems, w_sems = refs[:5]
-    rows = send_ref.shape[0]
+    rows = total_ref.shape[0]
+    edges = [0]
+    for ref in send_refs:
+        edges.append(edges[-1] + ref.shape[0])
     depth, width = w_ref.shape
     slots, rank, _ = a_ref.shape
     buffers, block_k, block_w = w_buf.shape
@@ -69,12 +73,13 @@
         ]
     for block in range(buffers):
         fetch(jnp.int32(block), block).start()
-    keep_ref[...] = jnp.zeros_like(keep_ref)
+    for ref in keep_refs:
+        ref[...] = jnp.zeros_like(ref)
     total_ref[...] = jnp.zeros_like(total_ref)
-    send_rank, keep_rank = outs[:2] if apart else (total_ref, keep_ref)
+    send_rank, keep_ranks = (outs[0], outs[1:2]) if apart else (total_ref, keep_refs)
     if apart:
-        send_rank[...] = jnp.zeros_like(send_rank)
-        keep_rank[...] = jnp.zeros_like(keep_rank)
+        for ref in outs[:2]:
+            ref[...] = jnp.zeros_like(ref)
     for copy in copies:
         copy.wait()
     if staged:
@@ -88,7 +93,8 @@
         )
         begin = slot * rank + (0 if apart else width)
         send_rank[:, begin:begin + rank] = part[:rows]
-        keep_rank[:, begin:begin + rank] = part[rows:]
+        for index, ref in enumerate(keep_ranks):
+            ref[:, begin:begin + rank] = part[rows + edges[index]:rows + edges[index + 1]]
 
     @pl.loop(0, count)
     def _(block):
@@ -103,13 +109,15 @@
                 x, w_buf[slot, :, place * block_n:(place + 1) * block_n], preferred_element_type=jnp.float32
             )
             total_ref[:, columns] += term[:rows]
-            keep_ref[:, columns] += term[rows:]
+            for index, ref in enumerate(keep_refs):
+                ref[:, columns] += term[rows + edges[index]:rows + edges[index + 1]]
 
         @pl.when(block + buffers < count)
         def _():
             fetch(block + buffers, slot).start()
 
-    send_ref[...] = total_ref[...].astype(send_ref.dtype)
+    for index, ref in enumerate(send_refs):
+        ref[...] = total_ref[edges[index]:edges[index + 1]].astype(ref.dtype)
     if staged:
         for copy in stage_out:
             copy.wait()
@@ -128,8 +136,8 @@
     extra = rank_columns(factors)
     columns = width + (0 if apart else extra)
     out_shape = [
-        jax.ShapeDtypeStruct((rows, columns), jnp.bfloat16),
-        jax.ShapeDtypeStruct((rows, columns), jnp.float32),
+        jax.ShapeDtypeStruct((length * per_block, columns), kind)
+        for kind in (jnp.bfloat16, jnp.float32) for _, length in spans
     ] + [jax.ShapeDtypeStruct((rows, extra), jnp.float32)] * (2 if apart else 0)
     out_specs = [vmem_spec] * len(out_shape)
     out_shape += [pltpu.HBM((1, per_block, depth), jnp.bfloat16)] * staged
@@ -357,29 +365,32 @@
     factors = jnp.swapaxes(down_a, 1, 2)
 
     lead = step_count // 2
-    parts, last_ranks, next_local = [((0, 0), lead)], {}, lead
+    last_ranks, next_local = {}, lead
     send, keep, *slices = partial_products(
         pos, [(source, siblings, 0, lead)], weight, factors, staged=step_count - 1
     )
     for step, rows in enumerate(slices, 1):
         remote.update({(step, shift): from_rep(rows, shift) for shift in range(1, n_rep)})
+    jobs = [([((0, 0), lead)], send, keep, jnp.bfloat16)]
     for piece, (step, shift) in enumerate(pieces):
-        sends = gap(send, [(parts, send, keep, jnp.bfloat16)])
+        sends = gap(send, jobs)
         own, panels, _ = lax.optimization_barrier((remote[step, shift], panels, send))
         if piece == 0:
             panels, order = panels + [swap_tensor(panels[1], bits[1])], order + [bits[0] ^ bits[1]]
             panels, order = spread_panels(panels, order, bits[2:])
         sib = swap_cores(own)
         own, sib, siblings, _ = lax.optimization_barrier((own, sib, siblings, sends))
-        last, chunks, parts = step == step_count - 1, [(own, sib, 0, 1)], [((step, shift), 1)]
+        last, chunks, keys = step == step_count - 1, [(own, sib, 0, 1)], [(step, shift)]
         if next_local < step_count:
-            chunks.insert(0, (source, siblings, next_local, 1))
-            parts.insert(0, ((next_local, 0), 1))
+            chunks.append((source, siblings, next_local, 1))
+            keys.append((next_local, 0))
             next_local += 1
-        send, keep, *ranks = partial_products(pos, chunks, weight, factors, last)
+        outs = partial_products(pos, chunks, weight, factors, last)
+        send, count = outs[0], len(chunks)
+        jobs = [([(key, 1)], outs[at], outs[count + at], jnp.bfloat16) for at, key in enumerate(keys)]
         if last:
-            last_ranks[shift] = ranks
-    gap(send, [(parts, send, keep, jnp.bfloat16)])
+            last_ranks[shift] = outs[2 * count:]
+    gap(send, jobs)
     for shift, ranks in last_ranks.items():
         halved[RANK_NAME, shift] = second_half(ranks[1], swap_tensor(ranks[0], group // 2), 1, jnp.float32)[0]
     values = [halved[RANK_NAME, at] for at in range(n_rep)]

time: 143 us -> 139 us (0.972)
  other arithmetic: 4.92 us -> 2.21 us
  Pallas kernels: 71.3 us -> 69.7 us
    ppermute x4, waiting for transfers between devices: 1.36 us -> 9.48 us  [from_rep(): lax.ppermute(value, 'rep', [((i + shift) % n_rep, i) for i in range(n_rep)])]
    ppermute x9 -> x11, waiting for transfers between devices: 7.12 us -> 1.01 us  [swap_tensor(): return lax.ppermute(value, 'tp', [(i, i ^ bit) for i in range(n_tensor)])]
    convert_element_type x4, other arithmetic: 1.94 us -> 0.37 us  [gap(): pick(values, (group_index + hop - rep_index) % n_rep).astype(jnp.bfloat16)]
    ppermute x9 -> x11, starting transfers between devices: 13.3 us -> 14.1 us  [swap_tensor(): return lax.ppermute(value, 'tp', [(i, i ^ bit) for i in range(n_tensor)])]
    unnamed x36 -> x34, local copies, waits for them, and re-layouts: 4.59 us -> 4.63 us
  transfers between devices with their start and end apart: 26 -> 28, of which waited for: 9 -> 10; matrix products, arithmetic and copies ran while one was open for 6% -> 4% of each run, Pallas kernels for 49% -> 50%
where the time goes in v15:
time: 139 us
  Pallas kernels  69.7 us (50%)
  waiting for transfers between devices  29.8 us (21%)
  starting transfers between devices  29.2 us (21%)
  local copies, waits for them, and re-layouts  7.73 us (6%)
  other arithmetic  2.21 us (2%)
    pallas_call x5, Pallas kernels, partial_products(): pl.pallas_call(functools.partial(matmul_body, spans, staged, apart), in_s...  66.4 us
    ppermute x5, waiting for transfers between devices, to_group(): lax.ppermute(value, 'tp', [(i, (i + moved) % n_tensor) for i in range(n_t...  15.6 us
    ppermute x11, starting transfers between devices, swap_tensor(): return lax.ppermute(value, 'tp', [(i, i ^ bit) for i in range(n_tensor)])  14.1 us
    ppermute x4, waiting for transfers between devices, from_rep(): lax.ppermute(value, 'rep', [((i + shift) % n_rep, i) for i in range(n_rep)])  9.48 us
    ppermute x5, starting transfers between devices, to_group(): lax.ppermute(value, 'tp', [(i, (i + moved) % n_tensor) for i in range(n_t...  7.87 us
    ppermute x4, starting transfers between devices, from_rep(): lax.ppermute(value, 'rep', [((i + shift) % n_rep, i) for i in range(n_rep)])  4.69 us
    unnamed x34, local copies, waits for them, and re-layouts  4.63 us
    ppermute x3, waiting for transfers between devices, per_device(): lax.ppermute(masked, ('rep', 'sub'), [(i, (i + turn) % n_owners) for i in...  3.59 us
  transfers between devices with their start and end apart: 28, of which 10 were waited for; matrix products, arithmetic and copies ran while one was open for 4% of the time, Pallas kernels for 50%

profile of v15, /device:TPU:0, one launch (start us, length us, event | category | flops | bytes accessed | tf_op | source)
XLA Modules:
  0.0 139.0 jit_solution(9102159737704224649)
XLA Ops:
  0.5 2.2 %slice.51 = bf16[1,64,7168]{2,1,0:T(8,128)(2,1)} slice(bf16[4,64,7168]{2,1,0:T(8,128)(2,1)} %refs_2_.7), slice={[0:1], [0:64], [0:7168]} | slice | bytes 1835008 | tf_op jit(solution)/shard_map/slice | solution.py:293
  2.7 2.6 %collective-permute-start.3 = (bf16[1,64,7168]{2,1,0:T(8,128)(2,1)}, bf16[1,64,7168]{2,1,0:T(8,128)(2,1)S(1)}, u32[]{:S(2)}, u32[]{:S(2)}) collective-permute-start(bf16[1,64,7168]{2,1,0:T(8,128)(2,1)} %slice.51), channel_id=1, source_target_pairs={{2,0},{0,2},{3,1},{1,3},{6,4},{4,6},{7,5},{5,7},{10,8},{8,10},{11,... | collective-permute-start | bytes 2752520 | tf_op jit(solution)/shard_map/ppermute | solution.py:271
  5.3 2.6 %collective-permute-start.4 = (bf16[1,64,2048]{2,1,0:T(8,128)(2,1)S(1)}, bf16[1,64,2048]{2,1,0:T(8,128)(2,1)}, u32[]{:S(2)}, u32[]{:S(2)}) collective-permute-start(bf16[1,64,2048]{2,1,0:T(8,128)(2,1)S(1)} %copy-done.7), channel_id=1, source_target_pairs={{0,8},{4,12},{8,0},{12,4},{1,9},{5,13},{9,1},{13,5},{2,10},{6,14},... | collective-permute-start | bytes 786440 | tf_op jit(solution)/shard_map/ppermute | solution.py:274
  7.9 1.6 %collective-permute-start.5 = (bf16[1,64,2048]{2,1,0:T(8,128)(2,1)S(1)}, bf16[1,64,2048]{2,1,0:T(8,128)(2,1)S(1)}, u32[]{:S(2)}, u32[]{:S(2)}) collective-permute-start(bf16[1,64,2048]{2,1,0:T(8,128)(2,1)S(1)} %copy-done.7), channel_id=1, source_target_pairs={{0,4},{4,0},{8,12},{12,8},{1,5},{5,1},{9,13},{13,9},{2,6},{6,2},{1... | collective-permute-start | bytes 786440 | tf_op jit(solution)/shard_map/ppermute | solution.py:274
  9.5 16.3 %partial_products.5 = (bf16[128,2176]{1,0:T(8,128)(2,1)S(1)}, f32[128,2176]{1,0:T(8,128)S(1)}, bf16[1,64,7168]{2,1,0:T(8,128)(2,1)}, bf16[1,64,7168]{2,1,0:T(8,128)(2,1)}, bf16[1,64,7168]{2,1,0:T(8,128)(2,1)}) custom-call(s32[1]{0:T(128)} %bitcast.1.pos_ref, bf16[4,64,7168]{2,1,0:T(8,128)(2,1)} %refs_2_.7, ...), custom_call_target="tpu_custom_call" | custom-call | tf_op jit(solution)/shard_map/partial_products/pallas_call | solution.py:145
  25.8 0.9 copy-done.13
  28.2 1.6 %collective-permute-start.6 = (bf16[1,64,2048]{2,1,0:T(8,128)(2,1)}, bf16[1,64,2048]{2,1,0:T(8,128)(2,1)S(1)}, u32[]{:S(2)}, u32[]{:S(2)}) collective-permute-start(bf16[1,64,2048]{2,1,0:T(8,128)(2,1)} %collective-permute-done.4), channel_id=1, source_target_pairs={{0,4},{4,0},{8,12},{12,8},{1,5},{5,1},{9,13},{13,9},{2,6},{6,2},{1... | collective-permute-start | bytes 786440 | tf_op jit(solution)/shard_map/ppermute | solution.py:274
  29.9 13.4 %partial_products.6 = (bf16[64,2176]{1,0:T(8,128)(2,1)S(1)}, bf16[64,2176]{1,0:T(8,128)(2,1)S(1)}, f32[64,2176]{1,0:T(8,128)S(1)}, f32[64,2176]{1,0:T(8,128)S(1)}) custom-call(s32[1]{0:T(128)} %bitcast.1.pos_ref, bf16[1,64,7168]{2,1,0:T(8,128)(2,1)S(1)} %collective-permute-done.3.refs_0_, bf16[1,64,7168]{2,1,0:T(8,128)(2,1)S(1)} %collective-permute-done.7.refs_1_, ...), custom_call_target="tpu_custom_call" | custom-call | tf_op jit(solution)/shard_map/partial_products/pallas_call | solution.py:145
  46.3 4.2 %collective-permute-done.2.refs_0_ = bf16[1,64,7168]{2,1,0:T(8,128)(2,1)} collective-permute-done((bf16[1,64,7168]{2,1,0:T(8,128)(2,1)}, bf16[1,64,7168]{2,1,0:T(8,128)(2,1)}, u32[]{:S(2)}, u32[]{:S(2)}) %collective-permute-start.2) | collective-permute-done | bytes 917536 | tf_op jit(solution)/shard_map/ppermute | solution.py:271
  51.3 1.6 %collective-permute-start.11 = (bf16[128,2176]{1,0:T(8,128)(2,1)}, bf16[128,2176]{1,0:T(8,128)(2,1)}, u32[]{:S(2)}, u32[]{:S(2)}) collective-permute-start(bf16[128,2176]{1,0:T(8,128)(2,1)} %copy-done.13), channel_id=1, source_target_pairs={{0,4},{4,0},{8,12},{12,8},{1,5},{5,1},{9,13},{13,9},{2,6},{6,2},{1... | collective-permute-start | bytes 1671176 | tf_op jit(solution)/shard_map/ppermute | solution.py:274
  54.5 1.2 collective-permute-start.10
  55.6 0.9 collective-permute-start.18
  56.5 15.3 %partial_products.7 = (bf16[64,2176]{1,0:T(8,128)(2,1)S(1)}, bf16[64,2176]{1,0:T(8,128)(2,1)S(1)}, f32[64,2176]{1,0:T(8,128)S(1)}, f32[64,2176]{1,0:T(8,128)S(1)}) custom-call(s32[1]{0:T(128)} %bitcast.1.pos_ref, bf16[1,64,7168]{2,1,0:T(8,128)(2,1)} %collective-permute-done.2.refs_0_, bf16[1,64,7168]{2,1,0:T(8,128)(2,1)} %collective-permute-done.8.refs_1_, ...), custom_call_target="tpu_custom_call" | custom-call | tf_op jit(solution)/shard_map/partial_products/pallas_call | solution.py:145
  71.8 2.0 %collective-permute-done.1.refs_0_ = bf16[1,64,7168]{2,1,0:T(8,128)(2,1)S(1)} collective-permute-done((bf16[1,64,7168]{2,1,0:T(8,128)(2,1)}, bf16[1,64,7168]{2,1,0:T(8,128)(2,1)S(1)}, u32[]{:S(2)}, u32[]{:S(2)}) %collective-permute-start.1) | collective-permute-done | bytes 917536 | tf_op jit(solution)/shard_map/ppermute | solution.py:271
  73.9 1.2 convert_add_fusion
  75.1 0.9 collective-permute-start.15
  76.1 2.7 %collective-permute-start.12 = (bf16[64,2176]{1,0:T(8,128)(2,1)S(1)}, bf16[64,2176]{1,0:T(8,128)(2,1)S(1)}, u32[]{:S(2)}, u32[]{:S(2)}) collective-permute-start(bf16[64,2176]{1,0:T(8,128)(2,1)S(1)} %select_convert_fusion.2), channel_id=1, source_target_pairs={{0,8},{4,12},{8,0},{12,4},{1,9},{5,13},{9,1},{13,5},{2,10},{6,14},... | collective-permute-start | bytes 835592 | tf_op jit(solution)/shard_map/ppermute | solution.py:278
  79.2 10.7 %partial_products.8 = (bf16[64,2176]{1,0:T(8,128)(2,1)S(1)}, f32[64,2176]{1,0:T(8,128)S(1)}) custom-call(s32[1]{0:T(128)} %bitcast.1.pos_ref, bf16[1,64,7168]{2,1,0:T(8,128)(2,1)S(1)} %collective-permute-done.1.refs_0_, bf16[1,64,7168]{2,1,0:T(8,128)(2,1)S(1)} %collective-permute-done.9.refs_1_, bf16[7168,2048]{1,0:T(8,128)(2,1)} %refs_2_.9, ...), custom_call_target="tpu_custom_call" | custom-call | tf_op jit(solution)/shard_map/partial_products/pallas_call | solution.py:145
  89.9 3.3 %collective-permute-done.13.refs_0_ = bf16[1,64,7168]{2,1,0:T(8,128)(2,1)S(1)} collective-permute-done((bf16[1,64,7168]{2,1,0:T(8,128)(2,1)}, bf16[1,64,7168]{2,1,0:T(8,128)(2,1)S(1)}, u32[]{:S(2)}, u32[]{:S(2)}) %collective-permute-start.13) | collective-permute-done | bytes 917536 | tf_op jit(solution)/shard_map/ppermute | solution.py:271
  93.4 1.9 %collective-permute-start.16 = (bf16[64,2176]{1,0:T(8,128)(2,1)S(1)}, bf16[64,2176]{1,0:T(8,128)(2,1)S(1)}, u32[]{:S(2)}, u32[]{:S(2)}) collective-permute-start(bf16[64,2176]{1,0:T(8,128)(2,1)S(1)} %select_convert_fusion.1), channel_id=1, source_target_pairs={{0,8},{4,12},{8,0},{12,4},{1,9},{5,13},{9,1},{13,5},{2,10},{6,14},... | collective-permute-start | bytes 835592 | tf_op jit(solution)/shard_map/ppermute | solution.py:278
  95.4 1.6 %collective-permute-start.17 = (bf16[64,2176]{1,0:T(8,128)(2,1)S(1)}, bf16[64,2176]{1,0:T(8,128)(2,1)S(1)}, u32[]{:S(2)}, u32[]{:S(2)}) collective-permute-start(bf16[64,2176]{1,0:T(8,128)(2,1)S(1)} %get-tuple-element.135), channel_id=1, source_target_pairs={{0,4},{4,0},{8,12},{12,8},{1,5},{5,1},{9,13},{13,9},{2,6},{6,2},{1... | collective-permute-start | bytes 835592 | tf_op jit(solution)/shard_map/ppermute | solution.py:274
  97.0 10.7 %partial_products.9 = (bf16[64,2048]{1,0:T(8,128)(2,1)S(1)}, f32[64,2048]{1,0:T(8,128)S(1)}, f32[64,128]{1,0:T(8,128)S(1)}, f32[64,128]{1,0:T(8,128)S(1)}) custom-call(s32[1]{0:T(128)} %bitcast.1.pos_ref, bf16[1,64,7168]{2,1,0:T(8,128)(2,1)S(1)} %collective-permute-done.13.refs_0_, bf16[1,64,7168]{2,1,0:T(8,128)(2,1)S(1)} %collective-permute-done.14.refs_1_, ...), custom_call_target="tpu_custom_call" | custom-call | tf_op jit(solution)/shard_map/partial_products/pallas_call | solution.py:145
  108.6 1.0 collective-permute-done.17
  109.8 0.9 collective-permute-start.23
  110.7 2.1 %collective-permute-start.19 = (bf16[64,2176]{1,0:T(8,128)(2,1)S(1)}, bf16[64,2176]{1,0:T(8,128)(2,1)S(1)}, u32[]{:S(2)}, u32[]{:S(2)}) collective-permute-start(bf16[64,2176]{1,0:T(8,128)(2,1)S(1)} %get-tuple-element.140), channel_id=1, source_target_pairs={{0,8},{4,12},{8,0},{12,4},{1,9},{5,13},{9,1},{13,5},{2,10},{6,14},... | collective-permute-start | bytes 835592 | tf_op jit(solution)/shard_map/ppermute | solution.py:278
  112.8 1.1 collective-permute-start.22
  113.9 13.9 %collective-permute-done.22 = f32[64,128]{1,0:T(8,128)S(1)} collective-permute-done((f32[64,128]{1,0:T(8,128)S(1)}, f32[64,128]{1,0:T(8,128)S(1)}, u32[]{:S(2)}, u32[]{:S(2)}) %collective-permute-start.22) | collective-permute-done | bytes 32800 | tf_op jit(solution)/shard_map/ppermute | solution.py:278
  128.2 1.6 %collective-permute-start.25 = (bf16[4,64,64]{2,1,0:T(8,128)(2,1)S(1)}, bf16[4,64,64]{2,1,0:T(8,128)(2,1)S(1)}, u32[]{:S(2)}, u32[]{:S(2)}) collective-permute-start(bf16[4,64,64]{2,1,0:T(8,128)(2,1)S(1)} %select_bitcast_fusion), channel_id=1, source_target_pairs={{0,2},{1,3},{2,0},{3,1},{4,6},{5,7},{6,4},{7,5},{8,10},{9,11},{10,... | collective-permute-start | bytes 98312 | tf_op jit(solution)/shard_map/ppermute | solution.py:417
  130.4 2.2 %collective-permute-done.25 = bf16[4,64,64]{2,1,0:T(8,128)(2,1)S(1)} collective-permute-done((bf16[4,64,64]{2,1,0:T(8,128)(2,1)S(1)}, bf16[4,64,64]{2,1,0:T(8,128)(2,1)S(1)}, u32[]{:S(2)}, u32[]{:S(2)}) %collective-permute-start.25) | collective-permute-done | bytes 32800 | tf_op jit(solution)/shard_map/ppermute | solution.py:417
  133.0 1.0 collective-permute-done.24
  134.1 2.5 %finish_steps.1 = (bf16[4,64,2048]{2,1,0:T(8,128)(2,1)}, bf16[64,2048]{1,0:T(8,128)(2,1)S(1)}) custom-call(bf16[256,64]{1,0:T(8,128)(2,1)S(1)} %bitcast.30, s32[256,1]{1,0:T(8,128)S(1)} %copy-done.4, s32[4]{0:T(128)S(1)} %pad_add_fusion.order_ref, bf16[64,2048]{1,0:T(8,128)(2,1)S(1)} %bitcast.31, bf16[64,2048]{1,0:T(8,128)(2,1)} %bitcast.14.refs_1_, ...), custom_call_target="tpu_custom_call" | custom-call | tf_op jit(solution)/shard_map/finish_steps/pallas_call | solution.py:203
  136.6 1.6 %collective-permute-done.27.refs_1_ = bf16[64,2048]{1,0:T(8,128)(2,1)S(1)} collective-permute-done((bf16[64,2048]{1,0:T(8,128)(2,1)S(1)}, bf16[64,2048]{1,0:T(8,128)(2,1)S(1)}, u32[]{:S(2)}, u32[]{:S(2)}) %collective-permute-start.27) | collective-permute-done | bytes 262176 | tf_op jit(solution)/shard_map/ppermute | solution.py:278
  (94 shorter events, 11.6 us)
Async XLA Ops:
  0.0 52.9 %copy-start = (s32[256,1]{0,1:T(1,128)S(1)}, s32[256,1]{0,1:T(1,128)}, u32[]{:S(2)}) copy-start(s32[256,1]{0,1:T(1,128)} %param.10) | copy-start | bytes 3076
  0.0 9.5 %collective-permute-start = (bf16[4,64,7168]{2,1,0:T(8,128)(2,1)}, bf16[4,64,7168]{2,1,0:T(8,128)(2,1)}, u32[]{:S(2)}, u32[]{:S(2)}) collective-permute-start(bf16[4,64,7168]{2,1,0:T(8,128)(2,1)} %refs_2_.7), channel_id=1, source_target_pairs={{0,1},{1,0},{2,3},{3,2},{4,5},{5,4},{6,7},{7,6},{8,9},{9,8},{10,11... | collective-permute-start | bytes 11010056 | tf_op jit(solution)/shard_map/ppermute | solution.py:268
  2.7 24.7 %collective-permute-start.3 = (bf16[1,64,7168]{2,1,0:T(8,128)(2,1)}, bf16[1,64,7168]{2,1,0:T(8,128)(2,1)S(1)}, u32[]{:S(2)}, u32[]{:S(2)}) collective-permute-start(bf16[1,64,7168]{2,1,0:T(8,128)(2,1)} %slice.51), channel_id=1, source_target_pairs={{2,0},{0,2},{3,1},{1,3},{6,4},{4,6},{7,5},{5,7},{10,8},{8,10},{11,... | collective-permute-start | bytes 2752520 | tf_op jit(solution)/shard_map/ppermute | solution.py:271
  5.3 21.4 %collective-permute-start.4 = (bf16[1,64,2048]{2,1,0:T(8,128)(2,1)S(1)}, bf16[1,64,2048]{2,1,0:T(8,128)(2,1)}, u32[]{:S(2)}, u32[]{:S(2)}) collective-permute-start(bf16[1,64,2048]{2,1,0:T(8,128)(2,1)S(1)} %copy-done.7), channel_id=1, source_target_pairs={{0,8},{4,12},{8,0},{12,4},{1,9},{5,13},{9,1},{13,5},{2,10},{6,14},... | collective-permute-start | bytes 786440 | tf_op jit(solution)/shard_map/ppermute | solution.py:274
  7.9 18.8 %collective-permute-start.5 = (bf16[1,64,2048]{2,1,0:T(8,128)(2,1)S(1)}, bf16[1,64,2048]{2,1,0:T(8,128)(2,1)S(1)}, u32[]{:S(2)}, u32[]{:S(2)}) collective-permute-start(bf16[1,64,2048]{2,1,0:T(8,128)(2,1)S(1)} %copy-done.7), channel_id=1, source_target_pairs={{0,4},{4,0},{8,12},{12,8},{1,5},{5,1},{9,13},{13,9},{2,6},{6,2},{1... | collective-permute-start | bytes 786440 | tf_op jit(solution)/shard_map/ppermute | solution.py:274
  27.4 2.5 %collective-permute-start.7 = (bf16[1,64,7168]{2,1,0:T(8,128)(2,1)S(1)}, bf16[1,64,7168]{2,1,0:T(8,128)(2,1)S(1)}, u32[]{:S(2)}, u32[]{:S(2)}) collective-permute-start(bf16[1,64,7168]{2,1,0:T(8,128)(2,1)S(1)} %collective-permute-done.3.refs_0_), channel_id=1, source_target_pairs={{0,1},{1,0},{2,3},{3,2},{4,5},{5,4},{6,7},{7,6},{8,9},{9,8},{10,11... | collective-permute-start | bytes 2752520 | tf_op jit(solution)/shard_map/ppermute | solution.py:268
  27.4 25.5 %copy-start.16 = (s32[4]{0:T(128)S(1)}, s32[4]{0:T(128)}, u32[]{:S(2)}) copy-start(s32[4]{0:T(128)} %param.11) | copy-start | bytes 52
  27.4 23.1 %collective-permute-start.2 = (bf16[1,64,7168]{2,1,0:T(8,128)(2,1)}, bf16[1,64,7168]{2,1,0:T(8,128)(2,1)}, u32[]{:S(2)}, u32[]{:S(2)}) collective-permute-start(bf16[1,64,7168]{2,1,0:T(8,128)(2,1)} %get-tuple-element.83), channel_id=1, source_target_pairs={{2,0},{0,2},{3,1},{1,3},{6,4},{4,6},{7,5},{5,7},{10,8},{8,10},{11,... | collective-permute-start | bytes 2752520 | tf_op jit(solution)/shard_map/ppermute | solution.py:271
  28.2 17.4 %collective-permute-start.6 = (bf16[1,64,2048]{2,1,0:T(8,128)(2,1)}, bf16[1,64,2048]{2,1,0:T(8,128)(2,1)S(1)}, u32[]{:S(2)}, u32[]{:S(2)}) collective-permute-start(bf16[1,64,2048]{2,1,0:T(8,128)(2,1)} %collective-permute-done.4), channel_id=1, source_target_pairs={{0,4},{4,0},{8,12},{12,8},{1,5},{5,1},{9,13},{13,9},{2,6},{6,2},{1... | collective-permute-start | bytes 786440 | tf_op jit(solution)/shard_map/ppermute | solution.py:274
  50.5 5.1 %collective-permute-start.8 = (bf16[1,64,7168]{2,1,0:T(8,128)(2,1)}, bf16[1,64,7168]{2,1,0:T(8,128)(2,1)}, u32[]{:S(2)}, u32[]{:S(2)}) collective-permute-start(bf16[1,64,7168]{2,1,0:T(8,128)(2,1)} %collective-permute-done.2.refs_0_), channel_id=1, source_target_pairs={{0,1},{1,0},{2,3},{3,2},{4,5},{5,4},{6,7},{7,6},{8,9},{9,8},{10,11... | collective-permute-start | bytes 2752520 | tf_op jit(solution)/shard_map/ppermute | solution.py:268
  50.5 23.4 %collective-permute-start.1 = (bf16[1,64,7168]{2,1,0:T(8,128)(2,1)}, bf16[1,64,7168]{2,1,0:T(8,128)(2,1)S(1)}, u32[]{:S(2)}, u32[]{:S(2)}) collective-permute-start(bf16[1,64,7168]{2,1,0:T(8,128)(2,1)} %get-tuple-element.82), channel_id=1, source_target_pairs={{2,0},{0,2},{3,1},{1,3},{6,4},{4,6},{7,5},{5,7},{10,8},{8,10},{11,... | collective-permute-start | bytes 2752520 | tf_op jit(solution)/shard_map/ppermute | solution.py:271
  51.3 22.6 %collective-permute-start.11 = (bf16[128,2176]{1,0:T(8,128)(2,1)}, bf16[128,2176]{1,0:T(8,128)(2,1)}, u32[]{:S(2)}, u32[]{:S(2)}) collective-permute-start(bf16[128,2176]{1,0:T(8,128)(2,1)} %copy-done.13), channel_id=1, source_target_pairs={{0,4},{4,0},{8,12},{12,8},{1,5},{5,1},{9,13},{13,9},{2,6},{6,2},{1... | collective-permute-start | bytes 1671176 | tf_op jit(solution)/shard_map/ppermute | solution.py:274
  53.9 39.2 %collective-permute-start.13 = (bf16[1,64,7168]{2,1,0:T(8,128)(2,1)}, bf16[1,64,7168]{2,1,0:T(8,128)(2,1)S(1)}, u32[]{:S(2)}, u32[]{:S(2)}) collective-permute-start(bf16[1,64,7168]{2,1,0:T(8,128)(2,1)} %get-tuple-element.116), channel_id=1, source_target_pairs={{2,0},{0,2},{3,1},{1,3},{6,4},{4,6},{7,5},{5,7},{10,8},{8,10},{11,... | collective-permute-start | bytes 2752520 | tf_op jit(solution)/shard_map/ppermute | solution.py:271
  54.5 21.5 %collective-permute-start.10 = (bf16[64,2176]{1,0:T(8,128)(2,1)}, bf16[64,2176]{1,0:T(8,128)(2,1)S(1)}, u32[]{:S(2)}, u32[]{:S(2)}) collective-permute-start(bf16[64,2176]{1,0:T(8,128)(2,1)} %copy-done.15), channel_id=1, source_target_pairs={{0,4},{4,0},{8,12},{12,8},{1,5},{5,1},{9,13},{13,9},{2,6},{6,2},{1... | collective-permute-start | bytes 835592 | tf_op jit(solution)/shard_map/ppermute | solution.py:274
  55.6 53.0 %collective-permute-start.18 = (bf16[64,2176]{1,0:T(8,128)(2,1)}, bf16[64,2176]{1,0:T(8,128)(2,1)S(1)}, u32[]{:S(2)}, u32[]{:S(2)}) collective-permute-start(bf16[64,2176]{1,0:T(8,128)(2,1)} %copy-done.14), channel_id=1, source_target_pairs={{0,4},{4,0},{8,12},{12,8},{1,5},{5,1},{9,13},{13,9},{2,6},{6,2},{1... | collective-permute-start | bytes 835592 | tf_op jit(solution)/shard_map/ppermute | solution.py:274
  73.9 4.9 %collective-permute-start.9 = (bf16[1,64,7168]{2,1,0:T(8,128)(2,1)S(1)}, bf16[1,64,7168]{2,1,0:T(8,128)(2,1)S(1)}, u32[]{:S(2)}, u32[]{:S(2)}) collective-permute-start(bf16[1,64,7168]{2,1,0:T(8,128)(2,1)S(1)} %collective-permute-done.1.refs_0_), channel_id=1, source_target_pairs={{0,1},{1,0},{2,3},{3,2},{4,5},{5,4},{6,7},{7,6},{8,9},{9,8},{10,11... | collective-permute-start | bytes 2752520 | tf_op jit(solution)/shard_map/ppermute | solution.py:268
  75.1 18.1 %collective-permute-start.15 = (bf16[64,2176]{1,0:T(8,128)(2,1)S(1)}, bf16[64,2176]{1,0:T(8,128)(2,1)S(1)}, u32[]{:S(2)}, u32[]{:S(2)}) collective-permute-start(bf16[64,2176]{1,0:T(8,128)(2,1)S(1)} %get-tuple-element.125), channel_id=1, source_target_pairs={{0,4},{4,0},{8,12},{12,8},{1,5},{5,1},{9,13},{13,9},{2,6},{6,2},{1... | collective-permute-start | bytes 835592 | tf_op jit(solution)/shard_map/ppermute | solution.py:274
  76.1 17.3 %collective-permute-start.12 = (bf16[64,2176]{1,0:T(8,128)(2,1)S(1)}, bf16[64,2176]{1,0:T(8,128)(2,1)S(1)}, u32[]{:S(2)}, u32[]{:S(2)}) collective-permute-start(bf16[64,2176]{1,0:T(8,128)(2,1)S(1)} %select_convert_fusion.2), channel_id=1, source_target_pairs={{0,8},{4,12},{8,0},{12,4},{1,9},{5,13},{9,1},{13,5},{2,10},{6,14},... | collective-permute-start | bytes 835592 | tf_op jit(solution)/shard_map/ppermute | solution.py:278
  78.7 18.2 %collective-permute-start.21 = (bf16[64,2176]{1,0:T(8,128)(2,1)S(1)}, bf16[64,2176]{1,0:T(8,128)(2,1)S(1)}, u32[]{:S(2)}, u32[]{:S(2)}) collective-permute-start(bf16[64,2176]{1,0:T(8,128)(2,1)S(1)} %get-tuple-element.147), channel_id=1, source_target_pairs={{0,4},{4,0},{8,12},{12,8},{1,5},{5,1},{9,13},{13,9},{2,6},{6,2},{1... | collective-permute-start | bytes 835592 | tf_op jit(solution)/shard_map/ppermute | solution.py:274
  93.1 3.9 %collective-permute-start.14 = (bf16[1,64,7168]{2,1,0:T(8,128)(2,1)S(1)}, bf16[1,64,7168]{2,1,0:T(8,128)(2,1)S(1)}, u32[]{:S(2)}, u32[]{:S(2)}) collective-permute-start(bf16[1,64,7168]{2,1,0:T(8,128)(2,1)S(1)} %collective-permute-done.13.refs_0_), channel_id=1, source_target_pairs={{0,1},{1,0},{2,3},{3,2},{4,5},{5,4},{6,7},{7,6},{8,9},{9,8},{10,11... | collective-permute-start | bytes 2752520 | tf_op jit(solution)/shard_map/ppermute | solution.py:268
  93.4 14.3 %copy-start.5 = (bf16[64,2176]{1,0:T(8,128)(2,1)}, bf16[64,2176]{1,0:T(8,128)(2,1)S(1)}, u32[]{:S(2)}) copy-start(bf16[64,2176]{1,0:T(8,128)(2,1)S(1)} %collective-permute-done.12.refs_5_) | copy-start | bytes 835588
  93.4 16.3 %collective-permute-start.16 = (bf16[64,2176]{1,0:T(8,128)(2,1)S(1)}, bf16[64,2176]{1,0:T(8,128)(2,1)S(1)}, u32[]{:S(2)}, u32[]{:S(2)}) collective-permute-start(bf16[64,2176]{1,0:T(8,128)(2,1)S(1)} %select_convert_fusion.1), channel_id=1, source_target_pairs={{0,8},{4,12},{8,0},{12,4},{1,9},{5,13},{9,1},{13,5},{2,10},{6,14},... | collective-permute-start | bytes 835592 | tf_op jit(solution)/shard_map/ppermute | solution.py:278
  95.4 14.2 %collective-permute-start.17 = (bf16[64,2176]{1,0:T(8,128)(2,1)S(1)}, bf16[64,2176]{1,0:T(8,128)(2,1)S(1)}, u32[]{:S(2)}, u32[]{:S(2)}) collective-permute-start(bf16[64,2176]{1,0:T(8,128)(2,1)S(1)} %get-tuple-element.135), channel_id=1, source_target_pairs={{0,4},{4,0},{8,12},{12,8},{1,5},{5,1},{9,13},{13,9},{2,6},{6,2},{1... | collective-permute-start | bytes 835592 | tf_op jit(solution)/shard_map/ppermute | solution.py:274
  97.0 12.6 %copy-start.3 = (f32[64,2176]{1,0:T(8,128)S(1)}, f32[64,2176]{1,0:T(8,128)}, u32[]{:S(2)}) copy-start(f32[64,2176]{1,0:T(8,128)} %copy-done.2) | copy-start | bytes 1671172
  107.7 5.0 %collective-permute-start.20 = (f32[64,128]{1,0:T(8,128)S(1)}, f32[64,128]{1,0:T(8,128)S(1)}, u32[]{:S(2)}, u32[]{:S(2)}) collective-permute-start(f32[64,128]{1,0:T(8,128)S(1)} %get-tuple-element.144), channel_id=1, source_target_pairs={{0,4},{4,0},{8,12},{12,8},{1,5},{5,1},{9,13},{13,9},{2,6},{6,2},{1... | collective-permute-start | bytes 98312 | tf_op jit(solution)/shard_map/ppermute | solution.py:274
  109.8 18.1 %collective-permute-start.23 = (bf16[64,2048]{1,0:T(8,128)(2,1)S(1)}, bf16[64,2048]{1,0:T(8,128)(2,1)S(1)}, u32[]{:S(2)}, u32[]{:S(2)}) collective-permute-start(bf16[64,2048]{1,0:T(8,128)(2,1)S(1)} %get-tuple-element.150), channel_id=1, source_target_pairs={{0,4},{4,0},{8,12},{12,8},{1,5},{5,1},{9,13},{13,9},{2,6},{6,2},{1... | collective-permute-start | bytes 786440 | tf_op jit(solution)/shard_map/ppermute | solution.py:274
  110.7 17.4 %collective-permute-start.19 = (bf16[64,2176]{1,0:T(8,128)(2,1)S(1)}, bf16[64,2176]{1,0:T(8,128)(2,1)S(1)}, u32[]{:S(2)}, u32[]{:S(2)}) collective-permute-start(bf16[64,2176]{1,0:T(8,128)(2,1)S(1)} %get-tuple-element.140), channel_id=1, source_target_pairs={{0,8},{4,12},{8,0},{12,4},{1,9},{5,13},{9,1},{13,5},{2,10},{6,14},... | collective-permute-start | bytes 835592 | tf_op jit(solution)/shard_map/ppermute | solution.py:278
  112.8 15.1 %collective-permute-start.22 = (f32[64,128]{1,0:T(8,128)S(1)}, f32[64,128]{1,0:T(8,128)S(1)}, u32[]{:S(2)}, u32[]{:S(2)}) collective-permute-start(f32[64,128]{1,0:T(8,128)S(1)} %get-tuple-element.159), channel_id=1, source_target_pairs={{0,8},{4,12},{8,0},{12,4},{1,9},{5,13},{9,1},{13,5},{2,10},{6,14},... | collective-permute-start | bytes 98312 | tf_op jit(solution)/shard_map/ppermute | solution.py:278
  128.0 10.3 %collective-permute-start.27 = (bf16[64,2048]{1,0:T(8,128)(2,1)S(1)}, bf16[64,2048]{1,0:T(8,128)(2,1)S(1)}, u32[]{:S(2)}, u32[]{:S(2)}) collective-permute-start(bf16[64,2048]{1,0:T(8,128)(2,1)S(1)} %select_convert_fusion.3), channel_id=1, source_target_pairs={{0,8},{4,12},{8,0},{12,4},{1,9},{5,13},{9,1},{13,5},{2,10},{6,14},... | collective-permute-start | bytes 786440 | tf_op jit(solution)/shard_map/ppermute | solution.py:278
  128.2 4.3 %collective-permute-start.25 = (bf16[4,64,64]{2,1,0:T(8,128)(2,1)S(1)}, bf16[4,64,64]{2,1,0:T(8,128)(2,1)S(1)}, u32[]{:S(2)}, u32[]{:S(2)}) collective-permute-start(bf16[4,64,64]{2,1,0:T(8,128)(2,1)S(1)} %select_bitcast_fusion), channel_id=1, source_target_pairs={{0,2},{1,3},{2,0},{3,1},{4,6},{5,7},{6,4},{7,5},{8,10},{9,11},{10,... | collective-permute-start | bytes 98312 | tf_op jit(solution)/shard_map/ppermute | solution.py:417
  129.8 3.1 %collective-permute-start.26 = (bf16[4,64,64]{2,1,0:T(8,128)(2,1)S(1)}, bf16[4,64,64]{2,1,0:T(8,128)(2,1)S(1)}, u32[]{:S(2)}, u32[]{:S(2)}) collective-permute-start(bf16[4,64,64]{2,1,0:T(8,128)(2,1)S(1)} %select_bitcast_fusion), channel_id=1, source_target_pairs={{0,3},{1,0},{2,1},{3,2},{4,7},{5,4},{6,5},{7,6},{8,11},{9,8},{10,9... | collective-permute-start | bytes 98312 | tf_op jit(solution)/shard_map/ppermute | solution.py:417
  129.8 4.2 %collective-permute-start.24 = (bf16[4,64,64]{2,1,0:T(8,128)(2,1)S(1)}, bf16[4,64,64]{2,1,0:T(8,128)(2,1)S(1)}, u32[]{:S(2)}, u32[]{:S(2)}) collective-permute-start(bf16[4,64,64]{2,1,0:T(8,128)(2,1)S(1)} %select_bitcast_fusion), channel_id=1, source_target_pairs={{0,1},{1,2},{2,3},{3,0},{4,5},{5,6},{6,7},{7,4},{8,9},{9,10},{10,1... | collective-permute-start | bytes 98312 | tf_op jit(solution)/shard_map/ppermute | solution.py:417
  (14 other events, 55.0 us)

commit v16 on v15

--- a/solution.py
+++ b/solution.py
@@ -373,8 +373,9 @@
         remote.update({(step, shift): from_rep(rows, shift) for shift in range(1, n_rep)})
     jobs = [([((0, 0), lead)], send, keep, jnp.bfloat16)]
     for piece, (step, shift) in enumerate(pieces):
+        arrived = [received for _, received, _, _ in first_leg]
         sends = gap(send, jobs)
-        own, panels, _ = lax.optimization_barrier((remote[step, shift], panels, send))
+        own, panels, *_ = lax.optimization_barrier((remote[step, shift], panels, arrived, send))
         if piece == 0:
             panels, order = panels + [swap_tensor(panels[1], bits[1])], order + [bits[0] ^ bits[1]]
             panels, order = spread_panels(panels, order, bits[2:])
@@ -398,6 +399,8 @@
         to_group(pick(values, (group_index + hop - rep_index) % n_rep), hop) for hop in range(1, n_rep)
     ])
     rounded = gap(send, [])
+    kept, *received = ended[RANK_NAME]
+    ended[RANK_NAME] = (after(kept, rounded), *received)
 
     def rank_sum(name):
         kept, *received = [value[:, -rank_columns(factors):] for value in ended[name]]
@@ -407,7 +410,6 @@
 
     finished = jnp.stack([rank_sum(step) for step in range(step_count - 1)] + [rank_sum(RANK_NAME)])
     finished = finished.astype(jnp.bfloat16).reshape(step_count, rows_mine, owned_slots, rank_size)
-    finished = lax.optimization_barrier((finished, rounded))[0]
     ended.update((name, (kept, *received)) for name, kept, received in second_leg)
     masked = jnp.sum(
         jnp.where(owned_hot[None, :, :, None], finished, 0), axis=2, dtype=jnp.float32

time: 139 us -> 146 us (1.050)
  waiting for transfers between devices: 29.8 us -> 35.3 us
  other arithmetic: 2.21 us -> 3.97 us
    ppermute x11, waiting for transfers between devices: 1.01 us -> 17.4 us  [swap_tensor(): return lax.ppermute(value, 'tp', [(i, i ^ bit) for i in range(n_tensor)])]
    ppermute x5, waiting for transfers between devices: 15.6 us -> 8.79 us  [to_group(): lax.ppermute(value, 'tp', [(i, (i + moved) % n_tensor) for i in range(n_t...]
    ppermute x4, waiting for transfers between devices: 9.48 us -> 5.39 us  [from_rep(): lax.ppermute(value, 'rep', [((i + shift) % n_rep, i) for i in range(n_rep)])]
    ppermute x5, starting transfers between devices: 7.87 us -> 5.89 us  [to_group(): lax.ppermute(value, 'tp', [(i, (i + moved) % n_tensor) for i in range(n_t...]
    convert_element_type x4, other arithmetic: 0.37 us -> 2.28 us  [gap(): pick(values, (group_index + hop - rep_index) % n_rep).astype(jnp.bfloat16)]
    ppermute x4, starting transfers between devices: 4.69 us -> 6.23 us  [from_rep(): lax.ppermute(value, 'rep', [((i + shift) % n_rep, i) for i in range(n_rep)])]
    unnamed x34 -> x36, local copies, waits for them, and re-layouts: 4.63 us -> 4.27 us
  transfers between devices with their start and end apart: 28 -> 28, of which waited for: 10 -> 11; matrix products, arithmetic and copies ran while one was open for 4% -> 5% of each run, Pallas kernels for 50% -> 47%
where the time goes in v16:
time: 146 us
  Pallas kernels  69.8 us (48%)
  waiting for transfers between devices  35.3 us (24%)
  starting transfers between devices  29.2 us (20%)
  local copies, waits for them, and re-layouts  7.35 us (5%)
  other arithmetic  3.97 us (3%)
    pallas_call x5, Pallas kernels, partial_products(): pl.pallas_call(functools.partial(matmul_body, spans, staged, apart), in_s...  66.5 us
    ppermute x11, waiting for transfers between devices, swap_tensor(): return lax.ppermute(value, 'tp', [(i, i ^ bit) for i in range(n_tensor)])  17.4 us
    ppermute x11, starting transfers between devices, swap_tensor(): return lax.ppermute(value, 'tp', [(i, i ^ bit) for i in range(n_tensor)])  14.9 us
    ppermute x5, waiting for transfers between devices, to_group(): lax.ppermute(value, 'tp', [(i, (i + moved) % n_tensor) for i in range(n_t...  8.79 us
    ppermute x4, starting transfers between devices, from_rep(): lax.ppermute(value, 'rep', [((i + shift) % n_rep, i) for i in range(n_rep)])  6.23 us
    ppermute x5, starting transfers between devices, to_group(): lax.ppermute(value, 'tp', [(i, (i + moved) % n_tensor) for i in range(n_t...  5.89 us
    ppermute x4, waiting for transfers between devices, from_rep(): lax.ppermute(value, 'rep', [((i + shift) % n_rep, i) for i in range(n_rep)])  5.39 us
    unnamed x36, local copies, waits for them, and re-layouts  4.27 us
  transfers between devices with their start and end apart: 28, of which 11 were waited for; matrix products, arithmetic and copies ran while one was open for 5% of the time, Pallas kernels for 47%

profile of v16, /device:TPU:0, one launch (start us, length us, event | category | flops | bytes accessed | tf_op | source)
XLA Modules:
  0.0 146.0 jit_solution(13620123261367128602)
XLA Ops:
  0.5 2.2 %slice.51 = bf16[1,64,7168]{2,1,0:T(8,128)(2,1)} slice(bf16[4,64,7168]{2,1,0:T(8,128)(2,1)} %refs_2_.7), slice={[0:1], [0:64], [0:7168]} | slice | bytes 1835008 | tf_op jit(solution)/shard_map/slice | solution.py:293
  2.7 2.6 %collective-permute-start.3 = (bf16[1,64,7168]{2,1,0:T(8,128)(2,1)}, bf16[1,64,7168]{2,1,0:T(8,128)(2,1)S(1)}, u32[]{:S(2)}, u32[]{:S(2)}) collective-permute-start(bf16[1,64,7168]{2,1,0:T(8,128)(2,1)} %slice.51), channel_id=1, source_target_pairs={{2,0},{0,2},{3,1},{1,3},{6,4},{4,6},{7,5},{5,7},{10,8},{8,10},{11,... | collective-permute-start | bytes 2752520 | tf_op jit(solution)/shard_map/ppermute | solution.py:271
  5.3 2.6 %collective-permute-start.4 = (bf16[1,64,2048]{2,1,0:T(8,128)(2,1)S(1)}, bf16[1,64,2048]{2,1,0:T(8,128)(2,1)}, u32[]{:S(2)}, u32[]{:S(2)}) collective-permute-start(bf16[1,64,2048]{2,1,0:T(8,128)(2,1)S(1)} %copy-done.7), channel_id=1, source_target_pairs={{0,8},{4,12},{8,0},{12,4},{1,9},{5,13},{9,1},{13,5},{2,10},{6,14},... | collective-permute-start | bytes 786440 | tf_op jit(solution)/shard_map/ppermute | solution.py:274
  7.9 1.6 %collective-permute-start.5 = (bf16[1,64,2048]{2,1,0:T(8,128)(2,1)S(1)}, bf16[1,64,2048]{2,1,0:T(8,128)(2,1)S(1)}, u32[]{:S(2)}, u32[]{:S(2)}) collective-permute-start(bf16[1,64,2048]{2,1,0:T(8,128)(2,1)S(1)} %copy-done.7), channel_id=1, source_target_pairs={{0,4},{4,0},{8,12},{12,8},{1,5},{5,1},{9,13},{13,9},{2,6},{6,2},{1... | collective-permute-start | bytes 786440 | tf_op jit(solution)/shard_map/ppermute | solution.py:274
  9.5 16.3 %partial_products.5 = (bf16[128,2176]{1,0:T(8,128)(2,1)S(1)}, f32[128,2176]{1,0:T(8,128)S(1)}, bf16[1,64,7168]{2,1,0:T(8,128)(2,1)}, bf16[1,64,7168]{2,1,0:T(8,128)(2,1)}, bf16[1,64,7168]{2,1,0:T(8,128)(2,1)}) custom-call(s32[1]{0:T(128)} %bitcast.1.pos_ref, bf16[4,64,7168]{2,1,0:T(8,128)(2,1)} %refs_2_.7, ...), custom_call_target="tpu_custom_call" | custom-call | tf_op jit(solution)/shard_map/partial_products/pallas_call | solution.py:145
  26.6 1.6 %collective-permute-start.2 = (bf16[1,64,7168]{2,1,0:T(8,128)(2,1)}, bf16[1,64,7168]{2,1,0:T(8,128)(2,1)}, u32[]{:S(2)}, u32[]{:S(2)}) collective-permute-start(bf16[1,64,7168]{2,1,0:T(8,128)(2,1)} %get-tuple-element.83), channel_id=1, source_target_pairs={{2,0},{0,2},{3,1},{1,3},{6,4},{4,6},{7,5},{5,7},{10,8},{8,10},{11,... | collective-permute-start | bytes 2752520 | tf_op jit(solution)/shard_map/ppermute | solution.py:271
  28.2 1.6 %collective-permute-start.7 = (bf16[128,2176]{1,0:T(8,128)(2,1)S(1)}, bf16[128,2176]{1,0:T(8,128)(2,1)S(1)}, u32[]{:S(2)}, u32[]{:S(2)}) collective-permute-start(bf16[128,2176]{1,0:T(8,128)(2,1)S(1)} %get-tuple-element.84), channel_id=1, source_target_pairs={{0,4},{4,0},{8,12},{12,8},{1,5},{5,1},{9,13},{13,9},{2,6},{6,2},{1... | collective-permute-start | bytes 1671176 | tf_op jit(solution)/shard_map/ppermute | solution.py:274
  30.2 13.4 %partial_products.6 = (bf16[64,2176]{1,0:T(8,128)(2,1)S(1)}, bf16[64,2176]{1,0:T(8,128)(2,1)S(1)}, f32[64,2176]{1,0:T(8,128)S(1)}, f32[64,2176]{1,0:T(8,128)S(1)}) custom-call(s32[1]{0:T(128)} %bitcast.1.pos_ref, bf16[1,64,7168]{2,1,0:T(8,128)(2,1)S(1)} %collective-permute-done.3.refs_0_, bf16[1,64,7168]{2,1,0:T(8,128)(2,1)S(1)} %collective-permute-done.8.refs_1_, ...), custom_call_target="tpu_custom_call" | custom-call | tf_op jit(solution)/shard_map/partial_products/pallas_call | solution.py:145
  45.9 2.7 %collective-permute-done.6 = bf16[1,64,2048]{2,1,0:T(8,128)(2,1)S(1)} collective-permute-done((bf16[1,64,2048]{2,1,0:T(8,128)(2,1)}, bf16[1,64,2048]{2,1,0:T(8,128)(2,1)S(1)}, u32[]{:S(2)}, u32[]{:S(2)}) %collective-permute-start.6) | collective-permute-done | bytes 262176 | tf_op jit(solution)/shard_map/ppermute | solution.py:274
  50.2 1.1 collective-permute-start.1
  51.5 1.6 %collective-permute-start.9 = (bf16[64,2176]{1,0:T(8,128)(2,1)}, bf16[64,2176]{1,0:T(8,128)(2,1)}, u32[]{:S(2)}, u32[]{:S(2)}) collective-permute-start(bf16[64,2176]{1,0:T(8,128)(2,1)} %copy-done.14), channel_id=1, source_target_pairs={{0,4},{4,0},{8,12},{12,8},{1,5},{5,1},{9,13},{13,9},{2,6},{6,2},{1... | collective-permute-start | bytes 835592 | tf_op jit(solution)/shard_map/ppermute | solution.py:274
  55.3 15.4 %partial_products.7 = (bf16[64,2176]{1,0:T(8,128)(2,1)S(1)}, bf16[64,2176]{1,0:T(8,128)(2,1)S(1)}, f32[64,2176]{1,0:T(8,128)S(1)}, f32[64,2176]{1,0:T(8,128)S(1)}) custom-call(s32[1]{0:T(128)} %bitcast.1.pos_ref, bf16[1,64,7168]{2,1,0:T(8,128)(2,1)} %collective-permute-done.2.refs_0_, bf16[1,64,7168]{2,1,0:T(8,128)(2,1)} %collective-permute-done.11.refs_1_, ...), custom_call_target="tpu_custom_call" | custom-call | tf_op jit(solution)/shard_map/partial_products/pallas_call | solution.py:145
  70.7 2.9 %collective-permute-done.1.refs_0_ = bf16[1,64,7168]{2,1,0:T(8,128)(2,1)S(1)} collective-permute-done((bf16[1,64,7168]{2,1,0:T(8,128)(2,1)}, bf16[1,64,7168]{2,1,0:T(8,128)(2,1)S(1)}, u32[]{:S(2)}, u32[]{:S(2)}) %collective-permute-start.1) | collective-permute-done | bytes 917536 | tf_op jit(solution)/shard_map/ppermute | solution.py:271
  73.7 1.6 %collective-permute-start.15 = (bf16[64,2176]{1,0:T(8,128)(2,1)S(1)}, bf16[64,2176]{1,0:T(8,128)(2,1)S(1)}, u32[]{:S(2)}, u32[]{:S(2)}) collective-permute-start(bf16[64,2176]{1,0:T(8,128)(2,1)S(1)} %get-tuple-element.123), channel_id=1, source_target_pairs={{0,4},{4,0},{8,12},{12,8},{1,5},{5,1},{9,13},{13,9},{2,6},{6,2},{1... | collective-permute-start | bytes 835592 | tf_op jit(solution)/shard_map/ppermute | solution.py:274
  76.9 2.6 %collective-permute-start.13 = (bf16[64,2176]{1,0:T(8,128)(2,1)S(1)}, bf16[64,2176]{1,0:T(8,128)(2,1)S(1)}, u32[]{:S(2)}, u32[]{:S(2)}) collective-permute-start(bf16[64,2176]{1,0:T(8,128)(2,1)S(1)} %select_convert_fusion.2), channel_id=1, source_target_pairs={{0,8},{4,12},{8,0},{12,4},{1,9},{5,13},{9,1},{13,5},{2,10},{6,14},... | collective-permute-start | bytes 835592 | tf_op jit(solution)/shard_map/ppermute | solution.py:278
  79.5 10.7 %partial_products.8 = (bf16[64,2176]{1,0:T(8,128)(2,1)S(1)}, f32[64,2176]{1,0:T(8,128)S(1)}) custom-call(s32[1]{0:T(128)} %bitcast.1.pos_ref, bf16[1,64,7168]{2,1,0:T(8,128)(2,1)S(1)} %collective-permute-done.1.refs_0_, bf16[1,64,7168]{2,1,0:T(8,128)(2,1)S(1)} %collective-permute-done.12.refs_1_, bf16[7168,2048]{1,0:T(8,128)(2,1)} %refs_2_.9, ...), custom_call_target="tpu_custom_call" | custom-call | tf_op jit(solution)/shard_map/partial_products/pallas_call | solution.py:145
  90.2 2.1 %collective-permute-done.14.refs_0_ = bf16[1,64,7168]{2,1,0:T(8,128)(2,1)S(1)} collective-permute-done((bf16[1,64,7168]{2,1,0:T(8,128)(2,1)}, bf16[1,64,7168]{2,1,0:T(8,128)(2,1)S(1)}, u32[]{:S(2)}, u32[]{:S(2)}) %collective-permute-start.14) | collective-permute-done | bytes 917536 | tf_op jit(solution)/shard_map/ppermute | solution.py:271
  92.3 2.5 %collective-permute-done.16 = bf16[64,2176]{1,0:T(8,128)(2,1)S(1)} collective-permute-done((bf16[64,2176]{1,0:T(8,128)(2,1)S(1)}, bf16[64,2176]{1,0:T(8,128)(2,1)S(1)}, u32[]{:S(2)}, u32[]{:S(2)}) %collective-permute-start.16) | collective-permute-done | bytes 278560 | tf_op jit(solution)/shard_map/ppermute | solution.py:274
  94.8 1.1 slice_select_fusion.1
  96.0 1.7 %collective-permute-start.18 = (bf16[64,2176]{1,0:T(8,128)(2,1)S(1)}, bf16[64,2176]{1,0:T(8,128)(2,1)S(1)}, u32[]{:S(2)}, u32[]{:S(2)}) collective-permute-start(bf16[64,2176]{1,0:T(8,128)(2,1)S(1)} %select_convert_fusion.1), channel_id=1, source_target_pairs={{0,8},{4,12},{8,0},{12,4},{1,9},{5,13},{9,1},{13,5},{2,10},{6,14},... | collective-permute-start | bytes 835592 | tf_op jit(solution)/shard_map/ppermute | solution.py:278
  97.8 2.5 %collective-permute-start.19 = (bf16[64,2176]{1,0:T(8,128)(2,1)S(1)}, bf16[64,2176]{1,0:T(8,128)(2,1)S(1)}, u32[]{:S(2)}, u32[]{:S(2)}) collective-permute-start(bf16[64,2176]{1,0:T(8,128)(2,1)S(1)} %get-tuple-element.137), channel_id=1, source_target_pairs={{0,4},{4,0},{8,12},{12,8},{1,5},{5,1},{9,13},{13,9},{2,6},{6,2},{1... | collective-permute-start | bytes 835592 | tf_op jit(solution)/shard_map/ppermute | solution.py:274
  100.3 10.7 %partial_products.9 = (bf16[64,2048]{1,0:T(8,128)(2,1)S(1)}, f32[64,2048]{1,0:T(8,128)S(1)}, f32[64,128]{1,0:T(8,128)S(1)}, f32[64,128]{1,0:T(8,128)S(1)}) custom-call(s32[1]{0:T(128)} %bitcast.1.pos_ref, bf16[1,64,7168]{2,1,0:T(8,128)(2,1)S(1)} %collective-permute-done.14.refs_0_, bf16[1,64,7168]{2,1,0:T(8,128)(2,1)S(1)} %collective-permute-done.17.refs_1_, ...), custom_call_target="tpu_custom_call" | custom-call | tf_op jit(solution)/shard_map/partial_products/pallas_call | solution.py:145
  111.0 1.2 collective-permute-done.19
  112.2 1.1 select_convert_fusion
  114.0 1.4 collective-permute-start.22
  115.4 1.4 collective-permute-start.20
  116.8 4.8 %collective-permute-done.21 = f32[64,128]{1,0:T(8,128)S(1)} collective-permute-done((f32[64,128]{1,0:T(8,128)S(1)}, f32[64,128]{1,0:T(8,128)S(1)}, u32[]{:S(2)}, u32[]{:S(2)}) %collective-permute-start.21) | collective-permute-done | bytes 32800 | tf_op jit(solution)/shard_map/ppermute | solution.py:274
  121.8 6.2 %collective-permute-done.22 = bf16[64,2048]{1,0:T(8,128)(2,1)S(1)} collective-permute-done((bf16[64,2048]{1,0:T(8,128)(2,1)S(1)}, bf16[64,2048]{1,0:T(8,128)(2,1)S(1)}, u32[]{:S(2)}, u32[]{:S(2)}) %collective-permute-start.22) | collective-permute-done | bytes 262176 | tf_op jit(solution)/shard_map/ppermute | solution.py:274
  128.1 8.8 %collective-permute-done.23 = f32[64,128]{1,0:T(8,128)S(1)} collective-permute-done((f32[64,128]{1,0:T(8,128)S(1)}, f32[64,128]{1,0:T(8,128)S(1)}, u32[]{:S(2)}, u32[]{:S(2)}) %collective-permute-start.23) | collective-permute-done | bytes 32800 | tf_op jit(solution)/shard_map/ppermute | solution.py:278
  137.1 1.1 collective-permute-start.25
  138.8 2.9 %collective-permute-done.25 = bf16[4,64,64]{2,1,0:T(8,128)(2,1)S(1)} collective-permute-done((bf16[4,64,64]{2,1,0:T(8,128)(2,1)S(1)}, bf16[4,64,64]{2,1,0:T(8,128)(2,1)S(1)}, u32[]{:S(2)}, u32[]{:S(2)}) %collective-permute-start.25) | collective-permute-done | bytes 32800 | tf_op jit(solution)/shard_map/ppermute | solution.py:419
  142.6 2.5 %finish_steps.1 = (bf16[4,64,2048]{2,1,0:T(8,128)(2,1)}, bf16[64,2048]{1,0:T(8,128)(2,1)S(1)}) custom-call(bf16[256,64]{1,0:T(8,128)(2,1)S(1)} %bitcast.26, s32[256,1]{1,0:T(8,128)S(1)} %copy-done.4, s32[4]{0:T(128)S(1)} %pad_add_fusion.order_ref, bf16[64,2048]{1,0:T(8,128)(2,1)S(1)} %bitcast.27, bf16[64,2048]{1,0:T(8,128)(2,1)} %bitcast.13.refs_1_, ...), custom_call_target="tpu_custom_call" | custom-call | tf_op jit(solution)/shard_map/finish_steps/pallas_call | solution.py:203
  (95 shorter events, 13.1 us)
Async XLA Ops:
  0.0 51.3 %copy-start = (s32[256,1]{0,1:T(1,128)S(1)}, s32[256,1]{0,1:T(1,128)}, u32[]{:S(2)}) copy-start(s32[256,1]{0,1:T(1,128)} %param.10) | copy-start | bytes 3076
  0.0 9.5 %collective-permute-start = (bf16[4,64,7168]{2,1,0:T(8,128)(2,1)}, bf16[4,64,7168]{2,1,0:T(8,128)(2,1)}, u32[]{:S(2)}, u32[]{:S(2)}) collective-permute-start(bf16[4,64,7168]{2,1,0:T(8,128)(2,1)} %refs_2_.7), channel_id=1, source_target_pairs={{0,1},{1,0},{2,3},{3,2},{4,5},{5,4},{6,7},{7,6},{8,9},{9,8},{10,11... | collective-permute-start | bytes 11010056 | tf_op jit(solution)/shard_map/ppermute | solution.py:268
  2.7 23.9 %collective-permute-start.3 = (bf16[1,64,7168]{2,1,0:T(8,128)(2,1)}, bf16[1,64,7168]{2,1,0:T(8,128)(2,1)S(1)}, u32[]{:S(2)}, u32[]{:S(2)}) collective-permute-start(bf16[1,64,7168]{2,1,0:T(8,128)(2,1)} %slice.51), channel_id=1, source_target_pairs={{2,0},{0,2},{3,1},{1,3},{6,4},{4,6},{7,5},{5,7},{10,8},{8,10},{11,... | collective-permute-start | bytes 2752520 | tf_op jit(solution)/shard_map/ppermute | solution.py:271
  5.3 20.5 %collective-permute-start.4 = (bf16[1,64,2048]{2,1,0:T(8,128)(2,1)S(1)}, bf16[1,64,2048]{2,1,0:T(8,128)(2,1)}, u32[]{:S(2)}, u32[]{:S(2)}) collective-permute-start(bf16[1,64,2048]{2,1,0:T(8,128)(2,1)S(1)} %copy-done.7), channel_id=1, source_target_pairs={{0,8},{4,12},{8,0},{12,4},{1,9},{5,13},{9,1},{13,5},{2,10},{6,14},... | collective-permute-start | bytes 786440 | tf_op jit(solution)/shard_map/ppermute | solution.py:274
  7.9 18.0 %collective-permute-start.5 = (bf16[1,64,2048]{2,1,0:T(8,128)(2,1)S(1)}, bf16[1,64,2048]{2,1,0:T(8,128)(2,1)S(1)}, u32[]{:S(2)}, u32[]{:S(2)}) collective-permute-start(bf16[1,64,2048]{2,1,0:T(8,128)(2,1)S(1)} %copy-done.7), channel_id=1, source_target_pairs={{0,4},{4,0},{8,12},{12,8},{1,5},{5,1},{9,13},{13,9},{2,6},{6,2},{1... | collective-permute-start | bytes 786440 | tf_op jit(solution)/shard_map/ppermute | solution.py:274
  26.6 3.7 %collective-permute-start.8 = (bf16[1,64,7168]{2,1,0:T(8,128)(2,1)S(1)}, bf16[1,64,7168]{2,1,0:T(8,128)(2,1)S(1)}, u32[]{:S(2)}, u32[]{:S(2)}) collective-permute-start(bf16[1,64,7168]{2,1,0:T(8,128)(2,1)S(1)} %collective-permute-done.3.refs_0_), channel_id=1, source_target_pairs={{0,1},{1,0},{2,3},{3,2},{4,5},{5,4},{6,7},{7,6},{8,9},{9,8},{10,11... | collective-permute-start | bytes 2752520 | tf_op jit(solution)/shard_map/ppermute | solution.py:268
  26.6 24.8 %copy-start.17 = (s32[4]{0:T(128)S(1)}, s32[4]{0:T(128)}, u32[]{:S(2)}) copy-start(s32[4]{0:T(128)} %param.11) | copy-start | bytes 52
  26.6 23.1 %collective-permute-start.2 = (bf16[1,64,7168]{2,1,0:T(8,128)(2,1)}, bf16[1,64,7168]{2,1,0:T(8,128)(2,1)}, u32[]{:S(2)}, u32[]{:S(2)}) collective-permute-start(bf16[1,64,7168]{2,1,0:T(8,128)(2,1)} %get-tuple-element.83), channel_id=1, source_target_pairs={{2,0},{0,2},{3,1},{1,3},{6,4},{4,6},{7,5},{5,7},{10,8},{8,10},{11,... | collective-permute-start | bytes 2752520 | tf_op jit(solution)/shard_map/ppermute | solution.py:271
  28.2 21.1 %collective-permute-start.7 = (bf16[128,2176]{1,0:T(8,128)(2,1)S(1)}, bf16[128,2176]{1,0:T(8,128)(2,1)S(1)}, u32[]{:S(2)}, u32[]{:S(2)}) collective-permute-start(bf16[128,2176]{1,0:T(8,128)(2,1)S(1)} %get-tuple-element.84), channel_id=1, source_target_pairs={{0,4},{4,0},{8,12},{12,8},{1,5},{5,1},{9,13},{13,9},{2,6},{6,2},{1... | collective-permute-start | bytes 1671176 | tf_op jit(solution)/shard_map/ppermute | solution.py:274
  29.8 18.8 %collective-permute-start.6 = (bf16[1,64,2048]{2,1,0:T(8,128)(2,1)}, bf16[1,64,2048]{2,1,0:T(8,128)(2,1)S(1)}, u32[]{:S(2)}, u32[]{:S(2)}) collective-permute-start(bf16[1,64,2048]{2,1,0:T(8,128)(2,1)} %collective-permute-done.4), channel_id=1, source_target_pairs={{0,4},{4,0},{8,12},{12,8},{1,5},{5,1},{9,13},{13,9},{2,6},{6,2},{1... | collective-permute-start | bytes 786440 | tf_op jit(solution)/shard_map/ppermute | solution.py:274
  49.7 5.6 %collective-permute-start.11 = (bf16[1,64,7168]{2,1,0:T(8,128)(2,1)}, bf16[1,64,7168]{2,1,0:T(8,128)(2,1)}, u32[]{:S(2)}, u32[]{:S(2)}) collective-permute-start(bf16[1,64,7168]{2,1,0:T(8,128)(2,1)} %collective-permute-done.2.refs_0_), channel_id=1, source_target_pairs={{0,1},{1,0},{2,3},{3,2},{4,5},{5,4},{6,7},{7,6},{8,9},{9,8},{10,11... | collective-permute-start | bytes 2752520 | tf_op jit(solution)/shard_map/ppermute | solution.py:268
  50.2 23.4 %collective-permute-start.1 = (bf16[1,64,7168]{2,1,0:T(8,128)(2,1)}, bf16[1,64,7168]{2,1,0:T(8,128)(2,1)S(1)}, u32[]{:S(2)}, u32[]{:S(2)}) collective-permute-start(bf16[1,64,7168]{2,1,0:T(8,128)(2,1)} %get-tuple-element.82), channel_id=1, source_target_pairs={{2,0},{0,2},{3,1},{1,3},{6,4},{4,6},{7,5},{5,7},{10,8},{8,10},{11,... | collective-permute-start | bytes 2752520 | tf_op jit(solution)/shard_map/ppermute | solution.py:271
  51.5 22.2 %collective-permute-start.9 = (bf16[64,2176]{1,0:T(8,128)(2,1)}, bf16[64,2176]{1,0:T(8,128)(2,1)}, u32[]{:S(2)}, u32[]{:S(2)}) collective-permute-start(bf16[64,2176]{1,0:T(8,128)(2,1)} %copy-done.14), channel_id=1, source_target_pairs={{0,4},{4,0},{8,12},{12,8},{1,5},{5,1},{9,13},{13,9},{2,6},{6,2},{1... | collective-permute-start | bytes 835592 | tf_op jit(solution)/shard_map/ppermute | solution.py:274
  53.0 20.6 %collective-permute-start.10 = (bf16[64,2176]{1,0:T(8,128)(2,1)}, bf16[64,2176]{1,0:T(8,128)(2,1)}, u32[]{:S(2)}, u32[]{:S(2)}) collective-permute-start(bf16[64,2176]{1,0:T(8,128)(2,1)} %copy-done.13), channel_id=1, source_target_pairs={{0,4},{4,0},{8,12},{12,8},{1,5},{5,1},{9,13},{13,9},{2,6},{6,2},{1... | collective-permute-start | bytes 835592 | tf_op jit(solution)/shard_map/ppermute | solution.py:274
  54.4 38.0 %collective-permute-start.14 = (bf16[1,64,7168]{2,1,0:T(8,128)(2,1)}, bf16[1,64,7168]{2,1,0:T(8,128)(2,1)S(1)}, u32[]{:S(2)}, u32[]{:S(2)}) collective-permute-start(bf16[1,64,7168]{2,1,0:T(8,128)(2,1)} %get-tuple-element.117), channel_id=1, source_target_pairs={{2,0},{0,2},{3,1},{1,3},{6,4},{4,6},{7,5},{5,7},{10,8},{8,10},{11,... | collective-permute-start | bytes 2752520 | tf_op jit(solution)/shard_map/ppermute | solution.py:271
  55.3 18.4 %copy-start.16 = (bf16[128,2176]{1,0:T(8,128)(2,1)S(1)}, bf16[128,2176]{1,0:T(8,128)(2,1)}, u32[]{:S(2)}) copy-start(bf16[128,2176]{1,0:T(8,128)(2,1)} %copy-done.15) | copy-start | bytes 1671172
  73.6 5.9 %collective-permute-start.12 = (bf16[1,64,7168]{2,1,0:T(8,128)(2,1)S(1)}, bf16[1,64,7168]{2,1,0:T(8,128)(2,1)S(1)}, u32[]{:S(2)}, u32[]{:S(2)}) collective-permute-start(bf16[1,64,7168]{2,1,0:T(8,128)(2,1)S(1)} %collective-permute-done.1.refs_0_), channel_id=1, source_target_pairs={{0,1},{1,0},{2,3},{3,2},{4,5},{5,4},{6,7},{7,6},{8,9},{9,8},{10,11... | collective-permute-start | bytes 2752520 | tf_op jit(solution)/shard_map/ppermute | solution.py:268
  73.7 18.6 %collective-permute-start.15 = (bf16[64,2176]{1,0:T(8,128)(2,1)S(1)}, bf16[64,2176]{1,0:T(8,128)(2,1)S(1)}, u32[]{:S(2)}, u32[]{:S(2)}) collective-permute-start(bf16[64,2176]{1,0:T(8,128)(2,1)S(1)} %get-tuple-element.123), channel_id=1, source_target_pairs={{0,4},{4,0},{8,12},{12,8},{1,5},{5,1},{9,13},{13,9},{2,6},{6,2},{1... | collective-permute-start | bytes 835592 | tf_op jit(solution)/shard_map/ppermute | solution.py:274
  75.4 19.4 %collective-permute-start.16 = (bf16[64,2176]{1,0:T(8,128)(2,1)S(1)}, bf16[64,2176]{1,0:T(8,128)(2,1)S(1)}, u32[]{:S(2)}, u32[]{:S(2)}) collective-permute-start(bf16[64,2176]{1,0:T(8,128)(2,1)S(1)} %get-tuple-element.124), channel_id=1, source_target_pairs={{0,4},{4,0},{8,12},{12,8},{1,5},{5,1},{9,13},{13,9},{2,6},{6,2},{1... | collective-permute-start | bytes 835592 | tf_op jit(solution)/shard_map/ppermute | solution.py:274
  76.9 19.1 %collective-permute-start.13 = (bf16[64,2176]{1,0:T(8,128)(2,1)S(1)}, bf16[64,2176]{1,0:T(8,128)(2,1)S(1)}, u32[]{:S(2)}, u32[]{:S(2)}) collective-permute-start(bf16[64,2176]{1,0:T(8,128)(2,1)S(1)} %select_convert_fusion.2), channel_id=1, source_target_pairs={{0,8},{4,12},{8,0},{12,4},{1,9},{5,13},{9,1},{13,5},{2,10},{6,14},... | collective-permute-start | bytes 835592 | tf_op jit(solution)/shard_map/ppermute | solution.py:278
  94.8 5.5 %collective-permute-start.17 = (bf16[1,64,7168]{2,1,0:T(8,128)(2,1)S(1)}, bf16[1,64,7168]{2,1,0:T(8,128)(2,1)S(1)}, u32[]{:S(2)}, u32[]{:S(2)}) collective-permute-start(bf16[1,64,7168]{2,1,0:T(8,128)(2,1)S(1)} %collective-permute-done.14.refs_0_), channel_id=1, source_target_pairs={{0,1},{1,0},{2,3},{3,2},{4,5},{5,4},{6,7},{7,6},{8,9},{9,8},{10,11... | collective-permute-start | bytes 2752520 | tf_op jit(solution)/shard_map/ppermute | solution.py:268
  96.0 15.0 %copy-start.5 = (bf16[64,2176]{1,0:T(8,128)(2,1)}, bf16[64,2176]{1,0:T(8,128)(2,1)S(1)}, u32[]{:S(2)}) copy-start(bf16[64,2176]{1,0:T(8,128)(2,1)S(1)} %collective-permute-done.13.refs_5_) | copy-start | bytes 835588
  96.0 17.3 %collective-permute-start.18 = (bf16[64,2176]{1,0:T(8,128)(2,1)S(1)}, bf16[64,2176]{1,0:T(8,128)(2,1)S(1)}, u32[]{:S(2)}, u32[]{:S(2)}) collective-permute-start(bf16[64,2176]{1,0:T(8,128)(2,1)S(1)} %select_convert_fusion.1), channel_id=1, source_target_pairs={{0,8},{4,12},{8,0},{12,4},{1,9},{5,13},{9,1},{13,5},{2,10},{6,14},... | collective-permute-start | bytes 835592 | tf_op jit(solution)/shard_map/ppermute | solution.py:278
  97.8 14.4 %collective-permute-start.19 = (bf16[64,2176]{1,0:T(8,128)(2,1)S(1)}, bf16[64,2176]{1,0:T(8,128)(2,1)S(1)}, u32[]{:S(2)}, u32[]{:S(2)}) collective-permute-start(bf16[64,2176]{1,0:T(8,128)(2,1)S(1)} %get-tuple-element.137), channel_id=1, source_target_pairs={{0,4},{4,0},{8,12},{12,8},{1,5},{5,1},{9,13},{13,9},{2,6},{6,2},{1... | collective-permute-start | bytes 835592 | tf_op jit(solution)/shard_map/ppermute | solution.py:274
  113.3 8.3 %collective-permute-start.21 = (f32[64,128]{1,0:T(8,128)S(1)}, f32[64,128]{1,0:T(8,128)S(1)}, u32[]{:S(2)}, u32[]{:S(2)}) collective-permute-start(f32[64,128]{1,0:T(8,128)S(1)} %get-tuple-element.145), channel_id=1, source_target_pairs={{0,4},{4,0},{8,12},{12,8},{1,5},{5,1},{9,13},{13,9},{2,6},{6,2},{1... | collective-permute-start | bytes 98312 | tf_op jit(solution)/shard_map/ppermute | solution.py:274
  114.0 13.9 %collective-permute-start.22 = (bf16[64,2048]{1,0:T(8,128)(2,1)S(1)}, bf16[64,2048]{1,0:T(8,128)(2,1)S(1)}, u32[]{:S(2)}, u32[]{:S(2)}) collective-permute-start(bf16[64,2048]{1,0:T(8,128)(2,1)S(1)} %get-tuple-element.150), channel_id=1, source_target_pairs={{0,4},{4,0},{8,12},{12,8},{1,5},{5,1},{9,13},{13,9},{2,6},{6,2},{1... | collective-permute-start | bytes 786440 | tf_op jit(solution)/shard_map/ppermute | solution.py:274
  115.4 21.5 %collective-permute-start.20 = (bf16[64,2176]{1,0:T(8,128)(2,1)S(1)}, bf16[64,2176]{1,0:T(8,128)(2,1)S(1)}, u32[]{:S(2)}, u32[]{:S(2)}) collective-permute-start(bf16[64,2176]{1,0:T(8,128)(2,1)S(1)} %get-tuple-element.141), channel_id=1, source_target_pairs={{0,8},{4,12},{8,0},{12,4},{1,9},{5,13},{9,1},{13,5},{2,10},{6,14},... | collective-permute-start | bytes 835592 | tf_op jit(solution)/shard_map/ppermute | solution.py:278
  121.7 15.2 %collective-permute-start.23 = (f32[64,128]{1,0:T(8,128)S(1)}, f32[64,128]{1,0:T(8,128)S(1)}, u32[]{:S(2)}, u32[]{:S(2)}) collective-permute-start(f32[64,128]{1,0:T(8,128)S(1)} %get-tuple-element.164), channel_id=1, source_target_pairs={{0,8},{4,12},{8,0},{12,4},{1,9},{5,13},{9,1},{13,5},{2,10},{6,14},... | collective-permute-start | bytes 98312 | tf_op jit(solution)/shard_map/ppermute | solution.py:278
  128.0 17.1 %collective-permute-start.27 = (bf16[64,2048]{1,0:T(8,128)(2,1)S(1)}, bf16[64,2048]{1,0:T(8,128)(2,1)S(1)}, u32[]{:S(2)}, u32[]{:S(2)}) collective-permute-start(bf16[64,2048]{1,0:T(8,128)(2,1)S(1)} %select_convert_fusion.3), channel_id=1, source_target_pairs={{0,8},{4,12},{8,0},{12,4},{1,9},{5,13},{9,1},{13,5},{2,10},{6,14},... | collective-permute-start | bytes 786440 | tf_op jit(solution)/shard_map/ppermute | solution.py:278
  137.1 4.6 %collective-permute-start.25 = (bf16[4,64,64]{2,1,0:T(8,128)(2,1)S(1)}, bf16[4,64,64]{2,1,0:T(8,128)(2,1)S(1)}, u32[]{:S(2)}, u32[]{:S(2)}) collective-permute-start(bf16[4,64,64]{2,1,0:T(8,128)(2,1)S(1)} %maximum_select_fusion), channel_id=1, source_target_pairs={{0,2},{1,3},{2,0},{3,1},{4,6},{5,7},{6,4},{7,5},{8,10},{9,11},{10,... | collective-permute-start | bytes 98312 | tf_op jit(solution)/shard_map/ppermute | solution.py:419
  138.2 3.5 %collective-permute-start.26 = (bf16[4,64,64]{2,1,0:T(8,128)(2,1)S(1)}, bf16[4,64,64]{2,1,0:T(8,128)(2,1)S(1)}, u32[]{:S(2)}, u32[]{:S(2)}) collective-permute-start(bf16[4,64,64]{2,1,0:T(8,128)(2,1)S(1)} %maximum_select_fusion), channel_id=1, source_target_pairs={{0,3},{1,0},{2,1},{3,2},{4,7},{5,4},{6,5},{7,6},{8,11},{9,8},{10,9... | collective-permute-start | bytes 98312 | tf_op jit(solution)/shard_map/ppermute | solution.py:419
  138.2 4.3 %collective-permute-start.24 = (bf16[4,64,64]{2,1,0:T(8,128)(2,1)S(1)}, bf16[4,64,64]{2,1,0:T(8,128)(2,1)S(1)}, u32[]{:S(2)}, u32[]{:S(2)}) collective-permute-start(bf16[4,64,64]{2,1,0:T(8,128)(2,1)S(1)} %maximum_select_fusion), channel_id=1, source_target_pairs={{0,1},{1,2},{2,3},{3,0},{4,5},{5,6},{6,7},{7,4},{8,9},{9,10},{10,1... | collective-permute-start | bytes 98312 | tf_op jit(solution)/shard_map/ppermute | solution.py:419
  (15 other events, 65.0 us)

commit v17 on v15

--- a/solution.py
+++ b/solution.py
@@ -325,7 +325,7 @@
             bit //= 2
         return total.reshape(steps, extent, columns)
 
-    def gap(token, jobs):
+    def gap(token, jobs, hold=False, lag=1):
         nonlocal first_leg, second_leg
         for parts, received, keep, kind in first_leg:
             steps = sum(length for _, length in parts)
@@ -336,9 +336,14 @@
                     if (key[0] + at - begin, key[1]) == (step_count - 1, 0):
                         halved[RANK_NAME, 0] = total[at][:, width:]
                 begin += length
-        closed = {name: (after(kept, token), *received) for name, kept, received in second_leg}
+        closed, waiting = {}, []
+        for name, kept, received, turns in second_leg:
+            if turns > 1:
+                waiting.append((name, kept, received, turns - 1))
+            else:
+                closed[name] = (after(kept, token), *received)
         started, sends = [], []
-        for name in sorted({name for name, _ in halved}):
+        for name in [] if hold else sorted({name for name, _ in halved}):
             if name in begun or name == RANK_NAME or any((name, at) not in halved for at in range(n_rep)):
                 continue
             begun.add(name)
@@ -356,8 +361,8 @@
         first_leg = [
             (parts, swap_tensor(send, group // 2), keep, kind) for (parts, _, keep, kind), send in zip(jobs, first_sends)
         ]
-        second_leg = [
-            (name, kept, [to_group(value, hop + 1) for hop, value in enumerate(sent)])
+        second_leg = waiting + [
+            (name, kept, [to_group(value, hop + 1) for hop, value in enumerate(sent)], lag)
             for (name, kept), sent in zip(started, sends)
         ]
         return sends
@@ -373,12 +378,14 @@
         remote.update({(step, shift): from_rep(rows, shift) for shift in range(1, n_rep)})
     jobs = [([((0, 0), lead)], send, keep, jnp.bfloat16)]
     for piece, (step, shift) in enumerate(pieces):
-        sends = gap(send, jobs)
+        sends = gap(send, jobs, hold=piece == len(pieces) - 1)
         own, panels, _ = lax.optimization_barrier((remote[step, shift], panels, send))
         if piece == 0:
             panels, order = panels + [swap_tensor(panels[1], bits[1])], order + [bits[0] ^ bits[1]]
             panels, order = spread_panels(panels, order, bits[2:])
         sib = swap_cores(own)
+        if piece == len(pieces) - 1:
+            sends = gap(send, [], lag=2)
         own, sib, siblings, _ = lax.optimization_barrier((own, sib, siblings, sends))
         last, chunks, keys = step == step_count - 1, [(own, sib, 0, 1)], [(step, shift)]
         if next_local < step_count:
@@ -391,12 +398,18 @@
         if last:
             last_ranks[shift] = outs[2 * count:]
     gap(send, jobs)
+    rank_received = {shift: swap_tensor(ranks[0], group // 2) for shift, ranks in last_ranks.items()}
     for shift, ranks in last_ranks.items():
-        halved[RANK_NAME, shift] = second_half(ranks[1], swap_tensor(ranks[0], group // 2), 1, jnp.float32)[0]
+        halved[RANK_NAME, shift] = second_half(ranks[1], rank_received[shift], 1, jnp.float32)[0]
     values = [halved[RANK_NAME, at] for at in range(n_rep)]
-    ended[RANK_NAME] = (pick(values, (group_index - rep_index) % n_rep), *[
-        to_group(pick(values, (group_index + hop - rep_index) % n_rep), hop) for hop in range(1, n_rep)
-    ])
+    rank_sends = [pick(values, (group_index + hop - rep_index) % n_rep) for hop in range(1, n_rep)]
+    ended[RANK_NAME] = (
+        pick(values, (group_index - rep_index) % n_rep),
+        *[to_group(value, hop + 1) for hop, value in enumerate(rank_sends)],
+    )
+    second_leg = [
+        (name, *after((kept, received), rank_sends), turns) for name, kept, received, turns in second_leg
+    ]
     rounded = gap(send, [])
 
     def rank_sum(name):
@@ -407,8 +420,8 @@
 
     finished = jnp.stack([rank_sum(step) for step in range(step_count - 1)] + [rank_sum(RANK_NAME)])
     finished = finished.astype(jnp.bfloat16).reshape(step_count, rows_mine, owned_slots, rank_size)
-    finished = lax.optimization_barrier((finished, rounded))[0]
-    ended.update((name, (kept, *received)) for name, kept, received in second_leg)
+    finished = after(finished, rounded)
+    ended.update((name, (kept, *received)) for name, kept, received, _ in second_leg)
     masked = jnp.sum(
         jnp.where(owned_hot[None, :, :, None], finished, 0), axis=2, dtype=jnp.float32
     ).astype(jnp.bfloat16)

time: 139 us -> 154 us (1.11)
  waiting for transfers between devices: 29.8 us -> 43.4 us
    ppermute x11, waiting for transfers between devices: 1.01 us -> 22.3 us  [swap_tensor(): return lax.ppermute(value, 'tp', [(i, i ^ bit) for i in range(n_tensor)])]
    ppermute x4, waiting for transfers between devices: 9.48 us -> 6.14 us  [from_rep(): lax.ppermute(value, 'rep', [((i + shift) % n_rep, i) for i in range(n_rep)])]
    ppermute x5, waiting for transfers between devices: 15.6 us -> 12.5 us  [to_group(): lax.ppermute(value, 'tp', [(i, (i + moved) % n_tensor) for i in range(n_t...]
    unnamed x34 -> x30, local copies, waits for them, and re-layouts: 4.63 us -> 4.57 us
  transfers between devices with their start and end apart: 28 -> 28, of which waited for: 10 -> 11; matrix products, arithmetic and copies ran while one was open for 4% -> 3% of each run, Pallas kernels for 50% -> 45%
where the time goes in v17:
time: 154 us
  Pallas kernels  70 us (45%)
  waiting for transfers between devices  43.4 us (28%)
  starting transfers between devices  30.6 us (20%)
  local copies, waits for them, and re-layouts  7.65 us (5%)
  other arithmetic  2.34 us (2%)
    pallas_call x5, Pallas kernels, partial_products(): pl.pallas_call(functools.partial(matmul_body, spans, staged, apart), in_s...  66.7 us
    ppermute x11, waiting for transfers between devices, swap_tensor(): return lax.ppermute(value, 'tp', [(i, i ^ bit) for i in range(n_tensor)])  22.3 us
    ppermute x11, starting transfers between devices, swap_tensor(): return lax.ppermute(value, 'tp', [(i, i ^ bit) for i in range(n_tensor)])  15.3 us
    ppermute x5, waiting for transfers between devices, to_group(): lax.ppermute(value, 'tp', [(i, (i + moved) % n_tensor) for i in range(n_t...  12.5 us
    ppermute x5, starting transfers between devices, to_group(): lax.ppermute(value, 'tp', [(i, (i + moved) % n_tensor) for i in range(n_t...  8.45 us
    ppermute x4, waiting for transfers between devices, from_rep(): lax.ppermute(value, 'rep', [((i + shift) % n_rep, i) for i in range(n_rep)])  6.14 us
    ppermute x4, starting transfers between devices, from_rep(): lax.ppermute(value, 'rep', [((i + shift) % n_rep, i) for i in range(n_rep)])  4.57 us
    unnamed x30, local copies, waits for them, and re-layouts  4.57 us
  transfers between devices with their start and end apart: 28, of which 11 were waited for; matrix products, arithmetic and copies ran while one was open for 3% of the time, Pallas kernels for 45%

profile of v17, /device:TPU:0, one launch (start us, length us, event | category | flops | bytes accessed | tf_op | source)
XLA Modules:
  0.0 154.3 jit_solution(8807779703019028746)
XLA Ops:
  0.5 2.2 %slice.51 = bf16[1,64,7168]{2,1,0:T(8,128)(2,1)} slice(bf16[4,64,7168]{2,1,0:T(8,128)(2,1)} %refs_2_.7), slice={[0:1], [0:64], [0:7168]} | slice | bytes 1835008 | tf_op jit(solution)/shard_map/slice | solution.py:293
  2.7 2.6 %collective-permute-start.3 = (bf16[1,64,7168]{2,1,0:T(8,128)(2,1)}, bf16[1,64,7168]{2,1,0:T(8,128)(2,1)S(1)}, u32[]{:S(2)}, u32[]{:S(2)}) collective-permute-start(bf16[1,64,7168]{2,1,0:T(8,128)(2,1)} %slice.51), channel_id=1, source_target_pairs={{2,0},{0,2},{3,1},{1,3},{6,4},{4,6},{7,5},{5,7},{10,8},{8,10},{11,... | collective-permute-start | bytes 2752520 | tf_op jit(solution)/shard_map/ppermute | solution.py:271
  5.3 2.6 %collective-permute-start.4 = (bf16[1,64,2048]{2,1,0:T(8,128)(2,1)S(1)}, bf16[1,64,2048]{2,1,0:T(8,128)(2,1)}, u32[]{:S(2)}, u32[]{:S(2)}) collective-permute-start(bf16[1,64,2048]{2,1,0:T(8,128)(2,1)S(1)} %copy-done.5), channel_id=1, source_target_pairs={{0,8},{4,12},{8,0},{12,4},{1,9},{5,13},{9,1},{13,5},{2,10},{6,14},... | collective-permute-start | bytes 786440 | tf_op jit(solution)/shard_map/ppermute | solution.py:274
  7.9 1.6 %collective-permute-start.5 = (bf16[1,64,2048]{2,1,0:T(8,128)(2,1)S(1)}, bf16[1,64,2048]{2,1,0:T(8,128)(2,1)S(1)}, u32[]{:S(2)}, u32[]{:S(2)}) collective-permute-start(bf16[1,64,2048]{2,1,0:T(8,128)(2,1)S(1)} %copy-done.5), channel_id=1, source_target_pairs={{0,4},{4,0},{8,12},{12,8},{1,5},{5,1},{9,13},{13,9},{2,6},{6,2},{1... | collective-permute-start | bytes 786440 | tf_op jit(solution)/shard_map/ppermute | solution.py:274
  9.5 16.4 %partial_products.5 = (bf16[128,2176]{1,0:T(8,128)(2,1)S(1)}, f32[128,2176]{1,0:T(8,128)S(1)}, bf16[1,64,7168]{2,1,0:T(8,128)(2,1)}, bf16[1,64,7168]{2,1,0:T(8,128)(2,1)}, bf16[1,64,7168]{2,1,0:T(8,128)(2,1)}) custom-call(s32[1]{0:T(128)} %bitcast.1.pos_ref, bf16[4,64,7168]{2,1,0:T(8,128)(2,1)} %refs_2_.7, ...), custom_call_target="tpu_custom_call" | custom-call | tf_op jit(solution)/shard_map/partial_products/pallas_call | solution.py:145
  25.9 0.9 copy-done.11
  28.2 1.6 %collective-permute-start.6 = (bf16[1,64,2048]{2,1,0:T(8,128)(2,1)}, bf16[1,64,2048]{2,1,0:T(8,128)(2,1)S(1)}, u32[]{:S(2)}, u32[]{:S(2)}) collective-permute-start(bf16[1,64,2048]{2,1,0:T(8,128)(2,1)} %collective-permute-done.4), channel_id=1, source_target_pairs={{0,4},{4,0},{8,12},{12,8},{1,5},{5,1},{9,13},{13,9},{2,6},{6,2},{1... | collective-permute-start | bytes 786440 | tf_op jit(solution)/shard_map/ppermute | solution.py:274
  30.0 13.4 %partial_products.6 = (bf16[64,2176]{1,0:T(8,128)(2,1)S(1)}, bf16[64,2176]{1,0:T(8,128)(2,1)S(1)}, f32[64,2176]{1,0:T(8,128)S(1)}, f32[64,2176]{1,0:T(8,128)S(1)}) custom-call(s32[1]{0:T(128)} %bitcast.1.pos_ref, bf16[1,64,7168]{2,1,0:T(8,128)(2,1)S(1)} %collective-permute-done.3.refs_0_, bf16[1,64,7168]{2,1,0:T(8,128)(2,1)S(1)} %collective-permute-done.7.refs_1_, ...), custom_call_target="tpu_custom_call" | custom-call | tf_op jit(solution)/shard_map/partial_products/pallas_call | solution.py:145
  46.4 4.2 %collective-permute-done.2.refs_0_ = bf16[1,64,7168]{2,1,0:T(8,128)(2,1)} collective-permute-done((bf16[1,64,7168]{2,1,0:T(8,128)(2,1)}, bf16[1,64,7168]{2,1,0:T(8,128)(2,1)}, u32[]{:S(2)}, u32[]{:S(2)}) %collective-permute-start.2) | collective-permute-done | bytes 917536 | tf_op jit(solution)/shard_map/ppermute | solution.py:271
  51.3 1.6 %collective-permute-start.11 = (bf16[128,2176]{1,0:T(8,128)(2,1)}, bf16[128,2176]{1,0:T(8,128)(2,1)}, u32[]{:S(2)}, u32[]{:S(2)}) collective-permute-start(bf16[128,2176]{1,0:T(8,128)(2,1)} %copy-done.11), channel_id=1, source_target_pairs={{0,4},{4,0},{8,12},{12,8},{1,5},{5,1},{9,13},{13,9},{2,6},{6,2},{1... | collective-permute-start | bytes 1671176 | tf_op jit(solution)/shard_map/ppermute | solution.py:274
  54.5 1.2 collective-permute-start.10
  56.5 15.5 %partial_products.7 = (bf16[64,2176]{1,0:T(8,128)(2,1)S(1)}, bf16[64,2176]{1,0:T(8,128)(2,1)S(1)}, f32[64,2176]{1,0:T(8,128)S(1)}, f32[64,2176]{1,0:T(8,128)S(1)}) custom-call(s32[1]{0:T(128)} %bitcast.1.pos_ref, bf16[1,64,7168]{2,1,0:T(8,128)(2,1)} %collective-permute-done.2.refs_0_, bf16[1,64,7168]{2,1,0:T(8,128)(2,1)} %collective-permute-done.8.refs_1_, ...), custom_call_target="tpu_custom_call" | custom-call | tf_op jit(solution)/shard_map/partial_products/pallas_call | solution.py:145
  72.0 2.0 %collective-permute-done.1.refs_0_ = bf16[1,64,7168]{2,1,0:T(8,128)(2,1)S(1)} collective-permute-done((bf16[1,64,7168]{2,1,0:T(8,128)(2,1)}, bf16[1,64,7168]{2,1,0:T(8,128)(2,1)S(1)}, u32[]{:S(2)}, u32[]{:S(2)}) %collective-permute-start.1) | collective-permute-done | bytes 917536 | tf_op jit(solution)/shard_map/ppermute | solution.py:271
  73.9 1.2 convert_add_fusion
  75.1 0.9 collective-permute-start.13
  76.1 2.7 %collective-permute-start.12 = (bf16[64,2176]{1,0:T(8,128)(2,1)S(1)}, bf16[64,2176]{1,0:T(8,128)(2,1)S(1)}, u32[]{:S(2)}, u32[]{:S(2)}) collective-permute-start(bf16[64,2176]{1,0:T(8,128)(2,1)S(1)} %select_convert_fusion.2), channel_id=1, source_target_pairs={{0,8},{4,12},{8,0},{12,4},{1,9},{5,13},{9,1},{13,5},{2,10},{6,14},... | collective-permute-start | bytes 835592 | tf_op jit(solution)/shard_map/ppermute | solution.py:278
  79.2 10.7 %partial_products.8 = (bf16[64,2176]{1,0:T(8,128)(2,1)S(1)}, f32[64,2176]{1,0:T(8,128)S(1)}) custom-call(s32[1]{0:T(128)} %bitcast.1.pos_ref, bf16[1,64,7168]{2,1,0:T(8,128)(2,1)S(1)} %collective-permute-done.1.refs_0_, bf16[1,64,7168]{2,1,0:T(8,128)(2,1)S(1)} %collective-permute-done.9.refs_1_, bf16[7168,2048]{1,0:T(8,128)(2,1)} %refs_2_.9, ...), custom_call_target="tpu_custom_call" | custom-call | tf_op jit(solution)/shard_map/partial_products/pallas_call | solution.py:145
  90.8 2.5 %collective-permute-start.14 = (bf16[64,2176]{1,0:T(8,128)(2,1)S(1)}, bf16[64,2176]{1,0:T(8,128)(2,1)S(1)}, u32[]{:S(2)}, u32[]{:S(2)}) collective-permute-start(bf16[64,2176]{1,0:T(8,128)(2,1)S(1)} %get-tuple-element.125), channel_id=1, source_target_pairs={{0,4},{4,0},{8,12},{12,8},{1,5},{5,1},{9,13},{13,9},{2,6},{6,2},{1... | collective-permute-start | bytes 835592 | tf_op jit(solution)/shard_map/ppermute | solution.py:274
  93.4 8.7 %collective-permute-done.14 = bf16[64,2176]{1,0:T(8,128)(2,1)S(1)} collective-permute-done((bf16[64,2176]{1,0:T(8,128)(2,1)S(1)}, bf16[64,2176]{1,0:T(8,128)(2,1)S(1)}, u32[]{:S(2)}, u32[]{:S(2)}) %collective-permute-start.14) | collective-permute-done | bytes 278560 | tf_op jit(solution)/shard_map/ppermute | solution.py:274
  102.3 2.6 %collective-permute-start.16 = (bf16[64,2176]{1,0:T(8,128)(2,1)S(1)}, bf16[64,2176]{1,0:T(8,128)(2,1)S(1)}, u32[]{:S(2)}, u32[]{:S(2)}) collective-permute-start(bf16[64,2176]{1,0:T(8,128)(2,1)S(1)} %select_convert_fusion.1), channel_id=1, source_target_pairs={{0,8},{4,12},{8,0},{12,4},{1,9},{5,13},{9,1},{13,5},{2,10},{6,14},... | collective-permute-start | bytes 835592 | tf_op jit(solution)/shard_map/ppermute | solution.py:278
  105.3 10.7 %partial_products.9 = (bf16[64,2048]{1,0:T(8,128)(2,1)S(1)}, f32[64,2048]{1,0:T(8,128)S(1)}, f32[64,128]{1,0:T(8,128)S(1)}, f32[64,128]{1,0:T(8,128)S(1)}) custom-call(s32[1]{0:T(128)} %bitcast.1.pos_ref, bf16[1,64,7168]{2,1,0:T(8,128)(2,1)S(1)} %collective-permute-done.17.refs_0_, bf16[1,64,7168]{2,1,0:T(8,128)(2,1)S(1)} %collective-permute-done.18.refs_1_, ...), custom_call_target="tpu_custom_call" | custom-call | tf_op jit(solution)/shard_map/partial_products/pallas_call | solution.py:145
  116.0 1.6 %collective-permute-start.19 = (f32[64,128]{1,0:T(8,128)S(1)}, f32[64,128]{1,0:T(8,128)S(1)}, u32[]{:S(2)}, u32[]{:S(2)}) collective-permute-start(f32[64,128]{1,0:T(8,128)S(1)} %get-tuple-element.140), channel_id=1, source_target_pairs={{0,4},{4,0},{8,12},{12,8},{1,5},{5,1},{9,13},{13,9},{2,6},{6,2},{1... | collective-permute-start | bytes 98312 | tf_op jit(solution)/shard_map/ppermute | solution.py:274
  118.2 12.0 %collective-permute-done.19 = f32[64,128]{1,0:T(8,128)S(1)} collective-permute-done((f32[64,128]{1,0:T(8,128)S(1)}, f32[64,128]{1,0:T(8,128)S(1)}, u32[]{:S(2)}, u32[]{:S(2)}) %collective-permute-start.19) | collective-permute-done | bytes 32800 | tf_op jit(solution)/shard_map/ppermute | solution.py:274
  130.2 1.3 collective-permute-start.22
  131.6 3.6 %collective-permute-done.22 = f32[64,128]{1,0:T(8,128)S(1)} collective-permute-done((f32[64,128]{1,0:T(8,128)S(1)}, f32[64,128]{1,0:T(8,128)S(1)}, u32[]{:S(2)}, u32[]{:S(2)}) %collective-permute-start.22) | collective-permute-done | bytes 32800 | tf_op jit(solution)/shard_map/ppermute | solution.py:278
  135.3 0.9 collective-permute-done.23
  136.3 1.2 collective-permute-start.25
  138.1 1.5 collective-permute-start.27
  139.7 1.1 collective-permute-done.25
  140.8 1.1 collective-permute-done.24
  142.0 2.5 %finish_steps.1 = (bf16[4,64,2048]{2,1,0:T(8,128)(2,1)}, bf16[64,2048]{1,0:T(8,128)(2,1)S(1)}) custom-call(bf16[256,64]{1,0:T(8,128)(2,1)S(1)} %bitcast.30, s32[256,1]{1,0:T(8,128)S(1)} %copy-done.4, s32[4]{0:T(128)S(1)} %pad_add_fusion.order_ref, bf16[64,2048]{1,0:T(8,128)(2,1)S(1)} %bitcast.31, bf16[64,2048]{1,0:T(8,128)(2,1)} %bitcast.14.refs_1_, ...), custom_call_target="tpu_custom_call" | custom-call | tf_op jit(solution)/shard_map/finish_steps/pallas_call | solution.py:203
  144.6 8.9 %collective-permute-done.27.refs_1_ = bf16[64,2048]{1,0:T(8,128)(2,1)S(1)} collective-permute-done((bf16[64,2048]{1,0:T(8,128)(2,1)S(1)}, bf16[64,2048]{1,0:T(8,128)(2,1)S(1)}, u32[]{:S(2)}, u32[]{:S(2)}) %collective-permute-start.27) | collective-permute-done | bytes 262176 | tf_op jit(solution)/shard_map/ppermute | solution.py:278
  (89 shorter events, 12.8 us)
Async XLA Ops:
  0.0 52.9 %copy-start = (s32[256,1]{0,1:T(1,128)S(1)}, s32[256,1]{0,1:T(1,128)}, u32[]{:S(2)}) copy-start(s32[256,1]{0,1:T(1,128)} %param.10) | copy-start | bytes 3076
  0.0 9.5 %copy-start.1 = (bf16[1,7168,64]{1,2,0:T(8,128)(2,1)S(1)}, bf16[1,7168,64]{1,2,0:T(8,128)(2,1)}, u32[]{:S(2)}) copy-start(bf16[1,7168,64]{1,2,0:T(8,128)(2,1)} %param.8) | copy-start | bytes 2752516
  0.0 9.5 %collective-permute-start = (bf16[4,64,7168]{2,1,0:T(8,128)(2,1)}, bf16[4,64,7168]{2,1,0:T(8,128)(2,1)}, u32[]{:S(2)}, u32[]{:S(2)}) collective-permute-start(bf16[4,64,7168]{2,1,0:T(8,128)(2,1)} %refs_2_.7), channel_id=1, source_target_pairs={{0,1},{1,0},{2,3},{3,2},{4,5},{5,4},{6,7},{7,6},{8,9},{9,8},{10,11... | collective-permute-start | bytes 11010056 | tf_op jit(solution)/shard_map/ppermute | solution.py:268
  2.7 24.8 %collective-permute-start.3 = (bf16[1,64,7168]{2,1,0:T(8,128)(2,1)}, bf16[1,64,7168]{2,1,0:T(8,128)(2,1)S(1)}, u32[]{:S(2)}, u32[]{:S(2)}) collective-permute-start(bf16[1,64,7168]{2,1,0:T(8,128)(2,1)} %slice.51), channel_id=1, source_target_pairs={{2,0},{0,2},{3,1},{1,3},{6,4},{4,6},{7,5},{5,7},{10,8},{8,10},{11,... | collective-permute-start | bytes 2752520 | tf_op jit(solution)/shard_map/ppermute | solution.py:271
  5.3 21.5 %collective-permute-start.4 = (bf16[1,64,2048]{2,1,0:T(8,128)(2,1)S(1)}, bf16[1,64,2048]{2,1,0:T(8,128)(2,1)}, u32[]{:S(2)}, u32[]{:S(2)}) collective-permute-start(bf16[1,64,2048]{2,1,0:T(8,128)(2,1)S(1)} %copy-done.5), channel_id=1, source_target_pairs={{0,8},{4,12},{8,0},{12,4},{1,9},{5,13},{9,1},{13,5},{2,10},{6,14},... | collective-permute-start | bytes 786440 | tf_op jit(solution)/shard_map/ppermute | solution.py:274
  7.9 18.9 %collective-permute-start.5 = (bf16[1,64,2048]{2,1,0:T(8,128)(2,1)S(1)}, bf16[1,64,2048]{2,1,0:T(8,128)(2,1)S(1)}, u32[]{:S(2)}, u32[]{:S(2)}) collective-permute-start(bf16[1,64,2048]{2,1,0:T(8,128)(2,1)S(1)} %copy-done.5), channel_id=1, source_target_pairs={{0,4},{4,0},{8,12},{12,8},{1,5},{5,1},{9,13},{13,9},{2,6},{6,2},{1... | collective-permute-start | bytes 786440 | tf_op jit(solution)/shard_map/ppermute | solution.py:274
  27.5 2.5 %collective-permute-start.7 = (bf16[1,64,7168]{2,1,0:T(8,128)(2,1)S(1)}, bf16[1,64,7168]{2,1,0:T(8,128)(2,1)S(1)}, u32[]{:S(2)}, u32[]{:S(2)}) collective-permute-start(bf16[1,64,7168]{2,1,0:T(8,128)(2,1)S(1)} %collective-permute-done.3.refs_0_), channel_id=1, source_target_pairs={{0,1},{1,0},{2,3},{3,2},{4,5},{5,4},{6,7},{7,6},{8,9},{9,8},{10,11... | collective-permute-start | bytes 2752520 | tf_op jit(solution)/shard_map/ppermute | solution.py:268
  27.5 25.5 %copy-start.14 = (s32[4]{0:T(128)S(1)}, s32[4]{0:T(128)}, u32[]{:S(2)}) copy-start(s32[4]{0:T(128)} %param.11) | copy-start | bytes 52
  27.5 23.1 %collective-permute-start.2 = (bf16[1,64,7168]{2,1,0:T(8,128)(2,1)}, bf16[1,64,7168]{2,1,0:T(8,128)(2,1)}, u32[]{:S(2)}, u32[]{:S(2)}) collective-permute-start(bf16[1,64,7168]{2,1,0:T(8,128)(2,1)} %get-tuple-element.86), channel_id=1, source_target_pairs={{2,0},{0,2},{3,1},{1,3},{6,4},{4,6},{7,5},{5,7},{10,8},{8,10},{11,... | collective-permute-start | bytes 2752520 | tf_op jit(solution)/shard_map/ppermute | solution.py:271
  28.2 17.5 %collective-permute-start.6 = (bf16[1,64,2048]{2,1,0:T(8,128)(2,1)}, bf16[1,64,2048]{2,1,0:T(8,128)(2,1)S(1)}, u32[]{:S(2)}, u32[]{:S(2)}) collective-permute-start(bf16[1,64,2048]{2,1,0:T(8,128)(2,1)} %collective-permute-done.4), channel_id=1, source_target_pairs={{0,4},{4,0},{8,12},{12,8},{1,5},{5,1},{9,13},{13,9},{2,6},{6,2},{1... | collective-permute-start | bytes 786440 | tf_op jit(solution)/shard_map/ppermute | solution.py:274
  50.6 5.1 %collective-permute-start.8 = (bf16[1,64,7168]{2,1,0:T(8,128)(2,1)}, bf16[1,64,7168]{2,1,0:T(8,128)(2,1)}, u32[]{:S(2)}, u32[]{:S(2)}) collective-permute-start(bf16[1,64,7168]{2,1,0:T(8,128)(2,1)} %collective-permute-done.2.refs_0_), channel_id=1, source_target_pairs={{0,1},{1,0},{2,3},{3,2},{4,5},{5,4},{6,7},{7,6},{8,9},{9,8},{10,11... | collective-permute-start | bytes 2752520 | tf_op jit(solution)/shard_map/ppermute | solution.py:268
  50.6 23.4 %collective-permute-start.1 = (bf16[1,64,7168]{2,1,0:T(8,128)(2,1)}, bf16[1,64,7168]{2,1,0:T(8,128)(2,1)S(1)}, u32[]{:S(2)}, u32[]{:S(2)}) collective-permute-start(bf16[1,64,7168]{2,1,0:T(8,128)(2,1)} %get-tuple-element.85), channel_id=1, source_target_pairs={{2,0},{0,2},{3,1},{1,3},{6,4},{4,6},{7,5},{5,7},{10,8},{8,10},{11,... | collective-permute-start | bytes 2752520 | tf_op jit(solution)/shard_map/ppermute | solution.py:271
  51.3 22.6 %collective-permute-start.11 = (bf16[128,2176]{1,0:T(8,128)(2,1)}, bf16[128,2176]{1,0:T(8,128)(2,1)}, u32[]{:S(2)}, u32[]{:S(2)}) collective-permute-start(bf16[128,2176]{1,0:T(8,128)(2,1)} %copy-done.11), channel_id=1, source_target_pairs={{0,4},{4,0},{8,12},{12,8},{1,5},{5,1},{9,13},{13,9},{2,6},{6,2},{1... | collective-permute-start | bytes 1671176 | tf_op jit(solution)/shard_map/ppermute | solution.py:274
  53.9 39.4 %collective-permute-start.17 = (bf16[1,64,7168]{2,1,0:T(8,128)(2,1)}, bf16[1,64,7168]{2,1,0:T(8,128)(2,1)S(1)}, u32[]{:S(2)}, u32[]{:S(2)}) collective-permute-start(bf16[1,64,7168]{2,1,0:T(8,128)(2,1)} %get-tuple-element.130), channel_id=1, source_target_pairs={{2,0},{0,2},{3,1},{1,3},{6,4},{4,6},{7,5},{5,7},{10,8},{8,10},{11,... | collective-permute-start | bytes 2752520 | tf_op jit(solution)/shard_map/ppermute | solution.py:271
  54.5 21.5 %collective-permute-start.10 = (bf16[64,2176]{1,0:T(8,128)(2,1)}, bf16[64,2176]{1,0:T(8,128)(2,1)S(1)}, u32[]{:S(2)}, u32[]{:S(2)}) collective-permute-start(bf16[64,2176]{1,0:T(8,128)(2,1)} %copy-done.13), channel_id=1, source_target_pairs={{0,4},{4,0},{8,12},{12,8},{1,5},{5,1},{9,13},{13,9},{2,6},{6,2},{1... | collective-permute-start | bytes 835592 | tf_op jit(solution)/shard_map/ppermute | solution.py:274
  55.7 37.7 %collective-permute-start.15 = (bf16[64,2176]{1,0:T(8,128)(2,1)}, bf16[64,2176]{1,0:T(8,128)(2,1)S(1)}, u32[]{:S(2)}, u32[]{:S(2)}) collective-permute-start(bf16[64,2176]{1,0:T(8,128)(2,1)} %copy-done.12), channel_id=1, source_target_pairs={{0,4},{4,0},{8,12},{12,8},{1,5},{5,1},{9,13},{13,9},{2,6},{6,2},{1... | collective-permute-start | bytes 835592 | tf_op jit(solution)/shard_map/ppermute | solution.py:274
  73.9 4.8 %collective-permute-start.9 = (bf16[1,64,7168]{2,1,0:T(8,128)(2,1)S(1)}, bf16[1,64,7168]{2,1,0:T(8,128)(2,1)S(1)}, u32[]{:S(2)}, u32[]{:S(2)}) collective-permute-start(bf16[1,64,7168]{2,1,0:T(8,128)(2,1)S(1)} %collective-permute-done.1.refs_0_), channel_id=1, source_target_pairs={{0,1},{1,0},{2,3},{3,2},{4,5},{5,4},{6,7},{7,6},{8,9},{9,8},{10,11... | collective-permute-start | bytes 2752520 | tf_op jit(solution)/shard_map/ppermute | solution.py:268
  75.1 15.5 %collective-permute-start.13 = (bf16[64,2176]{1,0:T(8,128)(2,1)S(1)}, bf16[64,2176]{1,0:T(8,128)(2,1)S(1)}, u32[]{:S(2)}, u32[]{:S(2)}) collective-permute-start(bf16[64,2176]{1,0:T(8,128)(2,1)S(1)} %get-tuple-element.122), channel_id=1, source_target_pairs={{0,4},{4,0},{8,12},{12,8},{1,5},{5,1},{9,13},{13,9},{2,6},{6,2},{1... | collective-permute-start | bytes 835592 | tf_op jit(solution)/shard_map/ppermute | solution.py:274
  76.1 14.7 %collective-permute-start.12 = (bf16[64,2176]{1,0:T(8,128)(2,1)S(1)}, bf16[64,2176]{1,0:T(8,128)(2,1)S(1)}, u32[]{:S(2)}, u32[]{:S(2)}) collective-permute-start(bf16[64,2176]{1,0:T(8,128)(2,1)S(1)} %select_convert_fusion.2), channel_id=1, source_target_pairs={{0,8},{4,12},{8,0},{12,4},{1,9},{5,13},{9,1},{13,5},{2,10},{6,14},... | collective-permute-start | bytes 835592 | tf_op jit(solution)/shard_map/ppermute | solution.py:278
  78.7 38.8 %collective-permute-start.20 = (bf16[64,2176]{1,0:T(8,128)(2,1)S(1)}, bf16[64,2176]{1,0:T(8,128)(2,1)S(1)}, u32[]{:S(2)}, u32[]{:S(2)}) collective-permute-start(bf16[64,2176]{1,0:T(8,128)(2,1)S(1)} %get-tuple-element.143), channel_id=1, source_target_pairs={{0,4},{4,0},{8,12},{12,8},{1,5},{5,1},{9,13},{13,9},{2,6},{6,2},{1... | collective-permute-start | bytes 835592 | tf_op jit(solution)/shard_map/ppermute | solution.py:274
  90.8 11.4 %copy-start.3 = (f32[64,2176]{1,0:T(8,128)S(1)}, f32[64,2176]{1,0:T(8,128)}, u32[]{:S(2)}) copy-start(f32[64,2176]{1,0:T(8,128)} %copy-done.2) | copy-start | bytes 1671172
  90.8 11.4 %collective-permute-start.14 = (bf16[64,2176]{1,0:T(8,128)(2,1)S(1)}, bf16[64,2176]{1,0:T(8,128)(2,1)S(1)}, u32[]{:S(2)}, u32[]{:S(2)}) collective-permute-start(bf16[64,2176]{1,0:T(8,128)(2,1)S(1)} %get-tuple-element.125), channel_id=1, source_target_pairs={{0,4},{4,0},{8,12},{12,8},{1,5},{5,1},{9,13},{13,9},{2,6},{6,2},{1... | collective-permute-start | bytes 835592 | tf_op jit(solution)/shard_map/ppermute | solution.py:274
  93.3 12.0 %collective-permute-start.18 = (bf16[1,64,7168]{2,1,0:T(8,128)(2,1)S(1)}, bf16[1,64,7168]{2,1,0:T(8,128)(2,1)S(1)}, u32[]{:S(2)}, u32[]{:S(2)}) collective-permute-start(bf16[1,64,7168]{2,1,0:T(8,128)(2,1)S(1)} %collective-permute-done.17.refs_0_), channel_id=1, source_target_pairs={{0,1},{1,0},{2,3},{3,2},{4,5},{5,4},{6,7},{7,6},{8,9},{9,8},{10,11... | collective-permute-start | bytes 2752520 | tf_op jit(solution)/shard_map/ppermute | solution.py:268
  102.3 29.2 %collective-permute-start.16 = (bf16[64,2176]{1,0:T(8,128)(2,1)S(1)}, bf16[64,2176]{1,0:T(8,128)(2,1)S(1)}, u32[]{:S(2)}, u32[]{:S(2)}) collective-permute-start(bf16[64,2176]{1,0:T(8,128)(2,1)S(1)} %select_convert_fusion.1), channel_id=1, source_target_pairs={{0,8},{4,12},{8,0},{12,4},{1,9},{5,13},{9,1},{13,5},{2,10},{6,14},... | collective-permute-start | bytes 835592 | tf_op jit(solution)/shard_map/ppermute | solution.py:278
  104.9 26.7 %collective-permute-start.21 = (bf16[64,2176]{1,0:T(8,128)(2,1)S(1)}, bf16[64,2176]{1,0:T(8,128)(2,1)S(1)}, u32[]{:S(2)}, u32[]{:S(2)}) collective-permute-start(bf16[64,2176]{1,0:T(8,128)(2,1)S(1)} %get-tuple-element.136), channel_id=1, source_target_pairs={{0,8},{4,12},{8,0},{12,4},{1,9},{5,13},{9,1},{13,5},{2,10},{6,14},... | collective-permute-start | bytes 835592 | tf_op jit(solution)/shard_map/ppermute | solution.py:278
  116.0 14.2 %collective-permute-start.19 = (f32[64,128]{1,0:T(8,128)S(1)}, f32[64,128]{1,0:T(8,128)S(1)}, u32[]{:S(2)}, u32[]{:S(2)}) collective-permute-start(f32[64,128]{1,0:T(8,128)S(1)} %get-tuple-element.140), channel_id=1, source_target_pairs={{0,4},{4,0},{8,12},{12,8},{1,5},{5,1},{9,13},{13,9},{2,6},{6,2},{1... | collective-permute-start | bytes 98312 | tf_op jit(solution)/shard_map/ppermute | solution.py:274
  117.7 18.5 %collective-permute-start.23 = (bf16[64,2048]{1,0:T(8,128)(2,1)S(1)}, bf16[64,2048]{1,0:T(8,128)(2,1)S(1)}, u32[]{:S(2)}, u32[]{:S(2)}) collective-permute-start(bf16[64,2048]{1,0:T(8,128)(2,1)S(1)} %get-tuple-element.145), channel_id=1, source_target_pairs={{0,4},{4,0},{8,12},{12,8},{1,5},{5,1},{9,13},{13,9},{2,6},{6,2},{1... | collective-permute-start | bytes 786440 | tf_op jit(solution)/shard_map/ppermute | solution.py:274
  130.2 5.0 %collective-permute-start.22 = (f32[64,128]{1,0:T(8,128)S(1)}, f32[64,128]{1,0:T(8,128)S(1)}, u32[]{:S(2)}, u32[]{:S(2)}) collective-permute-start(f32[64,128]{1,0:T(8,128)S(1)} %get-tuple-element.165), channel_id=1, source_target_pairs={{0,8},{4,12},{8,0},{12,4},{1,9},{5,13},{9,1},{13,5},{2,10},{6,14},... | collective-permute-start | bytes 98312 | tf_op jit(solution)/shard_map/ppermute | solution.py:278
  136.3 4.5 %collective-permute-start.25 = (bf16[4,64,64]{2,1,0:T(8,128)(2,1)S(1)}, bf16[4,64,64]{2,1,0:T(8,128)(2,1)S(1)}, u32[]{:S(2)}, u32[]{:S(2)}) collective-permute-start(bf16[4,64,64]{2,1,0:T(8,128)(2,1)S(1)} %select_bitcast_fusion), channel_id=1, source_target_pairs={{0,2},{1,3},{2,0},{3,1},{4,6},{5,7},{6,4},{7,5},{8,10},{9,11},{10,... | collective-permute-start | bytes 98312 | tf_op jit(solution)/shard_map/ppermute | solution.py:430
  137.6 3.3 %collective-permute-start.26 = (bf16[4,64,64]{2,1,0:T(8,128)(2,1)S(1)}, bf16[4,64,64]{2,1,0:T(8,128)(2,1)S(1)}, u32[]{:S(2)}, u32[]{:S(2)}) collective-permute-start(bf16[4,64,64]{2,1,0:T(8,128)(2,1)S(1)} %select_bitcast_fusion), channel_id=1, source_target_pairs={{0,3},{1,0},{2,1},{3,2},{4,7},{5,4},{6,5},{7,6},{8,11},{9,8},{10,9... | collective-permute-start | bytes 98312 | tf_op jit(solution)/shard_map/ppermute | solution.py:430
  137.6 4.3 %collective-permute-start.24 = (bf16[4,64,64]{2,1,0:T(8,128)(2,1)S(1)}, bf16[4,64,64]{2,1,0:T(8,128)(2,1)S(1)}, u32[]{:S(2)}, u32[]{:S(2)}) collective-permute-start(bf16[4,64,64]{2,1,0:T(8,128)(2,1)S(1)} %select_bitcast_fusion), channel_id=1, source_target_pairs={{0,1},{1,2},{2,3},{3,0},{4,5},{5,6},{6,7},{7,4},{8,9},{9,10},{10,1... | collective-permute-start | bytes 98312 | tf_op jit(solution)/shard_map/ppermute | solution.py:430
  138.1 15.4 %collective-permute-start.27 = (bf16[64,2048]{1,0:T(8,128)(2,1)S(1)}, bf16[64,2048]{1,0:T(8,128)(2,1)S(1)}, u32[]{:S(2)}, u32[]{:S(2)}) collective-permute-start(bf16[64,2048]{1,0:T(8,128)(2,1)S(1)} %select_convert_fusion.3), channel_id=1, source_target_pairs={{0,8},{4,12},{8,0},{12,4},{1,9},{5,13},{9,1},{13,5},{2,10},{6,14},... | collective-permute-start | bytes 786440 | tf_op jit(solution)/shard_map/ppermute | solution.py:278
  (11 other events, 32.6 us)

commit v18 on v15

--- a/solution.py
+++ b/solution.py
@@ -325,9 +325,10 @@
             bit //= 2
         return total.reshape(steps, extent, columns)
 
-    def gap(token, jobs):
+    def gap(token, jobs, short=False):
         nonlocal first_leg, second_leg
-        for parts, received, keep, kind in first_leg:
+        due, kept_back = (first_leg[:1], first_leg[1:]) if short else (first_leg, [])
+        for parts, received, keep, kind in due:
             steps = sum(length for _, length in parts)
             total, begin = second_half(after(keep, token), received, steps, kind), 0
             for key, length in parts:
@@ -336,7 +337,8 @@
                     if (key[0] + at - begin, key[1]) == (step_count - 1, 0):
                         halved[RANK_NAME, 0] = total[at][:, width:]
                 begin += length
-        closed = {name: (after(kept, token), *received) for name, kept, received in second_leg}
+        waiting = second_leg if short else []
+        closed = {name: (after(kept, token), *received) for name, kept, received in ([] if short else second_leg)}
         started, sends = [], []
         for name in sorted({name for name, _ in halved}):
             if name in begun or name == RANK_NAME or any((name, at) not in halved for at in range(n_rep)):
@@ -353,10 +355,10 @@
         sends, token = lax.optimization_barrier((sends, token))
         first_sends, closed = lax.optimization_barrier(([job[1] for job in jobs], closed))
         ended.update(closed)
-        first_leg = [
+        first_leg = kept_back + [
             (parts, swap_tensor(send, group // 2), keep, kind) for (parts, _, keep, kind), send in zip(jobs, first_sends)
         ]
-        second_leg = [
+        second_leg = waiting + [
             (name, kept, [to_group(value, hop + 1) for hop, value in enumerate(sent)])
             for (name, kept), sent in zip(started, sends)
         ]
@@ -373,12 +375,15 @@
         remote.update({(step, shift): from_rep(rows, shift) for shift in range(1, n_rep)})
     jobs = [([((0, 0), lead)], send, keep, jnp.bfloat16)]
     for piece, (step, shift) in enumerate(pieces):
+        arrived = [received for _, received, _, _ in first_leg] if piece > 0 else []
         sends = gap(send, jobs)
-        own, panels, _ = lax.optimization_barrier((remote[step, shift], panels, send))
+        own, panels, *_ = lax.optimization_barrier((remote[step, shift], panels, arrived, send))
         if piece == 0:
             panels, order = panels + [swap_tensor(panels[1], bits[1])], order + [bits[0] ^ bits[1]]
             panels, order = spread_panels(panels, order, bits[2:])
         sib = swap_cores(own)
+        if piece > 0:
+            sends = sends + gap(send, [], short=True)
         own, sib, siblings, _ = lax.optimization_barrier((own, sib, siblings, sends))
         last, chunks, keys = step == step_count - 1, [(own, sib, 0, 1)], [(step, shift)]
         if next_local < step_count:

time: 139 us -> 150 us (1.079)
  waiting for transfers between devices: 29.8 us -> 34.9 us
  other arithmetic: 2.21 us -> 6.4 us
  local copies, waits for them, and re-layouts: 7.73 us -> 5.16 us
  starting transfers between devices: 29.2 us -> 31.5 us
    ppermute x11, waiting for transfers between devices: 1.01 us -> 20.9 us  [swap_tensor(): return lax.ppermute(value, 'tp', [(i, i ^ bit) for i in range(n_tensor)])]
    ppermute x4, waiting for transfers between devices: 9.48 us -> 0.01 us  [from_rep(): lax.ppermute(value, 'rep', [((i + shift) % n_rep, i) for i in range(n_rep)])]
    ppermute x5, waiting for transfers between devices: 15.6 us -> 11.5 us  [to_group(): lax.ppermute(value, 'tp', [(i, (i + moved) % n_tensor) for i in range(n_t...]
    unnamed x34 -> x38, local copies, waits for them, and re-layouts: 4.63 us -> 2.26 us
    select_n x3 -> x5, other arithmetic: 0.23 us -> 2.48 us  [pick(): value = jnp.where(index == at, values[at], value)]
    ppermute x11, starting transfers between devices: 14.1 us -> 16.1 us  [swap_tensor(): return lax.ppermute(value, 'tp', [(i, i ^ bit) for i in range(n_tensor)])]
  transfers between devices with their start and end apart: 28 -> 28, of which waited for: 10 -> 9; matrix products, arithmetic and copies ran while one was open for 4% -> 6% of each run, Pallas kernels for 50% -> 47%
where the time goes in v18:
time: 150 us; the launch traced here: 149 us
  Pallas kernels  70.9 us (47%)
  waiting for transfers between devices  34.9 us (23%)
  starting transfers between devices  31.5 us (21%)
  other arithmetic  6.4 us (4%)
  local copies, waits for them, and re-layouts  5.16 us (3%)
    pallas_call x5, Pallas kernels, partial_products(): pl.pallas_call(functools.partial(matmul_body, spans, staged, apart), in_s...  67.3 us
    ppermute x11, waiting for transfers between devices, swap_tensor(): return lax.ppermute(value, 'tp', [(i, i ^ bit) for i in range(n_tensor)])  20.9 us
    ppermute x11, starting transfers between devices, swap_tensor(): return lax.ppermute(value, 'tp', [(i, i ^ bit) for i in range(n_tensor)])  16.1 us
    ppermute x5, waiting for transfers between devices, to_group(): lax.ppermute(value, 'tp', [(i, (i + moved) % n_tensor) for i in range(n_t...  11.5 us
    ppermute x5, starting transfers between devices, to_group(): lax.ppermute(value, 'tp', [(i, (i + moved) % n_tensor) for i in range(n_t...  7.84 us
    ppermute x4, starting transfers between devices, from_rep(): lax.ppermute(value, 'rep', [((i + shift) % n_rep, i) for i in range(n_rep)])  5.33 us
  transfers between devices with their start and end apart: 28, of which 9 were waited for; matrix products, arithmetic and copies ran while one was open for 6% of the time, Pallas kernels for 47%

profile of v18, /device:TPU:0, one launch (start us, length us, event | category | flops | bytes accessed | tf_op | source)
XLA Modules:
  0.0 149.3 jit_solution(10372535396100427303)
XLA Ops:
  0.5 1.2 slice.51
  1.8 2.7 %collective-permute-start.2 = (bf16[1,64,7168]{2,1,0:T(8,128)(2,1)S(1)}, bf16[1,64,7168]{2,1,0:T(8,128)(2,1)}, u32[]{:S(2)}, u32[]{:S(2)}) collective-permute-start(bf16[1,64,7168]{2,1,0:T(8,128)(2,1)S(1)} %slice.51), channel_id=1, source_target_pairs={{2,0},{0,2},{3,1},{1,3},{6,4},{4,6},{7,5},{5,7},{10,8},{8,10},{11,... | collective-permute-start | bytes 2752520 | tf_op jit(solution)/shard_map/ppermute | solution.py:271
  4.4 2.6 %collective-permute-start.3 = (bf16[1,64,2048]{2,1,0:T(8,128)(2,1)S(1)}, bf16[1,64,2048]{2,1,0:T(8,128)(2,1)}, u32[]{:S(2)}, u32[]{:S(2)}) collective-permute-start(bf16[1,64,2048]{2,1,0:T(8,128)(2,1)S(1)} %copy-done.11), channel_id=1, source_target_pairs={{0,8},{4,12},{8,0},{12,4},{1,9},{5,13},{9,1},{13,5},{2,10},{6,14},... | collective-permute-start | bytes 786440 | tf_op jit(solution)/shard_map/ppermute | solution.py:274
  7.0 1.6 %collective-permute-start.4 = (bf16[1,64,2048]{2,1,0:T(8,128)(2,1)S(1)}, bf16[1,64,2048]{2,1,0:T(8,128)(2,1)S(1)}, u32[]{:S(2)}, u32[]{:S(2)}) collective-permute-start(bf16[1,64,2048]{2,1,0:T(8,128)(2,1)S(1)} %copy-done.11), channel_id=1, source_target_pairs={{0,4},{4,0},{8,12},{12,8},{1,5},{5,1},{9,13},{13,9},{2,6},{6,2},{1... | collective-permute-start | bytes 786440 | tf_op jit(solution)/shard_map/ppermute | solution.py:274
  8.6 17.1 %partial_products.5 = (bf16[128,2176]{1,0:T(8,128)(2,1)}, f32[128,2176]{1,0:T(8,128)S(1)}, bf16[1,64,7168]{2,1,0:T(8,128)(2,1)}, bf16[1,64,7168]{2,1,0:T(8,128)(2,1)}, bf16[1,64,7168]{2,1,0:T(8,128)(2,1)}) custom-call(s32[1]{0:T(128)} %bitcast.1.pos_ref, bf16[4,64,7168]{2,1,0:T(8,128)(2,1)} %refs_2_.7, ...), custom_call_target="tpu_custom_call" | custom-call | tf_op jit(solution)/shard_map/partial_products/pallas_call | solution.py:145
  26.5 1.3 collective-permute-start.1
  27.8 1.6 %collective-permute-start.6 = (bf16[128,2176]{1,0:T(8,128)(2,1)}, bf16[128,2176]{1,0:T(8,128)(2,1)}, u32[]{:S(2)}, u32[]{:S(2)}) collective-permute-start(bf16[128,2176]{1,0:T(8,128)(2,1)} %get-tuple-element.83), channel_id=1, source_target_pairs={{0,4},{4,0},{8,12},{12,8},{1,5},{5,1},{9,13},{13,9},{2,6},{6,2},{1... | collective-permute-start | bytes 1671176 | tf_op jit(solution)/shard_map/ppermute | solution.py:274
  30.5 14.2 %partial_products.6 = (bf16[64,2176]{1,0:T(8,128)(2,1)S(1)}, bf16[64,2176]{1,0:T(8,128)(2,1)}, f32[64,2176]{1,0:T(8,128)S(1)}, f32[64,2176]{1,0:T(8,128)S(1)}) custom-call(s32[1]{0:T(128)} %bitcast.1.pos_ref, bf16[1,64,7168]{2,1,0:T(8,128)(2,1)} %collective-permute-done.2.refs_0_, bf16[1,64,7168]{2,1,0:T(8,128)(2,1)} %collective-permute-done.7.refs_1_, ...), custom_call_target="tpu_custom_call" | custom-call | tf_op jit(solution)/shard_map/partial_products/pallas_call | solution.py:145
  44.7 1.5 collective-permute-start.9
  46.2 3.0 %collective-permute-done.5 = bf16[1,64,2048]{2,1,0:T(8,128)(2,1)} collective-permute-done((bf16[1,64,2048]{2,1,0:T(8,128)(2,1)}, bf16[1,64,2048]{2,1,0:T(8,128)(2,1)}, u32[]{:S(2)}, u32[]{:S(2)}) %collective-permute-start.5) | collective-permute-done | bytes 262176 | tf_op jit(solution)/shard_map/ppermute | solution.py:274
  49.2 1.6 %collective-permute-start.12 = (bf16[64,2176]{1,0:T(8,128)(2,1)}, bf16[64,2176]{1,0:T(8,128)(2,1)}, u32[]{:S(2)}, u32[]{:S(2)}) collective-permute-start(bf16[64,2176]{1,0:T(8,128)(2,1)} %get-tuple-element.113), channel_id=1, source_target_pairs={{0,4},{4,0},{8,12},{12,8},{1,5},{5,1},{9,13},{13,9},{2,6},{6,2},{1... | collective-permute-start | bytes 835592 | tf_op jit(solution)/shard_map/ppermute | solution.py:274
  50.8 1.2 convert_add_fusion
  52.0 3.1 %collective-permute-done.9 = bf16[64,2176]{1,0:T(8,128)(2,1)S(1)} collective-permute-done((bf16[64,2176]{1,0:T(8,128)(2,1)S(1)}, bf16[64,2176]{1,0:T(8,128)(2,1)S(1)}, u32[]{:S(2)}, u32[]{:S(2)}) %collective-permute-start.9) | collective-permute-done | bytes 278560 | tf_op jit(solution)/shard_map/ppermute | solution.py:274
  55.1 2.7 %collective-permute-start.10 = (bf16[64,2176]{1,0:T(8,128)(2,1)S(1)}, bf16[64,2176]{1,0:T(8,128)(2,1)}, u32[]{:S(2)}, u32[]{:S(2)}) collective-permute-start(bf16[64,2176]{1,0:T(8,128)(2,1)S(1)} %select_convert_fusion.2), channel_id=1, source_target_pairs={{0,8},{4,12},{8,0},{12,4},{1,9},{5,13},{9,1},{13,5},{2,10},{6,14},... | collective-permute-start | bytes 835592 | tf_op jit(solution)/shard_map/ppermute | solution.py:278
  57.9 14.1 %partial_products.7 = (bf16[64,2176]{1,0:T(8,128)(2,1)}, bf16[64,2176]{1,0:T(8,128)(2,1)S(1)}, f32[64,2176]{1,0:T(8,128)S(1)}, f32[64,2176]{1,0:T(8,128)S(1)}) custom-call(s32[1]{0:T(128)} %bitcast.1.pos_ref, bf16[1,64,7168]{2,1,0:T(8,128)(2,1)} %collective-permute-done.1.refs_0_, bf16[1,64,7168]{2,1,0:T(8,128)(2,1)S(1)} %collective-permute-done.8.refs_1_, ...), custom_call_target="tpu_custom_call" | custom-call | tf_op jit(solution)/shard_map/partial_products/pallas_call | solution.py:145
  72.7 1.6 %collective-permute-start.14 = (bf16[64,2176]{1,0:T(8,128)(2,1)}, bf16[64,2176]{1,0:T(8,128)(2,1)}, u32[]{:S(2)}, u32[]{:S(2)}) collective-permute-start(bf16[64,2176]{1,0:T(8,128)(2,1)} %get-tuple-element.117), channel_id=1, source_target_pairs={{0,4},{4,0},{8,12},{12,8},{1,5},{5,1},{9,13},{13,9},{2,6},{6,2},{1... | collective-permute-start | bytes 835592 | tf_op jit(solution)/shard_map/ppermute | solution.py:274
  75.6 8.9 %collective-permute-done.14 = bf16[64,2176]{1,0:T(8,128)(2,1)} collective-permute-done((bf16[64,2176]{1,0:T(8,128)(2,1)}, bf16[64,2176]{1,0:T(8,128)(2,1)}, u32[]{:S(2)}, u32[]{:S(2)}) %collective-permute-start.14) | collective-permute-done | bytes 278560 | tf_op jit(solution)/shard_map/ppermute | solution.py:274
  84.4 1.2 select_convert_fusion.1
  87.3 11.4 %partial_products.8 = (bf16[64,2176]{1,0:T(8,128)(2,1)}, f32[64,2176]{1,0:T(8,128)S(1)}) custom-call(s32[1]{0:T(128)} %bitcast.1.pos_ref, bf16[1,64,7168]{2,1,0:T(8,128)(2,1)S(1)} %collective-permute-done.11.refs_0_, bf16[1,64,7168]{2,1,0:T(8,128)(2,1)S(1)} %collective-permute-done.13.refs_1_, bf16[7168,2048]{1,0:T(8,128)(2,1)} %refs_2_.9, ...), custom_call_target="tpu_custom_call" | custom-call | tf_op jit(solution)/shard_map/partial_products/pallas_call | solution.py:145
  99.5 2.6 %collective-permute-start.19 = (bf16[64,2176]{1,0:T(8,128)(2,1)}, bf16[64,2176]{1,0:T(8,128)(2,1)S(1)}, u32[]{:S(2)}, u32[]{:S(2)}) collective-permute-start(bf16[64,2176]{1,0:T(8,128)(2,1)} %get-tuple-element.134), channel_id=1, source_target_pairs={{0,4},{4,0},{8,12},{12,8},{1,5},{5,1},{9,13},{13,9},{2,6},{6,2},{1... | collective-permute-start | bytes 835592 | tf_op jit(solution)/shard_map/ppermute | solution.py:274
  103.2 4.2 %collective-permute-done.19 = bf16[64,2176]{1,0:T(8,128)(2,1)S(1)} collective-permute-done((bf16[64,2176]{1,0:T(8,128)(2,1)}, bf16[64,2176]{1,0:T(8,128)(2,1)S(1)}, u32[]{:S(2)}, u32[]{:S(2)}) %collective-permute-start.19) | collective-permute-done | bytes 278560 | tf_op jit(solution)/shard_map/ppermute | solution.py:274
  107.4 1.3 fusion
  108.7 1.5 collective-permute-start.20
  111.9 10.5 %partial_products.9 = (bf16[64,2048]{1,0:T(8,128)(2,1)S(1)}, f32[64,2048]{1,0:T(8,128)S(1)}, f32[64,128]{1,0:T(8,128)S(1)}, f32[64,128]{1,0:T(8,128)S(1)}) custom-call(s32[1]{0:T(128)} %bitcast.1.pos_ref, bf16[1,64,7168]{2,1,0:T(8,128)(2,1)} %collective-permute-done.16.refs_0_, bf16[1,64,7168]{2,1,0:T(8,128)(2,1)S(1)} %collective-permute-done.18.refs_1_, ...), custom_call_target="tpu_custom_call" | custom-call | tf_op jit(solution)/shard_map/partial_products/pallas_call | solution.py:145
  124.7 1.8 %collective-permute-done.21 = f32[64,128]{1,0:T(8,128)S(1)} collective-permute-done((f32[64,128]{1,0:T(8,128)S(1)}, f32[64,128]{1,0:T(8,128)S(1)}, u32[]{:S(2)}, u32[]{:S(2)}) %collective-permute-start.21) | collective-permute-done | bytes 32800 | tf_op jit(solution)/shard_map/ppermute | solution.py:274
  126.4 1.9 %collective-permute-start.22 = (f32[64,128]{1,0:T(8,128)S(1)}, f32[64,128]{1,0:T(8,128)S(1)}, u32[]{:S(2)}, u32[]{:S(2)}) collective-permute-start(f32[64,128]{1,0:T(8,128)S(1)} %get-tuple-element.159), channel_id=1, source_target_pairs={{0,8},{4,12},{8,0},{12,4},{1,9},{5,13},{9,1},{13,5},{2,10},{6,14},... | collective-permute-start | bytes 98312 | tf_op jit(solution)/shard_map/ppermute | solution.py:278
  128.4 2.9 %collective-permute-done.22 = f32[64,128]{1,0:T(8,128)S(1)} collective-permute-done((f32[64,128]{1,0:T(8,128)S(1)}, f32[64,128]{1,0:T(8,128)S(1)}, u32[]{:S(2)}, u32[]{:S(2)}) %collective-permute-start.22) | collective-permute-done | bytes 32800 | tf_op jit(solution)/shard_map/ppermute | solution.py:278
  131.6 1.2 collective-permute-start.25
  133.2 1.2 collective-permute-start.27
  134.5 1.6 %collective-permute-done.25 = bf16[4,64,64]{2,1,0:T(8,128)(2,1)S(1)} collective-permute-done((bf16[4,64,64]{2,1,0:T(8,128)(2,1)S(1)}, bf16[4,64,64]{2,1,0:T(8,128)(2,1)S(1)}, u32[]{:S(2)}, u32[]{:S(2)}) %collective-permute-start.25) | collective-permute-done | bytes 32800 | tf_op jit(solution)/shard_map/ppermute | solution.py:422
  137.2 2.8 %finish_steps.1 = (bf16[4,64,2048]{2,1,0:T(8,128)(2,1)}, bf16[64,2048]{1,0:T(8,128)(2,1)S(1)}) custom-call(bf16[256,64]{1,0:T(8,128)(2,1)S(1)} %bitcast.30, s32[256,1]{1,0:T(8,128)S(1)} %reshape.112.slot_ref, s32[4]{0:T(128)S(1)} %pad_add_fusion.order_ref, bf16[64,2048]{1,0:T(8,128)(2,1)S(1)} %bitcast.31, bf16[64,2048]{1,0:T(8,128)(2,1)} %bitcast.14.refs_1_, ...), custom_call_target="tpu_custom_call" | custom-call | tf_op jit(solution)/shard_map/finish_steps/pallas_call | solution.py:203
  140.0 8.5 %collective-permute-done.27.refs_1_ = bf16[64,2048]{1,0:T(8,128)(2,1)S(1)} collective-permute-done((bf16[64,2048]{1,0:T(8,128)(2,1)S(1)}, bf16[64,2048]{1,0:T(8,128)(2,1)S(1)}, u32[]{:S(2)}, u32[]{:S(2)}) %collective-permute-start.27) | collective-permute-done | bytes 262176 | tf_op jit(solution)/shard_map/ppermute | solution.py:278
  (100 shorter events, 14.5 us)
Async XLA Ops:
  0.0 74.3 %copy-start = (s32[256,1]{0,1:T(1,128)S(1)}, s32[256,1]{0,1:T(1,128)}, u32[]{:S(2)}) copy-start(s32[256,1]{0,1:T(1,128)} %param.10) | copy-start | bytes 3076
  0.0 8.6 %collective-permute-start = (bf16[4,64,7168]{2,1,0:T(8,128)(2,1)}, bf16[4,64,7168]{2,1,0:T(8,128)(2,1)}, u32[]{:S(2)}, u32[]{:S(2)}) collective-permute-start(bf16[4,64,7168]{2,1,0:T(8,128)(2,1)} %refs_2_.7), channel_id=1, source_target_pairs={{0,1},{1,0},{2,3},{3,2},{4,5},{5,4},{6,7},{7,6},{8,9},{9,8},{10,11... | collective-permute-start | bytes 11010056 | tf_op jit(solution)/shard_map/ppermute | solution.py:268
  1.8 24.7 %collective-permute-start.2 = (bf16[1,64,7168]{2,1,0:T(8,128)(2,1)S(1)}, bf16[1,64,7168]{2,1,0:T(8,128)(2,1)}, u32[]{:S(2)}, u32[]{:S(2)}) collective-permute-start(bf16[1,64,7168]{2,1,0:T(8,128)(2,1)S(1)} %slice.51), channel_id=1, source_target_pairs={{2,0},{0,2},{3,1},{1,3},{6,4},{4,6},{7,5},{5,7},{10,8},{8,10},{11,... | collective-permute-start | bytes 2752520 | tf_op jit(solution)/shard_map/ppermute | solution.py:271
  4.4 21.3 %collective-permute-start.3 = (bf16[1,64,2048]{2,1,0:T(8,128)(2,1)S(1)}, bf16[1,64,2048]{2,1,0:T(8,128)(2,1)}, u32[]{:S(2)}, u32[]{:S(2)}) collective-permute-start(bf16[1,64,2048]{2,1,0:T(8,128)(2,1)S(1)} %copy-done.11), channel_id=1, source_target_pairs={{0,8},{4,12},{8,0},{12,4},{1,9},{5,13},{9,1},{13,5},{2,10},{6,14},... | collective-permute-start | bytes 786440 | tf_op jit(solution)/shard_map/ppermute | solution.py:274
  7.0 18.7 %collective-permute-start.4 = (bf16[1,64,2048]{2,1,0:T(8,128)(2,1)S(1)}, bf16[1,64,2048]{2,1,0:T(8,128)(2,1)S(1)}, u32[]{:S(2)}, u32[]{:S(2)}) collective-permute-start(bf16[1,64,2048]{2,1,0:T(8,128)(2,1)S(1)} %copy-done.11), channel_id=1, source_target_pairs={{0,4},{4,0},{8,12},{12,8},{1,5},{5,1},{9,13},{13,9},{2,6},{6,2},{1... | collective-permute-start | bytes 786440 | tf_op jit(solution)/shard_map/ppermute | solution.py:274
  26.5 4.1 %collective-permute-start.7 = (bf16[1,64,7168]{2,1,0:T(8,128)(2,1)}, bf16[1,64,7168]{2,1,0:T(8,128)(2,1)}, u32[]{:S(2)}, u32[]{:S(2)}) collective-permute-start(bf16[1,64,7168]{2,1,0:T(8,128)(2,1)} %collective-permute-done.2.refs_0_), channel_id=1, source_target_pairs={{0,1},{1,0},{2,3},{3,2},{4,5},{5,4},{6,7},{7,6},{8,9},{9,8},{10,11... | collective-permute-start | bytes 2752520 | tf_op jit(solution)/shard_map/ppermute | solution.py:268
  26.5 24.3 %collective-permute-start.1 = (bf16[1,64,7168]{2,1,0:T(8,128)(2,1)}, bf16[1,64,7168]{2,1,0:T(8,128)(2,1)}, u32[]{:S(2)}, u32[]{:S(2)}) collective-permute-start(bf16[1,64,7168]{2,1,0:T(8,128)(2,1)} %get-tuple-element.82), channel_id=1, source_target_pairs={{2,0},{0,2},{3,1},{1,3},{6,4},{4,6},{7,5},{5,7},{10,8},{8,10},{11,... | collective-permute-start | bytes 2752520 | tf_op jit(solution)/shard_map/ppermute | solution.py:271
  27.8 23.0 %collective-permute-start.6 = (bf16[128,2176]{1,0:T(8,128)(2,1)}, bf16[128,2176]{1,0:T(8,128)(2,1)}, u32[]{:S(2)}, u32[]{:S(2)}) collective-permute-start(bf16[128,2176]{1,0:T(8,128)(2,1)} %get-tuple-element.83), channel_id=1, source_target_pairs={{0,4},{4,0},{8,12},{12,8},{1,5},{5,1},{9,13},{13,9},{2,6},{6,2},{1... | collective-permute-start | bytes 1671176 | tf_op jit(solution)/shard_map/ppermute | solution.py:274
  29.4 19.8 %collective-permute-start.5 = (bf16[1,64,2048]{2,1,0:T(8,128)(2,1)}, bf16[1,64,2048]{2,1,0:T(8,128)(2,1)}, u32[]{:S(2)}, u32[]{:S(2)}) collective-permute-start(bf16[1,64,2048]{2,1,0:T(8,128)(2,1)} %collective-permute-done.3), channel_id=1, source_target_pairs={{0,4},{4,0},{8,12},{12,8},{1,5},{5,1},{9,13},{13,9},{2,6},{6,2},{1... | collective-permute-start | bytes 786440 | tf_op jit(solution)/shard_map/ppermute | solution.py:274
  29.8 45.8 %collective-permute-start.11 = (bf16[1,64,7168]{2,1,0:T(8,128)(2,1)}, bf16[1,64,7168]{2,1,0:T(8,128)(2,1)S(1)}, u32[]{:S(2)}, u32[]{:S(2)}) collective-permute-start(bf16[1,64,7168]{2,1,0:T(8,128)(2,1)} %get-tuple-element.108), channel_id=1, source_target_pairs={{2,0},{0,2},{3,1},{1,3},{6,4},{4,6},{7,5},{5,7},{10,8},{8,10},{11,... | collective-permute-start | bytes 2752520 | tf_op jit(solution)/shard_map/ppermute | solution.py:271
  44.7 10.3 %collective-permute-start.9 = (bf16[64,2176]{1,0:T(8,128)(2,1)S(1)}, bf16[64,2176]{1,0:T(8,128)(2,1)S(1)}, u32[]{:S(2)}, u32[]{:S(2)}) collective-permute-start(bf16[64,2176]{1,0:T(8,128)(2,1)S(1)} %get-tuple-element.96), channel_id=1, source_target_pairs={{0,4},{4,0},{8,12},{12,8},{1,5},{5,1},{9,13},{13,9},{2,6},{6,2},{1... | collective-permute-start | bytes 835592 | tf_op jit(solution)/shard_map/ppermute | solution.py:274
  49.2 26.4 %collective-permute-start.12 = (bf16[64,2176]{1,0:T(8,128)(2,1)}, bf16[64,2176]{1,0:T(8,128)(2,1)}, u32[]{:S(2)}, u32[]{:S(2)}) collective-permute-start(bf16[64,2176]{1,0:T(8,128)(2,1)} %get-tuple-element.113), channel_id=1, source_target_pairs={{0,4},{4,0},{8,12},{12,8},{1,5},{5,1},{9,13},{13,9},{2,6},{6,2},{1... | collective-permute-start | bytes 835592 | tf_op jit(solution)/shard_map/ppermute | solution.py:274
  50.8 7.1 %collective-permute-start.8 = (bf16[1,64,7168]{2,1,0:T(8,128)(2,1)}, bf16[1,64,7168]{2,1,0:T(8,128)(2,1)S(1)}, u32[]{:S(2)}, u32[]{:S(2)}) collective-permute-start(bf16[1,64,7168]{2,1,0:T(8,128)(2,1)} %collective-permute-done.1.refs_0_), channel_id=1, source_target_pairs={{0,1},{1,0},{2,3},{3,2},{4,5},{5,4},{6,7},{7,6},{8,9},{9,8},{10,11... | collective-permute-start | bytes 2752520 | tf_op jit(solution)/shard_map/ppermute | solution.py:268
  55.1 17.6 %collective-permute-start.10 = (bf16[64,2176]{1,0:T(8,128)(2,1)S(1)}, bf16[64,2176]{1,0:T(8,128)(2,1)}, u32[]{:S(2)}, u32[]{:S(2)}) collective-permute-start(bf16[64,2176]{1,0:T(8,128)(2,1)S(1)} %select_convert_fusion.2), channel_id=1, source_target_pairs={{0,8},{4,12},{8,0},{12,4},{1,9},{5,13},{9,1},{13,5},{2,10},{6,14},... | collective-permute-start | bytes 835592 | tf_op jit(solution)/shard_map/ppermute | solution.py:278
  57.9 45.2 %copy-start.2 = (f32[64,2176]{1,0:T(8,128)}, f32[64,2176]{1,0:T(8,128)S(1)}, u32[]{:S(2)}) copy-start(f32[64,2176]{1,0:T(8,128)S(1)} %slice_select_fusion.1.refs_4_) | copy-start | bytes 1671172
  72.7 11.7 %collective-permute-start.14 = (bf16[64,2176]{1,0:T(8,128)(2,1)}, bf16[64,2176]{1,0:T(8,128)(2,1)}, u32[]{:S(2)}, u32[]{:S(2)}) collective-permute-start(bf16[64,2176]{1,0:T(8,128)(2,1)} %get-tuple-element.117), channel_id=1, source_target_pairs={{0,4},{4,0},{8,12},{12,8},{1,5},{5,1},{9,13},{13,9},{2,6},{6,2},{1... | collective-permute-start | bytes 835592 | tf_op jit(solution)/shard_map/ppermute | solution.py:274
  74.5 28.6 %collective-permute-start.16 = (bf16[1,64,7168]{2,1,0:T(8,128)(2,1)}, bf16[1,64,7168]{2,1,0:T(8,128)(2,1)}, u32[]{:S(2)}, u32[]{:S(2)}) collective-permute-start(bf16[1,64,7168]{2,1,0:T(8,128)(2,1)} %get-tuple-element.125), channel_id=1, source_target_pairs={{2,0},{0,2},{3,1},{1,3},{6,4},{4,6},{7,5},{5,7},{10,8},{8,10},{11,... | collective-permute-start | bytes 2752520 | tf_op jit(solution)/shard_map/ppermute | solution.py:271
  75.1 28.0 %collective-permute-start.17 = (bf16[64,2176]{1,0:T(8,128)(2,1)}, bf16[64,2176]{1,0:T(8,128)(2,1)}, u32[]{:S(2)}, u32[]{:S(2)}) collective-permute-start(bf16[64,2176]{1,0:T(8,128)(2,1)} %copy-done.15), channel_id=1, source_target_pairs={{0,4},{4,0},{8,12},{12,8},{1,5},{5,1},{9,13},{13,9},{2,6},{6,2},{1... | collective-permute-start | bytes 835592 | tf_op jit(solution)/shard_map/ppermute | solution.py:274
  75.6 11.7 %collective-permute-start.13 = (bf16[1,64,7168]{2,1,0:T(8,128)(2,1)S(1)}, bf16[1,64,7168]{2,1,0:T(8,128)(2,1)S(1)}, u32[]{:S(2)}, u32[]{:S(2)}) collective-permute-start(bf16[1,64,7168]{2,1,0:T(8,128)(2,1)S(1)} %collective-permute-done.11.refs_0_), channel_id=1, source_target_pairs={{0,1},{1,0},{2,3},{3,2},{4,5},{5,4},{6,7},{7,6},{8,9},{9,8},{10,11... | collective-permute-start | bytes 2752520 | tf_op jit(solution)/shard_map/ppermute | solution.py:268
  85.7 13.8 %collective-permute-start.15 = (bf16[64,2176]{1,0:T(8,128)(2,1)S(1)}, bf16[64,2176]{1,0:T(8,128)(2,1)}, u32[]{:S(2)}, u32[]{:S(2)}) collective-permute-start(bf16[64,2176]{1,0:T(8,128)(2,1)S(1)} %select_convert_fusion.1), channel_id=1, source_target_pairs={{0,8},{4,12},{8,0},{12,4},{1,9},{5,13},{9,1},{13,5},{2,10},{6,14},... | collective-permute-start | bytes 835592 | tf_op jit(solution)/shard_map/ppermute | solution.py:278
  87.3 24.7 %copy-start.4 = (f32[64,2176]{1,0:T(8,128)}, f32[64,2176]{1,0:T(8,128)S(1)}, u32[]{:S(2)}) copy-start(f32[64,2176]{1,0:T(8,128)S(1)} %slice_select_fusion.refs_6_) | copy-start | bytes 1671172
  87.3 20.1 %copy-start.7 = (f32[64,2176]{1,0:T(8,128)S(1)}, f32[64,2176]{1,0:T(8,128)}, u32[]{:S(2)}) copy-start(f32[64,2176]{1,0:T(8,128)} %copy-done.6) | copy-start | bytes 1671172
  99.5 7.9 %collective-permute-start.19 = (bf16[64,2176]{1,0:T(8,128)(2,1)}, bf16[64,2176]{1,0:T(8,128)(2,1)S(1)}, u32[]{:S(2)}, u32[]{:S(2)}) collective-permute-start(bf16[64,2176]{1,0:T(8,128)(2,1)} %get-tuple-element.134), channel_id=1, source_target_pairs={{0,4},{4,0},{8,12},{12,8},{1,5},{5,1},{9,13},{13,9},{2,6},{6,2},{1... | collective-permute-start | bytes 835592 | tf_op jit(solution)/shard_map/ppermute | solution.py:274
  103.1 8.8 %collective-permute-start.18 = (bf16[1,64,7168]{2,1,0:T(8,128)(2,1)}, bf16[1,64,7168]{2,1,0:T(8,128)(2,1)S(1)}, u32[]{:S(2)}, u32[]{:S(2)}) collective-permute-start(bf16[1,64,7168]{2,1,0:T(8,128)(2,1)} %collective-permute-done.16.refs_0_), channel_id=1, source_target_pairs={{0,1},{1,0},{2,3},{3,2},{4,5},{5,4},{6,7},{7,6},{8,9},{9,8},{10,11... | collective-permute-start | bytes 2752520 | tf_op jit(solution)/shard_map/ppermute | solution.py:268
  108.7 14.8 %collective-permute-start.20 = (bf16[64,2176]{1,0:T(8,128)(2,1)S(1)}, bf16[64,2176]{1,0:T(8,128)(2,1)S(1)}, u32[]{:S(2)}, u32[]{:S(2)}) collective-permute-start(bf16[64,2176]{1,0:T(8,128)(2,1)S(1)} %get-tuple-element.137), channel_id=1, source_target_pairs={{0,8},{4,12},{8,0},{12,4},{1,9},{5,13},{9,1},{13,5},{2,10},{6,14},... | collective-permute-start | bytes 835592 | tf_op jit(solution)/shard_map/ppermute | solution.py:278
  122.4 4.0 %collective-permute-start.21 = (f32[64,128]{1,0:T(8,128)S(1)}, f32[64,128]{1,0:T(8,128)S(1)}, u32[]{:S(2)}, u32[]{:S(2)}) collective-permute-start(f32[64,128]{1,0:T(8,128)S(1)} %get-tuple-element.145), channel_id=1, source_target_pairs={{0,4},{4,0},{8,12},{12,8},{1,5},{5,1},{9,13},{13,9},{2,6},{6,2},{1... | collective-permute-start | bytes 98312 | tf_op jit(solution)/shard_map/ppermute | solution.py:274
  123.5 7.8 %collective-permute-start.23 = (bf16[64,2048]{1,0:T(8,128)(2,1)S(1)}, bf16[64,2048]{1,0:T(8,128)(2,1)S(1)}, u32[]{:S(2)}, u32[]{:S(2)}) collective-permute-start(bf16[64,2048]{1,0:T(8,128)(2,1)S(1)} %get-tuple-element.150), channel_id=1, source_target_pairs={{0,4},{4,0},{8,12},{12,8},{1,5},{5,1},{9,13},{13,9},{2,6},{6,2},{1... | collective-permute-start | bytes 786440 | tf_op jit(solution)/shard_map/ppermute | solution.py:274
  126.4 4.9 %collective-permute-start.22 = (f32[64,128]{1,0:T(8,128)S(1)}, f32[64,128]{1,0:T(8,128)S(1)}, u32[]{:S(2)}, u32[]{:S(2)}) collective-permute-start(f32[64,128]{1,0:T(8,128)S(1)} %get-tuple-element.159), channel_id=1, source_target_pairs={{0,8},{4,12},{8,0},{12,4},{1,9},{5,13},{9,1},{13,5},{2,10},{6,14},... | collective-permute-start | bytes 98312 | tf_op jit(solution)/shard_map/ppermute | solution.py:278
  131.6 4.6 %collective-permute-start.25 = (bf16[4,64,64]{2,1,0:T(8,128)(2,1)S(1)}, bf16[4,64,64]{2,1,0:T(8,128)(2,1)S(1)}, u32[]{:S(2)}, u32[]{:S(2)}) collective-permute-start(bf16[4,64,64]{2,1,0:T(8,128)(2,1)S(1)} %select_bitcast_fusion), channel_id=1, source_target_pairs={{0,2},{1,3},{2,0},{3,1},{4,6},{5,7},{6,4},{7,5},{8,10},{9,11},{10,... | collective-permute-start | bytes 98312 | tf_op jit(solution)/shard_map/ppermute | solution.py:422
  132.7 3.4 %collective-permute-start.26 = (bf16[4,64,64]{2,1,0:T(8,128)(2,1)S(1)}, bf16[4,64,64]{2,1,0:T(8,128)(2,1)S(1)}, u32[]{:S(2)}, u32[]{:S(2)}) collective-permute-start(bf16[4,64,64]{2,1,0:T(8,128)(2,1)S(1)} %select_bitcast_fusion), channel_id=1, source_target_pairs={{0,3},{1,0},{2,1},{3,2},{4,7},{5,4},{6,5},{7,6},{8,11},{9,8},{10,9... | collective-permute-start | bytes 98312 | tf_op jit(solution)/shard_map/ppermute | solution.py:422
  132.7 4.3 %collective-permute-start.24 = (bf16[4,64,64]{2,1,0:T(8,128)(2,1)S(1)}, bf16[4,64,64]{2,1,0:T(8,128)(2,1)S(1)}, u32[]{:S(2)}, u32[]{:S(2)}) collective-permute-start(bf16[4,64,64]{2,1,0:T(8,128)(2,1)S(1)} %select_bitcast_fusion), channel_id=1, source_target_pairs={{0,1},{1,2},{2,3},{3,0},{4,5},{5,6},{6,7},{7,4},{8,9},{9,10},{10,1... | collective-permute-start | bytes 98312 | tf_op jit(solution)/shard_map/ppermute | solution.py:422
  133.2 15.3 %collective-permute-start.27 = (bf16[64,2048]{1,0:T(8,128)(2,1)S(1)}, bf16[64,2048]{1,0:T(8,128)(2,1)S(1)}, u32[]{:S(2)}, u32[]{:S(2)}) collective-permute-start(bf16[64,2048]{1,0:T(8,128)(2,1)S(1)} %select_convert_fusion.3), channel_id=1, source_target_pairs={{0,8},{4,12},{8,0},{12,4},{1,9},{5,13},{9,1},{13,5},{2,10},{6,14},... | collective-permute-start | bytes 786440 | tf_op jit(solution)/shard_map/ppermute | solution.py:278
  (17 other events, 122.4 us)

commit v19 on v15

--- a/solution.py
+++ b/solution.py
@@ -373,8 +373,9 @@
         remote.update({(step, shift): from_rep(rows, shift) for shift in range(1, n_rep)})
     jobs = [([((0, 0), lead)], send, keep, jnp.bfloat16)]
     for piece, (step, shift) in enumerate(pieces):
+        arrived = [received for _, received, _, _ in first_leg] if piece == 1 else []
         sends = gap(send, jobs)
-        own, panels, _ = lax.optimization_barrier((remote[step, shift], panels, send))
+        own, panels, *_ = lax.optimization_barrier((remote[step, shift], panels, arrived, send))
         if piece == 0:
             panels, order = panels + [swap_tensor(panels[1], bits[1])], order + [bits[0] ^ bits[1]]
             panels, order = spread_panels(panels, order, bits[2:])

time: 139 us -> 139 us (level)
  starting transfers between devices: 29.2 us -> 31.3 us
    ppermute x4, waiting for transfers between devices: 9.48 us -> 6.36 us  [from_rep(): lax.ppermute(value, 'rep', [((i + shift) % n_rep, i) for i in range(n_rep)])]
    ppermute x11, waiting for transfers between devices: 1.01 us -> 3.36 us  [swap_tensor(): return lax.ppermute(value, 'tp', [(i, i ^ bit) for i in range(n_tensor)])]
    ppermute x4, starting transfers between devices: 4.69 us -> 6.27 us  [from_rep(): lax.ppermute(value, 'rep', [((i + shift) % n_rep, i) for i in range(n_rep)])]
    unnamed x34 -> x36, local copies, waits for them, and re-layouts: 4.63 us -> 4.29 us
  transfers between devices with their start and end apart: 28 -> 28, of which waited for: 10 -> 10; matrix products, arithmetic and copies ran while one was open for 4% -> 3% of each run, Pallas kernels for 50% -> 50%
where the time goes in v19:
time: 139 us
  Pallas kernels  69.8 us (50%)
  starting transfers between devices  31.3 us (23%)
  waiting for transfers between devices  29.1 us (21%)
  local copies, waits for them, and re-layouts  7.37 us (5%)
    pallas_call x5, Pallas kernels, partial_products(): pl.pallas_call(functools.partial(matmul_body, spans, staged, apart), in_s...  66.5 us
    ppermute x5, waiting for transfers between devices, to_group(): lax.ppermute(value, 'tp', [(i, (i + moved) % n_tensor) for i in range(n_t...  15.8 us
    ppermute x11, starting transfers between devices, swap_tensor(): return lax.ppermute(value, 'tp', [(i, i ^ bit) for i in range(n_tensor)])  13.9 us
    ppermute x5, starting transfers between devices, to_group(): lax.ppermute(value, 'tp', [(i, (i + moved) % n_tensor) for i in range(n_t...  8.51 us
    ppermute x4, waiting for transfers between devices, from_rep(): lax.ppermute(value, 'rep', [((i + shift) % n_rep, i) for i in range(n_rep)])  6.36 us
    ppermute x4, starting transfers between devices, from_rep(): lax.ppermute(value, 'rep', [((i + shift) % n_rep, i) for i in range(n_rep)])  6.27 us
    unnamed x36, local copies, waits for them, and re-layouts  4.29 us
    ppermute x3, waiting for transfers between devices, per_device(): lax.ppermute(masked, ('rep', 'sub'), [(i, (i + turn) % n_owners) for i in...  3.6 us
  transfers between devices with their start and end apart: 28, of which 10 were waited for; matrix products, arithmetic and copies ran while one was open for 3% of the time, Pallas kernels for 50%

profile of v19, /device:TPU:0, one launch (start us, length us, event | category | flops | bytes accessed | tf_op | source)
XLA Modules:
  0.0 139.1 jit_solution(6790541827921122745)
XLA Ops:
  0.5 2.2 %slice.51 = bf16[1,64,7168]{2,1,0:T(8,128)(2,1)} slice(bf16[4,64,7168]{2,1,0:T(8,128)(2,1)} %refs_2_.7), slice={[0:1], [0:64], [0:7168]} | slice | bytes 1835008 | tf_op jit(solution)/shard_map/slice | solution.py:293
  2.7 2.6 %collective-permute-start.3 = (bf16[1,64,7168]{2,1,0:T(8,128)(2,1)}, bf16[1,64,7168]{2,1,0:T(8,128)(2,1)S(1)}, u32[]{:S(2)}, u32[]{:S(2)}) collective-permute-start(bf16[1,64,7168]{2,1,0:T(8,128)(2,1)} %slice.51), channel_id=1, source_target_pairs={{2,0},{0,2},{3,1},{1,3},{6,4},{4,6},{7,5},{5,7},{10,8},{8,10},{11,... | collective-permute-start | bytes 2752520 | tf_op jit(solution)/shard_map/ppermute | solution.py:271
  5.3 2.6 %collective-permute-start.4 = (bf16[1,64,2048]{2,1,0:T(8,128)(2,1)S(1)}, bf16[1,64,2048]{2,1,0:T(8,128)(2,1)}, u32[]{:S(2)}, u32[]{:S(2)}) collective-permute-start(bf16[1,64,2048]{2,1,0:T(8,128)(2,1)S(1)} %copy-done.7), channel_id=1, source_target_pairs={{0,8},{4,12},{8,0},{12,4},{1,9},{5,13},{9,1},{13,5},{2,10},{6,14},... | collective-permute-start | bytes 786440 | tf_op jit(solution)/shard_map/ppermute | solution.py:274
  7.9 1.6 %collective-permute-start.5 = (bf16[1,64,2048]{2,1,0:T(8,128)(2,1)S(1)}, bf16[1,64,2048]{2,1,0:T(8,128)(2,1)S(1)}, u32[]{:S(2)}, u32[]{:S(2)}) collective-permute-start(bf16[1,64,2048]{2,1,0:T(8,128)(2,1)S(1)} %copy-done.7), channel_id=1, source_target_pairs={{0,4},{4,0},{8,12},{12,8},{1,5},{5,1},{9,13},{13,9},{2,6},{6,2},{1... | collective-permute-start | bytes 786440 | tf_op jit(solution)/shard_map/ppermute | solution.py:274
  9.5 16.3 %partial_products.5 = (bf16[128,2176]{1,0:T(8,128)(2,1)S(1)}, f32[128,2176]{1,0:T(8,128)S(1)}, bf16[1,64,7168]{2,1,0:T(8,128)(2,1)}, bf16[1,64,7168]{2,1,0:T(8,128)(2,1)}, bf16[1,64,7168]{2,1,0:T(8,128)(2,1)}) custom-call(s32[1]{0:T(128)} %bitcast.1.pos_ref, bf16[4,64,7168]{2,1,0:T(8,128)(2,1)} %refs_2_.7, ...), custom_call_target="tpu_custom_call" | custom-call | tf_op jit(solution)/shard_map/partial_products/pallas_call | solution.py:145
  26.6 1.6 %collective-permute-start.2 = (bf16[1,64,7168]{2,1,0:T(8,128)(2,1)}, bf16[1,64,7168]{2,1,0:T(8,128)(2,1)}, u32[]{:S(2)}, u32[]{:S(2)}) collective-permute-start(bf16[1,64,7168]{2,1,0:T(8,128)(2,1)} %get-tuple-element.83), channel_id=1, source_target_pairs={{2,0},{0,2},{3,1},{1,3},{6,4},{4,6},{7,5},{5,7},{10,8},{8,10},{11,... | collective-permute-start | bytes 2752520 | tf_op jit(solution)/shard_map/ppermute | solution.py:271
  28.2 1.6 %collective-permute-start.7 = (bf16[128,2176]{1,0:T(8,128)(2,1)S(1)}, bf16[128,2176]{1,0:T(8,128)(2,1)S(1)}, u32[]{:S(2)}, u32[]{:S(2)}) collective-permute-start(bf16[128,2176]{1,0:T(8,128)(2,1)S(1)} %get-tuple-element.84), channel_id=1, source_target_pairs={{0,4},{4,0},{8,12},{12,8},{1,5},{5,1},{9,13},{13,9},{2,6},{6,2},{1... | collective-permute-start | bytes 1671176 | tf_op jit(solution)/shard_map/ppermute | solution.py:274
  30.2 13.4 %partial_products.6 = (bf16[64,2176]{1,0:T(8,128)(2,1)S(1)}, bf16[64,2176]{1,0:T(8,128)(2,1)S(1)}, f32[64,2176]{1,0:T(8,128)S(1)}, f32[64,2176]{1,0:T(8,128)S(1)}) custom-call(s32[1]{0:T(128)} %bitcast.1.pos_ref, bf16[1,64,7168]{2,1,0:T(8,128)(2,1)S(1)} %collective-permute-done.3.refs_0_, bf16[1,64,7168]{2,1,0:T(8,128)(2,1)S(1)} %collective-permute-done.8.refs_1_, ...), custom_call_target="tpu_custom_call" | custom-call | tf_op jit(solution)/shard_map/partial_products/pallas_call | solution.py:145
  43.7 0.9 copy-done.2
  45.9 2.6 %collective-permute-done.6 = bf16[1,64,2048]{2,1,0:T(8,128)(2,1)S(1)} collective-permute-done((bf16[1,64,2048]{2,1,0:T(8,128)(2,1)}, bf16[1,64,2048]{2,1,0:T(8,128)(2,1)S(1)}, u32[]{:S(2)}, u32[]{:S(2)}) %collective-permute-start.6) | collective-permute-done | bytes 262176 | tf_op jit(solution)/shard_map/ppermute | solution.py:274
  50.2 1.1 collective-permute-start.1
  52.3 0.9 collective-permute-start.13
  53.3 1.6 %collective-permute-start.11 = (bf16[64,2176]{1,0:T(8,128)(2,1)}, bf16[64,2176]{1,0:T(8,128)(2,1)S(1)}, u32[]{:S(2)}, u32[]{:S(2)}) collective-permute-start(bf16[64,2176]{1,0:T(8,128)(2,1)} %copy-done.14), channel_id=1, source_target_pairs={{0,4},{4,0},{8,12},{12,8},{1,5},{5,1},{9,13},{13,9},{2,6},{6,2},{1... | collective-permute-start | bytes 835592 | tf_op jit(solution)/shard_map/ppermute | solution.py:274
  55.3 15.3 %partial_products.7 = (bf16[64,2176]{1,0:T(8,128)(2,1)S(1)}, bf16[64,2176]{1,0:T(8,128)(2,1)S(1)}, f32[64,2176]{1,0:T(8,128)S(1)}, f32[64,2176]{1,0:T(8,128)S(1)}) custom-call(s32[1]{0:T(128)} %bitcast.1.pos_ref, bf16[1,64,7168]{2,1,0:T(8,128)(2,1)} %collective-permute-done.2.refs_0_, bf16[1,64,7168]{2,1,0:T(8,128)(2,1)} %collective-permute-done.9.refs_1_, ...), custom_call_target="tpu_custom_call" | custom-call | tf_op jit(solution)/shard_map/partial_products/pallas_call | solution.py:145
  70.7 3.0 %collective-permute-done.1.refs_0_ = bf16[1,64,7168]{2,1,0:T(8,128)(2,1)S(1)} collective-permute-done((bf16[1,64,7168]{2,1,0:T(8,128)(2,1)}, bf16[1,64,7168]{2,1,0:T(8,128)(2,1)S(1)}, u32[]{:S(2)}, u32[]{:S(2)}) %collective-permute-start.1) | collective-permute-done | bytes 917536 | tf_op jit(solution)/shard_map/ppermute | solution.py:271
  73.7 1.6 %collective-permute-start.15 = (bf16[64,2176]{1,0:T(8,128)(2,1)S(1)}, bf16[64,2176]{1,0:T(8,128)(2,1)S(1)}, u32[]{:S(2)}, u32[]{:S(2)}) collective-permute-start(bf16[64,2176]{1,0:T(8,128)(2,1)S(1)} %get-tuple-element.125), channel_id=1, source_target_pairs={{0,4},{4,0},{8,12},{12,8},{1,5},{5,1},{9,13},{13,9},{2,6},{6,2},{1... | collective-permute-start | bytes 835592 | tf_op jit(solution)/shard_map/ppermute | solution.py:274
  75.4 2.7 %collective-permute-start.12 = (bf16[64,2176]{1,0:T(8,128)(2,1)S(1)}, bf16[64,2176]{1,0:T(8,128)(2,1)S(1)}, u32[]{:S(2)}, u32[]{:S(2)}) collective-permute-start(bf16[64,2176]{1,0:T(8,128)(2,1)S(1)} %select_convert_fusion.2), channel_id=1, source_target_pairs={{0,8},{4,12},{8,0},{12,4},{1,9},{5,13},{9,1},{13,5},{2,10},{6,14},... | collective-permute-start | bytes 835592 | tf_op jit(solution)/shard_map/ppermute | solution.py:278
  78.5 10.7 %partial_products.8 = (bf16[64,2176]{1,0:T(8,128)(2,1)S(1)}, f32[64,2176]{1,0:T(8,128)S(1)}) custom-call(s32[1]{0:T(128)} %bitcast.1.pos_ref, bf16[1,64,7168]{2,1,0:T(8,128)(2,1)S(1)} %collective-permute-done.1.refs_0_, bf16[1,64,7168]{2,1,0:T(8,128)(2,1)S(1)} %collective-permute-done.10.refs_1_, bf16[7168,2048]{1,0:T(8,128)(2,1)} %refs_2_.9, ...), custom_call_target="tpu_custom_call" | custom-call | tf_op jit(solution)/shard_map/partial_products/pallas_call | solution.py:145
  89.2 3.1 %collective-permute-done.13.refs_0_ = bf16[1,64,7168]{2,1,0:T(8,128)(2,1)S(1)} collective-permute-done((bf16[1,64,7168]{2,1,0:T(8,128)(2,1)}, bf16[1,64,7168]{2,1,0:T(8,128)(2,1)S(1)}, u32[]{:S(2)}, u32[]{:S(2)}) %collective-permute-start.13) | collective-permute-done | bytes 917536 | tf_op jit(solution)/shard_map/ppermute | solution.py:271
  92.6 2.8 %collective-permute-start.16 = (bf16[64,2176]{1,0:T(8,128)(2,1)S(1)}, bf16[64,2176]{1,0:T(8,128)(2,1)S(1)}, u32[]{:S(2)}, u32[]{:S(2)}) collective-permute-start(bf16[64,2176]{1,0:T(8,128)(2,1)S(1)} %select_convert_fusion.1), channel_id=1, source_target_pairs={{0,8},{4,12},{8,0},{12,4},{1,9},{5,13},{9,1},{13,5},{2,10},{6,14},... | collective-permute-start | bytes 835592 | tf_op jit(solution)/shard_map/ppermute | solution.py:278
  95.4 1.6 %collective-permute-start.17 = (bf16[64,2176]{1,0:T(8,128)(2,1)S(1)}, bf16[64,2176]{1,0:T(8,128)(2,1)S(1)}, u32[]{:S(2)}, u32[]{:S(2)}) collective-permute-start(bf16[64,2176]{1,0:T(8,128)(2,1)S(1)} %get-tuple-element.135), channel_id=1, source_target_pairs={{0,4},{4,0},{8,12},{12,8},{1,5},{5,1},{9,13},{13,9},{2,6},{6,2},{1... | collective-permute-start | bytes 835592 | tf_op jit(solution)/shard_map/ppermute | solution.py:274
  97.0 10.7 %partial_products.9 = (bf16[64,2048]{1,0:T(8,128)(2,1)S(1)}, f32[64,2048]{1,0:T(8,128)S(1)}, f32[64,128]{1,0:T(8,128)S(1)}, f32[64,128]{1,0:T(8,128)S(1)}) custom-call(s32[1]{0:T(128)} %bitcast.1.pos_ref, bf16[1,64,7168]{2,1,0:T(8,128)(2,1)S(1)} %collective-permute-done.13.refs_0_, bf16[1,64,7168]{2,1,0:T(8,128)(2,1)S(1)} %collective-permute-done.14.refs_1_, ...), custom_call_target="tpu_custom_call" | custom-call | tf_op jit(solution)/shard_map/partial_products/pallas_call | solution.py:145
  109.1 1.6 %collective-permute-start.23 = (bf16[64,2048]{1,0:T(8,128)(2,1)S(1)}, bf16[64,2048]{1,0:T(8,128)(2,1)S(1)}, u32[]{:S(2)}, u32[]{:S(2)}) collective-permute-start(bf16[64,2048]{1,0:T(8,128)(2,1)S(1)} %get-tuple-element.150), channel_id=1, source_target_pairs={{0,4},{4,0},{8,12},{12,8},{1,5},{5,1},{9,13},{13,9},{2,6},{6,2},{1... | collective-permute-start | bytes 786440 | tf_op jit(solution)/shard_map/ppermute | solution.py:274
  110.7 2.1 %collective-permute-start.19 = (bf16[64,2176]{1,0:T(8,128)(2,1)S(1)}, bf16[64,2176]{1,0:T(8,128)(2,1)S(1)}, u32[]{:S(2)}, u32[]{:S(2)}) collective-permute-start(bf16[64,2176]{1,0:T(8,128)(2,1)S(1)} %get-tuple-element.140), channel_id=1, source_target_pairs={{0,8},{4,12},{8,0},{12,4},{1,9},{5,13},{9,1},{13,5},{2,10},{6,14},... | collective-permute-start | bytes 835592 | tf_op jit(solution)/shard_map/ppermute | solution.py:278
  112.8 0.9 collective-permute-start.22
  113.7 14.2 %collective-permute-done.22 = f32[64,128]{1,0:T(8,128)S(1)} collective-permute-done((f32[64,128]{1,0:T(8,128)S(1)}, f32[64,128]{1,0:T(8,128)S(1)}, u32[]{:S(2)}, u32[]{:S(2)}) %collective-permute-start.22) | collective-permute-done | bytes 32800 | tf_op jit(solution)/shard_map/ppermute | solution.py:278
  128.3 1.6 %collective-permute-start.25 = (bf16[4,64,64]{2,1,0:T(8,128)(2,1)S(1)}, bf16[4,64,64]{2,1,0:T(8,128)(2,1)S(1)}, u32[]{:S(2)}, u32[]{:S(2)}) collective-permute-start(bf16[4,64,64]{2,1,0:T(8,128)(2,1)S(1)} %select_bitcast_fusion), channel_id=1, source_target_pairs={{0,2},{1,3},{2,0},{3,1},{4,6},{5,7},{6,4},{7,5},{8,10},{9,11},{10,... | collective-permute-start | bytes 98312 | tf_op jit(solution)/shard_map/ppermute | solution.py:418
  130.4 2.2 %collective-permute-done.25 = bf16[4,64,64]{2,1,0:T(8,128)(2,1)S(1)} collective-permute-done((bf16[4,64,64]{2,1,0:T(8,128)(2,1)S(1)}, bf16[4,64,64]{2,1,0:T(8,128)(2,1)S(1)}, u32[]{:S(2)}, u32[]{:S(2)}) %collective-permute-start.25) | collective-permute-done | bytes 32800 | tf_op jit(solution)/shard_map/ppermute | solution.py:418
  133.0 1.0 collective-permute-done.24
  134.1 2.5 %finish_steps.1 = (bf16[4,64,2048]{2,1,0:T(8,128)(2,1)}, bf16[64,2048]{1,0:T(8,128)(2,1)S(1)}) custom-call(bf16[256,64]{1,0:T(8,128)(2,1)S(1)} %bitcast.30, s32[256,1]{1,0:T(8,128)S(1)} %copy-done.4, s32[4]{0:T(128)S(1)} %pad_add_fusion.order_ref, bf16[64,2048]{1,0:T(8,128)(2,1)S(1)} %bitcast.31, bf16[64,2048]{1,0:T(8,128)(2,1)} %bitcast.14.refs_1_, ...), custom_call_target="tpu_custom_call" | custom-call | tf_op jit(solution)/shard_map/finish_steps/pallas_call | solution.py:203
  136.6 1.6 %collective-permute-done.27.refs_1_ = bf16[64,2048]{1,0:T(8,128)(2,1)S(1)} collective-permute-done((bf16[64,2048]{1,0:T(8,128)(2,1)S(1)}, bf16[64,2048]{1,0:T(8,128)(2,1)S(1)}, u32[]{:S(2)}, u32[]{:S(2)}) %collective-permute-start.27) | collective-permute-done | bytes 262176 | tf_op jit(solution)/shard_map/ppermute | solution.py:278
  138.3 0.8 finish_last.1
  (96 shorter events, 9.9 us)
Async XLA Ops:
  0.0 51.3 %copy-start = (s32[256,1]{0,1:T(1,128)S(1)}, s32[256,1]{0,1:T(1,128)}, u32[]{:S(2)}) copy-start(s32[256,1]{0,1:T(1,128)} %param.10) | copy-start | bytes 3076
  0.0 9.5 %collective-permute-start = (bf16[4,64,7168]{2,1,0:T(8,128)(2,1)}, bf16[4,64,7168]{2,1,0:T(8,128)(2,1)}, u32[]{:S(2)}, u32[]{:S(2)}) collective-permute-start(bf16[4,64,7168]{2,1,0:T(8,128)(2,1)} %refs_2_.7), channel_id=1, source_target_pairs={{0,1},{1,0},{2,3},{3,2},{4,5},{5,4},{6,7},{7,6},{8,9},{9,8},{10,11... | collective-permute-start | bytes 11010056 | tf_op jit(solution)/shard_map/ppermute | solution.py:268
  2.7 23.8 %collective-permute-start.3 = (bf16[1,64,7168]{2,1,0:T(8,128)(2,1)}, bf16[1,64,7168]{2,1,0:T(8,128)(2,1)S(1)}, u32[]{:S(2)}, u32[]{:S(2)}) collective-permute-start(bf16[1,64,7168]{2,1,0:T(8,128)(2,1)} %slice.51), channel_id=1, source_target_pairs={{2,0},{0,2},{3,1},{1,3},{6,4},{4,6},{7,5},{5,7},{10,8},{8,10},{11,... | collective-permute-start | bytes 2752520 | tf_op jit(solution)/shard_map/ppermute | solution.py:271
  5.3 20.5 %collective-permute-start.4 = (bf16[1,64,2048]{2,1,0:T(8,128)(2,1)S(1)}, bf16[1,64,2048]{2,1,0:T(8,128)(2,1)}, u32[]{:S(2)}, u32[]{:S(2)}) collective-permute-start(bf16[1,64,2048]{2,1,0:T(8,128)(2,1)S(1)} %copy-done.7), channel_id=1, source_target_pairs={{0,8},{4,12},{8,0},{12,4},{1,9},{5,13},{9,1},{13,5},{2,10},{6,14},... | collective-permute-start | bytes 786440 | tf_op jit(solution)/shard_map/ppermute | solution.py:274
  7.9 18.0 %collective-permute-start.5 = (bf16[1,64,2048]{2,1,0:T(8,128)(2,1)S(1)}, bf16[1,64,2048]{2,1,0:T(8,128)(2,1)S(1)}, u32[]{:S(2)}, u32[]{:S(2)}) collective-permute-start(bf16[1,64,2048]{2,1,0:T(8,128)(2,1)S(1)} %copy-done.7), channel_id=1, source_target_pairs={{0,4},{4,0},{8,12},{12,8},{1,5},{5,1},{9,13},{13,9},{2,6},{6,2},{1... | collective-permute-start | bytes 786440 | tf_op jit(solution)/shard_map/ppermute | solution.py:274
  26.6 3.7 %collective-permute-start.8 = (bf16[1,64,7168]{2,1,0:T(8,128)(2,1)S(1)}, bf16[1,64,7168]{2,1,0:T(8,128)(2,1)S(1)}, u32[]{:S(2)}, u32[]{:S(2)}) collective-permute-start(bf16[1,64,7168]{2,1,0:T(8,128)(2,1)S(1)} %collective-permute-done.3.refs_0_), channel_id=1, source_target_pairs={{0,1},{1,0},{2,3},{3,2},{4,5},{5,4},{6,7},{7,6},{8,9},{9,8},{10,11... | collective-permute-start | bytes 2752520 | tf_op jit(solution)/shard_map/ppermute | solution.py:268
  26.6 24.8 %copy-start.17 = (s32[4]{0:T(128)S(1)}, s32[4]{0:T(128)}, u32[]{:S(2)}) copy-start(s32[4]{0:T(128)} %param.11) | copy-start | bytes 52
  26.6 23.1 %collective-permute-start.2 = (bf16[1,64,7168]{2,1,0:T(8,128)(2,1)}, bf16[1,64,7168]{2,1,0:T(8,128)(2,1)}, u32[]{:S(2)}, u32[]{:S(2)}) collective-permute-start(bf16[1,64,7168]{2,1,0:T(8,128)(2,1)} %get-tuple-element.83), channel_id=1, source_target_pairs={{2,0},{0,2},{3,1},{1,3},{6,4},{4,6},{7,5},{5,7},{10,8},{8,10},{11,... | collective-permute-start | bytes 2752520 | tf_op jit(solution)/shard_map/ppermute | solution.py:271
  28.2 21.1 %collective-permute-start.7 = (bf16[128,2176]{1,0:T(8,128)(2,1)S(1)}, bf16[128,2176]{1,0:T(8,128)(2,1)S(1)}, u32[]{:S(2)}, u32[]{:S(2)}) collective-permute-start(bf16[128,2176]{1,0:T(8,128)(2,1)S(1)} %get-tuple-element.84), channel_id=1, source_target_pairs={{0,4},{4,0},{8,12},{12,8},{1,5},{5,1},{9,13},{13,9},{2,6},{6,2},{1... | collective-permute-start | bytes 1671176 | tf_op jit(solution)/shard_map/ppermute | solution.py:274
  29.8 18.8 %collective-permute-start.6 = (bf16[1,64,2048]{2,1,0:T(8,128)(2,1)}, bf16[1,64,2048]{2,1,0:T(8,128)(2,1)S(1)}, u32[]{:S(2)}, u32[]{:S(2)}) collective-permute-start(bf16[1,64,2048]{2,1,0:T(8,128)(2,1)} %collective-permute-done.4), channel_id=1, source_target_pairs={{0,4},{4,0},{8,12},{12,8},{1,5},{5,1},{9,13},{13,9},{2,6},{6,2},{1... | collective-permute-start | bytes 786440 | tf_op jit(solution)/shard_map/ppermute | solution.py:274
  49.7 5.7 %collective-permute-start.9 = (bf16[1,64,7168]{2,1,0:T(8,128)(2,1)}, bf16[1,64,7168]{2,1,0:T(8,128)(2,1)}, u32[]{:S(2)}, u32[]{:S(2)}) collective-permute-start(bf16[1,64,7168]{2,1,0:T(8,128)(2,1)} %collective-permute-done.2.refs_0_), channel_id=1, source_target_pairs={{0,1},{1,0},{2,3},{3,2},{4,5},{5,4},{6,7},{7,6},{8,9},{9,8},{10,11... | collective-permute-start | bytes 2752520 | tf_op jit(solution)/shard_map/ppermute | solution.py:268
  50.2 23.4 %collective-permute-start.1 = (bf16[1,64,7168]{2,1,0:T(8,128)(2,1)}, bf16[1,64,7168]{2,1,0:T(8,128)(2,1)S(1)}, u32[]{:S(2)}, u32[]{:S(2)}) collective-permute-start(bf16[1,64,7168]{2,1,0:T(8,128)(2,1)} %get-tuple-element.82), channel_id=1, source_target_pairs={{2,0},{0,2},{3,1},{1,3},{6,4},{4,6},{7,5},{5,7},{10,8},{8,10},{11,... | collective-permute-start | bytes 2752520 | tf_op jit(solution)/shard_map/ppermute | solution.py:271
  52.3 40.0 %collective-permute-start.13 = (bf16[1,64,7168]{2,1,0:T(8,128)(2,1)}, bf16[1,64,7168]{2,1,0:T(8,128)(2,1)S(1)}, u32[]{:S(2)}, u32[]{:S(2)}) collective-permute-start(bf16[1,64,7168]{2,1,0:T(8,128)(2,1)} %get-tuple-element.116), channel_id=1, source_target_pairs={{2,0},{0,2},{3,1},{1,3},{6,4},{4,6},{7,5},{5,7},{10,8},{8,10},{11,... | collective-permute-start | bytes 2752520 | tf_op jit(solution)/shard_map/ppermute | solution.py:271
  53.3 20.3 %copy-start.16 = (bf16[128,2176]{1,0:T(8,128)(2,1)S(1)}, bf16[128,2176]{1,0:T(8,128)(2,1)}, u32[]{:S(2)}) copy-start(bf16[128,2176]{1,0:T(8,128)(2,1)} %copy-done.15) | copy-start | bytes 1671172
  53.3 22.1 %collective-permute-start.11 = (bf16[64,2176]{1,0:T(8,128)(2,1)}, bf16[64,2176]{1,0:T(8,128)(2,1)S(1)}, u32[]{:S(2)}, u32[]{:S(2)}) collective-permute-start(bf16[64,2176]{1,0:T(8,128)(2,1)} %copy-done.14), channel_id=1, source_target_pairs={{0,4},{4,0},{8,12},{12,8},{1,5},{5,1},{9,13},{13,9},{2,6},{6,2},{1... | collective-permute-start | bytes 835592 | tf_op jit(solution)/shard_map/ppermute | solution.py:274
  54.9 53.4 %collective-permute-start.18 = (bf16[64,2176]{1,0:T(8,128)(2,1)}, bf16[64,2176]{1,0:T(8,128)(2,1)S(1)}, u32[]{:S(2)}, u32[]{:S(2)}) collective-permute-start(bf16[64,2176]{1,0:T(8,128)(2,1)} %copy-done.13), channel_id=1, source_target_pairs={{0,4},{4,0},{8,12},{12,8},{1,5},{5,1},{9,13},{13,9},{2,6},{6,2},{1... | collective-permute-start | bytes 835592 | tf_op jit(solution)/shard_map/ppermute | solution.py:274
  73.6 4.5 %collective-permute-start.10 = (bf16[1,64,7168]{2,1,0:T(8,128)(2,1)S(1)}, bf16[1,64,7168]{2,1,0:T(8,128)(2,1)S(1)}, u32[]{:S(2)}, u32[]{:S(2)}) collective-permute-start(bf16[1,64,7168]{2,1,0:T(8,128)(2,1)S(1)} %collective-permute-done.1.refs_0_), channel_id=1, source_target_pairs={{0,1},{1,0},{2,3},{3,2},{4,5},{5,4},{6,7},{7,6},{8,9},{9,8},{10,11... | collective-permute-start | bytes 2752520 | tf_op jit(solution)/shard_map/ppermute | solution.py:268
  73.7 18.6 %collective-permute-start.15 = (bf16[64,2176]{1,0:T(8,128)(2,1)S(1)}, bf16[64,2176]{1,0:T(8,128)(2,1)S(1)}, u32[]{:S(2)}, u32[]{:S(2)}) collective-permute-start(bf16[64,2176]{1,0:T(8,128)(2,1)S(1)} %get-tuple-element.125), channel_id=1, source_target_pairs={{0,4},{4,0},{8,12},{12,8},{1,5},{5,1},{9,13},{13,9},{2,6},{6,2},{1... | collective-permute-start | bytes 835592 | tf_op jit(solution)/shard_map/ppermute | solution.py:274
  75.4 17.1 %collective-permute-start.12 = (bf16[64,2176]{1,0:T(8,128)(2,1)S(1)}, bf16[64,2176]{1,0:T(8,128)(2,1)S(1)}, u32[]{:S(2)}, u32[]{:S(2)}) collective-permute-start(bf16[64,2176]{1,0:T(8,128)(2,1)S(1)} %select_convert_fusion.2), channel_id=1, source_target_pairs={{0,8},{4,12},{8,0},{12,4},{1,9},{5,13},{9,1},{13,5},{2,10},{6,14},... | collective-permute-start | bytes 835592 | tf_op jit(solution)/shard_map/ppermute | solution.py:278
  78.1 18.8 %collective-permute-start.21 = (bf16[64,2176]{1,0:T(8,128)(2,1)S(1)}, bf16[64,2176]{1,0:T(8,128)(2,1)S(1)}, u32[]{:S(2)}, u32[]{:S(2)}) collective-permute-start(bf16[64,2176]{1,0:T(8,128)(2,1)S(1)} %get-tuple-element.147), channel_id=1, source_target_pairs={{0,4},{4,0},{8,12},{12,8},{1,5},{5,1},{9,13},{13,9},{2,6},{6,2},{1... | collective-permute-start | bytes 835592 | tf_op jit(solution)/shard_map/ppermute | solution.py:274
  92.3 4.7 %collective-permute-start.14 = (bf16[1,64,7168]{2,1,0:T(8,128)(2,1)S(1)}, bf16[1,64,7168]{2,1,0:T(8,128)(2,1)S(1)}, u32[]{:S(2)}, u32[]{:S(2)}) collective-permute-start(bf16[1,64,7168]{2,1,0:T(8,128)(2,1)S(1)} %collective-permute-done.13.refs_0_), channel_id=1, source_target_pairs={{0,1},{1,0},{2,3},{3,2},{4,5},{5,4},{6,7},{7,6},{8,9},{9,8},{10,11... | collective-permute-start | bytes 2752520 | tf_op jit(solution)/shard_map/ppermute | solution.py:268
  92.6 15.2 %copy-start.5 = (bf16[64,2176]{1,0:T(8,128)(2,1)}, bf16[64,2176]{1,0:T(8,128)(2,1)S(1)}, u32[]{:S(2)}) copy-start(bf16[64,2176]{1,0:T(8,128)(2,1)S(1)} %collective-permute-done.12.refs_5_) | copy-start | bytes 835588
  92.6 16.5 %collective-permute-start.16 = (bf16[64,2176]{1,0:T(8,128)(2,1)S(1)}, bf16[64,2176]{1,0:T(8,128)(2,1)S(1)}, u32[]{:S(2)}, u32[]{:S(2)}) collective-permute-start(bf16[64,2176]{1,0:T(8,128)(2,1)S(1)} %select_convert_fusion.1), channel_id=1, source_target_pairs={{0,8},{4,12},{8,0},{12,4},{1,9},{5,13},{9,1},{13,5},{2,10},{6,14},... | collective-permute-start | bytes 835592 | tf_op jit(solution)/shard_map/ppermute | solution.py:278
  95.4 13.6 %collective-permute-start.17 = (bf16[64,2176]{1,0:T(8,128)(2,1)S(1)}, bf16[64,2176]{1,0:T(8,128)(2,1)S(1)}, u32[]{:S(2)}, u32[]{:S(2)}) collective-permute-start(bf16[64,2176]{1,0:T(8,128)(2,1)S(1)} %get-tuple-element.135), channel_id=1, source_target_pairs={{0,4},{4,0},{8,12},{12,8},{1,5},{5,1},{9,13},{13,9},{2,6},{6,2},{1... | collective-permute-start | bytes 835592 | tf_op jit(solution)/shard_map/ppermute | solution.py:274
  107.8 5.0 %collective-permute-start.20 = (f32[64,128]{1,0:T(8,128)S(1)}, f32[64,128]{1,0:T(8,128)S(1)}, u32[]{:S(2)}, u32[]{:S(2)}) collective-permute-start(f32[64,128]{1,0:T(8,128)S(1)} %get-tuple-element.144), channel_id=1, source_target_pairs={{0,4},{4,0},{8,12},{12,8},{1,5},{5,1},{9,13},{13,9},{2,6},{6,2},{1... | collective-permute-start | bytes 98312 | tf_op jit(solution)/shard_map/ppermute | solution.py:274
  109.1 18.8 %collective-permute-start.23 = (bf16[64,2048]{1,0:T(8,128)(2,1)S(1)}, bf16[64,2048]{1,0:T(8,128)(2,1)S(1)}, u32[]{:S(2)}, u32[]{:S(2)}) collective-permute-start(bf16[64,2048]{1,0:T(8,128)(2,1)S(1)} %get-tuple-element.150), channel_id=1, source_target_pairs={{0,4},{4,0},{8,12},{12,8},{1,5},{5,1},{9,13},{13,9},{2,6},{6,2},{1... | collective-permute-start | bytes 786440 | tf_op jit(solution)/shard_map/ppermute | solution.py:274
  110.7 17.4 %collective-permute-start.19 = (bf16[64,2176]{1,0:T(8,128)(2,1)S(1)}, bf16[64,2176]{1,0:T(8,128)(2,1)S(1)}, u32[]{:S(2)}, u32[]{:S(2)}) collective-permute-start(bf16[64,2176]{1,0:T(8,128)(2,1)S(1)} %get-tuple-element.140), channel_id=1, source_target_pairs={{0,8},{4,12},{8,0},{12,4},{1,9},{5,13},{9,1},{13,5},{2,10},{6,14},... | collective-permute-start | bytes 835592 | tf_op jit(solution)/shard_map/ppermute | solution.py:278
  112.8 15.1 %collective-permute-start.22 = (f32[64,128]{1,0:T(8,128)S(1)}, f32[64,128]{1,0:T(8,128)S(1)}, u32[]{:S(2)}, u32[]{:S(2)}) collective-permute-start(f32[64,128]{1,0:T(8,128)S(1)} %get-tuple-element.159), channel_id=1, source_target_pairs={{0,8},{4,12},{8,0},{12,4},{1,9},{5,13},{9,1},{13,5},{2,10},{6,14},... | collective-permute-start | bytes 98312 | tf_op jit(solution)/shard_map/ppermute | solution.py:278
  128.0 10.3 %collective-permute-start.27 = (bf16[64,2048]{1,0:T(8,128)(2,1)S(1)}, bf16[64,2048]{1,0:T(8,128)(2,1)S(1)}, u32[]{:S(2)}, u32[]{:S(2)}) collective-permute-start(bf16[64,2048]{1,0:T(8,128)(2,1)S(1)} %select_convert_fusion.3), channel_id=1, source_target_pairs={{0,8},{4,12},{8,0},{12,4},{1,9},{5,13},{9,1},{13,5},{2,10},{6,14},... | collective-permute-start | bytes 786440 | tf_op jit(solution)/shard_map/ppermute | solution.py:278
  128.3 4.3 %collective-permute-start.25 = (bf16[4,64,64]{2,1,0:T(8,128)(2,1)S(1)}, bf16[4,64,64]{2,1,0:T(8,128)(2,1)S(1)}, u32[]{:S(2)}, u32[]{:S(2)}) collective-permute-start(bf16[4,64,64]{2,1,0:T(8,128)(2,1)S(1)} %select_bitcast_fusion), channel_id=1, source_target_pairs={{0,2},{1,3},{2,0},{3,1},{4,6},{5,7},{6,4},{7,5},{8,10},{9,11},{10,... | collective-permute-start | bytes 98312 | tf_op jit(solution)/shard_map/ppermute | solution.py:418
  129.8 3.2 %collective-permute-start.26 = (bf16[4,64,64]{2,1,0:T(8,128)(2,1)S(1)}, bf16[4,64,64]{2,1,0:T(8,128)(2,1)S(1)}, u32[]{:S(2)}, u32[]{:S(2)}) collective-permute-start(bf16[4,64,64]{2,1,0:T(8,128)(2,1)S(1)} %select_bitcast_fusion), channel_id=1, source_target_pairs={{0,3},{1,0},{2,1},{3,2},{4,7},{5,4},{6,5},{7,6},{8,11},{9,8},{10,9... | collective-permute-start | bytes 98312 | tf_op jit(solution)/shard_map/ppermute | solution.py:418
  129.8 4.2 %collective-permute-start.24 = (bf16[4,64,64]{2,1,0:T(8,128)(2,1)S(1)}, bf16[4,64,64]{2,1,0:T(8,128)(2,1)S(1)}, u32[]{:S(2)}, u32[]{:S(2)}) collective-permute-start(bf16[4,64,64]{2,1,0:T(8,128)(2,1)S(1)} %select_bitcast_fusion), channel_id=1, source_target_pairs={{0,1},{1,2},{2,3},{3,0},{4,5},{5,6},{6,7},{7,4},{8,9},{9,10},{10,1... | collective-permute-start | bytes 98312 | tf_op jit(solution)/shard_map/ppermute | solution.py:418
  (15 other events, 66.7 us)

commit v20 on v19

--- a/solution.py
+++ b/solution.py
@@ -325,7 +325,7 @@
             bit //= 2
         return total.reshape(steps, extent, columns)
 
-    def gap(token, jobs):
+    def gap(token, jobs, ahead=()):
         nonlocal first_leg, second_leg
         for parts, received, keep, kind in first_leg:
             steps = sum(length for _, length in parts)
@@ -350,7 +350,7 @@
                 pick(values, (group_index + hop - rep_index) % n_rep).astype(jnp.bfloat16) for hop in range(1, n_rep)
             ])
             started.append((name, kept))
-        sends, token = lax.optimization_barrier((sends, token))
+        sends, token, ahead = lax.optimization_barrier((sends, token, ahead))
         first_sends, closed = lax.optimization_barrier(([job[1] for job in jobs], closed))
         ended.update(closed)
         first_leg = [
@@ -360,7 +360,7 @@
             (name, kept, [to_group(value, hop + 1) for hop, value in enumerate(sent)])
             for (name, kept), sent in zip(started, sends)
         ]
-        return sends
+        return sends, ahead
 
     factors = jnp.swapaxes(down_a, 1, 2)
 
@@ -374,7 +374,7 @@
     jobs = [([((0, 0), lead)], send, keep, jnp.bfloat16)]
     for piece, (step, shift) in enumerate(pieces):
         arrived = [received for _, received, _, _ in first_leg] if piece == 1 else []
-        sends = gap(send, jobs)
+        sends, _ = gap(send, jobs)
         own, panels, *_ = lax.optimization_barrier((remote[step, shift], panels, arrived, send))
         if piece == 0:
             panels, order = panels + [swap_tensor(panels[1], bits[1])], order + [bits[0] ^ bits[1]]
@@ -391,14 +391,16 @@
         jobs = [([(key, 1)], outs[at], outs[count + at], jnp.bfloat16) for at, key in enumerate(keys)]
         if last:
             last_ranks[shift] = outs[2 * count:]
-    gap(send, jobs)
     for shift, ranks in last_ranks.items():
         halved[RANK_NAME, shift] = second_half(ranks[1], swap_tensor(ranks[0], group // 2), 1, jnp.float32)[0]
     values = [halved[RANK_NAME, at] for at in range(n_rep)]
-    ended[RANK_NAME] = (pick(values, (group_index - rep_index) % n_rep), *[
-        to_group(pick(values, (group_index + hop - rep_index) % n_rep), hop) for hop in range(1, n_rep)
-    ])
-    rounded = gap(send, [])
+    ahead = [pick(values, (group_index + hop - rep_index) % n_rep) for hop in range(1, n_rep)]
+    _, ahead = gap(send, jobs, ahead)
+    ended[RANK_NAME] = (
+        pick(values, (group_index - rep_index) % n_rep),
+        *[to_group(value, hop + 1) for hop, value in enumerate(ahead)],
+    )
+    rounded, _ = gap(send, [])
 
     def rank_sum(name):
         kept, *received = [value[:, -rank_columns(factors):] for value in ended[name]]

time: 139 us -> 144 us (1.036)
  waiting for transfers between devices: 29.1 us -> 32.8 us
    ppermute x11, waiting for transfers between devices: 3.36 us -> 7.02 us  [swap_tensor(): return lax.ppermute(value, 'tp', [(i, i ^ bit) for i in range(n_tensor)])]
  transfers between devices with their start and end apart: 28 -> 28, of which waited for: 10 -> 12; matrix products, arithmetic and copies ran while one was open for 3% -> 3% of each run, Pallas kernels for 50% -> 48%
where the time goes in v20:
time: 144 us
  Pallas kernels  69.8 us (48%)
  waiting for transfers between devices  32.8 us (23%)
  starting transfers between devices  32.7 us (23%)
  local copies, waits for them, and re-layouts  7.36 us (5%)
    pallas_call x5, Pallas kernels, partial_products(): pl.pallas_call(functools.partial(matmul_body, spans, staged, apart), in_s...  66.5 us
    ppermute x5, waiting for transfers between devices, to_group(): lax.ppermute(value, 'tp', [(i, (i + moved) % n_tensor) for i in range(n_t...  15.8 us
    ppermute x11, starting transfers between devices, swap_tensor(): return lax.ppermute(value, 'tp', [(i, i ^ bit) for i in range(n_tensor)])  14 us
    ppermute x5, starting transfers between devices, to_group(): lax.ppermute(value, 'tp', [(i, (i + moved) % n_tensor) for i in range(n_t...  9.88 us
    ppermute x11, waiting for transfers between devices, swap_tensor(): return lax.ppermute(value, 'tp', [(i, i ^ bit) for i in range(n_tensor)])  7.02 us
    ppermute x4, waiting for transfers between devices, from_rep(): lax.ppermute(value, 'rep', [((i + shift) % n_rep, i) for i in range(n_rep)])  6.36 us
    ppermute x4, starting transfers between devices, from_rep(): lax.ppermute(value, 'rep', [((i + shift) % n_rep, i) for i in range(n_rep)])  6.27 us
    unnamed x36, local copies, waits for them, and re-layouts  4.29 us
  transfers between devices with their start and end apart: 28, of which 12 were waited for; matrix products, arithmetic and copies ran while one was open for 3% of the time, Pallas kernels for 48%

profile of v20, /device:TPU:0, one launch (start us, length us, event | category | flops | bytes accessed | tf_op | source)
XLA Modules:
  0.0 144.1 jit_solution(9923627273229660147)
XLA Ops:
  0.5 2.2 %slice.51 = bf16[1,64,7168]{2,1,0:T(8,128)(2,1)} slice(bf16[4,64,7168]{2,1,0:T(8,128)(2,1)} %refs_2_.7), slice={[0:1], [0:64], [0:7168]} | slice | bytes 1835008 | tf_op jit(solution)/shard_map/slice | solution.py:293
  2.7 2.6 %collective-permute-start.3 = (bf16[1,64,7168]{2,1,0:T(8,128)(2,1)}, bf16[1,64,7168]{2,1,0:T(8,128)(2,1)S(1)}, u32[]{:S(2)}, u32[]{:S(2)}) collective-permute-start(bf16[1,64,7168]{2,1,0:T(8,128)(2,1)} %slice.51), channel_id=1, source_target_pairs={{2,0},{0,2},{3,1},{1,3},{6,4},{4,6},{7,5},{5,7},{10,8},{8,10},{11,... | collective-permute-start | bytes 2752520 | tf_op jit(solution)/shard_map/ppermute | solution.py:271
  5.3 2.6 %collective-permute-start.4 = (bf16[1,64,2048]{2,1,0:T(8,128)(2,1)S(1)}, bf16[1,64,2048]{2,1,0:T(8,128)(2,1)}, u32[]{:S(2)}, u32[]{:S(2)}) collective-permute-start(bf16[1,64,2048]{2,1,0:T(8,128)(2,1)S(1)} %copy-done.7), channel_id=1, source_target_pairs={{0,8},{4,12},{8,0},{12,4},{1,9},{5,13},{9,1},{13,5},{2,10},{6,14},... | collective-permute-start | bytes 786440 | tf_op jit(solution)/shard_map/ppermute | solution.py:274
  7.9 1.6 %collective-permute-start.5 = (bf16[1,64,2048]{2,1,0:T(8,128)(2,1)S(1)}, bf16[1,64,2048]{2,1,0:T(8,128)(2,1)S(1)}, u32[]{:S(2)}, u32[]{:S(2)}) collective-permute-start(bf16[1,64,2048]{2,1,0:T(8,128)(2,1)S(1)} %copy-done.7), channel_id=1, source_target_pairs={{0,4},{4,0},{8,12},{12,8},{1,5},{5,1},{9,13},{13,9},{2,6},{6,2},{1... | collective-permute-start | bytes 786440 | tf_op jit(solution)/shard_map/ppermute | solution.py:274
  9.5 16.3 %partial_products.5 = (bf16[128,2176]{1,0:T(8,128)(2,1)S(1)}, f32[128,2176]{1,0:T(8,128)S(1)}, bf16[1,64,7168]{2,1,0:T(8,128)(2,1)}, bf16[1,64,7168]{2,1,0:T(8,128)(2,1)}, bf16[1,64,7168]{2,1,0:T(8,128)(2,1)}) custom-call(s32[1]{0:T(128)} %bitcast.1.pos_ref, bf16[4,64,7168]{2,1,0:T(8,128)(2,1)} %refs_2_.7, ...), custom_call_target="tpu_custom_call" | custom-call | tf_op jit(solution)/shard_map/partial_products/pallas_call | solution.py:145
  26.6 1.6 %collective-permute-start.2 = (bf16[1,64,7168]{2,1,0:T(8,128)(2,1)}, bf16[1,64,7168]{2,1,0:T(8,128)(2,1)}, u32[]{:S(2)}, u32[]{:S(2)}) collective-permute-start(bf16[1,64,7168]{2,1,0:T(8,128)(2,1)} %get-tuple-element.84), channel_id=1, source_target_pairs={{2,0},{0,2},{3,1},{1,3},{6,4},{4,6},{7,5},{5,7},{10,8},{8,10},{11,... | collective-permute-start | bytes 2752520 | tf_op jit(solution)/shard_map/ppermute | solution.py:271
  28.2 1.6 %collective-permute-start.7 = (bf16[128,2176]{1,0:T(8,128)(2,1)S(1)}, bf16[128,2176]{1,0:T(8,128)(2,1)S(1)}, u32[]{:S(2)}, u32[]{:S(2)}) collective-permute-start(bf16[128,2176]{1,0:T(8,128)(2,1)S(1)} %get-tuple-element.85), channel_id=1, source_target_pairs={{0,4},{4,0},{8,12},{12,8},{1,5},{5,1},{9,13},{13,9},{2,6},{6,2},{1... | collective-permute-start | bytes 1671176 | tf_op jit(solution)/shard_map/ppermute | solution.py:274
  30.2 13.4 %partial_products.6 = (bf16[64,2176]{1,0:T(8,128)(2,1)S(1)}, bf16[64,2176]{1,0:T(8,128)(2,1)S(1)}, f32[64,2176]{1,0:T(8,128)S(1)}, f32[64,2176]{1,0:T(8,128)S(1)}) custom-call(s32[1]{0:T(128)} %bitcast.1.pos_ref, bf16[1,64,7168]{2,1,0:T(8,128)(2,1)S(1)} %collective-permute-done.3.refs_0_, bf16[1,64,7168]{2,1,0:T(8,128)(2,1)S(1)} %collective-permute-done.8.refs_1_, ...), custom_call_target="tpu_custom_call" | custom-call | tf_op jit(solution)/shard_map/partial_products/pallas_call | solution.py:145
  45.9 2.6 %collective-permute-done.6 = bf16[1,64,2048]{2,1,0:T(8,128)(2,1)S(1)} collective-permute-done((bf16[1,64,2048]{2,1,0:T(8,128)(2,1)}, bf16[1,64,2048]{2,1,0:T(8,128)(2,1)S(1)}, u32[]{:S(2)}, u32[]{:S(2)}) %collective-permute-start.6) | collective-permute-done | bytes 262176 | tf_op jit(solution)/shard_map/ppermute | solution.py:274
  50.2 1.1 collective-permute-start.1
  53.3 1.6 %collective-permute-start.11 = (bf16[64,2176]{1,0:T(8,128)(2,1)}, bf16[64,2176]{1,0:T(8,128)(2,1)S(1)}, u32[]{:S(2)}, u32[]{:S(2)}) collective-permute-start(bf16[64,2176]{1,0:T(8,128)(2,1)} %copy-done.14), channel_id=1, source_target_pairs={{0,4},{4,0},{8,12},{12,8},{1,5},{5,1},{9,13},{13,9},{2,6},{6,2},{1... | collective-permute-start | bytes 835592 | tf_op jit(solution)/shard_map/ppermute | solution.py:274
  55.3 15.3 %partial_products.7 = (bf16[64,2176]{1,0:T(8,128)(2,1)S(1)}, bf16[64,2176]{1,0:T(8,128)(2,1)S(1)}, f32[64,2176]{1,0:T(8,128)S(1)}, f32[64,2176]{1,0:T(8,128)S(1)}) custom-call(s32[1]{0:T(128)} %bitcast.1.pos_ref, bf16[1,64,7168]{2,1,0:T(8,128)(2,1)} %collective-permute-done.2.refs_0_, bf16[1,64,7168]{2,1,0:T(8,128)(2,1)} %collective-permute-done.9.refs_1_, ...), custom_call_target="tpu_custom_call" | custom-call | tf_op jit(solution)/shard_map/partial_products/pallas_call | solution.py:145
  70.7 3.0 %collective-permute-done.1.refs_0_ = bf16[1,64,7168]{2,1,0:T(8,128)(2,1)S(1)} collective-permute-done((bf16[1,64,7168]{2,1,0:T(8,128)(2,1)}, bf16[1,64,7168]{2,1,0:T(8,128)(2,1)S(1)}, u32[]{:S(2)}, u32[]{:S(2)}) %collective-permute-start.1) | collective-permute-done | bytes 917536 | tf_op jit(solution)/shard_map/ppermute | solution.py:271
  73.7 1.6 %collective-permute-start.15 = (bf16[64,2176]{1,0:T(8,128)(2,1)S(1)}, bf16[64,2176]{1,0:T(8,128)(2,1)S(1)}, u32[]{:S(2)}, u32[]{:S(2)}) collective-permute-start(bf16[64,2176]{1,0:T(8,128)(2,1)S(1)} %get-tuple-element.126), channel_id=1, source_target_pairs={{0,4},{4,0},{8,12},{12,8},{1,5},{5,1},{9,13},{13,9},{2,6},{6,2},{1... | collective-permute-start | bytes 835592 | tf_op jit(solution)/shard_map/ppermute | solution.py:274
  75.4 2.7 %collective-permute-start.12 = (bf16[64,2176]{1,0:T(8,128)(2,1)S(1)}, bf16[64,2176]{1,0:T(8,128)(2,1)S(1)}, u32[]{:S(2)}, u32[]{:S(2)}) collective-permute-start(bf16[64,2176]{1,0:T(8,128)(2,1)S(1)} %select_convert_fusion.2), channel_id=1, source_target_pairs={{0,8},{4,12},{8,0},{12,4},{1,9},{5,13},{9,1},{13,5},{2,10},{6,14},... | collective-permute-start | bytes 835592 | tf_op jit(solution)/shard_map/ppermute | solution.py:278
  78.5 10.7 %partial_products.8 = (bf16[64,2176]{1,0:T(8,128)(2,1)S(1)}, f32[64,2176]{1,0:T(8,128)S(1)}) custom-call(s32[1]{0:T(128)} %bitcast.1.pos_ref, bf16[1,64,7168]{2,1,0:T(8,128)(2,1)S(1)} %collective-permute-done.1.refs_0_, bf16[1,64,7168]{2,1,0:T(8,128)(2,1)S(1)} %collective-permute-done.10.refs_1_, bf16[7168,2048]{1,0:T(8,128)(2,1)} %refs_2_.9, ...), custom_call_target="tpu_custom_call" | custom-call | tf_op jit(solution)/shard_map/partial_products/pallas_call | solution.py:145
  89.2 3.1 %collective-permute-done.13.refs_0_ = bf16[1,64,7168]{2,1,0:T(8,128)(2,1)S(1)} collective-permute-done((bf16[1,64,7168]{2,1,0:T(8,128)(2,1)}, bf16[1,64,7168]{2,1,0:T(8,128)(2,1)S(1)}, u32[]{:S(2)}, u32[]{:S(2)}) %collective-permute-start.13) | collective-permute-done | bytes 917536 | tf_op jit(solution)/shard_map/ppermute | solution.py:271
  92.6 2.8 %collective-permute-start.16 = (bf16[64,2176]{1,0:T(8,128)(2,1)S(1)}, bf16[64,2176]{1,0:T(8,128)(2,1)S(1)}, u32[]{:S(2)}, u32[]{:S(2)}) collective-permute-start(bf16[64,2176]{1,0:T(8,128)(2,1)S(1)} %select_convert_fusion.1), channel_id=1, source_target_pairs={{0,8},{4,12},{8,0},{12,4},{1,9},{5,13},{9,1},{13,5},{2,10},{6,14},... | collective-permute-start | bytes 835592 | tf_op jit(solution)/shard_map/ppermute | solution.py:278
  95.4 1.6 %collective-permute-start.17 = (bf16[64,2176]{1,0:T(8,128)(2,1)S(1)}, bf16[64,2176]{1,0:T(8,128)(2,1)S(1)}, u32[]{:S(2)}, u32[]{:S(2)}) collective-permute-start(bf16[64,2176]{1,0:T(8,128)(2,1)S(1)} %get-tuple-element.136), channel_id=1, source_target_pairs={{0,4},{4,0},{8,12},{12,8},{1,5},{5,1},{9,13},{13,9},{2,6},{6,2},{1... | collective-permute-start | bytes 835592 | tf_op jit(solution)/shard_map/ppermute | solution.py:274
  97.0 10.7 %partial_products.9 = (bf16[64,2048]{1,0:T(8,128)(2,1)S(1)}, f32[64,2048]{1,0:T(8,128)S(1)}, f32[64,128]{1,0:T(8,128)S(1)}, f32[64,128]{1,0:T(8,128)S(1)}) custom-call(s32[1]{0:T(128)} %bitcast.1.pos_ref, bf16[1,64,7168]{2,1,0:T(8,128)(2,1)S(1)} %collective-permute-done.13.refs_0_, bf16[1,64,7168]{2,1,0:T(8,128)(2,1)S(1)} %collective-permute-done.14.refs_1_, ...), custom_call_target="tpu_custom_call" | custom-call | tf_op jit(solution)/shard_map/partial_products/pallas_call | solution.py:145
  109.5 1.4 collective-permute-start.23
  111.0 2.0 %collective-permute-done.19 = f32[64,128]{1,0:T(8,128)S(1)} collective-permute-done((f32[64,128]{1,0:T(8,128)S(1)}, f32[64,128]{1,0:T(8,128)S(1)}, u32[]{:S(2)}, u32[]{:S(2)}) %collective-permute-start.19) | collective-permute-done | bytes 32800 | tf_op jit(solution)/shard_map/ppermute | solution.py:274
  113.1 1.8 %collective-permute-start.22 = (f32[64,128]{1,0:T(8,128)S(1)}, f32[64,128]{1,0:T(8,128)S(1)}, u32[]{:S(2)}, u32[]{:S(2)}) collective-permute-start(f32[64,128]{1,0:T(8,128)S(1)} %get-tuple-element.149), channel_id=1, source_target_pairs={{0,8},{4,12},{8,0},{12,4},{1,9},{5,13},{9,1},{13,5},{2,10},{6,14},... | collective-permute-start | bytes 98312 | tf_op jit(solution)/shard_map/ppermute | solution.py:278
  114.8 1.3 collective-permute-start.21
  116.1 2.3 %collective-permute-done.22 = f32[64,128]{1,0:T(8,128)S(1)} collective-permute-done((f32[64,128]{1,0:T(8,128)S(1)}, f32[64,128]{1,0:T(8,128)S(1)}, u32[]{:S(2)}, u32[]{:S(2)}) %collective-permute-start.22) | collective-permute-done | bytes 32800 | tf_op jit(solution)/shard_map/ppermute | solution.py:278
  118.4 2.3 %collective-permute-done.23 = bf16[64,2048]{1,0:T(8,128)(2,1)S(1)} collective-permute-done((bf16[64,2048]{1,0:T(8,128)(2,1)S(1)}, bf16[64,2048]{1,0:T(8,128)(2,1)S(1)}, u32[]{:S(2)}, u32[]{:S(2)}) %collective-permute-start.23) | collective-permute-done | bytes 262176 | tf_op jit(solution)/shard_map/ppermute | solution.py:274
  120.8 1.4 collective-permute-start.27
  122.2 12.6 %collective-permute-done.21.refs_9_ = bf16[64,2176]{1,0:T(8,128)(2,1)S(1)} collective-permute-done((bf16[64,2176]{1,0:T(8,128)(2,1)S(1)}, bf16[64,2176]{1,0:T(8,128)(2,1)S(1)}, u32[]{:S(2)}, u32[]{:S(2)}) %collective-permute-start.21) | collective-permute-done | bytes 278560 | tf_op jit(solution)/shard_map/ppermute | solution.py:278
  134.9 1.6 %collective-permute-start.25 = (bf16[4,64,64]{2,1,0:T(8,128)(2,1)S(1)}, bf16[4,64,64]{2,1,0:T(8,128)(2,1)S(1)}, u32[]{:S(2)}, u32[]{:S(2)}) collective-permute-start(bf16[4,64,64]{2,1,0:T(8,128)(2,1)S(1)} %select_bitcast_fusion), channel_id=1, source_target_pairs={{0,2},{1,3},{2,0},{3,1},{4,6},{5,7},{6,4},{7,5},{8,10},{9,11},{10,... | collective-permute-start | bytes 98312 | tf_op jit(solution)/shard_map/ppermute | solution.py:420
  137.0 2.2 %collective-permute-done.25 = bf16[4,64,64]{2,1,0:T(8,128)(2,1)S(1)} collective-permute-done((bf16[4,64,64]{2,1,0:T(8,128)(2,1)S(1)}, bf16[4,64,64]{2,1,0:T(8,128)(2,1)S(1)}, u32[]{:S(2)}, u32[]{:S(2)}) %collective-permute-start.25) | collective-permute-done | bytes 32800 | tf_op jit(solution)/shard_map/ppermute | solution.py:420
  139.6 1.0 collective-permute-done.24
  140.8 2.5 %finish_steps.1 = (bf16[4,64,2048]{2,1,0:T(8,128)(2,1)}, bf16[64,2048]{1,0:T(8,128)(2,1)S(1)}) custom-call(bf16[256,64]{1,0:T(8,128)(2,1)S(1)} %bitcast.30, s32[256,1]{1,0:T(8,128)S(1)} %copy-done.4, s32[4]{0:T(128)S(1)} %pad_add_fusion.order_ref, bf16[64,2048]{1,0:T(8,128)(2,1)S(1)} %bitcast.31, bf16[64,2048]{1,0:T(8,128)(2,1)} %bitcast.14.refs_1_, ...), custom_call_target="tpu_custom_call" | custom-call | tf_op jit(solution)/shard_map/finish_steps/pallas_call | solution.py:203
  (96 shorter events, 12.9 us)
Async XLA Ops:
  0.0 51.3 %copy-start = (s32[256,1]{0,1:T(1,128)S(1)}, s32[256,1]{0,1:T(1,128)}, u32[]{:S(2)}) copy-start(s32[256,1]{0,1:T(1,128)} %param.10) | copy-start | bytes 3076
  0.0 9.5 %collective-permute-start = (bf16[4,64,7168]{2,1,0:T(8,128)(2,1)}, bf16[4,64,7168]{2,1,0:T(8,128)(2,1)}, u32[]{:S(2)}, u32[]{:S(2)}) collective-permute-start(bf16[4,64,7168]{2,1,0:T(8,128)(2,1)} %refs_2_.7), channel_id=1, source_target_pairs={{0,1},{1,0},{2,3},{3,2},{4,5},{5,4},{6,7},{7,6},{8,9},{9,8},{10,11... | collective-permute-start | bytes 11010056 | tf_op jit(solution)/shard_map/ppermute | solution.py:268
  2.7 23.8 %collective-permute-start.3 = (bf16[1,64,7168]{2,1,0:T(8,128)(2,1)}, bf16[1,64,7168]{2,1,0:T(8,128)(2,1)S(1)}, u32[]{:S(2)}, u32[]{:S(2)}) collective-permute-start(bf16[1,64,7168]{2,1,0:T(8,128)(2,1)} %slice.51), channel_id=1, source_target_pairs={{2,0},{0,2},{3,1},{1,3},{6,4},{4,6},{7,5},{5,7},{10,8},{8,10},{11,... | collective-permute-start | bytes 2752520 | tf_op jit(solution)/shard_map/ppermute | solution.py:271
  5.3 20.5 %collective-permute-start.4 = (bf16[1,64,2048]{2,1,0:T(8,128)(2,1)S(1)}, bf16[1,64,2048]{2,1,0:T(8,128)(2,1)}, u32[]{:S(2)}, u32[]{:S(2)}) collective-permute-start(bf16[1,64,2048]{2,1,0:T(8,128)(2,1)S(1)} %copy-done.7), channel_id=1, source_target_pairs={{0,8},{4,12},{8,0},{12,4},{1,9},{5,13},{9,1},{13,5},{2,10},{6,14},... | collective-permute-start | bytes 786440 | tf_op jit(solution)/shard_map/ppermute | solution.py:274
  7.9 18.0 %collective-permute-start.5 = (bf16[1,64,2048]{2,1,0:T(8,128)(2,1)S(1)}, bf16[1,64,2048]{2,1,0:T(8,128)(2,1)S(1)}, u32[]{:S(2)}, u32[]{:S(2)}) collective-permute-start(bf16[1,64,2048]{2,1,0:T(8,128)(2,1)S(1)} %copy-done.7), channel_id=1, source_target_pairs={{0,4},{4,0},{8,12},{12,8},{1,5},{5,1},{9,13},{13,9},{2,6},{6,2},{1... | collective-permute-start | bytes 786440 | tf_op jit(solution)/shard_map/ppermute | solution.py:274
  26.6 3.7 %collective-permute-start.8 = (bf16[1,64,7168]{2,1,0:T(8,128)(2,1)S(1)}, bf16[1,64,7168]{2,1,0:T(8,128)(2,1)S(1)}, u32[]{:S(2)}, u32[]{:S(2)}) collective-permute-start(bf16[1,64,7168]{2,1,0:T(8,128)(2,1)S(1)} %collective-permute-done.3.refs_0_), channel_id=1, source_target_pairs={{0,1},{1,0},{2,3},{3,2},{4,5},{5,4},{6,7},{7,6},{8,9},{9,8},{10,11... | collective-permute-start | bytes 2752520 | tf_op jit(solution)/shard_map/ppermute | solution.py:268
  26.6 24.8 %copy-start.17 = (s32[4]{0:T(128)S(1)}, s32[4]{0:T(128)}, u32[]{:S(2)}) copy-start(s32[4]{0:T(128)} %param.11) | copy-start | bytes 52
  26.6 23.1 %collective-permute-start.2 = (bf16[1,64,7168]{2,1,0:T(8,128)(2,1)}, bf16[1,64,7168]{2,1,0:T(8,128)(2,1)}, u32[]{:S(2)}, u32[]{:S(2)}) collective-permute-start(bf16[1,64,7168]{2,1,0:T(8,128)(2,1)} %get-tuple-element.84), channel_id=1, source_target_pairs={{2,0},{0,2},{3,1},{1,3},{6,4},{4,6},{7,5},{5,7},{10,8},{8,10},{11,... | collective-permute-start | bytes 2752520 | tf_op jit(solution)/shard_map/ppermute | solution.py:271
  28.2 21.1 %collective-permute-start.7 = (bf16[128,2176]{1,0:T(8,128)(2,1)S(1)}, bf16[128,2176]{1,0:T(8,128)(2,1)S(1)}, u32[]{:S(2)}, u32[]{:S(2)}) collective-permute-start(bf16[128,2176]{1,0:T(8,128)(2,1)S(1)} %get-tuple-element.85), channel_id=1, source_target_pairs={{0,4},{4,0},{8,12},{12,8},{1,5},{5,1},{9,13},{13,9},{2,6},{6,2},{1... | collective-permute-start | bytes 1671176 | tf_op jit(solution)/shard_map/ppermute | solution.py:274
  29.8 18.8 %collective-permute-start.6 = (bf16[1,64,2048]{2,1,0:T(8,128)(2,1)}, bf16[1,64,2048]{2,1,0:T(8,128)(2,1)S(1)}, u32[]{:S(2)}, u32[]{:S(2)}) collective-permute-start(bf16[1,64,2048]{2,1,0:T(8,128)(2,1)} %collective-permute-done.4), channel_id=1, source_target_pairs={{0,4},{4,0},{8,12},{12,8},{1,5},{5,1},{9,13},{13,9},{2,6},{6,2},{1... | collective-permute-start | bytes 786440 | tf_op jit(solution)/shard_map/ppermute | solution.py:274
  49.7 5.7 %collective-permute-start.9 = (bf16[1,64,7168]{2,1,0:T(8,128)(2,1)}, bf16[1,64,7168]{2,1,0:T(8,128)(2,1)}, u32[]{:S(2)}, u32[]{:S(2)}) collective-permute-start(bf16[1,64,7168]{2,1,0:T(8,128)(2,1)} %collective-permute-done.2.refs_0_), channel_id=1, source_target_pairs={{0,1},{1,0},{2,3},{3,2},{4,5},{5,4},{6,7},{7,6},{8,9},{9,8},{10,11... | collective-permute-start | bytes 2752520 | tf_op jit(solution)/shard_map/ppermute | solution.py:268
  50.2 23.4 %collective-permute-start.1 = (bf16[1,64,7168]{2,1,0:T(8,128)(2,1)}, bf16[1,64,7168]{2,1,0:T(8,128)(2,1)S(1)}, u32[]{:S(2)}, u32[]{:S(2)}) collective-permute-start(bf16[1,64,7168]{2,1,0:T(8,128)(2,1)} %get-tuple-element.83), channel_id=1, source_target_pairs={{2,0},{0,2},{3,1},{1,3},{6,4},{4,6},{7,5},{5,7},{10,8},{8,10},{11,... | collective-permute-start | bytes 2752520 | tf_op jit(solution)/shard_map/ppermute | solution.py:271
  52.3 40.0 %collective-permute-start.13 = (bf16[1,64,7168]{2,1,0:T(8,128)(2,1)}, bf16[1,64,7168]{2,1,0:T(8,128)(2,1)S(1)}, u32[]{:S(2)}, u32[]{:S(2)}) collective-permute-start(bf16[1,64,7168]{2,1,0:T(8,128)(2,1)} %get-tuple-element.117), channel_id=1, source_target_pairs={{2,0},{0,2},{3,1},{1,3},{6,4},{4,6},{7,5},{5,7},{10,8},{8,10},{11,... | collective-permute-start | bytes 2752520 | tf_op jit(solution)/shard_map/ppermute | solution.py:271
  53.3 20.3 %copy-start.16 = (bf16[128,2176]{1,0:T(8,128)(2,1)S(1)}, bf16[128,2176]{1,0:T(8,128)(2,1)}, u32[]{:S(2)}) copy-start(bf16[128,2176]{1,0:T(8,128)(2,1)} %copy-done.15) | copy-start | bytes 1671172
  53.3 22.1 %collective-permute-start.11 = (bf16[64,2176]{1,0:T(8,128)(2,1)}, bf16[64,2176]{1,0:T(8,128)(2,1)S(1)}, u32[]{:S(2)}, u32[]{:S(2)}) collective-permute-start(bf16[64,2176]{1,0:T(8,128)(2,1)} %copy-done.14), channel_id=1, source_target_pairs={{0,4},{4,0},{8,12},{12,8},{1,5},{5,1},{9,13},{13,9},{2,6},{6,2},{1... | collective-permute-start | bytes 835592 | tf_op jit(solution)/shard_map/ppermute | solution.py:274
  54.9 56.0 %collective-permute-start.18 = (bf16[64,2176]{1,0:T(8,128)(2,1)}, bf16[64,2176]{1,0:T(8,128)(2,1)S(1)}, u32[]{:S(2)}, u32[]{:S(2)}) collective-permute-start(bf16[64,2176]{1,0:T(8,128)(2,1)} %copy-done.13), channel_id=1, source_target_pairs={{0,4},{4,0},{8,12},{12,8},{1,5},{5,1},{9,13},{13,9},{2,6},{6,2},{1... | collective-permute-start | bytes 835592 | tf_op jit(solution)/shard_map/ppermute | solution.py:274
  73.6 4.5 %collective-permute-start.10 = (bf16[1,64,7168]{2,1,0:T(8,128)(2,1)S(1)}, bf16[1,64,7168]{2,1,0:T(8,128)(2,1)S(1)}, u32[]{:S(2)}, u32[]{:S(2)}) collective-permute-start(bf16[1,64,7168]{2,1,0:T(8,128)(2,1)S(1)} %collective-permute-done.1.refs_0_), channel_id=1, source_target_pairs={{0,1},{1,0},{2,3},{3,2},{4,5},{5,4},{6,7},{7,6},{8,9},{9,8},{10,11... | collective-permute-start | bytes 2752520 | tf_op jit(solution)/shard_map/ppermute | solution.py:268
  73.7 18.6 %collective-permute-start.15 = (bf16[64,2176]{1,0:T(8,128)(2,1)S(1)}, bf16[64,2176]{1,0:T(8,128)(2,1)S(1)}, u32[]{:S(2)}, u32[]{:S(2)}) collective-permute-start(bf16[64,2176]{1,0:T(8,128)(2,1)S(1)} %get-tuple-element.126), channel_id=1, source_target_pairs={{0,4},{4,0},{8,12},{12,8},{1,5},{5,1},{9,13},{13,9},{2,6},{6,2},{1... | collective-permute-start | bytes 835592 | tf_op jit(solution)/shard_map/ppermute | solution.py:274
  75.4 17.1 %collective-permute-start.12 = (bf16[64,2176]{1,0:T(8,128)(2,1)S(1)}, bf16[64,2176]{1,0:T(8,128)(2,1)S(1)}, u32[]{:S(2)}, u32[]{:S(2)}) collective-permute-start(bf16[64,2176]{1,0:T(8,128)(2,1)S(1)} %select_convert_fusion.2), channel_id=1, source_target_pairs={{0,8},{4,12},{8,0},{12,4},{1,9},{5,13},{9,1},{13,5},{2,10},{6,14},... | collective-permute-start | bytes 835592 | tf_op jit(solution)/shard_map/ppermute | solution.py:278
  78.1 18.8 %collective-permute-start.20 = (bf16[64,2176]{1,0:T(8,128)(2,1)S(1)}, bf16[64,2176]{1,0:T(8,128)(2,1)S(1)}, u32[]{:S(2)}, u32[]{:S(2)}) collective-permute-start(bf16[64,2176]{1,0:T(8,128)(2,1)S(1)} %get-tuple-element.145), channel_id=1, source_target_pairs={{0,4},{4,0},{8,12},{12,8},{1,5},{5,1},{9,13},{13,9},{2,6},{6,2},{1... | collective-permute-start | bytes 835592 | tf_op jit(solution)/shard_map/ppermute | solution.py:274
  92.3 4.7 %collective-permute-start.14 = (bf16[1,64,7168]{2,1,0:T(8,128)(2,1)S(1)}, bf16[1,64,7168]{2,1,0:T(8,128)(2,1)S(1)}, u32[]{:S(2)}, u32[]{:S(2)}) collective-permute-start(bf16[1,64,7168]{2,1,0:T(8,128)(2,1)S(1)} %collective-permute-done.13.refs_0_), channel_id=1, source_target_pairs={{0,1},{1,0},{2,3},{3,2},{4,5},{5,4},{6,7},{7,6},{8,9},{9,8},{10,11... | collective-permute-start | bytes 2752520 | tf_op jit(solution)/shard_map/ppermute | solution.py:268
  92.6 15.2 %copy-start.5 = (bf16[64,2176]{1,0:T(8,128)(2,1)}, bf16[64,2176]{1,0:T(8,128)(2,1)S(1)}, u32[]{:S(2)}) copy-start(bf16[64,2176]{1,0:T(8,128)(2,1)S(1)} %collective-permute-done.12.refs_5_) | copy-start | bytes 835588
  92.6 16.2 %collective-permute-start.16 = (bf16[64,2176]{1,0:T(8,128)(2,1)S(1)}, bf16[64,2176]{1,0:T(8,128)(2,1)S(1)}, u32[]{:S(2)}, u32[]{:S(2)}) collective-permute-start(bf16[64,2176]{1,0:T(8,128)(2,1)S(1)} %select_convert_fusion.1), channel_id=1, source_target_pairs={{0,8},{4,12},{8,0},{12,4},{1,9},{5,13},{9,1},{13,5},{2,10},{6,14},... | collective-permute-start | bytes 835592 | tf_op jit(solution)/shard_map/ppermute | solution.py:278
  95.4 15.5 %collective-permute-start.17 = (bf16[64,2176]{1,0:T(8,128)(2,1)S(1)}, bf16[64,2176]{1,0:T(8,128)(2,1)S(1)}, u32[]{:S(2)}, u32[]{:S(2)}) collective-permute-start(bf16[64,2176]{1,0:T(8,128)(2,1)S(1)} %get-tuple-element.136), channel_id=1, source_target_pairs={{0,4},{4,0},{8,12},{12,8},{1,5},{5,1},{9,13},{13,9},{2,6},{6,2},{1... | collective-permute-start | bytes 835592 | tf_op jit(solution)/shard_map/ppermute | solution.py:274
  108.8 4.3 %collective-permute-start.19 = (f32[64,128]{1,0:T(8,128)S(1)}, f32[64,128]{1,0:T(8,128)S(1)}, u32[]{:S(2)}, u32[]{:S(2)}) collective-permute-start(f32[64,128]{1,0:T(8,128)S(1)} %get-tuple-element.142), channel_id=1, source_target_pairs={{0,4},{4,0},{8,12},{12,8},{1,5},{5,1},{9,13},{13,9},{2,6},{6,2},{1... | collective-permute-start | bytes 98312 | tf_op jit(solution)/shard_map/ppermute | solution.py:274
  109.5 11.3 %collective-permute-start.23 = (bf16[64,2048]{1,0:T(8,128)(2,1)S(1)}, bf16[64,2048]{1,0:T(8,128)(2,1)S(1)}, u32[]{:S(2)}, u32[]{:S(2)}) collective-permute-start(bf16[64,2048]{1,0:T(8,128)(2,1)S(1)} %get-tuple-element.152), channel_id=1, source_target_pairs={{0,4},{4,0},{8,12},{12,8},{1,5},{5,1},{9,13},{13,9},{2,6},{6,2},{1... | collective-permute-start | bytes 786440 | tf_op jit(solution)/shard_map/ppermute | solution.py:274
  113.1 5.3 %collective-permute-start.22 = (f32[64,128]{1,0:T(8,128)S(1)}, f32[64,128]{1,0:T(8,128)S(1)}, u32[]{:S(2)}, u32[]{:S(2)}) collective-permute-start(f32[64,128]{1,0:T(8,128)S(1)} %get-tuple-element.149), channel_id=1, source_target_pairs={{0,8},{4,12},{8,0},{12,4},{1,9},{5,13},{9,1},{13,5},{2,10},{6,14},... | collective-permute-start | bytes 98312 | tf_op jit(solution)/shard_map/ppermute | solution.py:278
  114.8 19.9 %collective-permute-start.21 = (bf16[64,2176]{1,0:T(8,128)(2,1)S(1)}, bf16[64,2176]{1,0:T(8,128)(2,1)S(1)}, u32[]{:S(2)}, u32[]{:S(2)}) collective-permute-start(bf16[64,2176]{1,0:T(8,128)(2,1)S(1)} %get-tuple-element.146), channel_id=1, source_target_pairs={{0,8},{4,12},{8,0},{12,4},{1,9},{5,13},{9,1},{13,5},{2,10},{6,14},... | collective-permute-start | bytes 835592 | tf_op jit(solution)/shard_map/ppermute | solution.py:278
  120.8 22.5 %collective-permute-start.27 = (bf16[64,2048]{1,0:T(8,128)(2,1)S(1)}, bf16[64,2048]{1,0:T(8,128)(2,1)S(1)}, u32[]{:S(2)}, u32[]{:S(2)}) collective-permute-start(bf16[64,2048]{1,0:T(8,128)(2,1)S(1)} %select_convert_fusion.3), channel_id=1, source_target_pairs={{0,8},{4,12},{8,0},{12,4},{1,9},{5,13},{9,1},{13,5},{2,10},{6,14},... | collective-permute-start | bytes 786440 | tf_op jit(solution)/shard_map/ppermute | solution.py:278
  134.9 4.3 %collective-permute-start.25 = (bf16[4,64,64]{2,1,0:T(8,128)(2,1)S(1)}, bf16[4,64,64]{2,1,0:T(8,128)(2,1)S(1)}, u32[]{:S(2)}, u32[]{:S(2)}) collective-permute-start(bf16[4,64,64]{2,1,0:T(8,128)(2,1)S(1)} %select_bitcast_fusion), channel_id=1, source_target_pairs={{0,2},{1,3},{2,0},{3,1},{4,6},{5,7},{6,4},{7,5},{8,10},{9,11},{10,... | collective-permute-start | bytes 98312 | tf_op jit(solution)/shard_map/ppermute | solution.py:420
  136.5 3.2 %collective-permute-start.26 = (bf16[4,64,64]{2,1,0:T(8,128)(2,1)S(1)}, bf16[4,64,64]{2,1,0:T(8,128)(2,1)S(1)}, u32[]{:S(2)}, u32[]{:S(2)}) collective-permute-start(bf16[4,64,64]{2,1,0:T(8,128)(2,1)S(1)} %select_bitcast_fusion), channel_id=1, source_target_pairs={{0,3},{1,0},{2,1},{3,2},{4,7},{5,4},{6,5},{7,6},{8,11},{9,8},{10,9... | collective-permute-start | bytes 98312 | tf_op jit(solution)/shard_map/ppermute | solution.py:420
  136.5 4.2 %collective-permute-start.24 = (bf16[4,64,64]{2,1,0:T(8,128)(2,1)S(1)}, bf16[4,64,64]{2,1,0:T(8,128)(2,1)S(1)}, u32[]{:S(2)}, u32[]{:S(2)}) collective-permute-start(bf16[4,64,64]{2,1,0:T(8,128)(2,1)S(1)} %select_bitcast_fusion), channel_id=1, source_target_pairs={{0,1},{1,2},{2,3},{3,0},{4,5},{5,6},{6,7},{7,4},{8,9},{9,10},{10,1... | collective-permute-start | bytes 98312 | tf_op jit(solution)/shard_map/ppermute | solution.py:420
  (15 other events, 68.7 us)

commit v21 on v20

--- a/solution.py
+++ b/solution.py
@@ -400,7 +400,9 @@
         pick(values, (group_index - rep_index) % n_rep),
         *[to_group(value, hop + 1) for hop, value in enumerate(ahead)],
     )
-    rounded, _ = gap(send, [])
+    rounded, pending = gap(send, [], {name: received for name, _, received in second_leg})
+    for name, received in pending.items():
+        ended[name] = (ended[name][0], *received)
 
     def rank_sum(name):
         kept, *received = [value[:, -rank_columns(factors):] for value in ended[name]]

time: 144 us -> 147 us (1.021)
  waiting for transfers between devices: 32.8 us -> 37.4 us
    ppermute x5, waiting for transfers between devices: 15.8 us -> 20.4 us  [to_group(): lax.ppermute(value, 'tp', [(i, (i + moved) % n_tensor) for i in range(n_t...]
  transfers between devices with their start and end apart: 28 -> 28, of which waited for: 12 -> 13; matrix products, arithmetic and copies ran while one was open for 3% -> 3% of each run, Pallas kernels for 48% -> 47%
where the time goes in v21:
time: 147 us
  Pallas kernels  69.8 us (47%)
  waiting for transfers between devices  37.4 us (25%)
  starting transfers between devices  31.3 us (21%)
  local copies, waits for them, and re-layouts  7.36 us (5%)
    pallas_call x5, Pallas kernels, partial_products(): pl.pallas_call(functools.partial(matmul_body, spans, staged, apart), in_s...  66.5 us
    ppermute x5, waiting for transfers between devices, to_group(): lax.ppermute(value, 'tp', [(i, (i + moved) % n_tensor) for i in range(n_t...  20.4 us
    ppermute x11, starting transfers between devices, swap_tensor(): return lax.ppermute(value, 'tp', [(i, i ^ bit) for i in range(n_tensor)])  14 us
    ppermute x5, starting transfers between devices, to_group(): lax.ppermute(value, 'tp', [(i, (i + moved) % n_tensor) for i in range(n_t...  8.51 us
    ppermute x11, waiting for transfers between devices, swap_tensor(): return lax.ppermute(value, 'tp', [(i, i ^ bit) for i in range(n_tensor)])  7.02 us
    ppermute x4, waiting for transfers between devices, from_rep(): lax.ppermute(value, 'rep', [((i + shift) % n_rep, i) for i in range(n_rep)])  6.36 us
    ppermute x4, starting transfers between devices, from_rep(): lax.ppermute(value, 'rep', [((i + shift) % n_rep, i) for i in range(n_rep)])  6.27 us
    unnamed x36, local copies, waits for them, and re-layouts  4.29 us
  transfers between devices with their start and end apart: 28, of which 13 were waited for; matrix products, arithmetic and copies ran while one was open for 3% of the time, Pallas kernels for 47%

profile of v21, /device:TPU:0, one launch (start us, length us, event | category | flops | bytes accessed | tf_op | source)
XLA Modules:
  0.0 147.3 jit_solution(7145891978161506421)
XLA Ops:
  0.5 2.2 %slice.51 = bf16[1,64,7168]{2,1,0:T(8,128)(2,1)} slice(bf16[4,64,7168]{2,1,0:T(8,128)(2,1)} %refs_2_.7), slice={[0:1], [0:64], [0:7168]} | slice | bytes 1835008 | tf_op jit(solution)/shard_map/slice | solution.py:293
  2.7 2.6 %collective-permute-start.3 = (bf16[1,64,7168]{2,1,0:T(8,128)(2,1)}, bf16[1,64,7168]{2,1,0:T(8,128)(2,1)S(1)}, u32[]{:S(2)}, u32[]{:S(2)}) collective-permute-start(bf16[1,64,7168]{2,1,0:T(8,128)(2,1)} %slice.51), channel_id=1, source_target_pairs={{2,0},{0,2},{3,1},{1,3},{6,4},{4,6},{7,5},{5,7},{10,8},{8,10},{11,... | collective-permute-start | bytes 2752520 | tf_op jit(solution)/shard_map/ppermute | solution.py:271
  5.3 2.6 %collective-permute-start.4 = (bf16[1,64,2048]{2,1,0:T(8,128)(2,1)S(1)}, bf16[1,64,2048]{2,1,0:T(8,128)(2,1)}, u32[]{:S(2)}, u32[]{:S(2)}) collective-permute-start(bf16[1,64,2048]{2,1,0:T(8,128)(2,1)S(1)} %copy-done.7), channel_id=1, source_target_pairs={{0,8},{4,12},{8,0},{12,4},{1,9},{5,13},{9,1},{13,5},{2,10},{6,14},... | collective-permute-start | bytes 786440 | tf_op jit(solution)/shard_map/ppermute | solution.py:274
  7.9 1.6 %collective-permute-start.5 = (bf16[1,64,2048]{2,1,0:T(8,128)(2,1)S(1)}, bf16[1,64,2048]{2,1,0:T(8,128)(2,1)S(1)}, u32[]{:S(2)}, u32[]{:S(2)}) collective-permute-start(bf16[1,64,2048]{2,1,0:T(8,128)(2,1)S(1)} %copy-done.7), channel_id=1, source_target_pairs={{0,4},{4,0},{8,12},{12,8},{1,5},{5,1},{9,13},{13,9},{2,6},{6,2},{1... | collective-permute-start | bytes 786440 | tf_op jit(solution)/shard_map/ppermute | solution.py:274
  9.5 16.3 %partial_products.5 = (bf16[128,2176]{1,0:T(8,128)(2,1)S(1)}, f32[128,2176]{1,0:T(8,128)S(1)}, bf16[1,64,7168]{2,1,0:T(8,128)(2,1)}, bf16[1,64,7168]{2,1,0:T(8,128)(2,1)}, bf16[1,64,7168]{2,1,0:T(8,128)(2,1)}) custom-call(s32[1]{0:T(128)} %bitcast.1.pos_ref, bf16[4,64,7168]{2,1,0:T(8,128)(2,1)} %refs_2_.7, ...), custom_call_target="tpu_custom_call" | custom-call | tf_op jit(solution)/shard_map/partial_products/pallas_call | solution.py:145
  26.6 1.6 %collective-permute-start.2 = (bf16[1,64,7168]{2,1,0:T(8,128)(2,1)}, bf16[1,64,7168]{2,1,0:T(8,128)(2,1)}, u32[]{:S(2)}, u32[]{:S(2)}) collective-permute-start(bf16[1,64,7168]{2,1,0:T(8,128)(2,1)} %get-tuple-element.84), channel_id=1, source_target_pairs={{2,0},{0,2},{3,1},{1,3},{6,4},{4,6},{7,5},{5,7},{10,8},{8,10},{11,... | collective-permute-start | bytes 2752520 | tf_op jit(solution)/shard_map/ppermute | solution.py:271
  28.2 1.6 %collective-permute-start.7 = (bf16[128,2176]{1,0:T(8,128)(2,1)S(1)}, bf16[128,2176]{1,0:T(8,128)(2,1)S(1)}, u32[]{:S(2)}, u32[]{:S(2)}) collective-permute-start(bf16[128,2176]{1,0:T(8,128)(2,1)S(1)} %get-tuple-element.85), channel_id=1, source_target_pairs={{0,4},{4,0},{8,12},{12,8},{1,5},{5,1},{9,13},{13,9},{2,6},{6,2},{1... | collective-permute-start | bytes 1671176 | tf_op jit(solution)/shard_map/ppermute | solution.py:274
  30.2 13.4 %partial_products.6 = (bf16[64,2176]{1,0:T(8,128)(2,1)S(1)}, bf16[64,2176]{1,0:T(8,128)(2,1)S(1)}, f32[64,2176]{1,0:T(8,128)S(1)}, f32[64,2176]{1,0:T(8,128)S(1)}) custom-call(s32[1]{0:T(128)} %bitcast.1.pos_ref, bf16[1,64,7168]{2,1,0:T(8,128)(2,1)S(1)} %collective-permute-done.3.refs_0_, bf16[1,64,7168]{2,1,0:T(8,128)(2,1)S(1)} %collective-permute-done.8.refs_1_, ...), custom_call_target="tpu_custom_call" | custom-call | tf_op jit(solution)/shard_map/partial_products/pallas_call | solution.py:145
  45.9 2.6 %collective-permute-done.6 = bf16[1,64,2048]{2,1,0:T(8,128)(2,1)S(1)} collective-permute-done((bf16[1,64,2048]{2,1,0:T(8,128)(2,1)}, bf16[1,64,2048]{2,1,0:T(8,128)(2,1)S(1)}, u32[]{:S(2)}, u32[]{:S(2)}) %collective-permute-start.6) | collective-permute-done | bytes 262176 | tf_op jit(solution)/shard_map/ppermute | solution.py:274
  50.2 1.1 collective-permute-start.1
  53.3 1.6 %collective-permute-start.11 = (bf16[64,2176]{1,0:T(8,128)(2,1)}, bf16[64,2176]{1,0:T(8,128)(2,1)S(1)}, u32[]{:S(2)}, u32[]{:S(2)}) collective-permute-start(bf16[64,2176]{1,0:T(8,128)(2,1)} %copy-done.14), channel_id=1, source_target_pairs={{0,4},{4,0},{8,12},{12,8},{1,5},{5,1},{9,13},{13,9},{2,6},{6,2},{1... | collective-permute-start | bytes 835592 | tf_op jit(solution)/shard_map/ppermute | solution.py:274
  55.3 15.3 %partial_products.7 = (bf16[64,2176]{1,0:T(8,128)(2,1)S(1)}, bf16[64,2176]{1,0:T(8,128)(2,1)S(1)}, f32[64,2176]{1,0:T(8,128)S(1)}, f32[64,2176]{1,0:T(8,128)S(1)}) custom-call(s32[1]{0:T(128)} %bitcast.1.pos_ref, bf16[1,64,7168]{2,1,0:T(8,128)(2,1)} %collective-permute-done.2.refs_0_, bf16[1,64,7168]{2,1,0:T(8,128)(2,1)} %collective-permute-done.9.refs_1_, ...), custom_call_target="tpu_custom_call" | custom-call | tf_op jit(solution)/shard_map/partial_products/pallas_call | solution.py:145
  70.7 3.0 %collective-permute-done.1.refs_0_ = bf16[1,64,7168]{2,1,0:T(8,128)(2,1)S(1)} collective-permute-done((bf16[1,64,7168]{2,1,0:T(8,128)(2,1)}, bf16[1,64,7168]{2,1,0:T(8,128)(2,1)S(1)}, u32[]{:S(2)}, u32[]{:S(2)}) %collective-permute-start.1) | collective-permute-done | bytes 917536 | tf_op jit(solution)/shard_map/ppermute | solution.py:271
  73.7 1.6 %collective-permute-start.15 = (bf16[64,2176]{1,0:T(8,128)(2,1)S(1)}, bf16[64,2176]{1,0:T(8,128)(2,1)S(1)}, u32[]{:S(2)}, u32[]{:S(2)}) collective-permute-start(bf16[64,2176]{1,0:T(8,128)(2,1)S(1)} %get-tuple-element.126), channel_id=1, source_target_pairs={{0,4},{4,0},{8,12},{12,8},{1,5},{5,1},{9,13},{13,9},{2,6},{6,2},{1... | collective-permute-start | bytes 835592 | tf_op jit(solution)/shard_map/ppermute | solution.py:274
  75.4 2.7 %collective-permute-start.12 = (bf16[64,2176]{1,0:T(8,128)(2,1)S(1)}, bf16[64,2176]{1,0:T(8,128)(2,1)S(1)}, u32[]{:S(2)}, u32[]{:S(2)}) collective-permute-start(bf16[64,2176]{1,0:T(8,128)(2,1)S(1)} %select_convert_fusion.2), channel_id=1, source_target_pairs={{0,8},{4,12},{8,0},{12,4},{1,9},{5,13},{9,1},{13,5},{2,10},{6,14},... | collective-permute-start | bytes 835592 | tf_op jit(solution)/shard_map/ppermute | solution.py:278
  78.5 10.7 %partial_products.8 = (bf16[64,2176]{1,0:T(8,128)(2,1)S(1)}, f32[64,2176]{1,0:T(8,128)S(1)}) custom-call(s32[1]{0:T(128)} %bitcast.1.pos_ref, bf16[1,64,7168]{2,1,0:T(8,128)(2,1)S(1)} %collective-permute-done.1.refs_0_, bf16[1,64,7168]{2,1,0:T(8,128)(2,1)S(1)} %collective-permute-done.10.refs_1_, bf16[7168,2048]{1,0:T(8,128)(2,1)} %refs_2_.9, ...), custom_call_target="tpu_custom_call" | custom-call | tf_op jit(solution)/shard_map/partial_products/pallas_call | solution.py:145
  89.2 3.1 %collective-permute-done.13.refs_0_ = bf16[1,64,7168]{2,1,0:T(8,128)(2,1)S(1)} collective-permute-done((bf16[1,64,7168]{2,1,0:T(8,128)(2,1)}, bf16[1,64,7168]{2,1,0:T(8,128)(2,1)S(1)}, u32[]{:S(2)}, u32[]{:S(2)}) %collective-permute-start.13) | collective-permute-done | bytes 917536 | tf_op jit(solution)/shard_map/ppermute | solution.py:271
  92.6 2.8 %collective-permute-start.16 = (bf16[64,2176]{1,0:T(8,128)(2,1)S(1)}, bf16[64,2176]{1,0:T(8,128)(2,1)S(1)}, u32[]{:S(2)}, u32[]{:S(2)}) collective-permute-start(bf16[64,2176]{1,0:T(8,128)(2,1)S(1)} %select_convert_fusion.1), channel_id=1, source_target_pairs={{0,8},{4,12},{8,0},{12,4},{1,9},{5,13},{9,1},{13,5},{2,10},{6,14},... | collective-permute-start | bytes 835592 | tf_op jit(solution)/shard_map/ppermute | solution.py:278
  95.4 1.6 %collective-permute-start.17 = (bf16[64,2176]{1,0:T(8,128)(2,1)S(1)}, bf16[64,2176]{1,0:T(8,128)(2,1)S(1)}, u32[]{:S(2)}, u32[]{:S(2)}) collective-permute-start(bf16[64,2176]{1,0:T(8,128)(2,1)S(1)} %get-tuple-element.136), channel_id=1, source_target_pairs={{0,4},{4,0},{8,12},{12,8},{1,5},{5,1},{9,13},{13,9},{2,6},{6,2},{1... | collective-permute-start | bytes 835592 | tf_op jit(solution)/shard_map/ppermute | solution.py:274
  97.0 10.7 %partial_products.9 = (bf16[64,2048]{1,0:T(8,128)(2,1)S(1)}, f32[64,2048]{1,0:T(8,128)S(1)}, f32[64,128]{1,0:T(8,128)S(1)}, f32[64,128]{1,0:T(8,128)S(1)}) custom-call(s32[1]{0:T(128)} %bitcast.1.pos_ref, bf16[1,64,7168]{2,1,0:T(8,128)(2,1)S(1)} %collective-permute-done.13.refs_0_, bf16[1,64,7168]{2,1,0:T(8,128)(2,1)S(1)} %collective-permute-done.14.refs_1_, ...), custom_call_target="tpu_custom_call" | custom-call | tf_op jit(solution)/shard_map/partial_products/pallas_call | solution.py:145
  109.5 1.4 collective-permute-start.22
  111.0 2.0 %collective-permute-done.19 = f32[64,128]{1,0:T(8,128)S(1)} collective-permute-done((f32[64,128]{1,0:T(8,128)S(1)}, f32[64,128]{1,0:T(8,128)S(1)}, u32[]{:S(2)}, u32[]{:S(2)}) %collective-permute-start.19) | collective-permute-done | bytes 32800 | tf_op jit(solution)/shard_map/ppermute | solution.py:274
  113.1 1.8 %collective-permute-start.23 = (f32[64,128]{1,0:T(8,128)S(1)}, f32[64,128]{1,0:T(8,128)S(1)}, u32[]{:S(2)}, u32[]{:S(2)}) collective-permute-start(f32[64,128]{1,0:T(8,128)S(1)} %get-tuple-element.152), channel_id=1, source_target_pairs={{0,8},{4,12},{8,0},{12,4},{1,9},{5,13},{9,1},{13,5},{2,10},{6,14},... | collective-permute-start | bytes 98312 | tf_op jit(solution)/shard_map/ppermute | solution.py:278
  114.8 1.3 collective-permute-start.21
  116.1 2.3 %collective-permute-done.23 = f32[64,128]{1,0:T(8,128)S(1)} collective-permute-done((f32[64,128]{1,0:T(8,128)S(1)}, f32[64,128]{1,0:T(8,128)S(1)}, u32[]{:S(2)}, u32[]{:S(2)}) %collective-permute-start.23) | collective-permute-done | bytes 32800 | tf_op jit(solution)/shard_map/ppermute | solution.py:278
  118.4 2.3 %collective-permute-done.22 = bf16[64,2048]{1,0:T(8,128)(2,1)S(1)} collective-permute-done((bf16[64,2048]{1,0:T(8,128)(2,1)S(1)}, bf16[64,2048]{1,0:T(8,128)(2,1)S(1)}, u32[]{:S(2)}, u32[]{:S(2)}) %collective-permute-start.22) | collective-permute-done | bytes 262176 | tf_op jit(solution)/shard_map/ppermute | solution.py:274
  120.8 9.5 %collective-permute-done.21.refs_9_ = bf16[64,2176]{1,0:T(8,128)(2,1)S(1)} collective-permute-done((bf16[64,2176]{1,0:T(8,128)(2,1)S(1)}, bf16[64,2176]{1,0:T(8,128)(2,1)S(1)}, u32[]{:S(2)}, u32[]{:S(2)}) %collective-permute-start.21) | collective-permute-done | bytes 278560 | tf_op jit(solution)/shard_map/ppermute | solution.py:278
  130.5 1.6 %collective-permute-start.25 = (bf16[4,64,64]{2,1,0:T(8,128)(2,1)S(1)}, bf16[4,64,64]{2,1,0:T(8,128)(2,1)S(1)}, u32[]{:S(2)}, u32[]{:S(2)}) collective-permute-start(bf16[4,64,64]{2,1,0:T(8,128)(2,1)S(1)} %select_bitcast_fusion), channel_id=1, source_target_pairs={{0,2},{1,3},{2,0},{3,1},{4,6},{5,7},{6,4},{7,5},{8,10},{9,11},{10,... | collective-permute-start | bytes 98312 | tf_op jit(solution)/shard_map/ppermute | solution.py:422
  132.7 2.2 %collective-permute-done.25 = bf16[4,64,64]{2,1,0:T(8,128)(2,1)S(1)} collective-permute-done((bf16[4,64,64]{2,1,0:T(8,128)(2,1)S(1)}, bf16[4,64,64]{2,1,0:T(8,128)(2,1)S(1)}, u32[]{:S(2)}, u32[]{:S(2)}) %collective-permute-start.25) | collective-permute-done | bytes 32800 | tf_op jit(solution)/shard_map/ppermute | solution.py:422
  135.2 1.0 collective-permute-done.24
  136.4 2.5 %finish_steps.1 = (bf16[4,64,2048]{2,1,0:T(8,128)(2,1)}, bf16[64,2048]{1,0:T(8,128)(2,1)S(1)}) custom-call(bf16[256,64]{1,0:T(8,128)(2,1)S(1)} %bitcast.30, s32[256,1]{1,0:T(8,128)S(1)} %copy-done.4, s32[4]{0:T(128)S(1)} %pad_add_fusion.order_ref, bf16[64,2048]{1,0:T(8,128)(2,1)S(1)} %bitcast.31, bf16[64,2048]{1,0:T(8,128)(2,1)} %bitcast.14.refs_1_, ...), custom_call_target="tpu_custom_call" | custom-call | tf_op jit(solution)/shard_map/finish_steps/pallas_call | solution.py:203
  138.9 7.6 %collective-permute-done.27.refs_1_ = bf16[64,2048]{1,0:T(8,128)(2,1)S(1)} collective-permute-done((bf16[64,2048]{1,0:T(8,128)(2,1)S(1)}, bf16[64,2048]{1,0:T(8,128)(2,1)S(1)}, u32[]{:S(2)}, u32[]{:S(2)}) %collective-permute-start.27) | collective-permute-done | bytes 262176 | tf_op jit(solution)/shard_map/ppermute | solution.py:278
  (96 shorter events, 12.9 us)
Async XLA Ops:
  0.0 51.3 %copy-start = (s32[256,1]{0,1:T(1,128)S(1)}, s32[256,1]{0,1:T(1,128)}, u32[]{:S(2)}) copy-start(s32[256,1]{0,1:T(1,128)} %param.10) | copy-start | bytes 3076
  0.0 9.5 %collective-permute-start = (bf16[4,64,7168]{2,1,0:T(8,128)(2,1)}, bf16[4,64,7168]{2,1,0:T(8,128)(2,1)}, u32[]{:S(2)}, u32[]{:S(2)}) collective-permute-start(bf16[4,64,7168]{2,1,0:T(8,128)(2,1)} %refs_2_.7), channel_id=1, source_target_pairs={{0,1},{1,0},{2,3},{3,2},{4,5},{5,4},{6,7},{7,6},{8,9},{9,8},{10,11... | collective-permute-start | bytes 11010056 | tf_op jit(solution)/shard_map/ppermute | solution.py:268
  2.7 23.8 %collective-permute-start.3 = (bf16[1,64,7168]{2,1,0:T(8,128)(2,1)}, bf16[1,64,7168]{2,1,0:T(8,128)(2,1)S(1)}, u32[]{:S(2)}, u32[]{:S(2)}) collective-permute-start(bf16[1,64,7168]{2,1,0:T(8,128)(2,1)} %slice.51), channel_id=1, source_target_pairs={{2,0},{0,2},{3,1},{1,3},{6,4},{4,6},{7,5},{5,7},{10,8},{8,10},{11,... | collective-permute-start | bytes 2752520 | tf_op jit(solution)/shard_map/ppermute | solution.py:271
  5.3 20.5 %collective-permute-start.4 = (bf16[1,64,2048]{2,1,0:T(8,128)(2,1)S(1)}, bf16[1,64,2048]{2,1,0:T(8,128)(2,1)}, u32[]{:S(2)}, u32[]{:S(2)}) collective-permute-start(bf16[1,64,2048]{2,1,0:T(8,128)(2,1)S(1)} %copy-done.7), channel_id=1, source_target_pairs={{0,8},{4,12},{8,0},{12,4},{1,9},{5,13},{9,1},{13,5},{2,10},{6,14},... | collective-permute-start | bytes 786440 | tf_op jit(solution)/shard_map/ppermute | solution.py:274
  7.9 18.0 %collective-permute-start.5 = (bf16[1,64,2048]{2,1,0:T(8,128)(2,1)S(1)}, bf16[1,64,2048]{2,1,0:T(8,128)(2,1)S(1)}, u32[]{:S(2)}, u32[]{:S(2)}) collective-permute-start(bf16[1,64,2048]{2,1,0:T(8,128)(2,1)S(1)} %copy-done.7), channel_id=1, source_target_pairs={{0,4},{4,0},{8,12},{12,8},{1,5},{5,1},{9,13},{13,9},{2,6},{6,2},{1... | collective-permute-start | bytes 786440 | tf_op jit(solution)/shard_map/ppermute | solution.py:274
  26.6 3.7 %collective-permute-start.8 = (bf16[1,64,7168]{2,1,0:T(8,128)(2,1)S(1)}, bf16[1,64,7168]{2,1,0:T(8,128)(2,1)S(1)}, u32[]{:S(2)}, u32[]{:S(2)}) collective-permute-start(bf16[1,64,7168]{2,1,0:T(8,128)(2,1)S(1)} %collective-permute-done.3.refs_0_), channel_id=1, source_target_pairs={{0,1},{1,0},{2,3},{3,2},{4,5},{5,4},{6,7},{7,6},{8,9},{9,8},{10,11... | collective-permute-start | bytes 2752520 | tf_op jit(solution)/shard_map/ppermute | solution.py:268
  26.6 24.8 %copy-start.17 = (s32[4]{0:T(128)S(1)}, s32[4]{0:T(128)}, u32[]{:S(2)}) copy-start(s32[4]{0:T(128)} %param.11) | copy-start | bytes 52
  26.6 23.1 %collective-permute-start.2 = (bf16[1,64,7168]{2,1,0:T(8,128)(2,1)}, bf16[1,64,7168]{2,1,0:T(8,128)(2,1)}, u32[]{:S(2)}, u32[]{:S(2)}) collective-permute-start(bf16[1,64,7168]{2,1,0:T(8,128)(2,1)} %get-tuple-element.84), channel_id=1, source_target_pairs={{2,0},{0,2},{3,1},{1,3},{6,4},{4,6},{7,5},{5,7},{10,8},{8,10},{11,... | collective-permute-start | bytes 2752520 | tf_op jit(solution)/shard_map/ppermute | solution.py:271
  28.2 21.1 %collective-permute-start.7 = (bf16[128,2176]{1,0:T(8,128)(2,1)S(1)}, bf16[128,2176]{1,0:T(8,128)(2,1)S(1)}, u32[]{:S(2)}, u32[]{:S(2)}) collective-permute-start(bf16[128,2176]{1,0:T(8,128)(2,1)S(1)} %get-tuple-element.85), channel_id=1, source_target_pairs={{0,4},{4,0},{8,12},{12,8},{1,5},{5,1},{9,13},{13,9},{2,6},{6,2},{1... | collective-permute-start | bytes 1671176 | tf_op jit(solution)/shard_map/ppermute | solution.py:274
  29.8 18.8 %collective-permute-start.6 = (bf16[1,64,2048]{2,1,0:T(8,128)(2,1)}, bf16[1,64,2048]{2,1,0:T(8,128)(2,1)S(1)}, u32[]{:S(2)}, u32[]{:S(2)}) collective-permute-start(bf16[1,64,2048]{2,1,0:T(8,128)(2,1)} %collective-permute-done.4), channel_id=1, source_target_pairs={{0,4},{4,0},{8,12},{12,8},{1,5},{5,1},{9,13},{13,9},{2,6},{6,2},{1... | collective-permute-start | bytes 786440 | tf_op jit(solution)/shard_map/ppermute | solution.py:274
  49.7 5.7 %collective-permute-start.9 = (bf16[1,64,7168]{2,1,0:T(8,128)(2,1)}, bf16[1,64,7168]{2,1,0:T(8,128)(2,1)}, u32[]{:S(2)}, u32[]{:S(2)}) collective-permute-start(bf16[1,64,7168]{2,1,0:T(8,128)(2,1)} %collective-permute-done.2.refs_0_), channel_id=1, source_target_pairs={{0,1},{1,0},{2,3},{3,2},{4,5},{5,4},{6,7},{7,6},{8,9},{9,8},{10,11... | collective-permute-start | bytes 2752520 | tf_op jit(solution)/shard_map/ppermute | solution.py:268
  50.2 23.4 %collective-permute-start.1 = (bf16[1,64,7168]{2,1,0:T(8,128)(2,1)}, bf16[1,64,7168]{2,1,0:T(8,128)(2,1)S(1)}, u32[]{:S(2)}, u32[]{:S(2)}) collective-permute-start(bf16[1,64,7168]{2,1,0:T(8,128)(2,1)} %get-tuple-element.83), channel_id=1, source_target_pairs={{2,0},{0,2},{3,1},{1,3},{6,4},{4,6},{7,5},{5,7},{10,8},{8,10},{11,... | collective-permute-start | bytes 2752520 | tf_op jit(solution)/shard_map/ppermute | solution.py:271
  52.3 40.0 %collective-permute-start.13 = (bf16[1,64,7168]{2,1,0:T(8,128)(2,1)}, bf16[1,64,7168]{2,1,0:T(8,128)(2,1)S(1)}, u32[]{:S(2)}, u32[]{:S(2)}) collective-permute-start(bf16[1,64,7168]{2,1,0:T(8,128)(2,1)} %get-tuple-element.117), channel_id=1, source_target_pairs={{2,0},{0,2},{3,1},{1,3},{6,4},{4,6},{7,5},{5,7},{10,8},{8,10},{11,... | collective-permute-start | bytes 2752520 | tf_op jit(solution)/shard_map/ppermute | solution.py:271
  53.3 20.3 %copy-start.16 = (bf16[128,2176]{1,0:T(8,128)(2,1)S(1)}, bf16[128,2176]{1,0:T(8,128)(2,1)}, u32[]{:S(2)}) copy-start(bf16[128,2176]{1,0:T(8,128)(2,1)} %copy-done.15) | copy-start | bytes 1671172
  53.3 22.1 %collective-permute-start.11 = (bf16[64,2176]{1,0:T(8,128)(2,1)}, bf16[64,2176]{1,0:T(8,128)(2,1)S(1)}, u32[]{:S(2)}, u32[]{:S(2)}) collective-permute-start(bf16[64,2176]{1,0:T(8,128)(2,1)} %copy-done.14), channel_id=1, source_target_pairs={{0,4},{4,0},{8,12},{12,8},{1,5},{5,1},{9,13},{13,9},{2,6},{6,2},{1... | collective-permute-start | bytes 835592 | tf_op jit(solution)/shard_map/ppermute | solution.py:274
  54.9 56.0 %collective-permute-start.18 = (bf16[64,2176]{1,0:T(8,128)(2,1)}, bf16[64,2176]{1,0:T(8,128)(2,1)S(1)}, u32[]{:S(2)}, u32[]{:S(2)}) collective-permute-start(bf16[64,2176]{1,0:T(8,128)(2,1)} %copy-done.13), channel_id=1, source_target_pairs={{0,4},{4,0},{8,12},{12,8},{1,5},{5,1},{9,13},{13,9},{2,6},{6,2},{1... | collective-permute-start | bytes 835592 | tf_op jit(solution)/shard_map/ppermute | solution.py:274
  73.6 4.5 %collective-permute-start.10 = (bf16[1,64,7168]{2,1,0:T(8,128)(2,1)S(1)}, bf16[1,64,7168]{2,1,0:T(8,128)(2,1)S(1)}, u32[]{:S(2)}, u32[]{:S(2)}) collective-permute-start(bf16[1,64,7168]{2,1,0:T(8,128)(2,1)S(1)} %collective-permute-done.1.refs_0_), channel_id=1, source_target_pairs={{0,1},{1,0},{2,3},{3,2},{4,5},{5,4},{6,7},{7,6},{8,9},{9,8},{10,11... | collective-permute-start | bytes 2752520 | tf_op jit(solution)/shard_map/ppermute | solution.py:268
  73.7 18.6 %collective-permute-start.15 = (bf16[64,2176]{1,0:T(8,128)(2,1)S(1)}, bf16[64,2176]{1,0:T(8,128)(2,1)S(1)}, u32[]{:S(2)}, u32[]{:S(2)}) collective-permute-start(bf16[64,2176]{1,0:T(8,128)(2,1)S(1)} %get-tuple-element.126), channel_id=1, source_target_pairs={{0,4},{4,0},{8,12},{12,8},{1,5},{5,1},{9,13},{13,9},{2,6},{6,2},{1... | collective-permute-start | bytes 835592 | tf_op jit(solution)/shard_map/ppermute | solution.py:274
  75.4 17.1 %collective-permute-start.12 = (bf16[64,2176]{1,0:T(8,128)(2,1)S(1)}, bf16[64,2176]{1,0:T(8,128)(2,1)S(1)}, u32[]{:S(2)}, u32[]{:S(2)}) collective-permute-start(bf16[64,2176]{1,0:T(8,128)(2,1)S(1)} %select_convert_fusion.2), channel_id=1, source_target_pairs={{0,8},{4,12},{8,0},{12,4},{1,9},{5,13},{9,1},{13,5},{2,10},{6,14},... | collective-permute-start | bytes 835592 | tf_op jit(solution)/shard_map/ppermute | solution.py:278
  78.1 18.8 %collective-permute-start.20 = (bf16[64,2176]{1,0:T(8,128)(2,1)S(1)}, bf16[64,2176]{1,0:T(8,128)(2,1)S(1)}, u32[]{:S(2)}, u32[]{:S(2)}) collective-permute-start(bf16[64,2176]{1,0:T(8,128)(2,1)S(1)} %get-tuple-element.145), channel_id=1, source_target_pairs={{0,4},{4,0},{8,12},{12,8},{1,5},{5,1},{9,13},{13,9},{2,6},{6,2},{1... | collective-permute-start | bytes 835592 | tf_op jit(solution)/shard_map/ppermute | solution.py:274
  92.3 4.7 %collective-permute-start.14 = (bf16[1,64,7168]{2,1,0:T(8,128)(2,1)S(1)}, bf16[1,64,7168]{2,1,0:T(8,128)(2,1)S(1)}, u32[]{:S(2)}, u32[]{:S(2)}) collective-permute-start(bf16[1,64,7168]{2,1,0:T(8,128)(2,1)S(1)} %collective-permute-done.13.refs_0_), channel_id=1, source_target_pairs={{0,1},{1,0},{2,3},{3,2},{4,5},{5,4},{6,7},{7,6},{8,9},{9,8},{10,11... | collective-permute-start | bytes 2752520 | tf_op jit(solution)/shard_map/ppermute | solution.py:268
  92.6 15.2 %copy-start.5 = (bf16[64,2176]{1,0:T(8,128)(2,1)}, bf16[64,2176]{1,0:T(8,128)(2,1)S(1)}, u32[]{:S(2)}) copy-start(bf16[64,2176]{1,0:T(8,128)(2,1)S(1)} %collective-permute-done.12.refs_5_) | copy-start | bytes 835588
  92.6 16.2 %collective-permute-start.16 = (bf16[64,2176]{1,0:T(8,128)(2,1)S(1)}, bf16[64,2176]{1,0:T(8,128)(2,1)S(1)}, u32[]{:S(2)}, u32[]{:S(2)}) collective-permute-start(bf16[64,2176]{1,0:T(8,128)(2,1)S(1)} %select_convert_fusion.1), channel_id=1, source_target_pairs={{0,8},{4,12},{8,0},{12,4},{1,9},{5,13},{9,1},{13,5},{2,10},{6,14},... | collective-permute-start | bytes 835592 | tf_op jit(solution)/shard_map/ppermute | solution.py:278
  95.4 15.5 %collective-permute-start.17 = (bf16[64,2176]{1,0:T(8,128)(2,1)S(1)}, bf16[64,2176]{1,0:T(8,128)(2,1)S(1)}, u32[]{:S(2)}, u32[]{:S(2)}) collective-permute-start(bf16[64,2176]{1,0:T(8,128)(2,1)S(1)} %get-tuple-element.136), channel_id=1, source_target_pairs={{0,4},{4,0},{8,12},{12,8},{1,5},{5,1},{9,13},{13,9},{2,6},{6,2},{1... | collective-permute-start | bytes 835592 | tf_op jit(solution)/shard_map/ppermute | solution.py:274
  108.8 4.3 %collective-permute-start.19 = (f32[64,128]{1,0:T(8,128)S(1)}, f32[64,128]{1,0:T(8,128)S(1)}, u32[]{:S(2)}, u32[]{:S(2)}) collective-permute-start(f32[64,128]{1,0:T(8,128)S(1)} %get-tuple-element.142), channel_id=1, source_target_pairs={{0,4},{4,0},{8,12},{12,8},{1,5},{5,1},{9,13},{13,9},{2,6},{6,2},{1... | collective-permute-start | bytes 98312 | tf_op jit(solution)/shard_map/ppermute | solution.py:274
  109.5 11.3 %collective-permute-start.22 = (bf16[64,2048]{1,0:T(8,128)(2,1)S(1)}, bf16[64,2048]{1,0:T(8,128)(2,1)S(1)}, u32[]{:S(2)}, u32[]{:S(2)}) collective-permute-start(bf16[64,2048]{1,0:T(8,128)(2,1)S(1)} %get-tuple-element.150), channel_id=1, source_target_pairs={{0,4},{4,0},{8,12},{12,8},{1,5},{5,1},{9,13},{13,9},{2,6},{6,2},{1... | collective-permute-start | bytes 786440 | tf_op jit(solution)/shard_map/ppermute | solution.py:274
  113.1 5.3 %collective-permute-start.23 = (f32[64,128]{1,0:T(8,128)S(1)}, f32[64,128]{1,0:T(8,128)S(1)}, u32[]{:S(2)}, u32[]{:S(2)}) collective-permute-start(f32[64,128]{1,0:T(8,128)S(1)} %get-tuple-element.152), channel_id=1, source_target_pairs={{0,8},{4,12},{8,0},{12,4},{1,9},{5,13},{9,1},{13,5},{2,10},{6,14},... | collective-permute-start | bytes 98312 | tf_op jit(solution)/shard_map/ppermute | solution.py:278
  114.8 15.5 %collective-permute-start.21 = (bf16[64,2176]{1,0:T(8,128)(2,1)S(1)}, bf16[64,2176]{1,0:T(8,128)(2,1)S(1)}, u32[]{:S(2)}, u32[]{:S(2)}) collective-permute-start(bf16[64,2176]{1,0:T(8,128)(2,1)S(1)} %get-tuple-element.146), channel_id=1, source_target_pairs={{0,8},{4,12},{8,0},{12,4},{1,9},{5,13},{9,1},{13,5},{2,10},{6,14},... | collective-permute-start | bytes 835592 | tf_op jit(solution)/shard_map/ppermute | solution.py:278
  130.5 4.3 %collective-permute-start.25 = (bf16[4,64,64]{2,1,0:T(8,128)(2,1)S(1)}, bf16[4,64,64]{2,1,0:T(8,128)(2,1)S(1)}, u32[]{:S(2)}, u32[]{:S(2)}) collective-permute-start(bf16[4,64,64]{2,1,0:T(8,128)(2,1)S(1)} %select_bitcast_fusion), channel_id=1, source_target_pairs={{0,2},{1,3},{2,0},{3,1},{4,6},{5,7},{6,4},{7,5},{8,10},{9,11},{10,... | collective-permute-start | bytes 98312 | tf_op jit(solution)/shard_map/ppermute | solution.py:422
  132.1 3.2 %collective-permute-start.26 = (bf16[4,64,64]{2,1,0:T(8,128)(2,1)S(1)}, bf16[4,64,64]{2,1,0:T(8,128)(2,1)S(1)}, u32[]{:S(2)}, u32[]{:S(2)}) collective-permute-start(bf16[4,64,64]{2,1,0:T(8,128)(2,1)S(1)} %select_bitcast_fusion), channel_id=1, source_target_pairs={{0,3},{1,0},{2,1},{3,2},{4,7},{5,4},{6,5},{7,6},{8,11},{9,8},{10,9... | collective-permute-start | bytes 98312 | tf_op jit(solution)/shard_map/ppermute | solution.py:422
  132.1 4.2 %collective-permute-start.24 = (bf16[4,64,64]{2,1,0:T(8,128)(2,1)S(1)}, bf16[4,64,64]{2,1,0:T(8,128)(2,1)S(1)}, u32[]{:S(2)}, u32[]{:S(2)}) collective-permute-start(bf16[4,64,64]{2,1,0:T(8,128)(2,1)S(1)} %select_bitcast_fusion), channel_id=1, source_target_pairs={{0,1},{1,2},{2,3},{3,0},{4,5},{5,6},{6,7},{7,4},{8,9},{9,10},{10,1... | collective-permute-start | bytes 98312 | tf_op jit(solution)/shard_map/ppermute | solution.py:422
  132.6 13.9 %collective-permute-start.27 = (bf16[64,2048]{1,0:T(8,128)(2,1)S(1)}, bf16[64,2048]{1,0:T(8,128)(2,1)S(1)}, u32[]{:S(2)}, u32[]{:S(2)}) collective-permute-start(bf16[64,2048]{1,0:T(8,128)(2,1)S(1)} %select_convert_fusion.3), channel_id=1, source_target_pairs={{0,8},{4,12},{8,0},{12,4},{1,9},{5,13},{9,1},{13,5},{2,10},{6,14},... | collective-permute-start | bytes 786440 | tf_op jit(solution)/shard_map/ppermute | solution.py:278
  (15 other events, 68.7 us)

commit v22 on v15

--- a/solution.py
+++ b/solution.py
@@ -10,7 +10,7 @@
 ADAPTER_SCALE = 0.5
 BLOCK_N = 256
 BLOCK = 1024
-BUFFERS = 4
+BUFFERS = 5
 RANK_NAME = 1000
 VMEM_BYTES = 20 * 1024 * 1024
 

time: 139 us -> 139 us (level)
  Pallas kernels: 69.7 us -> 73.6 us
  starting transfers between devices: 29.2 us -> 27 us
  waiting for transfers between devices: 29.8 us -> 28.4 us
    pallas_call x5, Pallas kernels: 66.4 us -> 70.3 us  [partial_products(): pl.pallas_call(functools.partial(matmul_body, spans, staged, apart), in_s...]
    ppermute x4, waiting for transfers between devices: 9.48 us -> 7.21 us  [from_rep(): lax.ppermute(value, 'rep', [((i + shift) % n_rep, i) for i in range(n_rep)])]
  transfers between devices with their start and end apart: 28 -> 28, of which waited for: 10 -> 10; matrix products, arithmetic and copies ran while one was open for 4% -> 4% of each run, Pallas kernels for 50% -> 52%
where the time goes in v22:
time: 139 us
  Pallas kernels  73.6 us (53%)
  waiting for transfers between devices  28.4 us (20%)
  starting transfers between devices  27 us (19%)
  local copies, waits for them, and re-layouts  7.73 us (6%)
  other arithmetic  2.21 us (2%)
    pallas_call x5, Pallas kernels, partial_products(): pl.pallas_call(functools.partial(matmul_body, spans, staged, apart), in_s...  70.3 us
    ppermute x5, waiting for transfers between devices, to_group(): lax.ppermute(value, 'tp', [(i, (i + moved) % n_tensor) for i in range(n_t...  15.7 us
    ppermute x11, starting transfers between devices, swap_tensor(): return lax.ppermute(value, 'tp', [(i, i ^ bit) for i in range(n_tensor)])  12.8 us
    ppermute x5, starting transfers between devices, to_group(): lax.ppermute(value, 'tp', [(i, (i + moved) % n_tensor) for i in range(n_t...  7.21 us
    ppermute x4, waiting for transfers between devices, from_rep(): lax.ppermute(value, 'rep', [((i + shift) % n_rep, i) for i in range(n_rep)])  7.21 us
    unnamed x34, local copies, waits for them, and re-layouts  4.63 us
    ppermute x4, starting transfers between devices, from_rep(): lax.ppermute(value, 'rep', [((i + shift) % n_rep, i) for i in range(n_rep)])  4.34 us
    ppermute x3, waiting for transfers between devices, per_device(): lax.ppermute(masked, ('rep', 'sub'), [(i, (i + turn) % n_owners) for i in...  3.59 us
  transfers between devices with their start and end apart: 28, of which 10 were waited for; matrix products, arithmetic and copies ran while one was open for 4% of the time, Pallas kernels for 52%

profile of v22, /device:TPU:0, one launch (start us, length us, event | category | flops | bytes accessed | tf_op | source)
XLA Modules:
  0.0 139.2 jit_solution(14105877767490024637)
XLA Ops:
  0.5 2.2 %slice.51 = bf16[1,64,7168]{2,1,0:T(8,128)(2,1)} slice(bf16[4,64,7168]{2,1,0:T(8,128)(2,1)} %refs_2_.7), slice={[0:1], [0:64], [0:7168]} | slice | bytes 1835008 | tf_op jit(solution)/shard_map/slice | solution.py:293
  2.7 2.6 %collective-permute-start.3 = (bf16[1,64,7168]{2,1,0:T(8,128)(2,1)}, bf16[1,64,7168]{2,1,0:T(8,128)(2,1)S(1)}, u32[]{:S(2)}, u32[]{:S(2)}) collective-permute-start(bf16[1,64,7168]{2,1,0:T(8,128)(2,1)} %slice.51), channel_id=1, source_target_pairs={{2,0},{0,2},{3,1},{1,3},{6,4},{4,6},{7,5},{5,7},{10,8},{8,10},{11,... | collective-permute-start | bytes 2752520 | tf_op jit(solution)/shard_map/ppermute | solution.py:271
  5.3 2.6 %collective-permute-start.4 = (bf16[1,64,2048]{2,1,0:T(8,128)(2,1)S(1)}, bf16[1,64,2048]{2,1,0:T(8,128)(2,1)}, u32[]{:S(2)}, u32[]{:S(2)}) collective-permute-start(bf16[1,64,2048]{2,1,0:T(8,128)(2,1)S(1)} %copy-done.7), channel_id=1, source_target_pairs={{0,8},{4,12},{8,0},{12,4},{1,9},{5,13},{9,1},{13,5},{2,10},{6,14},... | collective-permute-start | bytes 786440 | tf_op jit(solution)/shard_map/ppermute | solution.py:274
  7.9 1.6 %collective-permute-start.5 = (bf16[1,64,2048]{2,1,0:T(8,128)(2,1)S(1)}, bf16[1,64,2048]{2,1,0:T(8,128)(2,1)S(1)}, u32[]{:S(2)}, u32[]{:S(2)}) collective-permute-start(bf16[1,64,2048]{2,1,0:T(8,128)(2,1)S(1)} %copy-done.7), channel_id=1, source_target_pairs={{0,4},{4,0},{8,12},{12,8},{1,5},{5,1},{9,13},{13,9},{2,6},{6,2},{1... | collective-permute-start | bytes 786440 | tf_op jit(solution)/shard_map/ppermute | solution.py:274
  9.5 17.0 %partial_products.5 = (bf16[128,2176]{1,0:T(8,128)(2,1)S(1)}, f32[128,2176]{1,0:T(8,128)S(1)}, bf16[1,64,7168]{2,1,0:T(8,128)(2,1)}, bf16[1,64,7168]{2,1,0:T(8,128)(2,1)}, bf16[1,64,7168]{2,1,0:T(8,128)(2,1)}) custom-call(s32[1]{0:T(128)} %bitcast.1.pos_ref, bf16[4,64,7168]{2,1,0:T(8,128)(2,1)} %refs_2_.7, ...), custom_call_target="tpu_custom_call" | custom-call | tf_op jit(solution)/shard_map/partial_products/pallas_call | solution.py:145
  26.5 0.9 copy-done.13
  28.7 1.4 %collective-permute-start.6 = (bf16[1,64,2048]{2,1,0:T(8,128)(2,1)}, bf16[1,64,2048]{2,1,0:T(8,128)(2,1)S(1)}, u32[]{:S(2)}, u32[]{:S(2)}) collective-permute-start(bf16[1,64,2048]{2,1,0:T(8,128)(2,1)} %collective-permute-done.4), channel_id=1, source_target_pairs={{0,4},{4,0},{8,12},{12,8},{1,5},{5,1},{9,13},{13,9},{2,6},{6,2},{1... | collective-permute-start | bytes 786440 | tf_op jit(solution)/shard_map/ppermute | solution.py:274
  30.5 15.9 %partial_products.6 = (bf16[64,2176]{1,0:T(8,128)(2,1)S(1)}, bf16[64,2176]{1,0:T(8,128)(2,1)S(1)}, f32[64,2176]{1,0:T(8,128)S(1)}, f32[64,2176]{1,0:T(8,128)S(1)}) custom-call(s32[1]{0:T(128)} %bitcast.1.pos_ref, bf16[1,64,7168]{2,1,0:T(8,128)(2,1)S(1)} %collective-permute-done.3.refs_0_, bf16[1,64,7168]{2,1,0:T(8,128)(2,1)S(1)} %collective-permute-done.7.refs_1_, ...), custom_call_target="tpu_custom_call" | custom-call | tf_op jit(solution)/shard_map/partial_products/pallas_call | solution.py:145
  46.4 0.8 copy-done.2
  49.5 1.7 %collective-permute-done.2.refs_0_ = bf16[1,64,7168]{2,1,0:T(8,128)(2,1)} collective-permute-done((bf16[1,64,7168]{2,1,0:T(8,128)(2,1)}, bf16[1,64,7168]{2,1,0:T(8,128)(2,1)}, u32[]{:S(2)}, u32[]{:S(2)}) %collective-permute-start.2) | collective-permute-done | bytes 917536 | tf_op jit(solution)/shard_map/ppermute | solution.py:271
  51.7 1.3 collective-permute-start.11
  54.7 1.6 %collective-permute-start.10 = (bf16[64,2176]{1,0:T(8,128)(2,1)}, bf16[64,2176]{1,0:T(8,128)(2,1)S(1)}, u32[]{:S(2)}, u32[]{:S(2)}) collective-permute-start(bf16[64,2176]{1,0:T(8,128)(2,1)} %copy-done.15), channel_id=1, source_target_pairs={{0,4},{4,0},{8,12},{12,8},{1,5},{5,1},{9,13},{13,9},{2,6},{6,2},{1... | collective-permute-start | bytes 835592 | tf_op jit(solution)/shard_map/ppermute | solution.py:274
  56.7 16.0 %partial_products.7 = (bf16[64,2176]{1,0:T(8,128)(2,1)S(1)}, bf16[64,2176]{1,0:T(8,128)(2,1)S(1)}, f32[64,2176]{1,0:T(8,128)S(1)}, f32[64,2176]{1,0:T(8,128)S(1)}) custom-call(s32[1]{0:T(128)} %bitcast.1.pos_ref, bf16[1,64,7168]{2,1,0:T(8,128)(2,1)} %collective-permute-done.2.refs_0_, bf16[1,64,7168]{2,1,0:T(8,128)(2,1)} %collective-permute-done.8.refs_1_, ...), custom_call_target="tpu_custom_call" | custom-call | tf_op jit(solution)/shard_map/partial_products/pallas_call | solution.py:145
  72.7 1.8 %collective-permute-done.1.refs_0_ = bf16[1,64,7168]{2,1,0:T(8,128)(2,1)S(1)} collective-permute-done((bf16[1,64,7168]{2,1,0:T(8,128)(2,1)}, bf16[1,64,7168]{2,1,0:T(8,128)(2,1)S(1)}, u32[]{:S(2)}, u32[]{:S(2)}) %collective-permute-start.1) | collective-permute-done | bytes 917536 | tf_op jit(solution)/shard_map/ppermute | solution.py:271
  74.5 1.2 convert_add_fusion
  76.3 2.6 %collective-permute-start.12 = (bf16[64,2176]{1,0:T(8,128)(2,1)S(1)}, bf16[64,2176]{1,0:T(8,128)(2,1)S(1)}, u32[]{:S(2)}, u32[]{:S(2)}) collective-permute-start(bf16[64,2176]{1,0:T(8,128)(2,1)S(1)} %select_convert_fusion.2), channel_id=1, source_target_pairs={{0,8},{4,12},{8,0},{12,4},{1,9},{5,13},{9,1},{13,5},{2,10},{6,14},... | collective-permute-start | bytes 835592 | tf_op jit(solution)/shard_map/ppermute | solution.py:278
  79.3 10.7 %partial_products.8 = (bf16[64,2176]{1,0:T(8,128)(2,1)S(1)}, f32[64,2176]{1,0:T(8,128)S(1)}) custom-call(s32[1]{0:T(128)} %bitcast.1.pos_ref, bf16[1,64,7168]{2,1,0:T(8,128)(2,1)S(1)} %collective-permute-done.1.refs_0_, bf16[1,64,7168]{2,1,0:T(8,128)(2,1)S(1)} %collective-permute-done.9.refs_1_, bf16[7168,2048]{1,0:T(8,128)(2,1)} %refs_2_.9, ...), custom_call_target="tpu_custom_call" | custom-call | tf_op jit(solution)/shard_map/partial_products/pallas_call | solution.py:145
  90.0 3.7 %collective-permute-done.13.refs_0_ = bf16[1,64,7168]{2,1,0:T(8,128)(2,1)S(1)} collective-permute-done((bf16[1,64,7168]{2,1,0:T(8,128)(2,1)}, bf16[1,64,7168]{2,1,0:T(8,128)(2,1)S(1)}, u32[]{:S(2)}, u32[]{:S(2)}) %collective-permute-start.13) | collective-permute-done | bytes 917536 | tf_op jit(solution)/shard_map/ppermute | solution.py:271
  94.0 1.5 %collective-permute-start.16 = (bf16[64,2176]{1,0:T(8,128)(2,1)S(1)}, bf16[64,2176]{1,0:T(8,128)(2,1)S(1)}, u32[]{:S(2)}, u32[]{:S(2)}) collective-permute-start(bf16[64,2176]{1,0:T(8,128)(2,1)S(1)} %select_convert_fusion.1), channel_id=1, source_target_pairs={{0,8},{4,12},{8,0},{12,4},{1,9},{5,13},{9,1},{13,5},{2,10},{6,14},... | collective-permute-start | bytes 835592 | tf_op jit(solution)/shard_map/ppermute | solution.py:278
  95.5 1.6 %collective-permute-start.17 = (bf16[64,2176]{1,0:T(8,128)(2,1)S(1)}, bf16[64,2176]{1,0:T(8,128)(2,1)S(1)}, u32[]{:S(2)}, u32[]{:S(2)}) collective-permute-start(bf16[64,2176]{1,0:T(8,128)(2,1)S(1)} %get-tuple-element.135), channel_id=1, source_target_pairs={{0,4},{4,0},{8,12},{12,8},{1,5},{5,1},{9,13},{13,9},{2,6},{6,2},{1... | collective-permute-start | bytes 835592 | tf_op jit(solution)/shard_map/ppermute | solution.py:274
  97.2 10.7 %partial_products.9 = (bf16[64,2048]{1,0:T(8,128)(2,1)S(1)}, f32[64,2048]{1,0:T(8,128)S(1)}, f32[64,128]{1,0:T(8,128)S(1)}, f32[64,128]{1,0:T(8,128)S(1)}) custom-call(s32[1]{0:T(128)} %bitcast.1.pos_ref, bf16[1,64,7168]{2,1,0:T(8,128)(2,1)S(1)} %collective-permute-done.13.refs_0_, bf16[1,64,7168]{2,1,0:T(8,128)(2,1)S(1)} %collective-permute-done.14.refs_1_, ...), custom_call_target="tpu_custom_call" | custom-call | tf_op jit(solution)/shard_map/partial_products/pallas_call | solution.py:145
  107.9 0.8 collective-permute-start.20
  108.7 1.4 %collective-permute-done.17 = bf16[64,2176]{1,0:T(8,128)(2,1)S(1)} collective-permute-done((bf16[64,2176]{1,0:T(8,128)(2,1)S(1)}, bf16[64,2176]{1,0:T(8,128)(2,1)S(1)}, u32[]{:S(2)}, u32[]{:S(2)}) %collective-permute-start.17) | collective-permute-done | bytes 278560 | tf_op jit(solution)/shard_map/ppermute | solution.py:274
  110.8 2.1 %collective-permute-start.19 = (bf16[64,2176]{1,0:T(8,128)(2,1)S(1)}, bf16[64,2176]{1,0:T(8,128)(2,1)S(1)}, u32[]{:S(2)}, u32[]{:S(2)}) collective-permute-start(bf16[64,2176]{1,0:T(8,128)(2,1)S(1)} %get-tuple-element.140), channel_id=1, source_target_pairs={{0,8},{4,12},{8,0},{12,4},{1,9},{5,13},{9,1},{13,5},{2,10},{6,14},... | collective-permute-start | bytes 835592 | tf_op jit(solution)/shard_map/ppermute | solution.py:278
  112.9 1.0 collective-permute-start.22
  114.0 14.0 %collective-permute-done.22 = f32[64,128]{1,0:T(8,128)S(1)} collective-permute-done((f32[64,128]{1,0:T(8,128)S(1)}, f32[64,128]{1,0:T(8,128)S(1)}, u32[]{:S(2)}, u32[]{:S(2)}) %collective-permute-start.22) | collective-permute-done | bytes 32800 | tf_op jit(solution)/shard_map/ppermute | solution.py:278
  128.4 1.6 %collective-permute-start.25 = (bf16[4,64,64]{2,1,0:T(8,128)(2,1)S(1)}, bf16[4,64,64]{2,1,0:T(8,128)(2,1)S(1)}, u32[]{:S(2)}, u32[]{:S(2)}) collective-permute-start(bf16[4,64,64]{2,1,0:T(8,128)(2,1)S(1)} %select_bitcast_fusion), channel_id=1, source_target_pairs={{0,2},{1,3},{2,0},{3,1},{4,6},{5,7},{6,4},{7,5},{8,10},{9,11},{10,... | collective-permute-start | bytes 98312 | tf_op jit(solution)/shard_map/ppermute | solution.py:417
  130.5 2.2 %collective-permute-done.25 = bf16[4,64,64]{2,1,0:T(8,128)(2,1)S(1)} collective-permute-done((bf16[4,64,64]{2,1,0:T(8,128)(2,1)S(1)}, bf16[4,64,64]{2,1,0:T(8,128)(2,1)S(1)}, u32[]{:S(2)}, u32[]{:S(2)}) %collective-permute-start.25) | collective-permute-done | bytes 32800 | tf_op jit(solution)/shard_map/ppermute | solution.py:417
  133.1 1.0 collective-permute-done.24
  134.3 2.5 %finish_steps.1 = (bf16[4,64,2048]{2,1,0:T(8,128)(2,1)}, bf16[64,2048]{1,0:T(8,128)(2,1)S(1)}) custom-call(bf16[256,64]{1,0:T(8,128)(2,1)S(1)} %bitcast.30, s32[256,1]{1,0:T(8,128)S(1)} %copy-done.4, s32[4]{0:T(128)S(1)} %pad_add_fusion.order_ref, bf16[64,2048]{1,0:T(8,128)(2,1)S(1)} %bitcast.31, bf16[64,2048]{1,0:T(8,128)(2,1)} %bitcast.14.refs_1_, ...), custom_call_target="tpu_custom_call" | custom-call | tf_op jit(solution)/shard_map/finish_steps/pallas_call | solution.py:203
  136.8 1.6 %collective-permute-done.27.refs_1_ = bf16[64,2048]{1,0:T(8,128)(2,1)S(1)} collective-permute-done((bf16[64,2048]{1,0:T(8,128)(2,1)S(1)}, bf16[64,2048]{1,0:T(8,128)(2,1)S(1)}, u32[]{:S(2)}, u32[]{:S(2)}) %collective-permute-start.27) | collective-permute-done | bytes 262176 | tf_op jit(solution)/shard_map/ppermute | solution.py:278
  138.4 0.8 finish_last.1
  (94 shorter events, 10.5 us)
Async XLA Ops:
  0.0 53.0 %copy-start = (s32[256,1]{0,1:T(1,128)S(1)}, s32[256,1]{0,1:T(1,128)}, u32[]{:S(2)}) copy-start(s32[256,1]{0,1:T(1,128)} %param.10) | copy-start | bytes 3076
  0.0 9.5 %collective-permute-start = (bf16[4,64,7168]{2,1,0:T(8,128)(2,1)}, bf16[4,64,7168]{2,1,0:T(8,128)(2,1)}, u32[]{:S(2)}, u32[]{:S(2)}) collective-permute-start(bf16[4,64,7168]{2,1,0:T(8,128)(2,1)} %refs_2_.7), channel_id=1, source_target_pairs={{0,1},{1,0},{2,3},{3,2},{4,5},{5,4},{6,7},{7,6},{8,9},{9,8},{10,11... | collective-permute-start | bytes 11010056 | tf_op jit(solution)/shard_map/ppermute | solution.py:268
  2.7 25.3 %collective-permute-start.3 = (bf16[1,64,7168]{2,1,0:T(8,128)(2,1)}, bf16[1,64,7168]{2,1,0:T(8,128)(2,1)S(1)}, u32[]{:S(2)}, u32[]{:S(2)}) collective-permute-start(bf16[1,64,7168]{2,1,0:T(8,128)(2,1)} %slice.51), channel_id=1, source_target_pairs={{2,0},{0,2},{3,1},{1,3},{6,4},{4,6},{7,5},{5,7},{10,8},{8,10},{11,... | collective-permute-start | bytes 2752520 | tf_op jit(solution)/shard_map/ppermute | solution.py:271
  5.3 22.0 %collective-permute-start.4 = (bf16[1,64,2048]{2,1,0:T(8,128)(2,1)S(1)}, bf16[1,64,2048]{2,1,0:T(8,128)(2,1)}, u32[]{:S(2)}, u32[]{:S(2)}) collective-permute-start(bf16[1,64,2048]{2,1,0:T(8,128)(2,1)S(1)} %copy-done.7), channel_id=1, source_target_pairs={{0,8},{4,12},{8,0},{12,4},{1,9},{5,13},{9,1},{13,5},{2,10},{6,14},... | collective-permute-start | bytes 786440 | tf_op jit(solution)/shard_map/ppermute | solution.py:274
  7.9 19.4 %collective-permute-start.5 = (bf16[1,64,2048]{2,1,0:T(8,128)(2,1)S(1)}, bf16[1,64,2048]{2,1,0:T(8,128)(2,1)S(1)}, u32[]{:S(2)}, u32[]{:S(2)}) collective-permute-start(bf16[1,64,2048]{2,1,0:T(8,128)(2,1)S(1)} %copy-done.7), channel_id=1, source_target_pairs={{0,4},{4,0},{8,12},{12,8},{1,5},{5,1},{9,13},{13,9},{2,6},{6,2},{1... | collective-permute-start | bytes 786440 | tf_op jit(solution)/shard_map/ppermute | solution.py:274
  28.1 2.5 %collective-permute-start.7 = (bf16[1,64,7168]{2,1,0:T(8,128)(2,1)S(1)}, bf16[1,64,7168]{2,1,0:T(8,128)(2,1)S(1)}, u32[]{:S(2)}, u32[]{:S(2)}) collective-permute-start(bf16[1,64,7168]{2,1,0:T(8,128)(2,1)S(1)} %collective-permute-done.3.refs_0_), channel_id=1, source_target_pairs={{0,1},{1,0},{2,3},{3,2},{4,5},{5,4},{6,7},{7,6},{8,9},{9,8},{10,11... | collective-permute-start | bytes 2752520 | tf_op jit(solution)/shard_map/ppermute | solution.py:268
  28.1 25.0 %copy-start.16 = (s32[4]{0:T(128)S(1)}, s32[4]{0:T(128)}, u32[]{:S(2)}) copy-start(s32[4]{0:T(128)} %param.11) | copy-start | bytes 52
  28.1 23.1 %collective-permute-start.2 = (bf16[1,64,7168]{2,1,0:T(8,128)(2,1)}, bf16[1,64,7168]{2,1,0:T(8,128)(2,1)}, u32[]{:S(2)}, u32[]{:S(2)}) collective-permute-start(bf16[1,64,7168]{2,1,0:T(8,128)(2,1)} %get-tuple-element.83), channel_id=1, source_target_pairs={{2,0},{0,2},{3,1},{1,3},{6,4},{4,6},{7,5},{5,7},{10,8},{8,10},{11,... | collective-permute-start | bytes 2752520 | tf_op jit(solution)/shard_map/ppermute | solution.py:271
  28.7 20.1 %collective-permute-start.6 = (bf16[1,64,2048]{2,1,0:T(8,128)(2,1)}, bf16[1,64,2048]{2,1,0:T(8,128)(2,1)S(1)}, u32[]{:S(2)}, u32[]{:S(2)}) collective-permute-start(bf16[1,64,2048]{2,1,0:T(8,128)(2,1)} %collective-permute-done.4), channel_id=1, source_target_pairs={{0,4},{4,0},{8,12},{12,8},{1,5},{5,1},{9,13},{13,9},{2,6},{6,2},{1... | collective-permute-start | bytes 786440 | tf_op jit(solution)/shard_map/ppermute | solution.py:274
  51.1 5.1 %collective-permute-start.8 = (bf16[1,64,7168]{2,1,0:T(8,128)(2,1)}, bf16[1,64,7168]{2,1,0:T(8,128)(2,1)}, u32[]{:S(2)}, u32[]{:S(2)}) collective-permute-start(bf16[1,64,7168]{2,1,0:T(8,128)(2,1)} %collective-permute-done.2.refs_0_), channel_id=1, source_target_pairs={{0,1},{1,0},{2,3},{3,2},{4,5},{5,4},{6,7},{7,6},{8,9},{9,8},{10,11... | collective-permute-start | bytes 2752520 | tf_op jit(solution)/shard_map/ppermute | solution.py:268
  51.1 23.4 %collective-permute-start.1 = (bf16[1,64,7168]{2,1,0:T(8,128)(2,1)}, bf16[1,64,7168]{2,1,0:T(8,128)(2,1)S(1)}, u32[]{:S(2)}, u32[]{:S(2)}) collective-permute-start(bf16[1,64,7168]{2,1,0:T(8,128)(2,1)} %get-tuple-element.82), channel_id=1, source_target_pairs={{2,0},{0,2},{3,1},{1,3},{6,4},{4,6},{7,5},{5,7},{10,8},{8,10},{11,... | collective-permute-start | bytes 2752520 | tf_op jit(solution)/shard_map/ppermute | solution.py:271
  51.7 22.8 %collective-permute-start.11 = (bf16[128,2176]{1,0:T(8,128)(2,1)}, bf16[128,2176]{1,0:T(8,128)(2,1)}, u32[]{:S(2)}, u32[]{:S(2)}) collective-permute-start(bf16[128,2176]{1,0:T(8,128)(2,1)} %copy-done.13), channel_id=1, source_target_pairs={{0,4},{4,0},{8,12},{12,8},{1,5},{5,1},{9,13},{13,9},{2,6},{6,2},{1... | collective-permute-start | bytes 1671176 | tf_op jit(solution)/shard_map/ppermute | solution.py:274
  54.1 39.7 %collective-permute-start.13 = (bf16[1,64,7168]{2,1,0:T(8,128)(2,1)}, bf16[1,64,7168]{2,1,0:T(8,128)(2,1)S(1)}, u32[]{:S(2)}, u32[]{:S(2)}) collective-permute-start(bf16[1,64,7168]{2,1,0:T(8,128)(2,1)} %get-tuple-element.116), channel_id=1, source_target_pairs={{2,0},{0,2},{3,1},{1,3},{6,4},{4,6},{7,5},{5,7},{10,8},{8,10},{11,... | collective-permute-start | bytes 2752520 | tf_op jit(solution)/shard_map/ppermute | solution.py:271
  54.7 21.5 %collective-permute-start.10 = (bf16[64,2176]{1,0:T(8,128)(2,1)}, bf16[64,2176]{1,0:T(8,128)(2,1)S(1)}, u32[]{:S(2)}, u32[]{:S(2)}) collective-permute-start(bf16[64,2176]{1,0:T(8,128)(2,1)} %copy-done.15), channel_id=1, source_target_pairs={{0,4},{4,0},{8,12},{12,8},{1,5},{5,1},{9,13},{13,9},{2,6},{6,2},{1... | collective-permute-start | bytes 835592 | tf_op jit(solution)/shard_map/ppermute | solution.py:274
  56.3 52.5 %collective-permute-start.18 = (bf16[64,2176]{1,0:T(8,128)(2,1)}, bf16[64,2176]{1,0:T(8,128)(2,1)S(1)}, u32[]{:S(2)}, u32[]{:S(2)}) collective-permute-start(bf16[64,2176]{1,0:T(8,128)(2,1)} %copy-done.14), channel_id=1, source_target_pairs={{0,4},{4,0},{8,12},{12,8},{1,5},{5,1},{9,13},{13,9},{2,6},{6,2},{1... | collective-permute-start | bytes 835592 | tf_op jit(solution)/shard_map/ppermute | solution.py:274
  74.5 4.4 %collective-permute-start.9 = (bf16[1,64,7168]{2,1,0:T(8,128)(2,1)S(1)}, bf16[1,64,7168]{2,1,0:T(8,128)(2,1)S(1)}, u32[]{:S(2)}, u32[]{:S(2)}) collective-permute-start(bf16[1,64,7168]{2,1,0:T(8,128)(2,1)S(1)} %collective-permute-done.1.refs_0_), channel_id=1, source_target_pairs={{0,1},{1,0},{2,3},{3,2},{4,5},{5,4},{6,7},{7,6},{8,9},{9,8},{10,11... | collective-permute-start | bytes 2752520 | tf_op jit(solution)/shard_map/ppermute | solution.py:268
  75.7 18.1 %collective-permute-start.15 = (bf16[64,2176]{1,0:T(8,128)(2,1)S(1)}, bf16[64,2176]{1,0:T(8,128)(2,1)S(1)}, u32[]{:S(2)}, u32[]{:S(2)}) collective-permute-start(bf16[64,2176]{1,0:T(8,128)(2,1)S(1)} %get-tuple-element.125), channel_id=1, source_target_pairs={{0,4},{4,0},{8,12},{12,8},{1,5},{5,1},{9,13},{13,9},{2,6},{6,2},{1... | collective-permute-start | bytes 835592 | tf_op jit(solution)/shard_map/ppermute | solution.py:274
  76.3 17.7 %collective-permute-start.12 = (bf16[64,2176]{1,0:T(8,128)(2,1)S(1)}, bf16[64,2176]{1,0:T(8,128)(2,1)S(1)}, u32[]{:S(2)}, u32[]{:S(2)}) collective-permute-start(bf16[64,2176]{1,0:T(8,128)(2,1)S(1)} %select_convert_fusion.2), channel_id=1, source_target_pairs={{0,8},{4,12},{8,0},{12,4},{1,9},{5,13},{9,1},{13,5},{2,10},{6,14},... | collective-permute-start | bytes 835592 | tf_op jit(solution)/shard_map/ppermute | solution.py:278
  78.9 18.2 %collective-permute-start.21 = (bf16[64,2176]{1,0:T(8,128)(2,1)S(1)}, bf16[64,2176]{1,0:T(8,128)(2,1)S(1)}, u32[]{:S(2)}, u32[]{:S(2)}) collective-permute-start(bf16[64,2176]{1,0:T(8,128)(2,1)S(1)} %get-tuple-element.147), channel_id=1, source_target_pairs={{0,4},{4,0},{8,12},{12,8},{1,5},{5,1},{9,13},{13,9},{2,6},{6,2},{1... | collective-permute-start | bytes 835592 | tf_op jit(solution)/shard_map/ppermute | solution.py:274
  93.8 3.4 %collective-permute-start.14 = (bf16[1,64,7168]{2,1,0:T(8,128)(2,1)S(1)}, bf16[1,64,7168]{2,1,0:T(8,128)(2,1)S(1)}, u32[]{:S(2)}, u32[]{:S(2)}) collective-permute-start(bf16[1,64,7168]{2,1,0:T(8,128)(2,1)S(1)} %collective-permute-done.13.refs_0_), channel_id=1, source_target_pairs={{0,1},{1,0},{2,3},{3,2},{4,5},{5,4},{6,7},{7,6},{8,9},{9,8},{10,11... | collective-permute-start | bytes 2752520 | tf_op jit(solution)/shard_map/ppermute | solution.py:268
  94.0 13.8 %copy-start.5 = (bf16[64,2176]{1,0:T(8,128)(2,1)}, bf16[64,2176]{1,0:T(8,128)(2,1)S(1)}, u32[]{:S(2)}) copy-start(bf16[64,2176]{1,0:T(8,128)(2,1)S(1)} %collective-permute-done.12.refs_5_) | copy-start | bytes 835588
  94.0 16.3 %collective-permute-start.16 = (bf16[64,2176]{1,0:T(8,128)(2,1)S(1)}, bf16[64,2176]{1,0:T(8,128)(2,1)S(1)}, u32[]{:S(2)}, u32[]{:S(2)}) collective-permute-start(bf16[64,2176]{1,0:T(8,128)(2,1)S(1)} %select_convert_fusion.1), channel_id=1, source_target_pairs={{0,8},{4,12},{8,0},{12,4},{1,9},{5,13},{9,1},{13,5},{2,10},{6,14},... | collective-permute-start | bytes 835592 | tf_op jit(solution)/shard_map/ppermute | solution.py:278
  95.5 14.7 %collective-permute-start.17 = (bf16[64,2176]{1,0:T(8,128)(2,1)S(1)}, bf16[64,2176]{1,0:T(8,128)(2,1)S(1)}, u32[]{:S(2)}, u32[]{:S(2)}) collective-permute-start(bf16[64,2176]{1,0:T(8,128)(2,1)S(1)} %get-tuple-element.135), channel_id=1, source_target_pairs={{0,4},{4,0},{8,12},{12,8},{1,5},{5,1},{9,13},{13,9},{2,6},{6,2},{1... | collective-permute-start | bytes 835592 | tf_op jit(solution)/shard_map/ppermute | solution.py:274
  97.1 13.0 %copy-start.3 = (f32[64,2176]{1,0:T(8,128)S(1)}, f32[64,2176]{1,0:T(8,128)}, u32[]{:S(2)}) copy-start(f32[64,2176]{1,0:T(8,128)} %copy-done.2) | copy-start | bytes 1671172
  107.9 5.0 %collective-permute-start.20 = (f32[64,128]{1,0:T(8,128)S(1)}, f32[64,128]{1,0:T(8,128)S(1)}, u32[]{:S(2)}, u32[]{:S(2)}) collective-permute-start(f32[64,128]{1,0:T(8,128)S(1)} %get-tuple-element.144), channel_id=1, source_target_pairs={{0,4},{4,0},{8,12},{12,8},{1,5},{5,1},{9,13},{13,9},{2,6},{6,2},{1... | collective-permute-start | bytes 98312 | tf_op jit(solution)/shard_map/ppermute | solution.py:274
  110.3 17.7 %collective-permute-start.23 = (bf16[64,2048]{1,0:T(8,128)(2,1)S(1)}, bf16[64,2048]{1,0:T(8,128)(2,1)S(1)}, u32[]{:S(2)}, u32[]{:S(2)}) collective-permute-start(bf16[64,2048]{1,0:T(8,128)(2,1)S(1)} %get-tuple-element.150), channel_id=1, source_target_pairs={{0,4},{4,0},{8,12},{12,8},{1,5},{5,1},{9,13},{13,9},{2,6},{6,2},{1... | collective-permute-start | bytes 786440 | tf_op jit(solution)/shard_map/ppermute | solution.py:274
  110.8 17.4 %collective-permute-start.19 = (bf16[64,2176]{1,0:T(8,128)(2,1)S(1)}, bf16[64,2176]{1,0:T(8,128)(2,1)S(1)}, u32[]{:S(2)}, u32[]{:S(2)}) collective-permute-start(bf16[64,2176]{1,0:T(8,128)(2,1)S(1)} %get-tuple-element.140), channel_id=1, source_target_pairs={{0,8},{4,12},{8,0},{12,4},{1,9},{5,13},{9,1},{13,5},{2,10},{6,14},... | collective-permute-start | bytes 835592 | tf_op jit(solution)/shard_map/ppermute | solution.py:278
  112.9 15.1 %collective-permute-start.22 = (f32[64,128]{1,0:T(8,128)S(1)}, f32[64,128]{1,0:T(8,128)S(1)}, u32[]{:S(2)}, u32[]{:S(2)}) collective-permute-start(f32[64,128]{1,0:T(8,128)S(1)} %get-tuple-element.159), channel_id=1, source_target_pairs={{0,8},{4,12},{8,0},{12,4},{1,9},{5,13},{9,1},{13,5},{2,10},{6,14},... | collective-permute-start | bytes 98312 | tf_op jit(solution)/shard_map/ppermute | solution.py:278
  128.1 10.3 %collective-permute-start.27 = (bf16[64,2048]{1,0:T(8,128)(2,1)S(1)}, bf16[64,2048]{1,0:T(8,128)(2,1)S(1)}, u32[]{:S(2)}, u32[]{:S(2)}) collective-permute-start(bf16[64,2048]{1,0:T(8,128)(2,1)S(1)} %select_convert_fusion.3), channel_id=1, source_target_pairs={{0,8},{4,12},{8,0},{12,4},{1,9},{5,13},{9,1},{13,5},{2,10},{6,14},... | collective-permute-start | bytes 786440 | tf_op jit(solution)/shard_map/ppermute | solution.py:278
  128.4 4.3 %collective-permute-start.25 = (bf16[4,64,64]{2,1,0:T(8,128)(2,1)S(1)}, bf16[4,64,64]{2,1,0:T(8,128)(2,1)S(1)}, u32[]{:S(2)}, u32[]{:S(2)}) collective-permute-start(bf16[4,64,64]{2,1,0:T(8,128)(2,1)S(1)} %select_bitcast_fusion), channel_id=1, source_target_pairs={{0,2},{1,3},{2,0},{3,1},{4,6},{5,7},{6,4},{7,5},{8,10},{9,11},{10,... | collective-permute-start | bytes 98312 | tf_op jit(solution)/shard_map/ppermute | solution.py:417
  130.0 3.1 %collective-permute-start.26 = (bf16[4,64,64]{2,1,0:T(8,128)(2,1)S(1)}, bf16[4,64,64]{2,1,0:T(8,128)(2,1)S(1)}, u32[]{:S(2)}, u32[]{:S(2)}) collective-permute-start(bf16[4,64,64]{2,1,0:T(8,128)(2,1)S(1)} %select_bitcast_fusion), channel_id=1, source_target_pairs={{0,3},{1,0},{2,1},{3,2},{4,7},{5,4},{6,5},{7,6},{8,11},{9,8},{10,9... | collective-permute-start | bytes 98312 | tf_op jit(solution)/shard_map/ppermute | solution.py:417
  130.0 4.2 %collective-permute-start.24 = (bf16[4,64,64]{2,1,0:T(8,128)(2,1)S(1)}, bf16[4,64,64]{2,1,0:T(8,128)(2,1)S(1)}, u32[]{:S(2)}, u32[]{:S(2)}) collective-permute-start(bf16[4,64,64]{2,1,0:T(8,128)(2,1)S(1)} %select_bitcast_fusion), channel_id=1, source_target_pairs={{0,1},{1,2},{2,3},{3,0},{4,5},{5,6},{6,7},{7,4},{8,9},{9,10},{10,1... | collective-permute-start | bytes 98312 | tf_op jit(solution)/shard_map/ppermute | solution.py:417
  (14 other events, 54.8 us)
